TPU v7x, 32 devices: a whole 2x2x4 slice. The times are simulated.
32 devices in a mesh: req: 8 (over z, x), tp: 4 (over y, core).
Axes of the slice: x: 2, y: 2, z: 4, core: 2. Of those that a mesh axis runs over, the one named last changes fastest.
Arguments:
- hidden_in: bfloat16 [1024, 2048], P('req', 'tp'), may hold values from -48 to 48
- norm_in_gain: float32 [2048], replicated, may hold values from 0.1 to 1.9
- q_weight: bfloat16 [2048, 2048], P(None, 'tp'), may hold values from -0.125 to 0.125
- k_weight: bfloat16 [2048, 512], P(None, 'tp'), may hold values from -0.125 to 0.125
- v_weight: bfloat16 [2048, 512], P(None, 'tp'), may hold values from -0.125 to 0.125
- q_gain: float32 [128], replicated, may hold values from 0.1 to 1.9
- k_gain: float32 [128], replicated, may hold values from 0.1 to 1.9
- o_weight: bfloat16 [2048, 2048], P('tp'), may hold values from -0.125 to 0.125
- key_pages: bfloat16 [4, 384, 128, 128], P('tp', 'req'), may hold values from -256 to 256
- value_pages: bfloat16 [4, 384, 128, 128], P('tp', 'req'), may hold values from -6 to 6
- page_table: int32 [72, 32], P('req'), may hold values from 0 to 47, as said below
- cache_len: int32 [72], P('req'), may hold values from 1 to 4096, as said below
- norm_post_gain: float32 [2048], replicated, may hold values from 0.1 to 1.9
- expert_ids: int32 [1024, 8], P('req'), may hold values from 0 to 15, all different within a row; in each aligned block of 128 rows (0 to 127, 128 to 255, ...) at most 96 rows name the same one
- route_weights: float32 [1024, 8], P('req'), may hold values from 0.02 to 0.25
- gate_weight: bfloat16 [16, 2048, 768], P('req', None, 'tp'), may hold values from -0.125 to 0.125
- up_weight: bfloat16 [16, 2048, 768], P('req', None, 'tp'), may hold values from -0.125 to 0.125
- down_weight: bfloat16 [16, 768, 2048], P('req', 'tp'), may hold values from -0.21875 to 0.21875
Outputs:
- layer_out: bfloat16 [1024, 2048], P('req', 'tp')
Inputs may be any that keep to these rules, and one draw needn't show every extreme that they name: `cache_len`: in each group of 9 consecutive requests one request holds 4096 cached tokens and another exactly 256; the others hold at most 256. `page_table`: for request r of group g = r // 9, entry j with j * 128 below cache_len[r] names the page, among group g's 48 pages of the caches, that holds the request's cached tokens j * 128 to j * 128 + 127; these pages are distinct within a group. Other entries name arbitrary pages of the group and are not read; pages that no read entry names hold unused data. `expert_ids`: among the 128 rows of one group no expert is named more than 96 times.
All inputs are finite; a program needn't handle non-finite values.
Results may differ from a plain program's by a relative error of at most 0.006.
Values may be sent and summed in bfloat16 or wider, within the bound.
No kernel may reach another device: no remote copies, remote signals or barrier semaphores. Data moves between devices by JAX's collectives and lax.ppermute only.
A program may use at most 128 MiB of HBM per device.

v0:
```python
import math

import jax
import jax.numpy as jnp
from jax import lax
from jax.sharding import PartitionSpec as P

PAGE = 128
MAXPG = 32
PRE = 120
TOK_DEV = 128
REQS_DEV = 9
POOL = 48


NORM_EPS = 1e-06
ROPE_BASE = 1000000.0


def rms_scale(values, gain_vec):
    mean_square = jnp.mean(values * values, axis=-1, keepdims=True)
    return values * lax.rsqrt(mean_square + NORM_EPS) * gain_vec


def rotate(values, positions):
    half_dim = values.shape[-1] // 2
    exponent = jnp.arange(half_dim, dtype=jnp.float32) * (2.0 / values.shape[-1])
    frequency = jnp.power(jnp.float32(ROPE_BASE), -exponent)
    angles = positions.astype(jnp.float32)[:, None] * frequency[None, :]
    cosine = jnp.cos(angles)[:, None, :]
    sine_val = jnp.sin(angles)[:, None, :]
    front_half = values[..., :half_dim]
    back_half = values[..., half_dim:]
    return jnp.concatenate(
        [front_half * cosine - back_half * sine_val, back_half * cosine + front_half * sine_val],
        axis=-1,
    )


def token_layout(lengths):
    local_idx = jnp.arange(TOK_DEV, dtype=jnp.int32)
    requests = jnp.where(local_idx < PRE, 0, local_idx - PRE + 1)
    offsets = jnp.where(local_idx < PRE, local_idx, 0)
    request_hot = (requests[:, None] == jnp.arange(REQS_DEV, dtype=jnp.int32)[None, :]).astype(
        jnp.int32
    )
    positions = jnp.sum(request_hot * lengths[None, :], axis=1) + offsets
    return (requests, positions)


def page_slots(table, lengths):
    pages_used = (lengths + PAGE - 1) // PAGE
    entry_live = jnp.arange(MAXPG, dtype=jnp.int32)[None, :] < pages_used[:, None]
    page_match = (
        (table[:, :, None] == jnp.arange(POOL, dtype=jnp.int32)[None, None, :])
        & entry_live[:, :, None]
    ).astype(jnp.int32)
    page_owner = jnp.sum(
        page_match * jnp.arange(REQS_DEV, dtype=jnp.int32)[:, None, None], axis=(0, 1)
    )
    page_start = jnp.sum(
        page_match * (jnp.arange(MAXPG, dtype=jnp.int32) * PAGE)[None, :, None], axis=(0, 1)
    )
    page_used = jnp.sum(page_match, axis=(0, 1)) > 0
    owner_length = jnp.sum(page_match * lengths[:, None, None], axis=(0, 1))
    slot_pos = page_start[:, None] + jnp.arange(PAGE, dtype=jnp.int32)[None, :]
    slot_live = page_used[:, None] & (slot_pos < owner_length[:, None])
    slot_owner = jnp.where(slot_live, page_owner[:, None], -1)
    return slot_owner.reshape(POOL * PAGE)


def attend(
    queries, keys_new, values_new, keys_cache, values_cache, requests, positions, slot_owner
):
    inv_root = 1.0 / math.sqrt(queries.shape[-1])
    cache_mask = slot_owner[None, :] == requests[:, None]
    new_mask = (requests[None, :] == requests[:, None]) & (positions[None, :] <= positions[:, None])
    score_cache = (
        jnp.einsum("tkgh,knh->kgtn", queries, keys_cache, preferred_element_type=jnp.float32)
        * inv_root
    )
    score_new = (
        jnp.einsum("tkgh,skh->kgts", queries, keys_new, preferred_element_type=jnp.float32)
        * inv_root
    )
    score_cache = jnp.where(cache_mask[None, None], score_cache, -1e30)
    score_new = jnp.where(new_mask[None, None], score_new, -1e30)
    row_max = jnp.maximum(
        jnp.max(score_cache, axis=-1, keepdims=True), jnp.max(score_new, axis=-1, keepdims=True)
    )
    exp_cache = jnp.where(cache_mask[None, None], jnp.exp(score_cache - row_max), 0.0)
    exp_new = jnp.where(new_mask[None, None], jnp.exp(score_new - row_max), 0.0)
    total = jnp.sum(exp_cache, axis=-1, keepdims=True) + jnp.sum(exp_new, axis=-1, keepdims=True)
    prob_cache = (exp_cache / total).astype(jnp.bfloat16)
    prob_new = (exp_new / total).astype(jnp.bfloat16)
    mixed = jnp.einsum(
        "kgtn,knh->tkgh", prob_cache, values_cache, preferred_element_type=jnp.float32
    )
    mixed = mixed + jnp.einsum(
        "kgts,skh->tkgh", prob_new, values_new, preferred_element_type=jnp.float32
    )
    return mixed.astype(jnp.bfloat16).reshape(queries.shape[0], -1)


def expert_apply(blocks, gate_weight, up_weight, down_weight):
    local_experts = gate_weight.shape[0]
    sources = blocks.shape[0] // local_experts
    slot_count = blocks.shape[1]
    grouped = blocks.reshape(sources, local_experts, slot_count, blocks.shape[2])
    gate_acts = jnp.einsum(
        "sekd,edf->sekf", grouped, gate_weight, preferred_element_type=jnp.float32
    )
    up_acts = jnp.einsum("sekd,edf->sekf", grouped, up_weight, preferred_element_type=jnp.float32)
    hidden_act = (jax.nn.silu(gate_acts) * up_acts).astype(jnp.bfloat16)
    part_sums = jnp.einsum(
        "sekf,efd->sekd", hidden_act, down_weight, preferred_element_type=jnp.float32
    ).astype(jnp.bfloat16)
    return part_sums.reshape(sources * local_experts, slot_count, part_sums.shape[3])


def build_buffer(normed, slot_index, top_count, expert_count, capacity):
    picked = jnp.repeat(normed, top_count, axis=0)
    buffer_rows = (
        jnp.zeros((expert_count * capacity, normed.shape[1]), normed.dtype)
        .at[slot_index]
        .set(picked)
    )
    return buffer_rows.reshape(expert_count, capacity, normed.shape[1])


def weigh_back(returned, slot_index, route_weights, token_count, top_count):
    row_width = returned.shape[2]
    back_rows = returned.reshape(returned.shape[0] * returned.shape[1], row_width)[slot_index]
    weighted = (
        back_rows.astype(jnp.float32) * route_weights.reshape(token_count * top_count)[:, None]
    )
    return jnp.sum(weighted.reshape(token_count, top_count, row_width), axis=1)


def body(
    hidden_in,
    norm_in_gain,
    q_weight,
    k_weight,
    v_weight,
    q_gain,
    k_gain,
    o_weight,
    key_pages,
    value_pages,
    page_table,
    cache_len,
    norm_post_gain,
    expert_ids,
    route_weights,
    gate_weight,
    up_weight,
    down_weight,
):
    req_count = lax.axis_size("req")
    tp_index = lax.axis_index("tp")
    share_width = hidden_in.shape[1]
    head_dim = q_gain.shape[0]
    kv_local = key_pages.shape[0]
    group_size = q_weight.shape[1] // head_dim // kv_local
    token_count = hidden_in.shape[0]
    x_full = lax.all_gather(hidden_in, "tp", axis=1, tiled=True)
    x_float = x_full.astype(jnp.float32)
    normed_in = rms_scale(x_float, norm_in_gain).astype(jnp.bfloat16)
    query_lin = jnp.dot(normed_in, q_weight, preferred_element_type=jnp.float32).reshape(
        token_count, kv_local * group_size, head_dim
    )
    key_lin = jnp.dot(normed_in, k_weight, preferred_element_type=jnp.float32).reshape(
        token_count, kv_local, head_dim
    )
    values_new = (
        jnp.dot(normed_in, v_weight, preferred_element_type=jnp.float32)
        .astype(jnp.bfloat16)
        .reshape(token_count, kv_local, head_dim)
    )
    requests, positions = token_layout(cache_len)
    queries = (
        rotate(rms_scale(query_lin, q_gain), positions)
        .astype(jnp.bfloat16)
        .reshape(token_count, kv_local, group_size, head_dim)
    )
    keys_new = rotate(rms_scale(key_lin, k_gain), positions).astype(jnp.bfloat16)
    slot_owner = page_slots(page_table, cache_len)
    cache_slots = key_pages.shape[1] * key_pages.shape[2]
    keys_cache = key_pages.reshape(kv_local, cache_slots, head_dim)
    values_cache = value_pages.reshape(kv_local, cache_slots, head_dim)
    attended = attend(
        queries, keys_new, values_new, keys_cache, values_cache, requests, positions, slot_owner
    )
    head_part = jnp.dot(attended, o_weight, preferred_element_type=jnp.float32)
    top_count = expert_ids.shape[1]
    expert_count = gate_weight.shape[0] * req_count
    capacity = max(2, 3 * token_count * top_count // (2 * expert_count))
    flat_expert = expert_ids.reshape(token_count * top_count)
    one_hot = (flat_expert[:, None] == jnp.arange(expert_count, dtype=jnp.int32)[None, :]).astype(
        jnp.int32
    )
    slot_rank = jnp.sum((jnp.cumsum(one_hot, axis=0) - one_hot) * one_hot, axis=1)
    slot_index = flat_expert * capacity + slot_rank
    head_sum = lax.psum(head_part.astype(jnp.bfloat16), "tp").astype(jnp.float32)
    residual_full = x_float + head_sum
    normed_post = rms_scale(residual_full, norm_post_gain).astype(jnp.bfloat16)
    residual = lax.dynamic_slice_in_dim(residual_full, tp_index * share_width, share_width, 1)
    send_buffer = build_buffer(normed_post, slot_index, top_count, expert_count, capacity)
    part_sums = expert_apply(
        lax.all_to_all(send_buffer, "req", split_axis=0, concat_axis=0, tiled=True),
        gate_weight,
        up_weight,
        down_weight,
    )
    returned = lax.all_to_all(part_sums, "req", split_axis=0, concat_axis=0, tiled=True)
    moe_term = weigh_back(returned, slot_index, route_weights, token_count, top_count)
    moe_share = lax.psum_scatter(
        moe_term.astype(jnp.bfloat16), "tp", scatter_dimension=1, tiled=True
    ).astype(jnp.float32)
    return (residual + moe_share).astype(jnp.bfloat16)


def solution(mesh):
    return jax.shard_map(
        body,
        mesh=mesh,
        in_specs=(
            P("req", "tp"),
            P(),
            P(None, "tp"),
            P(None, "tp"),
            P(None, "tp"),
            P(),
            P(),
            P("tp", None),
            P("tp", "req", None, None),
            P("tp", "req", None, None),
            P("req", None),
            P("req"),
            P(),
            P("req", None),
            P("req", None),
            P("req", None, "tp"),
            P("req", None, "tp"),
            P("req", "tp", None),
        ),
        out_specs=P("req", "tp"),
        check_vma=False,
    )
```

profile of v0, /device:TPU:0, one launch (start us, length us, event | category | flops | bytes accessed | tf_op | source)
XLA Modules:
  0.0 442.7 jit_solution(16416173384125219041)
XLA Ops:
  6.6 9.0 %all_gather.3 = bf16[128,2048]{1,0:T(8,128)(2,1)S(1)} all-gather(bf16[128,512]{1,0:T(8,128)(2,1)} %param.18), channel_id=1, replica_groups=mesh['req'=8,'tp'=4] {'tp'}, dimensions={1}, use_global_device_ids=true | all-gather | bytes 655360 | tf_op jit(solution)/shard_map/all_gather | solution.py:167
  15.8 2.1 fusion.77
  18.0 0.2 multiply_reduce_fusion.1
  18.3 0.7 and_select_fusion
  19.0 0.7 select_reduce_fusion.3
  19.8 1.5 multiply_reduce_fusion.2
  21.2 0.3 multiply_cosine_fusion
  21.7 0.2 fusion.63
  22.3 0.5 broadcast_compare_fusion
  23.1 4.2 fusion
  27.3 0.3 fusion.79
  27.7 3.7 fusion.1
  31.5 4.0 fusion.29
  35.5 1.6 fusion.32
  37.1 1.3 convolution_convert_fusion
  38.8 4.5 %reduce-window.6 = s32[16,8,128]{2,1,0:T(8,128)S(1)} reduce-window(s32[16,8,128]{2,1,0:T(8,128)S(1)} %fusion.49, s32[]{:T(128)} %constant.28.clone.1), window={size=1x1x128 pad=0_0x0_0x127_0}, to_apply=%region_13.14 | reduce-window | flops 2080768 | bytes 131076 | tf_op jit(solution)/shard_map/reduce-window
  43.9 28.7 %all-reduce.2.cloned.1.call-done = bf16[128,2048]{1,0:T(8,128)(2,1)} async-done(((bf16[128,2048]{1,0:T(8,128)(2,1)}), bf16[128,2048]{1,0:T(8,128)(2,1)}) %all-reduce.2.cloned.1.call-update) | async-done | bytes 524304 | tf_op jit(solution)/shard_map/psum | solution.py:205
  72.6 2.2 convert_add_fusion
  74.8 1.3 multiply_convert_fusion
  76.1 10.4 %scatter_custom_fusion = bf16[1536,2048]{1,0:T(8,128)(2,1)} fusion(s32[1024]{0:T(1024)S(1)} %bitcast.158, bf16[]{:T(256)} %constant.80.clone.1, bf16[128,2048]{1,0:T(8,128)(2,1)S(1)} %multiply_convert_fusion), kind=kCustom, calls=%fused_computation.16 | custom fusion | bytes 6815746 | tf_op jit(solution)/shard_map/scatter | solution.py:126
  86.5 143.1 %all_to_all.10 = bf16[16,96,2048]{2,1,0:T(8,128)(2,1)S(1)} all-to-all(bf16[16,96,2048]{2,1,0:T(8,128)(2,1)} %bitcast.150), channel_id=1, replica_groups=mesh['req'=8,'tp'=4] {'req'}, dimensions={0} | all-to-all | bytes 12582912 | tf_op jit(solution)/shard_map/all_to_all | solution.py:211
  229.7 2.7 copy-done.2
  232.3 3.0 fusion.7
  235.3 10.4 %convert_bitcast_fusion = bf16[8,2,96,2048]{3,2,0,1:T(8,128)(2,1)} fusion(bf16[2,192,2048]{2,1,0:T(8,128)(2,1)} %param.35, f32[2,8,96,192]{3,2,1,0:T(8,128)} %fusion.7, bf16[2,2048,192]{1,2,0:T(8,128)(2,1)} %param.34, bf16[8,2,96,2048]{3,2,1,0:T(8,128)(2,1)} %bitcast.152), kind=kOutput, calls=%fused_computation.11 | convolution fusion | flops 2420834304 | bytes 16908288 | tf_op jit(solution)/shard_map/sekf,efd->sekd/dot_general | solution.py:115
  245.7 6.6 %copy.81 = bf16[8,2,96,2048]{3,2,1,0:T(8,128)(2,1)} copy(bf16[8,2,96,2048]{3,2,0,1:T(8,128)(2,1)} %convert_bitcast_fusion) | data formatting | bytes 12582912 | tf_op jit(solution)/shard_map/convert_element_type | solution.py:117
  252.3 4.9 %all-to-all-start.1 = ((bf16[16,96,2048]{2,1,0:T(8,128)(2,1)}), bf16[16,96,2048]{2,1,0:T(8,128)(2,1)}, u32[]{:S(2)}, u32[]{:S(2)}) async-start(bf16[16,96,2048]{2,1,0:T(8,128)(2,1)} %bitcast.149), calls=%async_computation.1 | async-start | bytes 12582912 | tf_op jit(solution)/shard_map/all_to_all | solution.py:216
  257.2 0.3 reduce-scatter.2.cloned.1.call-start
  257.6 136.6 %all-to-all-done.1 = bf16[16,96,2048]{2,1,0:T(8,128)(2,1)} async-done(((bf16[16,96,2048]{2,1,0:T(8,128)(2,1)}), bf16[16,96,2048]{2,1,0:T(8,128)(2,1)}, u32[]{:S(2)}, u32[]{:S(2)}) %all-to-all-start.1) | async-done | bytes 6291488 | tf_op jit(solution)/shard_map/all_to_all | solution.py:216
  394.2 12.6 %gather_fusion = bf16[1024,2048]{1,0:T(8,128)(2,1)} fusion(bf16[1536,2048]{1,0:T(8,128)(2,1)} %bitcast.38, s32[1024]{0:T(1024)S(1)} %broadcast_clamp_fusion), kind=kCustom, calls=%fused_computation | custom fusion | bytes 8392704 | tf_op jit(solution)/shard_map/gather | solution.py:133
  406.8 7.4 %fusion.2 = bf16[128,2048]{1,0:T(8,128)(2,1)} fusion(bf16[1024,2048]{1,0:T(8,128)(2,1)} %gather_fusion, f32[128,8]{1,0:T(8,128)S(1)} %copy.82), kind=kLoop, calls=%fused_computation.8 | loop fusion | flops 6029312 | bytes 4722688 | tf_op jit(solution)/shard_map/reduce_sum | solution.py:137
  414.2 19.9 %reduce-scatter.2.cloned.1.call-done = bf16[128,512]{1,0:T(8,128)(2,1)} async-done(((bf16[128,2048]{1,0:T(8,128)(2,1)}), bf16[128,512]{1,0:T(8,128)(2,1)}) %reduce-scatter.2.cloned.1.call-update) | async-done | bytes 131088 | tf_op jit(solution)/shard_map/reduce_scatter | solution.py:218
  434.1 1.7 add_convert_fusion
  (67 shorter events, 2.4 us)
Async XLA Ops:
  6.5 30.6 %copy-start = (bf16[512,2048]{1,0:T(8,128)(2,1)S(1)}, bf16[512,2048]{1,0:T(8,128)(2,1)}, u32[]{:S(2)}) copy-start(bf16[512,2048]{1,0:T(8,128)(2,1)} %param.25) | copy-start | bytes 6291460
  6.5 15.5 %copy-start.10 = (s32[9]{0:T(128)S(1)}, s32[9]{0:T(128)}, u32[]{:S(2)}) copy-start(s32[9]{0:T(128)} %param.29) | copy-start | bytes 112
  6.5 15.0 %copy-start.8 = (f32[128]{0:T(128)S(1)}, f32[128]{0:T(128)}, u32[]{:S(2)}) copy-start(f32[128]{0:T(128)} %param.24) | copy-start | bytes 1540
  6.5 15.5 %copy-start.6 = (s32[9,32]{1,0:T(8,128)S(1)}, s32[9,32]{1,0:T(8,128)}, u32[]{:S(2)}) copy-start(s32[9,32]{1,0:T(8,128)} %param.28) | copy-start | bytes 3460
  6.5 16.3 %copy-start.9 = (f32[128]{0:T(128)S(1)}, f32[128]{0:T(128)}, u32[]{:S(2)}) copy-start(f32[128]{0:T(128)} %param.23) | copy-start | bytes 1540
  6.5 66.1 %all-reduce.2.cloned.1.call-start = ((), (), s32[]{:S(2)}) async-start(), calls=%async_computation.3 | async-start | bytes 1048576 | tf_op jit(solution)/shard_map/psum | solution.py:205
  27.7 3.8 copy-start.11
  31.5 4.0 copy-start.4
  31.5 7.0 %copy-start.3 = (s32[128,8]{0,1:T(8,128)S(1)}, s32[128,8]{0,1:T(8,128)}, u32[]{:S(2)}) copy-start(s32[128,8]{0,1:T(8,128)} %param.31) | copy-start | bytes 12292
  35.5 39.3 %copy-start.5 = (f32[2048]{0:T(1024)S(1)}, f32[2048]{0:T(1024)}, u32[]{:S(2)}) copy-start(f32[2048]{0:T(1024)} %param.30) | copy-start | bytes 24580
  86.5 145.8 %copy-start.12 = (bf16[2,2048,192]{1,2,0:T(8,128)(2,1)S(1)}, bf16[2,2048,192]{1,2,0:T(8,128)(2,1)}, u32[]{:S(2)}) copy-start(bf16[2,2048,192]{1,2,0:T(8,128)(2,1)} %param.33) | copy-start | bytes 4718596
  229.7 2.7 copy-start.2
  252.3 5.2 %copy-start.7 = (f32[128,8]{0,1:T(8,128)S(1)}, f32[128,8]{0,1:T(8,128)}, u32[]{:S(2)}) copy-start(f32[128,8]{0,1:T(8,128)} %param.32) | copy-start | bytes 12292
  252.3 141.9 %all-to-all-start.1 = ((bf16[16,96,2048]{2,1,0:T(8,128)(2,1)}), bf16[16,96,2048]{2,1,0:T(8,128)(2,1)}, u32[]{:S(2)}, u32[]{:S(2)}) async-start(bf16[16,96,2048]{2,1,0:T(8,128)(2,1)} %bitcast.149), calls=%async_computation.1 | async-start | bytes 12582912 | tf_op jit(solution)/shard_map/all_to_all | solution.py:216
  257.2 176.9 %reduce-scatter.2.cloned.1.call-start = ((), (), s32[]{:S(2)}) async-start(), calls=%async_computation.4 | async-start | bytes 655360 | tf_op jit(solution)/shard_map/reduce_scatter | solution.py:218
  394.2 41.6 %copy-start.1 = (bf16[512,2048]{1,0:T(8,128)(2,1)S(1)}, bf16[512,2048]{1,0:T(8,128)(2,1)}, u32[]{:S(2)}) copy-start(bf16[512,2048]{1,0:T(8,128)(2,1)} %param.25) | copy-start | bytes 6291460
Sparse Core Ops, SparseCore 0:
  38.6 34.0 all-reduce.1
  414.3 19.7 reduce-scatter.1
where the time goes:
time: 443 us
  waiting for transfers between devices  185 us (42%)
  blocking collectives  152 us (34%)
  local copies, waits for them, and re-layouts  33.3 us (8%)
  matrix products  28.3 us (6%)
  other arithmetic  24.7 us (6%)
  between operations  13.7 us (3%)
  starting transfers between devices  5.21 us (1%)
    all_to_all x1, blocking collectives, body(): lax.all_to_all(send_buffer, 'req', split_axis=0, concat_axis=0, tiled=True)  143 us
    all_to_all x1, waiting for transfers between devices, body(): lax.all_to_all(part_sums, 'req', split_axis=0, concat_axis=0, tiled=True)  137 us
    psum x1, waiting for transfers between devices, body(): lax.psum(head_part.astype(jnp.bfloat16), 'tp').astype(jnp.float32)  28.7 us
    reduce_scatter x1, waiting for transfers between devices, body(): lax.psum_scatter(moe_term.astype(jnp.bfloat16), 'tp', scatter_dimension=1...  19.9 us
    gather x1, local copies, waits for them, and re-layouts, weigh_back(): returned.reshape(returned.shape[0] * returned.shape[1], row_width)  12.6 us
    scatter x1, local copies, waits for them, and re-layouts, build_buffer(): buffer_rows = jnp.zeros((expert_count * capacity, normed.shape[1]), norme...  10.4 us
    dot_general x1, matrix products, expert_apply(): jnp.einsum('sekf,efd->sekd', hidden_act, down_weight, preferred_element_t...  10.4 us
    all_gather x1, blocking collectives, body(): x_full = lax.all_gather(hidden_in, 'tp', axis=1, tiled=True)  8.99 us
  transfers between devices with their start and end apart: 3, of which 3 were waited for; matrix products, arithmetic and copies ran while one was open for 1% of the time, Pallas kernels for 0%

commit v1 on v0

--- a/solution.py
+++ b/solution.py
@@ -135,6 +135,96 @@
         back_rows.astype(jnp.float32) * route_weights.reshape(token_count * top_count)[:, None]
     )
     return jnp.sum(weighted.reshape(token_count, top_count, row_width), axis=1)
+
+
+def experts_dense(rows, routes, gate_weight, up_weight, down_weight):
+    gate_acts = jnp.einsum("td,edf->tef", rows, gate_weight, preferred_element_type=jnp.float32)
+    up_acts = jnp.einsum("td,edf->tef", rows, up_weight, preferred_element_type=jnp.float32)
+    hidden_act = (jax.nn.silu(gate_acts) * up_acts * routes[:, :, None]).astype(jnp.bfloat16)
+    return jnp.einsum("tef,efd->td", hidden_act, down_weight, preferred_element_type=jnp.float32)
+
+
+def moe_dense(
+    x_float,
+    head_part,
+    norm_post_gain,
+    expert_ids,
+    route_weights,
+    gate_weight,
+    up_weight,
+    down_weight,
+):
+    req_count = lax.axis_size("req")
+    tp_index = lax.axis_index("tp")
+    token_count = x_float.shape[0]
+    tp_count = lax.axis_size("tp")
+    share_width = x_float.shape[1] // tp_count
+    expert_local = gate_weight.shape[0]
+    expert_count = expert_local * req_count
+    share_rows = token_count // tp_count
+    named = expert_ids[:, :, None] == jnp.arange(expert_count, dtype=jnp.int32)[None, None, :]
+    group_routes = jnp.sum(jnp.where(named, route_weights[:, :, None], 0.0), axis=1)
+    routes = lax.all_gather(group_routes, "req", axis=0, tiled=True)
+    routes = lax.dynamic_slice_in_dim(
+        routes, lax.axis_index("req") * expert_local, expert_local, 1
+    )
+    head_sum = lax.psum_scatter(
+        head_part.astype(jnp.bfloat16), "tp", scatter_dimension=0, tiled=True
+    ).astype(jnp.float32)
+    residual = lax.dynamic_slice_in_dim(x_float, tp_index * share_rows, share_rows, 0) + head_sum
+    normed_post = rms_scale(residual, norm_post_gain).astype(jnp.bfloat16)
+    rows = lax.all_gather(normed_post, ("req", "tp"), axis=0, tiled=True)
+    part_sums = experts_dense(rows, routes, gate_weight, up_weight, down_weight)
+    own_rows = (lax.axis_index("req") * tp_count + tp_index) * share_rows
+    own = lax.dynamic_slice_in_dim(part_sums, own_rows, share_rows, 0)
+    part_sums = lax.dynamic_update_slice_in_dim(part_sums, own + residual, own_rows, 0)
+    blocks = part_sums.astype(jnp.bfloat16).reshape(req_count, token_count, tp_count, share_width)
+    blocks = blocks.transpose(0, 2, 1, 3).reshape(
+        req_count * tp_count * token_count, share_width
+    )
+    return lax.psum_scatter(blocks, ("req", "tp"), scatter_dimension=0, tiled=True)
+
+
+def moe_routed(
+    x_float,
+    head_part,
+    norm_post_gain,
+    expert_ids,
+    route_weights,
+    gate_weight,
+    up_weight,
+    down_weight,
+):
+    req_count = lax.axis_size("req")
+    tp_index = lax.axis_index("tp")
+    token_count = x_float.shape[0]
+    share_width = x_float.shape[1] // lax.axis_size("tp")
+    top_count = expert_ids.shape[1]
+    expert_count = gate_weight.shape[0] * req_count
+    capacity = max(2, 3 * token_count * top_count // (2 * expert_count))
+    flat_expert = expert_ids.reshape(token_count * top_count)
+    one_hot = (flat_expert[:, None] == jnp.arange(expert_count, dtype=jnp.int32)[None, :]).astype(
+        jnp.int32
+    )
+    slot_rank = jnp.sum((jnp.cumsum(one_hot, axis=0) - one_hot) * one_hot, axis=1)
+    slot_index = flat_expert * capacity + slot_rank
+    head_sum = lax.psum(head_part.astype(jnp.bfloat16), "tp").astype(jnp.float32)
+    residual_full = x_float + head_sum
+    normed_post = rms_scale(residual_full, norm_post_gain).astype(jnp.bfloat16)
+    residual = lax.dynamic_slice_in_dim(residual_full, tp_index * share_width, share_width, 1)
+    send_buffer = build_buffer(normed_post, slot_index, top_count, expert_count, capacity)
+    part_sums = expert_apply(
+        lax.all_to_all(send_buffer, "req", split_axis=0, concat_axis=0, tiled=True),
+        gate_weight,
+        up_weight,
+        down_weight,
+    )
+    returned = lax.all_to_all(part_sums, "req", split_axis=0, concat_axis=0, tiled=True)
+    moe_term = weigh_back(returned, slot_index, route_weights, token_count, top_count)
+    moe_share = lax.psum_scatter(
+        moe_term.astype(jnp.bfloat16), "tp", scatter_dimension=1, tiled=True
+    ).astype(jnp.float32)
+    return (residual + moe_share).astype(jnp.bfloat16)
 
 
 def body(
@@ -158,8 +248,6 @@
     down_weight,
 ):
     req_count = lax.axis_size("req")
-    tp_index = lax.axis_index("tp")
-    share_width = hidden_in.shape[1]
     head_dim = q_gain.shape[0]
     kv_local = key_pages.shape[0]
     group_size = q_weight.shape[1] // head_dim // kv_local
@@ -193,32 +281,18 @@
         queries, keys_new, values_new, keys_cache, values_cache, requests, positions, slot_owner
     )
     head_part = jnp.dot(attended, o_weight, preferred_element_type=jnp.float32)
-    top_count = expert_ids.shape[1]
     expert_count = gate_weight.shape[0] * req_count
-    capacity = max(2, 3 * token_count * top_count // (2 * expert_count))
-    flat_expert = expert_ids.reshape(token_count * top_count)
-    one_hot = (flat_expert[:, None] == jnp.arange(expert_count, dtype=jnp.int32)[None, :]).astype(
-        jnp.int32
-    )
-    slot_rank = jnp.sum((jnp.cumsum(one_hot, axis=0) - one_hot) * one_hot, axis=1)
-    slot_index = flat_expert * capacity + slot_rank
-    head_sum = lax.psum(head_part.astype(jnp.bfloat16), "tp").astype(jnp.float32)
-    residual_full = x_float + head_sum
-    normed_post = rms_scale(residual_full, norm_post_gain).astype(jnp.bfloat16)
-    residual = lax.dynamic_slice_in_dim(residual_full, tp_index * share_width, share_width, 1)
-    send_buffer = build_buffer(normed_post, slot_index, top_count, expert_count, capacity)
-    part_sums = expert_apply(
-        lax.all_to_all(send_buffer, "req", split_axis=0, concat_axis=0, tiled=True),
+    moe_layer = moe_dense if expert_count <= 2 * expert_ids.shape[1] else moe_routed
+    return moe_layer(
+        x_float,
+        head_part,
+        norm_post_gain,
+        expert_ids,
+        route_weights,
         gate_weight,
         up_weight,
         down_weight,
     )
-    returned = lax.all_to_all(part_sums, "req", split_axis=0, concat_axis=0, tiled=True)
-    moe_term = weigh_back(returned, slot_index, route_weights, token_count, top_count)
-    moe_share = lax.psum_scatter(
-        moe_term.astype(jnp.bfloat16), "tp", scatter_dimension=1, tiled=True
-    ).astype(jnp.float32)
-    return (residual + moe_share).astype(jnp.bfloat16)
 
 
 def solution(mesh):

time: 443 us -> 300 us (0.68)
  blocking collectives: 152 us -> 39.6 us
  local copies, waits for them, and re-layouts: 33.3 us -> 13.3 us
  other arithmetic: 24.7 us -> 16.7 us
  waiting for transfers between devices: 185 us -> 193 us
  starting transfers between devices: 5.21 us -> 0.09 us
  matrix products: 28.3 us -> 23.6 us
    all_to_all x1 -> x0, blocking collectives: 143 us -> none  [body(): lax.all_to_all(send_buffer, 'req', split_axis=0, concat_axis=0, tiled=True)]
    reduce_scatter x1 -> x2, waiting for transfers between devices: 19.9 us -> 161 us  [the longest x1 139 us: moe_dense(): lax.psum_scatter(blocks, ('req', 'tp'), scatter_dimension=0, tiled=True)]
    all_to_all x1 -> x0, waiting for transfers between devices: 137 us -> none  [body(): lax.all_to_all(part_sums, 'req', split_axis=0, concat_axis=0, tiled=True)]
    all_gather x0 -> x1, waiting for transfers between devices: none -> 31.7 us  [moe_dense(): rows = lax.all_gather(normed_post, ('req', 'tp'), axis=0, tiled=True)]
    all_gather x0 -> x1, blocking collectives: none -> 30.8 us  [moe_dense(): routes = lax.all_gather(group_routes, 'req', axis=0, tiled=True)]
    psum x1 -> x0, waiting for transfers between devices: 28.7 us -> none  [body(): lax.psum(head_part.astype(jnp.bfloat16), 'tp').astype(jnp.float32)]
    gather x1 -> x0, local copies, waits for them, and re-layouts: 12.6 us -> none  [weigh_back(): returned.reshape(returned.shape[0] * returned.shape[1], row_width)]
    dot_general x2 -> x1, matrix products: 13.4 us -> 2.46 us  [experts_dense(): jnp.einsum('tef,efd->td', hidden_act, down_weight, preferred_element_type...]
  transfers between devices with their start and end apart: 3 -> 3, of which waited for: 3 -> 3; matrix products, arithmetic and copies ran while one was open for 1% -> 0% of each run, Pallas kernels for 0% -> 0%
where the time goes in v1:
time: 300 us; the launch traced here: 299 us
  waiting for transfers between devices  193 us (64%)
  blocking collectives  39.6 us (13%)
  matrix products  23.6 us (8%)
  other arithmetic  16.7 us (6%)
  between operations  13.5 us (4%)
  local copies, waits for them, and re-layouts  13.3 us (4%)
    reduce_scatter x1, waiting for transfers between devices, moe_dense(): lax.psum_scatter(blocks, ('req', 'tp'), scatter_dimension=0, tiled=True)  139 us
    all_gather x1, waiting for transfers between devices, moe_dense(): rows = lax.all_gather(normed_post, ('req', 'tp'), axis=0, tiled=True)  31.7 us
    all_gather x1, blocking collectives, moe_dense(): routes = lax.all_gather(group_routes, 'req', axis=0, tiled=True)  30.8 us
    reduce_scatter x1, waiting for transfers between devices, moe_dense(): lax.psum_scatter(head_part.astype(jnp.bfloat16), 'tp', scatter_dimension=...  21.5 us
    all_gather x1, blocking collectives, body(): x_full = lax.all_gather(hidden_in, 'tp', axis=1, tiled=True)  8.86 us
    reshape x1, local copies, waits for them, and re-layouts, moe_dense(): part_sums.astype(jnp.bfloat16)  7.82 us
    unnamed x2, matrix products  6.46 us
  transfers between devices with their start and end apart: 3, of which 3 were waited for; matrix products, arithmetic and copies ran while one was open for 0% of the time, Pallas kernels for 0%

profile of v1, /device:TPU:0, one launch (start us, length us, event | category | flops | bytes accessed | tf_op | source)
XLA Modules:
  0.0 299.5 jit_solution(7539480927932623906)
XLA Ops:
  6.6 0.8 and_select_fusion
  7.4 0.7 select_reduce_fusion.4
  8.2 0.9 convert_reduce_fusion
  9.2 8.9 %all_gather.9 = bf16[128,2048]{1,0:T(8,128)(2,1)S(1)} all-gather(bf16[128,512]{1,0:T(8,128)(2,1)} %param.18), channel_id=1, replica_groups=mesh['req'=8,'tp'=4] {'tp'}, dimensions={1}, use_global_device_ids=true | all-gather | bytes 655360 | tf_op jit(solution)/shard_map/all_gather | solution.py:255
  18.1 0.2 multiply_reduce_fusion
  18.3 1.5 multiply_reduce_fusion.3
  19.8 0.3 multiply_cosine_fusion
  20.1 0.7 multiply_bitcast_fusion
  20.8 0.2 fusion.33
  21.0 2.1 fusion.44
  23.2 0.2 multiply_reduce_fusion.2
  23.6 0.5 broadcast_compare_fusion
  24.4 4.0 %fusion = (f32[4,128]{1,0:T(4,128)S(1)}, f32[128,4,6144]{2,0,1:T(8,128)S(1)}) fusion(pred[128,6144]{1,0:T(8,128)(4,1)S(1)} %broadcast_compare_fusion, bf16[6144,128,1]{1,0,2:T(8,128)(2,1)} %bitcast.96, bf16[128,4,64]{2,0,1:T(8,128)(2,1)S(1)} %get-tuple-element.10, bf16[128,4,64]{2,0,1:T(8,128)(2,1)S(1)} %get-tuple-element.9), kind=kOutput, calls=%fused_computation.3 | convolution fusion | flops 815005184 | bytes 15075328 | tf_op jit(solution)/shard_map/tkgh,knh->kgtn/dot_general | solution.py:79
  28.4 0.3 fusion.45
  28.8 3.7 %fusion.1 = f32[4,128]{1,0:T(4,128)S(1)} fusion(f32[128,4,6144]{2,0,1:T(8,128)S(1)} %get-tuple-element.18, f32[4,128]{1,0:T(4,128)S(1)} %max.8, pred[128,6144]{1,0:T(8,128)(4,1)S(1)} %broadcast_compare_fusion), kind=kLoop, calls=%fused_computation.4 | loop fusion | flops 15728128 | bytes 13373440 | tf_op jit(solution)/shard_map/reduce_sum | solution.py:93
  32.6 4.0 %fusion.5 = f32[128,4,128]{2,0,1:T(8,128)S(1)} fusion(bf16[6144,128,1]{1,0,2:T(8,128)(2,1)S(1)} %bitcast.98, f32[4,128]{1,0:T(4,128)S(1)} %add.164, f32[4,128]{1,0:T(4,128)S(1)} %max.8, f32[128,4,6144]{2,0,1:T(8,128)S(1)} %get-tuple-element.18, pred[128,6144]{1,0:T(8,128)(4,1)S(1)} %broadcast_compare_fusion), kind=kOutput, calls=%fused_computation.14 | convolution fusion | flops 824180736 | bytes 15208448 | tf_op jit(solution)/shard_map/kgtn,knh->tkgh/dot_general | solution.py:96
  36.6 1.6 fusion.8
  38.3 1.3 convolution_convert_fusion
  39.6 1.1 convert_element_type.59
  40.7 21.5 %reduce-scatter.3.cloned.1.call-done = bf16[32,2048]{1,0:T(8,128)(2,1)} async-done(((bf16[128,2048]{1,0:T(8,128)(2,1)}), bf16[32,2048]{1,0:T(8,128)(2,1)}) %reduce-scatter.3.cloned.1.call-update) | async-done | bytes 131088 | tf_op jit(solution)/shard_map/reduce_scatter | solution.py:171
  62.2 1.2 multiply_reduce_fusion.1
  63.4 1.8 multiply_convert_fusion.3
  65.3 30.8 %all_gather.11 = f32[1024,16]{0,1:T(8,128)S(1)} all-gather(f32[128,16]{0,1:T(8,128)S(1)} %select_reduce_fusion.3), channel_id=1, replica_groups=mesh['req'=8,'tp'=4] {'req'}, dimensions={0}, use_global_device_ids=true | all-gather | bytes 73728 | tf_op jit(solution)/shard_map/all_gather | solution.py:167
  96.1 31.7 %all-gather.2.cloned.1.call-done = bf16[1024,2048]{1,0:T(8,128)(2,1)} async-done(((bf16[32,2048]{1,0:T(8,128)(2,1)}), bf16[1024,2048]{1,0:T(8,128)(2,1)}) %all-gather.2.cloned.1.call-update) | async-done | bytes 4194320 | tf_op jit(solution)/shard_map/all_gather | solution.py:176
  127.7 4.6 %fusion.47 = f32[1024,384]{0,1:S(1)} fusion(bf16[1024,2048]{1,0:T(8,128)(2,1)} %all-gather.2.cloned.1.call-done, bf16[2048,384]{0,1:T(8,128)(2,1)} %bitcast.99), kind=kOutput, calls=%fused_computation.103 | convolution fusion | flops 1610612736 | bytes 7340032
  132.4 1.8 fusion.46
  134.2 2.5 convolution_bitcast_fusion
  136.7 1.0 add_dynamic-update-slice_fusion
  137.8 2.6 convert_element_type.73
  140.4 7.8 %reshape.452 = bf16[8,128,4,512]{3,2,1,0:T(4,128)(2,1)} reshape(bf16[1024,2048]{1,0:T(8,128)(2,1)} %convert_element_type.73) | data formatting | bytes 8388608 | tf_op jit(solution)/shard_map/reshape | solution.py:181
  148.2 5.3 %copy.47 = bf16[8,4,128,512]{3,2,1,0:T(8,128)(2,1)} copy(bf16[8,4,128,512]{3,1,2,0:T(4,128)(2,1)} %bitcast.95) | data formatting | bytes 8388608 | tf_op jit(solution)/shard_map/transpose | solution.py:182
  153.5 139.5 %reduce-scatter.5.cloned.1.call-done = bf16[128,512]{1,0:T(8,128)(2,1)} async-done(((bf16[4096,512]{1,0:T(8,128)(2,1)}), bf16[128,512]{1,0:T(8,128)(2,1)}) %reduce-scatter.5.cloned.1.call-update) | async-done | bytes 131088 | tf_op jit(solution)/shard_map/reduce_scatter | solution.py:185
  (49 shorter events, 1.1 us)
Async XLA Ops:
  6.5 31.7 %copy-start = (bf16[512,2048]{1,0:T(8,128)(2,1)S(1)}, bf16[512,2048]{1,0:T(8,128)(2,1)}, u32[]{:S(2)}) copy-start(bf16[512,2048]{1,0:T(8,128)(2,1)} %param.25) | copy-start | bytes 6291460
  6.5 55.6 %reduce-scatter.3.cloned.1.call-start = ((), (), s32[]{:S(2)}) async-start(), calls=%async_computation.2 | async-start | bytes 655360 | tf_op jit(solution)/shard_map/reduce_scatter | solution.py:171
  18.2 5.9 %copy-start.6 = (f32[128]{0:T(128)S(1)}, f32[128]{0:T(128)}, u32[]{:S(2)}) copy-start(f32[128]{0:T(128)} %param.23) | copy-start | bytes 1540
  28.8 3.8 %copy-start.8 = (bf16[1,48,128,128]{3,2,1,0:T(8,128)(2,1)S(1)}, bf16[1,48,128,128]{3,2,1,0:T(8,128)(2,1)}, u32[]{:S(2)}) copy-start(bf16[1,48,128,128]{3,2,1,0:T(8,128)(2,1)} %param.27) | copy-start | bytes 4718596
  32.6 4.0 %copy-start.2 = (f32[2048]{0:T(1024)S(1)}, f32[2048]{0:T(1024)}, u32[]{:S(2)}) copy-start(f32[2048]{0:T(1024)} %param.19) | copy-start | bytes 24580
  38.2 25.1 %copy-start.3 = (f32[2048]{0:T(1024)S(1)}, f32[2048]{0:T(1024)}, u32[]{:S(2)}) copy-start(f32[2048]{0:T(1024)} %param.30) | copy-start | bytes 24580
  38.2 27.0 %copy-start.4 = (f32[128,8]{0,1:T(8,128)S(1)}, f32[128,8]{0,1:T(8,128)}, u32[]{:S(2)}) copy-start(f32[128,8]{0,1:T(8,128)} %param.32) | copy-start | bytes 12292
  38.2 27.0 %copy-start.5 = (s32[128,8]{0,1:T(8,128)S(1)}, s32[128,8]{0,1:T(8,128)}, u32[]{:S(2)}) copy-start(s32[128,8]{0,1:T(8,128)} %param.31) | copy-start | bytes 12292
  39.5 88.2 %all-gather.2.cloned.1.call-start = ((), (), s32[]{:S(2)}) async-start(), calls=%async_computation.3 | async-start | bytes 4325376 | tf_op jit(solution)/shard_map/all_gather | solution.py:176
  65.2 227.8 %reduce-scatter.5.cloned.1.call-start = ((), (), s32[]{:S(2)}) async-start(), calls=%async_computation.4 | async-start | bytes 4325376 | tf_op jit(solution)/shard_map/reduce_scatter | solution.py:185
  127.7 4.6 %copy-start.7 = (bf16[1024,2048]{1,0:T(8,128)(2,1)S(1)}, bf16[1024,2048]{1,0:T(8,128)(2,1)}, u32[]{:S(2)}) copy-start(bf16[1024,2048]{1,0:T(8,128)(2,1)} %all-gather.2.cloned.1.call-done) | copy-start | bytes 12582916
  127.7 4.7 %copy-start.9 = (bf16[2,2048,192]{1,2,0:T(8,128)(2,1)S(1)}, bf16[2,2048,192]{1,2,0:T(8,128)(2,1)}, u32[]{:S(2)}) copy-start(bf16[2,2048,192]{1,2,0:T(8,128)(2,1)} %param.33) | copy-start | bytes 4718596
  132.4 1.9 copy-start.10
  134.2 2.5 copy-start.1
Sparse Core Ops, SparseCore 0:
  39.7 22.4 reduce-scatter.2
  65.5 62.1 all-gather.1
  153.6 139.2 reduce-scatter.4

commit v2 on v1

--- a/solution.py
+++ b/solution.py
@@ -3,6 +3,8 @@
 import jax
 import jax.numpy as jnp
 from jax import lax
+from jax.experimental import pallas as pl
+from jax.experimental.pallas import tpu as pltpu
 from jax.sharding import PartitionSpec as P
 
 PAGE = 128
@@ -137,15 +139,162 @@
     return jnp.sum(weighted.reshape(token_count, top_count, row_width), axis=1)
 
 
-def experts_dense(rows, routes, gate_weight, up_weight, down_weight):
-    gate_acts = jnp.einsum("td,edf->tef", rows, gate_weight, preferred_element_type=jnp.float32)
-    up_acts = jnp.einsum("td,edf->tef", rows, up_weight, preferred_element_type=jnp.float32)
-    hidden_act = (jax.nn.silu(gate_acts) * up_acts * routes[:, :, None]).astype(jnp.bfloat16)
-    return jnp.einsum("tef,efd->td", hidden_act, down_weight, preferred_element_type=jnp.float32)
+LANES = 128
+VMEM = pl.BlockSpec(memory_space=pltpu.VMEM)
+SMEM = pl.BlockSpec(memory_space=pltpu.SMEM)
+VMEM_LIMIT = 48 * 1024 * 1024
+
+
+def flip(value, axis, bits):
+    return lax.ppermute(value, axis, [(i, i ^ bits) for i in range(lax.axis_size(axis))])
+
+
+def pack_kernel(
+    place_ref, own_ref, near_ref, far_ref, cross_ref, x_ref, gain_ref, ids_ref, routes_ref,
+    rows_ref, keep_ref, near_out, far_out, cross_out, residual_ref,
+):
+    tp_index = place_ref[1]
+    share_rows, width = own_ref.shape
+    share_width = keep_ref.shape[1]
+    mine = pl.ds(pl.multiple_of(tp_index * share_rows, share_rows), share_rows)
+    head_sum = (own_ref[...] + near_ref[...].astype(jnp.float32)) + (
+        far_ref[...].astype(jnp.float32) + cross_ref[...].astype(jnp.float32)
+    )
+    residual = x_ref[mine, :].astype(jnp.float32) + head_sum
+    residual_ref[...] = residual
+    rows_ref[:, :width] = rms_scale(residual, gain_ref[...]).astype(jnp.bfloat16)
+    ids = ids_ref[mine, :]
+    weights = routes_ref[mine, :]
+    lane = lax.broadcasted_iota(jnp.int32, (share_rows, LANES), 1)
+    spread = jnp.zeros((share_rows, LANES), jnp.float32)
+    for k in range(ids.shape[1]):
+        spread = spread + jnp.where(lane % (LANES // 2) == ids[:, k : k + 1], weights[:, k : k + 1], 0.0)
+    high = spread.astype(jnp.bfloat16).astype(jnp.float32)
+    rows_ref[:, width:] = jnp.where(lane < LANES // 2, high, spread - high).astype(jnp.bfloat16)
+    for step, out_ref in enumerate((keep_ref, near_out, far_out, cross_out)):
+        column = pl.multiple_of((tp_index ^ step) * share_width, share_width)
+        out_ref[...] = residual_ref[:, pl.ds(column, share_width)]
+
+
+def experts_kernel(place_ref, rows_ref, gate_up_ref, down_ref, send_ref, keep_ref):
+    req_index, tp_index = place_ref[0], place_ref[1]
+    width, doubled = gate_up_ref.shape
+    units = doubled // 2
+    half_rows, share_width = keep_ref.shape[3], keep_ref.shape[4]
+    acts = jnp.dot(rows_ref[:, :width], gate_up_ref[...], preferred_element_type=jnp.float32)
+    gate_acts, up_acts = acts[:, :units], acts[:, units:]
+    spread = rows_ref[:, width:].astype(jnp.float32)
+    lane = lax.broadcasted_iota(jnp.int32, spread.shape, 1) % (LANES // 2)
+    weights = [
+        jnp.sum(jnp.where(lane == 2 * req_index + e, spread, 0.0), axis=1, keepdims=True)
+        for e in range(2)
+    ]
+    unit = lax.broadcasted_iota(jnp.int32, gate_acts.shape, 1)
+    weight = jnp.where(unit < units // 2, weights[0], weights[1])
+    hidden_act = (gate_acts / (1.0 + jnp.exp(-gate_acts)) * up_acts * weight).astype(jnp.bfloat16)
+    for step in range(4):
+        column = pl.multiple_of((tp_index ^ step) * share_width, share_width)
+        part = jnp.dot(
+            hidden_act, down_ref[:, pl.ds(column, share_width)], preferred_element_type=jnp.float32
+        )
+        target = send_ref if step % 2 else keep_ref
+        for x in range(2):
+            target[step // 2, (req_index % 2) ^ x, 0] = part[
+                x * half_rows : (x + 1) * half_rows
+            ].astype(target.dtype)
+
+
+def finish_kernel(place_ref, total_ref, keep_ref, near_ref, far_ref, cross_ref, out_ref):
+    tp_index = place_ref[1]
+    share_rows = keep_ref.shape[0]
+    for step, part_ref in enumerate((keep_ref, near_ref, far_ref, cross_ref)):
+        rows = pl.ds(pl.multiple_of((tp_index ^ step) * share_rows, share_rows), share_rows)
+        out_ref[rows, :] = (total_ref[rows, :] + part_ref[...]).astype(jnp.bfloat16)
 
 
 def moe_dense(
-    x_float,
+    x_full,
+    head_part,
+    norm_post_gain,
+    expert_ids,
+    route_weights,
+    gate_weight,
+    up_weight,
+    down_weight,
+):
+    req_index, tp_index = lax.axis_index("req"), lax.axis_index("tp")
+    token_count, width = x_full.shape
+    share_rows, share_width = token_count // 4, width // 4
+    units = 2 * gate_weight.shape[2]
+    place = jnp.stack([req_index, tp_index]).astype(jnp.int32)
+
+    def head_rows(bits):
+        return lax.dynamic_slice_in_dim(head_part, (tp_index ^ bits) * share_rows, share_rows, 0)
+
+    received = [flip(head_rows(bits).astype(jnp.bfloat16), "tp", bits) for bits in (1, 2, 3)]
+    share_f32 = jax.ShapeDtypeStruct((share_rows, share_width), jnp.float32)
+    rows, *residuals = pl.pallas_call(
+        pack_kernel,
+        out_shape=[jax.ShapeDtypeStruct((share_rows, width + LANES), jnp.bfloat16)] + [share_f32] * 4,
+        in_specs=[SMEM] + [VMEM] * 8,
+        out_specs=[VMEM] * 5,
+        scratch_shapes=[pltpu.VMEM((share_rows, width), jnp.float32)],
+        name="pack_rows",
+    )(place, head_rows(0), *received, x_full, norm_post_gain[None, :], expert_ids, route_weights)
+    residuals = residuals[:1] + [flip(residuals[bits], "tp", bits) for bits in (1, 2, 3)]
+    all_rows = lax.all_gather(rows, ("req", "tp"), axis=0, tiled=True)
+    gate_up = jnp.concatenate([gate_weight[0], gate_weight[1], up_weight[0], up_weight[1]], axis=1)
+    block = (2, 2, 1, token_count, share_width)
+    parts = (2, 2, 4, token_count, share_width)
+    out_spec = pl.BlockSpec(block, lambda z: (0, 0, z, 0, 0))
+    send, keep = pl.pallas_call(
+        experts_kernel,
+        grid=(4,),
+        out_shape=[
+            jax.ShapeDtypeStruct(parts, jnp.bfloat16),
+            jax.ShapeDtypeStruct(parts, jnp.float32),
+        ],
+        in_specs=[
+            SMEM,
+            pl.BlockSpec((2 * token_count, width + LANES), lambda z: (z, 0)),
+            pl.BlockSpec((width, 2 * units), lambda z: (0, 0)),
+            pl.BlockSpec((units, width), lambda z: (0, 0)),
+        ],
+        out_specs=[out_spec, out_spec],
+        compiler_params=pltpu.CompilerParams(vmem_limit_bytes=VMEM_LIMIT),
+        name="experts",
+    )(place, all_rows, gate_up, down_weight.reshape(units, width))
+    half = token_count // 2
+    got = flip(send, "tp", 1)
+    low = keep[..., :half, :] + got[..., :half, :].astype(jnp.float32)
+    high = keep[..., half:, :] + got[..., half:, :].astype(jnp.float32)
+    got_low = flip(low[1].astype(jnp.bfloat16), "tp", 2)
+    got_high = flip(high[:, 1].astype(jnp.bfloat16), "req", 1)
+    low = low[0] + got_low.astype(jnp.float32)
+    high = high[:, 0] + got_high.astype(jnp.float32)
+    got_low = flip(low[1].astype(jnp.bfloat16), "req", 1)
+    got_high = flip(high[1].astype(jnp.bfloat16), "tp", 2)
+    low = low[0] + got_low.astype(jnp.float32)
+    high = high[0] + got_high.astype(jnp.float32)
+    both = jnp.concatenate([low, high], axis=1)
+
+    def level(bits):
+        return lax.dynamic_index_in_dim(both, (req_index // 2) ^ bits, 0, keepdims=False)
+
+    total = level(0)
+    for bits in (1, 2, 3):
+        total = total + flip(level(bits).astype(jnp.bfloat16), "req", 2 * bits).astype(jnp.float32)
+    return pl.pallas_call(
+        finish_kernel,
+        out_shape=jax.ShapeDtypeStruct((token_count, share_width), jnp.bfloat16),
+        in_specs=[SMEM] + [VMEM] * 5,
+        out_specs=VMEM,
+        name="finish",
+    )(place, total, *residuals)
+
+
+def moe_routed(
+    x_full,
     head_part,
     norm_post_gain,
     expert_ids,
@@ -156,47 +305,7 @@
 ):
     req_count = lax.axis_size("req")
     tp_index = lax.axis_index("tp")
-    token_count = x_float.shape[0]
-    tp_count = lax.axis_size("tp")
-    share_width = x_float.shape[1] // tp_count
-    expert_local = gate_weight.shape[0]
-    expert_count = expert_local * req_count
-    share_rows = token_count // tp_count
-    named = expert_ids[:, :, None] == jnp.arange(expert_count, dtype=jnp.int32)[None, None, :]
-    group_routes = jnp.sum(jnp.where(named, route_weights[:, :, None], 0.0), axis=1)
-    routes = lax.all_gather(group_routes, "req", axis=0, tiled=True)
-    routes = lax.dynamic_slice_in_dim(
-        routes, lax.axis_index("req") * expert_local, expert_local, 1
-    )
-    head_sum = lax.psum_scatter(
-        head_part.astype(jnp.bfloat16), "tp", scatter_dimension=0, tiled=True
-    ).astype(jnp.float32)
-    residual = lax.dynamic_slice_in_dim(x_float, tp_index * share_rows, share_rows, 0) + head_sum
-    normed_post = rms_scale(residual, norm_post_gain).astype(jnp.bfloat16)
-    rows = lax.all_gather(normed_post, ("req", "tp"), axis=0, tiled=True)
-    part_sums = experts_dense(rows, routes, gate_weight, up_weight, down_weight)
-    own_rows = (lax.axis_index("req") * tp_count + tp_index) * share_rows
-    own = lax.dynamic_slice_in_dim(part_sums, own_rows, share_rows, 0)
-    part_sums = lax.dynamic_update_slice_in_dim(part_sums, own + residual, own_rows, 0)
-    blocks = part_sums.astype(jnp.bfloat16).reshape(req_count, token_count, tp_count, share_width)
-    blocks = blocks.transpose(0, 2, 1, 3).reshape(
-        req_count * tp_count * token_count, share_width
-    )
-    return lax.psum_scatter(blocks, ("req", "tp"), scatter_dimension=0, tiled=True)
-
-
-def moe_routed(
-    x_float,
-    head_part,
-    norm_post_gain,
-    expert_ids,
-    route_weights,
-    gate_weight,
-    up_weight,
-    down_weight,
-):
-    req_count = lax.axis_size("req")
-    tp_index = lax.axis_index("tp")
+    x_float = x_full.astype(jnp.float32)
     token_count = x_float.shape[0]
     share_width = x_float.shape[1] // lax.axis_size("tp")
     top_count = expert_ids.shape[1]
@@ -282,9 +391,10 @@
     )
     head_part = jnp.dot(attended, o_weight, preferred_element_type=jnp.float32)
     expert_count = gate_weight.shape[0] * req_count
-    moe_layer = moe_dense if expert_count <= 2 * expert_ids.shape[1] else moe_routed
+    staged = (req_count, lax.axis_size("tp"), gate_weight.shape[0]) == (8, 4, 2)
+    moe_layer = moe_dense if staged and expert_count <= LANES // 2 else moe_routed
     return moe_layer(
-        x_float,
+        x_full,
         head_part,
         norm_post_gain,
         expert_ids,

time: 300 us -> 182 us (0.61)
  waiting for transfers between devices: 193 us -> 79.2 us
  blocking collectives: 39.6 us -> 8.99 us
  Pallas kernels: 0 us -> 16.2 us
  starting transfers between devices: 0.09 us -> 11.9 us
  matrix products: 23.6 us -> 13.3 us
  local copies, waits for them, and re-layouts: 13.3 us -> 20.2 us
    reduce_scatter x2 -> x0, waiting for transfers between devices: 161 us -> none  [the longest x1 139 us: moe_dense(): lax.psum_scatter(blocks, ('req', 'tp'), scatter_dimension=0, tiled=True)]
    ppermute x0 -> x14, waiting for transfers between devices: none -> 33 us  [flip(): lax.ppermute(value, axis, [(i, i ^ bits) for i in range(lax.axis_size(axi...]
    all_gather x1 -> x0, blocking collectives: 30.8 us -> none  [moe_dense(): routes = lax.all_gather(group_routes, 'req', axis=0, tiled=True)]
    pallas_call x0 -> x3, Pallas kernels: none -> 16.2 us  [the longest x1 12.1 us: moe_dense(): pl.pallas_call(experts_kernel, grid=(4,), out_shape=[jax.ShapeDtypeStruct...]
    all_gather x1, waiting for transfers between devices: 31.7 us -> 46.2 us  [moe_dense(): all_rows = lax.all_gather(rows, ('req', 'tp'), axis=0, tiled=True)]
    unnamed x22 -> x44, local copies, waits for them, and re-layouts: 0.06 us -> 12 us
    ppermute x0 -> x14, starting transfers between devices: none -> 11.9 us  [flip(): lax.ppermute(value, axis, [(i, i ^ bits) for i in range(lax.axis_size(axi...]
    reshape x1 -> x0, local copies, waits for them, and re-layouts: 7.82 us -> none  [moe_dense(): part_sums.astype(jnp.bfloat16)]
  transfers between devices with their start and end apart: 3 -> 15, of which waited for: 3 -> 9; matrix products, arithmetic and copies ran while one was open for 0% -> 14% of each run, Pallas kernels for 0% -> 0%
where the time goes in v2:
time: 182 us; the launch traced here: 181 us
  waiting for transfers between devices  79.2 us (44%)
  local copies, waits for them, and re-layouts  20.2 us (11%)
  other arithmetic  17.5 us (10%)
  Pallas kernels  16.2 us (9%)
  between operations  13.8 us (8%)
  matrix products  13.3 us (7%)
  starting transfers between devices  11.9 us (7%)
  blocking collectives  8.99 us (5%)
    all_gather x1, waiting for transfers between devices, moe_dense(): all_rows = lax.all_gather(rows, ('req', 'tp'), axis=0, tiled=True)  46.2 us
    ppermute x14, waiting for transfers between devices, flip(): lax.ppermute(value, axis, [(i, i ^ bits) for i in range(lax.axis_size(axi...  33 us
    pallas_call x1, Pallas kernels, moe_dense(): pl.pallas_call(experts_kernel, grid=(4,), out_shape=[jax.ShapeDtypeStruct...  12.1 us
    unnamed x44, local copies, waits for them, and re-layouts  12 us
    ppermute x14, starting transfers between devices, flip(): lax.ppermute(value, axis, [(i, i ^ bits) for i in range(lax.axis_size(axi...  11.9 us
    all_gather x1, blocking collectives, body(): x_full = lax.all_gather(hidden_in, 'tp', axis=1, tiled=True)  8.99 us
    dot_general x1, matrix products, attend(): jnp.einsum('kgtn,knh->tkgh', prob_cache, values_cache, preferred_element_...  4.7 us
    concatenate x1, other arithmetic, moe_dense(): jnp.concatenate([gate_weight[0], gate_weight[1], up_weight[0], up_weight[...  4.52 us
  transfers between devices with their start and end apart: 15, of which 9 were waited for; matrix products, arithmetic and copies ran while one was open for 14% of the time, Pallas kernels for 0%

profile of v2, /device:TPU:0, one launch (start us, length us, event | category | flops | bytes accessed | tf_op | source)
XLA Modules:
  0.0 181.0 jit_solution(13716325254989922821)
XLA Ops:
  6.6 9.0 %all_gather.6.x_ref = bf16[128,2048]{1,0:T(8,128)(2,1)S(1)} all-gather(bf16[128,512]{1,0:T(8,128)(2,1)} %param.18), channel_id=1, replica_groups=mesh['req'=8,'tp'=4] {'tp'}, dimensions={1}, use_global_device_ids=true | all-gather | bytes 655360 | tf_op jit(solution)/shard_map/all_gather | solution.py:364
  15.8 2.1 %fusion.69 = f32[128,512]{1,0:T(8,128)S(1)} fusion(bf16[2048,512]{1,0:T(8,128)(2,1)} %param.20, bf16[128,2048]{1,0:T(8,128)(2,1)S(1)} %all_gather.6.x_ref, f32[2048]{0:T(1024)} %param.19, f32[128]{0:T(128)S(1)} %add_rsqrt_fusion.2), kind=kOutput, calls=%fused_computation.135 | convolution fusion | flops 269484032 | bytes 2892288 | tf_op jit(solution)/shard_map/dot_general | solution.py:367
  18.4 1.6 multiply_reduce_fusion.1
  21.9 2.5 %fusion = (f32[4,128]{1,0:T(4,128)S(1)}, f32[128,4,6144]{2,0,1:T(8,128)S(1)}) fusion(pred[128,6144]{1,0:T(8,128)(4,1)S(1)} %broadcast_compare_fusion, bf16[6144,128,1]{1,0,2:T(8,128)(2,1)S(1)} %bitcast.130, bf16[128,4,64]{2,0,1:T(8,128)(2,1)S(1)} %get-tuple-element.36, bf16[128,4,64]{2,0,1:T(8,128)(2,1)S(1)} %get-tuple-element.35), kind=kOutput, calls=%fused_computation.3 | convolution fusion | flops 815005184 | bytes 15075328 | tf_op jit(solution)/shard_map/tkgh,knh->kgtn/dot_general | solution.py:81
  24.8 3.9 %fusion.1 = f32[4,128]{1,0:T(4,128)S(1)} fusion(f32[128,4,6144]{2,0,1:T(8,128)S(1)} %get-tuple-element.44, f32[4,128]{1,0:T(4,128)S(1)} %max.8, pred[128,6144]{1,0:T(8,128)(4,1)S(1)} %broadcast_compare_fusion), kind=kLoop, calls=%fused_computation.4 | loop fusion | flops 15728128 | bytes 13373440 | tf_op jit(solution)/shard_map/reduce_sum | solution.py:95
  28.8 4.7 %fusion.5 = f32[128,4,128]{2,0,1:T(8,128)} fusion(bf16[6144,128,1]{1,0,2:T(8,128)(2,1)S(1)} %bitcast.133, f32[4,128]{1,0:T(4,128)S(1)} %add.178, f32[4,128]{1,0:T(4,128)S(1)} %max.8, f32[128,4,6144]{2,0,1:T(8,128)S(1)} %get-tuple-element.44, pred[128,6144]{1,0:T(8,128)(4,1)S(1)} %broadcast_compare_fusion), kind=kOutput, calls=%fused_computation.24 | convolution fusion | flops 824180736 | bytes 15208448 | tf_op jit(solution)/shard_map/kgtn,knh->tkgh/dot_general | solution.py:98
  33.5 1.7 fusion.8
  41.2 2.2 %collective-permute-done.1.far_ref = bf16[32,2048]{1,0:T(8,128)(2,1)S(1)} collective-permute-done((bf16[32,2048]{1,0:T(8,128)(2,1)}, bf16[32,2048]{1,0:T(8,128)(2,1)S(1)}, u32[]{:S(2)}, u32[]{:S(2)}) %collective-permute-start.1) | collective-permute-done | bytes 131104 | tf_op jit(solution)/shard_map/ppermute | solution.py:149
  43.4 1.2 collective-permute-done.2.cross_ref
  45.3 2.3 %pack_rows.1 = (bf16[32,2176]{1,0:T(8,128)(2,1)}, f32[32,512]{1,0:T(8,128)}, f32[32,512]{1,0:T(8,128)}, f32[32,512]{1,0:T(8,128)}, f32[32,512]{1,0:T(8,128)}) custom-call(s32[2]{0:T(128)} %pad_add_fusion.place_ref, f32[32,2048]{1,0:T(8,128)} %constant_dynamic-slice_fusion.own_ref, bf16[32,2048]{1,0:T(8,128)(2,1)} %copy-done.8, bf16[32,2048]{1,0:T(8,128)(2,1)} %copy-done.9, ...), custom_call_target="tpu_custom_call" | custom-call | tf_op jit(solution)/shard_map/pack_rows/pallas_call | solution.py:236
  47.6 2.7 %fusion.71 = (bf16[1,2048,192]{1,2,0:T(8,128)(2,1)}, bf16[1,2048,192]{1,2,0:T(8,128)(2,1)}) fusion(bf16[2,2048,192]{1,2,0:T(8,128)(2,1)} %param.33), kind=kLoop, calls=%fused_computation.136 | loop fusion | bytes 3145728 | tf_op jit(solution)/shard_map/slice | solution.py:246
  50.3 1.4 copy.87
  51.7 2.2 %copy.88 = bf16[1,2048,192]{2,1,0:T(8,128)(2,1)} copy(bf16[1,2048,192]{1,2,0:T(8,128)(2,1)} %get-tuple-element.26) | data formatting | bytes 1572864
  54.0 2.7 %fusion.72 = (bf16[1,2048,192]{1,2,0:T(8,128)(2,1)}, bf16[1,2048,192]{1,2,0:T(8,128)(2,1)}) fusion(bf16[2,2048,192]{1,2,0:T(8,128)(2,1)} %param.34), kind=kLoop, calls=%fused_computation.137 | loop fusion | bytes 3145728 | tf_op jit(solution)/shard_map/slice | solution.py:246
  56.7 2.2 %copy.89 = bf16[1,2048,192]{2,1,0:T(8,128)(2,1)} copy(bf16[1,2048,192]{1,2,0:T(8,128)(2,1)} %get-tuple-element.27) | data formatting | bytes 1572864
  58.9 2.2 %copy.90 = bf16[1,2048,192]{2,1,0:T(8,128)(2,1)} copy(bf16[1,2048,192]{1,2,0:T(8,128)(2,1)} %get-tuple-element.28) | data formatting | bytes 1572864
  61.2 4.5 %pad_maximum_fusion.gate_up_ref = bf16[2048,768]{1,0:T(8,128)(2,1)} fusion(bf16[2048,192]{1,0:T(8,128)(2,1)} %bitcast.129, bf16[2048,192]{1,0:T(8,128)(2,1)} %bitcast.128, bf16[2048,192]{1,0:T(8,128)(2,1)} %bitcast.127, bf16[2048,192]{1,0:T(8,128)(2,1)S(1)} %bitcast.126), kind=kLoop, calls=%fused_computation.7 | loop fusion | flops 12582912 | bytes 6291456 | tf_op jit(solution)/shard_map/concatenate | solution.py:246
  65.7 46.2 %all-gather.2.cloned.1.call-done.rows_ref = bf16[1024,2176]{1,0:T(8,128)(2,1)} async-done(((bf16[32,2176]{1,0:T(8,128)(2,1)}), bf16[1024,2176]{1,0:T(8,128)(2,1)}) %all-gather.2.cloned.1.call-update) | async-done | bytes 4456464 | tf_op jit(solution)/shard_map/all_gather | solution.py:245
  111.8 1.4 copy-done.1
  113.2 12.1 %experts.1 = (bf16[2,2,4,128,512]{4,3,2,1,0:T(8,128)(2,1)S(1)}, f32[2,2,4,128,512]{4,3,2,1,0:T(8,128)}) custom-call(s32[2]{0:T(128)S(1)} %copy-done.2, bf16[1024,2176]{1,0:T(8,128)(2,1)} %all-gather.2.cloned.1.call-done.rows_ref, bf16[2048,768]{1,0:T(8,128)(2,1)} %pad_maximum_fusion.gate_up_ref, bf16[384,2048]{1,0:T(8,128)(2,1)S(1)} %bitcast.125), custom_call_target="tpu_custom_call" | custom-call | tf_op jit(solution)/shard_map/experts/pallas_call | solution.py:250
  125.8 3.9 %collective-permute-done.3 = bf16[2,2,4,128,512]{4,3,2,0,1:T(8,128)(2,1)S(1)} collective-permute-done((bf16[2,2,4,128,512]{4,3,2,0,1:T(8,128)(2,1)S(1)}, bf16[2,2,4,128,512]{4,3,2,0,1:T(8,128)(2,1)S(1)}, u32[]{:S(2)}, u32[]{:S(2)}) %collective-permute-start.3) | collective-permute-done | bytes 2097184 | tf_op jit(solution)/shard_map/ppermute | solution.py:149
  130.7 1.5 collective-permute-start.6
  133.0 11.9 %collective-permute-done.6 = bf16[2,4,64,512]{3,2,1,0:T(8,128)(2,1)S(1)} collective-permute-done((bf16[2,4,64,512]{3,2,1,0:T(8,128)(2,1)S(1)}, bf16[2,4,64,512]{3,2,1,0:T(8,128)(2,1)S(1)}, u32[]{:S(2)}, u32[]{:S(2)}) %collective-permute-start.6) | collective-permute-done | bytes 524320 | tf_op jit(solution)/shard_map/ppermute | solution.py:149
  145.1 1.6 collective-permute-start.7
  148.6 4.2 %collective-permute-done.7 = bf16[4,64,512]{2,1,0:T(8,128)(2,1)S(1)} collective-permute-done((bf16[4,64,512]{2,1,0:T(8,128)(2,1)S(1)}, bf16[4,64,512]{2,1,0:T(8,128)(2,1)S(1)}, u32[]{:S(2)}, u32[]{:S(2)}) %collective-permute-start.7) | collective-permute-done | bytes 262176 | tf_op jit(solution)/shard_map/ppermute | solution.py:149
  154.0 1.6 collective-permute-done.5
  157.4 1.7 collective-permute-start.10
  159.7 2.2 %collective-permute-start.9 = (bf16[128,512]{1,0:T(8,128)(2,1)S(1)}, bf16[128,512]{1,0:T(8,128)(2,1)}, u32[]{:S(2)}, u32[]{:S(2)}) collective-permute-start(bf16[128,512]{1,0:T(8,128)(2,1)S(1)} %get-tuple-element.30), channel_id=1, source_target_pairs={{0,16},{4,20},{8,24},{12,28},{16,0},{20,4},{24,8},{28,12},{1,17},{... | collective-permute-start | bytes 393224 | tf_op jit(solution)/shard_map/ppermute | solution.py:149
  162.8 3.2 %collective-permute-done.10 = bf16[128,512]{1,0:T(8,128)(2,1)S(1)} collective-permute-done((bf16[128,512]{1,0:T(8,128)(2,1)}, bf16[128,512]{1,0:T(8,128)(2,1)S(1)}, u32[]{:S(2)}, u32[]{:S(2)}) %collective-permute-start.10) | collective-permute-done | bytes 131104 | tf_op jit(solution)/shard_map/ppermute | solution.py:149
  166.0 4.7 %collective-permute-done.9 = bf16[128,512]{1,0:T(8,128)(2,1)} collective-permute-done((bf16[128,512]{1,0:T(8,128)(2,1)S(1)}, bf16[128,512]{1,0:T(8,128)(2,1)}, u32[]{:S(2)}, u32[]{:S(2)}) %collective-permute-start.9) | collective-permute-done | bytes 131104 | tf_op jit(solution)/shard_map/ppermute | solution.py:149
  170.7 1.7 fusion.28.total_ref
  172.5 1.7 finish.1
  (100 shorter events, 18.3 us)
Async XLA Ops:
  6.5 28.7 %copy-start = (bf16[512,2048]{1,0:T(8,128)(2,1)S(1)}, bf16[512,2048]{1,0:T(8,128)(2,1)}, u32[]{:S(2)}) copy-start(bf16[512,2048]{1,0:T(8,128)(2,1)} %param.25) | copy-start | bytes 6291460
  6.5 11.9 %copy-start.11 = (f32[2048]{0:T(1024)S(1)}, f32[2048]{0:T(1024)}, u32[]{:S(2)}) copy-start(f32[2048]{0:T(1024)} %param.19) | copy-start | bytes 24580
  6.5 11.8 %copy-start.17 = (s32[9]{0:T(128)S(1)}, s32[9]{0:T(128)}, u32[]{:S(2)}) copy-start(s32[9]{0:T(128)} %param.29) | copy-start | bytes 112
  6.5 105.3 %all-gather.2.cloned.1.call-start = ((), (), s32[]{:S(2)}) async-start(), calls=%async_computation | async-start | bytes 4595712 | tf_op jit(solution)/shard_map/all_gather | solution.py:245
  6.6 13.7 %copy-start.15 = (f32[128]{0:T(128)S(1)}, f32[128]{0:T(128)}, u32[]{:S(2)}) copy-start(f32[128]{0:T(128)} %param.24) | copy-start | bytes 1540
  15.6 17.9 %copy-start.3 = (bf16[128,2048]{1,0:T(8,128)(2,1)}, bf16[128,2048]{1,0:T(8,128)(2,1)S(1)}, u32[]{:S(2)}) copy-start(bf16[128,2048]{1,0:T(8,128)(2,1)S(1)} %all_gather.6.x_ref) | copy-start | bytes 1572868
  15.6 5.2 %copy-start.12 = (s32[9,32]{1,0:T(8,128)S(1)}, s32[9,32]{1,0:T(8,128)}, u32[]{:S(2)}) copy-start(s32[9,32]{1,0:T(8,128)} %param.28) | copy-start | bytes 3460
  15.8 5.8 %copy-start.16 = (f32[128]{0:T(128)S(1)}, f32[128]{0:T(128)}, u32[]{:S(2)}) copy-start(f32[128]{0:T(128)} %param.23) | copy-start | bytes 1540
  18.3 3.6 %copy-start.7 = (bf16[1,48,128,128]{3,2,1,0:T(8,128)(2,1)S(1)}, bf16[1,48,128,128]{3,2,1,0:T(8,128)(2,1)}, u32[]{:S(2)}) copy-start(bf16[1,48,128,128]{3,2,1,0:T(8,128)(2,1)} %param.26) | copy-start | bytes 4718596
  24.8 3.9 %copy-start.18 = (bf16[1,48,128,128]{3,2,1,0:T(8,128)(2,1)S(1)}, bf16[1,48,128,128]{3,2,1,0:T(8,128)(2,1)}, u32[]{:S(2)}) copy-start(bf16[1,48,128,128]{3,2,1,0:T(8,128)(2,1)} %param.27) | copy-start | bytes 4718596
  33.5 5.6 %copy-start.13 = (s32[128,8]{0,1:T(8,128)S(1)}, s32[128,8]{0,1:T(8,128)}, u32[]{:S(2)}) copy-start(s32[128,8]{0,1:T(8,128)} %param.31) | copy-start | bytes 12292
  33.5 6.3 %copy-start.14 = (f32[128,8]{0,1:T(8,128)S(1)}, f32[128,8]{0,1:T(8,128)}, u32[]{:S(2)}) copy-start(f32[128,8]{0,1:T(8,128)} %param.32) | copy-start | bytes 12292
  36.5 4.7 %collective-permute-start = (bf16[32,2048]{1,0:T(8,128)(2,1)}, bf16[32,2048]{1,0:T(8,128)(2,1)S(1)}, u32[]{:S(2)}, u32[]{:S(2)}) collective-permute-start(bf16[32,2048]{1,0:T(8,128)(2,1)} %get-tuple-element.34), channel_id=1, source_target_pairs={{0,1},{1,0},{2,3},{3,2},{4,5},{5,4},{6,7},{7,6},{8,9},{9,8},{10,11... | collective-permute-start | bytes 393224 | tf_op jit(solution)/shard_map/ppermute | solution.py:149
  36.8 6.6 %collective-permute-start.1 = (bf16[32,2048]{1,0:T(8,128)(2,1)}, bf16[32,2048]{1,0:T(8,128)(2,1)S(1)}, u32[]{:S(2)}, u32[]{:S(2)}) collective-permute-start(bf16[32,2048]{1,0:T(8,128)(2,1)} %get-tuple-element.33), channel_id=1, source_target_pairs={{0,2},{1,3},{2,0},{3,1},{4,6},{5,7},{6,4},{7,5},{8,10},{9,11},{10,... | collective-permute-start | bytes 393224 | tf_op jit(solution)/shard_map/ppermute | solution.py:149
  37.9 6.7 %collective-permute-start.2 = (bf16[32,2048]{1,0:T(8,128)(2,1)}, bf16[32,2048]{1,0:T(8,128)(2,1)S(1)}, u32[]{:S(2)}, u32[]{:S(2)}) collective-permute-start(bf16[32,2048]{1,0:T(8,128)(2,1)} %get-tuple-element.32), channel_id=1, source_target_pairs={{0,3},{1,2},{2,1},{3,0},{4,7},{5,6},{6,5},{7,4},{8,11},{9,10},{10,... | collective-permute-start | bytes 393224 | tf_op jit(solution)/shard_map/ppermute | solution.py:149
  41.2 3.4 %copy-start.8 = (bf16[32,2048]{1,0:T(8,128)(2,1)}, bf16[32,2048]{1,0:T(8,128)(2,1)S(1)}, u32[]{:S(2)}) copy-start(bf16[32,2048]{1,0:T(8,128)(2,1)S(1)} %collective-permute-done.near_ref) | copy-start | bytes 393220
  43.4 1.3 copy-start.9
  61.2 50.7 %copy-start.2 = (s32[2]{0:T(128)S(1)}, s32[2]{0:T(128)}, u32[]{:S(2)}) copy-start(s32[2]{0:T(128)} %pad_add_fusion.place_ref) | copy-start | bytes 28
  111.8 1.4 copy-start.1
  125.4 4.4 %copy-start.4 = (f32[2,2,4,128,512]{4,3,2,1,0:T(8,128)S(1)}, f32[2,2,4,128,512]{4,3,2,1,0:T(8,128)}, u32[]{:S(2)}) copy-start(f32[2,2,4,128,512]{4,3,2,1,0:T(8,128)} %get-tuple-element.13) | copy-start | bytes 12582916
  125.5 4.2 %collective-permute-start.3 = (bf16[2,2,4,128,512]{4,3,2,0,1:T(8,128)(2,1)S(1)}, bf16[2,2,4,128,512]{4,3,2,0,1:T(8,128)(2,1)S(1)}, u32[]{:S(2)}, u32[]{:S(2)}) collective-permute-start(bf16[2,2,4,128,512]{4,3,2,0,1:T(8,128)(2,1)S(1)} %copy.77), channel_id=1, source_target_pairs={{0,1},{1,0},{2,3},{3,2},{4,5},{5,4},{6,7},{7,6},{8,9},{9,8},{10,11... | collective-permute-start | bytes 6291464 | tf_op jit(solution)/shard_map/ppermute | solution.py:149
  130.7 14.2 %collective-permute-start.6 = (bf16[2,4,64,512]{3,2,1,0:T(8,128)(2,1)S(1)}, bf16[2,4,64,512]{3,2,1,0:T(8,128)(2,1)S(1)}, u32[]{:S(2)}, u32[]{:S(2)}) collective-permute-start(bf16[2,4,64,512]{3,2,1,0:T(8,128)(2,1)S(1)} %fusion.17), channel_id=1, source_target_pairs={{0,4},{4,0},{8,12},{12,8},{16,20},{20,16},{24,28},{28,24},{1,5},{5... | collective-permute-start | bytes 1572872 | tf_op jit(solution)/shard_map/ppermute | solution.py:149
  132.3 14.4 %collective-permute-start.4 = (bf16[2,4,64,512]{3,2,1,0:T(8,128)(2,1)S(1)}, bf16[2,4,64,512]{3,2,1,0:T(8,128)(2,1)S(1)}, u32[]{:S(2)}, u32[]{:S(2)}) collective-permute-start(bf16[2,4,64,512]{3,2,1,0:T(8,128)(2,1)S(1)} %fusion.16), channel_id=1, source_target_pairs={{0,2},{1,3},{2,0},{3,1},{4,6},{5,7},{6,4},{7,5},{8,10},{9,11},{10,... | collective-permute-start | bytes 1572872 | tf_op jit(solution)/shard_map/ppermute | solution.py:149
  145.1 1.8 copy-start.5
  145.1 7.7 %collective-permute-start.7 = (bf16[4,64,512]{2,1,0:T(8,128)(2,1)S(1)}, bf16[4,64,512]{2,1,0:T(8,128)(2,1)S(1)}, u32[]{:S(2)}, u32[]{:S(2)}) collective-permute-start(bf16[4,64,512]{2,1,0:T(8,128)(2,1)S(1)} %fusion.21), channel_id=1, source_target_pairs={{0,2},{1,3},{2,0},{3,1},{4,6},{5,7},{6,4},{7,5},{8,10},{9,11},{10,... | collective-permute-start | bytes 786440 | tf_op jit(solution)/shard_map/ppermute | solution.py:149
  148.0 7.6 %collective-permute-start.5 = (bf16[4,64,512]{2,1,0:T(8,128)(2,1)}, bf16[4,64,512]{2,1,0:T(8,128)(2,1)S(1)}, u32[]{:S(2)}, u32[]{:S(2)}) collective-permute-start(bf16[4,64,512]{2,1,0:T(8,128)(2,1)} %fusion.20), channel_id=1, source_target_pairs={{0,4},{4,0},{8,12},{12,8},{16,20},{20,16},{24,28},{28,24},{1,5},{5... | collective-permute-start | bytes 786440 | tf_op jit(solution)/shard_map/ppermute | solution.py:149
  157.4 8.5 %collective-permute-start.10 = (bf16[128,512]{1,0:T(8,128)(2,1)}, bf16[128,512]{1,0:T(8,128)(2,1)S(1)}, u32[]{:S(2)}, u32[]{:S(2)}) collective-permute-start(bf16[128,512]{1,0:T(8,128)(2,1)} %get-tuple-element.31), channel_id=1, source_target_pairs={{0,24},{4,28},{8,16},{12,20},{16,8},{20,12},{24,0},{28,4},{1,25},{... | collective-permute-start | bytes 393224 | tf_op jit(solution)/shard_map/ppermute | solution.py:149
  159.1 6.9 %collective-permute-start.8 = (bf16[128,512]{1,0:T(8,128)(2,1)S(1)}, bf16[128,512]{1,0:T(8,128)(2,1)}, u32[]{:S(2)}, u32[]{:S(2)}) collective-permute-start(bf16[128,512]{1,0:T(8,128)(2,1)S(1)} %get-tuple-element.29), channel_id=1, source_target_pairs={{0,8},{4,12},{8,0},{12,4},{16,24},{20,28},{24,16},{28,20},{1,9},{5... | collective-permute-start | bytes 393224 | tf_op jit(solution)/shard_map/ppermute | solution.py:149
  159.7 11.1 %collective-permute-start.9 = (bf16[128,512]{1,0:T(8,128)(2,1)S(1)}, bf16[128,512]{1,0:T(8,128)(2,1)}, u32[]{:S(2)}, u32[]{:S(2)}) collective-permute-start(bf16[128,512]{1,0:T(8,128)(2,1)S(1)} %get-tuple-element.30), channel_id=1, source_target_pairs={{0,16},{4,20},{8,24},{12,28},{16,0},{20,4},{24,8},{28,12},{1,17},{... | collective-permute-start | bytes 393224 | tf_op jit(solution)/shard_map/ppermute | solution.py:149
  161.8 10.6 %collective-permute-start.11 = (f32[32,512]{1,0:T(8,128)}, f32[32,512]{1,0:T(8,128)}, u32[]{:S(2)}, u32[]{:S(2)}) collective-permute-start(f32[32,512]{1,0:T(8,128)} %get-tuple-element.16), channel_id=1, source_target_pairs={{0,1},{1,0},{2,3},{3,2},{4,5},{5,4},{6,7},{7,6},{8,9},{9,8},{10,11... | collective-permute-start | bytes 196616 | tf_op jit(solution)/shard_map/ppermute | solution.py:149
  161.8 10.6 %collective-permute-start.12 = (f32[32,512]{1,0:T(8,128)}, f32[32,512]{1,0:T(8,128)}, u32[]{:S(2)}, u32[]{:S(2)}) collective-permute-start(f32[32,512]{1,0:T(8,128)} %get-tuple-element.17), channel_id=1, source_target_pairs={{0,2},{1,3},{2,0},{3,1},{4,6},{5,7},{6,4},{7,5},{8,10},{9,11},{10,... | collective-permute-start | bytes 196616 | tf_op jit(solution)/shard_map/ppermute | solution.py:149
  166.0 6.5 %collective-permute-start.13 = (f32[32,512]{1,0:T(8,128)}, f32[32,512]{1,0:T(8,128)}, u32[]{:S(2)}, u32[]{:S(2)}) collective-permute-start(f32[32,512]{1,0:T(8,128)} %get-tuple-element.18), channel_id=1, source_target_pairs={{0,3},{1,2},{2,1},{3,0},{4,7},{5,6},{6,5},{7,4},{8,11},{9,10},{10,... | collective-permute-start | bytes 196616 | tf_op jit(solution)/shard_map/ppermute | solution.py:149
  (2 other events, 1.8 us)
Sparse Core Ops, SparseCore 0:
  47.7 64.0 all-gather.1

commit v3 on v2

--- a/solution.py
+++ b/solution.py
@@ -1,3 +1,4 @@
+import functools
 import math
 
 import jax
@@ -151,7 +152,7 @@
 
 def pack_kernel(
     place_ref, own_ref, near_ref, far_ref, cross_ref, x_ref, gain_ref, ids_ref, routes_ref,
-    rows_ref, keep_ref, near_out, far_out, cross_out, residual_ref,
+    rows_ref, keep_ref, near_out, far_out, cross_out, residual_ref, spread_ref,
 ):
     tp_index = place_ref[1]
     share_rows, width = own_ref.shape
@@ -163,12 +164,13 @@
     residual = x_ref[mine, :].astype(jnp.float32) + head_sum
     residual_ref[...] = residual
     rows_ref[:, :width] = rms_scale(residual, gain_ref[...]).astype(jnp.bfloat16)
-    ids = ids_ref[mine, :]
-    weights = routes_ref[mine, :]
-    lane = lax.broadcasted_iota(jnp.int32, (share_rows, LANES), 1)
-    spread = jnp.zeros((share_rows, LANES), jnp.float32)
-    for k in range(ids.shape[1]):
-        spread = spread + jnp.where(lane % (LANES // 2) == ids[:, k : k + 1], weights[:, k : k + 1], 0.0)
+    expert = lax.broadcasted_iota(jnp.int32, (LANES, spread_ref.shape[0]), 0) % (LANES // 2)
+    spread = jnp.zeros(expert.shape, jnp.float32)
+    for k in range(ids_ref.shape[0]):
+        spread = spread + jnp.where(expert == ids_ref[k : k + 1, :], routes_ref[k : k + 1, :], 0.0)
+    spread_ref[...] = spread.T
+    spread = spread_ref[mine, :]
+    lane = lax.broadcasted_iota(jnp.int32, spread.shape, 1)
     high = spread.astype(jnp.bfloat16).astype(jnp.float32)
     rows_ref[:, width:] = jnp.where(lane < LANES // 2, high, spread - high).astype(jnp.bfloat16)
     for step, out_ref in enumerate((keep_ref, near_out, far_out, cross_out)):
@@ -176,40 +178,84 @@
         out_ref[...] = residual_ref[:, pl.ds(column, share_width)]
 
 
-def experts_kernel(place_ref, rows_ref, gate_up_ref, down_ref, send_ref, keep_ref):
+def experts_kernel(far_parts, place_ref, *refs):
+    near_ref, core_ref = refs[:2]
+    far_refs, far_core_refs = refs[2 : 2 + far_parts], refs[2 + far_parts : 2 + 2 * far_parts]
+    gate_ref, up_ref, down_ref = refs[2 + 2 * far_parts : 5 + 2 * far_parts]
+    out_refs, rows_ref = refs[5 + 2 * far_parts : -1], refs[-1]
     req_index, tp_index = place_ref[0], place_ref[1]
-    width, doubled = gate_up_ref.shape
-    units = doubled // 2
-    half_rows, share_width = keep_ref.shape[3], keep_ref.shape[4]
-    acts = jnp.dot(rows_ref[:, :width], gate_up_ref[...], preferred_element_type=jnp.float32)
-    gate_acts, up_acts = acts[:, :units], acts[:, units:]
+    levels, share_rows, _ = near_ref.shape
+    units = gate_ref.shape[2]
+    width = gate_ref.shape[1]
+    share_width = width // 4
+
+    def pick(parts):
+        if len(parts) == 1:
+            return parts[0][...]
+        return jnp.where(pl.program_id(0) == 0, parts[0][...], parts[1][...])
+
+    for step, value in enumerate((near_ref[...], core_ref[...], pick(far_refs), pick(far_core_refs))):
+        for level in range(levels):
+            start = (4 * level + (tp_index ^ step)) * share_rows
+            rows_ref[pl.ds(pl.multiple_of(start, share_rows), share_rows), :] = value[level]
     spread = rows_ref[:, width:].astype(jnp.float32)
     lane = lax.broadcasted_iota(jnp.int32, spread.shape, 1) % (LANES // 2)
-    weights = [
-        jnp.sum(jnp.where(lane == 2 * req_index + e, spread, 0.0), axis=1, keepdims=True)
-        for e in range(2)
-    ]
-    unit = lax.broadcasted_iota(jnp.int32, gate_acts.shape, 1)
-    weight = jnp.where(unit < units // 2, weights[0], weights[1])
-    hidden_act = (gate_acts / (1.0 + jnp.exp(-gate_acts)) * up_acts * weight).astype(jnp.bfloat16)
+    acts = []
+    for e in range(2):
+        weight = jnp.sum(jnp.where(lane == 2 * req_index + e, spread, 0.0), axis=1, keepdims=True)
+        gate = jnp.dot(rows_ref[:, :width], gate_ref[e], preferred_element_type=jnp.float32)
+        up = jnp.dot(rows_ref[:, :width], up_ref[e], preferred_element_type=jnp.float32)
+        acts.append((gate / (1.0 + jnp.exp(-gate)) * up * weight).astype(jnp.bfloat16))
     for step in range(4):
         column = pl.multiple_of((tp_index ^ step) * share_width, share_width)
         part = jnp.dot(
-            hidden_act, down_ref[:, pl.ds(column, share_width)], preferred_element_type=jnp.float32
+            acts[0], down_ref[0, :, pl.ds(column, share_width)], preferred_element_type=jnp.float32
+        ) + jnp.dot(
+            acts[1], down_ref[1, :, pl.ds(column, share_width)], preferred_element_type=jnp.float32
         )
-        target = send_ref if step % 2 else keep_ref
-        for x in range(2):
-            target[step // 2, (req_index % 2) ^ x, 0] = part[
-                x * half_rows : (x + 1) * half_rows
-            ].astype(target.dtype)
-
-
-def finish_kernel(place_ref, total_ref, keep_ref, near_ref, far_ref, cross_ref, out_ref):
+        target = out_refs[step]
+        target[...] = part.reshape(target.shape).astype(target.dtype)
+
+
+def run_experts(place, near, core, far, far_core, gate_weight, up_weight, down_weight):
+    levels, share_rows, packed = near.shape
+    share_width = down_weight.shape[2] // 4
+    block = pl.BlockSpec((2, share_rows, packed), lambda z: (z, 0, 0))
+    fixed = pl.BlockSpec((2, share_rows, packed), lambda z: (0, 0, 0))
+    far_spec = block if len(far) == 1 else fixed
+    weight_specs = [
+        pl.BlockSpec(w.shape, lambda z: (0, 0, 0), pipeline_mode=pl.Buffered(1))
+        for w in (gate_weight, up_weight, down_weight)
+    ]
+    out_shape = (levels, 4 * share_rows, share_width)
+    return pl.pallas_call(
+        functools.partial(experts_kernel, len(far)),
+        grid=(levels // 2,),
+        out_shape=[
+            jax.ShapeDtypeStruct(out_shape, jnp.bfloat16 if step % 2 else jnp.float32)
+            for step in range(4)
+        ],
+        in_specs=[SMEM, block, block] + [far_spec] * (2 * len(far)) + weight_specs,
+        out_specs=[pl.BlockSpec((2,) + out_shape[1:], lambda z: (z, 0, 0))] * 4,
+        scratch_shapes=[pltpu.VMEM((8 * share_rows, packed), jnp.bfloat16)],
+        compiler_params=pltpu.CompilerParams(vmem_limit_bytes=VMEM_LIMIT),
+        name="experts",
+    )(place, near, core, *far, *far_core, gate_weight, up_weight, down_weight)
+
+
+def finish_kernel(
+    place_ref, own_ref, x_ref, y_ref, z1_ref, z2_ref, z3_ref, keep_ref, near_ref, far_ref, cross_ref, out_ref
+):
     tp_index = place_ref[1]
     share_rows = keep_ref.shape[0]
     for step, part_ref in enumerate((keep_ref, near_ref, far_ref, cross_ref)):
         rows = pl.ds(pl.multiple_of((tp_index ^ step) * share_rows, share_rows), share_rows)
-        out_ref[rows, :] = (total_ref[rows, :] + part_ref[...]).astype(jnp.bfloat16)
+        total = own_ref[0, rows, :] + part_ref[...]
+        for extra_ref in (x_ref, y_ref):
+            total = total + extra_ref[0, rows, :].astype(jnp.float32)
+        for extra_ref in (z1_ref, z2_ref, z3_ref):
+            total = total + extra_ref[rows, :].astype(jnp.float32)
+        out_ref[rows, :] = total.astype(jnp.bfloat16)
 
 
 def moe_dense(
@@ -225,7 +271,6 @@
     req_index, tp_index = lax.axis_index("req"), lax.axis_index("tp")
     token_count, width = x_full.shape
     share_rows, share_width = token_count // 4, width // 4
-    units = 2 * gate_weight.shape[2]
     place = jnp.stack([req_index, tp_index]).astype(jnp.int32)
 
     def head_rows(bits):
@@ -238,59 +283,52 @@
         out_shape=[jax.ShapeDtypeStruct((share_rows, width + LANES), jnp.bfloat16)] + [share_f32] * 4,
         in_specs=[SMEM] + [VMEM] * 8,
         out_specs=[VMEM] * 5,
-        scratch_shapes=[pltpu.VMEM((share_rows, width), jnp.float32)],
+        scratch_shapes=[
+            pltpu.VMEM((share_rows, width), jnp.float32),
+            pltpu.VMEM((token_count, LANES), jnp.float32),
+        ],
         name="pack_rows",
-    )(place, head_rows(0), *received, x_full, norm_post_gain[None, :], expert_ids, route_weights)
+    )(place, head_rows(0), *received, x_full, norm_post_gain[None, :], expert_ids.T, route_weights.T)
     residuals = residuals[:1] + [flip(residuals[bits], "tp", bits) for bits in (1, 2, 3)]
-    all_rows = lax.all_gather(rows, ("req", "tp"), axis=0, tiled=True)
-    gate_up = jnp.concatenate([gate_weight[0], gate_weight[1], up_weight[0], up_weight[1]], axis=1)
-    block = (2, 2, 1, token_count, share_width)
-    parts = (2, 2, 4, token_count, share_width)
-    out_spec = pl.BlockSpec(block, lambda z: (0, 0, z, 0, 0))
-    send, keep = pl.pallas_call(
-        experts_kernel,
-        grid=(4,),
-        out_shape=[
-            jax.ShapeDtypeStruct(parts, jnp.bfloat16),
-            jax.ShapeDtypeStruct(parts, jnp.float32),
-        ],
-        in_specs=[
-            SMEM,
-            pl.BlockSpec((2 * token_count, width + LANES), lambda z: (z, 0)),
-            pl.BlockSpec((width, 2 * units), lambda z: (0, 0)),
-            pl.BlockSpec((units, width), lambda z: (0, 0)),
-        ],
-        out_specs=[out_spec, out_spec],
-        compiler_params=pltpu.CompilerParams(vmem_limit_bytes=VMEM_LIMIT),
-        name="experts",
-    )(place, all_rows, gate_up, down_weight.reshape(units, width))
-    half = token_count // 2
-    got = flip(send, "tp", 1)
-    low = keep[..., :half, :] + got[..., :half, :].astype(jnp.float32)
-    high = keep[..., half:, :] + got[..., half:, :].astype(jnp.float32)
-    got_low = flip(low[1].astype(jnp.bfloat16), "tp", 2)
-    got_high = flip(high[:, 1].astype(jnp.bfloat16), "req", 1)
-    low = low[0] + got_low.astype(jnp.float32)
-    high = high[:, 0] + got_high.astype(jnp.float32)
-    got_low = flip(low[1].astype(jnp.bfloat16), "req", 1)
-    got_high = flip(high[1].astype(jnp.bfloat16), "tp", 2)
-    low = low[0] + got_low.astype(jnp.float32)
-    high = high[0] + got_high.astype(jnp.float32)
-    both = jnp.concatenate([low, high], axis=1)
-
-    def level(bits):
-        return lax.dynamic_index_in_dim(both, (req_index // 2) ^ bits, 0, keepdims=False)
-
-    total = level(0)
-    for bits in (1, 2, 3):
-        total = total + flip(level(bits).astype(jnp.bfloat16), "req", 2 * bits).astype(jnp.float32)
+    line = jnp.stack([rows] + [flip(rows, "req", 2 * bits) for bits in (1, 2, 3)])
+    line_x, line_y = flip(line, "req", 1), flip(line, "tp", 2)
+    across = (flip(line_x[:2], "tp", 2), flip(line_y[2:], "req", 1))
+    line_core, line_x_core, line_y_core = (flip(part, "tp", 1) for part in (line, line_x, line_y))
+    across_core = tuple(flip(part, "tp", 1) for part in across)
+    weights = (gate_weight, up_weight, down_weight)
+    near = run_experts(place, line, line_core, (line_y,), (line_y_core,), *weights)
+    side = run_experts(place, line_x, line_x_core, across, across_core, *weights)
+    keep_00, keep_01, keep_10, keep_11 = (
+        (part[2 * y], flip(part[2 * y + 1], "tp", 1)) for part in (near, side) for y in range(2)
+    )
+
+    def both(pair, levels):
+        return pair[0][levels] + pair[1][levels].astype(jnp.float32)
+
+    low, high = slice(0, 2), slice(2, 4)
+    by_x = flip(both(keep_11, low).astype(jnp.bfloat16), "req", 1).astype(jnp.float32)
+    by_y = flip(both(keep_11, high).astype(jnp.bfloat16), "tp", 2).astype(jnp.float32)
+    from_y = [
+        flip((both(keep_01, low) + by_x).astype(jnp.bfloat16), "tp", 2),
+        flip(both(keep_01, high).astype(jnp.bfloat16), "tp", 2),
+    ]
+    from_x = [
+        flip(both(keep_10, low).astype(jnp.bfloat16), "req", 1),
+        flip((both(keep_10, high) + by_y).astype(jnp.bfloat16), "req", 1),
+    ]
+
+    def level(z):
+        part = from_x[z // 2][z % 2].astype(jnp.float32) + from_y[z // 2][z % 2].astype(jnp.float32)
+        return (both(keep_00, z) + part).astype(jnp.bfloat16)
+
+    from_z = [flip(level(z), "req", 2 * z) for z in (1, 2, 3)]
     return pl.pallas_call(
         finish_kernel,
         out_shape=jax.ShapeDtypeStruct((token_count, share_width), jnp.bfloat16),
-        in_specs=[SMEM] + [VMEM] * 5,
+        in_specs=[SMEM] + [VMEM] * 10,
         out_specs=VMEM,
         name="finish",
-    )(place, total, *residuals)
+    )(place, both(keep_00, low), from_x[0], from_y[0], *from_z, *residuals)
 
 
 def moe_routed(

time: 182 us -> 154 us (0.85)
  waiting for transfers between devices: 79.2 us -> 59.9 us
  starting transfers between devices: 11.9 us -> 26.8 us
  between operations: 13.8 us -> 0.41 us
  local copies, waits for them, and re-layouts: 20.2 us -> 12.1 us
  other arithmetic: 17.5 us -> 12.8 us
  Pallas kernels: 16.2 us -> 18.7 us
    all_gather x1 -> x0, waiting for transfers between devices: 46.2 us -> none  [moe_dense(): all_rows = lax.all_gather(rows, ('req', 'tp'), axis=0, tiled=True)]
    ppermute x14 -> x31, waiting for transfers between devices: 33 us -> 59.9 us  [flip(): lax.ppermute(value, axis, [(i, i ^ bits) for i in range(lax.axis_size(axi...]
    ppermute x14 -> x31, starting transfers between devices: 11.9 us -> 26.8 us  [flip(): lax.ppermute(value, axis, [(i, i ^ bits) for i in range(lax.axis_size(axi...]
    concatenate x1 -> x0, other arithmetic: 4.52 us -> none  [moe_dense(): jnp.concatenate([gate_weight[0], gate_weight[1], up_weight[0], up_weight[...]
    slice x2, local copies, waits for them, and re-layouts: 5.44 us -> 1 us  [moe_dense(): across = (flip(line_x[:2], 'tp', 2), flip(line_y[2:], 'req', 1))]
    add x6 -> x1, other arithmetic: 5.24 us -> 0.9 us  [both(): return pair[0][levels] + pair[1][levels].astype(jnp.float32)]
    unnamed x44 -> x40, local copies, waits for them, and re-layouts: 12 us -> 9.42 us
    pallas_call x1 -> x2, Pallas kernels: 12.1 us -> 14.3 us  [run_experts(): pl.pallas_call(functools.partial(experts_kernel, len(far)), grid=(levels...]
  transfers between devices with their start and end apart: 15 -> 31, of which waited for: 9 -> 13; matrix products, arithmetic and copies ran while one was open for 14% -> 7% of each run, Pallas kernels for 0% -> 9%
where the time goes in v3:
time: 154 us
  waiting for transfers between devices  59.9 us (39%)
  starting transfers between devices  26.8 us (17%)
  Pallas kernels  18.7 us (12%)
  matrix products  14.1 us (9%)
  other arithmetic  12.8 us (8%)
  local copies, waits for them, and re-layouts  12.1 us (8%)
  blocking collectives  9 us (6%)
    ppermute x31, waiting for transfers between devices, flip(): lax.ppermute(value, axis, [(i, i ^ bits) for i in range(lax.axis_size(axi...  59.9 us
    ppermute x31, starting transfers between devices, flip(): lax.ppermute(value, axis, [(i, i ^ bits) for i in range(lax.axis_size(axi...  26.8 us
    pallas_call x2, Pallas kernels, run_experts(): pl.pallas_call(functools.partial(experts_kernel, len(far)), grid=(levels...  14.3 us
    unnamed x40, local copies, waits for them, and re-layouts  9.42 us
    all_gather x1, blocking collectives, body(): x_full = lax.all_gather(hidden_in, 'tp', axis=1, tiled=True)  9 us
    dot_general x1, matrix products, attend(): jnp.einsum('tkgh,knh->kgtn', queries, keys_cache, preferred_element_type=...  4.18 us
    dot_general x1, matrix products, attend(): jnp.einsum('kgtn,knh->tkgh', prob_cache, values_cache, preferred_element_...  4.03 us
    reduce_sum x1, other arithmetic, attend(): jnp.sum(exp_cache, axis=-1, keepdims=True)  3.74 us
  transfers between devices with their start and end apart: 31, of which 13 were waited for; matrix products, arithmetic and copies ran while one was open for 7% of the time, Pallas kernels for 9%

profile of v3, /device:TPU:0, one launch (start us, length us, event | category | flops | bytes accessed | tf_op | source)
XLA Modules:
  0.0 153.9 jit_solution(16071023042679182922)
XLA Ops:
  0.0 9.0 %all_gather.3.x_ref = bf16[128,2048]{1,0:T(8,128)(2,1)S(1)} all-gather(bf16[128,512]{1,0:T(8,128)(2,1)} %param.18), channel_id=1, replica_groups=mesh['req'=8,'tp'=4] {'tp'}, dimensions={1}, use_global_device_ids=true | all-gather | bytes 655360 | tf_op jit(solution)/shard_map/all_gather | solution.py:402
  9.2 2.1 %fusion.50 = f32[128,512]{1,0:T(8,128)S(1)} fusion(bf16[2048,512]{1,0:T(8,128)(2,1)} %param.20, bf16[128,2048]{1,0:T(8,128)(2,1)S(1)} %all_gather.3.x_ref, f32[2048]{0:T(1024)} %param.19, f32[128]{0:T(128)S(1)} %add_rsqrt_fusion.2), kind=kOutput, calls=%fused_computation.108 | convolution fusion | flops 269484032 | bytes 2892288 | tf_op jit(solution)/shard_map/dot_general | solution.py:405
  13.2 1.5 multiply_reduce_fusion.1
  18.5 4.2 %fusion = (f32[4,128]{1,0:T(4,128)S(1)}, f32[128,4,6144]{2,0,1:T(8,128)S(1)}) fusion(pred[128,6144]{1,0:T(8,128)(4,1)S(1)} %broadcast_compare_fusion, bf16[6144,128,1]{1,0,2:T(8,128)(2,1)} %bitcast.92, bf16[128,4,64]{2,0,1:T(8,128)(2,1)S(1)} %get-tuple-element.48, bf16[128,4,64]{2,0,1:T(8,128)(2,1)S(1)} %get-tuple-element.47), kind=kOutput, calls=%fused_computation.3 | convolution fusion | flops 815005184 | bytes 15075328 | tf_op jit(solution)/shard_map/tkgh,knh->kgtn/dot_general | solution.py:82
  23.1 3.7 %fusion.1 = f32[4,128]{1,0:T(4,128)S(1)} fusion(f32[128,4,6144]{2,0,1:T(8,128)S(1)} %get-tuple-element.56, f32[4,128]{1,0:T(4,128)S(1)} %max.8, pred[128,6144]{1,0:T(8,128)(4,1)S(1)} %broadcast_compare_fusion), kind=kLoop, calls=%fused_computation.4 | loop fusion | flops 15728128 | bytes 13373440 | tf_op jit(solution)/shard_map/reduce_sum | solution.py:96
  26.9 4.0 %fusion.5 = f32[128,4,128]{2,0,1:T(8,128)S(1)} fusion(bf16[6144,128,1]{1,0,2:T(8,128)(2,1)S(1)} %bitcast.101, f32[4,128]{1,0:T(4,128)S(1)} %add.200, f32[4,128]{1,0:T(4,128)S(1)} %max.8, f32[128,4,6144]{2,0,1:T(8,128)S(1)} %get-tuple-element.56, pred[128,6144]{1,0:T(8,128)(4,1)S(1)} %broadcast_compare_fusion), kind=kOutput, calls=%fused_computation.13 | convolution fusion | flops 824180736 | bytes 15208448 | tf_op jit(solution)/shard_map/kgtn,knh->tkgh/dot_general | solution.py:99
  30.9 1.6 %fusion.8 = bf16[128,4,128]{2,0,1:T(8,128)(2,1)S(1)} fusion(f32[128,4,128]{2,0,1:T(8,128)S(1)} %fusion.5, bf16[2048,128]{1,0:T(8,128)(2,1)} %param.22, f32[1,4,128,128]{2,3,1,0:T(8,128)S(1)} %get-tuple-element.60, f32[4,128]{1,0:T(4,128)S(1)} %add.200, f32[4,128]{1,0:T(4,128)S(1)} %max.8, pred[128,128]{0,1:T(8,128)(4,1)S(1)} %compare_and_fusion, ...), kind=kOutput, calls=%fused_computation.14 | convolution fusion | flops 85344256 | bytes 1733120 | tf_op jit(solution)/shard_map/kgts,skh->tkgh/dot_general | solution.py:102
  37.0 3.7 %collective-permute-done.1.far_ref = bf16[32,2048]{1,0:T(8,128)(2,1)S(1)} collective-permute-done((bf16[32,2048]{1,0:T(8,128)(2,1)}, bf16[32,2048]{1,0:T(8,128)(2,1)S(1)}, u32[]{:S(2)}, u32[]{:S(2)}) %collective-permute-start.1) | collective-permute-done | bytes 131104 | tf_op jit(solution)/shard_map/ppermute | solution.py:150
  42.6 2.3 %pack_rows.1 = (bf16[32,2176]{1,0:T(8,128)(2,1)}, f32[32,512]{1,0:T(8,128)}, f32[32,512]{1,0:T(8,128)}, f32[32,512]{1,0:T(8,128)}, f32[32,512]{1,0:T(8,128)}) custom-call(s32[2]{0:T(128)} %pad_add_fusion.place_ref, f32[32,2048]{1,0:T(8,128)} %constant_dynamic-slice_fusion.own_ref, bf16[32,2048]{1,0:T(8,128)(2,1)} %copy-done.5, bf16[32,2048]{1,0:T(8,128)(2,1)} %copy-done.6, ...), custom_call_target="tpu_custom_call" | custom-call | tf_op jit(solution)/shard_map/pack_rows/pallas_call | solution.py:281
  44.9 1.6 %collective-permute-start.3 = (bf16[32,2176]{1,0:T(8,128)(2,1)}, bf16[32,2176]{1,0:T(8,128)(2,1)S(1)}, u32[]{:S(2)}, u32[]{:S(2)}) collective-permute-start(bf16[32,2176]{1,0:T(8,128)(2,1)} %get-tuple-element.18), channel_id=1, source_target_pairs={{0,8},{4,12},{8,0},{12,4},{16,24},{20,28},{24,16},{28,20},{1,9},{5... | collective-permute-start | bytes 417800 | tf_op jit(solution)/shard_map/ppermute | solution.py:150
  46.5 2.6 %collective-permute-start.4 = (bf16[32,2176]{1,0:T(8,128)(2,1)}, bf16[32,2176]{1,0:T(8,128)(2,1)S(1)}, u32[]{:S(2)}, u32[]{:S(2)}) collective-permute-start(bf16[32,2176]{1,0:T(8,128)(2,1)} %get-tuple-element.18), channel_id=1, source_target_pairs={{0,16},{4,20},{8,24},{12,28},{16,0},{20,4},{24,8},{28,12},{1,17},{... | collective-permute-start | bytes 417800 | tf_op jit(solution)/shard_map/ppermute | solution.py:150
  49.3 4.6 %collective-permute-done.3 = bf16[32,2176]{1,0:T(8,128)(2,1)S(1)} collective-permute-done((bf16[32,2176]{1,0:T(8,128)(2,1)}, bf16[32,2176]{1,0:T(8,128)(2,1)S(1)}, u32[]{:S(2)}, u32[]{:S(2)}) %collective-permute-start.3) | collective-permute-done | bytes 139296 | tf_op jit(solution)/shard_map/ppermute | solution.py:150
  53.9 6.2 %collective-permute-done.4 = bf16[32,2176]{1,0:T(8,128)(2,1)S(1)} collective-permute-done((bf16[32,2176]{1,0:T(8,128)(2,1)}, bf16[32,2176]{1,0:T(8,128)(2,1)S(1)}, u32[]{:S(2)}, u32[]{:S(2)}) %collective-permute-start.4) | collective-permute-done | bytes 139296 | tf_op jit(solution)/shard_map/ppermute | solution.py:150
  61.1 1.5 collective-permute-start.10
  63.8 11.1 %collective-permute-done.10.refs_0_ = bf16[4,32,2176]{2,1,0:T(8,128)(2,1)} collective-permute-done((bf16[4,32,2176]{2,1,0:T(8,128)(2,1)S(1)}, bf16[4,32,2176]{2,1,0:T(8,128)(2,1)}, u32[]{:S(2)}, u32[]{:S(2)}) %collective-permute-start.10) | collective-permute-done | bytes 557088 | tf_op jit(solution)/shard_map/ppermute | solution.py:150
  77.0 1.5 collective-permute-start.13
  78.5 4.1 %collective-permute-done.12.refs_2_ = bf16[2,32,2176]{2,1,0:T(8,128)(2,1)S(1)} collective-permute-done((bf16[2,32,2176]{2,1,0:T(8,128)(2,1)S(1)}, bf16[2,32,2176]{2,1,0:T(8,128)(2,1)S(1)}, u32[]{:S(2)}, u32[]{:S(2)}) %collective-permute-start.12) | collective-permute-done | bytes 278560 | tf_op jit(solution)/shard_map/ppermute | solution.py:150
  82.6 3.7 %collective-permute-done.13.refs_3_ = bf16[2,32,2176]{2,1,0:T(8,128)(2,1)} collective-permute-done((bf16[2,32,2176]{2,1,0:T(8,128)(2,1)S(1)}, bf16[2,32,2176]{2,1,0:T(8,128)(2,1)}, u32[]{:S(2)}, u32[]{:S(2)}) %collective-permute-start.13) | collective-permute-done | bytes 278560 | tf_op jit(solution)/shard_map/ppermute | solution.py:150
  86.8 3.7 %copy.52.refs_4_.refs_6_ = bf16[2,2048,192]{2,1,0:T(8,128)(2,1)} copy(bf16[2,2048,192]{1,2,0:T(8,128)(2,1)} %param.33) | data formatting | bytes 3145728 | tf_op args[15]
  90.5 3.7 %copy.53.refs_5_.refs_7_ = bf16[2,2048,192]{2,1,0:T(8,128)(2,1)} copy(bf16[2,2048,192]{1,2,0:T(8,128)(2,1)} %param.34) | data formatting | bytes 3145728 | tf_op args[16]
  94.9 7.2 %experts.3 = (f32[4,128,512]{2,1,0:T(8,128)S(1)}, bf16[4,128,512]{2,1,0:T(8,128)(2,1)S(1)}, f32[4,128,512]{2,1,0:T(8,128)S(1)}, bf16[4,128,512]{2,1,0:T(8,128)(2,1)S(1)}) custom-call(s32[2]{0:T(128)S(1)} %copy-done.1, bf16[4,32,2176]{2,1,0:T(8,128)(2,1)} %collective-permute-done.10.refs_0_, bf16[4,32,2176]{2,1,0:T(8,128)(2,1)} %collective-permute-done.11.refs_1_, ...), custom_call_target="tpu_custom_call" | custom-call | tf_op jit(solution)/shard_map/experts/pallas_call | solution.py:231
  102.7 7.1 %experts.2 = (f32[4,128,512]{2,1,0:T(8,128)S(1)}, bf16[4,128,512]{2,1,0:T(8,128)(2,1)S(1)}, f32[4,128,512]{2,1,0:T(8,128)S(1)}, bf16[4,128,512]{2,1,0:T(8,128)(2,1)S(1)}) custom-call(s32[2]{0:T(128)S(1)} %copy-done.1, bf16[4,32,2176]{2,1,0:T(8,128)(2,1)S(1)} %pad_maximum_fusion.refs_0_, bf16[4,32,2176]{2,1,0:T(8,128)(2,1)} %collective-permute-done.6.refs_1_, ...), custom_call_target="tpu_custom_call" | custom-call | tf_op jit(solution)/shard_map/experts/pallas_call | solution.py:231
  110.1 1.5 collective-permute-start.20
  113.1 5.8 %collective-permute-done.20 = bf16[2,128,512]{2,1,0:T(8,128)(2,1)S(1)} collective-permute-done((bf16[2,128,512]{2,1,0:T(8,128)(2,1)S(1)}, bf16[2,128,512]{2,1,0:T(8,128)(2,1)S(1)}, u32[]{:S(2)}, u32[]{:S(2)}) %collective-permute-start.20) | collective-permute-done | bytes 262176 | tf_op jit(solution)/shard_map/ppermute | solution.py:150
  121.3 1.5 collective-permute-start.17
  123.4 4.9 %collective-permute-done.21.y_ref = bf16[2,128,512]{2,1,0:T(8,128)(2,1)S(1)} collective-permute-done((bf16[2,128,512]{2,1,0:T(8,128)(2,1)S(1)}, bf16[2,128,512]{2,1,0:T(8,128)(2,1)S(1)}, u32[]{:S(2)}, u32[]{:S(2)}) %collective-permute-start.21) | collective-permute-done | bytes 262176 | tf_op jit(solution)/shard_map/ppermute | solution.py:150
  129.2 4.1 %collective-permute-done.25 = bf16[2,128,512]{2,1,0:T(8,128)(2,1)S(1)} collective-permute-done((bf16[2,128,512]{2,1,0:T(8,128)(2,1)S(1)}, bf16[2,128,512]{2,1,0:T(8,128)(2,1)S(1)}, u32[]{:S(2)}, u32[]{:S(2)}) %collective-permute-start.25) | collective-permute-done | bytes 262176 | tf_op jit(solution)/shard_map/ppermute | solution.py:150
  134.6 3.5 %collective-permute-start.22 = (bf16[128,512]{1,0:T(8,128)(2,1)S(1)}, bf16[128,512]{1,0:T(8,128)(2,1)S(1)}, u32[]{:S(2)}, u32[]{:S(2)}) collective-permute-start(bf16[128,512]{1,0:T(8,128)(2,1)S(1)} %get-tuple-element.37), channel_id=1, source_target_pairs={{0,8},{4,12},{8,0},{12,4},{16,24},{20,28},{24,16},{28,20},{1,9},{5... | collective-permute-start | bytes 393224 | tf_op jit(solution)/shard_map/ppermute | solution.py:150
  139.1 1.5 collective-permute-start.27
  141.5 1.9 %collective-permute-done.22.z1_ref = bf16[128,512]{1,0:T(8,128)(2,1)S(1)} collective-permute-done((bf16[128,512]{1,0:T(8,128)(2,1)S(1)}, bf16[128,512]{1,0:T(8,128)(2,1)S(1)}, u32[]{:S(2)}, u32[]{:S(2)}) %collective-permute-start.22) | collective-permute-done | bytes 131104 | tf_op jit(solution)/shard_map/ppermute | solution.py:150
  143.4 7.6 %collective-permute-done.26.z2_ref = bf16[128,512]{1,0:T(8,128)(2,1)S(1)} collective-permute-done((bf16[128,512]{1,0:T(8,128)(2,1)S(1)}, bf16[128,512]{1,0:T(8,128)(2,1)S(1)}, u32[]{:S(2)}, u32[]{:S(2)}) %collective-permute-start.26) | collective-permute-done | bytes 131104 | tf_op jit(solution)/shard_map/ppermute | solution.py:150
  151.7 2.2 %finish.1 = bf16[128,512]{1,0:T(8,128)(2,1)} custom-call(s32[2]{0:T(128)} %pad_add_fusion.place_ref, f32[2,128,512]{2,1,0:T(8,128)} %convert_add_fusion.own_ref, bf16[2,128,512]{2,1,0:T(8,128)(2,1)} %copy-done.4, bf16[2,128,512]{2,1,0:T(8,128)(2,1)} %copy-done.3, bf16[128,512]{1,0:T(8,128)(2,1)} %copy-done.8, bf16[128,512]{1,0:T(8,128)(2,1)} %copy-done.9, ...), custom_call_target="tpu_custom_call" | custom-call | tf_op jit(solution)/shard_map/finish/pallas_call | solution.py:325
  (121 shorter events, 28.5 us)
Async XLA Ops:
  33.8 3.2 %collective-permute-start = (bf16[32,2048]{1,0:T(8,128)(2,1)}, bf16[32,2048]{1,0:T(8,128)(2,1)S(1)}, u32[]{:S(2)}, u32[]{:S(2)}) collective-permute-start(bf16[32,2048]{1,0:T(8,128)(2,1)} %get-tuple-element.46), channel_id=1, source_target_pairs={{0,1},{1,0},{2,3},{3,2},{4,5},{5,4},{6,7},{7,6},{8,9},{9,8},{10,11... | collective-permute-start | bytes 393224 | tf_op jit(solution)/shard_map/ppermute | solution.py:150
  34.2 6.6 %collective-permute-start.1 = (bf16[32,2048]{1,0:T(8,128)(2,1)}, bf16[32,2048]{1,0:T(8,128)(2,1)S(1)}, u32[]{:S(2)}, u32[]{:S(2)}) collective-permute-start(bf16[32,2048]{1,0:T(8,128)(2,1)} %get-tuple-element.45), channel_id=1, source_target_pairs={{0,2},{1,3},{2,0},{3,1},{4,6},{5,7},{6,4},{7,5},{8,10},{9,11},{10,... | collective-permute-start | bytes 393224 | tf_op jit(solution)/shard_map/ppermute | solution.py:150
  35.3 6.7 %collective-permute-start.2 = (bf16[32,2048]{1,0:T(8,128)(2,1)}, bf16[32,2048]{1,0:T(8,128)(2,1)S(1)}, u32[]{:S(2)}, u32[]{:S(2)}) collective-permute-start(bf16[32,2048]{1,0:T(8,128)(2,1)} %get-tuple-element.44), channel_id=1, source_target_pairs={{0,3},{1,2},{2,1},{3,0},{4,7},{5,6},{6,5},{7,4},{8,11},{9,10},{10,... | collective-permute-start | bytes 393224 | tf_op jit(solution)/shard_map/ppermute | solution.py:150
  44.9 9.0 %collective-permute-start.3 = (bf16[32,2176]{1,0:T(8,128)(2,1)}, bf16[32,2176]{1,0:T(8,128)(2,1)S(1)}, u32[]{:S(2)}, u32[]{:S(2)}) collective-permute-start(bf16[32,2176]{1,0:T(8,128)(2,1)} %get-tuple-element.18), channel_id=1, source_target_pairs={{0,8},{4,12},{8,0},{12,4},{16,24},{20,28},{24,16},{28,20},{1,9},{5... | collective-permute-start | bytes 417800 | tf_op jit(solution)/shard_map/ppermute | solution.py:150
  46.5 13.6 %collective-permute-start.4 = (bf16[32,2176]{1,0:T(8,128)(2,1)}, bf16[32,2176]{1,0:T(8,128)(2,1)S(1)}, u32[]{:S(2)}, u32[]{:S(2)}) collective-permute-start(bf16[32,2176]{1,0:T(8,128)(2,1)} %get-tuple-element.18), channel_id=1, source_target_pairs={{0,16},{4,20},{8,24},{12,28},{16,0},{20,4},{24,8},{28,12},{1,17},{... | collective-permute-start | bytes 417800 | tf_op jit(solution)/shard_map/ppermute | solution.py:150
  49.0 11.1 %collective-permute-start.5 = (bf16[32,2176]{1,0:T(8,128)(2,1)}, bf16[32,2176]{1,0:T(8,128)(2,1)S(1)}, u32[]{:S(2)}, u32[]{:S(2)}) collective-permute-start(bf16[32,2176]{1,0:T(8,128)(2,1)} %get-tuple-element.18), channel_id=1, source_target_pairs={{0,24},{4,28},{8,16},{12,20},{16,8},{20,12},{24,0},{28,4},{1,25},{... | collective-permute-start | bytes 417800 | tf_op jit(solution)/shard_map/ppermute | solution.py:150
  61.1 13.7 %collective-permute-start.10 = (bf16[4,32,2176]{2,1,0:T(8,128)(2,1)S(1)}, bf16[4,32,2176]{2,1,0:T(8,128)(2,1)}, u32[]{:S(2)}, u32[]{:S(2)}) collective-permute-start(bf16[4,32,2176]{2,1,0:T(8,128)(2,1)S(1)} %pad_maximum_fusion.refs_0_), channel_id=1, source_target_pairs={{0,4},{4,0},{8,12},{12,8},{16,20},{20,16},{24,28},{28,24},{1,5},{5... | collective-permute-start | bytes 1671176 | tf_op jit(solution)/shard_map/ppermute | solution.py:150
  62.6 14.4 %collective-permute-start.7 = (bf16[4,32,2176]{2,1,0:T(8,128)(2,1)S(1)}, bf16[4,32,2176]{2,1,0:T(8,128)(2,1)S(1)}, u32[]{:S(2)}, u32[]{:S(2)}) collective-permute-start(bf16[4,32,2176]{2,1,0:T(8,128)(2,1)S(1)} %pad_maximum_fusion.refs_0_), channel_id=1, source_target_pairs={{0,2},{1,3},{2,0},{3,1},{4,6},{5,7},{6,4},{7,5},{8,10},{9,11},{10,... | collective-permute-start | bytes 1671176 | tf_op jit(solution)/shard_map/ppermute | solution.py:150
  75.8 6.7 %collective-permute-start.12 = (bf16[2,32,2176]{2,1,0:T(8,128)(2,1)S(1)}, bf16[2,32,2176]{2,1,0:T(8,128)(2,1)S(1)}, u32[]{:S(2)}, u32[]{:S(2)}) collective-permute-start(bf16[2,32,2176]{2,1,0:T(8,128)(2,1)S(1)} %slice.133), channel_id=1, source_target_pairs={{0,2},{1,3},{2,0},{3,1},{4,6},{5,7},{6,4},{7,5},{8,10},{9,11},{10,... | collective-permute-start | bytes 835592 | tf_op jit(solution)/shard_map/ppermute | solution.py:150
  77.0 17.3 %collective-permute-start.11 = (bf16[4,32,2176]{2,1,0:T(8,128)(2,1)}, bf16[4,32,2176]{2,1,0:T(8,128)(2,1)}, u32[]{:S(2)}, u32[]{:S(2)}) collective-permute-start(bf16[4,32,2176]{2,1,0:T(8,128)(2,1)} %collective-permute-done.10.refs_0_), channel_id=1, source_target_pairs={{0,1},{1,0},{2,3},{3,2},{4,5},{5,4},{6,7},{7,6},{8,9},{9,8},{10,11... | collective-permute-start | bytes 1671176 | tf_op jit(solution)/shard_map/ppermute | solution.py:150
  77.0 9.2 %collective-permute-start.13 = (bf16[2,32,2176]{2,1,0:T(8,128)(2,1)S(1)}, bf16[2,32,2176]{2,1,0:T(8,128)(2,1)}, u32[]{:S(2)}, u32[]{:S(2)}) collective-permute-start(bf16[2,32,2176]{2,1,0:T(8,128)(2,1)S(1)} %slice.134), channel_id=1, source_target_pairs={{0,4},{4,0},{8,12},{12,8},{16,20},{20,16},{24,28},{28,24},{1,5},{5... | collective-permute-start | bytes 835592 | tf_op jit(solution)/shard_map/ppermute | solution.py:150
  82.6 11.7 %collective-permute-start.14 = (bf16[2,32,2176]{2,1,0:T(8,128)(2,1)S(1)}, bf16[2,32,2176]{2,1,0:T(8,128)(2,1)}, u32[]{:S(2)}, u32[]{:S(2)}) collective-permute-start(bf16[2,32,2176]{2,1,0:T(8,128)(2,1)S(1)} %collective-permute-done.12.refs_2_), channel_id=1, source_target_pairs={{0,1},{1,0},{2,3},{3,2},{4,5},{5,4},{6,7},{7,6},{8,9},{9,8},{10,11... | collective-permute-start | bytes 835592 | tf_op jit(solution)/shard_map/ppermute | solution.py:150
  86.3 8.0 %collective-permute-start.15 = (bf16[2,32,2176]{2,1,0:T(8,128)(2,1)}, bf16[2,32,2176]{2,1,0:T(8,128)(2,1)}, u32[]{:S(2)}, u32[]{:S(2)}) collective-permute-start(bf16[2,32,2176]{2,1,0:T(8,128)(2,1)} %collective-permute-done.13.refs_3_), channel_id=1, source_target_pairs={{0,1},{1,0},{2,3},{3,2},{4,5},{5,4},{6,7},{7,6},{8,9},{9,8},{10,11... | collective-permute-start | bytes 835592 | tf_op jit(solution)/shard_map/ppermute | solution.py:150
  86.3 16.4 %collective-permute-start.6 = (bf16[4,32,2176]{2,1,0:T(8,128)(2,1)S(1)}, bf16[4,32,2176]{2,1,0:T(8,128)(2,1)}, u32[]{:S(2)}, u32[]{:S(2)}) collective-permute-start(bf16[4,32,2176]{2,1,0:T(8,128)(2,1)S(1)} %pad_maximum_fusion.refs_0_), channel_id=1, source_target_pairs={{0,1},{1,0},{2,3},{3,2},{4,5},{5,4},{6,7},{7,6},{8,9},{9,8},{10,11... | collective-permute-start | bytes 1671176 | tf_op jit(solution)/shard_map/ppermute | solution.py:150
  86.8 15.9 %collective-permute-start.8 = (bf16[4,32,2176]{2,1,0:T(8,128)(2,1)S(1)}, bf16[4,32,2176]{2,1,0:T(8,128)(2,1)}, u32[]{:S(2)}, u32[]{:S(2)}) collective-permute-start(bf16[4,32,2176]{2,1,0:T(8,128)(2,1)S(1)} %collective-permute-done.7.refs_2_), channel_id=1, source_target_pairs={{0,1},{1,0},{2,3},{3,2},{4,5},{5,4},{6,7},{7,6},{8,9},{9,8},{10,11... | collective-permute-start | bytes 1671176 | tf_op jit(solution)/shard_map/ppermute | solution.py:150
  90.5 42.8 %copy-start.16 = (f32[32,512]{1,0:T(8,128)S(1)}, f32[32,512]{1,0:T(8,128)}, u32[]{:S(2)}) copy-start(f32[32,512]{1,0:T(8,128)} %get-tuple-element.30) | copy-start | bytes 196612
  102.1 7.8 %collective-permute-start.19 = (bf16[4,128,512]{2,1,0:T(8,128)(2,1)S(1)}, bf16[4,128,512]{2,1,0:T(8,128)(2,1)S(1)}, u32[]{:S(2)}, u32[]{:S(2)}) collective-permute-start(bf16[4,128,512]{2,1,0:T(8,128)(2,1)S(1)} %get-tuple-element.26), channel_id=1, source_target_pairs={{0,1},{1,0},{2,3},{3,2},{4,5},{5,4},{6,7},{7,6},{8,9},{9,8},{10,11... | collective-permute-start | bytes 1572872 | tf_op jit(solution)/shard_map/ppermute | solution.py:150
  109.8 3.3 %collective-permute-start.18 = (bf16[4,128,512]{2,1,0:T(8,128)(2,1)S(1)}, bf16[4,128,512]{2,1,0:T(8,128)(2,1)S(1)}, u32[]{:S(2)}, u32[]{:S(2)}) collective-permute-start(bf16[4,128,512]{2,1,0:T(8,128)(2,1)S(1)} %get-tuple-element.24), channel_id=1, source_target_pairs={{0,1},{1,0},{2,3},{3,2},{4,5},{5,4},{6,7},{7,6},{8,9},{9,8},{10,11... | collective-permute-start | bytes 1572872 | tf_op jit(solution)/shard_map/ppermute | solution.py:150
  110.1 8.8 %collective-permute-start.20 = (bf16[2,128,512]{2,1,0:T(8,128)(2,1)S(1)}, bf16[2,128,512]{2,1,0:T(8,128)(2,1)S(1)}, u32[]{:S(2)}, u32[]{:S(2)}) collective-permute-start(bf16[2,128,512]{2,1,0:T(8,128)(2,1)S(1)} %get-tuple-element.41), channel_id=1, source_target_pairs={{0,4},{4,0},{8,12},{12,8},{16,20},{20,16},{24,28},{28,24},{1,5},{5... | collective-permute-start | bytes 786440 | tf_op jit(solution)/shard_map/ppermute | solution.py:150
  111.6 9.6 %collective-permute-start.16 = (bf16[4,128,512]{2,1,0:T(8,128)(2,1)S(1)}, bf16[4,128,512]{2,1,0:T(8,128)(2,1)S(1)}, u32[]{:S(2)}, u32[]{:S(2)}) collective-permute-start(bf16[4,128,512]{2,1,0:T(8,128)(2,1)S(1)} %get-tuple-element.22), channel_id=1, source_target_pairs={{0,1},{1,0},{2,3},{3,2},{4,5},{5,4},{6,7},{7,6},{8,9},{9,8},{10,11... | collective-permute-start | bytes 1572872 | tf_op jit(solution)/shard_map/ppermute | solution.py:150
  111.8 11.7 %collective-permute-start.9 = (bf16[4,128,512]{2,1,0:T(8,128)(2,1)S(1)}, bf16[4,128,512]{2,1,0:T(8,128)(2,1)S(1)}, u32[]{:S(2)}, u32[]{:S(2)}) collective-permute-start(bf16[4,128,512]{2,1,0:T(8,128)(2,1)S(1)} %get-tuple-element.20), channel_id=1, source_target_pairs={{0,1},{1,0},{2,3},{3,2},{4,5},{5,4},{6,7},{7,6},{8,9},{9,8},{10,11... | collective-permute-start | bytes 1572872 | tf_op jit(solution)/shard_map/ppermute | solution.py:150
  112.1 9.1 %collective-permute-start.23 = (bf16[2,128,512]{2,1,0:T(8,128)(2,1)S(1)}, bf16[2,128,512]{2,1,0:T(8,128)(2,1)S(1)}, u32[]{:S(2)}, u32[]{:S(2)}) collective-permute-start(bf16[2,128,512]{2,1,0:T(8,128)(2,1)S(1)} %get-tuple-element.40), channel_id=1, source_target_pairs={{0,2},{1,3},{2,0},{3,1},{4,6},{5,7},{6,4},{7,5},{8,10},{9,11},{10,... | collective-permute-start | bytes 786440 | tf_op jit(solution)/shard_map/ppermute | solution.py:150
  119.0 9.3 %collective-permute-start.21 = (bf16[2,128,512]{2,1,0:T(8,128)(2,1)S(1)}, bf16[2,128,512]{2,1,0:T(8,128)(2,1)S(1)}, u32[]{:S(2)}, u32[]{:S(2)}) collective-permute-start(bf16[2,128,512]{2,1,0:T(8,128)(2,1)S(1)} %get-tuple-element.43), channel_id=1, source_target_pairs={{0,2},{1,3},{2,0},{3,1},{4,6},{5,7},{6,4},{7,5},{8,10},{9,11},{10,... | collective-permute-start | bytes 786440 | tf_op jit(solution)/shard_map/ppermute | solution.py:150
  120.0 13.3 %collective-permute-start.25 = (bf16[2,128,512]{2,1,0:T(8,128)(2,1)S(1)}, bf16[2,128,512]{2,1,0:T(8,128)(2,1)S(1)}, u32[]{:S(2)}, u32[]{:S(2)}) collective-permute-start(bf16[2,128,512]{2,1,0:T(8,128)(2,1)S(1)} %get-tuple-element.42), channel_id=1, source_target_pairs={{0,2},{1,3},{2,0},{3,1},{4,6},{5,7},{6,4},{7,5},{8,10},{9,11},{10,... | collective-permute-start | bytes 786440 | tf_op jit(solution)/shard_map/ppermute | solution.py:150
  121.3 12.0 %collective-permute-start.17 = (bf16[2,128,512]{2,1,0:T(8,128)(2,1)S(1)}, bf16[2,128,512]{2,1,0:T(8,128)(2,1)S(1)}, u32[]{:S(2)}, u32[]{:S(2)}) collective-permute-start(bf16[2,128,512]{2,1,0:T(8,128)(2,1)S(1)} %get-tuple-element.39), channel_id=1, source_target_pairs={{0,4},{4,0},{8,12},{12,8},{16,20},{20,16},{24,28},{28,24},{1,5},{5... | collective-permute-start | bytes 786440 | tf_op jit(solution)/shard_map/ppermute | solution.py:150
  122.8 11.6 %collective-permute-start.24 = (bf16[2,128,512]{2,1,0:T(8,128)(2,1)S(1)}, bf16[2,128,512]{2,1,0:T(8,128)(2,1)S(1)}, u32[]{:S(2)}, u32[]{:S(2)}) collective-permute-start(bf16[2,128,512]{2,1,0:T(8,128)(2,1)S(1)} %get-tuple-element.38), channel_id=1, source_target_pairs={{0,4},{4,0},{8,12},{12,8},{16,20},{20,16},{24,28},{28,24},{1,5},{5... | collective-permute-start | bytes 786440 | tf_op jit(solution)/shard_map/ppermute | solution.py:150
  123.4 15.7 %collective-permute-start.28 = (f32[32,512]{1,0:T(8,128)S(1)}, f32[32,512]{1,0:T(8,128)S(1)}, u32[]{:S(2)}, u32[]{:S(2)}) collective-permute-start(f32[32,512]{1,0:T(8,128)S(1)} %copy-done.18), channel_id=1, source_target_pairs={{0,1},{1,0},{2,3},{3,2},{4,5},{5,4},{6,7},{7,6},{8,9},{9,8},{10,11... | collective-permute-start | bytes 196616 | tf_op jit(solution)/shard_map/ppermute | solution.py:150
  128.3 13.2 %collective-permute-start.29 = (f32[32,512]{1,0:T(8,128)S(1)}, f32[32,512]{1,0:T(8,128)S(1)}, u32[]{:S(2)}, u32[]{:S(2)}) collective-permute-start(f32[32,512]{1,0:T(8,128)S(1)} %copy-done.17), channel_id=1, source_target_pairs={{0,2},{1,3},{2,0},{3,1},{4,6},{5,7},{6,4},{7,5},{8,10},{9,11},{10,... | collective-permute-start | bytes 196616 | tf_op jit(solution)/shard_map/ppermute | solution.py:150
  133.3 8.2 %collective-permute-start.30 = (f32[32,512]{1,0:T(8,128)S(1)}, f32[32,512]{1,0:T(8,128)S(1)}, u32[]{:S(2)}, u32[]{:S(2)}) collective-permute-start(f32[32,512]{1,0:T(8,128)S(1)} %copy-done.16), channel_id=1, source_target_pairs={{0,3},{1,2},{2,1},{3,0},{4,7},{5,6},{6,5},{7,4},{8,11},{9,10},{10,... | collective-permute-start | bytes 196616 | tf_op jit(solution)/shard_map/ppermute | solution.py:150
  134.6 8.9 %collective-permute-start.22 = (bf16[128,512]{1,0:T(8,128)(2,1)S(1)}, bf16[128,512]{1,0:T(8,128)(2,1)S(1)}, u32[]{:S(2)}, u32[]{:S(2)}) collective-permute-start(bf16[128,512]{1,0:T(8,128)(2,1)S(1)} %get-tuple-element.37), channel_id=1, source_target_pairs={{0,8},{4,12},{8,0},{12,4},{16,24},{20,28},{24,16},{28,20},{1,9},{5... | collective-permute-start | bytes 393224 | tf_op jit(solution)/shard_map/ppermute | solution.py:150
  138.1 12.9 %collective-permute-start.26 = (bf16[128,512]{1,0:T(8,128)(2,1)S(1)}, bf16[128,512]{1,0:T(8,128)(2,1)S(1)}, u32[]{:S(2)}, u32[]{:S(2)}) collective-permute-start(bf16[128,512]{1,0:T(8,128)(2,1)S(1)} %get-tuple-element.36), channel_id=1, source_target_pairs={{0,16},{4,20},{8,24},{12,28},{16,0},{20,4},{24,8},{28,12},{1,17},{... | collective-permute-start | bytes 393224 | tf_op jit(solution)/shard_map/ppermute | solution.py:150
  139.1 11.9 %collective-permute-start.27 = (bf16[128,512]{1,0:T(8,128)(2,1)S(1)}, bf16[128,512]{1,0:T(8,128)(2,1)S(1)}, u32[]{:S(2)}, u32[]{:S(2)}) collective-permute-start(bf16[128,512]{1,0:T(8,128)(2,1)S(1)} %get-tuple-element.35), channel_id=1, source_target_pairs={{0,24},{4,28},{8,16},{12,20},{16,8},{20,12},{24,0},{28,4},{1,25},{... | collective-permute-start | bytes 393224 | tf_op jit(solution)/shard_map/ppermute | solution.py:150
  (18 other events, 212.5 us)

commit v4 on v3

--- a/solution.py
+++ b/solution.py
@@ -3,6 +3,7 @@
 
 import jax
 import jax.numpy as jnp
+import numpy as np
 from jax import lax
 from jax.experimental import pallas as pl
 from jax.experimental.pallas import tpu as pltpu
@@ -143,18 +144,206 @@
 LANES = 128
 VMEM = pl.BlockSpec(memory_space=pltpu.VMEM)
 SMEM = pl.BlockSpec(memory_space=pltpu.SMEM)
-VMEM_LIMIT = 48 * 1024 * 1024
+VMEM_LIMIT = 24 * 1024 * 1024
 
 
 def flip(value, axis, bits):
     return lax.ppermute(value, axis, [(i, i ^ bits) for i in range(lax.axis_size(axis))])
 
 
+def attention_kernel(
+    length_ref, table_ref, x_ref, gain_ref, frequency_ref, q_gain_ref, k_gain_ref,
+    q_hbm, k_hbm, v_hbm, key_hbm, value_hbm, o_hbm,
+    keep_out, near_out, far_out, cross_out,
+    q_ref, k_ref, v_ref, key_ref, value_ref, o_ref, query_ref, run_max, run_sum, run_mix,
+    mixed_ref, part_ref, owner_ref, slots_ref, page_owner, page_live, sems,
+):
+    sources = (q_hbm, k_hbm, v_hbm, key_hbm, value_hbm, o_hbm)
+    targets = (q_ref, k_ref, v_ref, key_ref, value_ref, o_ref)
+    copies = [
+        pltpu.make_async_copy(source, target, sems.at[i])
+        for i, (source, target) in enumerate(zip(sources, targets))
+    ]
+    for copy in copies:
+        copy.start()
+    tokens, head_dim = x_ref.shape[0], k_gain_ref.shape[1]
+    heads = q_ref.shape[1] // head_dim
+    decodes = tokens - PRE
+    for page in range(POOL):
+        page_owner[page] = -1
+        page_live[page] = 0
+    for request in range(1, REQS_DEV):
+
+        def name_page(entry, carry):
+            page = table_ref[request, entry]
+            page_owner[page] = request
+            page_live[page] = jnp.minimum(length_ref[request] - entry * PAGE, PAGE)
+            return carry
+
+        lax.fori_loop(0, (length_ref[request] + PAGE - 1) // PAGE, name_page, 0)
+    slot = lax.broadcasted_iota(jnp.int32, (1, PAGE), 1)
+    for page in range(POOL):
+        owner_ref[:, page * PAGE : (page + 1) * PAGE] = jnp.where(
+            slot < page_live[page], page_owner[page], -1
+        )
+    token = lax.broadcasted_iota(jnp.int32, (tokens, head_dim), 0)
+    lane = lax.broadcasted_iota(jnp.int32, (tokens, head_dim), 1)
+    position = length_ref[0] + token
+    for i in range(decodes):
+        position = jnp.where(token == PRE + i, length_ref[i + 1], position)
+    angle = position.astype(jnp.float32) * frequency_ref[...]
+    cosine = jnp.cos(angle)
+    sine = jnp.where(lane < head_dim // 2, -jnp.sin(angle), jnp.sin(angle))
+
+    def turned(values, gain):
+        values = rms_scale(values, gain)
+        return values * cosine + pltpu.roll(values, head_dim // 2, 1) * sine
+
+    normed = rms_scale(x_ref[...].astype(jnp.float32), gain_ref[...]).astype(jnp.bfloat16)
+    contract = (((1,), (1,)), ((), ()))
+    copies[0].wait()
+    query_lin = jnp.dot(normed, q_ref[...], preferred_element_type=jnp.float32)
+    copies[1].wait()
+    key_lin = jnp.dot(normed, k_ref[...], preferred_element_type=jnp.float32)
+    copies[2].wait()
+    values_new = jnp.dot(normed, v_ref[...], preferred_element_type=jnp.float32).astype(jnp.bfloat16)
+    keys_new = turned(key_lin, k_gain_ref[...]).astype(jnp.bfloat16)
+    to_log2 = math.log2(math.e) / math.sqrt(head_dim)
+    own_mask = (lane == token) | ((lane < token) & (token < PRE))
+    decode_q, decode_max, decode_sum, decode_mix = [], [], [], []
+    for head in range(heads):
+        span = slice(head * tokens, (head + 1) * tokens)
+        query = turned(query_lin[:, head * head_dim : (head + 1) * head_dim], q_gain_ref[...]) * to_log2
+        rounded = query.astype(jnp.bfloat16)
+        query_ref[span, :] = rounded
+        scores = lax.dot_general(rounded, keys_new, contract, preferred_element_type=jnp.float32)
+        scores = jnp.where(own_mask, scores, -1e30)
+        top = jnp.max(scores, axis=1, keepdims=True)
+        weights = jnp.exp2(scores - top)
+        total = jnp.sum(weights, axis=1, keepdims=True)
+        mix = jnp.dot(weights.astype(jnp.bfloat16), values_new, preferred_element_type=jnp.float32)
+        run_max[span, :] = jnp.broadcast_to(top, mix.shape)
+        run_sum[span, :] = jnp.broadcast_to(total, mix.shape)
+        run_mix[span, :] = mix
+        decode_q.append(query[PRE:])
+        decode_max.append(top[PRE:])
+        decode_sum.append(total[PRE:])
+        decode_mix.append(mix[PRE:])
+    copies[3].wait()
+    copies[4].wait()
+    decode_q = jnp.concatenate(decode_q, axis=0).astype(jnp.bfloat16)
+    decode_max, decode_sum, decode_mix = (
+        jnp.concatenate(part, axis=0) for part in (decode_max, decode_sum, decode_mix)
+    )
+    row_request = 1 + lax.broadcasted_iota(jnp.int32, (heads * decodes, 1), 0) % decodes
+    top = decode_max
+    width = 8 * PAGE
+    for start in range(0, POOL * PAGE, width):
+        keys = key_ref[start // PAGE : (start + width) // PAGE].reshape(width, head_dim)
+        scores = lax.dot_general(decode_q, keys, contract, preferred_element_type=jnp.float32)
+        scores = jnp.where(owner_ref[:, start : start + width] == row_request, scores, -1e30)
+        slots_ref[:, start : start + width] = scores
+        top = jnp.maximum(top, jnp.max(scores, axis=1, keepdims=True))
+    scale = jnp.exp2(decode_max - top)
+    total = decode_sum * scale
+    mix = decode_mix * scale
+    for start in range(0, POOL * PAGE, width):
+        weights = jnp.exp2(slots_ref[:, start : start + width] - top)
+        total = total + jnp.sum(weights, axis=1, keepdims=True)
+        values = value_ref[start // PAGE : (start + width) // PAGE].reshape(width, head_dim)
+        mix = mix + jnp.dot(weights.astype(jnp.bfloat16), values, preferred_element_type=jnp.float32)
+    decoded = mix / total
+    pages = 4
+    width = pages * PAGE
+    length = length_ref[0]
+    column = lax.broadcasted_iota(jnp.int32, (1, width), 1)
+
+    def prefill(step, carry):
+        names = [table_ref[0, jnp.minimum(step * pages + i, MAXPG - 1)] for i in range(pages)]
+        keys = jnp.concatenate([key_ref[name] for name in names], axis=0)
+        values = jnp.concatenate([value_ref[name] for name in names], axis=0)
+        live = column + step * width < length
+        for head in range(heads):
+            span = slice(head * tokens, (head + 1) * tokens)
+            scores = lax.dot_general(
+                query_ref[span, :], keys, contract, preferred_element_type=jnp.float32
+            )
+            scores = jnp.where(live, scores, -1e30)
+            before = run_max[span, :1]
+            top = jnp.maximum(before, jnp.max(scores, axis=1, keepdims=True))
+            scale = jnp.exp2(before - top)
+            weights = jnp.exp2(scores - top)
+            total = run_sum[span, :1] * scale + jnp.sum(weights, axis=1, keepdims=True)
+            mix = run_mix[span, :] * scale + jnp.dot(
+                weights.astype(jnp.bfloat16), values, preferred_element_type=jnp.float32
+            )
+            run_max[span, :] = jnp.broadcast_to(top, mix.shape)
+            run_sum[span, :] = jnp.broadcast_to(total, mix.shape)
+            run_mix[span, :] = mix
+        return carry
+
+    lax.fori_loop(0, (length + width - 1) // width, prefill, 0)
+    for head in range(heads):
+        span = slice(head * tokens, (head + 1) * tokens)
+        columns = slice(head * head_dim, (head + 1) * head_dim)
+        mixed_ref[:, columns] = run_mix[span, :] / run_sum[span, :]
+        mixed_ref[PRE:, columns] = decoded[head * decodes : (head + 1) * decodes]
+    copies[5].wait()
+    part_ref[...] = jnp.dot(
+        mixed_ref[...].astype(jnp.bfloat16), o_ref[...], preferred_element_type=jnp.float32
+    )
+    tp_index = lax.axis_index("tp")
+    share_rows = keep_out.shape[0]
+    for step, out_ref in enumerate((keep_out, near_out, far_out, cross_out)):
+        start = pl.multiple_of((tp_index ^ step) * share_rows, share_rows)
+        out_ref[...] = part_ref[pl.ds(start, share_rows), :].astype(out_ref.dtype)
+
+
+def attention_shares(
+    x_full, norm_in_gain, q_weight, k_weight, v_weight, q_gain, k_gain, o_weight,
+    key_pages, value_pages, page_table, cache_len,
+):
+    tokens, width = x_full.shape
+    head_dim = q_gain.shape[0]
+    rows = q_weight.shape[1] // head_dim * tokens
+    decode_rows = rows // tokens * (tokens - PRE)
+    half = ROPE_BASE ** (-np.arange(head_dim // 2) / (head_dim // 2))
+    frequency = jnp.asarray(np.concatenate([half, half])[None, :], jnp.float32)
+    large = (q_weight, k_weight, v_weight, key_pages[0], value_pages[0], o_weight)
+    share = (tokens // 4, width)
+    return pl.pallas_call(
+        attention_kernel,
+        out_shape=[jax.ShapeDtypeStruct(share, jnp.float32)]
+        + [jax.ShapeDtypeStruct(share, jnp.bfloat16)] * 3,
+        in_specs=[SMEM] * 2 + [VMEM] * 5 + [pl.BlockSpec(memory_space=pl.ANY)] * 6,
+        out_specs=[VMEM] * 4,
+        scratch_shapes=[pltpu.VMEM(array.shape, array.dtype) for array in large]
+        + [
+            pltpu.VMEM((rows, head_dim), jnp.bfloat16),
+            pltpu.VMEM((rows, head_dim), jnp.float32),
+            pltpu.VMEM((rows, head_dim), jnp.float32),
+            pltpu.VMEM((rows, head_dim), jnp.float32),
+            pltpu.VMEM((tokens, q_weight.shape[1]), jnp.float32),
+            pltpu.VMEM((tokens, width), jnp.float32),
+            pltpu.VMEM((1, POOL * PAGE), jnp.int32),
+            pltpu.VMEM((decode_rows, POOL * PAGE), jnp.float32),
+            pltpu.SMEM((POOL,), jnp.int32),
+            pltpu.SMEM((POOL,), jnp.int32),
+            pltpu.SemaphoreType.DMA((6,)),
+        ],
+        compiler_params=pltpu.CompilerParams(vmem_limit_bytes=24 * 1024 * 1024),
+        name="attention",
+    )(
+        cache_len, page_table, x_full, norm_in_gain[None, :], frequency, q_gain[None, :],
+        k_gain[None, :], *large,
+    )
+
+
 def pack_kernel(
-    place_ref, own_ref, near_ref, far_ref, cross_ref, x_ref, gain_ref, ids_ref, routes_ref,
+    own_ref, near_ref, far_ref, cross_ref, x_ref, gain_ref, ids_ref, routes_ref,
     rows_ref, keep_ref, near_out, far_out, cross_out, residual_ref, spread_ref,
 ):
-    tp_index = place_ref[1]
+    tp_index = lax.axis_index("tp")
     share_rows, width = own_ref.shape
     share_width = keep_ref.shape[1]
     mine = pl.ds(pl.multiple_of(tp_index * share_rows, share_rows), share_rows)
@@ -178,15 +367,15 @@
         out_ref[...] = residual_ref[:, pl.ds(column, share_width)]
 
 
-def experts_kernel(far_parts, place_ref, *refs):
+def experts_kernel(far_parts, *refs):
     near_ref, core_ref = refs[:2]
     far_refs, far_core_refs = refs[2 : 2 + far_parts], refs[2 + far_parts : 2 + 2 * far_parts]
     gate_ref, up_ref, down_ref = refs[2 + 2 * far_parts : 5 + 2 * far_parts]
     out_refs, rows_ref = refs[5 + 2 * far_parts : -1], refs[-1]
-    req_index, tp_index = place_ref[0], place_ref[1]
+    req_index, tp_index = lax.axis_index("req"), lax.axis_index("tp")
     levels, share_rows, _ = near_ref.shape
-    units = gate_ref.shape[2]
     width = gate_ref.shape[1]
+    units = gate_ref.shape[0] // 2
     share_width = width // 4
 
     def pick(parts):
@@ -200,31 +389,34 @@
             rows_ref[pl.ds(pl.multiple_of(start, share_rows), share_rows), :] = value[level]
     spread = rows_ref[:, width:].astype(jnp.float32)
     lane = lax.broadcasted_iota(jnp.int32, spread.shape, 1) % (LANES // 2)
-    acts = []
-    for e in range(2):
-        weight = jnp.sum(jnp.where(lane == 2 * req_index + e, spread, 0.0), axis=1, keepdims=True)
-        gate = jnp.dot(rows_ref[:, :width], gate_ref[e], preferred_element_type=jnp.float32)
-        up = jnp.dot(rows_ref[:, :width], up_ref[e], preferred_element_type=jnp.float32)
-        acts.append((gate / (1.0 + jnp.exp(-gate)) * up * weight).astype(jnp.bfloat16))
+    weights = [
+        jnp.sum(jnp.where(lane == 2 * req_index + e, spread, 0.0), axis=1, keepdims=True)
+        for e in range(2)
+    ]
+    contract = (((1,), (1,)), ((), ()))
+    rows = rows_ref[:, :width]
+    gate = lax.dot_general(rows, gate_ref[...], contract, preferred_element_type=jnp.float32)
+    up = lax.dot_general(rows, up_ref[...], contract, preferred_element_type=jnp.float32)
+    unit = lax.broadcasted_iota(jnp.int32, gate.shape, 1)
+    weight = jnp.where(unit < units, weights[0], weights[1])
+    acts = (gate / (1.0 + jnp.exp(-gate)) * up * weight).astype(jnp.bfloat16)
     for step in range(4):
         column = pl.multiple_of((tp_index ^ step) * share_width, share_width)
         part = jnp.dot(
-            acts[0], down_ref[0, :, pl.ds(column, share_width)], preferred_element_type=jnp.float32
-        ) + jnp.dot(
-            acts[1], down_ref[1, :, pl.ds(column, share_width)], preferred_element_type=jnp.float32
+            acts, down_ref[:, pl.ds(column, share_width)], preferred_element_type=jnp.float32
         )
         target = out_refs[step]
         target[...] = part.reshape(target.shape).astype(target.dtype)
 
 
-def run_experts(place, near, core, far, far_core, gate_weight, up_weight, down_weight):
+def run_experts(near, core, far, far_core, gate_weight, up_weight, down_weight):
     levels, share_rows, packed = near.shape
-    share_width = down_weight.shape[2] // 4
+    share_width = down_weight.shape[1] // 4
     block = pl.BlockSpec((2, share_rows, packed), lambda z: (z, 0, 0))
     fixed = pl.BlockSpec((2, share_rows, packed), lambda z: (0, 0, 0))
     far_spec = block if len(far) == 1 else fixed
     weight_specs = [
-        pl.BlockSpec(w.shape, lambda z: (0, 0, 0), pipeline_mode=pl.Buffered(1))
+        pl.BlockSpec(w.shape, lambda z: (0, 0), pipeline_mode=pl.Buffered(1))
         for w in (gate_weight, up_weight, down_weight)
     ]
     out_shape = (levels, 4 * share_rows, share_width)
@@ -235,18 +427,18 @@
             jax.ShapeDtypeStruct(out_shape, jnp.bfloat16 if step % 2 else jnp.float32)
             for step in range(4)
         ],
-        in_specs=[SMEM, block, block] + [far_spec] * (2 * len(far)) + weight_specs,
+        in_specs=[block, block] + [far_spec] * (2 * len(far)) + weight_specs,
         out_specs=[pl.BlockSpec((2,) + out_shape[1:], lambda z: (z, 0, 0))] * 4,
         scratch_shapes=[pltpu.VMEM((8 * share_rows, packed), jnp.bfloat16)],
         compiler_params=pltpu.CompilerParams(vmem_limit_bytes=VMEM_LIMIT),
         name="experts",
-    )(place, near, core, *far, *far_core, gate_weight, up_weight, down_weight)
+    )(near, core, *far, *far_core, gate_weight, up_weight, down_weight)
 
 
 def finish_kernel(
-    place_ref, own_ref, x_ref, y_ref, z1_ref, z2_ref, z3_ref, keep_ref, near_ref, far_ref, cross_ref, out_ref
-):
-    tp_index = place_ref[1]
+    own_ref, x_ref, y_ref, z1_ref, z2_ref, z3_ref, keep_ref, near_ref, far_ref, cross_ref, out_ref
+):
+    tp_index = lax.axis_index("tp")
     share_rows = keep_ref.shape[0]
     for step, part_ref in enumerate((keep_ref, near_ref, far_ref, cross_ref)):
         rows = pl.ds(pl.multiple_of((tp_index ^ step) * share_rows, share_rows), share_rows)
@@ -260,7 +452,8 @@
 
 def moe_dense(
     x_full,
-    head_part,
+    kept,
+    sent,
     norm_post_gain,
     expert_ids,
     route_weights,
@@ -268,36 +461,33 @@
     up_weight,
     down_weight,
 ):
-    req_index, tp_index = lax.axis_index("req"), lax.axis_index("tp")
     token_count, width = x_full.shape
     share_rows, share_width = token_count // 4, width // 4
-    place = jnp.stack([req_index, tp_index]).astype(jnp.int32)
-
-    def head_rows(bits):
-        return lax.dynamic_slice_in_dim(head_part, (tp_index ^ bits) * share_rows, share_rows, 0)
-
-    received = [flip(head_rows(bits).astype(jnp.bfloat16), "tp", bits) for bits in (1, 2, 3)]
+
+    received = [flip(part, "tp", bits) for bits, part in enumerate(sent, 1)]
     share_f32 = jax.ShapeDtypeStruct((share_rows, share_width), jnp.float32)
     rows, *residuals = pl.pallas_call(
         pack_kernel,
         out_shape=[jax.ShapeDtypeStruct((share_rows, width + LANES), jnp.bfloat16)] + [share_f32] * 4,
-        in_specs=[SMEM] + [VMEM] * 8,
+        in_specs=[VMEM] * 8,
         out_specs=[VMEM] * 5,
         scratch_shapes=[
             pltpu.VMEM((share_rows, width), jnp.float32),
             pltpu.VMEM((token_count, LANES), jnp.float32),
         ],
+        compiler_params=pltpu.CompilerParams(vmem_limit_bytes=8 * 1024 * 1024),
         name="pack_rows",
-    )(place, head_rows(0), *received, x_full, norm_post_gain[None, :], expert_ids.T, route_weights.T)
+    )(kept, *received, x_full, norm_post_gain[None, :], expert_ids.T, route_weights.T)
     residuals = residuals[:1] + [flip(residuals[bits], "tp", bits) for bits in (1, 2, 3)]
     line = jnp.stack([rows] + [flip(rows, "req", 2 * bits) for bits in (1, 2, 3)])
     line_x, line_y = flip(line, "req", 1), flip(line, "tp", 2)
     across = (flip(line_x[:2], "tp", 2), flip(line_y[2:], "req", 1))
     line_core, line_x_core, line_y_core = (flip(part, "tp", 1) for part in (line, line_x, line_y))
     across_core = tuple(flip(part, "tp", 1) for part in across)
-    weights = (gate_weight, up_weight, down_weight)
-    near = run_experts(place, line, line_core, (line_y,), (line_y_core,), *weights)
-    side = run_experts(place, line_x, line_x_core, across, across_core, *weights)
+    gate_up = [w.transpose(0, 2, 1).reshape(-1, width) for w in (gate_weight, up_weight)]
+    weights = (*gate_up, down_weight.reshape(-1, width))
+    near = run_experts(line, line_core, (line_y,), (line_y_core,), *weights)
+    side = run_experts(line_x, line_x_core, across, across_core, *weights)
     keep_00, keep_01, keep_10, keep_11 = (
         (part[2 * y], flip(part[2 * y + 1], "tp", 1)) for part in (near, side) for y in range(2)
     )
@@ -325,10 +515,11 @@
     return pl.pallas_call(
         finish_kernel,
         out_shape=jax.ShapeDtypeStruct((token_count, share_width), jnp.bfloat16),
-        in_specs=[SMEM] + [VMEM] * 10,
+        in_specs=[VMEM] * 10,
         out_specs=VMEM,
+        compiler_params=pltpu.CompilerParams(vmem_limit_bytes=8 * 1024 * 1024),
         name="finish",
-    )(place, both(keep_00, low), from_x[0], from_y[0], *from_z, *residuals)
+    )(both(keep_00, low), from_x[0], from_y[0], *from_z, *residuals)
 
 
 def moe_routed(
@@ -372,6 +563,54 @@
         moe_term.astype(jnp.bfloat16), "tp", scatter_dimension=1, tiled=True
     ).astype(jnp.float32)
     return (residual + moe_share).astype(jnp.bfloat16)
+
+
+def attention_part(
+    x_full,
+    norm_in_gain,
+    q_weight,
+    k_weight,
+    v_weight,
+    q_gain,
+    k_gain,
+    o_weight,
+    key_pages,
+    value_pages,
+    page_table,
+    cache_len,
+):
+    head_dim = q_gain.shape[0]
+    kv_local = key_pages.shape[0]
+    group_size = q_weight.shape[1] // head_dim // kv_local
+    token_count = x_full.shape[0]
+    x_float = x_full.astype(jnp.float32)
+    normed_in = rms_scale(x_float, norm_in_gain).astype(jnp.bfloat16)
+    query_lin = jnp.dot(normed_in, q_weight, preferred_element_type=jnp.float32).reshape(
+        token_count, kv_local * group_size, head_dim
+    )
+    key_lin = jnp.dot(normed_in, k_weight, preferred_element_type=jnp.float32).reshape(
+        token_count, kv_local, head_dim
+    )
+    values_new = (
+        jnp.dot(normed_in, v_weight, preferred_element_type=jnp.float32)
+        .astype(jnp.bfloat16)
+        .reshape(token_count, kv_local, head_dim)
+    )
+    requests, positions = token_layout(cache_len)
+    queries = (
+        rotate(rms_scale(query_lin, q_gain), positions)
+        .astype(jnp.bfloat16)
+        .reshape(token_count, kv_local, group_size, head_dim)
+    )
+    keys_new = rotate(rms_scale(key_lin, k_gain), positions).astype(jnp.bfloat16)
+    slot_owner = page_slots(page_table, cache_len)
+    cache_slots = key_pages.shape[1] * key_pages.shape[2]
+    keys_cache = key_pages.reshape(kv_local, cache_slots, head_dim)
+    values_cache = value_pages.reshape(kv_local, cache_slots, head_dim)
+    attended = attend(
+        queries, keys_new, values_new, keys_cache, values_cache, requests, positions, slot_owner
+    )
+    return jnp.dot(attended, o_weight, preferred_element_type=jnp.float32)
 
 
 def body(
@@ -395,52 +634,28 @@
     down_weight,
 ):
     req_count = lax.axis_size("req")
-    head_dim = q_gain.shape[0]
-    kv_local = key_pages.shape[0]
-    group_size = q_weight.shape[1] // head_dim // kv_local
-    token_count = hidden_in.shape[0]
     x_full = lax.all_gather(hidden_in, "tp", axis=1, tiled=True)
-    x_float = x_full.astype(jnp.float32)
-    normed_in = rms_scale(x_float, norm_in_gain).astype(jnp.bfloat16)
-    query_lin = jnp.dot(normed_in, q_weight, preferred_element_type=jnp.float32).reshape(
-        token_count, kv_local * group_size, head_dim
-    )
-    key_lin = jnp.dot(normed_in, k_weight, preferred_element_type=jnp.float32).reshape(
-        token_count, kv_local, head_dim
-    )
-    values_new = (
-        jnp.dot(normed_in, v_weight, preferred_element_type=jnp.float32)
-        .astype(jnp.bfloat16)
-        .reshape(token_count, kv_local, head_dim)
-    )
-    requests, positions = token_layout(cache_len)
-    queries = (
-        rotate(rms_scale(query_lin, q_gain), positions)
-        .astype(jnp.bfloat16)
-        .reshape(token_count, kv_local, group_size, head_dim)
-    )
-    keys_new = rotate(rms_scale(key_lin, k_gain), positions).astype(jnp.bfloat16)
-    slot_owner = page_slots(page_table, cache_len)
-    cache_slots = key_pages.shape[1] * key_pages.shape[2]
-    keys_cache = key_pages.reshape(kv_local, cache_slots, head_dim)
-    values_cache = value_pages.reshape(kv_local, cache_slots, head_dim)
-    attended = attend(
-        queries, keys_new, values_new, keys_cache, values_cache, requests, positions, slot_owner
-    )
-    head_part = jnp.dot(attended, o_weight, preferred_element_type=jnp.float32)
+    attention = (
+        x_full,
+        norm_in_gain,
+        q_weight,
+        k_weight,
+        v_weight,
+        q_gain,
+        k_gain,
+        o_weight,
+        key_pages,
+        value_pages,
+        page_table,
+        cache_len,
+    )
+    experts = (norm_post_gain, expert_ids, route_weights, gate_weight, up_weight, down_weight)
     expert_count = gate_weight.shape[0] * req_count
     staged = (req_count, lax.axis_size("tp"), gate_weight.shape[0]) == (8, 4, 2)
-    moe_layer = moe_dense if staged and expert_count <= LANES // 2 else moe_routed
-    return moe_layer(
-        x_full,
-        head_part,
-        norm_post_gain,
-        expert_ids,
-        route_weights,
-        gate_weight,
-        up_weight,
-        down_weight,
-    )
+    if staged and expert_count <= LANES // 2:
+        kept, *sent = attention_shares(*attention)
+        return moe_dense(x_full, kept, sent, *experts)
+    return moe_routed(x_full, attention_part(*attention), *experts)
 
 
 def solution(mesh):

time: 154 us -> 135 us (0.88)
  matrix products: 14.1 us -> 0 us
  other arithmetic: 12.8 us -> 0.9 us
  Pallas kernels: 18.7 us -> 27.1 us
  starting transfers between devices: 26.8 us -> 24.6 us
    pallas_call x0 -> x1, Pallas kernels: none -> 18.2 us  [attention_shares(): pl.pallas_call(attention_kernel, out_shape=[jax.ShapeDtypeStruct(share, j...]
    dot_general x7 -> x0, matrix products: 14.1 us -> none  [the longest x1 4.18 us: attend(): jnp.einsum('tkgh,knh->kgtn', queries, keys_cache, preferred_element_type=...]
    pallas_call x2, Pallas kernels: 14.3 us -> 7.85 us  [run_experts(): pl.pallas_call(functools.partial(experts_kernel, len(far)), grid=(levels...]
    reduce_sum x6 -> x0, other arithmetic: 5.81 us -> none  [the longest x1 3.74 us: attend(): jnp.sum(exp_cache, axis=-1, keepdims=True)]
    unnamed x40 -> x36, local copies, waits for them, and re-layouts: 9.42 us -> 12.1 us
    ppermute x31, starting transfers between devices: 26.8 us -> 24.6 us  [flip(): lax.ppermute(value, axis, [(i, i ^ bits) for i in range(lax.axis_size(axi...]
    pallas_call x1, Pallas kernels: 2.26 us -> 0.24 us  [moe_dense(): pl.pallas_call(pack_kernel, out_shape=[jax.ShapeDtypeStruct((share_rows,...]
  transfers between devices with their start and end apart: 31 -> 31, of which waited for: 13 -> 14; matrix products, arithmetic and copies ran while one was open for 7% -> 1% of each run, Pallas kernels for 9% -> 6%
where the time goes in v4:
time: 135 us; the launch traced here: 134 us
  waiting for transfers between devices  60 us (44%)
  Pallas kernels  27.1 us (20%)
  starting transfers between devices  24.6 us (18%)
  local copies, waits for them, and re-layouts  12.2 us (9%)
  blocking collectives  8.84 us (7%)
    ppermute x31, waiting for transfers between devices, flip(): lax.ppermute(value, axis, [(i, i ^ bits) for i in range(lax.axis_size(axi...  60 us
    ppermute x31, starting transfers between devices, flip(): lax.ppermute(value, axis, [(i, i ^ bits) for i in range(lax.axis_size(axi...  24.6 us
    pallas_call x1, Pallas kernels, attention_shares(): pl.pallas_call(attention_kernel, out_shape=[jax.ShapeDtypeStruct(share, j...  18.2 us
    unnamed x36, local copies, waits for them, and re-layouts  12.1 us
    all_gather x1, blocking collectives, body(): x_full = lax.all_gather(hidden_in, 'tp', axis=1, tiled=True)  8.84 us
    pallas_call x2, Pallas kernels, run_experts(): pl.pallas_call(functools.partial(experts_kernel, len(far)), grid=(levels...  7.85 us
  transfers between devices with their start and end apart: 31, of which 14 were waited for; matrix products, arithmetic and copies ran while one was open for 1% of the time, Pallas kernels for 6%

profile of v4, /device:TPU:0, one launch (start us, length us, event | category | flops | bytes accessed | tf_op | source)
XLA Modules:
  0.0 133.7 jit_solution(8215022032813605135)
XLA Ops:
  0.0 8.8 %all_gather.3.x_ref = bf16[128,2048]{1,0:T(8,128)(2,1)S(1)} all-gather(bf16[128,512]{1,0:T(8,128)(2,1)} %param.19), channel_id=1, replica_groups=mesh['req'=8,'tp'=4] {'tp'}, dimensions={1}, use_global_device_ids=true | all-gather | bytes 655360 | tf_op jit(solution)/shard_map/all_gather | solution.py:637
  8.8 1.6 %copy-done.3 = bf16[2048,512]{1,0:T(8,128)(2,1)S(1)} copy-done((bf16[2048,512]{1,0:T(8,128)(2,1)S(1)}, bf16[2048,512]{1,0:T(8,128)(2,1)}, u32[]{:S(2)}) %copy-start.3) | copy-done | bytes 2097176
  10.4 1.6 %copy-done.4 = bf16[512,2048]{1,0:T(8,128)(2,1)S(1)} copy-done((bf16[512,2048]{1,0:T(8,128)(2,1)S(1)}, bf16[512,2048]{1,0:T(8,128)(2,1)}, u32[]{:S(2)}) %copy-start.4) | copy-done | bytes 2097176
  12.0 1.4 %copy-done.5 = bf16[1,48,128,128]{3,2,1,0:T(8,128)(2,1)S(1)} copy-done((bf16[1,48,128,128]{3,2,1,0:T(8,128)(2,1)S(1)}, bf16[1,48,128,128]{3,2,1,0:T(8,128)(2,1)}, u32[]{:S(2)}) %copy-start.5) | copy-done | bytes 1572888
  13.4 1.4 %copy-done.6 = bf16[1,48,128,128]{3,2,1,0:T(8,128)(2,1)S(1)} copy-done((bf16[1,48,128,128]{3,2,1,0:T(8,128)(2,1)S(1)}, bf16[1,48,128,128]{3,2,1,0:T(8,128)(2,1)}, u32[]{:S(2)}) %copy-start.6) | copy-done | bytes 1572888
  14.8 1.0 copy-done.7
  21.0 18.2 %attention.1 = (f32[32,2048]{1,0:T(8,128)S(1)}, bf16[32,2048]{1,0:T(8,128)(2,1)S(1)}, bf16[32,2048]{1,0:T(8,128)(2,1)S(1)}, bf16[32,2048]{1,0:T(8,128)(2,1)S(1)}) custom-call(s32[9]{0:T(128)S(1)} %copy-done.14, s32[9,32]{1,0:T(8,128)S(1)} %copy-done.9, bf16[128,2048]{1,0:T(8,128)(2,1)S(1)} %all_gather.3.x_ref, f32[1,2048]{1,0:T(1,128)S(1)} %bitcast.34, ...), custom_call_target="tpu_custom_call" | custom-call | tf_op jit(solution)/shard_map/attention/pallas_call | solution.py:314
  39.6 1.1 collective-permute-start.1
  41.1 4.8 %collective-permute-done.1.far_ref = bf16[32,2048]{1,0:T(8,128)(2,1)S(1)} collective-permute-done((bf16[32,2048]{1,0:T(8,128)(2,1)S(1)}, bf16[32,2048]{1,0:T(8,128)(2,1)S(1)}, u32[]{:S(2)}, u32[]{:S(2)}) %collective-permute-start.1) | collective-permute-done | bytes 131104 | tf_op jit(solution)/shard_map/ppermute | solution.py:151
  45.9 1.3 collective-permute-done.2.cross_ref
  47.6 3.4 %collective-permute-start.3 = (bf16[32,2176]{1,0:T(8,128)(2,1)S(1)}, bf16[32,2176]{1,0:T(8,128)(2,1)S(1)}, u32[]{:S(2)}, u32[]{:S(2)}) collective-permute-start(bf16[32,2176]{1,0:T(8,128)(2,1)S(1)} %get-tuple-element.26), channel_id=1, source_target_pairs={{0,8},{4,12},{8,0},{12,4},{16,24},{20,28},{24,16},{28,20},{1,9},{5... | collective-permute-start | bytes 417800 | tf_op jit(solution)/shard_map/ppermute | solution.py:151
  51.0 6.9 %collective-permute-done.4 = bf16[32,2176]{1,0:T(8,128)(2,1)S(1)} collective-permute-done((bf16[32,2176]{1,0:T(8,128)(2,1)S(1)}, bf16[32,2176]{1,0:T(8,128)(2,1)S(1)}, u32[]{:S(2)}, u32[]{:S(2)}) %collective-permute-start.4) | collective-permute-done | bytes 139296 | tf_op jit(solution)/shard_map/ppermute | solution.py:151
  57.9 2.6 %collective-permute-done.3 = bf16[32,2176]{1,0:T(8,128)(2,1)S(1)} collective-permute-done((bf16[32,2176]{1,0:T(8,128)(2,1)S(1)}, bf16[32,2176]{1,0:T(8,128)(2,1)S(1)}, u32[]{:S(2)}, u32[]{:S(2)}) %collective-permute-start.3) | collective-permute-done | bytes 139296 | tf_op jit(solution)/shard_map/ppermute | solution.py:151
  60.7 1.6 %collective-permute-start.10 = (bf16[4,32,2176]{2,1,0:T(8,128)(2,1)S(1)}, bf16[4,32,2176]{2,1,0:T(8,128)(2,1)S(1)}, u32[]{:S(2)}, u32[]{:S(2)}) collective-permute-start(bf16[4,32,2176]{2,1,0:T(8,128)(2,1)S(1)} %pad_maximum_fusion.refs_0_), channel_id=1, source_target_pairs={{0,4},{4,0},{8,12},{12,8},{16,20},{20,16},{24,28},{28,24},{1,5},{5... | collective-permute-start | bytes 1671176 | tf_op jit(solution)/shard_map/ppermute | solution.py:151
  62.2 1.1 collective-permute-start.7
  63.3 12.0 %collective-permute-done.10.refs_0_ = bf16[4,32,2176]{2,1,0:T(8,128)(2,1)S(1)} collective-permute-done((bf16[4,32,2176]{2,1,0:T(8,128)(2,1)S(1)}, bf16[4,32,2176]{2,1,0:T(8,128)(2,1)S(1)}, u32[]{:S(2)}, u32[]{:S(2)}) %collective-permute-start.10) | collective-permute-done | bytes 557088 | tf_op jit(solution)/shard_map/ppermute | solution.py:151
  75.3 1.2 collective-permute-start.12
  76.6 1.5 %collective-permute-start.13 = (bf16[2,32,2176]{2,1,0:T(8,128)(2,1)S(1)}, bf16[2,32,2176]{2,1,0:T(8,128)(2,1)S(1)}, u32[]{:S(2)}, u32[]{:S(2)}) collective-permute-start(bf16[2,32,2176]{2,1,0:T(8,128)(2,1)S(1)} %slice.114), channel_id=1, source_target_pairs={{0,4},{4,0},{8,12},{12,8},{16,20},{20,16},{24,28},{28,24},{1,5},{5... | collective-permute-start | bytes 835592 | tf_op jit(solution)/shard_map/ppermute | solution.py:151
  78.1 5.1 %collective-permute-done.12.refs_2_ = bf16[2,32,2176]{2,1,0:T(8,128)(2,1)S(1)} collective-permute-done((bf16[2,32,2176]{2,1,0:T(8,128)(2,1)S(1)}, bf16[2,32,2176]{2,1,0:T(8,128)(2,1)S(1)}, u32[]{:S(2)}, u32[]{:S(2)}) %collective-permute-start.12) | collective-permute-done | bytes 278560 | tf_op jit(solution)/shard_map/ppermute | solution.py:151
  83.2 2.5 %collective-permute-done.13.refs_3_ = bf16[2,32,2176]{2,1,0:T(8,128)(2,1)S(1)} collective-permute-done((bf16[2,32,2176]{2,1,0:T(8,128)(2,1)S(1)}, bf16[2,32,2176]{2,1,0:T(8,128)(2,1)S(1)}, u32[]{:S(2)}, u32[]{:S(2)}) %collective-permute-start.13) | collective-permute-done | bytes 278560 | tf_op jit(solution)/shard_map/ppermute | solution.py:151
  87.2 3.9 %experts.3 = (f32[4,128,512]{2,1,0:T(8,128)S(1)}, bf16[4,128,512]{2,1,0:T(8,128)(2,1)S(1)}, f32[4,128,512]{2,1,0:T(8,128)S(1)}, bf16[4,128,512]{2,1,0:T(8,128)(2,1)S(1)}) custom-call(bf16[4,32,2176]{2,1,0:T(8,128)(2,1)S(1)} %collective-permute-done.10.refs_0_, bf16[4,32,2176]{2,1,0:T(8,128)(2,1)S(1)} %collective-permute-done.11.refs_1_, ...), custom_call_target="tpu_custom_call" | custom-call | tf_op jit(solution)/shard_map/experts/pallas_call | solution.py:423
  91.4 3.9 %experts.2 = (f32[4,128,512]{2,1,0:T(8,128)S(1)}, bf16[4,128,512]{2,1,0:T(8,128)(2,1)S(1)}, f32[4,128,512]{2,1,0:T(8,128)S(1)}, bf16[4,128,512]{2,1,0:T(8,128)(2,1)S(1)}) custom-call(bf16[4,32,2176]{2,1,0:T(8,128)(2,1)S(1)} %pad_maximum_fusion.refs_0_, bf16[4,32,2176]{2,1,0:T(8,128)(2,1)S(1)} %collective-permute-done.6.refs_1_, ...), custom_call_target="tpu_custom_call" | custom-call | tf_op jit(solution)/shard_map/experts/pallas_call | solution.py:423
  95.9 1.6 %collective-permute-start.20 = (bf16[2,128,512]{2,1,0:T(8,128)(2,1)S(1)}, bf16[2,128,512]{2,1,0:T(8,128)(2,1)S(1)}, u32[]{:S(2)}, u32[]{:S(2)}) collective-permute-start(bf16[2,128,512]{2,1,0:T(8,128)(2,1)S(1)} %get-tuple-element.45), channel_id=1, source_target_pairs={{0,4},{4,0},{8,12},{12,8},{16,20},{20,16},{24,28},{28,24},{1,5},{5... | collective-permute-start | bytes 786440 | tf_op jit(solution)/shard_map/ppermute | solution.py:151
  98.9 5.4 %collective-permute-done.20 = bf16[2,128,512]{2,1,0:T(8,128)(2,1)S(1)} collective-permute-done((bf16[2,128,512]{2,1,0:T(8,128)(2,1)S(1)}, bf16[2,128,512]{2,1,0:T(8,128)(2,1)S(1)}, u32[]{:S(2)}, u32[]{:S(2)}) %collective-permute-start.20) | collective-permute-done | bytes 262176 | tf_op jit(solution)/shard_map/ppermute | solution.py:151
  105.5 1.1 collective-permute-start.25
  106.8 1.6 %collective-permute-start.17 = (bf16[2,128,512]{2,1,0:T(8,128)(2,1)S(1)}, bf16[2,128,512]{2,1,0:T(8,128)(2,1)S(1)}, u32[]{:S(2)}, u32[]{:S(2)}) collective-permute-start(bf16[2,128,512]{2,1,0:T(8,128)(2,1)S(1)} %get-tuple-element.43), channel_id=1, source_target_pairs={{0,4},{4,0},{8,12},{12,8},{16,20},{20,16},{24,28},{28,24},{1,5},{5... | collective-permute-start | bytes 786440 | tf_op jit(solution)/shard_map/ppermute | solution.py:151
  108.9 4.9 %collective-permute-done.21.y_ref = bf16[2,128,512]{2,1,0:T(8,128)(2,1)S(1)} collective-permute-done((bf16[2,128,512]{2,1,0:T(8,128)(2,1)S(1)}, bf16[2,128,512]{2,1,0:T(8,128)(2,1)S(1)}, u32[]{:S(2)}, u32[]{:S(2)}) %collective-permute-start.21) | collective-permute-done | bytes 262176 | tf_op jit(solution)/shard_map/ppermute | solution.py:151
  114.7 3.7 %collective-permute-done.25 = bf16[2,128,512]{2,1,0:T(8,128)(2,1)S(1)} collective-permute-done((bf16[2,128,512]{2,1,0:T(8,128)(2,1)S(1)}, bf16[2,128,512]{2,1,0:T(8,128)(2,1)S(1)}, u32[]{:S(2)}, u32[]{:S(2)}) %collective-permute-start.25) | collective-permute-done | bytes 262176 | tf_op jit(solution)/shard_map/ppermute | solution.py:151
  118.4 1.1 collective-permute-done.24
  120.1 4.0 %collective-permute-start.27 = (bf16[128,512]{1,0:T(8,128)(2,1)S(1)}, bf16[128,512]{1,0:T(8,128)(2,1)S(1)}, u32[]{:S(2)}, u32[]{:S(2)}) collective-permute-start(bf16[128,512]{1,0:T(8,128)(2,1)S(1)} %get-tuple-element.39), channel_id=1, source_target_pairs={{0,24},{4,28},{8,16},{12,20},{16,8},{20,12},{24,0},{28,4},{1,25},{... | collective-permute-start | bytes 393224 | tf_op jit(solution)/shard_map/ppermute | solution.py:151
  124.2 2.5 %collective-permute-done.22.z1_ref = bf16[128,512]{1,0:T(8,128)(2,1)S(1)} collective-permute-done((bf16[128,512]{1,0:T(8,128)(2,1)S(1)}, bf16[128,512]{1,0:T(8,128)(2,1)S(1)}, u32[]{:S(2)}, u32[]{:S(2)}) %collective-permute-start.22) | collective-permute-done | bytes 131104 | tf_op jit(solution)/shard_map/ppermute | solution.py:151
  126.7 6.3 %collective-permute-done.26.z2_ref = bf16[128,512]{1,0:T(8,128)(2,1)S(1)} collective-permute-done((bf16[128,512]{1,0:T(8,128)(2,1)S(1)}, bf16[128,512]{1,0:T(8,128)(2,1)S(1)}, u32[]{:S(2)}, u32[]{:S(2)}) %collective-permute-start.26) | collective-permute-done | bytes 131104 | tf_op jit(solution)/shard_map/ppermute | solution.py:151
  (80 shorter events, 14.6 us)
Async XLA Ops:
  21.0 66.3 %copy-start.2 = (bf16[2,192,2048]{2,1,0:T(8,128)(2,1)S(1)}, bf16[2,192,2048]{2,1,0:T(8,128)(2,1)}, u32[]{:S(2)}) copy-start(bf16[2,192,2048]{2,1,0:T(8,128)(2,1)} %param.36) | copy-start | bytes 4718596
  39.2 1.9 %collective-permute-start = (bf16[32,2048]{1,0:T(8,128)(2,1)S(1)}, bf16[32,2048]{1,0:T(8,128)(2,1)S(1)}, u32[]{:S(2)}, u32[]{:S(2)}) collective-permute-start(bf16[32,2048]{1,0:T(8,128)(2,1)S(1)} %get-tuple-element.23), channel_id=1, source_target_pairs={{0,1},{1,0},{2,3},{3,2},{4,5},{5,4},{6,7},{7,6},{8,9},{9,8},{10,11... | collective-permute-start | bytes 393224 | tf_op jit(solution)/shard_map/ppermute | solution.py:151
  39.6 6.3 %collective-permute-start.1 = (bf16[32,2048]{1,0:T(8,128)(2,1)S(1)}, bf16[32,2048]{1,0:T(8,128)(2,1)S(1)}, u32[]{:S(2)}, u32[]{:S(2)}) collective-permute-start(bf16[32,2048]{1,0:T(8,128)(2,1)S(1)} %get-tuple-element.24), channel_id=1, source_target_pairs={{0,2},{1,3},{2,0},{3,1},{4,6},{5,7},{6,4},{7,5},{8,10},{9,11},{10,... | collective-permute-start | bytes 393224 | tf_op jit(solution)/shard_map/ppermute | solution.py:151
  40.7 6.5 %collective-permute-start.2 = (bf16[32,2048]{1,0:T(8,128)(2,1)S(1)}, bf16[32,2048]{1,0:T(8,128)(2,1)S(1)}, u32[]{:S(2)}, u32[]{:S(2)}) collective-permute-start(bf16[32,2048]{1,0:T(8,128)(2,1)S(1)} %get-tuple-element.25), channel_id=1, source_target_pairs={{0,3},{1,2},{2,1},{3,0},{4,7},{5,6},{6,5},{7,4},{8,11},{9,10},{10,... | collective-permute-start | bytes 393224 | tf_op jit(solution)/shard_map/ppermute | solution.py:151
  47.5 10.4 %collective-permute-start.4 = (bf16[32,2176]{1,0:T(8,128)(2,1)S(1)}, bf16[32,2176]{1,0:T(8,128)(2,1)S(1)}, u32[]{:S(2)}, u32[]{:S(2)}) collective-permute-start(bf16[32,2176]{1,0:T(8,128)(2,1)S(1)} %get-tuple-element.26), channel_id=1, source_target_pairs={{0,16},{4,20},{8,24},{12,28},{16,0},{20,4},{24,8},{28,12},{1,17},{... | collective-permute-start | bytes 417800 | tf_op jit(solution)/shard_map/ppermute | solution.py:151
  47.6 10.4 %collective-permute-start.5 = (bf16[32,2176]{1,0:T(8,128)(2,1)S(1)}, bf16[32,2176]{1,0:T(8,128)(2,1)S(1)}, u32[]{:S(2)}, u32[]{:S(2)}) collective-permute-start(bf16[32,2176]{1,0:T(8,128)(2,1)S(1)} %get-tuple-element.26), channel_id=1, source_target_pairs={{0,24},{4,28},{8,16},{12,20},{16,8},{20,12},{24,0},{28,4},{1,25},{... | collective-permute-start | bytes 417800 | tf_op jit(solution)/shard_map/ppermute | solution.py:151
  47.6 12.9 %collective-permute-start.3 = (bf16[32,2176]{1,0:T(8,128)(2,1)S(1)}, bf16[32,2176]{1,0:T(8,128)(2,1)S(1)}, u32[]{:S(2)}, u32[]{:S(2)}) collective-permute-start(bf16[32,2176]{1,0:T(8,128)(2,1)S(1)} %get-tuple-element.26), channel_id=1, source_target_pairs={{0,8},{4,12},{8,0},{12,4},{16,24},{20,28},{24,16},{28,20},{1,9},{5... | collective-permute-start | bytes 417800 | tf_op jit(solution)/shard_map/ppermute | solution.py:151
  60.7 14.6 %collective-permute-start.10 = (bf16[4,32,2176]{2,1,0:T(8,128)(2,1)S(1)}, bf16[4,32,2176]{2,1,0:T(8,128)(2,1)S(1)}, u32[]{:S(2)}, u32[]{:S(2)}) collective-permute-start(bf16[4,32,2176]{2,1,0:T(8,128)(2,1)S(1)} %pad_maximum_fusion.refs_0_), channel_id=1, source_target_pairs={{0,4},{4,0},{8,12},{12,8},{16,20},{20,16},{24,28},{28,24},{1,5},{5... | collective-permute-start | bytes 1671176 | tf_op jit(solution)/shard_map/ppermute | solution.py:151
  62.2 14.3 %collective-permute-start.7 = (bf16[4,32,2176]{2,1,0:T(8,128)(2,1)S(1)}, bf16[4,32,2176]{2,1,0:T(8,128)(2,1)S(1)}, u32[]{:S(2)}, u32[]{:S(2)}) collective-permute-start(bf16[4,32,2176]{2,1,0:T(8,128)(2,1)S(1)} %pad_maximum_fusion.refs_0_), channel_id=1, source_target_pairs={{0,2},{1,3},{2,0},{3,1},{4,6},{5,7},{6,4},{7,5},{8,10},{9,11},{10,... | collective-permute-start | bytes 1671176 | tf_op jit(solution)/shard_map/ppermute | solution.py:151
  75.3 7.8 %collective-permute-start.12 = (bf16[2,32,2176]{2,1,0:T(8,128)(2,1)S(1)}, bf16[2,32,2176]{2,1,0:T(8,128)(2,1)S(1)}, u32[]{:S(2)}, u32[]{:S(2)}) collective-permute-start(bf16[2,32,2176]{2,1,0:T(8,128)(2,1)S(1)} %slice.113), channel_id=1, source_target_pairs={{0,2},{1,3},{2,0},{3,1},{4,6},{5,7},{6,4},{7,5},{8,10},{9,11},{10,... | collective-permute-start | bytes 835592 | tf_op jit(solution)/shard_map/ppermute | solution.py:151
  76.5 9.7 %collective-permute-start.11 = (bf16[4,32,2176]{2,1,0:T(8,128)(2,1)S(1)}, bf16[4,32,2176]{2,1,0:T(8,128)(2,1)S(1)}, u32[]{:S(2)}, u32[]{:S(2)}) collective-permute-start(bf16[4,32,2176]{2,1,0:T(8,128)(2,1)S(1)} %collective-permute-done.10.refs_0_), channel_id=1, source_target_pairs={{0,1},{1,0},{2,3},{3,2},{4,5},{5,4},{6,7},{7,6},{8,9},{9,8},{10,11... | collective-permute-start | bytes 1671176 | tf_op jit(solution)/shard_map/ppermute | solution.py:151
  76.6 9.1 %collective-permute-start.13 = (bf16[2,32,2176]{2,1,0:T(8,128)(2,1)S(1)}, bf16[2,32,2176]{2,1,0:T(8,128)(2,1)S(1)}, u32[]{:S(2)}, u32[]{:S(2)}) collective-permute-start(bf16[2,32,2176]{2,1,0:T(8,128)(2,1)S(1)} %slice.114), channel_id=1, source_target_pairs={{0,4},{4,0},{8,12},{12,8},{16,20},{20,16},{24,28},{28,24},{1,5},{5... | collective-permute-start | bytes 835592 | tf_op jit(solution)/shard_map/ppermute | solution.py:151
  83.2 3.0 %collective-permute-start.14 = (bf16[2,32,2176]{2,1,0:T(8,128)(2,1)S(1)}, bf16[2,32,2176]{2,1,0:T(8,128)(2,1)S(1)}, u32[]{:S(2)}, u32[]{:S(2)}) collective-permute-start(bf16[2,32,2176]{2,1,0:T(8,128)(2,1)S(1)} %collective-permute-done.12.refs_2_), channel_id=1, source_target_pairs={{0,1},{1,0},{2,3},{3,2},{4,5},{5,4},{6,7},{7,6},{8,9},{9,8},{10,11... | collective-permute-start | bytes 835592 | tf_op jit(solution)/shard_map/ppermute | solution.py:151
  85.7 1.6 %collective-permute-start.15 = (bf16[2,32,2176]{2,1,0:T(8,128)(2,1)S(1)}, bf16[2,32,2176]{2,1,0:T(8,128)(2,1)S(1)}, u32[]{:S(2)}, u32[]{:S(2)}) collective-permute-start(bf16[2,32,2176]{2,1,0:T(8,128)(2,1)S(1)} %collective-permute-done.13.refs_3_), channel_id=1, source_target_pairs={{0,1},{1,0},{2,3},{3,2},{4,5},{5,4},{6,7},{7,6},{8,9},{9,8},{10,11... | collective-permute-start | bytes 835592 | tf_op jit(solution)/shard_map/ppermute | solution.py:151
  85.7 5.7 %collective-permute-start.6 = (bf16[4,32,2176]{2,1,0:T(8,128)(2,1)S(1)}, bf16[4,32,2176]{2,1,0:T(8,128)(2,1)S(1)}, u32[]{:S(2)}, u32[]{:S(2)}) collective-permute-start(bf16[4,32,2176]{2,1,0:T(8,128)(2,1)S(1)} %pad_maximum_fusion.refs_0_), channel_id=1, source_target_pairs={{0,1},{1,0},{2,3},{3,2},{4,5},{5,4},{6,7},{7,6},{8,9},{9,8},{10,11... | collective-permute-start | bytes 1671176 | tf_op jit(solution)/shard_map/ppermute | solution.py:151
  86.2 5.2 %collective-permute-start.8 = (bf16[4,32,2176]{2,1,0:T(8,128)(2,1)S(1)}, bf16[4,32,2176]{2,1,0:T(8,128)(2,1)S(1)}, u32[]{:S(2)}, u32[]{:S(2)}) collective-permute-start(bf16[4,32,2176]{2,1,0:T(8,128)(2,1)S(1)} %collective-permute-done.7.refs_2_), channel_id=1, source_target_pairs={{0,1},{1,0},{2,3},{3,2},{4,5},{5,4},{6,7},{7,6},{8,9},{9,8},{10,11... | collective-permute-start | bytes 1671176 | tf_op jit(solution)/shard_map/ppermute | solution.py:151
  91.2 4.6 %collective-permute-start.19 = (bf16[4,128,512]{2,1,0:T(8,128)(2,1)S(1)}, bf16[4,128,512]{2,1,0:T(8,128)(2,1)S(1)}, u32[]{:S(2)}, u32[]{:S(2)}) collective-permute-start(bf16[4,128,512]{2,1,0:T(8,128)(2,1)S(1)} %get-tuple-element.34), channel_id=1, source_target_pairs={{0,1},{1,0},{2,3},{3,2},{4,5},{5,4},{6,7},{7,6},{8,9},{9,8},{10,11... | collective-permute-start | bytes 1572872 | tf_op jit(solution)/shard_map/ppermute | solution.py:151
  95.3 3.6 %collective-permute-start.18 = (bf16[4,128,512]{2,1,0:T(8,128)(2,1)S(1)}, bf16[4,128,512]{2,1,0:T(8,128)(2,1)S(1)}, u32[]{:S(2)}, u32[]{:S(2)}) collective-permute-start(bf16[4,128,512]{2,1,0:T(8,128)(2,1)S(1)} %get-tuple-element.32), channel_id=1, source_target_pairs={{0,1},{1,0},{2,3},{3,2},{4,5},{5,4},{6,7},{7,6},{8,9},{9,8},{10,11... | collective-permute-start | bytes 1572872 | tf_op jit(solution)/shard_map/ppermute | solution.py:151
  95.9 8.4 %collective-permute-start.20 = (bf16[2,128,512]{2,1,0:T(8,128)(2,1)S(1)}, bf16[2,128,512]{2,1,0:T(8,128)(2,1)S(1)}, u32[]{:S(2)}, u32[]{:S(2)}) collective-permute-start(bf16[2,128,512]{2,1,0:T(8,128)(2,1)S(1)} %get-tuple-element.45), channel_id=1, source_target_pairs={{0,4},{4,0},{8,12},{12,8},{16,20},{20,16},{24,28},{28,24},{1,5},{5... | collective-permute-start | bytes 786440 | tf_op jit(solution)/shard_map/ppermute | solution.py:151
  97.5 9.1 %collective-permute-start.16 = (bf16[4,128,512]{2,1,0:T(8,128)(2,1)S(1)}, bf16[4,128,512]{2,1,0:T(8,128)(2,1)S(1)}, u32[]{:S(2)}, u32[]{:S(2)}) collective-permute-start(bf16[4,128,512]{2,1,0:T(8,128)(2,1)S(1)} %get-tuple-element.30), channel_id=1, source_target_pairs={{0,1},{1,0},{2,3},{3,2},{4,5},{5,4},{6,7},{7,6},{8,9},{9,8},{10,11... | collective-permute-start | bytes 1572872 | tf_op jit(solution)/shard_map/ppermute | solution.py:151
  97.5 11.4 %collective-permute-start.9 = (bf16[4,128,512]{2,1,0:T(8,128)(2,1)S(1)}, bf16[4,128,512]{2,1,0:T(8,128)(2,1)S(1)}, u32[]{:S(2)}, u32[]{:S(2)}) collective-permute-start(bf16[4,128,512]{2,1,0:T(8,128)(2,1)S(1)} %get-tuple-element.28), channel_id=1, source_target_pairs={{0,1},{1,0},{2,3},{3,2},{4,5},{5,4},{6,7},{7,6},{8,9},{9,8},{10,11... | collective-permute-start | bytes 1572872 | tf_op jit(solution)/shard_map/ppermute | solution.py:151
  98.0 8.6 %collective-permute-start.23 = (bf16[2,128,512]{2,1,0:T(8,128)(2,1)S(1)}, bf16[2,128,512]{2,1,0:T(8,128)(2,1)S(1)}, u32[]{:S(2)}, u32[]{:S(2)}) collective-permute-start(bf16[2,128,512]{2,1,0:T(8,128)(2,1)S(1)} %get-tuple-element.44), channel_id=1, source_target_pairs={{0,2},{1,3},{2,0},{3,1},{4,6},{5,7},{6,4},{7,5},{8,10},{9,11},{10,... | collective-permute-start | bytes 786440 | tf_op jit(solution)/shard_map/ppermute | solution.py:151
  104.5 9.3 %collective-permute-start.21 = (bf16[2,128,512]{2,1,0:T(8,128)(2,1)S(1)}, bf16[2,128,512]{2,1,0:T(8,128)(2,1)S(1)}, u32[]{:S(2)}, u32[]{:S(2)}) collective-permute-start(bf16[2,128,512]{2,1,0:T(8,128)(2,1)S(1)} %get-tuple-element.47), channel_id=1, source_target_pairs={{0,2},{1,3},{2,0},{3,1},{4,6},{5,7},{6,4},{7,5},{8,10},{9,11},{10,... | collective-permute-start | bytes 786440 | tf_op jit(solution)/shard_map/ppermute | solution.py:151
  105.5 12.9 %collective-permute-start.25 = (bf16[2,128,512]{2,1,0:T(8,128)(2,1)S(1)}, bf16[2,128,512]{2,1,0:T(8,128)(2,1)S(1)}, u32[]{:S(2)}, u32[]{:S(2)}) collective-permute-start(bf16[2,128,512]{2,1,0:T(8,128)(2,1)S(1)} %get-tuple-element.46), channel_id=1, source_target_pairs={{0,2},{1,3},{2,0},{3,1},{4,6},{5,7},{6,4},{7,5},{8,10},{9,11},{10,... | collective-permute-start | bytes 786440 | tf_op jit(solution)/shard_map/ppermute | solution.py:151
  106.8 11.6 %collective-permute-start.17 = (bf16[2,128,512]{2,1,0:T(8,128)(2,1)S(1)}, bf16[2,128,512]{2,1,0:T(8,128)(2,1)S(1)}, u32[]{:S(2)}, u32[]{:S(2)}) collective-permute-start(bf16[2,128,512]{2,1,0:T(8,128)(2,1)S(1)} %get-tuple-element.43), channel_id=1, source_target_pairs={{0,4},{4,0},{8,12},{12,8},{16,20},{20,16},{24,28},{28,24},{1,5},{5... | collective-permute-start | bytes 786440 | tf_op jit(solution)/shard_map/ppermute | solution.py:151
  108.4 11.1 %collective-permute-start.24 = (bf16[2,128,512]{2,1,0:T(8,128)(2,1)S(1)}, bf16[2,128,512]{2,1,0:T(8,128)(2,1)S(1)}, u32[]{:S(2)}, u32[]{:S(2)}) collective-permute-start(bf16[2,128,512]{2,1,0:T(8,128)(2,1)S(1)} %get-tuple-element.42), channel_id=1, source_target_pairs={{0,4},{4,0},{8,12},{12,8},{16,20},{20,16},{24,28},{28,24},{1,5},{5... | collective-permute-start | bytes 786440 | tf_op jit(solution)/shard_map/ppermute | solution.py:151
  108.9 11.3 %collective-permute-start.28 = (f32[32,512]{1,0:T(8,128)S(1)}, f32[32,512]{1,0:T(8,128)S(1)}, u32[]{:S(2)}, u32[]{:S(2)}) collective-permute-start(f32[32,512]{1,0:T(8,128)S(1)} %get-tuple-element.36), channel_id=1, source_target_pairs={{0,1},{1,0},{2,3},{3,2},{4,5},{5,4},{6,7},{7,6},{8,9},{9,8},{10,11... | collective-permute-start | bytes 196616 | tf_op jit(solution)/shard_map/ppermute | solution.py:151
  113.8 10.4 %collective-permute-start.29 = (f32[32,512]{1,0:T(8,128)S(1)}, f32[32,512]{1,0:T(8,128)S(1)}, u32[]{:S(2)}, u32[]{:S(2)}) collective-permute-start(f32[32,512]{1,0:T(8,128)S(1)} %get-tuple-element.37), channel_id=1, source_target_pairs={{0,2},{1,3},{2,0},{3,1},{4,6},{5,7},{6,4},{7,5},{8,10},{9,11},{10,... | collective-permute-start | bytes 196616 | tf_op jit(solution)/shard_map/ppermute | solution.py:151
  118.4 5.8 %collective-permute-start.30 = (f32[32,512]{1,0:T(8,128)S(1)}, f32[32,512]{1,0:T(8,128)S(1)}, u32[]{:S(2)}, u32[]{:S(2)}) collective-permute-start(f32[32,512]{1,0:T(8,128)S(1)} %get-tuple-element.38), channel_id=1, source_target_pairs={{0,3},{1,2},{2,1},{3,0},{4,7},{5,6},{6,5},{7,4},{8,11},{9,10},{10,... | collective-permute-start | bytes 196616 | tf_op jit(solution)/shard_map/ppermute | solution.py:151
  119.7 7.0 %collective-permute-start.22 = (bf16[128,512]{1,0:T(8,128)(2,1)S(1)}, bf16[128,512]{1,0:T(8,128)(2,1)S(1)}, u32[]{:S(2)}, u32[]{:S(2)}) collective-permute-start(bf16[128,512]{1,0:T(8,128)(2,1)S(1)} %get-tuple-element.41), channel_id=1, source_target_pairs={{0,8},{4,12},{8,0},{12,4},{16,24},{20,28},{24,16},{28,20},{1,9},{5... | collective-permute-start | bytes 393224 | tf_op jit(solution)/shard_map/ppermute | solution.py:151
  120.1 12.8 %collective-permute-start.26 = (bf16[128,512]{1,0:T(8,128)(2,1)S(1)}, bf16[128,512]{1,0:T(8,128)(2,1)S(1)}, u32[]{:S(2)}, u32[]{:S(2)}) collective-permute-start(bf16[128,512]{1,0:T(8,128)(2,1)S(1)} %get-tuple-element.40), channel_id=1, source_target_pairs={{0,16},{4,20},{8,24},{12,28},{16,0},{20,4},{24,8},{28,12},{1,17},{... | collective-permute-start | bytes 393224 | tf_op jit(solution)/shard_map/ppermute | solution.py:151
  120.1 12.8 %collective-permute-start.27 = (bf16[128,512]{1,0:T(8,128)(2,1)S(1)}, bf16[128,512]{1,0:T(8,128)(2,1)S(1)}, u32[]{:S(2)}, u32[]{:S(2)}) collective-permute-start(bf16[128,512]{1,0:T(8,128)(2,1)S(1)} %get-tuple-element.39), channel_id=1, source_target_pairs={{0,24},{4,28},{8,16},{12,20},{16,8},{20,12},{24,0},{28,4},{1,25},{... | collective-permute-start | bytes 393224 | tf_op jit(solution)/shard_map/ppermute | solution.py:151
  (17 other events, 170.9 us)

commit v5 on v4

--- a/solution.py
+++ b/solution.py
@@ -151,49 +151,42 @@
     return lax.ppermute(value, axis, [(i, i ^ bits) for i in range(lax.axis_size(axis))])
 
 
-def attention_kernel(
-    length_ref, table_ref, x_ref, gain_ref, frequency_ref, q_gain_ref, k_gain_ref,
-    q_hbm, k_hbm, v_hbm, key_hbm, value_hbm, o_hbm,
-    keep_out, near_out, far_out, cross_out,
-    q_ref, k_ref, v_ref, key_ref, value_ref, o_ref, query_ref, run_max, run_sum, run_mix,
-    mixed_ref, part_ref, owner_ref, slots_ref, page_owner, page_live, sems,
-):
-    sources = (q_hbm, k_hbm, v_hbm, key_hbm, value_hbm, o_hbm)
-    targets = (q_ref, k_ref, v_ref, key_ref, value_ref, o_ref)
+def attention_kernel(*refs):
+    pieces, hbm_refs, (keep_out, near_out, far_out, cross_out) = refs[:4], refs[4:16], refs[16:20]
+    local_refs, value_hbm = refs[20:31], hbm_refs[11]
+    (length_ref, table_ref, gain_ref, frequency_ref, q_gain_ref, k_gain_ref) = local_refs[:6]
+    (q_ref, k_ref, v_ref, key_ref, o_ref) = local_refs[6:]
+    (
+        value_ref, x_ref, query_ref, own_scores, top_ref, scores_ref, mix_ref, mixed_ref, part_ref,
+        owner_ref, slots_ref, page_owner, page_live, sems,
+    ) = refs[31:]
+    tokens, head_dim = x_ref.shape[0], k_gain_ref.shape[1]
+    targets = (*local_refs, value_ref.at[:, :, :head_dim])
     copies = [
         pltpu.make_async_copy(source, target, sems.at[i])
-        for i, (source, target) in enumerate(zip(sources, targets))
+        for i, (source, target) in enumerate(zip(hbm_refs, targets))
     ]
     for copy in copies:
         copy.start()
-    tokens, head_dim = x_ref.shape[0], k_gain_ref.shape[1]
+    tp_index = lax.axis_index("tp")
     heads = q_ref.shape[1] // head_dim
     decodes = tokens - PRE
-    for page in range(POOL):
-        page_owner[page] = -1
-        page_live[page] = 0
-    for request in range(1, REQS_DEV):
-
-        def name_page(entry, carry):
-            page = table_ref[request, entry]
-            page_owner[page] = request
-            page_live[page] = jnp.minimum(length_ref[request] - entry * PAGE, PAGE)
-            return carry
-
-        lax.fori_loop(0, (length_ref[request] + PAGE - 1) // PAGE, name_page, 0)
-    slot = lax.broadcasted_iota(jnp.int32, (1, PAGE), 1)
-    for page in range(POOL):
-        owner_ref[:, page * PAGE : (page + 1) * PAGE] = jnp.where(
-            slot < page_live[page], page_owner[page], -1
-        )
+    rows = heads * tokens
+    value_ref[:, :, head_dim:] = jnp.ones((POOL, PAGE, head_dim), jnp.bfloat16)
+    for step, piece in enumerate(pieces):
+        width = piece.shape[1]
+        start = pl.multiple_of((tp_index ^ step) * width, width)
+        x_ref[:, pl.ds(start, width)] = piece[...]
+    for copy in copies[:6]:
+        copy.wait()
     token = lax.broadcasted_iota(jnp.int32, (tokens, head_dim), 0)
     lane = lax.broadcasted_iota(jnp.int32, (tokens, head_dim), 1)
     position = length_ref[0] + token
     for i in range(decodes):
         position = jnp.where(token == PRE + i, length_ref[i + 1], position)
     angle = position.astype(jnp.float32) * frequency_ref[...]
-    cosine = jnp.cos(angle)
-    sine = jnp.where(lane < head_dim // 2, -jnp.sin(angle), jnp.sin(angle))
+    cosine, sine = jnp.cos(angle), jnp.sin(angle)
+    sine = jnp.where(lane < head_dim // 2, -sine, sine)
 
     def turned(values, gain):
         values = rms_scale(values, gain)
@@ -201,16 +194,16 @@
 
     normed = rms_scale(x_ref[...].astype(jnp.float32), gain_ref[...]).astype(jnp.bfloat16)
     contract = (((1,), (1,)), ((), ()))
-    copies[0].wait()
+    for copy in copies[6:9]:
+        copy.wait()
+    key_lin = jnp.dot(normed, k_ref[...], preferred_element_type=jnp.float32)
+    values_new = jnp.dot(normed, v_ref[...], preferred_element_type=jnp.float32).astype(jnp.bfloat16)
     query_lin = jnp.dot(normed, q_ref[...], preferred_element_type=jnp.float32)
-    copies[1].wait()
-    key_lin = jnp.dot(normed, k_ref[...], preferred_element_type=jnp.float32)
-    copies[2].wait()
-    values_new = jnp.dot(normed, v_ref[...], preferred_element_type=jnp.float32).astype(jnp.bfloat16)
     keys_new = turned(key_lin, k_gain_ref[...]).astype(jnp.bfloat16)
+    values_new = jnp.concatenate([values_new, jnp.ones_like(values_new)], axis=1)
     to_log2 = math.log2(math.e) / math.sqrt(head_dim)
     own_mask = (lane == token) | ((lane < token) & (token < PRE))
-    decode_q, decode_max, decode_sum, decode_mix = [], [], [], []
+    decode_query, decode_own = [], []
     for head in range(heads):
         span = slice(head * tokens, (head + 1) * tokens)
         query = turned(query_lin[:, head * head_dim : (head + 1) * head_dim], q_gain_ref[...]) * to_log2
@@ -218,139 +211,162 @@
         query_ref[span, :] = rounded
         scores = lax.dot_general(rounded, keys_new, contract, preferred_element_type=jnp.float32)
         scores = jnp.where(own_mask, scores, -1e30)
-        top = jnp.max(scores, axis=1, keepdims=True)
-        weights = jnp.exp2(scores - top)
-        total = jnp.sum(weights, axis=1, keepdims=True)
-        mix = jnp.dot(weights.astype(jnp.bfloat16), values_new, preferred_element_type=jnp.float32)
-        run_max[span, :] = jnp.broadcast_to(top, mix.shape)
-        run_sum[span, :] = jnp.broadcast_to(total, mix.shape)
-        run_mix[span, :] = mix
-        decode_q.append(query[PRE:])
-        decode_max.append(top[PRE:])
-        decode_sum.append(total[PRE:])
-        decode_mix.append(mix[PRE:])
-    copies[3].wait()
-    copies[4].wait()
-    decode_q = jnp.concatenate(decode_q, axis=0).astype(jnp.bfloat16)
-    decode_max, decode_sum, decode_mix = (
-        jnp.concatenate(part, axis=0) for part in (decode_max, decode_sum, decode_mix)
-    )
-    row_request = 1 + lax.broadcasted_iota(jnp.int32, (heads * decodes, 1), 0) % decodes
-    top = decode_max
-    width = 8 * PAGE
-    for start in range(0, POOL * PAGE, width):
-        keys = key_ref[start // PAGE : (start + width) // PAGE].reshape(width, head_dim)
-        scores = lax.dot_general(decode_q, keys, contract, preferred_element_type=jnp.float32)
-        scores = jnp.where(owner_ref[:, start : start + width] == row_request, scores, -1e30)
-        slots_ref[:, start : start + width] = scores
-        top = jnp.maximum(top, jnp.max(scores, axis=1, keepdims=True))
-    scale = jnp.exp2(decode_max - top)
-    total = decode_sum * scale
-    mix = decode_mix * scale
-    for start in range(0, POOL * PAGE, width):
-        weights = jnp.exp2(slots_ref[:, start : start + width] - top)
-        total = total + jnp.sum(weights, axis=1, keepdims=True)
-        values = value_ref[start // PAGE : (start + width) // PAGE].reshape(width, head_dim)
-        mix = mix + jnp.dot(weights.astype(jnp.bfloat16), values, preferred_element_type=jnp.float32)
-    decoded = mix / total
-    pages = 4
+        own_scores[span, :] = scores
+        top_ref[span, :] = scores
+        decode_query.append(query[PRE:])
+        decode_own.append(scores[PRE:])
+    decode_query = jnp.concatenate(decode_query, axis=0).astype(jnp.bfloat16)
+    decode_own = jnp.concatenate(decode_own, axis=0)
+    for page in range(POOL):
+        page_owner[page] = -1
+        page_live[page] = 0
+    for request in range(1, REQS_DEV):
+
+        def name_page(entry, carry):
+            page = table_ref[request, entry]
+            page_owner[page] = request
+            page_live[page] = jnp.minimum(length_ref[request] - entry * PAGE, PAGE)
+            return carry
+
+        lax.fori_loop(0, (length_ref[request] + PAGE - 1) // PAGE, name_page, 0)
+    slot = lax.broadcasted_iota(jnp.int32, (1, PAGE), 1)
+    for page in range(POOL):
+        owner_ref[:, page * PAGE : (page + 1) * PAGE] = jnp.where(
+            slot < page_live[page], page_owner[page], -1
+        )
+    copies[9].wait()
+    pages = scores_ref.shape[2] // PAGE
     width = pages * PAGE
     length = length_ref[0]
+    steps = (length + width - 1) // width
     column = lax.broadcasted_iota(jnp.int32, (1, width), 1)
 
-    def prefill(step, carry):
+    def named(ref, step):
         names = [table_ref[0, jnp.minimum(step * pages + i, MAXPG - 1)] for i in range(pages)]
-        keys = jnp.concatenate([key_ref[name] for name in names], axis=0)
-        values = jnp.concatenate([value_ref[name] for name in names], axis=0)
-        live = column + step * width < length
-        for head in range(heads):
-            span = slice(head * tokens, (head + 1) * tokens)
-            scores = lax.dot_general(
-                query_ref[span, :], keys, contract, preferred_element_type=jnp.float32
-            )
-            scores = jnp.where(live, scores, -1e30)
-            before = run_max[span, :1]
-            top = jnp.maximum(before, jnp.max(scores, axis=1, keepdims=True))
-            scale = jnp.exp2(before - top)
-            weights = jnp.exp2(scores - top)
-            total = run_sum[span, :1] * scale + jnp.sum(weights, axis=1, keepdims=True)
-            mix = run_mix[span, :] * scale + jnp.dot(
-                weights.astype(jnp.bfloat16), values, preferred_element_type=jnp.float32
-            )
-            run_max[span, :] = jnp.broadcast_to(top, mix.shape)
-            run_sum[span, :] = jnp.broadcast_to(total, mix.shape)
-            run_mix[span, :] = mix
+        return jnp.concatenate([ref[name] for name in names], axis=0)
+
+    def score(step, carry):
+        scores = lax.dot_general(
+            query_ref[...], named(key_ref, step), contract, preferred_element_type=jnp.float32
+        )
+        scores = jnp.where(column + step * width < length, scores, -1e30)
+        scores_ref[step] = scores
+        top = top_ref[...]
+        for page in range(pages):
+            top = jnp.maximum(top, scores[:, page * PAGE : (page + 1) * PAGE])
+        top_ref[...] = top
         return carry
 
-    lax.fori_loop(0, (length + width - 1) // width, prefill, 0)
+    lax.fori_loop(0, steps, score, 0)
+    row_request = 1 + lax.broadcasted_iota(jnp.int32, (heads * decodes, 1), 0) % decodes
+    top = decode_own
+    span = 8 * PAGE
+    for start in range(0, POOL * PAGE, span):
+        keys = key_ref[start // PAGE : (start + span) // PAGE].reshape(span, head_dim)
+        scores = lax.dot_general(decode_query, keys, contract, preferred_element_type=jnp.float32)
+        scores = jnp.where(owner_ref[:, start : start + span] == row_request, scores, -1e30)
+        slots_ref[:, start : start + span] = scores
+        for page in range(8):
+            top = jnp.maximum(top, scores[:, page * PAGE : (page + 1) * PAGE])
+    top = jnp.max(top, axis=1, keepdims=True)
+    copies[11].wait()
+    decode_mix = jnp.dot(
+        jnp.exp2(decode_own - top).astype(jnp.bfloat16), values_new, preferred_element_type=jnp.float32
+    )
+    for start in range(0, POOL * PAGE, span):
+        weights = jnp.exp2(slots_ref[:, start : start + span] - top).astype(jnp.bfloat16)
+        values = value_ref[start // PAGE : (start + span) // PAGE].reshape(span, 2 * head_dim)
+        decode_mix = decode_mix + jnp.dot(weights, values, preferred_element_type=jnp.float32)
+    decoded = decode_mix[:, :head_dim] / decode_mix[:, head_dim:]
+    top = jnp.max(top_ref[...], axis=1, keepdims=True)
+    top_ref[...] = jnp.broadcast_to(top, top_ref.shape)
+    mix_ref[...] = jnp.dot(
+        jnp.exp2(own_scores[...] - top).astype(jnp.bfloat16), values_new, preferred_element_type=jnp.float32
+    )
+
+    def mix(step, carry):
+        weights = jnp.exp2(scores_ref[step] - top_ref[:, :1]).astype(jnp.bfloat16)
+        mix_ref[...] += jnp.dot(weights, named(value_ref, step), preferred_element_type=jnp.float32)
+        return carry
+
+    lax.fori_loop(0, steps, mix, 0)
     for head in range(heads):
-        span = slice(head * tokens, (head + 1) * tokens)
+        part = mix_ref[head * tokens : (head + 1) * tokens, :]
         columns = slice(head * head_dim, (head + 1) * head_dim)
-        mixed_ref[:, columns] = run_mix[span, :] / run_sum[span, :]
+        mixed_ref[:, columns] = part[:, :head_dim] / part[:, head_dim:]
         mixed_ref[PRE:, columns] = decoded[head * decodes : (head + 1) * decodes]
-    copies[5].wait()
+    copies[10].wait()
     part_ref[...] = jnp.dot(
         mixed_ref[...].astype(jnp.bfloat16), o_ref[...], preferred_element_type=jnp.float32
     )
-    tp_index = lax.axis_index("tp")
     share_rows = keep_out.shape[0]
     for step, out_ref in enumerate((keep_out, near_out, far_out, cross_out)):
-        start = pl.multiple_of((tp_index ^ step) * share_rows, share_rows)
-        out_ref[...] = part_ref[pl.ds(start, share_rows), :].astype(out_ref.dtype)
+        mine = pl.ds(pl.multiple_of((tp_index ^ step) * share_rows, share_rows), share_rows)
+        part = part_ref[mine, :]
+        if step == 0:
+            part = part + x_ref[mine, :].astype(jnp.float32)
+        out_ref[...] = part.astype(out_ref.dtype)
 
 
 def attention_shares(
-    x_full, norm_in_gain, q_weight, k_weight, v_weight, q_gain, k_gain, o_weight,
+    hidden_in, norm_in_gain, q_weight, k_weight, v_weight, q_gain, k_gain, o_weight,
     key_pages, value_pages, page_table, cache_len,
 ):
-    tokens, width = x_full.shape
+    far = flip(hidden_in, "tp", 2)
+    pieces = (hidden_in, flip(hidden_in, "tp", 1), far, flip(far, "tp", 1))
+    tokens, width = hidden_in.shape[0], 4 * hidden_in.shape[1]
     head_dim = q_gain.shape[0]
     rows = q_weight.shape[1] // head_dim * tokens
     decode_rows = rows // tokens * (tokens - PRE)
     half = ROPE_BASE ** (-np.arange(head_dim // 2) / (head_dim // 2))
     frequency = jnp.asarray(np.concatenate([half, half])[None, :], jnp.float32)
-    large = (q_weight, k_weight, v_weight, key_pages[0], value_pages[0], o_weight)
+    scalars = (cache_len, page_table)
+    arrays = (
+        norm_in_gain[None, :], frequency, q_gain[None, :], k_gain[None, :],
+        q_weight, k_weight, v_weight, key_pages[0], o_weight,
+    )
     share = (tokens // 4, width)
+    score_pages = 4
     return pl.pallas_call(
         attention_kernel,
         out_shape=[jax.ShapeDtypeStruct(share, jnp.float32)]
         + [jax.ShapeDtypeStruct(share, jnp.bfloat16)] * 3,
-        in_specs=[SMEM] * 2 + [VMEM] * 5 + [pl.BlockSpec(memory_space=pl.ANY)] * 6,
+        in_specs=[VMEM] * 4 + [pl.BlockSpec(memory_space=pltpu.HBM)] * 12,
         out_specs=[VMEM] * 4,
-        scratch_shapes=[pltpu.VMEM(array.shape, array.dtype) for array in large]
+        scratch_shapes=[pltpu.SMEM(array.shape, array.dtype) for array in scalars]
+        + [pltpu.VMEM(array.shape, array.dtype) for array in arrays]
         + [
+            pltpu.VMEM((POOL, PAGE, 2 * head_dim), jnp.bfloat16),
+            pltpu.VMEM((tokens, width), jnp.bfloat16),
             pltpu.VMEM((rows, head_dim), jnp.bfloat16),
+            pltpu.VMEM((rows, tokens), jnp.float32),
             pltpu.VMEM((rows, head_dim), jnp.float32),
-            pltpu.VMEM((rows, head_dim), jnp.float32),
-            pltpu.VMEM((rows, head_dim), jnp.float32),
+            pltpu.VMEM((MAXPG // score_pages, rows, score_pages * PAGE), jnp.float32),
+            pltpu.VMEM((rows, 2 * head_dim), jnp.float32),
             pltpu.VMEM((tokens, q_weight.shape[1]), jnp.float32),
             pltpu.VMEM((tokens, width), jnp.float32),
             pltpu.VMEM((1, POOL * PAGE), jnp.int32),
             pltpu.VMEM((decode_rows, POOL * PAGE), jnp.float32),
             pltpu.SMEM((POOL,), jnp.int32),
             pltpu.SMEM((POOL,), jnp.int32),
-            pltpu.SemaphoreType.DMA((6,)),
+            pltpu.SemaphoreType.DMA((12,)),
         ],
-        compiler_params=pltpu.CompilerParams(vmem_limit_bytes=24 * 1024 * 1024),
+        compiler_params=pltpu.CompilerParams(vmem_limit_bytes=56 * 1024 * 1024),
         name="attention",
-    )(
-        cache_len, page_table, x_full, norm_in_gain[None, :], frequency, q_gain[None, :],
-        k_gain[None, :], *large,
-    )
+    )(*pieces, *scalars, *arrays, value_pages[0])
 
 
 def pack_kernel(
-    own_ref, near_ref, far_ref, cross_ref, x_ref, gain_ref, ids_ref, routes_ref,
+    own_ref, near_ref, far_ref, cross_ref, gain_ref, ids_ref, routes_ref,
     rows_ref, keep_ref, near_out, far_out, cross_out, residual_ref, spread_ref,
 ):
     tp_index = lax.axis_index("tp")
     share_rows, width = own_ref.shape
     share_width = keep_ref.shape[1]
     mine = pl.ds(pl.multiple_of(tp_index * share_rows, share_rows), share_rows)
-    head_sum = (own_ref[...] + near_ref[...].astype(jnp.float32)) + (
+    residual = (own_ref[...] + near_ref[...].astype(jnp.float32)) + (
         far_ref[...].astype(jnp.float32) + cross_ref[...].astype(jnp.float32)
     )
-    residual = x_ref[mine, :].astype(jnp.float32) + head_sum
     residual_ref[...] = residual
     rows_ref[:, :width] = rms_scale(residual, gain_ref[...]).astype(jnp.bfloat16)
     expert = lax.broadcasted_iota(jnp.int32, (LANES, spread_ref.shape[0]), 0) % (LANES // 2)
@@ -451,7 +467,6 @@
 
 
 def moe_dense(
-    x_full,
     kept,
     sent,
     norm_post_gain,
@@ -461,15 +476,14 @@
     up_weight,
     down_weight,
 ):
-    token_count, width = x_full.shape
-    share_rows, share_width = token_count // 4, width // 4
-
+    share_rows, width = kept.shape
+    token_count, share_width = 4 * share_rows, width // 4
     received = [flip(part, "tp", bits) for bits, part in enumerate(sent, 1)]
     share_f32 = jax.ShapeDtypeStruct((share_rows, share_width), jnp.float32)
     rows, *residuals = pl.pallas_call(
         pack_kernel,
         out_shape=[jax.ShapeDtypeStruct((share_rows, width + LANES), jnp.bfloat16)] + [share_f32] * 4,
-        in_specs=[VMEM] * 8,
+        in_specs=[VMEM] * 7,
         out_specs=[VMEM] * 5,
         scratch_shapes=[
             pltpu.VMEM((share_rows, width), jnp.float32),
@@ -477,16 +491,21 @@
         ],
         compiler_params=pltpu.CompilerParams(vmem_limit_bytes=8 * 1024 * 1024),
         name="pack_rows",
-    )(kept, *received, x_full, norm_post_gain[None, :], expert_ids.T, route_weights.T)
+    )(kept, *received, norm_post_gain[None, :], expert_ids.T, route_weights.T)
     residuals = residuals[:1] + [flip(residuals[bits], "tp", bits) for bits in (1, 2, 3)]
     line = jnp.stack([rows] + [flip(rows, "req", 2 * bits) for bits in (1, 2, 3)])
-    line_x, line_y = flip(line, "req", 1), flip(line, "tp", 2)
-    across = (flip(line_x[:2], "tp", 2), flip(line_y[2:], "req", 1))
-    line_core, line_x_core, line_y_core = (flip(part, "tp", 1) for part in (line, line_x, line_y))
-    across_core = tuple(flip(part, "tp", 1) for part in across)
     gate_up = [w.transpose(0, 2, 1).reshape(-1, width) for w in (gate_weight, up_weight)]
     weights = (*gate_up, down_weight.reshape(-1, width))
+    line_x, line_y, line_core = lax.optimization_barrier(
+        (flip(line, "req", 1), flip(line, "tp", 2), flip(line, "tp", 1))
+    )
+    across = (flip(line_x[:2], "tp", 2), flip(line_y[2:], "req", 1))
+    line_y_core, line_x_core = flip(line_y, "tp", 1), flip(line_x, "tp", 1)
     near = run_experts(line, line_core, (line_y,), (line_y_core,), *weights)
+    near, across, line_x_core, residuals = lax.optimization_barrier(
+        (near, across, line_x_core, residuals)
+    )
+    across_core = tuple(flip(part, "tp", 1) for part in across)
     side = run_experts(line_x, line_x_core, across, across_core, *weights)
     keep_00, keep_01, keep_10, keep_11 = (
         (part[2 * y], flip(part[2 * y + 1], "tp", 1)) for part in (near, side) for y in range(2)
@@ -634,9 +653,7 @@
     down_weight,
 ):
     req_count = lax.axis_size("req")
-    x_full = lax.all_gather(hidden_in, "tp", axis=1, tiled=True)
     attention = (
-        x_full,
         norm_in_gain,
         q_weight,
         k_weight,
@@ -653,9 +670,10 @@
     expert_count = gate_weight.shape[0] * req_count
     staged = (req_count, lax.axis_size("tp"), gate_weight.shape[0]) == (8, 4, 2)
     if staged and expert_count <= LANES // 2:
-        kept, *sent = attention_shares(*attention)
-        return moe_dense(x_full, kept, sent, *experts)
-    return moe_routed(x_full, attention_part(*attention), *experts)
+        kept, *sent = attention_shares(hidden_in, *attention)
+        return moe_dense(kept, sent, *experts)
+    x_full = lax.all_gather(hidden_in, "tp", axis=1, tiled=True)
+    return moe_routed(x_full, attention_part(x_full, *attention), *experts)
 
 
 def solution(mesh):

time: 135 us -> 119 us (0.88)
  local copies, waits for them, and re-layouts: 12.2 us -> 1.65 us
  Pallas kernels: 27.1 us -> 17.5 us
  blocking collectives: 8.84 us -> 0 us
  waiting for transfers between devices: 60 us -> 66.4 us
  starting transfers between devices: 24.6 us -> 30.5 us
    unnamed x36 -> x20, local copies, waits for them, and re-layouts: 12.1 us -> 1.61 us
    pallas_call x1, Pallas kernels: 18.2 us -> 8.71 us  [attention_shares(): pl.pallas_call(attention_kernel, out_shape=[jax.ShapeDtypeStruct(share, j...]
    all_gather x1 -> x0, blocking collectives: 8.84 us -> none  [body(): x_full = lax.all_gather(hidden_in, 'tp', axis=1, tiled=True)]
    ppermute x31 -> x34, waiting for transfers between devices: 60 us -> 66.4 us  [flip(): lax.ppermute(value, axis, [(i, i ^ bits) for i in range(lax.axis_size(axi...]
    ppermute x31 -> x34, starting transfers between devices: 24.6 us -> 30.5 us  [flip(): lax.ppermute(value, axis, [(i, i ^ bits) for i in range(lax.axis_size(axi...]
  transfers between devices with their start and end apart: 31 -> 34, of which waited for: 14 -> 19; matrix products, arithmetic and copies ran while one was open for 1% -> 1% of each run, Pallas kernels for 6% -> 3%
where the time goes in v5:
time: 119 us; the launch traced here: 117 us
  waiting for transfers between devices  66.4 us (56%)
  starting transfers between devices  30.5 us (26%)
  Pallas kernels  17.5 us (15%)
  local copies, waits for them, and re-layouts  1.65 us (1%)
    ppermute x34, waiting for transfers between devices, flip(): lax.ppermute(value, axis, [(i, i ^ bits) for i in range(lax.axis_size(axi...  66.4 us
    ppermute x34, starting transfers between devices, flip(): lax.ppermute(value, axis, [(i, i ^ bits) for i in range(lax.axis_size(axi...  30.5 us
    pallas_call x1, Pallas kernels, attention_shares(): pl.pallas_call(attention_kernel, out_shape=[jax.ShapeDtypeStruct(share, j...  8.71 us
    pallas_call x2, Pallas kernels, run_experts(): pl.pallas_call(functools.partial(experts_kernel, len(far)), grid=(levels...  7.85 us
  transfers between devices with their start and end apart: 34, of which 19 were waited for; matrix products, arithmetic and copies ran while one was open for 1% of the time, Pallas kernels for 3%

profile of v5, /device:TPU:0, one launch (start us, length us, event | category | flops | bytes accessed | tf_op | source)
XLA Modules:
  0.0 117.1 jit_solution(9069061982033511346)
XLA Ops:
  0.0 3.0 %collective-permute-start.1 = (bf16[128,512]{1,0:T(8,128)(2,1)}, bf16[128,512]{1,0:T(8,128)(2,1)S(1)}, u32[]{:S(2)}, u32[]{:S(2)}) collective-permute-start(bf16[128,512]{1,0:T(8,128)(2,1)} %refs_0_.1), channel_id=1, source_target_pairs={{0,2},{1,3},{2,0},{3,1},{4,6},{5,7},{6,4},{7,5},{8,10},{9,11},{10,... | collective-permute-start | bytes 393224 | tf_op jit(solution)/shard_map/ppermute | solution.py:151
  3.0 3.7 %collective-permute-done.1.refs_2_ = bf16[128,512]{1,0:T(8,128)(2,1)S(1)} collective-permute-done((bf16[128,512]{1,0:T(8,128)(2,1)}, bf16[128,512]{1,0:T(8,128)(2,1)S(1)}, u32[]{:S(2)}, u32[]{:S(2)}) %collective-permute-start.1) | collective-permute-done | bytes 131104 | tf_op jit(solution)/shard_map/ppermute | solution.py:151
  6.7 1.3 %collective-permute-done.2.refs_3_ = bf16[128,512]{1,0:T(8,128)(2,1)S(1)} collective-permute-done((bf16[128,512]{1,0:T(8,128)(2,1)S(1)}, bf16[128,512]{1,0:T(8,128)(2,1)S(1)}, u32[]{:S(2)}, u32[]{:S(2)}) %collective-permute-start.2) | collective-permute-done | bytes 131104 | tf_op jit(solution)/shard_map/ppermute | solution.py:151
  8.7 8.7 %attention.1 = (f32[32,2048]{1,0:T(8,128)}, bf16[32,2048]{1,0:T(8,128)(2,1)}, bf16[32,2048]{1,0:T(8,128)(2,1)}, bf16[32,2048]{1,0:T(8,128)(2,1)}) custom-call(bf16[128,512]{1,0:T(8,128)(2,1)} %refs_0_.1, bf16[128,512]{1,0:T(8,128)(2,1)} %copy-done.8, bf16[128,512]{1,0:T(8,128)(2,1)} %copy-done.7, bf16[128,512]{1,0:T(8,128)(2,1)} %copy-done.9, s32[9]{0:T(128)} %refs_4_.1, ...), custom_call_target="tpu_custom_call" | custom-call | tf_op jit(solution)/shard_map/attention/pallas_call | solution.py:330
  17.6 1.8 %collective-permute-start.4 = (bf16[32,2048]{1,0:T(8,128)(2,1)}, bf16[32,2048]{1,0:T(8,128)(2,1)S(1)}, u32[]{:S(2)}, u32[]{:S(2)}) collective-permute-start(bf16[32,2048]{1,0:T(8,128)(2,1)} %get-tuple-element.38), channel_id=1, source_target_pairs={{0,2},{1,3},{2,0},{3,1},{4,6},{5,7},{6,4},{7,5},{8,10},{9,11},{10,... | collective-permute-start | bytes 393224 | tf_op jit(solution)/shard_map/ppermute | solution.py:151
  19.4 4.8 %collective-permute-done.4.far_ref = bf16[32,2048]{1,0:T(8,128)(2,1)S(1)} collective-permute-done((bf16[32,2048]{1,0:T(8,128)(2,1)}, bf16[32,2048]{1,0:T(8,128)(2,1)S(1)}, u32[]{:S(2)}, u32[]{:S(2)}) %collective-permute-start.4) | collective-permute-done | bytes 131104 | tf_op jit(solution)/shard_map/ppermute | solution.py:151
  24.2 1.7 %collective-permute-done.5.cross_ref = bf16[32,2048]{1,0:T(8,128)(2,1)S(1)} collective-permute-done((bf16[32,2048]{1,0:T(8,128)(2,1)}, bf16[32,2048]{1,0:T(8,128)(2,1)S(1)}, u32[]{:S(2)}, u32[]{:S(2)}) %collective-permute-start.5) | collective-permute-done | bytes 131104 | tf_op jit(solution)/shard_map/ppermute | solution.py:151
  27.0 2.9 %collective-permute-start.7 = (bf16[32,2176]{1,0:T(8,128)(2,1)S(1)}, bf16[32,2176]{1,0:T(8,128)(2,1)S(1)}, u32[]{:S(2)}, u32[]{:S(2)}) collective-permute-start(bf16[32,2176]{1,0:T(8,128)(2,1)S(1)} %get-tuple-element.40), channel_id=1, source_target_pairs={{0,16},{4,20},{8,24},{12,28},{16,0},{20,4},{24,8},{28,12},{1,17},{... | collective-permute-start | bytes 417800 | tf_op jit(solution)/shard_map/ppermute | solution.py:151
  29.9 1.3 %collective-permute-start.8 = (bf16[32,2176]{1,0:T(8,128)(2,1)S(1)}, bf16[32,2176]{1,0:T(8,128)(2,1)S(1)}, u32[]{:S(2)}, u32[]{:S(2)}) collective-permute-start(bf16[32,2176]{1,0:T(8,128)(2,1)S(1)} %get-tuple-element.40), channel_id=1, source_target_pairs={{0,24},{4,28},{8,16},{12,20},{16,8},{20,12},{24,0},{28,4},{1,25},{... | collective-permute-start | bytes 417800 | tf_op jit(solution)/shard_map/ppermute | solution.py:151
  31.5 9.0 %collective-permute-done.7 = bf16[32,2176]{1,0:T(8,128)(2,1)S(1)} collective-permute-done((bf16[32,2176]{1,0:T(8,128)(2,1)S(1)}, bf16[32,2176]{1,0:T(8,128)(2,1)S(1)}, u32[]{:S(2)}, u32[]{:S(2)}) %collective-permute-start.7) | collective-permute-done | bytes 139296 | tf_op jit(solution)/shard_map/ppermute | solution.py:151
  41.6 1.6 %collective-permute-start.10 = (bf16[4,32,2176]{2,1,0:T(8,128)(2,1)S(1)}, bf16[4,32,2176]{2,1,0:T(8,128)(2,1)S(1)}, u32[]{:S(2)}, u32[]{:S(2)}) collective-permute-start(bf16[4,32,2176]{2,1,0:T(8,128)(2,1)S(1)} %pad_maximum_fusion.refs_0_), channel_id=1, source_target_pairs={{0,2},{1,3},{2,0},{3,1},{4,6},{5,7},{6,4},{7,5},{8,10},{9,11},{10,... | collective-permute-start | bytes 1671176 | tf_op jit(solution)/shard_map/ppermute | solution.py:151
  43.2 1.5 %collective-permute-start.9 = (bf16[4,32,2176]{2,1,0:T(8,128)(2,1)S(1)}, bf16[4,32,2176]{2,1,0:T(8,128)(2,1)S(1)}, u32[]{:S(2)}, u32[]{:S(2)}) collective-permute-start(bf16[4,32,2176]{2,1,0:T(8,128)(2,1)S(1)} %pad_maximum_fusion.refs_0_), channel_id=1, source_target_pairs={{0,4},{4,0},{8,12},{12,8},{16,20},{20,16},{24,28},{28,24},{1,5},{5... | collective-permute-start | bytes 1671176 | tf_op jit(solution)/shard_map/ppermute | solution.py:151
  44.7 10.4 %collective-permute-done.10.refs_2_ = bf16[4,32,2176]{2,1,0:T(8,128)(2,1)S(1)} collective-permute-done((bf16[4,32,2176]{2,1,0:T(8,128)(2,1)S(1)}, bf16[4,32,2176]{2,1,0:T(8,128)(2,1)S(1)}, u32[]{:S(2)}, u32[]{:S(2)}) %collective-permute-start.10) | collective-permute-done | bytes 557088 | tf_op jit(solution)/shard_map/ppermute | solution.py:151
  55.1 3.2 %collective-permute-done.9.refs_0_ = bf16[4,32,2176]{2,1,0:T(8,128)(2,1)S(1)} collective-permute-done((bf16[4,32,2176]{2,1,0:T(8,128)(2,1)S(1)}, bf16[4,32,2176]{2,1,0:T(8,128)(2,1)S(1)}, u32[]{:S(2)}, u32[]{:S(2)}) %collective-permute-start.9) | collective-permute-done | bytes 557088 | tf_op jit(solution)/shard_map/ppermute | solution.py:151
  59.4 1.5 %collective-permute-start.14 = (bf16[2,32,2176]{2,1,0:T(8,128)(2,1)S(1)}, bf16[2,32,2176]{2,1,0:T(8,128)(2,1)S(1)}, u32[]{:S(2)}, u32[]{:S(2)}) collective-permute-start(bf16[2,32,2176]{2,1,0:T(8,128)(2,1)S(1)} %slice.85), channel_id=1, source_target_pairs={{0,4},{4,0},{8,12},{12,8},{16,20},{20,16},{24,28},{28,24},{1,5},{5... | collective-permute-start | bytes 835592 | tf_op jit(solution)/shard_map/ppermute | solution.py:151
  60.9 1.3 %collective-permute-done.16.near_ref = f32[32,512]{1,0:T(8,128)S(1)} collective-permute-done((f32[32,512]{1,0:T(8,128)S(1)}, f32[32,512]{1,0:T(8,128)S(1)}, u32[]{:S(2)}, u32[]{:S(2)}) %collective-permute-start.16) | collective-permute-done | bytes 65568 | tf_op jit(solution)/shard_map/ppermute | solution.py:151
  62.1 1.5 %collective-permute-start.17 = (f32[32,512]{1,0:T(8,128)S(1)}, f32[32,512]{1,0:T(8,128)S(1)}, u32[]{:S(2)}, u32[]{:S(2)}) collective-permute-start(f32[32,512]{1,0:T(8,128)S(1)} %get-tuple-element.50), channel_id=1, source_target_pairs={{0,2},{1,3},{2,0},{3,1},{4,6},{5,7},{6,4},{7,5},{8,10},{9,11},{10,... | collective-permute-start | bytes 196616 | tf_op jit(solution)/shard_map/ppermute | solution.py:151
  63.7 3.9 %experts.2 = (f32[4,128,512]{2,1,0:T(8,128)S(1)}, bf16[4,128,512]{2,1,0:T(8,128)(2,1)S(1)}, f32[4,128,512]{2,1,0:T(8,128)S(1)}, bf16[4,128,512]{2,1,0:T(8,128)(2,1)S(1)}) custom-call(bf16[4,32,2176]{2,1,0:T(8,128)(2,1)S(1)} %pad_maximum_fusion.refs_0_, bf16[4,32,2176]{2,1,0:T(8,128)(2,1)S(1)} %collective-permute-done.11.refs_1_, ...), custom_call_target="tpu_custom_call" | custom-call | tf_op jit(solution)/shard_map/experts/pallas_call | solution.py:439
  67.6 1.9 %collective-permute-done.17.far_ref = f32[32,512]{1,0:T(8,128)S(1)} collective-permute-done((f32[32,512]{1,0:T(8,128)S(1)}, f32[32,512]{1,0:T(8,128)S(1)}, u32[]{:S(2)}, u32[]{:S(2)}) %collective-permute-start.17) | collective-permute-done | bytes 65568 | tf_op jit(solution)/shard_map/ppermute | solution.py:151
  71.8 3.9 %experts.3 = (f32[4,128,512]{2,1,0:T(8,128)S(1)}, bf16[4,128,512]{2,1,0:T(8,128)(2,1)S(1)}, f32[4,128,512]{2,1,0:T(8,128)S(1)}, bf16[4,128,512]{2,1,0:T(8,128)(2,1)S(1)}) custom-call(bf16[4,32,2176]{2,1,0:T(8,128)(2,1)S(1)} %collective-permute-done.9.refs_0_, bf16[4,32,2176]{2,1,0:T(8,128)(2,1)S(1)} %collective-permute-done.15.refs_1_, ...), custom_call_target="tpu_custom_call" | custom-call | tf_op jit(solution)/shard_map/experts/pallas_call | solution.py:439
  76.3 1.4 %collective-permute-done.25 = bf16[4,128,512]{2,1,0:T(8,128)(2,1)S(1)} collective-permute-done((bf16[4,128,512]{2,1,0:T(8,128)(2,1)S(1)}, bf16[4,128,512]{2,1,0:T(8,128)(2,1)S(1)}, u32[]{:S(2)}, u32[]{:S(2)}) %collective-permute-start.25) | collective-permute-done | bytes 524320 | tf_op jit(solution)/shard_map/ppermute | solution.py:151
  77.8 1.6 %collective-permute-start.26 = (bf16[2,128,512]{2,1,0:T(8,128)(2,1)S(1)}, bf16[2,128,512]{2,1,0:T(8,128)(2,1)S(1)}, u32[]{:S(2)}, u32[]{:S(2)}) collective-permute-start(bf16[2,128,512]{2,1,0:T(8,128)(2,1)S(1)} %get-tuple-element.73), channel_id=1, source_target_pairs={{0,4},{4,0},{8,12},{12,8},{16,20},{20,16},{24,28},{28,24},{1,5},{5... | collective-permute-start | bytes 786440 | tf_op jit(solution)/shard_map/ppermute | solution.py:151
  80.4 6.1 %collective-permute-done.26 = bf16[2,128,512]{2,1,0:T(8,128)(2,1)S(1)} collective-permute-done((bf16[2,128,512]{2,1,0:T(8,128)(2,1)S(1)}, bf16[2,128,512]{2,1,0:T(8,128)(2,1)S(1)}, u32[]{:S(2)}, u32[]{:S(2)}) %collective-permute-start.26) | collective-permute-done | bytes 262176 | tf_op jit(solution)/shard_map/ppermute | solution.py:151
  87.2 1.6 %collective-permute-start.31 = (bf16[2,128,512]{2,1,0:T(8,128)(2,1)S(1)}, bf16[2,128,512]{2,1,0:T(8,128)(2,1)S(1)}, u32[]{:S(2)}, u32[]{:S(2)}) collective-permute-start(bf16[2,128,512]{2,1,0:T(8,128)(2,1)S(1)} %get-tuple-element.74), channel_id=1, source_target_pairs={{0,2},{1,3},{2,0},{3,1},{4,6},{5,7},{6,4},{7,5},{8,10},{9,11},{10,... | collective-permute-start | bytes 786440 | tf_op jit(solution)/shard_map/ppermute | solution.py:151
  89.0 1.6 %collective-permute-start.23 = (bf16[2,128,512]{2,1,0:T(8,128)(2,1)S(1)}, bf16[2,128,512]{2,1,0:T(8,128)(2,1)S(1)}, u32[]{:S(2)}, u32[]{:S(2)}) collective-permute-start(bf16[2,128,512]{2,1,0:T(8,128)(2,1)S(1)} %get-tuple-element.71), channel_id=1, source_target_pairs={{0,4},{4,0},{8,12},{12,8},{16,20},{20,16},{24,28},{28,24},{1,5},{5... | collective-permute-start | bytes 786440 | tf_op jit(solution)/shard_map/ppermute | solution.py:151
  91.1 4.9 %collective-permute-done.27.y_ref = bf16[2,128,512]{2,1,0:T(8,128)(2,1)S(1)} collective-permute-done((bf16[2,128,512]{2,1,0:T(8,128)(2,1)S(1)}, bf16[2,128,512]{2,1,0:T(8,128)(2,1)S(1)}, u32[]{:S(2)}, u32[]{:S(2)}) %collective-permute-start.27) | collective-permute-done | bytes 262176 | tf_op jit(solution)/shard_map/ppermute | solution.py:151
  96.0 4.2 %collective-permute-done.31 = bf16[2,128,512]{2,1,0:T(8,128)(2,1)S(1)} collective-permute-done((bf16[2,128,512]{2,1,0:T(8,128)(2,1)S(1)}, bf16[2,128,512]{2,1,0:T(8,128)(2,1)S(1)}, u32[]{:S(2)}, u32[]{:S(2)}) %collective-permute-start.31) | collective-permute-done | bytes 262176 | tf_op jit(solution)/shard_map/ppermute | solution.py:151
  100.1 1.7 %collective-permute-done.30 = bf16[2,128,512]{2,1,0:T(8,128)(2,1)S(1)} collective-permute-done((bf16[2,128,512]{2,1,0:T(8,128)(2,1)S(1)}, bf16[2,128,512]{2,1,0:T(8,128)(2,1)S(1)}, u32[]{:S(2)}, u32[]{:S(2)}) %collective-permute-start.30) | collective-permute-done | bytes 262176 | tf_op jit(solution)/shard_map/ppermute | solution.py:151
  102.1 2.4 %collective-permute-start.28 = (bf16[128,512]{1,0:T(8,128)(2,1)S(1)}, bf16[128,512]{1,0:T(8,128)(2,1)S(1)}, u32[]{:S(2)}, u32[]{:S(2)}) collective-permute-start(bf16[128,512]{1,0:T(8,128)(2,1)S(1)} %get-tuple-element.69), channel_id=1, source_target_pairs={{0,8},{4,12},{8,0},{12,4},{16,24},{20,28},{24,16},{28,20},{1,9},{5... | collective-permute-start | bytes 393224 | tf_op jit(solution)/shard_map/ppermute | solution.py:151
  104.5 2.0 %collective-permute-start.32 = (bf16[128,512]{1,0:T(8,128)(2,1)S(1)}, bf16[128,512]{1,0:T(8,128)(2,1)S(1)}, u32[]{:S(2)}, u32[]{:S(2)}) collective-permute-start(bf16[128,512]{1,0:T(8,128)(2,1)S(1)} %get-tuple-element.68), channel_id=1, source_target_pairs={{0,16},{4,20},{8,24},{12,28},{16,0},{20,4},{24,8},{28,12},{1,17},{... | collective-permute-start | bytes 393224 | tf_op jit(solution)/shard_map/ppermute | solution.py:151
  106.5 1.4 %collective-permute-start.33 = (bf16[128,512]{1,0:T(8,128)(2,1)S(1)}, bf16[128,512]{1,0:T(8,128)(2,1)S(1)}, u32[]{:S(2)}, u32[]{:S(2)}) collective-permute-start(bf16[128,512]{1,0:T(8,128)(2,1)S(1)} %get-tuple-element.67), channel_id=1, source_target_pairs={{0,24},{4,28},{8,16},{12,20},{16,8},{20,12},{24,0},{28,4},{1,25},{... | collective-permute-start | bytes 393224 | tf_op jit(solution)/shard_map/ppermute | solution.py:151
  108.6 7.7 %collective-permute-done.32.z2_ref = bf16[128,512]{1,0:T(8,128)(2,1)S(1)} collective-permute-done((bf16[128,512]{1,0:T(8,128)(2,1)S(1)}, bf16[128,512]{1,0:T(8,128)(2,1)S(1)}, u32[]{:S(2)}, u32[]{:S(2)}) %collective-permute-start.32) | collective-permute-done | bytes 131104 | tf_op jit(solution)/shard_map/ppermute | solution.py:151
  (69 shorter events, 11.5 us)
Async XLA Ops:
  0.0 6.7 %collective-permute-start.1 = (bf16[128,512]{1,0:T(8,128)(2,1)}, bf16[128,512]{1,0:T(8,128)(2,1)S(1)}, u32[]{:S(2)}, u32[]{:S(2)}) collective-permute-start(bf16[128,512]{1,0:T(8,128)(2,1)} %refs_0_.1), channel_id=1, source_target_pairs={{0,2},{1,3},{2,0},{3,1},{4,6},{5,7},{6,4},{7,5},{8,10},{9,11},{10,... | collective-permute-start | bytes 393224 | tf_op jit(solution)/shard_map/ppermute | solution.py:151
  3.0 3.7 %collective-permute-start = (bf16[128,512]{1,0:T(8,128)(2,1)}, bf16[128,512]{1,0:T(8,128)(2,1)S(1)}, u32[]{:S(2)}, u32[]{:S(2)}) collective-permute-start(bf16[128,512]{1,0:T(8,128)(2,1)} %refs_0_.1), channel_id=1, source_target_pairs={{0,1},{1,0},{2,3},{3,2},{4,5},{5,4},{6,7},{7,6},{8,9},{9,8},{10,11... | collective-permute-start | bytes 393224 | tf_op jit(solution)/shard_map/ppermute | solution.py:151
  17.4 2.0 %collective-permute-start.3 = (bf16[32,2048]{1,0:T(8,128)(2,1)}, bf16[32,2048]{1,0:T(8,128)(2,1)S(1)}, u32[]{:S(2)}, u32[]{:S(2)}) collective-permute-start(bf16[32,2048]{1,0:T(8,128)(2,1)} %get-tuple-element.37), channel_id=1, source_target_pairs={{0,1},{1,0},{2,3},{3,2},{4,5},{5,4},{6,7},{7,6},{8,9},{9,8},{10,11... | collective-permute-start | bytes 393224 | tf_op jit(solution)/shard_map/ppermute | solution.py:151
  17.6 6.5 %collective-permute-start.4 = (bf16[32,2048]{1,0:T(8,128)(2,1)}, bf16[32,2048]{1,0:T(8,128)(2,1)S(1)}, u32[]{:S(2)}, u32[]{:S(2)}) collective-permute-start(bf16[32,2048]{1,0:T(8,128)(2,1)} %get-tuple-element.38), channel_id=1, source_target_pairs={{0,2},{1,3},{2,0},{3,1},{4,6},{5,7},{6,4},{7,5},{8,10},{9,11},{10,... | collective-permute-start | bytes 393224 | tf_op jit(solution)/shard_map/ppermute | solution.py:151
  19.4 6.5 %collective-permute-start.5 = (bf16[32,2048]{1,0:T(8,128)(2,1)}, bf16[32,2048]{1,0:T(8,128)(2,1)S(1)}, u32[]{:S(2)}, u32[]{:S(2)}) collective-permute-start(bf16[32,2048]{1,0:T(8,128)(2,1)} %get-tuple-element.39), channel_id=1, source_target_pairs={{0,3},{1,2},{2,1},{3,0},{4,7},{5,6},{6,5},{7,4},{8,11},{9,10},{10,... | collective-permute-start | bytes 393224 | tf_op jit(solution)/shard_map/ppermute | solution.py:151
  27.0 13.5 %collective-permute-start.7 = (bf16[32,2176]{1,0:T(8,128)(2,1)S(1)}, bf16[32,2176]{1,0:T(8,128)(2,1)S(1)}, u32[]{:S(2)}, u32[]{:S(2)}) collective-permute-start(bf16[32,2176]{1,0:T(8,128)(2,1)S(1)} %get-tuple-element.40), channel_id=1, source_target_pairs={{0,16},{4,20},{8,24},{12,28},{16,0},{20,4},{24,8},{28,12},{1,17},{... | collective-permute-start | bytes 417800 | tf_op jit(solution)/shard_map/ppermute | solution.py:151
  29.9 10.6 %collective-permute-start.8 = (bf16[32,2176]{1,0:T(8,128)(2,1)S(1)}, bf16[32,2176]{1,0:T(8,128)(2,1)S(1)}, u32[]{:S(2)}, u32[]{:S(2)}) collective-permute-start(bf16[32,2176]{1,0:T(8,128)(2,1)S(1)} %get-tuple-element.40), channel_id=1, source_target_pairs={{0,24},{4,28},{8,16},{12,20},{16,8},{20,12},{24,0},{28,4},{1,25},{... | collective-permute-start | bytes 417800 | tf_op jit(solution)/shard_map/ppermute | solution.py:151
  31.3 10.2 %collective-permute-start.6 = (bf16[32,2176]{1,0:T(8,128)(2,1)S(1)}, bf16[32,2176]{1,0:T(8,128)(2,1)S(1)}, u32[]{:S(2)}, u32[]{:S(2)}) collective-permute-start(bf16[32,2176]{1,0:T(8,128)(2,1)S(1)} %get-tuple-element.40), channel_id=1, source_target_pairs={{0,8},{4,12},{8,0},{12,4},{16,24},{20,28},{24,16},{28,20},{1,9},{5... | collective-permute-start | bytes 417800 | tf_op jit(solution)/shard_map/ppermute | solution.py:151
  41.6 13.5 %collective-permute-start.10 = (bf16[4,32,2176]{2,1,0:T(8,128)(2,1)S(1)}, bf16[4,32,2176]{2,1,0:T(8,128)(2,1)S(1)}, u32[]{:S(2)}, u32[]{:S(2)}) collective-permute-start(bf16[4,32,2176]{2,1,0:T(8,128)(2,1)S(1)} %pad_maximum_fusion.refs_0_), channel_id=1, source_target_pairs={{0,2},{1,3},{2,0},{3,1},{4,6},{5,7},{6,4},{7,5},{8,10},{9,11},{10,... | collective-permute-start | bytes 1671176 | tf_op jit(solution)/shard_map/ppermute | solution.py:151
  43.2 11.9 %collective-permute-start.11 = (bf16[4,32,2176]{2,1,0:T(8,128)(2,1)S(1)}, bf16[4,32,2176]{2,1,0:T(8,128)(2,1)S(1)}, u32[]{:S(2)}, u32[]{:S(2)}) collective-permute-start(bf16[4,32,2176]{2,1,0:T(8,128)(2,1)S(1)} %pad_maximum_fusion.refs_0_), channel_id=1, source_target_pairs={{0,1},{1,0},{2,3},{3,2},{4,5},{5,4},{6,7},{7,6},{8,9},{9,8},{10,11... | collective-permute-start | bytes 1671176 | tf_op jit(solution)/shard_map/ppermute | solution.py:151
  43.2 15.0 %collective-permute-start.9 = (bf16[4,32,2176]{2,1,0:T(8,128)(2,1)S(1)}, bf16[4,32,2176]{2,1,0:T(8,128)(2,1)S(1)}, u32[]{:S(2)}, u32[]{:S(2)}) collective-permute-start(bf16[4,32,2176]{2,1,0:T(8,128)(2,1)S(1)} %pad_maximum_fusion.refs_0_), channel_id=1, source_target_pairs={{0,4},{4,0},{8,12},{12,8},{16,20},{20,16},{24,28},{28,24},{1,5},{5... | collective-permute-start | bytes 1671176 | tf_op jit(solution)/shard_map/ppermute | solution.py:151
  58.3 5.4 %collective-permute-start.12 = (bf16[4,32,2176]{2,1,0:T(8,128)(2,1)S(1)}, bf16[4,32,2176]{2,1,0:T(8,128)(2,1)S(1)}, u32[]{:S(2)}, u32[]{:S(2)}) collective-permute-start(bf16[4,32,2176]{2,1,0:T(8,128)(2,1)S(1)} %collective-permute-done.10.refs_2_), channel_id=1, source_target_pairs={{0,1},{1,0},{2,3},{3,2},{4,5},{5,4},{6,7},{7,6},{8,9},{9,8},{10,11... | collective-permute-start | bytes 1671176 | tf_op jit(solution)/shard_map/ppermute | solution.py:151
  58.3 11.3 %collective-permute-start.15 = (bf16[4,32,2176]{2,1,0:T(8,128)(2,1)S(1)}, bf16[4,32,2176]{2,1,0:T(8,128)(2,1)S(1)}, u32[]{:S(2)}, u32[]{:S(2)}) collective-permute-start(bf16[4,32,2176]{2,1,0:T(8,128)(2,1)S(1)} %collective-permute-done.9.refs_0_), channel_id=1, source_target_pairs={{0,1},{1,0},{2,3},{3,2},{4,5},{5,4},{6,7},{7,6},{8,9},{9,8},{10,11... | collective-permute-start | bytes 1671176 | tf_op jit(solution)/shard_map/ppermute | solution.py:151
  58.8 10.7 %collective-permute-start.13 = (bf16[2,32,2176]{2,1,0:T(8,128)(2,1)S(1)}, bf16[2,32,2176]{2,1,0:T(8,128)(2,1)S(1)}, u32[]{:S(2)}, u32[]{:S(2)}) collective-permute-start(bf16[2,32,2176]{2,1,0:T(8,128)(2,1)S(1)} %slice.84), channel_id=1, source_target_pairs={{0,2},{1,3},{2,0},{3,1},{4,6},{5,7},{6,4},{7,5},{8,10},{9,11},{10,... | collective-permute-start | bytes 835592 | tf_op jit(solution)/shard_map/ppermute | solution.py:151
  59.4 10.2 %collective-permute-start.14 = (bf16[2,32,2176]{2,1,0:T(8,128)(2,1)S(1)}, bf16[2,32,2176]{2,1,0:T(8,128)(2,1)S(1)}, u32[]{:S(2)}, u32[]{:S(2)}) collective-permute-start(bf16[2,32,2176]{2,1,0:T(8,128)(2,1)S(1)} %slice.85), channel_id=1, source_target_pairs={{0,4},{4,0},{8,12},{12,8},{16,20},{20,16},{24,28},{28,24},{1,5},{5... | collective-permute-start | bytes 835592 | tf_op jit(solution)/shard_map/ppermute | solution.py:151
  62.1 7.4 %collective-permute-start.17 = (f32[32,512]{1,0:T(8,128)S(1)}, f32[32,512]{1,0:T(8,128)S(1)}, u32[]{:S(2)}, u32[]{:S(2)}) collective-permute-start(f32[32,512]{1,0:T(8,128)S(1)} %get-tuple-element.50), channel_id=1, source_target_pairs={{0,2},{1,3},{2,0},{3,1},{4,6},{5,7},{6,4},{7,5},{8,10},{9,11},{10,... | collective-permute-start | bytes 196616 | tf_op jit(solution)/shard_map/ppermute | solution.py:151
  63.7 5.9 %collective-permute-start.18 = (f32[32,512]{1,0:T(8,128)S(1)}, f32[32,512]{1,0:T(8,128)S(1)}, u32[]{:S(2)}, u32[]{:S(2)}) collective-permute-start(f32[32,512]{1,0:T(8,128)S(1)} %get-tuple-element.51), channel_id=1, source_target_pairs={{0,3},{1,2},{2,1},{3,0},{4,7},{5,6},{6,5},{7,4},{8,11},{9,10},{10,... | collective-permute-start | bytes 196616 | tf_op jit(solution)/shard_map/ppermute | solution.py:151
  69.6 1.8 %collective-permute-start.20 = (bf16[2,32,2176]{2,1,0:T(8,128)(2,1)S(1)}, bf16[2,32,2176]{2,1,0:T(8,128)(2,1)S(1)}, u32[]{:S(2)}, u32[]{:S(2)}) collective-permute-start(bf16[2,32,2176]{2,1,0:T(8,128)(2,1)S(1)} %collective-permute-done.13.refs_2_), channel_id=1, source_target_pairs={{0,1},{1,0},{2,3},{3,2},{4,5},{5,4},{6,7},{7,6},{8,9},{9,8},{10,11... | collective-permute-start | bytes 835592 | tf_op jit(solution)/shard_map/ppermute | solution.py:151
  70.2 1.6 %collective-permute-start.21 = (bf16[2,32,2176]{2,1,0:T(8,128)(2,1)S(1)}, bf16[2,32,2176]{2,1,0:T(8,128)(2,1)S(1)}, u32[]{:S(2)}, u32[]{:S(2)}) collective-permute-start(bf16[2,32,2176]{2,1,0:T(8,128)(2,1)S(1)} %collective-permute-done.14.refs_3_), channel_id=1, source_target_pairs={{0,1},{1,0},{2,3},{3,2},{4,5},{5,4},{6,7},{7,6},{8,9},{9,8},{10,11... | collective-permute-start | bytes 835592 | tf_op jit(solution)/shard_map/ppermute | solution.py:151
  75.7 2.0 %collective-permute-start.25 = (bf16[4,128,512]{2,1,0:T(8,128)(2,1)S(1)}, bf16[4,128,512]{2,1,0:T(8,128)(2,1)S(1)}, u32[]{:S(2)}, u32[]{:S(2)}) collective-permute-start(bf16[4,128,512]{2,1,0:T(8,128)(2,1)S(1)} %get-tuple-element.62), channel_id=1, source_target_pairs={{0,1},{1,0},{2,3},{3,2},{4,5},{5,4},{6,7},{7,6},{8,9},{9,8},{10,11... | collective-permute-start | bytes 1572872 | tf_op jit(solution)/shard_map/ppermute | solution.py:151
  76.1 4.3 %collective-permute-start.24 = (bf16[4,128,512]{2,1,0:T(8,128)(2,1)S(1)}, bf16[4,128,512]{2,1,0:T(8,128)(2,1)S(1)}, u32[]{:S(2)}, u32[]{:S(2)}) collective-permute-start(bf16[4,128,512]{2,1,0:T(8,128)(2,1)S(1)} %get-tuple-element.60), channel_id=1, source_target_pairs={{0,1},{1,0},{2,3},{3,2},{4,5},{5,4},{6,7},{7,6},{8,9},{9,8},{10,11... | collective-permute-start | bytes 1572872 | tf_op jit(solution)/shard_map/ppermute | solution.py:151
  77.8 8.7 %collective-permute-start.26 = (bf16[2,128,512]{2,1,0:T(8,128)(2,1)S(1)}, bf16[2,128,512]{2,1,0:T(8,128)(2,1)S(1)}, u32[]{:S(2)}, u32[]{:S(2)}) collective-permute-start(bf16[2,128,512]{2,1,0:T(8,128)(2,1)S(1)} %get-tuple-element.73), channel_id=1, source_target_pairs={{0,4},{4,0},{8,12},{12,8},{16,20},{20,16},{24,28},{28,24},{1,5},{5... | collective-permute-start | bytes 786440 | tf_op jit(solution)/shard_map/ppermute | solution.py:151
  79.4 9.4 %collective-permute-start.22 = (bf16[4,128,512]{2,1,0:T(8,128)(2,1)S(1)}, bf16[4,128,512]{2,1,0:T(8,128)(2,1)S(1)}, u32[]{:S(2)}, u32[]{:S(2)}) collective-permute-start(bf16[4,128,512]{2,1,0:T(8,128)(2,1)S(1)} %get-tuple-element.58), channel_id=1, source_target_pairs={{0,1},{1,0},{2,3},{3,2},{4,5},{5,4},{6,7},{7,6},{8,9},{9,8},{10,11... | collective-permute-start | bytes 1572872 | tf_op jit(solution)/shard_map/ppermute | solution.py:151
  79.5 11.6 %collective-permute-start.19 = (bf16[4,128,512]{2,1,0:T(8,128)(2,1)S(1)}, bf16[4,128,512]{2,1,0:T(8,128)(2,1)S(1)}, u32[]{:S(2)}, u32[]{:S(2)}) collective-permute-start(bf16[4,128,512]{2,1,0:T(8,128)(2,1)S(1)} %get-tuple-element.53), channel_id=1, source_target_pairs={{0,1},{1,0},{2,3},{3,2},{4,5},{5,4},{6,7},{7,6},{8,9},{9,8},{10,11... | collective-permute-start | bytes 1572872 | tf_op jit(solution)/shard_map/ppermute | solution.py:151
  79.9 8.9 %collective-permute-start.29 = (bf16[2,128,512]{2,1,0:T(8,128)(2,1)S(1)}, bf16[2,128,512]{2,1,0:T(8,128)(2,1)S(1)}, u32[]{:S(2)}, u32[]{:S(2)}) collective-permute-start(bf16[2,128,512]{2,1,0:T(8,128)(2,1)S(1)} %get-tuple-element.72), channel_id=1, source_target_pairs={{0,2},{1,3},{2,0},{3,1},{4,6},{5,7},{6,4},{7,5},{8,10},{9,11},{10,... | collective-permute-start | bytes 786440 | tf_op jit(solution)/shard_map/ppermute | solution.py:151
  86.7 9.3 %collective-permute-start.27 = (bf16[2,128,512]{2,1,0:T(8,128)(2,1)S(1)}, bf16[2,128,512]{2,1,0:T(8,128)(2,1)S(1)}, u32[]{:S(2)}, u32[]{:S(2)}) collective-permute-start(bf16[2,128,512]{2,1,0:T(8,128)(2,1)S(1)} %get-tuple-element.75), channel_id=1, source_target_pairs={{0,2},{1,3},{2,0},{3,1},{4,6},{5,7},{6,4},{7,5},{8,10},{9,11},{10,... | collective-permute-start | bytes 786440 | tf_op jit(solution)/shard_map/ppermute | solution.py:151
  87.2 12.9 %collective-permute-start.31 = (bf16[2,128,512]{2,1,0:T(8,128)(2,1)S(1)}, bf16[2,128,512]{2,1,0:T(8,128)(2,1)S(1)}, u32[]{:S(2)}, u32[]{:S(2)}) collective-permute-start(bf16[2,128,512]{2,1,0:T(8,128)(2,1)S(1)} %get-tuple-element.74), channel_id=1, source_target_pairs={{0,2},{1,3},{2,0},{3,1},{4,6},{5,7},{6,4},{7,5},{8,10},{9,11},{10,... | collective-permute-start | bytes 786440 | tf_op jit(solution)/shard_map/ppermute | solution.py:151
  89.0 11.2 %collective-permute-start.23 = (bf16[2,128,512]{2,1,0:T(8,128)(2,1)S(1)}, bf16[2,128,512]{2,1,0:T(8,128)(2,1)S(1)}, u32[]{:S(2)}, u32[]{:S(2)}) collective-permute-start(bf16[2,128,512]{2,1,0:T(8,128)(2,1)S(1)} %get-tuple-element.71), channel_id=1, source_target_pairs={{0,4},{4,0},{8,12},{12,8},{16,20},{20,16},{24,28},{28,24},{1,5},{5... | collective-permute-start | bytes 786440 | tf_op jit(solution)/shard_map/ppermute | solution.py:151
  90.5 11.3 %collective-permute-start.30 = (bf16[2,128,512]{2,1,0:T(8,128)(2,1)S(1)}, bf16[2,128,512]{2,1,0:T(8,128)(2,1)S(1)}, u32[]{:S(2)}, u32[]{:S(2)}) collective-permute-start(bf16[2,128,512]{2,1,0:T(8,128)(2,1)S(1)} %get-tuple-element.70), channel_id=1, source_target_pairs={{0,4},{4,0},{8,12},{12,8},{16,20},{20,16},{24,28},{28,24},{1,5},{5... | collective-permute-start | bytes 786440 | tf_op jit(solution)/shard_map/ppermute | solution.py:151
  102.1 6.5 %collective-permute-start.28 = (bf16[128,512]{1,0:T(8,128)(2,1)S(1)}, bf16[128,512]{1,0:T(8,128)(2,1)S(1)}, u32[]{:S(2)}, u32[]{:S(2)}) collective-permute-start(bf16[128,512]{1,0:T(8,128)(2,1)S(1)} %get-tuple-element.69), channel_id=1, source_target_pairs={{0,8},{4,12},{8,0},{12,4},{16,24},{20,28},{24,16},{28,20},{1,9},{5... | collective-permute-start | bytes 393224 | tf_op jit(solution)/shard_map/ppermute | solution.py:151
  104.5 11.8 %collective-permute-start.32 = (bf16[128,512]{1,0:T(8,128)(2,1)S(1)}, bf16[128,512]{1,0:T(8,128)(2,1)S(1)}, u32[]{:S(2)}, u32[]{:S(2)}) collective-permute-start(bf16[128,512]{1,0:T(8,128)(2,1)S(1)} %get-tuple-element.68), channel_id=1, source_target_pairs={{0,16},{4,20},{8,24},{12,28},{16,0},{20,4},{24,8},{28,12},{1,17},{... | collective-permute-start | bytes 393224 | tf_op jit(solution)/shard_map/ppermute | solution.py:151
  106.5 9.9 %collective-permute-start.33 = (bf16[128,512]{1,0:T(8,128)(2,1)S(1)}, bf16[128,512]{1,0:T(8,128)(2,1)S(1)}, u32[]{:S(2)}, u32[]{:S(2)}) collective-permute-start(bf16[128,512]{1,0:T(8,128)(2,1)S(1)} %get-tuple-element.67), channel_id=1, source_target_pairs={{0,24},{4,28},{8,16},{12,20},{16,8},{20,12},{24,0},{28,4},{1,25},{... | collective-permute-start | bytes 393224 | tf_op jit(solution)/shard_map/ppermute | solution.py:151
  (12 other events, 214.9 us)

commit v6 on v5

--- a/solution.py
+++ b/solution.py
@@ -358,7 +358,7 @@
 
 def pack_kernel(
     own_ref, near_ref, far_ref, cross_ref, gain_ref, ids_ref, routes_ref,
-    rows_ref, keep_ref, near_out, far_out, cross_out, residual_ref, spread_ref,
+    low_ref, high_ref, keep_ref, near_out, far_out, cross_out, residual_ref, spread_ref, rows_ref,
 ):
     tp_index = lax.axis_index("tp")
     share_rows, width = own_ref.shape
@@ -378,6 +378,8 @@
     lane = lax.broadcasted_iota(jnp.int32, spread.shape, 1)
     high = spread.astype(jnp.bfloat16).astype(jnp.float32)
     rows_ref[:, width:] = jnp.where(lane < LANES // 2, high, spread - high).astype(jnp.bfloat16)
+    low_ref[...] = rows_ref[: share_rows // 2, :]
+    high_ref[...] = rows_ref[share_rows // 2 :, :]
     for step, out_ref in enumerate((keep_ref, near_out, far_out, cross_out)):
         column = pl.multiple_of((tp_index ^ step) * share_width, share_width)
         out_ref[...] = residual_ref[:, pl.ds(column, share_width)]
@@ -386,23 +388,19 @@
 def experts_kernel(far_parts, *refs):
     near_ref, core_ref = refs[:2]
     far_refs, far_core_refs = refs[2 : 2 + far_parts], refs[2 + far_parts : 2 + 2 * far_parts]
-    gate_ref, up_ref, down_ref = refs[2 + 2 * far_parts : 5 + 2 * far_parts]
-    out_refs, rows_ref = refs[5 + 2 * far_parts : -1], refs[-1]
+    gate_ref, up_ref, down_ref, keep_ref, send_ref, rows_ref = refs[2 + 2 * far_parts :]
     req_index, tp_index = lax.axis_index("req"), lax.axis_index("tp")
-    levels, share_rows, _ = near_ref.shape
     width = gate_ref.shape[1]
     units = gate_ref.shape[0] // 2
     share_width = width // 4
-
-    def pick(parts):
-        if len(parts) == 1:
-            return parts[0][...]
-        return jnp.where(pl.program_id(0) == 0, parts[0][...], parts[1][...])
-
-    for step, value in enumerate((near_ref[...], core_ref[...], pick(far_refs), pick(far_core_refs))):
-        for level in range(levels):
-            start = (4 * level + (tp_index ^ step)) * share_rows
-            rows_ref[pl.ds(pl.multiple_of(start, share_rows), share_rows), :] = value[level]
+    for step, parts in enumerate(((near_ref,), (core_ref,), far_refs, far_core_refs)):
+        level = 0
+        for part in parts:
+            levels, share_rows, _ = part.shape
+            for i in range(levels):
+                start = (4 * level + (tp_index ^ step)) * share_rows
+                rows_ref[pl.ds(pl.multiple_of(start, share_rows), share_rows), :] = part[i]
+                level += 1
     spread = rows_ref[:, width:].astype(jnp.float32)
     lane = lax.broadcasted_iota(jnp.int32, spread.shape, 1) % (LANES // 2)
     weights = [
@@ -421,49 +419,91 @@
         part = jnp.dot(
             acts, down_ref[:, pl.ds(column, share_width)], preferred_element_type=jnp.float32
         )
-        target = out_refs[step]
-        target[...] = part.reshape(target.shape).astype(target.dtype)
-
-
-def run_experts(near, core, far, far_core, gate_weight, up_weight, down_weight):
+        target = send_ref if step % 2 else keep_ref
+        target[step // 2] = part.reshape(target.shape[1:]).astype(target.dtype)
+
+
+def run_experts(near, core, far, far_core, weights):
     levels, share_rows, packed = near.shape
-    share_width = down_weight.shape[1] // 4
-    block = pl.BlockSpec((2, share_rows, packed), lambda z: (z, 0, 0))
-    fixed = pl.BlockSpec((2, share_rows, packed), lambda z: (0, 0, 0))
-    far_spec = block if len(far) == 1 else fixed
-    weight_specs = [
-        pl.BlockSpec(w.shape, lambda z: (0, 0), pipeline_mode=pl.Buffered(1))
-        for w in (gate_weight, up_weight, down_weight)
-    ]
-    out_shape = (levels, 4 * share_rows, share_width)
+    units, width = weights[2].shape
+    rows = 4 * levels * share_rows
+    out_shape = (2, levels, 4 * share_rows, width // 4)
     return pl.pallas_call(
         functools.partial(experts_kernel, len(far)),
-        grid=(levels // 2,),
         out_shape=[
-            jax.ShapeDtypeStruct(out_shape, jnp.bfloat16 if step % 2 else jnp.float32)
-            for step in range(4)
+            jax.ShapeDtypeStruct(out_shape, jnp.float32),
+            jax.ShapeDtypeStruct(out_shape, jnp.bfloat16),
         ],
-        in_specs=[block, block] + [far_spec] * (2 * len(far)) + weight_specs,
-        out_specs=[pl.BlockSpec((2,) + out_shape[1:], lambda z: (z, 0, 0))] * 4,
-        scratch_shapes=[pltpu.VMEM((8 * share_rows, packed), jnp.bfloat16)],
+        in_specs=[VMEM] * (5 + 2 * len(far)),
+        out_specs=[VMEM] * 2,
+        scratch_shapes=[pltpu.VMEM((rows, packed), jnp.bfloat16)],
         compiler_params=pltpu.CompilerParams(vmem_limit_bytes=VMEM_LIMIT),
+        cost_estimate=pl.CostEstimate(
+            flops=6 * rows * width * units,
+            bytes_accessed=6 * width * units + 5 * rows * width,
+            transcendentals=rows * units,
+        ),
         name="experts",
-    )(near, core, *far, *far_core, gate_weight, up_weight, down_weight)
-
-
-def finish_kernel(
-    own_ref, x_ref, y_ref, z1_ref, z2_ref, z3_ref, keep_ref, near_ref, far_ref, cross_ref, out_ref
-):
+    )(near, core, *far, *far_core, *weights)
+
+
+def finish_kernel(*refs):
     tp_index = lax.axis_index("tp")
-    share_rows = keep_ref.shape[0]
-    for step, part_ref in enumerate((keep_ref, near_ref, far_ref, cross_ref)):
-        rows = pl.ds(pl.multiple_of((tp_index ^ step) * share_rows, share_rows), share_rows)
-        total = own_ref[0, rows, :] + part_ref[...]
-        for extra_ref in (x_ref, y_ref):
-            total = total + extra_ref[0, rows, :].astype(jnp.float32)
-        for extra_ref in (z1_ref, z2_ref, z3_ref):
-            total = total + extra_ref[rows, :].astype(jnp.float32)
-        out_ref[rows, :] = total.astype(jnp.bfloat16)
+    halves, residual_refs, out_ref = (refs[:6], refs[6:12]), refs[12:16], refs[16]
+    count = refs[0].shape[1] // 4
+    for half, (own_ref, x_ref, y_ref, *z_refs) in enumerate(halves):
+        for step, residual_ref in enumerate(residual_refs):
+            index = tp_index ^ step
+            rows = pl.ds(pl.multiple_of(index * count, count), count)
+            total = own_ref[0, rows, :] + residual_ref[half * count : (half + 1) * count, :]
+            for extra_ref in (x_ref, y_ref):
+                total = total + extra_ref[0, rows, :].astype(jnp.float32)
+            for extra_ref in z_refs:
+                total = total + extra_ref[rows, :].astype(jnp.float32)
+            target = pl.ds(pl.multiple_of((2 * index + half) * count, count), count)
+            out_ref[target, :] = total.astype(jnp.bfloat16)
+
+
+def ordered(*values):
+    return lax.optimization_barrier(values)
+
+
+def z_line(rows):
+    return [rows] + [flip(rows, "req", 2 * bits) for bits in (1, 2, 3)]
+
+
+def across_parts(line_x, line_y):
+    return flip(line_x[:2], "tp", 2), flip(line_y[2:], "req", 1)
+
+
+def other_core(parts):
+    return tuple(flip(part, "tp", 1) for part in parts)
+
+
+def with_core(pair):
+    return pair[0], flip(pair[1], "tp", 1)
+
+
+def joined(pair, y):
+    return pair[0][y] + pair[1][y].astype(jnp.float32)
+
+
+def relayed(side):
+    part = joined(side, 1).astype(jnp.bfloat16)
+    return flip(part[:2], "req", 1), flip(part[2:], "tp", 2)
+
+
+def neighbours(near, side, by_x, by_y):
+    to_y, to_x = joined(near, 1), joined(side, 0)
+    to_y = jnp.concatenate([to_y[:2] + by_x.astype(jnp.float32), to_y[2:]])
+    to_x = jnp.concatenate([to_x[:2], to_x[2:] + by_y.astype(jnp.float32)])
+    return flip(to_x.astype(jnp.bfloat16), "req", 1), flip(to_y.astype(jnp.bfloat16), "tp", 2)
+
+
+def z_share(near, from_x, from_y):
+    total = joined(near, 0)
+    sent = (total + from_x.astype(jnp.float32) + from_y.astype(jnp.float32)).astype(jnp.bfloat16)
+    return [total, from_x, from_y] + [flip(sent[bits], "req", 2 * bits) for bits in (1, 2, 3)]
 
 
 def moe_dense(
@@ -480,65 +520,62 @@
     token_count, share_width = 4 * share_rows, width // 4
     received = [flip(part, "tp", bits) for bits, part in enumerate(sent, 1)]
     share_f32 = jax.ShapeDtypeStruct((share_rows, share_width), jnp.float32)
-    rows, *residuals = pl.pallas_call(
+    half_rows = jax.ShapeDtypeStruct((share_rows // 2, width + LANES), jnp.bfloat16)
+    rows_a, rows_b, *residuals = pl.pallas_call(
         pack_kernel,
-        out_shape=[jax.ShapeDtypeStruct((share_rows, width + LANES), jnp.bfloat16)] + [share_f32] * 4,
+        out_shape=[half_rows] * 2 + [share_f32] * 4,
         in_specs=[VMEM] * 7,
-        out_specs=[VMEM] * 5,
+        out_specs=[VMEM] * 6,
         scratch_shapes=[
             pltpu.VMEM((share_rows, width), jnp.float32),
             pltpu.VMEM((token_count, LANES), jnp.float32),
+            pltpu.VMEM((share_rows, width + LANES), jnp.bfloat16),
         ],
         compiler_params=pltpu.CompilerParams(vmem_limit_bytes=8 * 1024 * 1024),
         name="pack_rows",
     )(kept, *received, norm_post_gain[None, :], expert_ids.T, route_weights.T)
-    residuals = residuals[:1] + [flip(residuals[bits], "tp", bits) for bits in (1, 2, 3)]
-    line = jnp.stack([rows] + [flip(rows, "req", 2 * bits) for bits in (1, 2, 3)])
     gate_up = [w.transpose(0, 2, 1).reshape(-1, width) for w in (gate_weight, up_weight)]
     weights = (*gate_up, down_weight.reshape(-1, width))
-    line_x, line_y, line_core = lax.optimization_barrier(
-        (flip(line, "req", 1), flip(line, "tp", 2), flip(line, "tp", 1))
-    )
-    across = (flip(line_x[:2], "tp", 2), flip(line_y[2:], "req", 1))
-    line_y_core, line_x_core = flip(line_y, "tp", 1), flip(line_x, "tp", 1)
-    near = run_experts(line, line_core, (line_y,), (line_y_core,), *weights)
-    near, across, line_x_core, residuals = lax.optimization_barrier(
-        (near, across, line_x_core, residuals)
-    )
-    across_core = tuple(flip(part, "tp", 1) for part in across)
-    side = run_experts(line_x, line_x_core, across, across_core, *weights)
-    keep_00, keep_01, keep_10, keep_11 = (
-        (part[2 * y], flip(part[2 * y + 1], "tp", 1)) for part in (near, side) for y in range(2)
-    )
-
-    def both(pair, levels):
-        return pair[0][levels] + pair[1][levels].astype(jnp.float32)
-
-    low, high = slice(0, 2), slice(2, 4)
-    by_x = flip(both(keep_11, low).astype(jnp.bfloat16), "req", 1).astype(jnp.float32)
-    by_y = flip(both(keep_11, high).astype(jnp.bfloat16), "tp", 2).astype(jnp.float32)
-    from_y = [
-        flip((both(keep_01, low) + by_x).astype(jnp.bfloat16), "tp", 2),
-        flip(both(keep_01, high).astype(jnp.bfloat16), "tp", 2),
-    ]
-    from_x = [
-        flip(both(keep_10, low).astype(jnp.bfloat16), "req", 1),
-        flip((both(keep_10, high) + by_y).astype(jnp.bfloat16), "req", 1),
-    ]
-
-    def level(z):
-        part = from_x[z // 2][z % 2].astype(jnp.float32) + from_y[z // 2][z % 2].astype(jnp.float32)
-        return (both(keep_00, z) + part).astype(jnp.bfloat16)
-
-    from_z = [flip(level(z), "req", 2 * z) for z in (1, 2, 3)]
+    residuals = residuals[:1] + [flip(residuals[bits], "tp", bits) for bits in (1, 2, 3)]
+    line_a, residuals, rows_b = ordered(z_line(rows_a), residuals, rows_b)
+    line_a = jnp.stack(line_a)
+    x_a, y_a, core_a, line_b = ordered(
+        flip(line_a, "req", 1), flip(line_a, "tp", 2), flip(line_a, "tp", 1), z_line(rows_b)
+    )
+    line_b = jnp.stack(line_b)
+    across_a = across_parts(x_a, y_a)
+    x_b, y_b = flip(line_b, "req", 1), flip(line_b, "tp", 2)
+    y_core_a = flip(y_a, "tp", 1)
+    near_a = run_experts(line_a, core_a, (y_a,), (y_core_a,), weights)
+    near_a, across_a, x_b, y_b = ordered(near_a, across_a, x_b, y_b)
+    across_b = across_parts(x_b, y_b)
+    side_a = run_experts(x_a, flip(x_a, "tp", 1), across_a, other_core(across_a), weights)
+    across_b, side_a, near_a, line_b, x_b, y_b = ordered(
+        across_b, side_a, near_a, line_b, x_b, y_b
+    )
+    side_a = with_core(side_a)
+    side_b = run_experts(x_b, flip(x_b, "tp", 1), across_b, other_core(across_b), weights)
+    side_a, side_b, near_a, line_b, y_b = ordered(side_a, side_b, near_a, line_b, y_b)
+    relay_a = relayed(side_a)
+    near_a, side_b = with_core(near_a), with_core(side_b)
+    core_b, y_core_b = other_core((line_b, y_b))
+    near_b = run_experts(line_b, core_b, (y_b,), (y_core_b,), weights)
+    sides_a = neighbours(near_a, side_a, *relay_a)
+    relay_b = relayed(side_b)
+    near_b = with_core(near_b)
+    sides_a, relay_b, near_b = ordered(sides_a, relay_b, near_b)
+    sides_b = neighbours(near_b, side_b, *relay_b)
+    parts_a = z_share(near_a, *sides_a)
+    sides_b, parts_a = ordered(sides_b, parts_a)
+    parts_b = z_share(near_b, *sides_b)
     return pl.pallas_call(
         finish_kernel,
         out_shape=jax.ShapeDtypeStruct((token_count, share_width), jnp.bfloat16),
-        in_specs=[VMEM] * 10,
+        in_specs=[VMEM] * 16,
         out_specs=VMEM,
         compiler_params=pltpu.CompilerParams(vmem_limit_bytes=8 * 1024 * 1024),
         name="finish",
-    )(both(keep_00, low), from_x[0], from_y[0], *from_z, *residuals)
+    )(*parts_a, *parts_b, *residuals)
 
 
 def moe_routed(

time: 119 us -> 123 us (1.034); the launches traced: 117 us -> 123 us
  starting transfers between devices: 30.5 us -> 50.1 us
  waiting for transfers between devices: 66.4 us -> 52.4 us
    ppermute x34 -> x51, starting transfers between devices: 30.5 us -> 50.1 us  [flip(): lax.ppermute(value, axis, [(i, i ^ bits) for i in range(lax.axis_size(axi...]
    ppermute x34 -> x51, waiting for transfers between devices: 66.4 us -> 52.4 us  [flip(): lax.ppermute(value, axis, [(i, i ^ bits) for i in range(lax.axis_size(axi...]
    pallas_call x3 -> x5, Pallas kernels: 8.06 us -> 7.98 us  [the longest x4 7.75 us: run_experts(): pl.pallas_call(functools.partial(experts_kernel, len(far)), out_shape=[ja...]
  transfers between devices with their start and end apart: 34 -> 51, of which waited for: 19 -> 22; matrix products, arithmetic and copies ran while one was open for 1% -> 1% of each run, Pallas kernels for 3% -> 6%
where the time goes in v6:
time: 123 us
  waiting for transfers between devices  52.4 us (43%)
  starting transfers between devices  50.1 us (41%)
  Pallas kernels  17.6 us (14%)
  local copies, waits for them, and re-layouts  1.81 us (1%)
    ppermute x51, waiting for transfers between devices, flip(): lax.ppermute(value, axis, [(i, i ^ bits) for i in range(lax.axis_size(axi...  52.4 us
    ppermute x51, starting transfers between devices, flip(): lax.ppermute(value, axis, [(i, i ^ bits) for i in range(lax.axis_size(axi...  50.1 us
    pallas_call x1, Pallas kernels, attention_shares(): pl.pallas_call(attention_kernel, out_shape=[jax.ShapeDtypeStruct(share, j...  8.9 us
    pallas_call x4, Pallas kernels, run_experts(): pl.pallas_call(functools.partial(experts_kernel, len(far)), out_shape=[ja...  7.75 us
  transfers between devices with their start and end apart: 51, of which 22 were waited for; matrix products, arithmetic and copies ran while one was open for 1% of the time, Pallas kernels for 6%

profile of v6, /device:TPU:0, one launch (start us, length us, event | category | flops | bytes accessed | tf_op | source)
XLA Modules:
  0.0 123.4 jit_solution(6084941967151931379)
XLA Ops:
  0.0 3.0 %collective-permute-start.1 = (bf16[128,512]{1,0:T(8,128)(2,1)}, bf16[128,512]{1,0:T(8,128)(2,1)S(1)}, u32[]{:S(2)}, u32[]{:S(2)}) collective-permute-start(bf16[128,512]{1,0:T(8,128)(2,1)} %refs_0_.1), channel_id=1, source_target_pairs={{0,2},{1,3},{2,0},{3,1},{4,6},{5,7},{6,4},{7,5},{8,10},{9,11},{10,... | collective-permute-start | bytes 393224 | tf_op jit(solution)/shard_map/ppermute | solution.py:151
  3.0 3.7 %collective-permute-done.1.refs_2_ = bf16[128,512]{1,0:T(8,128)(2,1)S(1)} collective-permute-done((bf16[128,512]{1,0:T(8,128)(2,1)}, bf16[128,512]{1,0:T(8,128)(2,1)S(1)}, u32[]{:S(2)}, u32[]{:S(2)}) %collective-permute-start.1) | collective-permute-done | bytes 131104 | tf_op jit(solution)/shard_map/ppermute | solution.py:151
  8.7 8.9 %attention.1 = (f32[32,2048]{1,0:T(8,128)}, bf16[32,2048]{1,0:T(8,128)(2,1)}, bf16[32,2048]{1,0:T(8,128)(2,1)}, bf16[32,2048]{1,0:T(8,128)(2,1)}) custom-call(bf16[128,512]{1,0:T(8,128)(2,1)} %refs_0_.1, bf16[128,512]{1,0:T(8,128)(2,1)} %copy-done.8, bf16[128,512]{1,0:T(8,128)(2,1)} %copy-done.7, bf16[128,512]{1,0:T(8,128)(2,1)} %copy-done.9, s32[9]{0:T(128)} %refs_4_.1, ...), custom_call_target="tpu_custom_call" | custom-call | tf_op jit(solution)/shard_map/attention/pallas_call | solution.py:330
  17.8 1.8 %collective-permute-start.4 = (bf16[32,2048]{1,0:T(8,128)(2,1)}, bf16[32,2048]{1,0:T(8,128)(2,1)S(1)}, u32[]{:S(2)}, u32[]{:S(2)}) collective-permute-start(bf16[32,2048]{1,0:T(8,128)(2,1)} %get-tuple-element.78), channel_id=1, source_target_pairs={{0,2},{1,3},{2,0},{3,1},{4,6},{5,7},{6,4},{7,5},{8,10},{9,11},{10,... | collective-permute-start | bytes 393224 | tf_op jit(solution)/shard_map/ppermute | solution.py:151
  19.6 4.8 %collective-permute-done.4.far_ref = bf16[32,2048]{1,0:T(8,128)(2,1)S(1)} collective-permute-done((bf16[32,2048]{1,0:T(8,128)(2,1)}, bf16[32,2048]{1,0:T(8,128)(2,1)S(1)}, u32[]{:S(2)}, u32[]{:S(2)}) %collective-permute-start.4) | collective-permute-done | bytes 131104 | tf_op jit(solution)/shard_map/ppermute | solution.py:151
  27.7 1.8 %collective-permute-start.6 = (bf16[16,2176]{1,0:T(8,128)(2,1)S(1)}, bf16[16,2176]{1,0:T(8,128)(2,1)S(1)}, u32[]{:S(2)}, u32[]{:S(2)}) collective-permute-start(bf16[16,2176]{1,0:T(8,128)(2,1)S(1)} %get-tuple-element.86), channel_id=1, source_target_pairs={{0,8},{4,12},{8,0},{12,4},{16,24},{20,28},{24,16},{28,20},{1,9},{5... | collective-permute-start | bytes 208904 | tf_op jit(solution)/shard_map/ppermute | solution.py:151
  29.5 5.5 %collective-permute-start.7 = (bf16[16,2176]{1,0:T(8,128)(2,1)S(1)}, bf16[16,2176]{1,0:T(8,128)(2,1)S(1)}, u32[]{:S(2)}, u32[]{:S(2)}) collective-permute-start(bf16[16,2176]{1,0:T(8,128)(2,1)S(1)} %get-tuple-element.86), channel_id=1, source_target_pairs={{0,16},{4,20},{8,24},{12,28},{16,0},{20,4},{24,8},{28,12},{1,17},{... | collective-permute-start | bytes 208904 | tf_op jit(solution)/shard_map/ppermute | solution.py:151
  38.0 2.7 %collective-permute-done.10.refs_14_ = f32[32,512]{1,0:T(8,128)S(1)} collective-permute-done((f32[32,512]{1,0:T(8,128)S(1)}, f32[32,512]{1,0:T(8,128)S(1)}, u32[]{:S(2)}, u32[]{:S(2)}) %collective-permute-start.10) | collective-permute-done | bytes 65568 | tf_op jit(solution)/shard_map/ppermute | solution.py:151
  42.2 1.9 %collective-permute-start.12 = (bf16[4,16,2176]{2,1,0:T(8,128)(2,1)S(1)}, bf16[4,16,2176]{2,1,0:T(8,128)(2,1)S(1)}, u32[]{:S(2)}, u32[]{:S(2)}) collective-permute-start(bf16[4,16,2176]{2,1,0:T(8,128)(2,1)S(1)} %pad_maximum_fusion.refs_0_), channel_id=1, source_target_pairs={{0,4},{4,0},{8,12},{12,8},{16,20},{20,16},{24,28},{28,24},{1,5},{5... | collective-permute-start | bytes 835592 | tf_op jit(solution)/shard_map/ppermute | solution.py:151
  46.7 2.8 %collective-permute-done.15 = bf16[16,2176]{1,0:T(8,128)(2,1)S(1)} collective-permute-done((bf16[16,2176]{1,0:T(8,128)(2,1)S(1)}, bf16[16,2176]{1,0:T(8,128)(2,1)S(1)}, u32[]{:S(2)}, u32[]{:S(2)}) %collective-permute-start.15) | collective-permute-done | bytes 69664 | tf_op jit(solution)/shard_map/ppermute | solution.py:151
  50.7 2.0 %collective-permute-done.16 = bf16[16,2176]{1,0:T(8,128)(2,1)S(1)} collective-permute-done((bf16[16,2176]{1,0:T(8,128)(2,1)S(1)}, bf16[16,2176]{1,0:T(8,128)(2,1)S(1)}, u32[]{:S(2)}, u32[]{:S(2)}) %collective-permute-start.16) | collective-permute-done | bytes 69664 | tf_op jit(solution)/shard_map/ppermute | solution.py:151
  52.7 2.9 %collective-permute-done.17 = bf16[16,2176]{1,0:T(8,128)(2,1)S(1)} collective-permute-done((bf16[16,2176]{1,0:T(8,128)(2,1)S(1)}, bf16[16,2176]{1,0:T(8,128)(2,1)S(1)}, u32[]{:S(2)}, u32[]{:S(2)}) %collective-permute-start.17) | collective-permute-done | bytes 69664 | tf_op jit(solution)/shard_map/ppermute | solution.py:151
  56.3 2.0 %collective-permute-start.22 = (bf16[4,16,2176]{2,1,0:T(8,128)(2,1)S(1)}, bf16[4,16,2176]{2,1,0:T(8,128)(2,1)S(1)}, u32[]{:S(2)}, u32[]{:S(2)}) collective-permute-start(bf16[4,16,2176]{2,1,0:T(8,128)(2,1)S(1)} %pad_maximum_fusion.1.refs_0_), channel_id=1, source_target_pairs={{0,2},{1,3},{2,0},{3,1},{4,6},{5,7},{6,4},{7,5},{8,10},{9,11},{10,... | collective-permute-start | bytes 835592 | tf_op jit(solution)/shard_map/ppermute | solution.py:151
  58.4 2.0 %collective-permute-start.20 = (bf16[2,16,2176]{2,1,0:T(8,128)(2,1)S(1)}, bf16[2,16,2176]{2,1,0:T(8,128)(2,1)S(1)}, u32[]{:S(2)}, u32[]{:S(2)}) collective-permute-start(bf16[2,16,2176]{2,1,0:T(8,128)(2,1)S(1)} %slice.155), channel_id=1, source_target_pairs={{0,4},{4,0},{8,12},{12,8},{16,20},{20,16},{24,28},{28,24},{1,5},{5... | collective-permute-start | bytes 417800 | tf_op jit(solution)/shard_map/ppermute | solution.py:151
  60.4 1.9 %experts.4 = (f32[2,4,64,512]{3,2,1,0:T(8,128)S(1)}, bf16[2,4,64,512]{3,2,1,0:T(8,128)(2,1)S(1)}) custom-call(bf16[4,16,2176]{2,1,0:T(8,128)(2,1)S(1)} %pad_maximum_fusion.refs_0_, bf16[4,16,2176]{2,1,0:T(8,128)(2,1)S(1)} %collective-permute-done.14.refs_1_, bf16[4,16,2176]{2,1,0:T(8,128)(2,1)S(1)} %collective-permute-done.13.refs_2_, ...), custom_call_target="tpu_custom_call" | custom-call | flops 1207959552 | bytes 7340032 | tf_op jit(solution)/shard_map/experts/pallas_call | solution.py:431
  62.4 6.2 %collective-permute-done.19.refs_2_ = bf16[2,16,2176]{2,1,0:T(8,128)(2,1)S(1)} collective-permute-done((bf16[2,16,2176]{2,1,0:T(8,128)(2,1)S(1)}, bf16[2,16,2176]{2,1,0:T(8,128)(2,1)S(1)}, u32[]{:S(2)}, u32[]{:S(2)}) %collective-permute-start.19) | collective-permute-done | bytes 139296 | tf_op jit(solution)/shard_map/ppermute | solution.py:151
  69.2 1.8 %collective-permute-start.23 = (bf16[2,16,2176]{2,1,0:T(8,128)(2,1)S(1)}, bf16[2,16,2176]{2,1,0:T(8,128)(2,1)S(1)}, u32[]{:S(2)}, u32[]{:S(2)}) collective-permute-start(bf16[2,16,2176]{2,1,0:T(8,128)(2,1)S(1)} %slice.156), channel_id=1, source_target_pairs={{0,2},{1,3},{2,0},{3,1},{4,6},{5,7},{6,4},{7,5},{8,10},{9,11},{10,... | collective-permute-start | bytes 417800 | tf_op jit(solution)/shard_map/ppermute | solution.py:151
  71.0 1.7 %collective-permute-start.24 = (bf16[2,16,2176]{2,1,0:T(8,128)(2,1)S(1)}, bf16[2,16,2176]{2,1,0:T(8,128)(2,1)S(1)}, u32[]{:S(2)}, u32[]{:S(2)}) collective-permute-start(bf16[2,16,2176]{2,1,0:T(8,128)(2,1)S(1)} %slice.157), channel_id=1, source_target_pairs={{0,4},{4,0},{8,12},{12,8},{16,20},{20,16},{24,28},{28,24},{1,5},{5... | collective-permute-start | bytes 417800 | tf_op jit(solution)/shard_map/ppermute | solution.py:151
  72.7 1.9 %experts.5 = (f32[2,4,64,512]{3,2,1,0:T(8,128)S(1)}, bf16[2,4,64,512]{3,2,1,0:T(8,128)(2,1)S(1)}) custom-call(bf16[4,16,2176]{2,1,0:T(8,128)(2,1)S(1)} %collective-permute-done.12.refs_0_, bf16[4,16,2176]{2,1,0:T(8,128)(2,1)S(1)} %collective-permute-done.25.refs_1_, bf16[2,16,2176]{2,1,0:T(8,128)(2,1)S(1)} %collective-permute-done.19.refs_2_, ...), custom_call_target="tpu_custom_call" | custom-call | flops 1207959552 | bytes 7340032 | tf_op jit(solution)/shard_map/experts/pallas_call | solution.py:431
  79.2 1.9 %experts.6 = (f32[2,4,64,512]{3,2,1,0:T(8,128)S(1)}, bf16[2,4,64,512]{3,2,1,0:T(8,128)(2,1)S(1)}) custom-call(bf16[4,16,2176]{2,1,0:T(8,128)(2,1)S(1)} %collective-permute-done.21.refs_0_, bf16[4,16,2176]{2,1,0:T(8,128)(2,1)S(1)} %collective-permute-done.29.refs_1_, bf16[2,16,2176]{2,1,0:T(8,128)(2,1)S(1)} %collective-permute-done.23.refs_2_, ...), custom_call_target="tpu_custom_call" | custom-call | flops 1207959552 | bytes 7340032 | tf_op jit(solution)/shard_map/experts/pallas_call | solution.py:431
  82.0 1.8 %collective-permute-start.36 = (bf16[2,64,512]{2,1,0:T(8,128)(2,1)S(1)}, bf16[2,64,512]{2,1,0:T(8,128)(2,1)S(1)}, u32[]{:S(2)}, u32[]{:S(2)}) collective-permute-start(bf16[2,64,512]{2,1,0:T(8,128)(2,1)S(1)} %get-tuple-element.163), channel_id=1, source_target_pairs={{0,4},{4,0},{8,12},{12,8},{16,20},{20,16},{24,28},{28,24},{1,5},{5... | collective-permute-start | bytes 393224 | tf_op jit(solution)/shard_map/ppermute | solution.py:151
  83.9 3.5 %collective-permute-done.33 = bf16[2,64,512]{2,1,0:T(8,128)(2,1)S(1)} collective-permute-done((bf16[2,64,512]{2,1,0:T(8,128)(2,1)S(1)}, bf16[2,64,512]{2,1,0:T(8,128)(2,1)S(1)}, u32[]{:S(2)}, u32[]{:S(2)}) %collective-permute-start.33) | collective-permute-done | bytes 131104 | tf_op jit(solution)/shard_map/ppermute | solution.py:151
  87.4 1.7 %collective-permute-start.34 = (bf16[4,64,512]{2,1,0:T(8,128)(2,1)S(1)}, bf16[4,64,512]{2,1,0:T(8,128)(2,1)S(1)}, u32[]{:S(2)}, u32[]{:S(2)}) collective-permute-start(bf16[4,64,512]{2,1,0:T(8,128)(2,1)S(1)} %pad_maximum_fusion.2), channel_id=1, source_target_pairs={{0,4},{4,0},{8,12},{12,8},{16,20},{20,16},{24,28},{28,24},{1,5},{5... | collective-permute-start | bytes 786440 | tf_op jit(solution)/shard_map/ppermute | solution.py:151
  89.2 1.9 %experts.7 = (f32[2,4,64,512]{3,2,1,0:T(8,128)S(1)}, bf16[2,4,64,512]{3,2,1,0:T(8,128)(2,1)S(1)}) custom-call(bf16[4,16,2176]{2,1,0:T(8,128)(2,1)S(1)} %pad_maximum_fusion.1.refs_0_, bf16[4,16,2176]{2,1,0:T(8,128)(2,1)S(1)} %collective-permute-done.40.refs_1_, bf16[4,16,2176]{2,1,0:T(8,128)(2,1)S(1)} %collective-permute-done.22.refs_2_, ...), custom_call_target="tpu_custom_call" | custom-call | flops 1207959552 | bytes 7340032 | tf_op jit(solution)/shard_map/experts/pallas_call | solution.py:431
  93.5 1.7 %collective-permute-start.39 = (bf16[2,64,512]{2,1,0:T(8,128)(2,1)S(1)}, bf16[2,64,512]{2,1,0:T(8,128)(2,1)S(1)}, u32[]{:S(2)}, u32[]{:S(2)}) collective-permute-start(bf16[2,64,512]{2,1,0:T(8,128)(2,1)S(1)} %get-tuple-element.161), channel_id=1, source_target_pairs={{0,2},{1,3},{2,0},{3,1},{4,6},{5,7},{6,4},{7,5},{8,10},{9,11},{10,... | collective-permute-start | bytes 393224 | tf_op jit(solution)/shard_map/ppermute | solution.py:151
  96.6 2.4 %collective-permute-done.38 = bf16[2,64,512]{2,1,0:T(8,128)(2,1)S(1)} collective-permute-done((bf16[2,64,512]{2,1,0:T(8,128)(2,1)S(1)}, bf16[2,64,512]{2,1,0:T(8,128)(2,1)S(1)}, u32[]{:S(2)}, u32[]{:S(2)}) %collective-permute-start.38) | collective-permute-done | bytes 131104 | tf_op jit(solution)/shard_map/ppermute | solution.py:151
  99.0 4.0 %collective-permute-done.39 = bf16[2,64,512]{2,1,0:T(8,128)(2,1)S(1)} collective-permute-done((bf16[2,64,512]{2,1,0:T(8,128)(2,1)S(1)}, bf16[2,64,512]{2,1,0:T(8,128)(2,1)S(1)}, u32[]{:S(2)}, u32[]{:S(2)}) %collective-permute-start.39) | collective-permute-done | bytes 131104 | tf_op jit(solution)/shard_map/ppermute | solution.py:151
  106.9 2.8 %collective-permute-start.47 = (bf16[64,512]{1,0:T(8,128)(2,1)S(1)}, bf16[64,512]{1,0:T(8,128)(2,1)S(1)}, u32[]{:S(2)}, u32[]{:S(2)}) collective-permute-start(bf16[64,512]{1,0:T(8,128)(2,1)S(1)} %get-tuple-element.158), channel_id=1, source_target_pairs={{0,24},{4,28},{8,16},{12,20},{16,8},{20,12},{24,0},{28,4},{1,25},{... | collective-permute-start | bytes 196616 | tf_op jit(solution)/shard_map/ppermute | solution.py:151
  109.7 2.5 %collective-permute-done.46.refs_4_ = bf16[64,512]{1,0:T(8,128)(2,1)S(1)} collective-permute-done((bf16[64,512]{1,0:T(8,128)(2,1)S(1)}, bf16[64,512]{1,0:T(8,128)(2,1)S(1)}, u32[]{:S(2)}, u32[]{:S(2)}) %collective-permute-start.46) | collective-permute-done | bytes 65568 | tf_op jit(solution)/shard_map/ppermute | solution.py:151
  114.4 2.1 %collective-permute-start.49 = (bf16[64,512]{1,0:T(8,128)(2,1)S(1)}, bf16[64,512]{1,0:T(8,128)(2,1)S(1)}, u32[]{:S(2)}, u32[]{:S(2)}) collective-permute-start(bf16[64,512]{1,0:T(8,128)(2,1)S(1)} %get-tuple-element.156), channel_id=1, source_target_pairs={{0,16},{4,20},{8,24},{12,28},{16,0},{20,4},{24,8},{28,12},{1,17},{... | collective-permute-start | bytes 196616 | tf_op jit(solution)/shard_map/ppermute | solution.py:151
  117.7 2.7 %collective-permute-done.49.refs_10_ = bf16[64,512]{1,0:T(8,128)(2,1)S(1)} collective-permute-done((bf16[64,512]{1,0:T(8,128)(2,1)S(1)}, bf16[64,512]{1,0:T(8,128)(2,1)S(1)}, u32[]{:S(2)}, u32[]{:S(2)}) %collective-permute-start.49) | collective-permute-done | bytes 65568 | tf_op jit(solution)/shard_map/ppermute | solution.py:151
  120.3 2.3 %collective-permute-done.50.refs_11_ = bf16[64,512]{1,0:T(8,128)(2,1)S(1)} collective-permute-done((bf16[64,512]{1,0:T(8,128)(2,1)S(1)}, bf16[64,512]{1,0:T(8,128)(2,1)S(1)}, u32[]{:S(2)}, u32[]{:S(2)}) %collective-permute-start.50) | collective-permute-done | bytes 65568 | tf_op jit(solution)/shard_map/ppermute | solution.py:151
  (125 shorter events, 32.5 us)
Async XLA Ops:
  0.0 6.7 %collective-permute-start.1 = (bf16[128,512]{1,0:T(8,128)(2,1)}, bf16[128,512]{1,0:T(8,128)(2,1)S(1)}, u32[]{:S(2)}, u32[]{:S(2)}) collective-permute-start(bf16[128,512]{1,0:T(8,128)(2,1)} %refs_0_.1), channel_id=1, source_target_pairs={{0,2},{1,3},{2,0},{3,1},{4,6},{5,7},{6,4},{7,5},{8,10},{9,11},{10,... | collective-permute-start | bytes 393224 | tf_op jit(solution)/shard_map/ppermute | solution.py:151
  17.8 6.5 %collective-permute-start.4 = (bf16[32,2048]{1,0:T(8,128)(2,1)}, bf16[32,2048]{1,0:T(8,128)(2,1)S(1)}, u32[]{:S(2)}, u32[]{:S(2)}) collective-permute-start(bf16[32,2048]{1,0:T(8,128)(2,1)} %get-tuple-element.78), channel_id=1, source_target_pairs={{0,2},{1,3},{2,0},{3,1},{4,6},{5,7},{6,4},{7,5},{8,10},{9,11},{10,... | collective-permute-start | bytes 393224 | tf_op jit(solution)/shard_map/ppermute | solution.py:151
  19.6 6.5 %collective-permute-start.5 = (bf16[32,2048]{1,0:T(8,128)(2,1)}, bf16[32,2048]{1,0:T(8,128)(2,1)S(1)}, u32[]{:S(2)}, u32[]{:S(2)}) collective-permute-start(bf16[32,2048]{1,0:T(8,128)(2,1)} %get-tuple-element.79), channel_id=1, source_target_pairs={{0,3},{1,2},{2,1},{3,0},{4,7},{5,6},{6,5},{7,4},{8,11},{9,10},{10,... | collective-permute-start | bytes 393224 | tf_op jit(solution)/shard_map/ppermute | solution.py:151
  27.2 10.7 %collective-permute-start.9 = (f32[32,512]{1,0:T(8,128)S(1)}, f32[32,512]{1,0:T(8,128)S(1)}, u32[]{:S(2)}, u32[]{:S(2)}) collective-permute-start(f32[32,512]{1,0:T(8,128)S(1)} %get-tuple-element.82), channel_id=1, source_target_pairs={{0,1},{1,0},{2,3},{3,2},{4,5},{5,4},{6,7},{7,6},{8,9},{9,8},{10,11... | collective-permute-start | bytes 196616 | tf_op jit(solution)/shard_map/ppermute | solution.py:151
  27.7 14.4 %collective-permute-start.6 = (bf16[16,2176]{1,0:T(8,128)(2,1)S(1)}, bf16[16,2176]{1,0:T(8,128)(2,1)S(1)}, u32[]{:S(2)}, u32[]{:S(2)}) collective-permute-start(bf16[16,2176]{1,0:T(8,128)(2,1)S(1)} %get-tuple-element.86), channel_id=1, source_target_pairs={{0,8},{4,12},{8,0},{12,4},{16,24},{20,28},{24,16},{28,20},{1,9},{5... | collective-permute-start | bytes 208904 | tf_op jit(solution)/shard_map/ppermute | solution.py:151
  29.5 12.6 %collective-permute-start.7 = (bf16[16,2176]{1,0:T(8,128)(2,1)S(1)}, bf16[16,2176]{1,0:T(8,128)(2,1)S(1)}, u32[]{:S(2)}, u32[]{:S(2)}) collective-permute-start(bf16[16,2176]{1,0:T(8,128)(2,1)S(1)} %get-tuple-element.86), channel_id=1, source_target_pairs={{0,16},{4,20},{8,24},{12,28},{16,0},{20,4},{24,8},{28,12},{1,17},{... | collective-permute-start | bytes 208904 | tf_op jit(solution)/shard_map/ppermute | solution.py:151
  35.0 7.1 %collective-permute-start.8 = (bf16[16,2176]{1,0:T(8,128)(2,1)S(1)}, bf16[16,2176]{1,0:T(8,128)(2,1)S(1)}, u32[]{:S(2)}, u32[]{:S(2)}) collective-permute-start(bf16[16,2176]{1,0:T(8,128)(2,1)S(1)} %get-tuple-element.86), channel_id=1, source_target_pairs={{0,24},{4,28},{8,16},{12,20},{16,8},{20,12},{24,0},{28,4},{1,25},{... | collective-permute-start | bytes 208904 | tf_op jit(solution)/shard_map/ppermute | solution.py:151
  42.2 13.4 %collective-permute-start.12 = (bf16[4,16,2176]{2,1,0:T(8,128)(2,1)S(1)}, bf16[4,16,2176]{2,1,0:T(8,128)(2,1)S(1)}, u32[]{:S(2)}, u32[]{:S(2)}) collective-permute-start(bf16[4,16,2176]{2,1,0:T(8,128)(2,1)S(1)} %pad_maximum_fusion.refs_0_), channel_id=1, source_target_pairs={{0,4},{4,0},{8,12},{12,8},{16,20},{20,16},{24,28},{28,24},{1,5},{5... | collective-permute-start | bytes 835592 | tf_op jit(solution)/shard_map/ppermute | solution.py:151
  44.0 11.5 %collective-permute-start.13 = (bf16[4,16,2176]{2,1,0:T(8,128)(2,1)S(1)}, bf16[4,16,2176]{2,1,0:T(8,128)(2,1)S(1)}, u32[]{:S(2)}, u32[]{:S(2)}) collective-permute-start(bf16[4,16,2176]{2,1,0:T(8,128)(2,1)S(1)} %pad_maximum_fusion.refs_0_), channel_id=1, source_target_pairs={{0,2},{1,3},{2,0},{3,1},{4,6},{5,7},{6,4},{7,5},{8,10},{9,11},{10,... | collective-permute-start | bytes 835592 | tf_op jit(solution)/shard_map/ppermute | solution.py:151
  44.8 10.8 %collective-permute-start.14 = (bf16[4,16,2176]{2,1,0:T(8,128)(2,1)S(1)}, bf16[4,16,2176]{2,1,0:T(8,128)(2,1)S(1)}, u32[]{:S(2)}, u32[]{:S(2)}) collective-permute-start(bf16[4,16,2176]{2,1,0:T(8,128)(2,1)S(1)} %pad_maximum_fusion.refs_0_), channel_id=1, source_target_pairs={{0,1},{1,0},{2,3},{3,2},{4,5},{5,4},{6,7},{7,6},{8,9},{9,8},{10,11... | collective-permute-start | bytes 835592 | tf_op jit(solution)/shard_map/ppermute | solution.py:151
  45.7 7.0 %collective-permute-start.16 = (bf16[16,2176]{1,0:T(8,128)(2,1)S(1)}, bf16[16,2176]{1,0:T(8,128)(2,1)S(1)}, u32[]{:S(2)}, u32[]{:S(2)}) collective-permute-start(bf16[16,2176]{1,0:T(8,128)(2,1)S(1)} %get-tuple-element.96), channel_id=1, source_target_pairs={{0,16},{4,20},{8,24},{12,28},{16,0},{20,4},{24,8},{28,12},{1,17},{... | collective-permute-start | bytes 208904 | tf_op jit(solution)/shard_map/ppermute | solution.py:151
  49.4 6.2 %collective-permute-start.17 = (bf16[16,2176]{1,0:T(8,128)(2,1)S(1)}, bf16[16,2176]{1,0:T(8,128)(2,1)S(1)}, u32[]{:S(2)}, u32[]{:S(2)}) collective-permute-start(bf16[16,2176]{1,0:T(8,128)(2,1)S(1)} %get-tuple-element.96), channel_id=1, source_target_pairs={{0,24},{4,28},{8,16},{12,20},{16,8},{20,12},{24,0},{28,4},{1,25},{... | collective-permute-start | bytes 208904 | tf_op jit(solution)/shard_map/ppermute | solution.py:151
  55.7 12.9 %collective-permute-start.21 = (bf16[4,16,2176]{2,1,0:T(8,128)(2,1)S(1)}, bf16[4,16,2176]{2,1,0:T(8,128)(2,1)S(1)}, u32[]{:S(2)}, u32[]{:S(2)}) collective-permute-start(bf16[4,16,2176]{2,1,0:T(8,128)(2,1)S(1)} %pad_maximum_fusion.1.refs_0_), channel_id=1, source_target_pairs={{0,4},{4,0},{8,12},{12,8},{16,20},{20,16},{24,28},{28,24},{1,5},{5... | collective-permute-start | bytes 835592 | tf_op jit(solution)/shard_map/ppermute | solution.py:151
  56.3 12.3 %collective-permute-start.22 = (bf16[4,16,2176]{2,1,0:T(8,128)(2,1)S(1)}, bf16[4,16,2176]{2,1,0:T(8,128)(2,1)S(1)}, u32[]{:S(2)}, u32[]{:S(2)}) collective-permute-start(bf16[4,16,2176]{2,1,0:T(8,128)(2,1)S(1)} %pad_maximum_fusion.1.refs_0_), channel_id=1, source_target_pairs={{0,2},{1,3},{2,0},{3,1},{4,6},{5,7},{6,4},{7,5},{8,10},{9,11},{10,... | collective-permute-start | bytes 835592 | tf_op jit(solution)/shard_map/ppermute | solution.py:151
  58.3 10.3 %collective-permute-start.19 = (bf16[2,16,2176]{2,1,0:T(8,128)(2,1)S(1)}, bf16[2,16,2176]{2,1,0:T(8,128)(2,1)S(1)}, u32[]{:S(2)}, u32[]{:S(2)}) collective-permute-start(bf16[2,16,2176]{2,1,0:T(8,128)(2,1)S(1)} %slice.154), channel_id=1, source_target_pairs={{0,2},{1,3},{2,0},{3,1},{4,6},{5,7},{6,4},{7,5},{8,10},{9,11},{10,... | collective-permute-start | bytes 417800 | tf_op jit(solution)/shard_map/ppermute | solution.py:151
  58.4 10.1 %collective-permute-start.20 = (bf16[2,16,2176]{2,1,0:T(8,128)(2,1)S(1)}, bf16[2,16,2176]{2,1,0:T(8,128)(2,1)S(1)}, u32[]{:S(2)}, u32[]{:S(2)}) collective-permute-start(bf16[2,16,2176]{2,1,0:T(8,128)(2,1)S(1)} %slice.155), channel_id=1, source_target_pairs={{0,4},{4,0},{8,12},{12,8},{16,20},{20,16},{24,28},{28,24},{1,5},{5... | collective-permute-start | bytes 417800 | tf_op jit(solution)/shard_map/ppermute | solution.py:151
  60.4 12.3 %collective-permute-start.25 = (bf16[4,16,2176]{2,1,0:T(8,128)(2,1)S(1)}, bf16[4,16,2176]{2,1,0:T(8,128)(2,1)S(1)}, u32[]{:S(2)}, u32[]{:S(2)}) collective-permute-start(bf16[4,16,2176]{2,1,0:T(8,128)(2,1)S(1)} %collective-permute-done.12.refs_0_), channel_id=1, source_target_pairs={{0,1},{1,0},{2,3},{3,2},{4,5},{5,4},{6,7},{7,6},{8,9},{9,8},{10,11... | collective-permute-start | bytes 835592 | tf_op jit(solution)/shard_map/ppermute | solution.py:151
  81.1 10.8 %collective-permute-start.32 = (bf16[2,4,64,512]{3,2,1,0:T(8,128)(2,1)S(1)}, bf16[2,4,64,512]{3,2,1,0:T(8,128)(2,1)S(1)}, u32[]{:S(2)}, u32[]{:S(2)}) collective-permute-start(bf16[2,4,64,512]{3,2,1,0:T(8,128)(2,1)S(1)} %get-tuple-element.120), channel_id=1, source_target_pairs={{0,1},{1,0},{2,3},{3,2},{4,5},{5,4},{6,7},{7,6},{8,9},{9,8},{10,11... | collective-permute-start | bytes 1572872 | tf_op jit(solution)/shard_map/ppermute | solution.py:151
  81.5 5.8 %collective-permute-start.33 = (bf16[2,64,512]{2,1,0:T(8,128)(2,1)S(1)}, bf16[2,64,512]{2,1,0:T(8,128)(2,1)S(1)}, u32[]{:S(2)}, u32[]{:S(2)}) collective-permute-start(bf16[2,64,512]{2,1,0:T(8,128)(2,1)S(1)} %get-tuple-element.164), channel_id=1, source_target_pairs={{0,2},{1,3},{2,0},{3,1},{4,6},{5,7},{6,4},{7,5},{8,10},{9,11},{10,... | collective-permute-start | bytes 393224 | tf_op jit(solution)/shard_map/ppermute | solution.py:151
  81.9 9.5 %collective-permute-start.35 = (bf16[2,4,64,512]{3,2,1,0:T(8,128)(2,1)S(1)}, bf16[2,4,64,512]{3,2,1,0:T(8,128)(2,1)S(1)}, u32[]{:S(2)}, u32[]{:S(2)}) collective-permute-start(bf16[2,4,64,512]{3,2,1,0:T(8,128)(2,1)S(1)} %get-tuple-element.124), channel_id=1, source_target_pairs={{0,1},{1,0},{2,3},{3,2},{4,5},{5,4},{6,7},{7,6},{8,9},{9,8},{10,11... | collective-permute-start | bytes 1572872 | tf_op jit(solution)/shard_map/ppermute | solution.py:151
  82.0 9.5 %collective-permute-start.36 = (bf16[2,64,512]{2,1,0:T(8,128)(2,1)S(1)}, bf16[2,64,512]{2,1,0:T(8,128)(2,1)S(1)}, u32[]{:S(2)}, u32[]{:S(2)}) collective-permute-start(bf16[2,64,512]{2,1,0:T(8,128)(2,1)S(1)} %get-tuple-element.163), channel_id=1, source_target_pairs={{0,4},{4,0},{8,12},{12,8},{16,20},{20,16},{24,28},{28,24},{1,5},{5... | collective-permute-start | bytes 393224 | tf_op jit(solution)/shard_map/ppermute | solution.py:151
  87.4 9.2 %collective-permute-start.34 = (bf16[4,64,512]{2,1,0:T(8,128)(2,1)S(1)}, bf16[4,64,512]{2,1,0:T(8,128)(2,1)S(1)}, u32[]{:S(2)}, u32[]{:S(2)}) collective-permute-start(bf16[4,64,512]{2,1,0:T(8,128)(2,1)S(1)} %pad_maximum_fusion.2), channel_id=1, source_target_pairs={{0,4},{4,0},{8,12},{12,8},{16,20},{20,16},{24,28},{28,24},{1,5},{5... | collective-permute-start | bytes 786440 | tf_op jit(solution)/shard_map/ppermute | solution.py:151
  91.1 11.9 %collective-permute-start.42 = (bf16[2,4,64,512]{3,2,1,0:T(8,128)(2,1)S(1)}, bf16[2,4,64,512]{3,2,1,0:T(8,128)(2,1)S(1)}, u32[]{:S(2)}, u32[]{:S(2)}) collective-permute-start(bf16[2,4,64,512]{3,2,1,0:T(8,128)(2,1)S(1)} %get-tuple-element.128), channel_id=1, source_target_pairs={{0,1},{1,0},{2,3},{3,2},{4,5},{5,4},{6,7},{7,6},{8,9},{9,8},{10,11... | collective-permute-start | bytes 1572872 | tf_op jit(solution)/shard_map/ppermute | solution.py:151
  91.6 11.4 %collective-permute-start.37 = (bf16[4,64,512]{2,1,0:T(8,128)(2,1)S(1)}, bf16[4,64,512]{2,1,0:T(8,128)(2,1)S(1)}, u32[]{:S(2)}, u32[]{:S(2)}) collective-permute-start(bf16[4,64,512]{2,1,0:T(8,128)(2,1)S(1)} %pad_maximum_fusion.3), channel_id=1, source_target_pairs={{0,2},{1,3},{2,0},{3,1},{4,6},{5,7},{6,4},{7,5},{8,10},{9,11},{10,... | collective-permute-start | bytes 786440 | tf_op jit(solution)/shard_map/ppermute | solution.py:151
  92.1 6.9 %collective-permute-start.38 = (bf16[2,64,512]{2,1,0:T(8,128)(2,1)S(1)}, bf16[2,64,512]{2,1,0:T(8,128)(2,1)S(1)}, u32[]{:S(2)}, u32[]{:S(2)}) collective-permute-start(bf16[2,64,512]{2,1,0:T(8,128)(2,1)S(1)} %get-tuple-element.162), channel_id=1, source_target_pairs={{0,4},{4,0},{8,12},{12,8},{16,20},{20,16},{24,28},{28,24},{1,5},{5... | collective-permute-start | bytes 393224 | tf_op jit(solution)/shard_map/ppermute | solution.py:151
  93.5 9.4 %collective-permute-start.39 = (bf16[2,64,512]{2,1,0:T(8,128)(2,1)S(1)}, bf16[2,64,512]{2,1,0:T(8,128)(2,1)S(1)}, u32[]{:S(2)}, u32[]{:S(2)}) collective-permute-start(bf16[2,64,512]{2,1,0:T(8,128)(2,1)S(1)} %get-tuple-element.161), channel_id=1, source_target_pairs={{0,2},{1,3},{2,0},{3,1},{4,6},{5,7},{6,4},{7,5},{8,10},{9,11},{10,... | collective-permute-start | bytes 393224 | tf_op jit(solution)/shard_map/ppermute | solution.py:151
  103.0 10.0 %collective-permute-start.43 = (bf16[4,64,512]{2,1,0:T(8,128)(2,1)S(1)}, bf16[4,64,512]{2,1,0:T(8,128)(2,1)S(1)}, u32[]{:S(2)}, u32[]{:S(2)}) collective-permute-start(bf16[4,64,512]{2,1,0:T(8,128)(2,1)S(1)} %pad_maximum_fusion.4), channel_id=1, source_target_pairs={{0,4},{4,0},{8,12},{12,8},{16,20},{20,16},{24,28},{28,24},{1,5},{5... | collective-permute-start | bytes 786440 | tf_op jit(solution)/shard_map/ppermute | solution.py:151
  104.7 8.3 %collective-permute-start.44 = (bf16[4,64,512]{2,1,0:T(8,128)(2,1)S(1)}, bf16[4,64,512]{2,1,0:T(8,128)(2,1)S(1)}, u32[]{:S(2)}, u32[]{:S(2)}) collective-permute-start(bf16[4,64,512]{2,1,0:T(8,128)(2,1)S(1)} %pad_maximum_fusion.5), channel_id=1, source_target_pairs={{0,2},{1,3},{2,0},{3,1},{4,6},{5,7},{6,4},{7,5},{8,10},{9,11},{10,... | collective-permute-start | bytes 786440 | tf_op jit(solution)/shard_map/ppermute | solution.py:151
  105.3 6.9 %collective-permute-start.46 = (bf16[64,512]{1,0:T(8,128)(2,1)S(1)}, bf16[64,512]{1,0:T(8,128)(2,1)S(1)}, u32[]{:S(2)}, u32[]{:S(2)}) collective-permute-start(bf16[64,512]{1,0:T(8,128)(2,1)S(1)} %get-tuple-element.159), channel_id=1, source_target_pairs={{0,16},{4,20},{8,24},{12,28},{16,0},{20,4},{24,8},{28,12},{1,17},{... | collective-permute-start | bytes 196616 | tf_op jit(solution)/shard_map/ppermute | solution.py:151
  106.9 6.1 %collective-permute-start.47 = (bf16[64,512]{1,0:T(8,128)(2,1)S(1)}, bf16[64,512]{1,0:T(8,128)(2,1)S(1)}, u32[]{:S(2)}, u32[]{:S(2)}) collective-permute-start(bf16[64,512]{1,0:T(8,128)(2,1)S(1)} %get-tuple-element.158), channel_id=1, source_target_pairs={{0,24},{4,28},{8,16},{12,20},{16,8},{20,12},{24,0},{28,4},{1,25},{... | collective-permute-start | bytes 196616 | tf_op jit(solution)/shard_map/ppermute | solution.py:151
  114.4 5.9 %collective-permute-start.49 = (bf16[64,512]{1,0:T(8,128)(2,1)S(1)}, bf16[64,512]{1,0:T(8,128)(2,1)S(1)}, u32[]{:S(2)}, u32[]{:S(2)}) collective-permute-start(bf16[64,512]{1,0:T(8,128)(2,1)S(1)} %get-tuple-element.156), channel_id=1, source_target_pairs={{0,16},{4,20},{8,24},{12,28},{16,0},{20,4},{24,8},{28,12},{1,17},{... | collective-permute-start | bytes 196616 | tf_op jit(solution)/shard_map/ppermute | solution.py:151
  116.6 6.1 %collective-permute-start.50 = (bf16[64,512]{1,0:T(8,128)(2,1)S(1)}, bf16[64,512]{1,0:T(8,128)(2,1)S(1)}, u32[]{:S(2)}, u32[]{:S(2)}) collective-permute-start(bf16[64,512]{1,0:T(8,128)(2,1)S(1)} %get-tuple-element.155), channel_id=1, source_target_pairs={{0,24},{4,28},{8,16},{12,20},{16,8},{20,12},{24,0},{28,4},{1,25},{... | collective-permute-start | bytes 196616 | tf_op jit(solution)/shard_map/ppermute | solution.py:151
  (29 other events, 272.9 us)

commit v7 on v5

--- a/solution.py
+++ b/solution.py
@@ -358,11 +358,10 @@
 
 def pack_kernel(
     own_ref, near_ref, far_ref, cross_ref, gain_ref, ids_ref, routes_ref,
-    rows_ref, keep_ref, near_out, far_out, cross_out, residual_ref, spread_ref,
+    rows_ref, residual_ref, spread_ref,
 ):
     tp_index = lax.axis_index("tp")
     share_rows, width = own_ref.shape
-    share_width = keep_ref.shape[1]
     mine = pl.ds(pl.multiple_of(tp_index * share_rows, share_rows), share_rows)
     residual = (own_ref[...] + near_ref[...].astype(jnp.float32)) + (
         far_ref[...].astype(jnp.float32) + cross_ref[...].astype(jnp.float32)
@@ -378,31 +377,21 @@
     lane = lax.broadcasted_iota(jnp.int32, spread.shape, 1)
     high = spread.astype(jnp.bfloat16).astype(jnp.float32)
     rows_ref[:, width:] = jnp.where(lane < LANES // 2, high, spread - high).astype(jnp.bfloat16)
-    for step, out_ref in enumerate((keep_ref, near_out, far_out, cross_out)):
-        column = pl.multiple_of((tp_index ^ step) * share_width, share_width)
-        out_ref[...] = residual_ref[:, pl.ds(column, share_width)]
-
-
-def experts_kernel(far_parts, *refs):
-    near_ref, core_ref = refs[:2]
-    far_refs, far_core_refs = refs[2 : 2 + far_parts], refs[2 + far_parts : 2 + 2 * far_parts]
-    gate_ref, up_ref, down_ref = refs[2 + 2 * far_parts : 5 + 2 * far_parts]
-    out_refs, rows_ref = refs[5 + 2 * far_parts : -1], refs[-1]
+
+
+def experts_kernel(plan, *refs):
+    pieces, residual_refs = refs[: len(plan)], refs[len(plan) : -7]
+    gate_ref, up_ref, down_ref, keep_ref, send_ref, rows_ref, sums_ref = refs[-7:]
     req_index, tp_index = lax.axis_index("req"), lax.axis_index("tp")
-    levels, share_rows, _ = near_ref.shape
+    columns, _, levels, group_rows, share_width = keep_ref.shape
     width = gate_ref.shape[1]
     units = gate_ref.shape[0] // 2
-    share_width = width // 4
-
-    def pick(parts):
-        if len(parts) == 1:
-            return parts[0][...]
-        return jnp.where(pl.program_id(0) == 0, parts[0][...], parts[1][...])
-
-    for step, value in enumerate((near_ref[...], core_ref[...], pick(far_refs), pick(far_core_refs))):
+    for (column, step, first), piece in zip(plan, pieces):
+        count = piece.shape[1]
         for level in range(levels):
-            start = (4 * level + (tp_index ^ step)) * share_rows
-            rows_ref[pl.ds(pl.multiple_of(start, share_rows), share_rows), :] = value[level]
+            start = (column * levels + level) * group_rows + first
+            start = start + (tp_index ^ step) * (group_rows // 4)
+            rows_ref[pl.ds(pl.multiple_of(start, count), count), :] = piece[level]
     spread = rows_ref[:, width:].astype(jnp.float32)
     lane = lax.broadcasted_iota(jnp.int32, spread.shape, 1) % (LANES // 2)
     weights = [
@@ -417,53 +406,99 @@
     weight = jnp.where(unit < units, weights[0], weights[1])
     acts = (gate / (1.0 + jnp.exp(-gate)) * up * weight).astype(jnp.bfloat16)
     for step in range(4):
-        column = pl.multiple_of((tp_index ^ step) * share_width, share_width)
+        start = pl.multiple_of((tp_index ^ step) * share_width, share_width)
         part = jnp.dot(
-            acts, down_ref[:, pl.ds(column, share_width)], preferred_element_type=jnp.float32
+            acts, down_ref[:, pl.ds(start, share_width)], preferred_element_type=jnp.float32
         )
-        target = out_refs[step]
-        target[...] = part.reshape(target.shape).astype(target.dtype)
-
-
-def run_experts(near, core, far, far_core, gate_weight, up_weight, down_weight):
-    levels, share_rows, packed = near.shape
-    share_width = down_weight.shape[1] // 4
-    block = pl.BlockSpec((2, share_rows, packed), lambda z: (z, 0, 0))
-    fixed = pl.BlockSpec((2, share_rows, packed), lambda z: (0, 0, 0))
-    far_spec = block if len(far) == 1 else fixed
-    weight_specs = [
-        pl.BlockSpec(w.shape, lambda z: (0, 0), pipeline_mode=pl.Buffered(1))
-        for w in (gate_weight, up_weight, down_weight)
-    ]
-    out_shape = (levels, 4 * share_rows, share_width)
+        for residual_ref in residual_refs:
+            count = residual_ref.shape[0]
+            mine = pl.ds(pl.multiple_of(tp_index * count, count), count)
+            sums_ref[...] = part
+            sums_ref[mine, :] += residual_ref[:, pl.ds(start, share_width)]
+            part = sums_ref[...]
+        target = send_ref if step % 2 else keep_ref
+        part = part.reshape(columns, levels, group_rows, share_width).astype(target.dtype)
+        for column in range(columns):
+            target[column, step // 2] = part[column]
+
+
+def run_experts(pieces, weights, group_rows, *residual):
+    plan = tuple(place for place, _ in pieces)
+    pieces = [piece for _, piece in pieces]
+    columns, levels, packed = 1 + max(place[0] for place in plan), *pieces[0].shape[::2]
+    rows, share_width = columns * levels * group_rows, weights[2].shape[1] // 4
+    out_shape = (columns, 2, levels, group_rows, share_width)
     return pl.pallas_call(
-        functools.partial(experts_kernel, len(far)),
-        grid=(levels // 2,),
+        functools.partial(experts_kernel, plan),
         out_shape=[
-            jax.ShapeDtypeStruct(out_shape, jnp.bfloat16 if step % 2 else jnp.float32)
-            for step in range(4)
+            jax.ShapeDtypeStruct(out_shape, jnp.float32),
+            jax.ShapeDtypeStruct(out_shape, jnp.bfloat16),
         ],
-        in_specs=[block, block] + [far_spec] * (2 * len(far)) + weight_specs,
-        out_specs=[pl.BlockSpec((2,) + out_shape[1:], lambda z: (z, 0, 0))] * 4,
-        scratch_shapes=[pltpu.VMEM((8 * share_rows, packed), jnp.bfloat16)],
+        in_specs=[VMEM] * (len(pieces) + len(residual) + 3),
+        out_specs=[VMEM] * 2,
+        scratch_shapes=[
+            pltpu.VMEM((rows, packed), jnp.bfloat16),
+            pltpu.VMEM((rows, share_width), jnp.float32),
+        ],
         compiler_params=pltpu.CompilerParams(vmem_limit_bytes=VMEM_LIMIT),
         name="experts",
-    )(near, core, *far, *far_core, gate_weight, up_weight, down_weight)
-
-
-def finish_kernel(
-    own_ref, x_ref, y_ref, z1_ref, z2_ref, z3_ref, keep_ref, near_ref, far_ref, cross_ref, out_ref
-):
-    tp_index = lax.axis_index("tp")
-    share_rows = keep_ref.shape[0]
-    for step, part_ref in enumerate((keep_ref, near_ref, far_ref, cross_ref)):
-        rows = pl.ds(pl.multiple_of((tp_index ^ step) * share_rows, share_rows), share_rows)
-        total = own_ref[0, rows, :] + part_ref[...]
-        for extra_ref in (x_ref, y_ref):
-            total = total + extra_ref[0, rows, :].astype(jnp.float32)
-        for extra_ref in (z1_ref, z2_ref, z3_ref):
-            total = total + extra_ref[rows, :].astype(jnp.float32)
-        out_ref[rows, :] = total.astype(jnp.bfloat16)
+    )(*pieces, *residual, *weights)
+
+
+def finish_kernel(own_ref, x_ref, y_ref, z1_ref, z2_ref, z3_ref, out_ref):
+    total = own_ref[0]
+    for extra_ref in (x_ref, y_ref):
+        total = total + extra_ref[0].astype(jnp.float32)
+    for extra_ref in (z1_ref, z2_ref, z3_ref):
+        total = total + extra_ref[...].astype(jnp.float32)
+    out_ref[...] = total.astype(jnp.bfloat16)
+
+
+def ordered(*values):
+    return lax.optimization_barrier(values)
+
+
+def across_parts(line_x, line_y):
+    half = line_x.shape[1] // 2
+    return flip(line_x[:, :half], "tp", 2), flip(line_y[:, half:], "req", 1)
+
+
+def other_core(parts):
+    return tuple(flip(part, "tp", 1) for part in parts)
+
+
+def with_core(pair):
+    return pair[0], flip(pair[1], "tp", 1)
+
+
+def joined(pair, column, y):
+    return pair[0][column, y] + pair[1][column, y].astype(jnp.float32)
+
+
+def near_pieces(column, line, core):
+    return [((column, 0, 0), line), ((column, 1, 0), core)]
+
+
+def far_pieces(column, parts, cores):
+    half = parts[0].shape[1]
+    if len(parts) == 1:
+        return [((column, 2, 0), parts[0]), ((column, 3, 0), cores[0])]
+    return [((column, 2, i * half), part) for i, part in enumerate(parts)] + [
+        ((column, 3, i * half), part) for i, part in enumerate(cores)
+    ]
+
+
+def relayed(side):
+    part = side.astype(jnp.bfloat16)
+    half = part.shape[1] // 2
+    return flip(part[:, :half], "req", 1), flip(part[:, half:], "tp", 2)
+
+
+def neighbours(to_x, to_y, by_x, by_y):
+    half = by_x.shape[1]
+    to_y = jnp.concatenate([to_y[:, :half] + by_x.astype(jnp.float32), to_y[:, half:]], axis=1)
+    to_x = jnp.concatenate([to_x[:, :half], to_x[:, half:] + by_y.astype(jnp.float32)], axis=1)
+    return flip(to_x.astype(jnp.bfloat16), "req", 1), flip(to_y.astype(jnp.bfloat16), "tp", 2)
 
 
 def moe_dense(
@@ -479,66 +514,73 @@
     share_rows, width = kept.shape
     token_count, share_width = 4 * share_rows, width // 4
     received = [flip(part, "tp", bits) for bits, part in enumerate(sent, 1)]
-    share_f32 = jax.ShapeDtypeStruct((share_rows, share_width), jnp.float32)
-    rows, *residuals = pl.pallas_call(
+    rows, residual = pl.pallas_call(
         pack_kernel,
-        out_shape=[jax.ShapeDtypeStruct((share_rows, width + LANES), jnp.bfloat16)] + [share_f32] * 4,
+        out_shape=[
+            jax.ShapeDtypeStruct((share_rows, width + LANES), jnp.bfloat16),
+            jax.ShapeDtypeStruct((share_rows, width), jnp.float32),
+        ],
         in_specs=[VMEM] * 7,
-        out_specs=[VMEM] * 5,
-        scratch_shapes=[
-            pltpu.VMEM((share_rows, width), jnp.float32),
-            pltpu.VMEM((token_count, LANES), jnp.float32),
-        ],
+        out_specs=[VMEM] * 2,
+        scratch_shapes=[pltpu.VMEM((token_count, LANES), jnp.float32)],
         compiler_params=pltpu.CompilerParams(vmem_limit_bytes=8 * 1024 * 1024),
         name="pack_rows",
     )(kept, *received, norm_post_gain[None, :], expert_ids.T, route_weights.T)
-    residuals = residuals[:1] + [flip(residuals[bits], "tp", bits) for bits in (1, 2, 3)]
-    line = jnp.stack([rows] + [flip(rows, "req", 2 * bits) for bits in (1, 2, 3)])
     gate_up = [w.transpose(0, 2, 1).reshape(-1, width) for w in (gate_weight, up_weight)]
     weights = (*gate_up, down_weight.reshape(-1, width))
-    line_x, line_y, line_core = lax.optimization_barrier(
-        (flip(line, "req", 1), flip(line, "tp", 2), flip(line, "tp", 1))
-    )
-    across = (flip(line_x[:2], "tp", 2), flip(line_y[2:], "req", 1))
-    line_y_core, line_x_core = flip(line_y, "tp", 1), flip(line_x, "tp", 1)
-    near = run_experts(line, line_core, (line_y,), (line_y_core,), *weights)
-    near, across, line_x_core, residuals = lax.optimization_barrier(
-        (near, across, line_x_core, residuals)
-    )
-    across_core = tuple(flip(part, "tp", 1) for part in across)
-    side = run_experts(line_x, line_x_core, across, across_core, *weights)
-    keep_00, keep_01, keep_10, keep_11 = (
-        (part[2 * y], flip(part[2 * y + 1], "tp", 1)) for part in (near, side) for y in range(2)
-    )
-
-    def both(pair, levels):
-        return pair[0][levels] + pair[1][levels].astype(jnp.float32)
-
-    low, high = slice(0, 2), slice(2, 4)
-    by_x = flip(both(keep_11, low).astype(jnp.bfloat16), "req", 1).astype(jnp.float32)
-    by_y = flip(both(keep_11, high).astype(jnp.bfloat16), "tp", 2).astype(jnp.float32)
-    from_y = [
-        flip((both(keep_01, low) + by_x).astype(jnp.bfloat16), "tp", 2),
-        flip(both(keep_01, high).astype(jnp.bfloat16), "tp", 2),
-    ]
-    from_x = [
-        flip(both(keep_10, low).astype(jnp.bfloat16), "req", 1),
-        flip((both(keep_10, high) + by_y).astype(jnp.bfloat16), "req", 1),
-    ]
-
-    def level(z):
-        part = from_x[z // 2][z % 2].astype(jnp.float32) + from_y[z // 2][z % 2].astype(jnp.float32)
-        return (both(keep_00, z) + part).astype(jnp.bfloat16)
-
-    from_z = [flip(level(z), "req", 2 * z) for z in (1, 2, 3)]
+    line_0 = rows[None]
+    levels = [flip(rows, "req", 2 * bits) for bits in (1, 2, 3)]
+    y_0, x_0 = flip(line_0, "tp", 2), flip(line_0, "req", 1)
+    line_3, y_0, x_0 = ordered(jnp.stack(levels), y_0, x_0)
+    core_0, across_0, y_3, x_3 = ordered(
+        flip(line_0, "tp", 1),
+        across_parts(x_0, y_0),
+        flip(line_3, "tp", 2),
+        flip(line_3, "req", 1),
+    )
+    core_3, y_core_3, x_core_3 = other_core((line_3, y_3, x_3))
+    near_3 = run_experts(
+        near_pieces(0, line_3, core_3) + far_pieces(0, (y_3,), (y_core_3,)), weights, token_count
+    )
+    near_3, x_core_0, y_core_0, x_core_3, across_3 = ordered(
+        near_3, flip(x_0, "tp", 1), flip(y_0, "tp", 1), x_core_3, across_parts(x_3, y_3)
+    )
+    side_3 = run_experts(
+        near_pieces(0, x_3, x_core_3) + far_pieces(0, across_3, other_core(across_3)),
+        weights,
+        token_count,
+    )
+    side_3, across_core_0 = ordered(side_3, other_core(across_0))
+    side_3 = with_core(side_3)
+    all_0 = run_experts(
+        near_pieces(0, line_0, core_0)
+        + far_pieces(0, (y_0,), (y_core_0,))
+        + near_pieces(1, x_0, x_core_0)
+        + far_pieces(1, across_0, across_core_0),
+        weights,
+        token_count,
+        residual,
+    )
+    all_0, near_3, side_3 = ordered(all_0, near_3, side_3)
+    near_3, all_0, relay_3 = ordered(
+        with_core(near_3), with_core(all_0), relayed(joined(side_3, 0, 1))
+    )
+    relay_0, sums_3 = ordered(
+        relayed(joined(all_0, 1, 1)),
+        neighbours(joined(side_3, 0, 0), joined(near_3, 0, 1), *relay_3),
+    )
+    sent = joined(near_3, 0, 0) + sums_3[0].astype(jnp.float32) + sums_3[1].astype(jnp.float32)
+    sent = sent.astype(jnp.bfloat16)
+    from_z = [flip(sent[bits - 1], "req", 2 * bits) for bits in (1, 2, 3)]
+    sums_0 = neighbours(joined(all_0, 1, 0), joined(all_0, 0, 1), *relay_0)
     return pl.pallas_call(
         finish_kernel,
         out_shape=jax.ShapeDtypeStruct((token_count, share_width), jnp.bfloat16),
-        in_specs=[VMEM] * 10,
+        in_specs=[VMEM] * 6,
         out_specs=VMEM,
         compiler_params=pltpu.CompilerParams(vmem_limit_bytes=8 * 1024 * 1024),
         name="finish",
-    )(both(keep_00, low), from_x[0], from_y[0], *from_z, *residuals)
+    )(joined(all_0, 0, 0), *sums_0, *from_z)
 
 
 def moe_routed(

time: 119 us -> 109 us (0.916); the launches traced: 117 us -> 109 us
  waiting for transfers between devices: 66.4 us -> 47.4 us
  starting transfers between devices: 30.5 us -> 41.1 us
    ppermute x34 -> x41, waiting for transfers between devices: 66.4 us -> 47.4 us  [flip(): lax.ppermute(value, axis, [(i, i ^ bits) for i in range(lax.axis_size(axi...]
    ppermute x34 -> x41, starting transfers between devices: 30.5 us -> 41.1 us  [flip(): lax.ppermute(value, axis, [(i, i ^ bits) for i in range(lax.axis_size(axi...]
    pallas_call x2 -> x3, Pallas kernels: 7.85 us -> 7.46 us  [run_experts(): pl.pallas_call(functools.partial(experts_kernel, plan), out_shape=[jax.Sh...]
  transfers between devices with their start and end apart: 34 -> 41, of which waited for: 19 -> 20; matrix products, arithmetic and copies ran while one was open for 1% -> 1% of each run, Pallas kernels for 3% -> 7%
where the time goes in v7:
time: 109 us
  waiting for transfers between devices  47.4 us (43%)
  starting transfers between devices  41.1 us (38%)
  Pallas kernels  17.3 us (16%)
  local copies, waits for them, and re-layouts  1.81 us (2%)
    ppermute x41, waiting for transfers between devices, flip(): lax.ppermute(value, axis, [(i, i ^ bits) for i in range(lax.axis_size(axi...  47.4 us
    ppermute x41, starting transfers between devices, flip(): lax.ppermute(value, axis, [(i, i ^ bits) for i in range(lax.axis_size(axi...  41.1 us
    pallas_call x1, Pallas kernels, attention_shares(): pl.pallas_call(attention_kernel, out_shape=[jax.ShapeDtypeStruct(share, j...  8.86 us
    pallas_call x3, Pallas kernels, run_experts(): pl.pallas_call(functools.partial(experts_kernel, plan), out_shape=[jax.Sh...  7.46 us
  transfers between devices with their start and end apart: 41, of which 20 were waited for; matrix products, arithmetic and copies ran while one was open for 1% of the time, Pallas kernels for 7%

profile of v7, /device:TPU:0, one launch (start us, length us, event | category | flops | bytes accessed | tf_op | source)
XLA Modules:
  0.0 109.0 jit_solution(10560249714218943318)
XLA Ops:
  0.0 3.0 %collective-permute-start.1 = (bf16[128,512]{1,0:T(8,128)(2,1)}, bf16[128,512]{1,0:T(8,128)(2,1)S(1)}, u32[]{:S(2)}, u32[]{:S(2)}) collective-permute-start(bf16[128,512]{1,0:T(8,128)(2,1)} %refs_0_.1), channel_id=1, source_target_pairs={{0,2},{1,3},{2,0},{3,1},{4,6},{5,7},{6,4},{7,5},{8,10},{9,11},{10,... | collective-permute-start | bytes 393224 | tf_op jit(solution)/shard_map/ppermute | solution.py:151
  3.0 3.7 %collective-permute-done.1.refs_2_ = bf16[128,512]{1,0:T(8,128)(2,1)S(1)} collective-permute-done((bf16[128,512]{1,0:T(8,128)(2,1)}, bf16[128,512]{1,0:T(8,128)(2,1)S(1)}, u32[]{:S(2)}, u32[]{:S(2)}) %collective-permute-start.1) | collective-permute-done | bytes 131104 | tf_op jit(solution)/shard_map/ppermute | solution.py:151
  6.7 1.3 %collective-permute-done.2.refs_3_ = bf16[128,512]{1,0:T(8,128)(2,1)S(1)} collective-permute-done((bf16[128,512]{1,0:T(8,128)(2,1)S(1)}, bf16[128,512]{1,0:T(8,128)(2,1)S(1)}, u32[]{:S(2)}, u32[]{:S(2)}) %collective-permute-start.2) | collective-permute-done | bytes 131104 | tf_op jit(solution)/shard_map/ppermute | solution.py:151
  8.7 8.9 %attention.1 = (f32[32,2048]{1,0:T(8,128)}, bf16[32,2048]{1,0:T(8,128)(2,1)}, bf16[32,2048]{1,0:T(8,128)(2,1)}, bf16[32,2048]{1,0:T(8,128)(2,1)}) custom-call(bf16[128,512]{1,0:T(8,128)(2,1)} %refs_0_.1, bf16[128,512]{1,0:T(8,128)(2,1)} %copy-done.8, bf16[128,512]{1,0:T(8,128)(2,1)} %copy-done.7, bf16[128,512]{1,0:T(8,128)(2,1)} %copy-done.9, s32[9]{0:T(128)} %refs_4_.1, ...), custom_call_target="tpu_custom_call" | custom-call | tf_op jit(solution)/shard_map/attention/pallas_call | solution.py:330
  17.8 1.8 %collective-permute-start.4 = (bf16[32,2048]{1,0:T(8,128)(2,1)}, bf16[32,2048]{1,0:T(8,128)(2,1)S(1)}, u32[]{:S(2)}, u32[]{:S(2)}) collective-permute-start(bf16[32,2048]{1,0:T(8,128)(2,1)} %get-tuple-element.54), channel_id=1, source_target_pairs={{0,2},{1,3},{2,0},{3,1},{4,6},{5,7},{6,4},{7,5},{8,10},{9,11},{10,... | collective-permute-start | bytes 393224 | tf_op jit(solution)/shard_map/ppermute | solution.py:151
  19.6 4.8 %collective-permute-done.4.far_ref = bf16[32,2048]{1,0:T(8,128)(2,1)S(1)} collective-permute-done((bf16[32,2048]{1,0:T(8,128)(2,1)}, bf16[32,2048]{1,0:T(8,128)(2,1)S(1)}, u32[]{:S(2)}, u32[]{:S(2)}) %collective-permute-start.4) | collective-permute-done | bytes 131104 | tf_op jit(solution)/shard_map/ppermute | solution.py:151
  24.3 1.7 %collective-permute-done.5.cross_ref = bf16[32,2048]{1,0:T(8,128)(2,1)S(1)} collective-permute-done((bf16[32,2048]{1,0:T(8,128)(2,1)}, bf16[32,2048]{1,0:T(8,128)(2,1)S(1)}, u32[]{:S(2)}, u32[]{:S(2)}) %collective-permute-start.5) | collective-permute-done | bytes 131104 | tf_op jit(solution)/shard_map/ppermute | solution.py:151
  27.2 2.9 %collective-permute-start.8 = (bf16[32,2176]{1,0:T(8,128)(2,1)S(1)}, bf16[32,2176]{1,0:T(8,128)(2,1)S(1)}, u32[]{:S(2)}, u32[]{:S(2)}) collective-permute-start(bf16[32,2176]{1,0:T(8,128)(2,1)S(1)} %get-tuple-element.56), channel_id=1, source_target_pairs={{0,16},{4,20},{8,24},{12,28},{16,0},{20,4},{24,8},{28,12},{1,17},{... | collective-permute-start | bytes 417800 | tf_op jit(solution)/shard_map/ppermute | solution.py:151
  30.1 1.4 %collective-permute-start.9 = (bf16[32,2176]{1,0:T(8,128)(2,1)S(1)}, bf16[32,2176]{1,0:T(8,128)(2,1)S(1)}, u32[]{:S(2)}, u32[]{:S(2)}) collective-permute-start(bf16[32,2176]{1,0:T(8,128)(2,1)S(1)} %get-tuple-element.56), channel_id=1, source_target_pairs={{0,24},{4,28},{8,16},{12,20},{16,8},{20,12},{24,0},{28,4},{1,25},{... | collective-permute-start | bytes 417800 | tf_op jit(solution)/shard_map/ppermute | solution.py:151
  31.7 1.5 %collective-permute-start.10 = (bf16[1,32,2176]{2,1,0:T(8,128)(2,1)S(1)}, bf16[1,32,2176]{2,1,0:T(8,128)(2,1)S(1)}, u32[]{:S(2)}, u32[]{:S(2)}) collective-permute-start(bf16[1,32,2176]{2,1,0:T(8,128)(2,1)S(1)} %bitcast.54), channel_id=1, source_target_pairs={{0,2},{1,3},{2,0},{3,1},{4,6},{5,7},{6,4},{7,5},{8,10},{9,11},{10,... | collective-permute-start | bytes 417800 | tf_op jit(solution)/shard_map/ppermute | solution.py:151
  33.2 5.7 %collective-permute-start.11 = (bf16[1,32,2176]{2,1,0:T(8,128)(2,1)S(1)}, bf16[1,32,2176]{2,1,0:T(8,128)(2,1)S(1)}, u32[]{:S(2)}, u32[]{:S(2)}) collective-permute-start(bf16[1,32,2176]{2,1,0:T(8,128)(2,1)S(1)} %bitcast.55), channel_id=1, source_target_pairs={{0,4},{4,0},{8,12},{12,8},{16,20},{20,16},{24,28},{28,24},{1,5},{5... | collective-permute-start | bytes 417800 | tf_op jit(solution)/shard_map/ppermute | solution.py:151
  38.9 1.7 %collective-permute-done.8 = bf16[32,2176]{1,0:T(8,128)(2,1)S(1)} collective-permute-done((bf16[32,2176]{1,0:T(8,128)(2,1)S(1)}, bf16[32,2176]{1,0:T(8,128)(2,1)S(1)}, u32[]{:S(2)}, u32[]{:S(2)}) %collective-permute-start.8) | collective-permute-done | bytes 139296 | tf_op jit(solution)/shard_map/ppermute | solution.py:151
  40.7 1.0 collective-permute-done.7
  42.3 1.1 %collective-permute-start.14 = (bf16[3,32,2176]{2,1,0:T(8,128)(2,1)S(1)}, bf16[3,32,2176]{2,1,0:T(8,128)(2,1)S(1)}, u32[]{:S(2)}, u32[]{:S(2)}) collective-permute-start(bf16[3,32,2176]{2,1,0:T(8,128)(2,1)S(1)} %pad_maximum_fusion.refs_0_), channel_id=1, source_target_pairs={{0,2},{1,3},{2,0},{3,1},{4,6},{5,7},{6,4},{7,5},{8,10},{9,11},{10,... | collective-permute-start | bytes 1253384 | tf_op jit(solution)/shard_map/ppermute | solution.py:151
  43.4 4.0 %collective-permute-start.15 = (bf16[3,32,2176]{2,1,0:T(8,128)(2,1)S(1)}, bf16[3,32,2176]{2,1,0:T(8,128)(2,1)S(1)}, u32[]{:S(2)}, u32[]{:S(2)}) collective-permute-start(bf16[3,32,2176]{2,1,0:T(8,128)(2,1)S(1)} %pad_maximum_fusion.refs_0_), channel_id=1, source_target_pairs={{0,4},{4,0},{8,12},{12,8},{16,20},{20,16},{24,28},{28,24},{1,5},{5... | collective-permute-start | bytes 1253384 | tf_op jit(solution)/shard_map/ppermute | solution.py:151
  48.9 5.3 %collective-permute-done.12.refs_6_ = bf16[1,16,2176]{2,1,0:T(8,128)(2,1)S(1)} collective-permute-done((bf16[1,16,2176]{2,1,0:T(8,128)(2,1)S(1)}, bf16[1,16,2176]{2,1,0:T(8,128)(2,1)S(1)}, u32[]{:S(2)}, u32[]{:S(2)}) %collective-permute-start.12) | collective-permute-done | bytes 69664 | tf_op jit(solution)/shard_map/ppermute | solution.py:151
  54.2 2.9 %collective-permute-done.13.refs_7_ = bf16[1,16,2176]{2,1,0:T(8,128)(2,1)S(1)} collective-permute-done((bf16[1,16,2176]{2,1,0:T(8,128)(2,1)S(1)}, bf16[1,16,2176]{2,1,0:T(8,128)(2,1)S(1)}, u32[]{:S(2)}, u32[]{:S(2)}) %collective-permute-start.13) | collective-permute-done | bytes 69664 | tf_op jit(solution)/shard_map/ppermute | solution.py:151
  58.2 1.7 %collective-permute-start.22 = (bf16[3,16,2176]{2,1,0:T(8,128)(2,1)S(1)}, bf16[3,16,2176]{2,1,0:T(8,128)(2,1)S(1)}, u32[]{:S(2)}, u32[]{:S(2)}) collective-permute-start(bf16[3,16,2176]{2,1,0:T(8,128)(2,1)S(1)} %slice.112), channel_id=1, source_target_pairs={{0,4},{4,0},{8,12},{12,8},{16,20},{20,16},{24,28},{28,24},{1,5},{5... | collective-permute-start | bytes 626696 | tf_op jit(solution)/shard_map/ppermute | solution.py:151
  60.5 2.7 %experts.3 = (f32[1,2,3,128,512]{4,3,2,1,0:T(8,128)S(1)}, bf16[1,2,3,128,512]{4,3,2,1,0:T(8,128)(2,1)S(1)}) custom-call(bf16[3,32,2176]{2,1,0:T(8,128)(2,1)S(1)} %pad_maximum_fusion.refs_0_, bf16[3,32,2176]{2,1,0:T(8,128)(2,1)S(1)} %collective-permute-done.16.refs_1_, bf16[3,32,2176]{2,1,0:T(8,128)(2,1)S(1)} %collective-permute-done.14.refs_2_, ...), custom_call_target="tpu_custom_call" | custom-call | tf_op jit(solution)/shard_map/experts/pallas_call | solution.py:431
  63.3 1.6 %collective-permute-done.21.refs_2_ = bf16[3,16,2176]{2,1,0:T(8,128)(2,1)S(1)} collective-permute-done((bf16[3,16,2176]{2,1,0:T(8,128)(2,1)S(1)}, bf16[3,16,2176]{2,1,0:T(8,128)(2,1)S(1)}, u32[]{:S(2)}, u32[]{:S(2)}) %collective-permute-start.21) | collective-permute-done | bytes 208928 | tf_op jit(solution)/shard_map/ppermute | solution.py:151
  66.9 2.7 %experts.4 = (f32[1,2,3,128,512]{4,3,2,1,0:T(8,128)S(1)}, bf16[1,2,3,128,512]{4,3,2,1,0:T(8,128)(2,1)S(1)}) custom-call(bf16[3,32,2176]{2,1,0:T(8,128)(2,1)S(1)} %collective-permute-done.15.refs_0_, bf16[3,32,2176]{2,1,0:T(8,128)(2,1)S(1)} %collective-permute-done.20.refs_1_, bf16[3,16,2176]{2,1,0:T(8,128)(2,1)S(1)} %collective-permute-done.21.refs_2_, ...), custom_call_target="tpu_custom_call" | custom-call | tf_op jit(solution)/shard_map/experts/pallas_call | solution.py:431
  69.9 2.0 %experts.5 = (f32[2,2,1,128,512]{4,3,2,1,0:T(8,128)S(1)}, bf16[2,2,1,128,512]{4,3,2,1,0:T(8,128)(2,1)S(1)}) custom-call(bf16[1,32,2176]{2,1,0:T(8,128)(2,1)S(1)} %bitcast.57, bf16[1,32,2176]{2,1,0:T(8,128)(2,1)S(1)} %collective-permute-done.6.refs_1_, bf16[1,32,2176]{2,1,0:T(8,128)(2,1)S(1)} %collective-permute-done.10.refs_2_, ...), custom_call_target="tpu_custom_call" | custom-call | tf_op jit(solution)/shard_map/experts/pallas_call | solution.py:431
  72.8 1.8 %collective-permute-start.30 = (bf16[3,64,512]{2,1,0:T(8,128)(2,1)S(1)}, bf16[3,64,512]{2,1,0:T(8,128)(2,1)S(1)}, u32[]{:S(2)}, u32[]{:S(2)}) collective-permute-start(bf16[3,64,512]{2,1,0:T(8,128)(2,1)S(1)} %get-tuple-element.109), channel_id=1, source_target_pairs={{0,4},{4,0},{8,12},{12,8},{16,20},{20,16},{24,28},{28,24},{1,5},{5... | collective-permute-start | bytes 589832 | tf_op jit(solution)/shard_map/ppermute | solution.py:151
  74.6 1.5 %collective-permute-start.31 = (bf16[3,64,512]{2,1,0:T(8,128)(2,1)S(1)}, bf16[3,64,512]{2,1,0:T(8,128)(2,1)S(1)}, u32[]{:S(2)}, u32[]{:S(2)}) collective-permute-start(bf16[3,64,512]{2,1,0:T(8,128)(2,1)S(1)} %get-tuple-element.108), channel_id=1, source_target_pairs={{0,2},{1,3},{2,0},{3,1},{4,6},{5,7},{6,4},{7,5},{8,10},{9,11},{10,... | collective-permute-start | bytes 589832 | tf_op jit(solution)/shard_map/ppermute | solution.py:151
  76.2 3.8 %collective-permute-done.30 = bf16[3,64,512]{2,1,0:T(8,128)(2,1)S(1)} collective-permute-done((bf16[3,64,512]{2,1,0:T(8,128)(2,1)S(1)}, bf16[3,64,512]{2,1,0:T(8,128)(2,1)S(1)}, u32[]{:S(2)}, u32[]{:S(2)}) %collective-permute-start.30) | collective-permute-done | bytes 196640 | tf_op jit(solution)/shard_map/ppermute | solution.py:151
  80.0 1.5 %collective-permute-done.31 = bf16[3,64,512]{2,1,0:T(8,128)(2,1)S(1)} collective-permute-done((bf16[3,64,512]{2,1,0:T(8,128)(2,1)S(1)}, bf16[3,64,512]{2,1,0:T(8,128)(2,1)S(1)}, u32[]{:S(2)}, u32[]{:S(2)}) %collective-permute-start.31) | collective-permute-done | bytes 196640 | tf_op jit(solution)/shard_map/ppermute | solution.py:151
  81.7 1.6 %collective-permute-start.35 = (bf16[3,128,512]{2,1,0:T(8,128)(2,1)S(1)}, bf16[3,128,512]{2,1,0:T(8,128)(2,1)S(1)}, u32[]{:S(2)}, u32[]{:S(2)}) collective-permute-start(bf16[3,128,512]{2,1,0:T(8,128)(2,1)S(1)} %pad_maximum_fusion.2), channel_id=1, source_target_pairs={{0,2},{1,3},{2,0},{3,1},{4,6},{5,7},{6,4},{7,5},{8,10},{9,11},{10,... | collective-permute-start | bytes 1179656 | tf_op jit(solution)/shard_map/ppermute | solution.py:151
  84.0 1.7 %collective-permute-start.32 = (bf16[1,64,512]{2,1,0:T(8,128)(2,1)S(1)}, bf16[1,64,512]{2,1,0:T(8,128)(2,1)S(1)}, u32[]{:S(2)}, u32[]{:S(2)}) collective-permute-start(bf16[1,64,512]{2,1,0:T(8,128)(2,1)S(1)} %get-tuple-element.111), channel_id=1, source_target_pairs={{0,4},{4,0},{8,12},{12,8},{16,20},{20,16},{24,28},{28,24},{1,5},{5... | collective-permute-start | bytes 196616 | tf_op jit(solution)/shard_map/ppermute | solution.py:151
  86.2 8.5 %collective-permute-done.32 = bf16[1,64,512]{2,1,0:T(8,128)(2,1)S(1)} collective-permute-done((bf16[1,64,512]{2,1,0:T(8,128)(2,1)S(1)}, bf16[1,64,512]{2,1,0:T(8,128)(2,1)S(1)}, u32[]{:S(2)}, u32[]{:S(2)}) %collective-permute-start.32) | collective-permute-done | bytes 65568 | tf_op jit(solution)/shard_map/ppermute | solution.py:151
  95.0 2.2 %collective-permute-start.38 = (bf16[128,512]{1,0:T(8,128)(2,1)S(1)}, bf16[128,512]{1,0:T(8,128)(2,1)S(1)}, u32[]{:S(2)}, u32[]{:S(2)}) collective-permute-start(bf16[128,512]{1,0:T(8,128)(2,1)S(1)} %get-tuple-element.107), channel_id=1, source_target_pairs={{0,8},{4,12},{8,0},{12,4},{16,24},{20,28},{24,16},{28,20},{1,9},{5... | collective-permute-start | bytes 393224 | tf_op jit(solution)/shard_map/ppermute | solution.py:151
  97.2 2.3 %collective-permute-start.39 = (bf16[128,512]{1,0:T(8,128)(2,1)S(1)}, bf16[128,512]{1,0:T(8,128)(2,1)S(1)}, u32[]{:S(2)}, u32[]{:S(2)}) collective-permute-start(bf16[128,512]{1,0:T(8,128)(2,1)S(1)} %get-tuple-element.106), channel_id=1, source_target_pairs={{0,16},{4,20},{8,24},{12,28},{16,0},{20,4},{24,8},{28,12},{1,17},{... | collective-permute-start | bytes 393224 | tf_op jit(solution)/shard_map/ppermute | solution.py:151
  101.1 7.1 %collective-permute-done.39.z2_ref = bf16[128,512]{1,0:T(8,128)(2,1)S(1)} collective-permute-done((bf16[128,512]{1,0:T(8,128)(2,1)S(1)}, bf16[128,512]{1,0:T(8,128)(2,1)S(1)}, u32[]{:S(2)}, u32[]{:S(2)}) %collective-permute-start.39) | collective-permute-done | bytes 131104 | tf_op jit(solution)/shard_map/ppermute | solution.py:151
  (100 shorter events, 13.2 us)
Async XLA Ops:
  0.0 6.7 %collective-permute-start.1 = (bf16[128,512]{1,0:T(8,128)(2,1)}, bf16[128,512]{1,0:T(8,128)(2,1)S(1)}, u32[]{:S(2)}, u32[]{:S(2)}) collective-permute-start(bf16[128,512]{1,0:T(8,128)(2,1)} %refs_0_.1), channel_id=1, source_target_pairs={{0,2},{1,3},{2,0},{3,1},{4,6},{5,7},{6,4},{7,5},{8,10},{9,11},{10,... | collective-permute-start | bytes 393224 | tf_op jit(solution)/shard_map/ppermute | solution.py:151
  3.0 3.7 %collective-permute-start = (bf16[128,512]{1,0:T(8,128)(2,1)}, bf16[128,512]{1,0:T(8,128)(2,1)S(1)}, u32[]{:S(2)}, u32[]{:S(2)}) collective-permute-start(bf16[128,512]{1,0:T(8,128)(2,1)} %refs_0_.1), channel_id=1, source_target_pairs={{0,1},{1,0},{2,3},{3,2},{4,5},{5,4},{6,7},{7,6},{8,9},{9,8},{10,11... | collective-permute-start | bytes 393224 | tf_op jit(solution)/shard_map/ppermute | solution.py:151
  17.8 6.5 %collective-permute-start.4 = (bf16[32,2048]{1,0:T(8,128)(2,1)}, bf16[32,2048]{1,0:T(8,128)(2,1)S(1)}, u32[]{:S(2)}, u32[]{:S(2)}) collective-permute-start(bf16[32,2048]{1,0:T(8,128)(2,1)} %get-tuple-element.54), channel_id=1, source_target_pairs={{0,2},{1,3},{2,0},{3,1},{4,6},{5,7},{6,4},{7,5},{8,10},{9,11},{10,... | collective-permute-start | bytes 393224 | tf_op jit(solution)/shard_map/ppermute | solution.py:151
  19.6 6.5 %collective-permute-start.5 = (bf16[32,2048]{1,0:T(8,128)(2,1)}, bf16[32,2048]{1,0:T(8,128)(2,1)S(1)}, u32[]{:S(2)}, u32[]{:S(2)}) collective-permute-start(bf16[32,2048]{1,0:T(8,128)(2,1)} %get-tuple-element.55), channel_id=1, source_target_pairs={{0,3},{1,2},{2,1},{3,0},{4,7},{5,6},{6,5},{7,4},{8,11},{9,10},{10,... | collective-permute-start | bytes 393224 | tf_op jit(solution)/shard_map/ppermute | solution.py:151
  27.2 13.5 %collective-permute-start.8 = (bf16[32,2176]{1,0:T(8,128)(2,1)S(1)}, bf16[32,2176]{1,0:T(8,128)(2,1)S(1)}, u32[]{:S(2)}, u32[]{:S(2)}) collective-permute-start(bf16[32,2176]{1,0:T(8,128)(2,1)S(1)} %get-tuple-element.56), channel_id=1, source_target_pairs={{0,16},{4,20},{8,24},{12,28},{16,0},{20,4},{24,8},{28,12},{1,17},{... | collective-permute-start | bytes 417800 | tf_op jit(solution)/shard_map/ppermute | solution.py:151
  30.1 10.6 %collective-permute-start.9 = (bf16[32,2176]{1,0:T(8,128)(2,1)S(1)}, bf16[32,2176]{1,0:T(8,128)(2,1)S(1)}, u32[]{:S(2)}, u32[]{:S(2)}) collective-permute-start(bf16[32,2176]{1,0:T(8,128)(2,1)S(1)} %get-tuple-element.56), channel_id=1, source_target_pairs={{0,24},{4,28},{8,16},{12,20},{16,8},{20,12},{24,0},{28,4},{1,25},{... | collective-permute-start | bytes 417800 | tf_op jit(solution)/shard_map/ppermute | solution.py:151
  31.5 10.2 %collective-permute-start.7 = (bf16[32,2176]{1,0:T(8,128)(2,1)S(1)}, bf16[32,2176]{1,0:T(8,128)(2,1)S(1)}, u32[]{:S(2)}, u32[]{:S(2)}) collective-permute-start(bf16[32,2176]{1,0:T(8,128)(2,1)S(1)} %get-tuple-element.56), channel_id=1, source_target_pairs={{0,8},{4,12},{8,0},{12,4},{16,24},{20,28},{24,16},{28,20},{1,9},{5... | collective-permute-start | bytes 417800 | tf_op jit(solution)/shard_map/ppermute | solution.py:151
  31.7 10.0 %collective-permute-start.10 = (bf16[1,32,2176]{2,1,0:T(8,128)(2,1)S(1)}, bf16[1,32,2176]{2,1,0:T(8,128)(2,1)S(1)}, u32[]{:S(2)}, u32[]{:S(2)}) collective-permute-start(bf16[1,32,2176]{2,1,0:T(8,128)(2,1)S(1)} %bitcast.54), channel_id=1, source_target_pairs={{0,2},{1,3},{2,0},{3,1},{4,6},{5,7},{6,4},{7,5},{8,10},{9,11},{10,... | collective-permute-start | bytes 417800 | tf_op jit(solution)/shard_map/ppermute | solution.py:151
  33.2 9.1 %collective-permute-start.11 = (bf16[1,32,2176]{2,1,0:T(8,128)(2,1)S(1)}, bf16[1,32,2176]{2,1,0:T(8,128)(2,1)S(1)}, u32[]{:S(2)}, u32[]{:S(2)}) collective-permute-start(bf16[1,32,2176]{2,1,0:T(8,128)(2,1)S(1)} %bitcast.55), channel_id=1, source_target_pairs={{0,4},{4,0},{8,12},{12,8},{16,20},{20,16},{24,28},{28,24},{1,5},{5... | collective-permute-start | bytes 417800 | tf_op jit(solution)/shard_map/ppermute | solution.py:151
  42.3 14.9 %collective-permute-start.14 = (bf16[3,32,2176]{2,1,0:T(8,128)(2,1)S(1)}, bf16[3,32,2176]{2,1,0:T(8,128)(2,1)S(1)}, u32[]{:S(2)}, u32[]{:S(2)}) collective-permute-start(bf16[3,32,2176]{2,1,0:T(8,128)(2,1)S(1)} %pad_maximum_fusion.refs_0_), channel_id=1, source_target_pairs={{0,2},{1,3},{2,0},{3,1},{4,6},{5,7},{6,4},{7,5},{8,10},{9,11},{10,... | collective-permute-start | bytes 1253384 | tf_op jit(solution)/shard_map/ppermute | solution.py:151
  43.4 13.7 %collective-permute-start.15 = (bf16[3,32,2176]{2,1,0:T(8,128)(2,1)S(1)}, bf16[3,32,2176]{2,1,0:T(8,128)(2,1)S(1)}, u32[]{:S(2)}, u32[]{:S(2)}) collective-permute-start(bf16[3,32,2176]{2,1,0:T(8,128)(2,1)S(1)} %pad_maximum_fusion.refs_0_), channel_id=1, source_target_pairs={{0,4},{4,0},{8,12},{12,8},{16,20},{20,16},{24,28},{28,24},{1,5},{5... | collective-permute-start | bytes 1253384 | tf_op jit(solution)/shard_map/ppermute | solution.py:151
  47.4 6.8 %collective-permute-start.12 = (bf16[1,16,2176]{2,1,0:T(8,128)(2,1)S(1)}, bf16[1,16,2176]{2,1,0:T(8,128)(2,1)S(1)}, u32[]{:S(2)}, u32[]{:S(2)}) collective-permute-start(bf16[1,16,2176]{2,1,0:T(8,128)(2,1)S(1)} %slice.109), channel_id=1, source_target_pairs={{0,2},{1,3},{2,0},{3,1},{4,6},{5,7},{6,4},{7,5},{8,10},{9,11},{10,... | collective-permute-start | bytes 208904 | tf_op jit(solution)/shard_map/ppermute | solution.py:151
  48.0 9.1 %collective-permute-start.13 = (bf16[1,16,2176]{2,1,0:T(8,128)(2,1)S(1)}, bf16[1,16,2176]{2,1,0:T(8,128)(2,1)S(1)}, u32[]{:S(2)}, u32[]{:S(2)}) collective-permute-start(bf16[1,16,2176]{2,1,0:T(8,128)(2,1)S(1)} %slice.110), channel_id=1, source_target_pairs={{0,4},{4,0},{8,12},{12,8},{16,20},{20,16},{24,28},{28,24},{1,5},{5... | collective-permute-start | bytes 208904 | tf_op jit(solution)/shard_map/ppermute | solution.py:151
  48.8 11.2 %collective-permute-start.16 = (bf16[3,32,2176]{2,1,0:T(8,128)(2,1)S(1)}, bf16[3,32,2176]{2,1,0:T(8,128)(2,1)S(1)}, u32[]{:S(2)}, u32[]{:S(2)}) collective-permute-start(bf16[3,32,2176]{2,1,0:T(8,128)(2,1)S(1)} %pad_maximum_fusion.refs_0_), channel_id=1, source_target_pairs={{0,1},{1,0},{2,3},{3,2},{4,5},{5,4},{6,7},{7,6},{8,9},{9,8},{10,11... | collective-permute-start | bytes 1253384 | tf_op jit(solution)/shard_map/ppermute | solution.py:151
  57.1 8.0 %collective-permute-start.20 = (bf16[3,32,2176]{2,1,0:T(8,128)(2,1)S(1)}, bf16[3,32,2176]{2,1,0:T(8,128)(2,1)S(1)}, u32[]{:S(2)}, u32[]{:S(2)}) collective-permute-start(bf16[3,32,2176]{2,1,0:T(8,128)(2,1)S(1)} %collective-permute-done.15.refs_0_), channel_id=1, source_target_pairs={{0,1},{1,0},{2,3},{3,2},{4,5},{5,4},{6,7},{7,6},{8,9},{9,8},{10,11... | collective-permute-start | bytes 1253384 | tf_op jit(solution)/shard_map/ppermute | solution.py:151
  57.7 7.2 %collective-permute-start.21 = (bf16[3,16,2176]{2,1,0:T(8,128)(2,1)S(1)}, bf16[3,16,2176]{2,1,0:T(8,128)(2,1)S(1)}, u32[]{:S(2)}, u32[]{:S(2)}) collective-permute-start(bf16[3,16,2176]{2,1,0:T(8,128)(2,1)S(1)} %slice.111), channel_id=1, source_target_pairs={{0,2},{1,3},{2,0},{3,1},{4,6},{5,7},{6,4},{7,5},{8,10},{9,11},{10,... | collective-permute-start | bytes 626696 | tf_op jit(solution)/shard_map/ppermute | solution.py:151
  58.2 6.9 %collective-permute-start.22 = (bf16[3,16,2176]{2,1,0:T(8,128)(2,1)S(1)}, bf16[3,16,2176]{2,1,0:T(8,128)(2,1)S(1)}, u32[]{:S(2)}, u32[]{:S(2)}) collective-permute-start(bf16[3,16,2176]{2,1,0:T(8,128)(2,1)S(1)} %slice.112), channel_id=1, source_target_pairs={{0,4},{4,0},{8,12},{12,8},{16,20},{20,16},{24,28},{28,24},{1,5},{5... | collective-permute-start | bytes 626696 | tf_op jit(solution)/shard_map/ppermute | solution.py:151
  65.6 4.0 %collective-permute-start.25 = (bf16[1,16,2176]{2,1,0:T(8,128)(2,1)S(1)}, bf16[1,16,2176]{2,1,0:T(8,128)(2,1)S(1)}, u32[]{:S(2)}, u32[]{:S(2)}) collective-permute-start(bf16[1,16,2176]{2,1,0:T(8,128)(2,1)S(1)} %collective-permute-done.12.refs_6_), channel_id=1, source_target_pairs={{0,1},{1,0},{2,3},{3,2},{4,5},{5,4},{6,7},{7,6},{8,9},{9,8},{10,11... | collective-permute-start | bytes 208904 | tf_op jit(solution)/shard_map/ppermute | solution.py:151
  65.6 4.0 %collective-permute-start.26 = (bf16[1,16,2176]{2,1,0:T(8,128)(2,1)S(1)}, bf16[1,16,2176]{2,1,0:T(8,128)(2,1)S(1)}, u32[]{:S(2)}, u32[]{:S(2)}) collective-permute-start(bf16[1,16,2176]{2,1,0:T(8,128)(2,1)S(1)} %collective-permute-done.13.refs_7_), channel_id=1, source_target_pairs={{0,1},{1,0},{2,3},{3,2},{4,5},{5,4},{6,7},{7,6},{8,9},{9,8},{10,11... | collective-permute-start | bytes 208904 | tf_op jit(solution)/shard_map/ppermute | solution.py:151
  72.0 9.5 %collective-permute-start.28 = (bf16[1,2,3,128,512]{4,3,2,1,0:T(8,128)(2,1)S(1)}, bf16[1,2,3,128,512]{4,3,2,1,0:T(8,128)(2,1)S(1)}, u32[]{:S(2)}, u32[]{:S(2)}) collective-permute-start(bf16[1,2,3,128,512]{4,3,2,1,0:T(8,128)(2,1)S(1)} %get-tuple-element.84), channel_id=1, source_target_pairs={{0,1},{1,0},{2,3},{3,2},{4,5},{5,4},{6,7},{7,6},{8,9},{9,8},{10,11... | collective-permute-start | bytes 2359304 | tf_op jit(solution)/shard_map/ppermute | solution.py:151
  72.3 9.2 %collective-permute-start.29 = (bf16[2,2,1,128,512]{4,3,2,1,0:T(8,128)(2,1)S(1)}, bf16[2,2,1,128,512]{4,3,2,1,0:T(8,128)(2,1)S(1)}, u32[]{:S(2)}, u32[]{:S(2)}) collective-permute-start(bf16[2,2,1,128,512]{4,3,2,1,0:T(8,128)(2,1)S(1)} %get-tuple-element.86), channel_id=1, source_target_pairs={{0,1},{1,0},{2,3},{3,2},{4,5},{5,4},{6,7},{7,6},{8,9},{9,8},{10,11... | collective-permute-start | bytes 1572872 | tf_op jit(solution)/shard_map/ppermute | solution.py:151
  72.8 7.2 %collective-permute-start.30 = (bf16[3,64,512]{2,1,0:T(8,128)(2,1)S(1)}, bf16[3,64,512]{2,1,0:T(8,128)(2,1)S(1)}, u32[]{:S(2)}, u32[]{:S(2)}) collective-permute-start(bf16[3,64,512]{2,1,0:T(8,128)(2,1)S(1)} %get-tuple-element.109), channel_id=1, source_target_pairs={{0,4},{4,0},{8,12},{12,8},{16,20},{20,16},{24,28},{28,24},{1,5},{5... | collective-permute-start | bytes 589832 | tf_op jit(solution)/shard_map/ppermute | solution.py:151
  74.6 6.8 %collective-permute-start.31 = (bf16[3,64,512]{2,1,0:T(8,128)(2,1)S(1)}, bf16[3,64,512]{2,1,0:T(8,128)(2,1)S(1)}, u32[]{:S(2)}, u32[]{:S(2)}) collective-permute-start(bf16[3,64,512]{2,1,0:T(8,128)(2,1)S(1)} %get-tuple-element.108), channel_id=1, source_target_pairs={{0,2},{1,3},{2,0},{3,1},{4,6},{5,7},{6,4},{7,5},{8,10},{9,11},{10,... | collective-permute-start | bytes 589832 | tf_op jit(solution)/shard_map/ppermute | solution.py:151
  81.7 13.0 %collective-permute-start.35 = (bf16[3,128,512]{2,1,0:T(8,128)(2,1)S(1)}, bf16[3,128,512]{2,1,0:T(8,128)(2,1)S(1)}, u32[]{:S(2)}, u32[]{:S(2)}) collective-permute-start(bf16[3,128,512]{2,1,0:T(8,128)(2,1)S(1)} %pad_maximum_fusion.2), channel_id=1, source_target_pairs={{0,2},{1,3},{2,0},{3,1},{4,6},{5,7},{6,4},{7,5},{8,10},{9,11},{10,... | collective-permute-start | bytes 1179656 | tf_op jit(solution)/shard_map/ppermute | solution.py:151
  83.3 11.4 %collective-permute-start.34 = (bf16[3,128,512]{2,1,0:T(8,128)(2,1)S(1)}, bf16[3,128,512]{2,1,0:T(8,128)(2,1)S(1)}, u32[]{:S(2)}, u32[]{:S(2)}) collective-permute-start(bf16[3,128,512]{2,1,0:T(8,128)(2,1)S(1)} %pad_maximum_fusion.1), channel_id=1, source_target_pairs={{0,4},{4,0},{8,12},{12,8},{16,20},{20,16},{24,28},{28,24},{1,5},{5... | collective-permute-start | bytes 1179656 | tf_op jit(solution)/shard_map/ppermute | solution.py:151
  84.0 10.8 %collective-permute-start.32 = (bf16[1,64,512]{2,1,0:T(8,128)(2,1)S(1)}, bf16[1,64,512]{2,1,0:T(8,128)(2,1)S(1)}, u32[]{:S(2)}, u32[]{:S(2)}) collective-permute-start(bf16[1,64,512]{2,1,0:T(8,128)(2,1)S(1)} %get-tuple-element.111), channel_id=1, source_target_pairs={{0,4},{4,0},{8,12},{12,8},{16,20},{20,16},{24,28},{28,24},{1,5},{5... | collective-permute-start | bytes 196616 | tf_op jit(solution)/shard_map/ppermute | solution.py:151
  85.7 9.0 %collective-permute-start.33 = (bf16[1,64,512]{2,1,0:T(8,128)(2,1)S(1)}, bf16[1,64,512]{2,1,0:T(8,128)(2,1)S(1)}, u32[]{:S(2)}, u32[]{:S(2)}) collective-permute-start(bf16[1,64,512]{2,1,0:T(8,128)(2,1)S(1)} %get-tuple-element.110), channel_id=1, source_target_pairs={{0,2},{1,3},{2,0},{3,1},{4,6},{5,7},{6,4},{7,5},{8,10},{9,11},{10,... | collective-permute-start | bytes 196616 | tf_op jit(solution)/shard_map/ppermute | solution.py:151
  95.0 6.1 %collective-permute-start.38 = (bf16[128,512]{1,0:T(8,128)(2,1)S(1)}, bf16[128,512]{1,0:T(8,128)(2,1)S(1)}, u32[]{:S(2)}, u32[]{:S(2)}) collective-permute-start(bf16[128,512]{1,0:T(8,128)(2,1)S(1)} %get-tuple-element.107), channel_id=1, source_target_pairs={{0,8},{4,12},{8,0},{12,4},{16,24},{20,28},{24,16},{28,20},{1,9},{5... | collective-permute-start | bytes 393224 | tf_op jit(solution)/shard_map/ppermute | solution.py:151
  97.2 11.0 %collective-permute-start.39 = (bf16[128,512]{1,0:T(8,128)(2,1)S(1)}, bf16[128,512]{1,0:T(8,128)(2,1)S(1)}, u32[]{:S(2)}, u32[]{:S(2)}) collective-permute-start(bf16[128,512]{1,0:T(8,128)(2,1)S(1)} %get-tuple-element.106), channel_id=1, source_target_pairs={{0,16},{4,20},{8,24},{12,28},{16,0},{20,4},{24,8},{28,12},{1,17},{... | collective-permute-start | bytes 393224 | tf_op jit(solution)/shard_map/ppermute | solution.py:151
  99.5 8.7 %collective-permute-start.40 = (bf16[128,512]{1,0:T(8,128)(2,1)S(1)}, bf16[128,512]{1,0:T(8,128)(2,1)S(1)}, u32[]{:S(2)}, u32[]{:S(2)}) collective-permute-start(bf16[128,512]{1,0:T(8,128)(2,1)S(1)} %get-tuple-element.105), channel_id=1, source_target_pairs={{0,24},{4,28},{8,16},{12,20},{16,8},{20,12},{24,0},{28,4},{1,25},{... | collective-permute-start | bytes 393224 | tf_op jit(solution)/shard_map/ppermute | solution.py:151
  99.7 8.5 %collective-permute-start.37 = (bf16[1,128,512]{2,1,0:T(8,128)(2,1)S(1)}, bf16[1,128,512]{2,1,0:T(8,128)(2,1)S(1)}, u32[]{:S(2)}, u32[]{:S(2)}) collective-permute-start(bf16[1,128,512]{2,1,0:T(8,128)(2,1)S(1)} %pad_maximum_fusion.4), channel_id=1, source_target_pairs={{0,2},{1,3},{2,0},{3,1},{4,6},{5,7},{6,4},{7,5},{8,10},{9,11},{10,... | collective-permute-start | bytes 393224 | tf_op jit(solution)/shard_map/ppermute | solution.py:151
  100.3 7.9 %collective-permute-start.36 = (bf16[1,128,512]{2,1,0:T(8,128)(2,1)S(1)}, bf16[1,128,512]{2,1,0:T(8,128)(2,1)S(1)}, u32[]{:S(2)}, u32[]{:S(2)}) collective-permute-start(bf16[1,128,512]{2,1,0:T(8,128)(2,1)S(1)} %pad_maximum_fusion.3), channel_id=1, source_target_pairs={{0,4},{4,0},{8,12},{12,8},{16,20},{20,16},{24,28},{28,24},{1,5},{5... | collective-permute-start | bytes 393224 | tf_op jit(solution)/shard_map/ppermute | solution.py:151
  (19 other events, 222.6 us)

commit v8 on v7

--- a/solution.py
+++ b/solution.py
@@ -151,56 +151,87 @@
     return lax.ppermute(value, axis, [(i, i ^ bits) for i in range(lax.axis_size(axis))])
 
 
+def layout_kernel(
+    length_ref, table_ref, frequency_ref, cosine_ref, sine_ref, owner_ref, list_ref, count_ref, live_ref
+):
+    tokens, head_dim = cosine_ref.shape
+    slots = list_ref.shape[0]
+    owners = live_ref
+    for entry in range(slots):
+        list_ref[entry] = 0
+        owners[0, entry] = -1
+        owners[1, entry] = 0
+    count = jnp.int32(0)
+    for request in range(1, REQS_DEV):
+
+        def name_page(entry, count):
+            list_ref[count] = table_ref[request, entry]
+            owners[0, count] = request
+            owners[1, count] = jnp.minimum(length_ref[request] - entry * PAGE, PAGE)
+            return count + 1
+
+        count = lax.fori_loop(0, (length_ref[request] + PAGE - 1) // PAGE, name_page, count)
+    count_ref[0] = count
+    slot = lax.broadcasted_iota(jnp.int32, (1, PAGE), 1)
+    for entry in range(slots):
+        owner_ref[:, entry * PAGE : (entry + 1) * PAGE] = jnp.where(
+            slot < owners[1, entry], owners[0, entry], -1
+        )
+    token = lax.broadcasted_iota(jnp.int32, (tokens, head_dim), 0)
+    lane = lax.broadcasted_iota(jnp.int32, (tokens, head_dim), 1)
+    position = length_ref[0] + token
+    for i in range(tokens - PRE):
+        position = jnp.where(token == PRE + i, length_ref[i + 1], position)
+    angle = position.astype(jnp.float32) * frequency_ref[...]
+    sine = jnp.sin(angle)
+    cosine_ref[...] = jnp.cos(angle)
+    sine_ref[...] = jnp.where(lane < head_dim // 2, -sine, sine)
+
+
 def attention_kernel(*refs):
-    pieces, hbm_refs, (keep_out, near_out, far_out, cross_out) = refs[:4], refs[4:16], refs[16:20]
-    local_refs, value_hbm = refs[20:31], hbm_refs[11]
-    (length_ref, table_ref, gain_ref, frequency_ref, q_gain_ref, k_gain_ref) = local_refs[:6]
-    (q_ref, k_ref, v_ref, key_ref, o_ref) = local_refs[6:]
+    pieces, hbm_refs, (keep_out, far_out, core_out) = refs[:4], refs[4:20], refs[20:23]
+    local_refs = refs[23:39]
+    (length_ref, table_ref, list_ref, count_ref, gain_ref, q_gain_ref, k_gain_ref) = local_refs[:7]
+    (cosine_ref, sine_ref, owner_ref, q_ref, k_ref, v_ref, key_ref, value_ref, o_ref) = local_refs[7:]
     (
-        value_ref, x_ref, query_ref, own_scores, top_ref, scores_ref, mix_ref, mixed_ref, part_ref,
-        owner_ref, slots_ref, page_owner, page_live, sems,
-    ) = refs[31:]
+        x_ref, query_ref, own_scores, top_ref, scores_ref, mix_ref, mixed_ref, part_ref, slots_ref,
+        decode_top, decode_mix, sems,
+    ) = refs[39:]
     tokens, head_dim = x_ref.shape[0], k_gain_ref.shape[1]
-    targets = (*local_refs, value_ref.at[:, :, :head_dim])
     copies = [
         pltpu.make_async_copy(source, target, sems.at[i])
-        for i, (source, target) in enumerate(zip(hbm_refs, targets))
+        for i, (source, target) in enumerate(zip(hbm_refs, local_refs))
     ]
     for copy in copies:
         copy.start()
     tp_index = lax.axis_index("tp")
     heads = q_ref.shape[1] // head_dim
     decodes = tokens - PRE
-    rows = heads * tokens
-    value_ref[:, :, head_dim:] = jnp.ones((POOL, PAGE, head_dim), jnp.bfloat16)
     for step, piece in enumerate(pieces):
         width = piece.shape[1]
         start = pl.multiple_of((tp_index ^ step) * width, width)
         x_ref[:, pl.ds(start, width)] = piece[...]
-    for copy in copies[:6]:
+    for copy in copies[:10]:
         copy.wait()
     token = lax.broadcasted_iota(jnp.int32, (tokens, head_dim), 0)
     lane = lax.broadcasted_iota(jnp.int32, (tokens, head_dim), 1)
-    position = length_ref[0] + token
-    for i in range(decodes):
-        position = jnp.where(token == PRE + i, length_ref[i + 1], position)
-    angle = position.astype(jnp.float32) * frequency_ref[...]
-    cosine, sine = jnp.cos(angle), jnp.sin(angle)
-    sine = jnp.where(lane < head_dim // 2, -sine, sine)
 
     def turned(values, gain):
         values = rms_scale(values, gain)
-        return values * cosine + pltpu.roll(values, head_dim // 2, 1) * sine
+        return values * cosine_ref[...] + pltpu.roll(values, head_dim // 2, 1) * sine_ref[...]
+
+    def with_ones(values):
+        return jnp.concatenate([values, jnp.ones_like(values)], axis=1)
 
     normed = rms_scale(x_ref[...].astype(jnp.float32), gain_ref[...]).astype(jnp.bfloat16)
     contract = (((1,), (1,)), ((), ()))
-    for copy in copies[6:9]:
+    for copy in copies[10:13]:
         copy.wait()
     key_lin = jnp.dot(normed, k_ref[...], preferred_element_type=jnp.float32)
     values_new = jnp.dot(normed, v_ref[...], preferred_element_type=jnp.float32).astype(jnp.bfloat16)
     query_lin = jnp.dot(normed, q_ref[...], preferred_element_type=jnp.float32)
     keys_new = turned(key_lin, k_gain_ref[...]).astype(jnp.bfloat16)
-    values_new = jnp.concatenate([values_new, jnp.ones_like(values_new)], axis=1)
+    values_new = with_ones(values_new)
     to_log2 = math.log2(math.e) / math.sqrt(head_dim)
     own_mask = (lane == token) | ((lane < token) & (token < PRE))
     decode_query, decode_own = [], []
@@ -217,66 +248,66 @@
         decode_own.append(scores[PRE:])
     decode_query = jnp.concatenate(decode_query, axis=0).astype(jnp.bfloat16)
     decode_own = jnp.concatenate(decode_own, axis=0)
-    for page in range(POOL):
-        page_owner[page] = -1
-        page_live[page] = 0
-    for request in range(1, REQS_DEV):
-
-        def name_page(entry, carry):
-            page = table_ref[request, entry]
-            page_owner[page] = request
-            page_live[page] = jnp.minimum(length_ref[request] - entry * PAGE, PAGE)
-            return carry
-
-        lax.fori_loop(0, (length_ref[request] + PAGE - 1) // PAGE, name_page, 0)
-    slot = lax.broadcasted_iota(jnp.int32, (1, PAGE), 1)
-    for page in range(POOL):
-        owner_ref[:, page * PAGE : (page + 1) * PAGE] = jnp.where(
-            slot < page_live[page], page_owner[page], -1
-        )
-    copies[9].wait()
+    for copy in copies[13:15]:
+        copy.wait()
+
+    def raised(top, scores):
+        for start in range(0, scores.shape[1], head_dim):
+            top = jnp.maximum(top, scores[:, start : start + head_dim])
+        return top
+
     pages = scores_ref.shape[2] // PAGE
     width = pages * PAGE
     length = length_ref[0]
     steps = (length + width - 1) // width
     column = lax.broadcasted_iota(jnp.int32, (1, width), 1)
 
-    def named(ref, step):
+    def own_pages(ref, step):
         names = [table_ref[0, jnp.minimum(step * pages + i, MAXPG - 1)] for i in range(pages)]
         return jnp.concatenate([ref[name] for name in names], axis=0)
 
     def score(step, carry):
         scores = lax.dot_general(
-            query_ref[...], named(key_ref, step), contract, preferred_element_type=jnp.float32
+            query_ref[...], own_pages(key_ref, step), contract, preferred_element_type=jnp.float32
         )
         scores = jnp.where(column + step * width < length, scores, -1e30)
         scores_ref[step] = scores
-        top = top_ref[...]
-        for page in range(pages):
-            top = jnp.maximum(top, scores[:, page * PAGE : (page + 1) * PAGE])
-        top_ref[...] = top
+        top_ref[...] = raised(top_ref[...], scores)
         return carry
 
     lax.fori_loop(0, steps, score, 0)
+    listed = slots_ref.shape[2] // PAGE
+    decode_steps = (count_ref[0] + listed - 1) // listed
     row_request = 1 + lax.broadcasted_iota(jnp.int32, (heads * decodes, 1), 0) % decodes
-    top = decode_own
-    span = 8 * PAGE
-    for start in range(0, POOL * PAGE, span):
-        keys = key_ref[start // PAGE : (start + span) // PAGE].reshape(span, head_dim)
-        scores = lax.dot_general(decode_query, keys, contract, preferred_element_type=jnp.float32)
-        scores = jnp.where(owner_ref[:, start : start + span] == row_request, scores, -1e30)
-        slots_ref[:, start : start + span] = scores
-        for page in range(8):
-            top = jnp.maximum(top, scores[:, page * PAGE : (page + 1) * PAGE])
-    top = jnp.max(top, axis=1, keepdims=True)
-    copies[11].wait()
-    decode_mix = jnp.dot(
+    decode_top[...] = decode_own
+
+    def listed_pages(ref, step):
+        return jnp.concatenate([ref[list_ref[step * listed + i]] for i in range(listed)], axis=0)
+
+    def decode_score(step, carry):
+        scores = lax.dot_general(
+            decode_query, listed_pages(key_ref, step), contract, preferred_element_type=jnp.float32
+        )
+        start = pl.multiple_of(step * listed * PAGE, listed * PAGE)
+        scores = jnp.where(owner_ref[:, pl.ds(start, listed * PAGE)] == row_request, scores, -1e30)
+        slots_ref[step] = scores
+        decode_top[...] = raised(decode_top[...], scores)
+        return carry
+
+    lax.fori_loop(0, decode_steps, decode_score, 0)
+    top = jnp.max(decode_top[...], axis=1, keepdims=True)
+    decode_mix[...] = jnp.dot(
         jnp.exp2(decode_own - top).astype(jnp.bfloat16), values_new, preferred_element_type=jnp.float32
     )
-    for start in range(0, POOL * PAGE, span):
-        weights = jnp.exp2(slots_ref[:, start : start + span] - top).astype(jnp.bfloat16)
-        values = value_ref[start // PAGE : (start + span) // PAGE].reshape(span, 2 * head_dim)
-        decode_mix = decode_mix + jnp.dot(weights, values, preferred_element_type=jnp.float32)
+
+    def decode_mixed(step, carry):
+        weights = jnp.exp2(slots_ref[step] - top).astype(jnp.bfloat16)
+        decode_mix[...] += jnp.dot(
+            weights, with_ones(listed_pages(value_ref, step)), preferred_element_type=jnp.float32
+        )
+        return carry
+
+    lax.fori_loop(0, decode_steps, decode_mixed, 0)
     decoded = decode_mix[:, :head_dim] / decode_mix[:, head_dim:]
     top = jnp.max(top_ref[...], axis=1, keepdims=True)
     top_ref[...] = jnp.broadcast_to(top, top_ref.shape)
@@ -286,7 +317,9 @@
 
     def mix(step, carry):
         weights = jnp.exp2(scores_ref[step] - top_ref[:, :1]).astype(jnp.bfloat16)
-        mix_ref[...] += jnp.dot(weights, named(value_ref, step), preferred_element_type=jnp.float32)
+        mix_ref[...] += jnp.dot(
+            weights, with_ones(own_pages(value_ref, step)), preferred_element_type=jnp.float32
+        )
         return carry
 
     lax.fori_loop(0, steps, mix, 0)
@@ -295,48 +328,71 @@
         columns = slice(head * head_dim, (head + 1) * head_dim)
         mixed_ref[:, columns] = part[:, :head_dim] / part[:, head_dim:]
         mixed_ref[PRE:, columns] = decoded[head * decodes : (head + 1) * decodes]
-    copies[10].wait()
+    copies[15].wait()
     part_ref[...] = jnp.dot(
         mixed_ref[...].astype(jnp.bfloat16), o_ref[...], preferred_element_type=jnp.float32
     )
     share_rows = keep_out.shape[0]
-    for step, out_ref in enumerate((keep_out, near_out, far_out, cross_out)):
-        mine = pl.ds(pl.multiple_of((tp_index ^ step) * share_rows, share_rows), share_rows)
-        part = part_ref[mine, :]
-        if step == 0:
-            part = part + x_ref[mine, :].astype(jnp.float32)
-        out_ref[...] = part.astype(out_ref.dtype)
+
+    def quarter(step):
+        return pl.ds(pl.multiple_of((tp_index ^ step) * share_rows, share_rows), share_rows)
+
+    keep_out[...] = part_ref[quarter(0), :] + x_ref[quarter(0), :].astype(jnp.float32)
+    far_out[...] = part_ref[quarter(2), :]
+    core_out[0] = part_ref[quarter(1), :].astype(jnp.bfloat16)
+    core_out[1] = part_ref[quarter(3), :].astype(jnp.bfloat16)
 
 
 def attention_shares(
     hidden_in, norm_in_gain, q_weight, k_weight, v_weight, q_gain, k_gain, o_weight,
     key_pages, value_pages, page_table, cache_len,
 ):
-    far = flip(hidden_in, "tp", 2)
-    pieces = (hidden_in, flip(hidden_in, "tp", 1), far, flip(far, "tp", 1))
     tokens, width = hidden_in.shape[0], 4 * hidden_in.shape[1]
     head_dim = q_gain.shape[0]
     rows = q_weight.shape[1] // head_dim * tokens
     decode_rows = rows // tokens * (tokens - PRE)
     half = ROPE_BASE ** (-np.arange(head_dim // 2) / (head_dim // 2))
     frequency = jnp.asarray(np.concatenate([half, half])[None, :], jnp.float32)
-    scalars = (cache_len, page_table)
+    params = pltpu.CompilerParams(vmem_limit_bytes=56 * 1024 * 1024)
+    rope = jax.ShapeDtypeStruct((tokens, head_dim), jnp.float32)
+    cosine, sine, owner, page_list, page_count = pl.pallas_call(
+        layout_kernel,
+        out_shape=[
+            rope,
+            rope,
+            jax.ShapeDtypeStruct((1, POOL * PAGE), jnp.int32),
+            jax.ShapeDtypeStruct((POOL,), jnp.int32),
+            jax.ShapeDtypeStruct((1,), jnp.int32),
+        ],
+        in_specs=[SMEM, SMEM, VMEM],
+        out_specs=[VMEM, VMEM, VMEM, SMEM, SMEM],
+        scratch_shapes=[pltpu.SMEM((2, POOL), jnp.int32)],
+        compiler_params=params,
+        name="layout",
+    )(cache_len, page_table, frequency)
+    far, cosine, sine, owner, page_list, page_count = ordered(
+        flip(hidden_in, "tp", 2), cosine, sine, owner, page_list, page_count
+    )
+    pieces = (hidden_in, flip(hidden_in, "tp", 1), far, flip(far, "tp", 1))
+    scalars = (cache_len, page_table, page_list, page_count)
     arrays = (
-        norm_in_gain[None, :], frequency, q_gain[None, :], k_gain[None, :],
-        q_weight, k_weight, v_weight, key_pages[0], o_weight,
+        norm_in_gain[None, :], q_gain[None, :], k_gain[None, :], cosine, sine, owner,
+        q_weight, k_weight, v_weight, key_pages[0], value_pages[0], o_weight,
     )
     share = (tokens // 4, width)
-    score_pages = 4
+    score_pages, list_pages = 4, 8
     return pl.pallas_call(
         attention_kernel,
-        out_shape=[jax.ShapeDtypeStruct(share, jnp.float32)]
-        + [jax.ShapeDtypeStruct(share, jnp.bfloat16)] * 3,
-        in_specs=[VMEM] * 4 + [pl.BlockSpec(memory_space=pltpu.HBM)] * 12,
-        out_specs=[VMEM] * 4,
+        out_shape=[
+            jax.ShapeDtypeStruct(share, jnp.float32),
+            jax.ShapeDtypeStruct(share, jnp.float32),
+            jax.ShapeDtypeStruct((2, *share), jnp.bfloat16),
+        ],
+        in_specs=[VMEM] * 4 + [pl.BlockSpec(memory_space=pltpu.HBM)] * 16,
+        out_specs=[VMEM] * 3,
         scratch_shapes=[pltpu.SMEM(array.shape, array.dtype) for array in scalars]
         + [pltpu.VMEM(array.shape, array.dtype) for array in arrays]
         + [
-            pltpu.VMEM((POOL, PAGE, 2 * head_dim), jnp.bfloat16),
             pltpu.VMEM((tokens, width), jnp.bfloat16),
             pltpu.VMEM((rows, head_dim), jnp.bfloat16),
             pltpu.VMEM((rows, tokens), jnp.float32),
@@ -345,27 +401,24 @@
             pltpu.VMEM((rows, 2 * head_dim), jnp.float32),
             pltpu.VMEM((tokens, q_weight.shape[1]), jnp.float32),
             pltpu.VMEM((tokens, width), jnp.float32),
-            pltpu.VMEM((1, POOL * PAGE), jnp.int32),
-            pltpu.VMEM((decode_rows, POOL * PAGE), jnp.float32),
-            pltpu.SMEM((POOL,), jnp.int32),
-            pltpu.SMEM((POOL,), jnp.int32),
-            pltpu.SemaphoreType.DMA((12,)),
+            pltpu.VMEM((POOL // list_pages, decode_rows, list_pages * PAGE), jnp.float32),
+            pltpu.VMEM((decode_rows, head_dim), jnp.float32),
+            pltpu.VMEM((decode_rows, 2 * head_dim), jnp.float32),
+            pltpu.SemaphoreType.DMA((16,)),
         ],
-        compiler_params=pltpu.CompilerParams(vmem_limit_bytes=56 * 1024 * 1024),
+        compiler_params=params,
         name="attention",
-    )(*pieces, *scalars, *arrays, value_pages[0])
+    )(*pieces, *scalars, *arrays)
 
 
 def pack_kernel(
-    own_ref, near_ref, far_ref, cross_ref, gain_ref, ids_ref, routes_ref,
+    own_ref, core_ref, far_ref, gain_ref, ids_ref, routes_ref,
     rows_ref, residual_ref, spread_ref,
 ):
     tp_index = lax.axis_index("tp")
     share_rows, width = own_ref.shape
     mine = pl.ds(pl.multiple_of(tp_index * share_rows, share_rows), share_rows)
-    residual = (own_ref[...] + near_ref[...].astype(jnp.float32)) + (
-        far_ref[...].astype(jnp.float32) + cross_ref[...].astype(jnp.float32)
-    )
+    residual = own_ref[...] + core_ref[0].astype(jnp.float32) + far_ref[...].astype(jnp.float32)
     residual_ref[...] = residual
     rows_ref[:, :width] = rms_scale(residual, gain_ref[...]).astype(jnp.bfloat16)
     expert = lax.broadcasted_iota(jnp.int32, (LANES, spread_ref.shape[0]), 0) % (LANES // 2)
@@ -503,7 +556,8 @@
 
 def moe_dense(
     kept,
-    sent,
+    far,
+    core,
     norm_post_gain,
     expert_ids,
     route_weights,
@@ -513,19 +567,20 @@
 ):
     share_rows, width = kept.shape
     token_count, share_width = 4 * share_rows, width // 4
-    received = [flip(part, "tp", bits) for bits, part in enumerate(sent, 1)]
+    core = flip(core, "tp", 1)
+    far = flip((far + core[1].astype(jnp.float32)).astype(jnp.bfloat16), "tp", 2)
     rows, residual = pl.pallas_call(
         pack_kernel,
         out_shape=[
             jax.ShapeDtypeStruct((share_rows, width + LANES), jnp.bfloat16),
             jax.ShapeDtypeStruct((share_rows, width), jnp.float32),
         ],
-        in_specs=[VMEM] * 7,
+        in_specs=[VMEM] * 6,
         out_specs=[VMEM] * 2,
         scratch_shapes=[pltpu.VMEM((token_count, LANES), jnp.float32)],
         compiler_params=pltpu.CompilerParams(vmem_limit_bytes=8 * 1024 * 1024),
         name="pack_rows",
-    )(kept, *received, norm_post_gain[None, :], expert_ids.T, route_weights.T)
+    )(kept, core, far, norm_post_gain[None, :], expert_ids.T, route_weights.T)
     gate_up = [w.transpose(0, 2, 1).reshape(-1, width) for w in (gate_weight, up_weight)]
     weights = (*gate_up, down_weight.reshape(-1, width))
     line_0 = rows[None]
@@ -712,8 +767,7 @@
     expert_count = gate_weight.shape[0] * req_count
     staged = (req_count, lax.axis_size("tp"), gate_weight.shape[0]) == (8, 4, 2)
     if staged and expert_count <= LANES // 2:
-        kept, *sent = attention_shares(hidden_in, *attention)
-        return moe_dense(kept, sent, *experts)
+        return moe_dense(*attention_shares(hidden_in, *attention), *experts)
     x_full = lax.all_gather(hidden_in, "tp", axis=1, tiled=True)
     return moe_routed(x_full, attention_part(x_full, *attention), *experts)
 

time: 109 us -> 108 us (level)
  starting transfers between devices: 41.1 us -> 37 us
  Pallas kernels: 17.3 us -> 21 us
  waiting for transfers between devices: 47.4 us -> 45.7 us
  other arithmetic: 1 us -> 2.13 us
    ppermute x41 -> x40, starting transfers between devices: 41.1 us -> 37 us  [flip(): lax.ppermute(value, axis, [(i, i ^ bits) for i in range(lax.axis_size(axi...]
    pallas_call x0 -> x1, Pallas kernels: none -> 2.31 us  [attention_shares(): pl.pallas_call(layout_kernel, out_shape=[rope, rope, jax.ShapeDtypeStruct...]
    ppermute x41 -> x40, waiting for transfers between devices: 47.4 us -> 45.7 us  [flip(): lax.ppermute(value, axis, [(i, i ^ bits) for i in range(lax.axis_size(axi...]
    pallas_call x1, Pallas kernels: 8.86 us -> 10.3 us  [attention_shares(): pl.pallas_call(attention_kernel, out_shape=[jax.ShapeDtypeStruct(share, j...]
    convert_element_type x0 -> x1, other arithmetic: none -> 1.13 us  [moe_dense(): (far + core[1].astype(jnp.float32)).astype(jnp.bfloat16)]
  transfers between devices with their start and end apart: 41 -> 40, of which waited for: 20 -> 17; matrix products, arithmetic and copies ran while one was open for 1% -> 1% of each run, Pallas kernels for 7% -> 9%
where the time goes in v8:
time: 108 us
  waiting for transfers between devices  45.7 us (42%)
  starting transfers between devices  37 us (34%)
  Pallas kernels  21 us (19%)
  other arithmetic  2.13 us (2%)
  local copies, waits for them, and re-layouts  1.82 us (2%)
    ppermute x40, waiting for transfers between devices, flip(): lax.ppermute(value, axis, [(i, i ^ bits) for i in range(lax.axis_size(axi...  45.7 us
    ppermute x40, starting transfers between devices, flip(): lax.ppermute(value, axis, [(i, i ^ bits) for i in range(lax.axis_size(axi...  37 us
    pallas_call x1, Pallas kernels, attention_shares(): pl.pallas_call(attention_kernel, out_shape=[jax.ShapeDtypeStruct(share, j...  10.3 us
    pallas_call x3, Pallas kernels, run_experts(): pl.pallas_call(functools.partial(experts_kernel, plan), out_shape=[jax.Sh...  7.46 us
    pallas_call x1, Pallas kernels, attention_shares(): pl.pallas_call(layout_kernel, out_shape=[rope, rope, jax.ShapeDtypeStruct...  2.31 us
  transfers between devices with their start and end apart: 40, of which 17 were waited for; matrix products, arithmetic and copies ran while one was open for 1% of the time, Pallas kernels for 9%

profile of v8, /device:TPU:0, one launch (start us, length us, event | category | flops | bytes accessed | tf_op | source)
XLA Modules:
  0.0 108.0 jit_solution(11400377792134248733)
XLA Ops:
  0.0 3.0 %collective-permute-start.1 = (bf16[128,512]{1,0:T(8,128)(2,1)}, bf16[128,512]{1,0:T(8,128)(2,1)S(1)}, u32[]{:S(2)}, u32[]{:S(2)}) collective-permute-start(bf16[128,512]{1,0:T(8,128)(2,1)} %refs_0_.1), channel_id=1, source_target_pairs={{0,2},{1,3},{2,0},{3,1},{4,6},{5,7},{6,4},{7,5},{8,10},{9,11},{10,... | collective-permute-start | bytes 393224 | tf_op jit(solution)/shard_map/ppermute | solution.py:151
  3.0 2.3 %layout.1 = (f32[128,128]{1,0:T(8,128)}, f32[128,128]{1,0:T(8,128)}, s32[1,6144]{1,0:T(1,128)}, s32[48]{0:T(128)}, s32[1]{0:T(128)}) custom-call(s32[9]{0:T(128)} %refs_4_.1, s32[9,32]{1,0:T(8,128)} %refs_5_.1, f32[1,128]{1,0:T(1,128)} %constant.2.clone.frequency_ref), custom_call_target="tpu_custom_call" | custom-call | tf_op jit(solution)/shard_map/layout/pallas_call | solution.py:358
  5.3 1.4 %collective-permute-done.1.refs_2_ = bf16[128,512]{1,0:T(8,128)(2,1)S(1)} collective-permute-done((bf16[128,512]{1,0:T(8,128)(2,1)}, bf16[128,512]{1,0:T(8,128)(2,1)S(1)}, u32[]{:S(2)}, u32[]{:S(2)}) %collective-permute-start.1) | collective-permute-done | bytes 131104 | tf_op jit(solution)/shard_map/ppermute | solution.py:151
  6.7 1.3 %collective-permute-done.2.refs_3_ = bf16[128,512]{1,0:T(8,128)(2,1)S(1)} collective-permute-done((bf16[128,512]{1,0:T(8,128)(2,1)S(1)}, bf16[128,512]{1,0:T(8,128)(2,1)S(1)}, u32[]{:S(2)}, u32[]{:S(2)}) %collective-permute-start.2) | collective-permute-done | bytes 131104 | tf_op jit(solution)/shard_map/ppermute | solution.py:151
  8.7 10.3 %attention.1 = (f32[32,2048]{1,0:T(8,128)}, f32[32,2048]{1,0:T(8,128)}, bf16[2,32,2048]{2,1,0:T(8,128)(2,1)}) custom-call(bf16[128,512]{1,0:T(8,128)(2,1)} %refs_0_.1, bf16[128,512]{1,0:T(8,128)(2,1)} %copy-done.8, bf16[128,512]{1,0:T(8,128)(2,1)} %copy-done.7, bf16[128,512]{1,0:T(8,128)(2,1)} %copy-done.9, s32[9]{0:T(128)} %refs_4_.1, s32[9,32]{1,0:T(8,128)} %refs_5_.1, ...), custom_call_target="tpu_custom_call" | custom-call | tf_op jit(solution)/shard_map/attention/pallas_call | solution.py:384
  19.2 1.6 %collective-permute-done.3.core_ref = bf16[2,32,2048]{2,1,0:T(8,128)(2,1)S(1)} collective-permute-done((bf16[2,32,2048]{2,1,0:T(8,128)(2,1)}, bf16[2,32,2048]{2,1,0:T(8,128)(2,1)S(1)}, u32[]{:S(2)}, u32[]{:S(2)}) %collective-permute-start.3) | collective-permute-done | bytes 262176 | tf_op jit(solution)/shard_map/ppermute | solution.py:151
  21.9 1.8 %collective-permute-start.4 = (bf16[32,2048]{1,0:T(8,128)(2,1)S(1)}, bf16[32,2048]{1,0:T(8,128)(2,1)S(1)}, u32[]{:S(2)}, u32[]{:S(2)}) collective-permute-start(bf16[32,2048]{1,0:T(8,128)(2,1)S(1)} %fusion.5), channel_id=1, source_target_pairs={{0,2},{1,3},{2,0},{3,1},{4,6},{5,7},{6,4},{7,5},{8,10},{9,11},{10,... | collective-permute-start | bytes 393224 | tf_op jit(solution)/shard_map/ppermute | solution.py:151
  23.7 3.8 %collective-permute-done.4.far_ref = bf16[32,2048]{1,0:T(8,128)(2,1)S(1)} collective-permute-done((bf16[32,2048]{1,0:T(8,128)(2,1)S(1)}, bf16[32,2048]{1,0:T(8,128)(2,1)S(1)}, u32[]{:S(2)}, u32[]{:S(2)}) %collective-permute-start.4) | collective-permute-done | bytes 131104 | tf_op jit(solution)/shard_map/ppermute | solution.py:151
  28.7 1.4 %collective-permute-start.6 = (bf16[32,2176]{1,0:T(8,128)(2,1)S(1)}, bf16[32,2176]{1,0:T(8,128)(2,1)S(1)}, u32[]{:S(2)}, u32[]{:S(2)}) collective-permute-start(bf16[32,2176]{1,0:T(8,128)(2,1)S(1)} %get-tuple-element.76), channel_id=1, source_target_pairs={{0,8},{4,12},{8,0},{12,4},{16,24},{20,28},{24,16},{28,20},{1,9},{5... | collective-permute-start | bytes 417800 | tf_op jit(solution)/shard_map/ppermute | solution.py:151
  30.2 3.0 %collective-permute-start.7 = (bf16[32,2176]{1,0:T(8,128)(2,1)S(1)}, bf16[32,2176]{1,0:T(8,128)(2,1)S(1)}, u32[]{:S(2)}, u32[]{:S(2)}) collective-permute-start(bf16[32,2176]{1,0:T(8,128)(2,1)S(1)} %get-tuple-element.76), channel_id=1, source_target_pairs={{0,16},{4,20},{8,24},{12,28},{16,0},{20,4},{24,8},{28,12},{1,17},{... | collective-permute-start | bytes 417800 | tf_op jit(solution)/shard_map/ppermute | solution.py:151
  33.2 1.7 %collective-permute-start.10 = (bf16[1,32,2176]{2,1,0:T(8,128)(2,1)S(1)}, bf16[1,32,2176]{2,1,0:T(8,128)(2,1)S(1)}, u32[]{:S(2)}, u32[]{:S(2)}) collective-permute-start(bf16[1,32,2176]{2,1,0:T(8,128)(2,1)S(1)} %bitcast.59), channel_id=1, source_target_pairs={{0,4},{4,0},{8,12},{12,8},{16,20},{20,16},{24,28},{28,24},{1,5},{5... | collective-permute-start | bytes 417800 | tf_op jit(solution)/shard_map/ppermute | solution.py:151
  34.9 1.5 %collective-permute-start.9 = (bf16[1,32,2176]{2,1,0:T(8,128)(2,1)S(1)}, bf16[1,32,2176]{2,1,0:T(8,128)(2,1)S(1)}, u32[]{:S(2)}, u32[]{:S(2)}) collective-permute-start(bf16[1,32,2176]{2,1,0:T(8,128)(2,1)S(1)} %bitcast.60), channel_id=1, source_target_pairs={{0,2},{1,3},{2,0},{3,1},{4,6},{5,7},{6,4},{7,5},{8,10},{9,11},{10,... | collective-permute-start | bytes 417800 | tf_op jit(solution)/shard_map/ppermute | solution.py:151
  36.4 7.1 %collective-permute-done.7 = bf16[32,2176]{1,0:T(8,128)(2,1)S(1)} collective-permute-done((bf16[32,2176]{1,0:T(8,128)(2,1)S(1)}, bf16[32,2176]{1,0:T(8,128)(2,1)S(1)}, u32[]{:S(2)}, u32[]{:S(2)}) %collective-permute-start.7) | collective-permute-done | bytes 139296 | tf_op jit(solution)/shard_map/ppermute | solution.py:151
  43.6 1.6 %collective-permute-start.13 = (bf16[3,32,2176]{2,1,0:T(8,128)(2,1)S(1)}, bf16[3,32,2176]{2,1,0:T(8,128)(2,1)S(1)}, u32[]{:S(2)}, u32[]{:S(2)}) collective-permute-start(bf16[3,32,2176]{2,1,0:T(8,128)(2,1)S(1)} %pad_maximum_fusion.refs_0_), channel_id=1, source_target_pairs={{0,2},{1,3},{2,0},{3,1},{4,6},{5,7},{6,4},{7,5},{8,10},{9,11},{10,... | collective-permute-start | bytes 1253384 | tf_op jit(solution)/shard_map/ppermute | solution.py:151
  45.2 1.5 %collective-permute-start.14 = (bf16[3,32,2176]{2,1,0:T(8,128)(2,1)S(1)}, bf16[3,32,2176]{2,1,0:T(8,128)(2,1)S(1)}, u32[]{:S(2)}, u32[]{:S(2)}) collective-permute-start(bf16[3,32,2176]{2,1,0:T(8,128)(2,1)S(1)} %pad_maximum_fusion.refs_0_), channel_id=1, source_target_pairs={{0,4},{4,0},{8,12},{12,8},{16,20},{20,16},{24,28},{28,24},{1,5},{5... | collective-permute-start | bytes 1253384 | tf_op jit(solution)/shard_map/ppermute | solution.py:151
  48.3 5.0 %collective-permute-done.11.refs_6_ = bf16[1,16,2176]{2,1,0:T(8,128)(2,1)S(1)} collective-permute-done((bf16[1,16,2176]{2,1,0:T(8,128)(2,1)S(1)}, bf16[1,16,2176]{2,1,0:T(8,128)(2,1)S(1)}, u32[]{:S(2)}, u32[]{:S(2)}) %collective-permute-start.11) | collective-permute-done | bytes 69664 | tf_op jit(solution)/shard_map/ppermute | solution.py:151
  53.2 1.5 %collective-permute-done.12.refs_7_ = bf16[1,16,2176]{2,1,0:T(8,128)(2,1)S(1)} collective-permute-done((bf16[1,16,2176]{2,1,0:T(8,128)(2,1)S(1)}, bf16[1,16,2176]{2,1,0:T(8,128)(2,1)S(1)}, u32[]{:S(2)}, u32[]{:S(2)}) %collective-permute-start.12) | collective-permute-done | bytes 69664 | tf_op jit(solution)/shard_map/ppermute | solution.py:151
  55.9 1.5 %collective-permute-start.21 = (bf16[3,16,2176]{2,1,0:T(8,128)(2,1)S(1)}, bf16[3,16,2176]{2,1,0:T(8,128)(2,1)S(1)}, u32[]{:S(2)}, u32[]{:S(2)}) collective-permute-start(bf16[3,16,2176]{2,1,0:T(8,128)(2,1)S(1)} %slice.116), channel_id=1, source_target_pairs={{0,4},{4,0},{8,12},{12,8},{16,20},{20,16},{24,28},{28,24},{1,5},{5... | collective-permute-start | bytes 626696 | tf_op jit(solution)/shard_map/ppermute | solution.py:151
  58.0 2.7 %experts.3 = (f32[1,2,3,128,512]{4,3,2,1,0:T(8,128)S(1)}, bf16[1,2,3,128,512]{4,3,2,1,0:T(8,128)(2,1)S(1)}) custom-call(bf16[3,32,2176]{2,1,0:T(8,128)(2,1)S(1)} %pad_maximum_fusion.refs_0_, bf16[3,32,2176]{2,1,0:T(8,128)(2,1)S(1)} %collective-permute-done.15.refs_1_, bf16[3,32,2176]{2,1,0:T(8,128)(2,1)S(1)} %collective-permute-done.13.refs_2_, ...), custom_call_target="tpu_custom_call" | custom-call | tf_op jit(solution)/shard_map/experts/pallas_call | solution.py:484
  60.7 1.8 %collective-permute-done.20.refs_2_ = bf16[3,16,2176]{2,1,0:T(8,128)(2,1)S(1)} collective-permute-done((bf16[3,16,2176]{2,1,0:T(8,128)(2,1)S(1)}, bf16[3,16,2176]{2,1,0:T(8,128)(2,1)S(1)}, u32[]{:S(2)}, u32[]{:S(2)}) %collective-permute-start.20) | collective-permute-done | bytes 208928 | tf_op jit(solution)/shard_map/ppermute | solution.py:151
  64.5 2.7 %experts.4 = (f32[1,2,3,128,512]{4,3,2,1,0:T(8,128)S(1)}, bf16[1,2,3,128,512]{4,3,2,1,0:T(8,128)(2,1)S(1)}) custom-call(bf16[3,32,2176]{2,1,0:T(8,128)(2,1)S(1)} %collective-permute-done.14.refs_0_, bf16[3,32,2176]{2,1,0:T(8,128)(2,1)S(1)} %collective-permute-done.19.refs_1_, bf16[3,16,2176]{2,1,0:T(8,128)(2,1)S(1)} %collective-permute-done.20.refs_2_, ...), custom_call_target="tpu_custom_call" | custom-call | tf_op jit(solution)/shard_map/experts/pallas_call | solution.py:484
  67.6 2.0 %experts.5 = (f32[2,2,1,128,512]{4,3,2,1,0:T(8,128)S(1)}, bf16[2,2,1,128,512]{4,3,2,1,0:T(8,128)(2,1)S(1)}) custom-call(bf16[1,32,2176]{2,1,0:T(8,128)(2,1)S(1)} %bitcast.62, bf16[1,32,2176]{2,1,0:T(8,128)(2,1)S(1)} %collective-permute-done.5.refs_1_, bf16[1,32,2176]{2,1,0:T(8,128)(2,1)S(1)} %collective-permute-done.9.refs_2_, ...), custom_call_target="tpu_custom_call" | custom-call | tf_op jit(solution)/shard_map/experts/pallas_call | solution.py:484
  70.4 1.6 %collective-permute-start.29 = (bf16[3,64,512]{2,1,0:T(8,128)(2,1)S(1)}, bf16[3,64,512]{2,1,0:T(8,128)(2,1)S(1)}, u32[]{:S(2)}, u32[]{:S(2)}) collective-permute-start(bf16[3,64,512]{2,1,0:T(8,128)(2,1)S(1)} %get-tuple-element.129), channel_id=1, source_target_pairs={{0,4},{4,0},{8,12},{12,8},{16,20},{20,16},{24,28},{28,24},{1,5},{5... | collective-permute-start | bytes 589832 | tf_op jit(solution)/shard_map/ppermute | solution.py:151
  72.0 1.5 %collective-permute-start.30 = (bf16[3,64,512]{2,1,0:T(8,128)(2,1)S(1)}, bf16[3,64,512]{2,1,0:T(8,128)(2,1)S(1)}, u32[]{:S(2)}, u32[]{:S(2)}) collective-permute-start(bf16[3,64,512]{2,1,0:T(8,128)(2,1)S(1)} %get-tuple-element.128), channel_id=1, source_target_pairs={{0,2},{1,3},{2,0},{3,1},{4,6},{5,7},{6,4},{7,5},{8,10},{9,11},{10,... | collective-permute-start | bytes 589832 | tf_op jit(solution)/shard_map/ppermute | solution.py:151
  73.6 4.0 %collective-permute-done.29 = bf16[3,64,512]{2,1,0:T(8,128)(2,1)S(1)} collective-permute-done((bf16[3,64,512]{2,1,0:T(8,128)(2,1)S(1)}, bf16[3,64,512]{2,1,0:T(8,128)(2,1)S(1)}, u32[]{:S(2)}, u32[]{:S(2)}) %collective-permute-start.29) | collective-permute-done | bytes 196640 | tf_op jit(solution)/shard_map/ppermute | solution.py:151
  79.1 1.6 %collective-permute-start.34 = (bf16[3,128,512]{2,1,0:T(8,128)(2,1)S(1)}, bf16[3,128,512]{2,1,0:T(8,128)(2,1)S(1)}, u32[]{:S(2)}, u32[]{:S(2)}) collective-permute-start(bf16[3,128,512]{2,1,0:T(8,128)(2,1)S(1)} %pad_maximum_fusion.2), channel_id=1, source_target_pairs={{0,2},{1,3},{2,0},{3,1},{4,6},{5,7},{6,4},{7,5},{8,10},{9,11},{10,... | collective-permute-start | bytes 1179656 | tf_op jit(solution)/shard_map/ppermute | solution.py:151
  81.5 1.6 %collective-permute-start.31 = (bf16[1,64,512]{2,1,0:T(8,128)(2,1)S(1)}, bf16[1,64,512]{2,1,0:T(8,128)(2,1)S(1)}, u32[]{:S(2)}, u32[]{:S(2)}) collective-permute-start(bf16[1,64,512]{2,1,0:T(8,128)(2,1)S(1)} %get-tuple-element.131), channel_id=1, source_target_pairs={{0,4},{4,0},{8,12},{12,8},{16,20},{20,16},{24,28},{28,24},{1,5},{5... | collective-permute-start | bytes 196616 | tf_op jit(solution)/shard_map/ppermute | solution.py:151
  83.7 8.5 %collective-permute-done.31 = bf16[1,64,512]{2,1,0:T(8,128)(2,1)S(1)} collective-permute-done((bf16[1,64,512]{2,1,0:T(8,128)(2,1)S(1)}, bf16[1,64,512]{2,1,0:T(8,128)(2,1)S(1)}, u32[]{:S(2)}, u32[]{:S(2)}) %collective-permute-start.31) | collective-permute-done | bytes 65568 | tf_op jit(solution)/shard_map/ppermute | solution.py:151
  92.4 3.6 %collective-permute-start.37 = (bf16[128,512]{1,0:T(8,128)(2,1)S(1)}, bf16[128,512]{1,0:T(8,128)(2,1)S(1)}, u32[]{:S(2)}, u32[]{:S(2)}) collective-permute-start(bf16[128,512]{1,0:T(8,128)(2,1)S(1)} %get-tuple-element.127), channel_id=1, source_target_pairs={{0,8},{4,12},{8,0},{12,4},{16,24},{20,28},{24,16},{28,20},{1,9},{5... | collective-permute-start | bytes 393224 | tf_op jit(solution)/shard_map/ppermute | solution.py:151
  96.1 1.4 %collective-permute-start.38 = (bf16[128,512]{1,0:T(8,128)(2,1)S(1)}, bf16[128,512]{1,0:T(8,128)(2,1)S(1)}, u32[]{:S(2)}, u32[]{:S(2)}) collective-permute-start(bf16[128,512]{1,0:T(8,128)(2,1)S(1)} %get-tuple-element.126), channel_id=1, source_target_pairs={{0,16},{4,20},{8,24},{12,28},{16,0},{20,4},{24,8},{28,12},{1,17},{... | collective-permute-start | bytes 393224 | tf_op jit(solution)/shard_map/ppermute | solution.py:151
  97.5 1.4 %collective-permute-start.39 = (bf16[128,512]{1,0:T(8,128)(2,1)S(1)}, bf16[128,512]{1,0:T(8,128)(2,1)S(1)}, u32[]{:S(2)}, u32[]{:S(2)}) collective-permute-start(bf16[128,512]{1,0:T(8,128)(2,1)S(1)} %get-tuple-element.125), channel_id=1, source_target_pairs={{0,24},{4,28},{8,16},{12,20},{16,8},{20,12},{24,0},{28,4},{1,25},{... | collective-permute-start | bytes 393224 | tf_op jit(solution)/shard_map/ppermute | solution.py:151
  100.2 7.0 %collective-permute-done.38.z2_ref = bf16[128,512]{1,0:T(8,128)(2,1)S(1)} collective-permute-done((bf16[128,512]{1,0:T(8,128)(2,1)S(1)}, bf16[128,512]{1,0:T(8,128)(2,1)S(1)}, u32[]{:S(2)}, u32[]{:S(2)}) %collective-permute-start.38) | collective-permute-done | bytes 131104 | tf_op jit(solution)/shard_map/ppermute | solution.py:151
  (100 shorter events, 14.7 us)
Async XLA Ops:
  0.0 6.7 %collective-permute-start.1 = (bf16[128,512]{1,0:T(8,128)(2,1)}, bf16[128,512]{1,0:T(8,128)(2,1)S(1)}, u32[]{:S(2)}, u32[]{:S(2)}) collective-permute-start(bf16[128,512]{1,0:T(8,128)(2,1)} %refs_0_.1), channel_id=1, source_target_pairs={{0,2},{1,3},{2,0},{3,1},{4,6},{5,7},{6,4},{7,5},{8,10},{9,11},{10,... | collective-permute-start | bytes 393224 | tf_op jit(solution)/shard_map/ppermute | solution.py:151
  3.0 3.7 %collective-permute-start = (bf16[128,512]{1,0:T(8,128)(2,1)}, bf16[128,512]{1,0:T(8,128)(2,1)S(1)}, u32[]{:S(2)}, u32[]{:S(2)}) collective-permute-start(bf16[128,512]{1,0:T(8,128)(2,1)} %refs_0_.1), channel_id=1, source_target_pairs={{0,1},{1,0},{2,3},{3,2},{4,5},{5,4},{6,7},{7,6},{8,9},{9,8},{10,11... | collective-permute-start | bytes 393224 | tf_op jit(solution)/shard_map/ppermute | solution.py:151
  21.9 5.6 %collective-permute-start.4 = (bf16[32,2048]{1,0:T(8,128)(2,1)S(1)}, bf16[32,2048]{1,0:T(8,128)(2,1)S(1)}, u32[]{:S(2)}, u32[]{:S(2)}) collective-permute-start(bf16[32,2048]{1,0:T(8,128)(2,1)S(1)} %fusion.5), channel_id=1, source_target_pairs={{0,2},{1,3},{2,0},{3,1},{4,6},{5,7},{6,4},{7,5},{8,10},{9,11},{10,... | collective-permute-start | bytes 393224 | tf_op jit(solution)/shard_map/ppermute | solution.py:151
  28.7 7.7 %collective-permute-start.6 = (bf16[32,2176]{1,0:T(8,128)(2,1)S(1)}, bf16[32,2176]{1,0:T(8,128)(2,1)S(1)}, u32[]{:S(2)}, u32[]{:S(2)}) collective-permute-start(bf16[32,2176]{1,0:T(8,128)(2,1)S(1)} %get-tuple-element.76), channel_id=1, source_target_pairs={{0,8},{4,12},{8,0},{12,4},{16,24},{20,28},{24,16},{28,20},{1,9},{5... | collective-permute-start | bytes 417800 | tf_op jit(solution)/shard_map/ppermute | solution.py:151
  30.2 13.4 %collective-permute-start.7 = (bf16[32,2176]{1,0:T(8,128)(2,1)S(1)}, bf16[32,2176]{1,0:T(8,128)(2,1)S(1)}, u32[]{:S(2)}, u32[]{:S(2)}) collective-permute-start(bf16[32,2176]{1,0:T(8,128)(2,1)S(1)} %get-tuple-element.76), channel_id=1, source_target_pairs={{0,16},{4,20},{8,24},{12,28},{16,0},{20,4},{24,8},{28,12},{1,17},{... | collective-permute-start | bytes 417800 | tf_op jit(solution)/shard_map/ppermute | solution.py:151
  33.2 10.4 %collective-permute-start.8 = (bf16[32,2176]{1,0:T(8,128)(2,1)S(1)}, bf16[32,2176]{1,0:T(8,128)(2,1)S(1)}, u32[]{:S(2)}, u32[]{:S(2)}) collective-permute-start(bf16[32,2176]{1,0:T(8,128)(2,1)S(1)} %get-tuple-element.76), channel_id=1, source_target_pairs={{0,24},{4,28},{8,16},{12,20},{16,8},{20,12},{24,0},{28,4},{1,25},{... | collective-permute-start | bytes 417800 | tf_op jit(solution)/shard_map/ppermute | solution.py:151
  33.2 10.4 %collective-permute-start.10 = (bf16[1,32,2176]{2,1,0:T(8,128)(2,1)S(1)}, bf16[1,32,2176]{2,1,0:T(8,128)(2,1)S(1)}, u32[]{:S(2)}, u32[]{:S(2)}) collective-permute-start(bf16[1,32,2176]{2,1,0:T(8,128)(2,1)S(1)} %bitcast.59), channel_id=1, source_target_pairs={{0,4},{4,0},{8,12},{12,8},{16,20},{20,16},{24,28},{28,24},{1,5},{5... | collective-permute-start | bytes 417800 | tf_op jit(solution)/shard_map/ppermute | solution.py:151
  34.9 8.8 %collective-permute-start.9 = (bf16[1,32,2176]{2,1,0:T(8,128)(2,1)S(1)}, bf16[1,32,2176]{2,1,0:T(8,128)(2,1)S(1)}, u32[]{:S(2)}, u32[]{:S(2)}) collective-permute-start(bf16[1,32,2176]{2,1,0:T(8,128)(2,1)S(1)} %bitcast.60), channel_id=1, source_target_pairs={{0,2},{1,3},{2,0},{3,1},{4,6},{5,7},{6,4},{7,5},{8,10},{9,11},{10,... | collective-permute-start | bytes 417800 | tf_op jit(solution)/shard_map/ppermute | solution.py:151
  43.6 11.1 %collective-permute-start.13 = (bf16[3,32,2176]{2,1,0:T(8,128)(2,1)S(1)}, bf16[3,32,2176]{2,1,0:T(8,128)(2,1)S(1)}, u32[]{:S(2)}, u32[]{:S(2)}) collective-permute-start(bf16[3,32,2176]{2,1,0:T(8,128)(2,1)S(1)} %pad_maximum_fusion.refs_0_), channel_id=1, source_target_pairs={{0,2},{1,3},{2,0},{3,1},{4,6},{5,7},{6,4},{7,5},{8,10},{9,11},{10,... | collective-permute-start | bytes 1253384 | tf_op jit(solution)/shard_map/ppermute | solution.py:151
  45.2 9.5 %collective-permute-start.14 = (bf16[3,32,2176]{2,1,0:T(8,128)(2,1)S(1)}, bf16[3,32,2176]{2,1,0:T(8,128)(2,1)S(1)}, u32[]{:S(2)}, u32[]{:S(2)}) collective-permute-start(bf16[3,32,2176]{2,1,0:T(8,128)(2,1)S(1)} %pad_maximum_fusion.refs_0_), channel_id=1, source_target_pairs={{0,4},{4,0},{8,12},{12,8},{16,20},{20,16},{24,28},{28,24},{1,5},{5... | collective-permute-start | bytes 1253384 | tf_op jit(solution)/shard_map/ppermute | solution.py:151
  46.8 6.5 %collective-permute-start.11 = (bf16[1,16,2176]{2,1,0:T(8,128)(2,1)S(1)}, bf16[1,16,2176]{2,1,0:T(8,128)(2,1)S(1)}, u32[]{:S(2)}, u32[]{:S(2)}) collective-permute-start(bf16[1,16,2176]{2,1,0:T(8,128)(2,1)S(1)} %slice.113), channel_id=1, source_target_pairs={{0,2},{1,3},{2,0},{3,1},{4,6},{5,7},{6,4},{7,5},{8,10},{9,11},{10,... | collective-permute-start | bytes 208904 | tf_op jit(solution)/shard_map/ppermute | solution.py:151
  47.4 7.4 %collective-permute-start.12 = (bf16[1,16,2176]{2,1,0:T(8,128)(2,1)S(1)}, bf16[1,16,2176]{2,1,0:T(8,128)(2,1)S(1)}, u32[]{:S(2)}, u32[]{:S(2)}) collective-permute-start(bf16[1,16,2176]{2,1,0:T(8,128)(2,1)S(1)} %slice.114), channel_id=1, source_target_pairs={{0,4},{4,0},{8,12},{12,8},{16,20},{20,16},{24,28},{28,24},{1,5},{5... | collective-permute-start | bytes 208904 | tf_op jit(solution)/shard_map/ppermute | solution.py:151
  48.1 9.3 %collective-permute-start.15 = (bf16[3,32,2176]{2,1,0:T(8,128)(2,1)S(1)}, bf16[3,32,2176]{2,1,0:T(8,128)(2,1)S(1)}, u32[]{:S(2)}, u32[]{:S(2)}) collective-permute-start(bf16[3,32,2176]{2,1,0:T(8,128)(2,1)S(1)} %pad_maximum_fusion.refs_0_), channel_id=1, source_target_pairs={{0,1},{1,0},{2,3},{3,2},{4,5},{5,4},{6,7},{7,6},{8,9},{9,8},{10,11... | collective-permute-start | bytes 1253384 | tf_op jit(solution)/shard_map/ppermute | solution.py:151
  54.8 8.0 %collective-permute-start.19 = (bf16[3,32,2176]{2,1,0:T(8,128)(2,1)S(1)}, bf16[3,32,2176]{2,1,0:T(8,128)(2,1)S(1)}, u32[]{:S(2)}, u32[]{:S(2)}) collective-permute-start(bf16[3,32,2176]{2,1,0:T(8,128)(2,1)S(1)} %collective-permute-done.14.refs_0_), channel_id=1, source_target_pairs={{0,1},{1,0},{2,3},{3,2},{4,5},{5,4},{6,7},{7,6},{8,9},{9,8},{10,11... | collective-permute-start | bytes 1253384 | tf_op jit(solution)/shard_map/ppermute | solution.py:151
  55.3 7.2 %collective-permute-start.20 = (bf16[3,16,2176]{2,1,0:T(8,128)(2,1)S(1)}, bf16[3,16,2176]{2,1,0:T(8,128)(2,1)S(1)}, u32[]{:S(2)}, u32[]{:S(2)}) collective-permute-start(bf16[3,16,2176]{2,1,0:T(8,128)(2,1)S(1)} %slice.115), channel_id=1, source_target_pairs={{0,2},{1,3},{2,0},{3,1},{4,6},{5,7},{6,4},{7,5},{8,10},{9,11},{10,... | collective-permute-start | bytes 626696 | tf_op jit(solution)/shard_map/ppermute | solution.py:151
  55.9 6.9 %collective-permute-start.21 = (bf16[3,16,2176]{2,1,0:T(8,128)(2,1)S(1)}, bf16[3,16,2176]{2,1,0:T(8,128)(2,1)S(1)}, u32[]{:S(2)}, u32[]{:S(2)}) collective-permute-start(bf16[3,16,2176]{2,1,0:T(8,128)(2,1)S(1)} %slice.116), channel_id=1, source_target_pairs={{0,4},{4,0},{8,12},{12,8},{16,20},{20,16},{24,28},{28,24},{1,5},{5... | collective-permute-start | bytes 626696 | tf_op jit(solution)/shard_map/ppermute | solution.py:151
  57.4 3.3 %collective-permute-start.18 = (bf16[1,32,2176]{2,1,0:T(8,128)(2,1)S(1)}, bf16[1,32,2176]{2,1,0:T(8,128)(2,1)S(1)}, u32[]{:S(2)}, u32[]{:S(2)}) collective-permute-start(bf16[1,32,2176]{2,1,0:T(8,128)(2,1)S(1)} %collective-permute-done.9.refs_2_), channel_id=1, source_target_pairs={{0,1},{1,0},{2,3},{3,2},{4,5},{5,4},{6,7},{7,6},{8,9},{9,8},{10,11... | collective-permute-start | bytes 417800 | tf_op jit(solution)/shard_map/ppermute | solution.py:151
  63.3 4.0 %collective-permute-start.24 = (bf16[1,16,2176]{2,1,0:T(8,128)(2,1)S(1)}, bf16[1,16,2176]{2,1,0:T(8,128)(2,1)S(1)}, u32[]{:S(2)}, u32[]{:S(2)}) collective-permute-start(bf16[1,16,2176]{2,1,0:T(8,128)(2,1)S(1)} %collective-permute-done.11.refs_6_), channel_id=1, source_target_pairs={{0,1},{1,0},{2,3},{3,2},{4,5},{5,4},{6,7},{7,6},{8,9},{9,8},{10,11... | collective-permute-start | bytes 208904 | tf_op jit(solution)/shard_map/ppermute | solution.py:151
  63.3 4.0 %collective-permute-start.25 = (bf16[1,16,2176]{2,1,0:T(8,128)(2,1)S(1)}, bf16[1,16,2176]{2,1,0:T(8,128)(2,1)S(1)}, u32[]{:S(2)}, u32[]{:S(2)}) collective-permute-start(bf16[1,16,2176]{2,1,0:T(8,128)(2,1)S(1)} %collective-permute-done.12.refs_7_), channel_id=1, source_target_pairs={{0,1},{1,0},{2,3},{3,2},{4,5},{5,4},{6,7},{7,6},{8,9},{9,8},{10,11... | collective-permute-start | bytes 208904 | tf_op jit(solution)/shard_map/ppermute | solution.py:151
  69.6 9.2 %collective-permute-start.27 = (bf16[1,2,3,128,512]{4,3,2,1,0:T(8,128)(2,1)S(1)}, bf16[1,2,3,128,512]{4,3,2,1,0:T(8,128)(2,1)S(1)}, u32[]{:S(2)}, u32[]{:S(2)}) collective-permute-start(bf16[1,2,3,128,512]{4,3,2,1,0:T(8,128)(2,1)S(1)} %get-tuple-element.104), channel_id=1, source_target_pairs={{0,1},{1,0},{2,3},{3,2},{4,5},{5,4},{6,7},{7,6},{8,9},{9,8},{10,11... | collective-permute-start | bytes 2359304 | tf_op jit(solution)/shard_map/ppermute | solution.py:151
  69.9 8.9 %collective-permute-start.28 = (bf16[2,2,1,128,512]{4,3,2,1,0:T(8,128)(2,1)S(1)}, bf16[2,2,1,128,512]{4,3,2,1,0:T(8,128)(2,1)S(1)}, u32[]{:S(2)}, u32[]{:S(2)}) collective-permute-start(bf16[2,2,1,128,512]{4,3,2,1,0:T(8,128)(2,1)S(1)} %get-tuple-element.106), channel_id=1, source_target_pairs={{0,1},{1,0},{2,3},{3,2},{4,5},{5,4},{6,7},{7,6},{8,9},{9,8},{10,11... | collective-permute-start | bytes 1572872 | tf_op jit(solution)/shard_map/ppermute | solution.py:151
  70.4 7.2 %collective-permute-start.29 = (bf16[3,64,512]{2,1,0:T(8,128)(2,1)S(1)}, bf16[3,64,512]{2,1,0:T(8,128)(2,1)S(1)}, u32[]{:S(2)}, u32[]{:S(2)}) collective-permute-start(bf16[3,64,512]{2,1,0:T(8,128)(2,1)S(1)} %get-tuple-element.129), channel_id=1, source_target_pairs={{0,4},{4,0},{8,12},{12,8},{16,20},{20,16},{24,28},{28,24},{1,5},{5... | collective-permute-start | bytes 589832 | tf_op jit(solution)/shard_map/ppermute | solution.py:151
  72.0 6.8 %collective-permute-start.30 = (bf16[3,64,512]{2,1,0:T(8,128)(2,1)S(1)}, bf16[3,64,512]{2,1,0:T(8,128)(2,1)S(1)}, u32[]{:S(2)}, u32[]{:S(2)}) collective-permute-start(bf16[3,64,512]{2,1,0:T(8,128)(2,1)S(1)} %get-tuple-element.128), channel_id=1, source_target_pairs={{0,2},{1,3},{2,0},{3,1},{4,6},{5,7},{6,4},{7,5},{8,10},{9,11},{10,... | collective-permute-start | bytes 589832 | tf_op jit(solution)/shard_map/ppermute | solution.py:151
  79.1 13.0 %collective-permute-start.34 = (bf16[3,128,512]{2,1,0:T(8,128)(2,1)S(1)}, bf16[3,128,512]{2,1,0:T(8,128)(2,1)S(1)}, u32[]{:S(2)}, u32[]{:S(2)}) collective-permute-start(bf16[3,128,512]{2,1,0:T(8,128)(2,1)S(1)} %pad_maximum_fusion.2), channel_id=1, source_target_pairs={{0,2},{1,3},{2,0},{3,1},{4,6},{5,7},{6,4},{7,5},{8,10},{9,11},{10,... | collective-permute-start | bytes 1179656 | tf_op jit(solution)/shard_map/ppermute | solution.py:151
  80.8 11.4 %collective-permute-start.33 = (bf16[3,128,512]{2,1,0:T(8,128)(2,1)S(1)}, bf16[3,128,512]{2,1,0:T(8,128)(2,1)S(1)}, u32[]{:S(2)}, u32[]{:S(2)}) collective-permute-start(bf16[3,128,512]{2,1,0:T(8,128)(2,1)S(1)} %pad_maximum_fusion.1), channel_id=1, source_target_pairs={{0,4},{4,0},{8,12},{12,8},{16,20},{20,16},{24,28},{28,24},{1,5},{5... | collective-permute-start | bytes 1179656 | tf_op jit(solution)/shard_map/ppermute | solution.py:151
  81.5 10.6 %collective-permute-start.31 = (bf16[1,64,512]{2,1,0:T(8,128)(2,1)S(1)}, bf16[1,64,512]{2,1,0:T(8,128)(2,1)S(1)}, u32[]{:S(2)}, u32[]{:S(2)}) collective-permute-start(bf16[1,64,512]{2,1,0:T(8,128)(2,1)S(1)} %get-tuple-element.131), channel_id=1, source_target_pairs={{0,4},{4,0},{8,12},{12,8},{16,20},{20,16},{24,28},{28,24},{1,5},{5... | collective-permute-start | bytes 196616 | tf_op jit(solution)/shard_map/ppermute | solution.py:151
  83.1 9.0 %collective-permute-start.32 = (bf16[1,64,512]{2,1,0:T(8,128)(2,1)S(1)}, bf16[1,64,512]{2,1,0:T(8,128)(2,1)S(1)}, u32[]{:S(2)}, u32[]{:S(2)}) collective-permute-start(bf16[1,64,512]{2,1,0:T(8,128)(2,1)S(1)} %get-tuple-element.130), channel_id=1, source_target_pairs={{0,2},{1,3},{2,0},{3,1},{4,6},{5,7},{6,4},{7,5},{8,10},{9,11},{10,... | collective-permute-start | bytes 196616 | tf_op jit(solution)/shard_map/ppermute | solution.py:151
  92.4 7.8 %collective-permute-start.37 = (bf16[128,512]{1,0:T(8,128)(2,1)S(1)}, bf16[128,512]{1,0:T(8,128)(2,1)S(1)}, u32[]{:S(2)}, u32[]{:S(2)}) collective-permute-start(bf16[128,512]{1,0:T(8,128)(2,1)S(1)} %get-tuple-element.127), channel_id=1, source_target_pairs={{0,8},{4,12},{8,0},{12,4},{16,24},{20,28},{24,16},{28,20},{1,9},{5... | collective-permute-start | bytes 393224 | tf_op jit(solution)/shard_map/ppermute | solution.py:151
  96.1 11.2 %collective-permute-start.38 = (bf16[128,512]{1,0:T(8,128)(2,1)S(1)}, bf16[128,512]{1,0:T(8,128)(2,1)S(1)}, u32[]{:S(2)}, u32[]{:S(2)}) collective-permute-start(bf16[128,512]{1,0:T(8,128)(2,1)S(1)} %get-tuple-element.126), channel_id=1, source_target_pairs={{0,16},{4,20},{8,24},{12,28},{16,0},{20,4},{24,8},{28,12},{1,17},{... | collective-permute-start | bytes 393224 | tf_op jit(solution)/shard_map/ppermute | solution.py:151
  97.5 9.7 %collective-permute-start.39 = (bf16[128,512]{1,0:T(8,128)(2,1)S(1)}, bf16[128,512]{1,0:T(8,128)(2,1)S(1)}, u32[]{:S(2)}, u32[]{:S(2)}) collective-permute-start(bf16[128,512]{1,0:T(8,128)(2,1)S(1)} %get-tuple-element.125), channel_id=1, source_target_pairs={{0,24},{4,28},{8,16},{12,20},{16,8},{20,12},{24,0},{28,4},{1,25},{... | collective-permute-start | bytes 393224 | tf_op jit(solution)/shard_map/ppermute | solution.py:151
  98.9 8.3 %collective-permute-start.36 = (bf16[1,128,512]{2,1,0:T(8,128)(2,1)S(1)}, bf16[1,128,512]{2,1,0:T(8,128)(2,1)S(1)}, u32[]{:S(2)}, u32[]{:S(2)}) collective-permute-start(bf16[1,128,512]{2,1,0:T(8,128)(2,1)S(1)} %pad_maximum_fusion.4), channel_id=1, source_target_pairs={{0,2},{1,3},{2,0},{3,1},{4,6},{5,7},{6,4},{7,5},{8,10},{9,11},{10,... | collective-permute-start | bytes 393224 | tf_op jit(solution)/shard_map/ppermute | solution.py:151
  99.5 7.7 %collective-permute-start.35 = (bf16[1,128,512]{2,1,0:T(8,128)(2,1)S(1)}, bf16[1,128,512]{2,1,0:T(8,128)(2,1)S(1)}, u32[]{:S(2)}, u32[]{:S(2)}) collective-permute-start(bf16[1,128,512]{2,1,0:T(8,128)(2,1)S(1)} %pad_maximum_fusion.3), channel_id=1, source_target_pairs={{0,4},{4,0},{8,12},{12,8},{16,20},{20,16},{24,28},{28,24},{1,5},{5... | collective-permute-start | bytes 393224 | tf_op jit(solution)/shard_map/ppermute | solution.py:151
  (18 other events, 200.5 us)

commit v9 on v8

--- a/solution.py
+++ b/solution.py
@@ -15,6 +15,8 @@
 TOK_DEV = 128
 REQS_DEV = 9
 POOL = 48
+SHORT_PG = 2
+SHORT_LIST = (REQS_DEV - 1) * SHORT_PG
 
 
 NORM_EPS = 1e-06
@@ -152,28 +154,28 @@
 
 
 def layout_kernel(
-    length_ref, table_ref, frequency_ref, cosine_ref, sine_ref, owner_ref, list_ref, count_ref, live_ref
+    length_ref, table_ref, frequency_ref, cosine_ref, sine_ref, owner_ref, list_ref, owners
 ):
     tokens, head_dim = cosine_ref.shape
-    slots = list_ref.shape[0]
-    owners = live_ref
-    for entry in range(slots):
+    for entry in range(POOL):
         list_ref[entry] = 0
         owners[0, entry] = -1
         owners[1, entry] = 0
+    prefill_long = length_ref[0] > SHORT_PG * PAGE
     count = jnp.int32(0)
     for request in range(1, REQS_DEV):
 
         def name_page(entry, count):
-            list_ref[count] = table_ref[request, entry]
-            owners[0, count] = request
-            owners[1, count] = jnp.minimum(length_ref[request] - entry * PAGE, PAGE)
+            page = table_ref[request, entry]
+            place = jnp.where(prefill_long, count, page)
+            list_ref[place] = page
+            owners[0, place] = request
+            owners[1, place] = jnp.minimum(length_ref[request] - entry * PAGE, PAGE)
             return count + 1
 
         count = lax.fori_loop(0, (length_ref[request] + PAGE - 1) // PAGE, name_page, count)
-    count_ref[0] = count
     slot = lax.broadcasted_iota(jnp.int32, (1, PAGE), 1)
-    for entry in range(slots):
+    for entry in range(POOL):
         owner_ref[:, entry * PAGE : (entry + 1) * PAGE] = jnp.where(
             slot < owners[1, entry], owners[0, entry], -1
         )
@@ -189,14 +191,14 @@
 
 
 def attention_kernel(*refs):
-    pieces, hbm_refs, (keep_out, far_out, core_out) = refs[:4], refs[4:20], refs[20:23]
-    local_refs = refs[23:39]
-    (length_ref, table_ref, list_ref, count_ref, gain_ref, q_gain_ref, k_gain_ref) = local_refs[:7]
-    (cosine_ref, sine_ref, owner_ref, q_ref, k_ref, v_ref, key_ref, value_ref, o_ref) = local_refs[7:]
+    pieces, hbm_refs, (keep_out, far_out, core_out) = refs[:4], refs[4:19], refs[19:22]
+    local_refs = refs[22:37]
+    (length_ref, table_ref, list_ref, gain_ref, q_gain_ref, k_gain_ref) = local_refs[:6]
+    (cosine_ref, sine_ref, owner_ref, q_ref, k_ref, v_ref, key_ref, value_ref, o_ref) = local_refs[6:]
     (
-        x_ref, query_ref, own_scores, top_ref, scores_ref, mix_ref, mixed_ref, part_ref, slots_ref,
-        decode_top, decode_mix, sems,
-    ) = refs[39:]
+        x_ref, query_ref, own_scores, scores_ref, mix_ref, mixed_ref, part_ref, slots_ref, decoded_ref,
+        sems,
+    ) = refs[37:]
     tokens, head_dim = x_ref.shape[0], k_gain_ref.shape[1]
     copies = [
         pltpu.make_async_copy(source, target, sems.at[i])
@@ -211,7 +213,7 @@
         width = piece.shape[1]
         start = pl.multiple_of((tp_index ^ step) * width, width)
         x_ref[:, pl.ds(start, width)] = piece[...]
-    for copy in copies[:10]:
+    for copy in copies[:9]:
         copy.wait()
     token = lax.broadcasted_iota(jnp.int32, (tokens, head_dim), 0)
     lane = lax.broadcasted_iota(jnp.int32, (tokens, head_dim), 1)
@@ -225,7 +227,7 @@
 
     normed = rms_scale(x_ref[...].astype(jnp.float32), gain_ref[...]).astype(jnp.bfloat16)
     contract = (((1,), (1,)), ((), ()))
-    for copy in copies[10:13]:
+    for copy in copies[9:12]:
         copy.wait()
     key_lin = jnp.dot(normed, k_ref[...], preferred_element_type=jnp.float32)
     values_new = jnp.dot(normed, v_ref[...], preferred_element_type=jnp.float32).astype(jnp.bfloat16)
@@ -243,12 +245,11 @@
         scores = lax.dot_general(rounded, keys_new, contract, preferred_element_type=jnp.float32)
         scores = jnp.where(own_mask, scores, -1e30)
         own_scores[span, :] = scores
-        top_ref[span, :] = scores
         decode_query.append(query[PRE:])
         decode_own.append(scores[PRE:])
     decode_query = jnp.concatenate(decode_query, axis=0).astype(jnp.bfloat16)
     decode_own = jnp.concatenate(decode_own, axis=0)
-    for copy in copies[13:15]:
+    for copy in copies[12:14]:
         copy.wait()
 
     def raised(top, scores):
@@ -256,79 +257,85 @@
             top = jnp.maximum(top, scores[:, start : start + head_dim])
         return top
 
+    def weigh(own, score_steps, value_steps, scores_ref):
+        top = own
+        for step, score_step in enumerate(score_steps):
+            scores = score_step()
+            scores_ref[step, :, : scores.shape[1]] = scores
+            top = raised(top, scores)
+        top = jnp.max(top, axis=1, keepdims=True)
+        mix = jnp.dot(
+            jnp.exp2(own - top).astype(jnp.bfloat16), values_new, preferred_element_type=jnp.float32
+        )
+        for step, value_step in enumerate(value_steps):
+            values = value_step()
+            weights = jnp.exp2(scores_ref[step, :, : values.shape[0]] - top).astype(jnp.bfloat16)
+            mix = mix + jnp.dot(weights, with_ones(values), preferred_element_type=jnp.float32)
+        return mix
+
+    def taken(ref, names):
+        return jnp.concatenate([ref[name] for name in names], axis=0)
+
+    def against(queries, keys):
+        return lax.dot_general(queries, keys, contract, preferred_element_type=jnp.float32)
+
+    def prefill(names, live):
+        def score(pages):
+            scores = against(query_ref[...], taken(key_ref, pages))
+            return scores if live is None else jnp.where(live, scores, -1e30)
+
+        mix_ref[...] = weigh(
+            own_scores[...],
+            [functools.partial(score, pages) for pages in names],
+            [functools.partial(taken, value_ref, pages) for pages in names],
+            scores_ref,
+        )
+
+    def decode(steps, pages_of):
+        row_request = 1 + lax.broadcasted_iota(jnp.int32, (heads * decodes, 1), 0) % decodes
+        width = slots_ref.shape[2]
+
+        def score(step):
+            scores = against(decode_query, pages_of(key_ref, step))
+            owner = owner_ref[:, step * width : (step + 1) * width]
+            return jnp.where(owner == row_request, scores, -1e30)
+
+        mix = weigh(
+            decode_own,
+            [functools.partial(score, step) for step in range(steps)],
+            [functools.partial(pages_of, value_ref, step) for step in range(steps)],
+            slots_ref,
+        )
+        decoded_ref[...] = mix[:, :head_dim] / mix[:, head_dim:]
+
+    length = length_ref[0]
+    listed = slots_ref.shape[2] // PAGE
     pages = scores_ref.shape[2] // PAGE
-    width = pages * PAGE
-    length = length_ref[0]
-    steps = (length + width - 1) // width
-    column = lax.broadcasted_iota(jnp.int32, (1, width), 1)
-
-    def own_pages(ref, step):
-        names = [table_ref[0, jnp.minimum(step * pages + i, MAXPG - 1)] for i in range(pages)]
-        return jnp.concatenate([ref[name] for name in names], axis=0)
-
-    def score(step, carry):
-        scores = lax.dot_general(
-            query_ref[...], own_pages(key_ref, step), contract, preferred_element_type=jnp.float32
+
+    @pl.when(length > SHORT_PG * PAGE)
+    def _():
+        names = [table_ref[0, entry] for entry in range(MAXPG)]
+        prefill([names[first : first + pages] for first in range(0, MAXPG, pages)], None)
+        decode(
+            SHORT_LIST // listed,
+            lambda ref, step: taken(ref, [list_ref[step * listed + i] for i in range(listed)]),
         )
-        scores = jnp.where(column + step * width < length, scores, -1e30)
-        scores_ref[step] = scores
-        top_ref[...] = raised(top_ref[...], scores)
-        return carry
-
-    lax.fori_loop(0, steps, score, 0)
-    listed = slots_ref.shape[2] // PAGE
-    decode_steps = (count_ref[0] + listed - 1) // listed
-    row_request = 1 + lax.broadcasted_iota(jnp.int32, (heads * decodes, 1), 0) % decodes
-    decode_top[...] = decode_own
-
-    def listed_pages(ref, step):
-        return jnp.concatenate([ref[list_ref[step * listed + i]] for i in range(listed)], axis=0)
-
-    def decode_score(step, carry):
-        scores = lax.dot_general(
-            decode_query, listed_pages(key_ref, step), contract, preferred_element_type=jnp.float32
+
+    @pl.when(length <= SHORT_PG * PAGE)
+    def _():
+        column = lax.broadcasted_iota(jnp.int32, (1, SHORT_PG * PAGE), 1)
+        prefill([[table_ref[0, entry] for entry in range(SHORT_PG)]], column < length)
+        decode(
+            POOL // listed,
+            lambda ref, step: ref[step * listed : (step + 1) * listed].reshape(-1, head_dim),
         )
-        start = pl.multiple_of(step * listed * PAGE, listed * PAGE)
-        scores = jnp.where(owner_ref[:, pl.ds(start, listed * PAGE)] == row_request, scores, -1e30)
-        slots_ref[step] = scores
-        decode_top[...] = raised(decode_top[...], scores)
-        return carry
-
-    lax.fori_loop(0, decode_steps, decode_score, 0)
-    top = jnp.max(decode_top[...], axis=1, keepdims=True)
-    decode_mix[...] = jnp.dot(
-        jnp.exp2(decode_own - top).astype(jnp.bfloat16), values_new, preferred_element_type=jnp.float32
-    )
-
-    def decode_mixed(step, carry):
-        weights = jnp.exp2(slots_ref[step] - top).astype(jnp.bfloat16)
-        decode_mix[...] += jnp.dot(
-            weights, with_ones(listed_pages(value_ref, step)), preferred_element_type=jnp.float32
-        )
-        return carry
-
-    lax.fori_loop(0, decode_steps, decode_mixed, 0)
-    decoded = decode_mix[:, :head_dim] / decode_mix[:, head_dim:]
-    top = jnp.max(top_ref[...], axis=1, keepdims=True)
-    top_ref[...] = jnp.broadcast_to(top, top_ref.shape)
-    mix_ref[...] = jnp.dot(
-        jnp.exp2(own_scores[...] - top).astype(jnp.bfloat16), values_new, preferred_element_type=jnp.float32
-    )
-
-    def mix(step, carry):
-        weights = jnp.exp2(scores_ref[step] - top_ref[:, :1]).astype(jnp.bfloat16)
-        mix_ref[...] += jnp.dot(
-            weights, with_ones(own_pages(value_ref, step)), preferred_element_type=jnp.float32
-        )
-        return carry
-
-    lax.fori_loop(0, steps, mix, 0)
+
     for head in range(heads):
         part = mix_ref[head * tokens : (head + 1) * tokens, :]
         columns = slice(head * head_dim, (head + 1) * head_dim)
         mixed_ref[:, columns] = part[:, :head_dim] / part[:, head_dim:]
-        mixed_ref[PRE:, columns] = decoded[head * decodes : (head + 1) * decodes]
-    copies[15].wait()
+        mixed_ref[PRE:, columns] = decoded_ref[head * decodes : (head + 1) * decodes]
+    copies[14].wait()
     part_ref[...] = jnp.dot(
         mixed_ref[...].astype(jnp.bfloat16), o_ref[...], preferred_element_type=jnp.float32
     )
@@ -355,26 +362,25 @@
     frequency = jnp.asarray(np.concatenate([half, half])[None, :], jnp.float32)
     params = pltpu.CompilerParams(vmem_limit_bytes=56 * 1024 * 1024)
     rope = jax.ShapeDtypeStruct((tokens, head_dim), jnp.float32)
-    cosine, sine, owner, page_list, page_count = pl.pallas_call(
+    cosine, sine, owner, page_list = pl.pallas_call(
         layout_kernel,
         out_shape=[
             rope,
             rope,
             jax.ShapeDtypeStruct((1, POOL * PAGE), jnp.int32),
             jax.ShapeDtypeStruct((POOL,), jnp.int32),
-            jax.ShapeDtypeStruct((1,), jnp.int32),
         ],
         in_specs=[SMEM, SMEM, VMEM],
-        out_specs=[VMEM, VMEM, VMEM, SMEM, SMEM],
+        out_specs=[VMEM, VMEM, VMEM, SMEM],
         scratch_shapes=[pltpu.SMEM((2, POOL), jnp.int32)],
         compiler_params=params,
         name="layout",
     )(cache_len, page_table, frequency)
-    far, cosine, sine, owner, page_list, page_count = ordered(
-        flip(hidden_in, "tp", 2), cosine, sine, owner, page_list, page_count
+    far, cosine, sine, owner, page_list = ordered(
+        flip(hidden_in, "tp", 2), cosine, sine, owner, page_list
     )
     pieces = (hidden_in, flip(hidden_in, "tp", 1), far, flip(far, "tp", 1))
-    scalars = (cache_len, page_table, page_list, page_count)
+    scalars = (cache_len, page_table, page_list)
     arrays = (
         norm_in_gain[None, :], q_gain[None, :], k_gain[None, :], cosine, sine, owner,
         q_weight, k_weight, v_weight, key_pages[0], value_pages[0], o_weight,
@@ -388,7 +394,7 @@
             jax.ShapeDtypeStruct(share, jnp.float32),
             jax.ShapeDtypeStruct((2, *share), jnp.bfloat16),
         ],
-        in_specs=[VMEM] * 4 + [pl.BlockSpec(memory_space=pltpu.HBM)] * 16,
+        in_specs=[VMEM] * 4 + [pl.BlockSpec(memory_space=pltpu.HBM)] * 15,
         out_specs=[VMEM] * 3,
         scratch_shapes=[pltpu.SMEM(array.shape, array.dtype) for array in scalars]
         + [pltpu.VMEM(array.shape, array.dtype) for array in arrays]
@@ -396,15 +402,13 @@
             pltpu.VMEM((tokens, width), jnp.bfloat16),
             pltpu.VMEM((rows, head_dim), jnp.bfloat16),
             pltpu.VMEM((rows, tokens), jnp.float32),
-            pltpu.VMEM((rows, head_dim), jnp.float32),
             pltpu.VMEM((MAXPG // score_pages, rows, score_pages * PAGE), jnp.float32),
             pltpu.VMEM((rows, 2 * head_dim), jnp.float32),
             pltpu.VMEM((tokens, q_weight.shape[1]), jnp.float32),
             pltpu.VMEM((tokens, width), jnp.float32),
             pltpu.VMEM((POOL // list_pages, decode_rows, list_pages * PAGE), jnp.float32),
             pltpu.VMEM((decode_rows, head_dim), jnp.float32),
-            pltpu.VMEM((decode_rows, 2 * head_dim), jnp.float32),
-            pltpu.SemaphoreType.DMA((16,)),
+            pltpu.SemaphoreType.DMA((15,)),
         ],
         compiler_params=params,
         name="attention",
@@ -412,13 +416,13 @@
 
 
 def pack_kernel(
-    own_ref, core_ref, far_ref, gain_ref, ids_ref, routes_ref,
+    own_ref, far_ref, gain_ref, ids_ref, routes_ref,
     rows_ref, residual_ref, spread_ref,
 ):
     tp_index = lax.axis_index("tp")
     share_rows, width = own_ref.shape
     mine = pl.ds(pl.multiple_of(tp_index * share_rows, share_rows), share_rows)
-    residual = own_ref[...] + core_ref[0].astype(jnp.float32) + far_ref[...].astype(jnp.float32)
+    residual = own_ref[...] + far_ref[...].astype(jnp.float32)
     residual_ref[...] = residual
     rows_ref[:, :width] = rms_scale(residual, gain_ref[...]).astype(jnp.bfloat16)
     expert = lax.broadcasted_iota(jnp.int32, (LANES, spread_ref.shape[0]), 0) % (LANES // 2)
@@ -569,18 +573,19 @@
     token_count, share_width = 4 * share_rows, width // 4
     core = flip(core, "tp", 1)
     far = flip((far + core[1].astype(jnp.float32)).astype(jnp.bfloat16), "tp", 2)
+    kept, far = ordered(kept + core[0].astype(jnp.float32), far)
     rows, residual = pl.pallas_call(
         pack_kernel,
         out_shape=[
             jax.ShapeDtypeStruct((share_rows, width + LANES), jnp.bfloat16),
             jax.ShapeDtypeStruct((share_rows, width), jnp.float32),
         ],
-        in_specs=[VMEM] * 6,
+        in_specs=[VMEM] * 5,
         out_specs=[VMEM] * 2,
         scratch_shapes=[pltpu.VMEM((token_count, LANES), jnp.float32)],
         compiler_params=pltpu.CompilerParams(vmem_limit_bytes=8 * 1024 * 1024),
         name="pack_rows",
-    )(kept, core, far, norm_post_gain[None, :], expert_ids.T, route_weights.T)
+    )(kept, far, norm_post_gain[None, :], expert_ids.T, route_weights.T)
     gate_up = [w.transpose(0, 2, 1).reshape(-1, width) for w in (gate_weight, up_weight)]
     weights = (*gate_up, down_weight.reshape(-1, width))
     line_0 = rows[None]

time: 108 us -> 107 us (level); the launches traced: 108 us -> 105 us
  Pallas kernels: 21 us -> 19 us
    pallas_call x1, Pallas kernels: 10.3 us -> 8.2 us  [attention_shares(): pl.pallas_call(attention_kernel, out_shape=[jax.ShapeDtypeStruct(share, j...]
where the time goes in v9:
time: 107 us; the launch traced here: 105 us
  waiting for transfers between devices  45.7 us (43%)
  starting transfers between devices  36.9 us (34%)
  Pallas kernels  19 us (18%)
  other arithmetic  2.24 us (2%)
    ppermute x40, waiting for transfers between devices, flip(): lax.ppermute(value, axis, [(i, i ^ bits) for i in range(lax.axis_size(axi...  45.7 us
    ppermute x40, starting transfers between devices, flip(): lax.ppermute(value, axis, [(i, i ^ bits) for i in range(lax.axis_size(axi...  36.9 us
    pallas_call x1, Pallas kernels, attention_shares(): pl.pallas_call(attention_kernel, out_shape=[jax.ShapeDtypeStruct(share, j...  8.2 us
    pallas_call x3, Pallas kernels, run_experts(): pl.pallas_call(functools.partial(experts_kernel, plan), out_shape=[jax.Sh...  7.45 us
    pallas_call x1, Pallas kernels, attention_shares(): pl.pallas_call(layout_kernel, out_shape=[rope, rope, jax.ShapeDtypeStruct...  2.39 us
  transfers between devices with their start and end apart: 40, of which 17 were waited for; matrix products, arithmetic and copies ran while one was open for 1% of the time, Pallas kernels for 9%

profile of v9, /device:TPU:0, one launch (start us, length us, event | category | flops | bytes accessed | tf_op | source)
XLA Modules:
  0.0 105.1 jit_solution(12399332780283065495)
XLA Ops:
  0.0 3.0 %collective-permute-start.1 = (bf16[128,512]{1,0:T(8,128)(2,1)}, bf16[128,512]{1,0:T(8,128)(2,1)S(1)}, u32[]{:S(2)}, u32[]{:S(2)}) collective-permute-start(bf16[128,512]{1,0:T(8,128)(2,1)} %refs_0_.1), channel_id=1, source_target_pairs={{0,2},{1,3},{2,0},{3,1},{4,6},{5,7},{6,4},{7,5},{8,10},{9,11},{10,... | collective-permute-start | bytes 393224 | tf_op jit(solution)/shard_map/ppermute | solution.py:153
  3.0 2.4 %layout.1 = (f32[128,128]{1,0:T(8,128)}, f32[128,128]{1,0:T(8,128)}, s32[1,6144]{1,0:T(1,128)}, s32[48]{0:T(128)}) custom-call(s32[9]{0:T(128)} %refs_4_.1, s32[9,32]{1,0:T(8,128)} %refs_5_.1, f32[1,128]{1,0:T(1,128)} %constant.2.clone.frequency_ref), custom_call_target="tpu_custom_call" | custom-call | tf_op jit(solution)/shard_map/layout/pallas_call | solution.py:365
  5.4 1.3 %collective-permute-done.1.refs_2_ = bf16[128,512]{1,0:T(8,128)(2,1)S(1)} collective-permute-done((bf16[128,512]{1,0:T(8,128)(2,1)}, bf16[128,512]{1,0:T(8,128)(2,1)S(1)}, u32[]{:S(2)}, u32[]{:S(2)}) %collective-permute-start.1) | collective-permute-done | bytes 131104 | tf_op jit(solution)/shard_map/ppermute | solution.py:153
  6.7 1.3 %collective-permute-done.2.refs_3_ = bf16[128,512]{1,0:T(8,128)(2,1)S(1)} collective-permute-done((bf16[128,512]{1,0:T(8,128)(2,1)S(1)}, bf16[128,512]{1,0:T(8,128)(2,1)S(1)}, u32[]{:S(2)}, u32[]{:S(2)}) %collective-permute-start.2) | collective-permute-done | bytes 131104 | tf_op jit(solution)/shard_map/ppermute | solution.py:153
  8.7 8.2 %attention.1 = (f32[32,2048]{1,0:T(8,128)}, f32[32,2048]{1,0:T(8,128)}, bf16[2,32,2048]{2,1,0:T(8,128)(2,1)}) custom-call(bf16[128,512]{1,0:T(8,128)(2,1)} %refs_0_.1, bf16[128,512]{1,0:T(8,128)(2,1)} %copy-done.7, bf16[128,512]{1,0:T(8,128)(2,1)} %copy-done.6, bf16[128,512]{1,0:T(8,128)(2,1)} %copy-done.8, s32[9]{0:T(128)} %refs_4_.1, s32[9,32]{1,0:T(8,128)} %refs_5_.1, ...), custom_call_target="tpu_custom_call" | custom-call | tf_op jit(solution)/shard_map/attention/pallas_call | solution.py:390
  17.1 1.6 %collective-permute-done.3 = bf16[2,32,2048]{2,1,0:T(8,128)(2,1)S(1)} collective-permute-done((bf16[2,32,2048]{2,1,0:T(8,128)(2,1)}, bf16[2,32,2048]{2,1,0:T(8,128)(2,1)S(1)}, u32[]{:S(2)}, u32[]{:S(2)}) %collective-permute-start.3) | collective-permute-done | bytes 262176 | tf_op jit(solution)/shard_map/ppermute | solution.py:153
  20.0 1.8 %collective-permute-start.4 = (bf16[32,2048]{1,0:T(8,128)(2,1)S(1)}, bf16[32,2048]{1,0:T(8,128)(2,1)S(1)}, u32[]{:S(2)}, u32[]{:S(2)}) collective-permute-start(bf16[32,2048]{1,0:T(8,128)(2,1)S(1)} %get-tuple-element.130), channel_id=1, source_target_pairs={{0,2},{1,3},{2,0},{3,1},{4,6},{5,7},{6,4},{7,5},{8,10},{9,11},{10,... | collective-permute-start | bytes 393224 | tf_op jit(solution)/shard_map/ppermute | solution.py:153
  21.8 3.8 %collective-permute-done.4.far_ref = bf16[32,2048]{1,0:T(8,128)(2,1)S(1)} collective-permute-done((bf16[32,2048]{1,0:T(8,128)(2,1)S(1)}, bf16[32,2048]{1,0:T(8,128)(2,1)S(1)}, u32[]{:S(2)}, u32[]{:S(2)}) %collective-permute-start.4) | collective-permute-done | bytes 131104 | tf_op jit(solution)/shard_map/ppermute | solution.py:153
  25.8 1.9 %collective-permute-start.6 = (bf16[32,2176]{1,0:T(8,128)(2,1)S(1)}, bf16[32,2176]{1,0:T(8,128)(2,1)S(1)}, u32[]{:S(2)}, u32[]{:S(2)}) collective-permute-start(bf16[32,2176]{1,0:T(8,128)(2,1)S(1)} %get-tuple-element.76), channel_id=1, source_target_pairs={{0,8},{4,12},{8,0},{12,4},{16,24},{20,28},{24,16},{28,20},{1,9},{5... | collective-permute-start | bytes 417800 | tf_op jit(solution)/shard_map/ppermute | solution.py:153
  27.6 2.6 %collective-permute-start.7 = (bf16[32,2176]{1,0:T(8,128)(2,1)S(1)}, bf16[32,2176]{1,0:T(8,128)(2,1)S(1)}, u32[]{:S(2)}, u32[]{:S(2)}) collective-permute-start(bf16[32,2176]{1,0:T(8,128)(2,1)S(1)} %get-tuple-element.76), channel_id=1, source_target_pairs={{0,16},{4,20},{8,24},{12,28},{16,0},{20,4},{24,8},{28,12},{1,17},{... | collective-permute-start | bytes 417800 | tf_op jit(solution)/shard_map/ppermute | solution.py:153
  30.2 1.7 %collective-permute-start.10 = (bf16[1,32,2176]{2,1,0:T(8,128)(2,1)S(1)}, bf16[1,32,2176]{2,1,0:T(8,128)(2,1)S(1)}, u32[]{:S(2)}, u32[]{:S(2)}) collective-permute-start(bf16[1,32,2176]{2,1,0:T(8,128)(2,1)S(1)} %bitcast.64), channel_id=1, source_target_pairs={{0,4},{4,0},{8,12},{12,8},{16,20},{20,16},{24,28},{28,24},{1,5},{5... | collective-permute-start | bytes 417800 | tf_op jit(solution)/shard_map/ppermute | solution.py:153
  32.0 1.5 %collective-permute-start.9 = (bf16[1,32,2176]{2,1,0:T(8,128)(2,1)S(1)}, bf16[1,32,2176]{2,1,0:T(8,128)(2,1)S(1)}, u32[]{:S(2)}, u32[]{:S(2)}) collective-permute-start(bf16[1,32,2176]{2,1,0:T(8,128)(2,1)S(1)} %bitcast.65), channel_id=1, source_target_pairs={{0,2},{1,3},{2,0},{3,1},{4,6},{5,7},{6,4},{7,5},{8,10},{9,11},{10,... | collective-permute-start | bytes 417800 | tf_op jit(solution)/shard_map/ppermute | solution.py:153
  33.5 7.2 %collective-permute-done.7 = bf16[32,2176]{1,0:T(8,128)(2,1)S(1)} collective-permute-done((bf16[32,2176]{1,0:T(8,128)(2,1)S(1)}, bf16[32,2176]{1,0:T(8,128)(2,1)S(1)}, u32[]{:S(2)}, u32[]{:S(2)}) %collective-permute-start.7) | collective-permute-done | bytes 139296 | tf_op jit(solution)/shard_map/ppermute | solution.py:153
  40.8 1.6 %collective-permute-start.13 = (bf16[3,32,2176]{2,1,0:T(8,128)(2,1)S(1)}, bf16[3,32,2176]{2,1,0:T(8,128)(2,1)S(1)}, u32[]{:S(2)}, u32[]{:S(2)}) collective-permute-start(bf16[3,32,2176]{2,1,0:T(8,128)(2,1)S(1)} %pad_maximum_fusion.refs_0_), channel_id=1, source_target_pairs={{0,2},{1,3},{2,0},{3,1},{4,6},{5,7},{6,4},{7,5},{8,10},{9,11},{10,... | collective-permute-start | bytes 1253384 | tf_op jit(solution)/shard_map/ppermute | solution.py:153
  42.4 1.5 %collective-permute-start.14 = (bf16[3,32,2176]{2,1,0:T(8,128)(2,1)S(1)}, bf16[3,32,2176]{2,1,0:T(8,128)(2,1)S(1)}, u32[]{:S(2)}, u32[]{:S(2)}) collective-permute-start(bf16[3,32,2176]{2,1,0:T(8,128)(2,1)S(1)} %pad_maximum_fusion.refs_0_), channel_id=1, source_target_pairs={{0,4},{4,0},{8,12},{12,8},{16,20},{20,16},{24,28},{28,24},{1,5},{5... | collective-permute-start | bytes 1253384 | tf_op jit(solution)/shard_map/ppermute | solution.py:153
  45.3 5.0 %collective-permute-done.11.refs_6_ = bf16[1,16,2176]{2,1,0:T(8,128)(2,1)S(1)} collective-permute-done((bf16[1,16,2176]{2,1,0:T(8,128)(2,1)S(1)}, bf16[1,16,2176]{2,1,0:T(8,128)(2,1)S(1)}, u32[]{:S(2)}, u32[]{:S(2)}) %collective-permute-start.11) | collective-permute-done | bytes 69664 | tf_op jit(solution)/shard_map/ppermute | solution.py:153
  50.4 1.5 %collective-permute-done.12.refs_7_ = bf16[1,16,2176]{2,1,0:T(8,128)(2,1)S(1)} collective-permute-done((bf16[1,16,2176]{2,1,0:T(8,128)(2,1)S(1)}, bf16[1,16,2176]{2,1,0:T(8,128)(2,1)S(1)}, u32[]{:S(2)}, u32[]{:S(2)}) %collective-permute-start.12) | collective-permute-done | bytes 69664 | tf_op jit(solution)/shard_map/ppermute | solution.py:153
  53.0 1.5 %collective-permute-start.21 = (bf16[3,16,2176]{2,1,0:T(8,128)(2,1)S(1)}, bf16[3,16,2176]{2,1,0:T(8,128)(2,1)S(1)}, u32[]{:S(2)}, u32[]{:S(2)}) collective-permute-start(bf16[3,16,2176]{2,1,0:T(8,128)(2,1)S(1)} %slice.120), channel_id=1, source_target_pairs={{0,4},{4,0},{8,12},{12,8},{16,20},{20,16},{24,28},{28,24},{1,5},{5... | collective-permute-start | bytes 626696 | tf_op jit(solution)/shard_map/ppermute | solution.py:153
  55.0 2.7 %experts.3 = (f32[1,2,3,128,512]{4,3,2,1,0:T(8,128)S(1)}, bf16[1,2,3,128,512]{4,3,2,1,0:T(8,128)(2,1)S(1)}) custom-call(bf16[3,32,2176]{2,1,0:T(8,128)(2,1)S(1)} %pad_maximum_fusion.refs_0_, bf16[3,32,2176]{2,1,0:T(8,128)(2,1)S(1)} %collective-permute-done.15.refs_1_, bf16[3,32,2176]{2,1,0:T(8,128)(2,1)S(1)} %collective-permute-done.13.refs_2_, ...), custom_call_target="tpu_custom_call" | custom-call | tf_op jit(solution)/shard_map/experts/pallas_call | solution.py:488
  57.8 1.9 %collective-permute-done.20.refs_2_ = bf16[3,16,2176]{2,1,0:T(8,128)(2,1)S(1)} collective-permute-done((bf16[3,16,2176]{2,1,0:T(8,128)(2,1)S(1)}, bf16[3,16,2176]{2,1,0:T(8,128)(2,1)S(1)}, u32[]{:S(2)}, u32[]{:S(2)}) %collective-permute-start.20) | collective-permute-done | bytes 208928 | tf_op jit(solution)/shard_map/ppermute | solution.py:153
  61.6 2.7 %experts.4 = (f32[1,2,3,128,512]{4,3,2,1,0:T(8,128)S(1)}, bf16[1,2,3,128,512]{4,3,2,1,0:T(8,128)(2,1)S(1)}) custom-call(bf16[3,32,2176]{2,1,0:T(8,128)(2,1)S(1)} %collective-permute-done.14.refs_0_, bf16[3,32,2176]{2,1,0:T(8,128)(2,1)S(1)} %collective-permute-done.19.refs_1_, bf16[3,16,2176]{2,1,0:T(8,128)(2,1)S(1)} %collective-permute-done.20.refs_2_, ...), custom_call_target="tpu_custom_call" | custom-call | tf_op jit(solution)/shard_map/experts/pallas_call | solution.py:488
  64.7 2.0 %experts.5 = (f32[2,2,1,128,512]{4,3,2,1,0:T(8,128)S(1)}, bf16[2,2,1,128,512]{4,3,2,1,0:T(8,128)(2,1)S(1)}) custom-call(bf16[1,32,2176]{2,1,0:T(8,128)(2,1)S(1)} %bitcast.67, bf16[1,32,2176]{2,1,0:T(8,128)(2,1)S(1)} %collective-permute-done.5.refs_1_, bf16[1,32,2176]{2,1,0:T(8,128)(2,1)S(1)} %collective-permute-done.9.refs_2_, ...), custom_call_target="tpu_custom_call" | custom-call | tf_op jit(solution)/shard_map/experts/pallas_call | solution.py:488
  67.6 1.6 %collective-permute-start.29 = (bf16[3,64,512]{2,1,0:T(8,128)(2,1)S(1)}, bf16[3,64,512]{2,1,0:T(8,128)(2,1)S(1)}, u32[]{:S(2)}, u32[]{:S(2)}) collective-permute-start(bf16[3,64,512]{2,1,0:T(8,128)(2,1)S(1)} %get-tuple-element.129), channel_id=1, source_target_pairs={{0,4},{4,0},{8,12},{12,8},{16,20},{20,16},{24,28},{28,24},{1,5},{5... | collective-permute-start | bytes 589832 | tf_op jit(solution)/shard_map/ppermute | solution.py:153
  69.1 1.5 %collective-permute-start.30 = (bf16[3,64,512]{2,1,0:T(8,128)(2,1)S(1)}, bf16[3,64,512]{2,1,0:T(8,128)(2,1)S(1)}, u32[]{:S(2)}, u32[]{:S(2)}) collective-permute-start(bf16[3,64,512]{2,1,0:T(8,128)(2,1)S(1)} %get-tuple-element.128), channel_id=1, source_target_pairs={{0,2},{1,3},{2,0},{3,1},{4,6},{5,7},{6,4},{7,5},{8,10},{9,11},{10,... | collective-permute-start | bytes 589832 | tf_op jit(solution)/shard_map/ppermute | solution.py:153
  70.7 4.1 %collective-permute-done.29 = bf16[3,64,512]{2,1,0:T(8,128)(2,1)S(1)} collective-permute-done((bf16[3,64,512]{2,1,0:T(8,128)(2,1)S(1)}, bf16[3,64,512]{2,1,0:T(8,128)(2,1)S(1)}, u32[]{:S(2)}, u32[]{:S(2)}) %collective-permute-start.29) | collective-permute-done | bytes 196640 | tf_op jit(solution)/shard_map/ppermute | solution.py:153
  76.2 1.6 %collective-permute-start.34 = (bf16[3,128,512]{2,1,0:T(8,128)(2,1)S(1)}, bf16[3,128,512]{2,1,0:T(8,128)(2,1)S(1)}, u32[]{:S(2)}, u32[]{:S(2)}) collective-permute-start(bf16[3,128,512]{2,1,0:T(8,128)(2,1)S(1)} %pad_maximum_fusion.2), channel_id=1, source_target_pairs={{0,2},{1,3},{2,0},{3,1},{4,6},{5,7},{6,4},{7,5},{8,10},{9,11},{10,... | collective-permute-start | bytes 1179656 | tf_op jit(solution)/shard_map/ppermute | solution.py:153
  78.7 1.6 %collective-permute-start.31 = (bf16[1,64,512]{2,1,0:T(8,128)(2,1)S(1)}, bf16[1,64,512]{2,1,0:T(8,128)(2,1)S(1)}, u32[]{:S(2)}, u32[]{:S(2)}) collective-permute-start(bf16[1,64,512]{2,1,0:T(8,128)(2,1)S(1)} %get-tuple-element.133), channel_id=1, source_target_pairs={{0,4},{4,0},{8,12},{12,8},{16,20},{20,16},{24,28},{28,24},{1,5},{5... | collective-permute-start | bytes 196616 | tf_op jit(solution)/shard_map/ppermute | solution.py:153
  80.8 8.5 %collective-permute-done.31 = bf16[1,64,512]{2,1,0:T(8,128)(2,1)S(1)} collective-permute-done((bf16[1,64,512]{2,1,0:T(8,128)(2,1)S(1)}, bf16[1,64,512]{2,1,0:T(8,128)(2,1)S(1)}, u32[]{:S(2)}, u32[]{:S(2)}) %collective-permute-start.31) | collective-permute-done | bytes 65568 | tf_op jit(solution)/shard_map/ppermute | solution.py:153
  89.5 3.6 %collective-permute-start.37 = (bf16[128,512]{1,0:T(8,128)(2,1)S(1)}, bf16[128,512]{1,0:T(8,128)(2,1)S(1)}, u32[]{:S(2)}, u32[]{:S(2)}) collective-permute-start(bf16[128,512]{1,0:T(8,128)(2,1)S(1)} %get-tuple-element.127), channel_id=1, source_target_pairs={{0,8},{4,12},{8,0},{12,4},{16,24},{20,28},{24,16},{28,20},{1,9},{5... | collective-permute-start | bytes 393224 | tf_op jit(solution)/shard_map/ppermute | solution.py:153
  93.1 1.4 %collective-permute-start.38 = (bf16[128,512]{1,0:T(8,128)(2,1)S(1)}, bf16[128,512]{1,0:T(8,128)(2,1)S(1)}, u32[]{:S(2)}, u32[]{:S(2)}) collective-permute-start(bf16[128,512]{1,0:T(8,128)(2,1)S(1)} %get-tuple-element.126), channel_id=1, source_target_pairs={{0,16},{4,20},{8,24},{12,28},{16,0},{20,4},{24,8},{28,12},{1,17},{... | collective-permute-start | bytes 393224 | tf_op jit(solution)/shard_map/ppermute | solution.py:153
  94.6 1.4 %collective-permute-start.39 = (bf16[128,512]{1,0:T(8,128)(2,1)S(1)}, bf16[128,512]{1,0:T(8,128)(2,1)S(1)}, u32[]{:S(2)}, u32[]{:S(2)}) collective-permute-start(bf16[128,512]{1,0:T(8,128)(2,1)S(1)} %get-tuple-element.125), channel_id=1, source_target_pairs={{0,24},{4,28},{8,16},{12,20},{16,8},{20,12},{24,0},{28,4},{1,25},{... | collective-permute-start | bytes 393224 | tf_op jit(solution)/shard_map/ppermute | solution.py:153
  97.3 7.0 %collective-permute-done.38.z2_ref = bf16[128,512]{1,0:T(8,128)(2,1)S(1)} collective-permute-done((bf16[128,512]{1,0:T(8,128)(2,1)S(1)}, bf16[128,512]{1,0:T(8,128)(2,1)S(1)}, u32[]{:S(2)}, u32[]{:S(2)}) %collective-permute-start.38) | collective-permute-done | bytes 131104 | tf_op jit(solution)/shard_map/ppermute | solution.py:153
  (98 shorter events, 13.9 us)
Async XLA Ops:
  0.0 6.7 %collective-permute-start.1 = (bf16[128,512]{1,0:T(8,128)(2,1)}, bf16[128,512]{1,0:T(8,128)(2,1)S(1)}, u32[]{:S(2)}, u32[]{:S(2)}) collective-permute-start(bf16[128,512]{1,0:T(8,128)(2,1)} %refs_0_.1), channel_id=1, source_target_pairs={{0,2},{1,3},{2,0},{3,1},{4,6},{5,7},{6,4},{7,5},{8,10},{9,11},{10,... | collective-permute-start | bytes 393224 | tf_op jit(solution)/shard_map/ppermute | solution.py:153
  3.0 3.7 %collective-permute-start = (bf16[128,512]{1,0:T(8,128)(2,1)}, bf16[128,512]{1,0:T(8,128)(2,1)S(1)}, u32[]{:S(2)}, u32[]{:S(2)}) collective-permute-start(bf16[128,512]{1,0:T(8,128)(2,1)} %refs_0_.1), channel_id=1, source_target_pairs={{0,1},{1,0},{2,3},{3,2},{4,5},{5,4},{6,7},{7,6},{8,9},{9,8},{10,11... | collective-permute-start | bytes 393224 | tf_op jit(solution)/shard_map/ppermute | solution.py:153
  20.0 5.6 %collective-permute-start.4 = (bf16[32,2048]{1,0:T(8,128)(2,1)S(1)}, bf16[32,2048]{1,0:T(8,128)(2,1)S(1)}, u32[]{:S(2)}, u32[]{:S(2)}) collective-permute-start(bf16[32,2048]{1,0:T(8,128)(2,1)S(1)} %get-tuple-element.130), channel_id=1, source_target_pairs={{0,2},{1,3},{2,0},{3,1},{4,6},{5,7},{6,4},{7,5},{8,10},{9,11},{10,... | collective-permute-start | bytes 393224 | tf_op jit(solution)/shard_map/ppermute | solution.py:153
  25.8 7.7 %collective-permute-start.6 = (bf16[32,2176]{1,0:T(8,128)(2,1)S(1)}, bf16[32,2176]{1,0:T(8,128)(2,1)S(1)}, u32[]{:S(2)}, u32[]{:S(2)}) collective-permute-start(bf16[32,2176]{1,0:T(8,128)(2,1)S(1)} %get-tuple-element.76), channel_id=1, source_target_pairs={{0,8},{4,12},{8,0},{12,4},{16,24},{20,28},{24,16},{28,20},{1,9},{5... | collective-permute-start | bytes 417800 | tf_op jit(solution)/shard_map/ppermute | solution.py:153
  27.6 13.0 %collective-permute-start.7 = (bf16[32,2176]{1,0:T(8,128)(2,1)S(1)}, bf16[32,2176]{1,0:T(8,128)(2,1)S(1)}, u32[]{:S(2)}, u32[]{:S(2)}) collective-permute-start(bf16[32,2176]{1,0:T(8,128)(2,1)S(1)} %get-tuple-element.76), channel_id=1, source_target_pairs={{0,16},{4,20},{8,24},{12,28},{16,0},{20,4},{24,8},{28,12},{1,17},{... | collective-permute-start | bytes 417800 | tf_op jit(solution)/shard_map/ppermute | solution.py:153
  30.2 10.4 %collective-permute-start.8 = (bf16[32,2176]{1,0:T(8,128)(2,1)S(1)}, bf16[32,2176]{1,0:T(8,128)(2,1)S(1)}, u32[]{:S(2)}, u32[]{:S(2)}) collective-permute-start(bf16[32,2176]{1,0:T(8,128)(2,1)S(1)} %get-tuple-element.76), channel_id=1, source_target_pairs={{0,24},{4,28},{8,16},{12,20},{16,8},{20,12},{24,0},{28,4},{1,25},{... | collective-permute-start | bytes 417800 | tf_op jit(solution)/shard_map/ppermute | solution.py:153
  30.2 10.5 %collective-permute-start.10 = (bf16[1,32,2176]{2,1,0:T(8,128)(2,1)S(1)}, bf16[1,32,2176]{2,1,0:T(8,128)(2,1)S(1)}, u32[]{:S(2)}, u32[]{:S(2)}) collective-permute-start(bf16[1,32,2176]{2,1,0:T(8,128)(2,1)S(1)} %bitcast.64), channel_id=1, source_target_pairs={{0,4},{4,0},{8,12},{12,8},{16,20},{20,16},{24,28},{28,24},{1,5},{5... | collective-permute-start | bytes 417800 | tf_op jit(solution)/shard_map/ppermute | solution.py:153
  32.0 8.8 %collective-permute-start.9 = (bf16[1,32,2176]{2,1,0:T(8,128)(2,1)S(1)}, bf16[1,32,2176]{2,1,0:T(8,128)(2,1)S(1)}, u32[]{:S(2)}, u32[]{:S(2)}) collective-permute-start(bf16[1,32,2176]{2,1,0:T(8,128)(2,1)S(1)} %bitcast.65), channel_id=1, source_target_pairs={{0,2},{1,3},{2,0},{3,1},{4,6},{5,7},{6,4},{7,5},{8,10},{9,11},{10,... | collective-permute-start | bytes 417800 | tf_op jit(solution)/shard_map/ppermute | solution.py:153
  40.8 11.1 %collective-permute-start.13 = (bf16[3,32,2176]{2,1,0:T(8,128)(2,1)S(1)}, bf16[3,32,2176]{2,1,0:T(8,128)(2,1)S(1)}, u32[]{:S(2)}, u32[]{:S(2)}) collective-permute-start(bf16[3,32,2176]{2,1,0:T(8,128)(2,1)S(1)} %pad_maximum_fusion.refs_0_), channel_id=1, source_target_pairs={{0,2},{1,3},{2,0},{3,1},{4,6},{5,7},{6,4},{7,5},{8,10},{9,11},{10,... | collective-permute-start | bytes 1253384 | tf_op jit(solution)/shard_map/ppermute | solution.py:153
  42.4 9.5 %collective-permute-start.14 = (bf16[3,32,2176]{2,1,0:T(8,128)(2,1)S(1)}, bf16[3,32,2176]{2,1,0:T(8,128)(2,1)S(1)}, u32[]{:S(2)}, u32[]{:S(2)}) collective-permute-start(bf16[3,32,2176]{2,1,0:T(8,128)(2,1)S(1)} %pad_maximum_fusion.refs_0_), channel_id=1, source_target_pairs={{0,4},{4,0},{8,12},{12,8},{16,20},{20,16},{24,28},{28,24},{1,5},{5... | collective-permute-start | bytes 1253384 | tf_op jit(solution)/shard_map/ppermute | solution.py:153
  43.9 6.5 %collective-permute-start.11 = (bf16[1,16,2176]{2,1,0:T(8,128)(2,1)S(1)}, bf16[1,16,2176]{2,1,0:T(8,128)(2,1)S(1)}, u32[]{:S(2)}, u32[]{:S(2)}) collective-permute-start(bf16[1,16,2176]{2,1,0:T(8,128)(2,1)S(1)} %slice.117), channel_id=1, source_target_pairs={{0,2},{1,3},{2,0},{3,1},{4,6},{5,7},{6,4},{7,5},{8,10},{9,11},{10,... | collective-permute-start | bytes 208904 | tf_op jit(solution)/shard_map/ppermute | solution.py:153
  44.4 7.5 %collective-permute-start.12 = (bf16[1,16,2176]{2,1,0:T(8,128)(2,1)S(1)}, bf16[1,16,2176]{2,1,0:T(8,128)(2,1)S(1)}, u32[]{:S(2)}, u32[]{:S(2)}) collective-permute-start(bf16[1,16,2176]{2,1,0:T(8,128)(2,1)S(1)} %slice.118), channel_id=1, source_target_pairs={{0,4},{4,0},{8,12},{12,8},{16,20},{20,16},{24,28},{28,24},{1,5},{5... | collective-permute-start | bytes 208904 | tf_op jit(solution)/shard_map/ppermute | solution.py:153
  45.2 9.3 %collective-permute-start.15 = (bf16[3,32,2176]{2,1,0:T(8,128)(2,1)S(1)}, bf16[3,32,2176]{2,1,0:T(8,128)(2,1)S(1)}, u32[]{:S(2)}, u32[]{:S(2)}) collective-permute-start(bf16[3,32,2176]{2,1,0:T(8,128)(2,1)S(1)} %pad_maximum_fusion.refs_0_), channel_id=1, source_target_pairs={{0,1},{1,0},{2,3},{3,2},{4,5},{5,4},{6,7},{7,6},{8,9},{9,8},{10,11... | collective-permute-start | bytes 1253384 | tf_op jit(solution)/shard_map/ppermute | solution.py:153
  51.9 8.0 %collective-permute-start.19 = (bf16[3,32,2176]{2,1,0:T(8,128)(2,1)S(1)}, bf16[3,32,2176]{2,1,0:T(8,128)(2,1)S(1)}, u32[]{:S(2)}, u32[]{:S(2)}) collective-permute-start(bf16[3,32,2176]{2,1,0:T(8,128)(2,1)S(1)} %collective-permute-done.14.refs_0_), channel_id=1, source_target_pairs={{0,1},{1,0},{2,3},{3,2},{4,5},{5,4},{6,7},{7,6},{8,9},{9,8},{10,11... | collective-permute-start | bytes 1253384 | tf_op jit(solution)/shard_map/ppermute | solution.py:153
  52.4 7.2 %collective-permute-start.20 = (bf16[3,16,2176]{2,1,0:T(8,128)(2,1)S(1)}, bf16[3,16,2176]{2,1,0:T(8,128)(2,1)S(1)}, u32[]{:S(2)}, u32[]{:S(2)}) collective-permute-start(bf16[3,16,2176]{2,1,0:T(8,128)(2,1)S(1)} %slice.119), channel_id=1, source_target_pairs={{0,2},{1,3},{2,0},{3,1},{4,6},{5,7},{6,4},{7,5},{8,10},{9,11},{10,... | collective-permute-start | bytes 626696 | tf_op jit(solution)/shard_map/ppermute | solution.py:153
  53.0 6.9 %collective-permute-start.21 = (bf16[3,16,2176]{2,1,0:T(8,128)(2,1)S(1)}, bf16[3,16,2176]{2,1,0:T(8,128)(2,1)S(1)}, u32[]{:S(2)}, u32[]{:S(2)}) collective-permute-start(bf16[3,16,2176]{2,1,0:T(8,128)(2,1)S(1)} %slice.120), channel_id=1, source_target_pairs={{0,4},{4,0},{8,12},{12,8},{16,20},{20,16},{24,28},{28,24},{1,5},{5... | collective-permute-start | bytes 626696 | tf_op jit(solution)/shard_map/ppermute | solution.py:153
  54.5 3.3 %collective-permute-start.18 = (bf16[1,32,2176]{2,1,0:T(8,128)(2,1)S(1)}, bf16[1,32,2176]{2,1,0:T(8,128)(2,1)S(1)}, u32[]{:S(2)}, u32[]{:S(2)}) collective-permute-start(bf16[1,32,2176]{2,1,0:T(8,128)(2,1)S(1)} %collective-permute-done.9.refs_2_), channel_id=1, source_target_pairs={{0,1},{1,0},{2,3},{3,2},{4,5},{5,4},{6,7},{7,6},{8,9},{9,8},{10,11... | collective-permute-start | bytes 417800 | tf_op jit(solution)/shard_map/ppermute | solution.py:153
  60.4 4.0 %collective-permute-start.24 = (bf16[1,16,2176]{2,1,0:T(8,128)(2,1)S(1)}, bf16[1,16,2176]{2,1,0:T(8,128)(2,1)S(1)}, u32[]{:S(2)}, u32[]{:S(2)}) collective-permute-start(bf16[1,16,2176]{2,1,0:T(8,128)(2,1)S(1)} %collective-permute-done.11.refs_6_), channel_id=1, source_target_pairs={{0,1},{1,0},{2,3},{3,2},{4,5},{5,4},{6,7},{7,6},{8,9},{9,8},{10,11... | collective-permute-start | bytes 208904 | tf_op jit(solution)/shard_map/ppermute | solution.py:153
  60.4 4.0 %collective-permute-start.25 = (bf16[1,16,2176]{2,1,0:T(8,128)(2,1)S(1)}, bf16[1,16,2176]{2,1,0:T(8,128)(2,1)S(1)}, u32[]{:S(2)}, u32[]{:S(2)}) collective-permute-start(bf16[1,16,2176]{2,1,0:T(8,128)(2,1)S(1)} %collective-permute-done.12.refs_7_), channel_id=1, source_target_pairs={{0,1},{1,0},{2,3},{3,2},{4,5},{5,4},{6,7},{7,6},{8,9},{9,8},{10,11... | collective-permute-start | bytes 208904 | tf_op jit(solution)/shard_map/ppermute | solution.py:153
  66.8 9.2 %collective-permute-start.27 = (bf16[1,2,3,128,512]{4,3,2,1,0:T(8,128)(2,1)S(1)}, bf16[1,2,3,128,512]{4,3,2,1,0:T(8,128)(2,1)S(1)}, u32[]{:S(2)}, u32[]{:S(2)}) collective-permute-start(bf16[1,2,3,128,512]{4,3,2,1,0:T(8,128)(2,1)S(1)} %get-tuple-element.104), channel_id=1, source_target_pairs={{0,1},{1,0},{2,3},{3,2},{4,5},{5,4},{6,7},{7,6},{8,9},{9,8},{10,11... | collective-permute-start | bytes 2359304 | tf_op jit(solution)/shard_map/ppermute | solution.py:153
  67.1 8.9 %collective-permute-start.28 = (bf16[2,2,1,128,512]{4,3,2,1,0:T(8,128)(2,1)S(1)}, bf16[2,2,1,128,512]{4,3,2,1,0:T(8,128)(2,1)S(1)}, u32[]{:S(2)}, u32[]{:S(2)}) collective-permute-start(bf16[2,2,1,128,512]{4,3,2,1,0:T(8,128)(2,1)S(1)} %get-tuple-element.106), channel_id=1, source_target_pairs={{0,1},{1,0},{2,3},{3,2},{4,5},{5,4},{6,7},{7,6},{8,9},{9,8},{10,11... | collective-permute-start | bytes 1572872 | tf_op jit(solution)/shard_map/ppermute | solution.py:153
  67.6 7.2 %collective-permute-start.29 = (bf16[3,64,512]{2,1,0:T(8,128)(2,1)S(1)}, bf16[3,64,512]{2,1,0:T(8,128)(2,1)S(1)}, u32[]{:S(2)}, u32[]{:S(2)}) collective-permute-start(bf16[3,64,512]{2,1,0:T(8,128)(2,1)S(1)} %get-tuple-element.129), channel_id=1, source_target_pairs={{0,4},{4,0},{8,12},{12,8},{16,20},{20,16},{24,28},{28,24},{1,5},{5... | collective-permute-start | bytes 589832 | tf_op jit(solution)/shard_map/ppermute | solution.py:153
  69.1 6.8 %collective-permute-start.30 = (bf16[3,64,512]{2,1,0:T(8,128)(2,1)S(1)}, bf16[3,64,512]{2,1,0:T(8,128)(2,1)S(1)}, u32[]{:S(2)}, u32[]{:S(2)}) collective-permute-start(bf16[3,64,512]{2,1,0:T(8,128)(2,1)S(1)} %get-tuple-element.128), channel_id=1, source_target_pairs={{0,2},{1,3},{2,0},{3,1},{4,6},{5,7},{6,4},{7,5},{8,10},{9,11},{10,... | collective-permute-start | bytes 589832 | tf_op jit(solution)/shard_map/ppermute | solution.py:153
  76.2 13.0 %collective-permute-start.34 = (bf16[3,128,512]{2,1,0:T(8,128)(2,1)S(1)}, bf16[3,128,512]{2,1,0:T(8,128)(2,1)S(1)}, u32[]{:S(2)}, u32[]{:S(2)}) collective-permute-start(bf16[3,128,512]{2,1,0:T(8,128)(2,1)S(1)} %pad_maximum_fusion.2), channel_id=1, source_target_pairs={{0,2},{1,3},{2,0},{3,1},{4,6},{5,7},{6,4},{7,5},{8,10},{9,11},{10,... | collective-permute-start | bytes 1179656 | tf_op jit(solution)/shard_map/ppermute | solution.py:153
  77.9 11.4 %collective-permute-start.33 = (bf16[3,128,512]{2,1,0:T(8,128)(2,1)S(1)}, bf16[3,128,512]{2,1,0:T(8,128)(2,1)S(1)}, u32[]{:S(2)}, u32[]{:S(2)}) collective-permute-start(bf16[3,128,512]{2,1,0:T(8,128)(2,1)S(1)} %pad_maximum_fusion.1), channel_id=1, source_target_pairs={{0,4},{4,0},{8,12},{12,8},{16,20},{20,16},{24,28},{28,24},{1,5},{5... | collective-permute-start | bytes 1179656 | tf_op jit(solution)/shard_map/ppermute | solution.py:153
  78.7 10.6 %collective-permute-start.31 = (bf16[1,64,512]{2,1,0:T(8,128)(2,1)S(1)}, bf16[1,64,512]{2,1,0:T(8,128)(2,1)S(1)}, u32[]{:S(2)}, u32[]{:S(2)}) collective-permute-start(bf16[1,64,512]{2,1,0:T(8,128)(2,1)S(1)} %get-tuple-element.133), channel_id=1, source_target_pairs={{0,4},{4,0},{8,12},{12,8},{16,20},{20,16},{24,28},{28,24},{1,5},{5... | collective-permute-start | bytes 196616 | tf_op jit(solution)/shard_map/ppermute | solution.py:153
  80.2 9.0 %collective-permute-start.32 = (bf16[1,64,512]{2,1,0:T(8,128)(2,1)S(1)}, bf16[1,64,512]{2,1,0:T(8,128)(2,1)S(1)}, u32[]{:S(2)}, u32[]{:S(2)}) collective-permute-start(bf16[1,64,512]{2,1,0:T(8,128)(2,1)S(1)} %get-tuple-element.132), channel_id=1, source_target_pairs={{0,2},{1,3},{2,0},{3,1},{4,6},{5,7},{6,4},{7,5},{8,10},{9,11},{10,... | collective-permute-start | bytes 196616 | tf_op jit(solution)/shard_map/ppermute | solution.py:153
  89.5 7.8 %collective-permute-start.37 = (bf16[128,512]{1,0:T(8,128)(2,1)S(1)}, bf16[128,512]{1,0:T(8,128)(2,1)S(1)}, u32[]{:S(2)}, u32[]{:S(2)}) collective-permute-start(bf16[128,512]{1,0:T(8,128)(2,1)S(1)} %get-tuple-element.127), channel_id=1, source_target_pairs={{0,8},{4,12},{8,0},{12,4},{16,24},{20,28},{24,16},{28,20},{1,9},{5... | collective-permute-start | bytes 393224 | tf_op jit(solution)/shard_map/ppermute | solution.py:153
  93.1 11.2 %collective-permute-start.38 = (bf16[128,512]{1,0:T(8,128)(2,1)S(1)}, bf16[128,512]{1,0:T(8,128)(2,1)S(1)}, u32[]{:S(2)}, u32[]{:S(2)}) collective-permute-start(bf16[128,512]{1,0:T(8,128)(2,1)S(1)} %get-tuple-element.126), channel_id=1, source_target_pairs={{0,16},{4,20},{8,24},{12,28},{16,0},{20,4},{24,8},{28,12},{1,17},{... | collective-permute-start | bytes 393224 | tf_op jit(solution)/shard_map/ppermute | solution.py:153
  94.6 9.7 %collective-permute-start.39 = (bf16[128,512]{1,0:T(8,128)(2,1)S(1)}, bf16[128,512]{1,0:T(8,128)(2,1)S(1)}, u32[]{:S(2)}, u32[]{:S(2)}) collective-permute-start(bf16[128,512]{1,0:T(8,128)(2,1)S(1)} %get-tuple-element.125), channel_id=1, source_target_pairs={{0,24},{4,28},{8,16},{12,20},{16,8},{20,12},{24,0},{28,4},{1,25},{... | collective-permute-start | bytes 393224 | tf_op jit(solution)/shard_map/ppermute | solution.py:153
  96.0 8.3 %collective-permute-start.36 = (bf16[1,128,512]{2,1,0:T(8,128)(2,1)S(1)}, bf16[1,128,512]{2,1,0:T(8,128)(2,1)S(1)}, u32[]{:S(2)}, u32[]{:S(2)}) collective-permute-start(bf16[1,128,512]{2,1,0:T(8,128)(2,1)S(1)} %pad_maximum_fusion.4), channel_id=1, source_target_pairs={{0,2},{1,3},{2,0},{3,1},{4,6},{5,7},{6,4},{7,5},{8,10},{9,11},{10,... | collective-permute-start | bytes 393224 | tf_op jit(solution)/shard_map/ppermute | solution.py:153
  96.6 7.7 %collective-permute-start.35 = (bf16[1,128,512]{2,1,0:T(8,128)(2,1)S(1)}, bf16[1,128,512]{2,1,0:T(8,128)(2,1)S(1)}, u32[]{:S(2)}, u32[]{:S(2)}) collective-permute-start(bf16[1,128,512]{2,1,0:T(8,128)(2,1)S(1)} %pad_maximum_fusion.3), channel_id=1, source_target_pairs={{0,4},{4,0},{8,12},{12,8},{16,20},{20,16},{24,28},{28,24},{1,5},{5... | collective-permute-start | bytes 393224 | tf_op jit(solution)/shard_map/ppermute | solution.py:153
  (17 other events, 189.0 us)

commit v10 on v9

--- a/solution.py
+++ b/solution.py
@@ -204,7 +204,7 @@
         pltpu.make_async_copy(source, target, sems.at[i])
         for i, (source, target) in enumerate(zip(hbm_refs, local_refs))
     ]
-    for copy in copies:
+    for copy in copies[:12]:
         copy.start()
     tp_index = lax.axis_index("tp")
     heads = q_ref.shape[1] // head_dim
@@ -229,6 +229,8 @@
     contract = (((1,), (1,)), ((), ()))
     for copy in copies[9:12]:
         copy.wait()
+    for copy in copies[12:]:
+        copy.start()
     key_lin = jnp.dot(normed, k_ref[...], preferred_element_type=jnp.float32)
     values_new = jnp.dot(normed, v_ref[...], preferred_element_type=jnp.float32).astype(jnp.bfloat16)
     query_lin = jnp.dot(normed, q_ref[...], preferred_element_type=jnp.float32)
@@ -502,11 +504,11 @@
     )(*pieces, *residual, *weights)
 
 
-def finish_kernel(own_ref, x_ref, y_ref, z1_ref, z2_ref, z3_ref, out_ref):
+def finish_kernel(own_ref, z1_ref, z2_ref, x_ref, y_ref, out_ref):
     total = own_ref[0]
     for extra_ref in (x_ref, y_ref):
         total = total + extra_ref[0].astype(jnp.float32)
-    for extra_ref in (z1_ref, z2_ref, z3_ref):
+    for extra_ref in (z1_ref, z2_ref):
         total = total + extra_ref[...].astype(jnp.float32)
     out_ref[...] = total.astype(jnp.bfloat16)
 
@@ -589,58 +591,59 @@
     gate_up = [w.transpose(0, 2, 1).reshape(-1, width) for w in (gate_weight, up_weight)]
     weights = (*gate_up, down_weight.reshape(-1, width))
     line_0 = rows[None]
-    levels = [flip(rows, "req", 2 * bits) for bits in (1, 2, 3)]
+    z_1, z_2 = flip(line_0, "req", 2), flip(line_0, "req", 4)
     y_0, x_0 = flip(line_0, "tp", 2), flip(line_0, "req", 1)
-    line_3, y_0, x_0 = ordered(jnp.stack(levels), y_0, x_0)
-    core_0, across_0, y_3, x_3 = ordered(
+    line_12, z_2, y_0, x_0 = ordered(jnp.concatenate([z_1, z_2]), z_2, y_0, x_0)
+    line_3, across_0, core_0, y_core_0 = ordered(
+        jnp.concatenate([line_12, flip(z_2, "req", 2)]),
+        across_parts(x_0, y_0),
         flip(line_0, "tp", 1),
-        across_parts(x_0, y_0),
-        flip(line_3, "tp", 2),
-        flip(line_3, "req", 1),
-    )
-    core_3, y_core_3, x_core_3 = other_core((line_3, y_3, x_3))
+        flip(y_0, "tp", 1),
+    )
+    y_3, x_3 = flip(line_3, "tp", 2), flip(line_3, "req", 1)
+    all_0 = run_experts(
+        near_pieces(0, line_0, core_0)
+        + far_pieces(0, (y_0,), (y_core_0,))
+        + near_pieces(1, x_0, flip(x_0, "tp", 1))
+        + far_pieces(1, across_0, other_core(across_0)),
+        weights,
+        token_count,
+        residual,
+    )
+    all_0, core_3, y_3, x_3 = ordered(all_0, flip(line_3, "tp", 1), y_3, x_3)
+    y_core_3, x_core_3 = other_core((y_3, x_3))
     near_3 = run_experts(
         near_pieces(0, line_3, core_3) + far_pieces(0, (y_3,), (y_core_3,)), weights, token_count
     )
-    near_3, x_core_0, y_core_0, x_core_3, across_3 = ordered(
-        near_3, flip(x_0, "tp", 1), flip(y_0, "tp", 1), x_core_3, across_parts(x_3, y_3)
-    )
+    near_3, x_core_3, across_3 = ordered(near_3, x_core_3, across_parts(x_3, y_3))
     side_3 = run_experts(
         near_pieces(0, x_3, x_core_3) + far_pieces(0, across_3, other_core(across_3)),
         weights,
         token_count,
     )
-    side_3, across_core_0 = ordered(side_3, other_core(across_0))
-    side_3 = with_core(side_3)
-    all_0 = run_experts(
-        near_pieces(0, line_0, core_0)
-        + far_pieces(0, (y_0,), (y_core_0,))
-        + near_pieces(1, x_0, x_core_0)
-        + far_pieces(1, across_0, across_core_0),
-        weights,
-        token_count,
-        residual,
-    )
     all_0, near_3, side_3 = ordered(all_0, near_3, side_3)
+    all_0, near_3, side_3 = ordered(all_0, near_3, with_core(side_3))
     near_3, all_0, relay_3 = ordered(
         with_core(near_3), with_core(all_0), relayed(joined(side_3, 0, 1))
     )
-    relay_0, sums_3 = ordered(
-        relayed(joined(all_0, 1, 1)),
-        neighbours(joined(side_3, 0, 0), joined(near_3, 0, 1), *relay_3),
-    )
+    sums_3 = ordered(*neighbours(joined(side_3, 0, 0), joined(near_3, 0, 1), *relay_3))
     sent = joined(near_3, 0, 0) + sums_3[0].astype(jnp.float32) + sums_3[1].astype(jnp.float32)
-    sent = sent.astype(jnp.bfloat16)
-    from_z = [flip(sent[bits - 1], "req", 2 * bits) for bits in (1, 2, 3)]
+    sent_3, relay_0 = ordered(
+        flip(sent[2].astype(jnp.bfloat16), "req", 2), relayed(joined(all_0, 1, 1))
+    )
+    sent_2, relay_0 = ordered(
+        (sent[1] + sent_3.astype(jnp.float32)).astype(jnp.bfloat16), relay_0
+    )
+    from_z = [flip(sent[0].astype(jnp.bfloat16), "req", 2), flip(sent_2, "req", 4)]
     sums_0 = neighbours(joined(all_0, 1, 0), joined(all_0, 0, 1), *relay_0)
     return pl.pallas_call(
         finish_kernel,
         out_shape=jax.ShapeDtypeStruct((token_count, share_width), jnp.bfloat16),
-        in_specs=[VMEM] * 6,
+        in_specs=[VMEM] * 5,
         out_specs=VMEM,
         compiler_params=pltpu.CompilerParams(vmem_limit_bytes=8 * 1024 * 1024),
         name="finish",
-    )(joined(all_0, 0, 0), *sums_0, *from_z)
+    )(joined(all_0, 0, 0), *from_z, *sums_0)
 
 
 def moe_routed(

time: 107 us -> 109 us (1.019); the launches traced: 105 us -> 109 us
  waiting for transfers between devices: 45.7 us -> 49.5 us
    ppermute x40, waiting for transfers between devices: 45.7 us -> 49.5 us  [flip(): lax.ppermute(value, axis, [(i, i ^ bits) for i in range(lax.axis_size(axi...]
  transfers between devices with their start and end apart: 40 -> 40, of which waited for: 17 -> 26; matrix products, arithmetic and copies ran while one was open for 1% -> 1% of each run, Pallas kernels for 9% -> 6%
where the time goes in v10:
time: 109 us
  waiting for transfers between devices  49.5 us (45%)
  starting transfers between devices  36.5 us (33%)
  Pallas kernels  19.8 us (18%)
  other arithmetic  2.27 us (2%)
    ppermute x40, waiting for transfers between devices, flip(): lax.ppermute(value, axis, [(i, i ^ bits) for i in range(lax.axis_size(axi...  49.5 us
    ppermute x40, starting transfers between devices, flip(): lax.ppermute(value, axis, [(i, i ^ bits) for i in range(lax.axis_size(axi...  36.5 us
    pallas_call x1, Pallas kernels, attention_shares(): pl.pallas_call(attention_kernel, out_shape=[jax.ShapeDtypeStruct(share, j...  9.08 us
    pallas_call x3, Pallas kernels, run_experts(): pl.pallas_call(functools.partial(experts_kernel, plan), out_shape=[jax.Sh...  7.44 us
    pallas_call x1, Pallas kernels, attention_shares(): pl.pallas_call(layout_kernel, out_shape=[rope, rope, jax.ShapeDtypeStruct...  2.37 us
  transfers between devices with their start and end apart: 40, of which 26 were waited for; matrix products, arithmetic and copies ran while one was open for 1% of the time, Pallas kernels for 6%

profile of v10, /device:TPU:0, one launch (start us, length us, event | category | flops | bytes accessed | tf_op | source)
XLA Modules:
  0.0 109.3 jit_solution(6049902288897453957)
XLA Ops:
  0.0 3.0 %collective-permute-start.1 = (bf16[128,512]{1,0:T(8,128)(2,1)}, bf16[128,512]{1,0:T(8,128)(2,1)S(1)}, u32[]{:S(2)}, u32[]{:S(2)}) collective-permute-start(bf16[128,512]{1,0:T(8,128)(2,1)} %refs_0_.1), channel_id=1, source_target_pairs={{0,2},{1,3},{2,0},{3,1},{4,6},{5,7},{6,4},{7,5},{8,10},{9,11},{10,... | collective-permute-start | bytes 393224 | tf_op jit(solution)/shard_map/ppermute | solution.py:153
  3.0 2.4 %layout.1 = (f32[128,128]{1,0:T(8,128)}, f32[128,128]{1,0:T(8,128)}, s32[1,6144]{1,0:T(1,128)}, s32[48]{0:T(128)}) custom-call(s32[9]{0:T(128)} %refs_4_.1, s32[9,32]{1,0:T(8,128)} %refs_5_.1, f32[1,128]{1,0:T(1,128)} %constant.2.clone.frequency_ref), custom_call_target="tpu_custom_call" | custom-call | tf_op jit(solution)/shard_map/layout/pallas_call | solution.py:367
  5.3 1.3 %collective-permute-done.1.refs_2_ = bf16[128,512]{1,0:T(8,128)(2,1)S(1)} collective-permute-done((bf16[128,512]{1,0:T(8,128)(2,1)}, bf16[128,512]{1,0:T(8,128)(2,1)S(1)}, u32[]{:S(2)}, u32[]{:S(2)}) %collective-permute-start.1) | collective-permute-done | bytes 131104 | tf_op jit(solution)/shard_map/ppermute | solution.py:153
  6.7 1.3 %collective-permute-done.2.refs_3_ = bf16[128,512]{1,0:T(8,128)(2,1)S(1)} collective-permute-done((bf16[128,512]{1,0:T(8,128)(2,1)S(1)}, bf16[128,512]{1,0:T(8,128)(2,1)S(1)}, u32[]{:S(2)}, u32[]{:S(2)}) %collective-permute-start.2) | collective-permute-done | bytes 131104 | tf_op jit(solution)/shard_map/ppermute | solution.py:153
  8.7 9.1 %attention.1 = (f32[32,2048]{1,0:T(8,128)}, f32[32,2048]{1,0:T(8,128)}, bf16[2,32,2048]{2,1,0:T(8,128)(2,1)}) custom-call(bf16[128,512]{1,0:T(8,128)(2,1)} %refs_0_.1, bf16[128,512]{1,0:T(8,128)(2,1)} %copy-done.7, bf16[128,512]{1,0:T(8,128)(2,1)} %copy-done.6, bf16[128,512]{1,0:T(8,128)(2,1)} %copy-done.8, s32[9]{0:T(128)} %refs_4_.1, s32[9,32]{1,0:T(8,128)} %refs_5_.1, ...), custom_call_target="tpu_custom_call" | custom-call | tf_op jit(solution)/shard_map/attention/pallas_call | solution.py:392
  18.0 1.6 %collective-permute-done.3 = bf16[2,32,2048]{2,1,0:T(8,128)(2,1)S(1)} collective-permute-done((bf16[2,32,2048]{2,1,0:T(8,128)(2,1)}, bf16[2,32,2048]{2,1,0:T(8,128)(2,1)S(1)}, u32[]{:S(2)}, u32[]{:S(2)}) %collective-permute-start.3) | collective-permute-done | bytes 262176 | tf_op jit(solution)/shard_map/ppermute | solution.py:153
  20.8 1.8 %collective-permute-start.4 = (bf16[32,2048]{1,0:T(8,128)(2,1)S(1)}, bf16[32,2048]{1,0:T(8,128)(2,1)S(1)}, u32[]{:S(2)}, u32[]{:S(2)}) collective-permute-start(bf16[32,2048]{1,0:T(8,128)(2,1)S(1)} %get-tuple-element.151), channel_id=1, source_target_pairs={{0,2},{1,3},{2,0},{3,1},{4,6},{5,7},{6,4},{7,5},{8,10},{9,11},{10,... | collective-permute-start | bytes 393224 | tf_op jit(solution)/shard_map/ppermute | solution.py:153
  22.6 3.8 %collective-permute-done.4.far_ref = bf16[32,2048]{1,0:T(8,128)(2,1)S(1)} collective-permute-done((bf16[32,2048]{1,0:T(8,128)(2,1)S(1)}, bf16[32,2048]{1,0:T(8,128)(2,1)S(1)}, u32[]{:S(2)}, u32[]{:S(2)}) %collective-permute-start.4) | collective-permute-done | bytes 131104 | tf_op jit(solution)/shard_map/ppermute | solution.py:153
  26.6 5.2 %collective-permute-start.6 = (bf16[1,32,2176]{2,1,0:T(8,128)(2,1)S(1)}, bf16[1,32,2176]{2,1,0:T(8,128)(2,1)S(1)}, u32[]{:S(2)}, u32[]{:S(2)}) collective-permute-start(bf16[1,32,2176]{2,1,0:T(8,128)(2,1)S(1)} %bitcast.64), channel_id=1, source_target_pairs={{0,16},{4,20},{8,24},{12,28},{16,0},{20,4},{24,8},{28,12},{1,17},{... | collective-permute-start | bytes 417800 | tf_op jit(solution)/shard_map/ppermute | solution.py:153
  32.6 1.5 %collective-permute-start.7 = (bf16[1,32,2176]{2,1,0:T(8,128)(2,1)S(1)}, bf16[1,32,2176]{2,1,0:T(8,128)(2,1)S(1)}, u32[]{:S(2)}, u32[]{:S(2)}) collective-permute-start(bf16[1,32,2176]{2,1,0:T(8,128)(2,1)S(1)} %bitcast.67), channel_id=1, source_target_pairs={{0,2},{1,3},{2,0},{3,1},{4,6},{5,7},{6,4},{7,5},{8,10},{9,11},{10,... | collective-permute-start | bytes 417800 | tf_op jit(solution)/shard_map/ppermute | solution.py:153
  34.1 2.7 %collective-permute-done.6 = bf16[1,32,2176]{2,1,0:T(8,128)(2,1)S(1)} collective-permute-done((bf16[1,32,2176]{2,1,0:T(8,128)(2,1)S(1)}, bf16[1,32,2176]{2,1,0:T(8,128)(2,1)S(1)}, u32[]{:S(2)}, u32[]{:S(2)}) %collective-permute-start.6) | collective-permute-done | bytes 139296 | tf_op jit(solution)/shard_map/ppermute | solution.py:153
  36.8 2.3 %collective-permute-done.5 = bf16[1,32,2176]{2,1,0:T(8,128)(2,1)S(1)} collective-permute-done((bf16[1,32,2176]{2,1,0:T(8,128)(2,1)S(1)}, bf16[1,32,2176]{2,1,0:T(8,128)(2,1)S(1)}, u32[]{:S(2)}, u32[]{:S(2)}) %collective-permute-start.5) | collective-permute-done | bytes 139296 | tf_op jit(solution)/shard_map/ppermute | solution.py:153
  41.4 1.5 %collective-permute-start.10 = (bf16[1,16,2176]{2,1,0:T(8,128)(2,1)S(1)}, bf16[1,16,2176]{2,1,0:T(8,128)(2,1)S(1)}, u32[]{:S(2)}, u32[]{:S(2)}) collective-permute-start(bf16[1,16,2176]{2,1,0:T(8,128)(2,1)S(1)} %slice.119), channel_id=1, source_target_pairs={{0,2},{1,3},{2,0},{3,1},{4,6},{5,7},{6,4},{7,5},{8,10},{9,11},{10,... | collective-permute-start | bytes 208904 | tf_op jit(solution)/shard_map/ppermute | solution.py:153
  43.0 1.4 %collective-permute-done.9 = bf16[1,32,2176]{2,1,0:T(8,128)(2,1)S(1)} collective-permute-done((bf16[1,32,2176]{2,1,0:T(8,128)(2,1)S(1)}, bf16[1,32,2176]{2,1,0:T(8,128)(2,1)S(1)}, u32[]{:S(2)}, u32[]{:S(2)}) %collective-permute-start.9) | collective-permute-done | bytes 139296 | tf_op jit(solution)/shard_map/ppermute | solution.py:153
  46.7 1.5 %collective-permute-start.18 = (bf16[3,32,2176]{2,1,0:T(8,128)(2,1)S(1)}, bf16[3,32,2176]{2,1,0:T(8,128)(2,1)S(1)}, u32[]{:S(2)}, u32[]{:S(2)}) collective-permute-start(bf16[3,32,2176]{2,1,0:T(8,128)(2,1)S(1)} %pad_maximum_fusion.refs_0_), channel_id=1, source_target_pairs={{0,2},{1,3},{2,0},{3,1},{4,6},{5,7},{6,4},{7,5},{8,10},{9,11},{10,... | collective-permute-start | bytes 1253384 | tf_op jit(solution)/shard_map/ppermute | solution.py:153
  48.8 1.4 %collective-permute-done.14.refs_5_ = bf16[1,32,2176]{2,1,0:T(8,128)(2,1)S(1)} collective-permute-done((bf16[1,32,2176]{2,1,0:T(8,128)(2,1)S(1)}, bf16[1,32,2176]{2,1,0:T(8,128)(2,1)S(1)}, u32[]{:S(2)}, u32[]{:S(2)}) %collective-permute-start.14) | collective-permute-done | bytes 139296 | tf_op jit(solution)/shard_map/ppermute | solution.py:153
  51.5 2.0 %experts.3 = (f32[2,2,1,128,512]{4,3,2,1,0:T(8,128)S(1)}, bf16[2,2,1,128,512]{4,3,2,1,0:T(8,128)(2,1)S(1)}) custom-call(bf16[1,32,2176]{2,1,0:T(8,128)(2,1)S(1)} %bitcast.69, bf16[1,32,2176]{2,1,0:T(8,128)(2,1)S(1)} %collective-permute-done.12.refs_1_, bf16[1,32,2176]{2,1,0:T(8,128)(2,1)S(1)} %collective-permute-done.7.refs_2_, ...), custom_call_target="tpu_custom_call" | custom-call | tf_op jit(solution)/shard_map/experts/pallas_call | solution.py:490
  53.5 2.8 %collective-permute-done.19.refs_0_ = bf16[3,32,2176]{2,1,0:T(8,128)(2,1)S(1)} collective-permute-done((bf16[3,32,2176]{2,1,0:T(8,128)(2,1)S(1)}, bf16[3,32,2176]{2,1,0:T(8,128)(2,1)S(1)}, u32[]{:S(2)}, u32[]{:S(2)}) %collective-permute-start.19) | collective-permute-done | bytes 417824 | tf_op jit(solution)/shard_map/ppermute | solution.py:153
  57.5 1.6 %collective-permute-start.22 = (bf16[3,16,2176]{2,1,0:T(8,128)(2,1)S(1)}, bf16[3,16,2176]{2,1,0:T(8,128)(2,1)S(1)}, u32[]{:S(2)}, u32[]{:S(2)}) collective-permute-start(bf16[3,16,2176]{2,1,0:T(8,128)(2,1)S(1)} %slice.121), channel_id=1, source_target_pairs={{0,2},{1,3},{2,0},{3,1},{4,6},{5,7},{6,4},{7,5},{8,10},{9,11},{10,... | collective-permute-start | bytes 626696 | tf_op jit(solution)/shard_map/ppermute | solution.py:153
  60.2 2.7 %experts.4 = (f32[1,2,3,128,512]{4,3,2,1,0:T(8,128)S(1)}, bf16[1,2,3,128,512]{4,3,2,1,0:T(8,128)(2,1)S(1)}) custom-call(bf16[3,32,2176]{2,1,0:T(8,128)(2,1)S(1)} %pad_maximum_fusion.refs_0_, bf16[3,32,2176]{2,1,0:T(8,128)(2,1)S(1)} %collective-permute-done.17.refs_1_, bf16[3,32,2176]{2,1,0:T(8,128)(2,1)S(1)} %collective-permute-done.18.refs_2_, ...), custom_call_target="tpu_custom_call" | custom-call | tf_op jit(solution)/shard_map/experts/pallas_call | solution.py:490
  62.9 1.8 %collective-permute-done.22.refs_2_ = bf16[3,16,2176]{2,1,0:T(8,128)(2,1)S(1)} collective-permute-done((bf16[3,16,2176]{2,1,0:T(8,128)(2,1)S(1)}, bf16[3,16,2176]{2,1,0:T(8,128)(2,1)S(1)}, u32[]{:S(2)}, u32[]{:S(2)}) %collective-permute-start.22) | collective-permute-done | bytes 208928 | tf_op jit(solution)/shard_map/ppermute | solution.py:153
  67.7 2.7 %experts.5 = (f32[1,2,3,128,512]{4,3,2,1,0:T(8,128)S(1)}, bf16[1,2,3,128,512]{4,3,2,1,0:T(8,128)(2,1)S(1)}) custom-call(bf16[3,32,2176]{2,1,0:T(8,128)(2,1)S(1)} %collective-permute-done.19.refs_0_, bf16[3,32,2176]{2,1,0:T(8,128)(2,1)S(1)} %collective-permute-done.21.refs_1_, bf16[3,16,2176]{2,1,0:T(8,128)(2,1)S(1)} %collective-permute-done.22.refs_2_, ...), custom_call_target="tpu_custom_call" | custom-call | tf_op jit(solution)/shard_map/experts/pallas_call | solution.py:490
  70.7 2.1 %collective-permute-done.26 = bf16[1,2,3,128,512]{4,3,2,1,0:T(8,128)(2,1)S(1)} collective-permute-done((bf16[1,2,3,128,512]{4,3,2,1,0:T(8,128)(2,1)S(1)}, bf16[1,2,3,128,512]{4,3,2,1,0:T(8,128)(2,1)S(1)}, u32[]{:S(2)}, u32[]{:S(2)}) %collective-permute-start.26) | collective-permute-done | bytes 786464 | tf_op jit(solution)/shard_map/ppermute | solution.py:153
  75.2 5.4 %collective-permute-done.30 = bf16[3,64,512]{2,1,0:T(8,128)(2,1)S(1)} collective-permute-done((bf16[3,64,512]{2,1,0:T(8,128)(2,1)S(1)}, bf16[3,64,512]{2,1,0:T(8,128)(2,1)S(1)}, u32[]{:S(2)}, u32[]{:S(2)}) %collective-permute-start.30) | collective-permute-done | bytes 196640 | tf_op jit(solution)/shard_map/ppermute | solution.py:153
  82.3 1.6 %collective-permute-start.32 = (bf16[3,128,512]{2,1,0:T(8,128)(2,1)S(1)}, bf16[3,128,512]{2,1,0:T(8,128)(2,1)S(1)}, u32[]{:S(2)}, u32[]{:S(2)}) collective-permute-start(bf16[3,128,512]{2,1,0:T(8,128)(2,1)S(1)} %pad_maximum_fusion.2), channel_id=1, source_target_pairs={{0,2},{1,3},{2,0},{3,1},{4,6},{5,7},{6,4},{7,5},{8,10},{9,11},{10,... | collective-permute-start | bytes 1179656 | tf_op jit(solution)/shard_map/ppermute | solution.py:153
  84.0 7.1 %collective-permute-done.31 = bf16[3,128,512]{2,1,0:T(8,128)(2,1)S(1)} collective-permute-done((bf16[3,128,512]{2,1,0:T(8,128)(2,1)S(1)}, bf16[3,128,512]{2,1,0:T(8,128)(2,1)S(1)}, u32[]{:S(2)}, u32[]{:S(2)}) %collective-permute-start.31) | collective-permute-done | bytes 393248 | tf_op jit(solution)/shard_map/ppermute | solution.py:153
  93.1 1.5 %collective-permute-start.36 = (bf16[1,64,512]{2,1,0:T(8,128)(2,1)S(1)}, bf16[1,64,512]{2,1,0:T(8,128)(2,1)S(1)}, u32[]{:S(2)}, u32[]{:S(2)}) collective-permute-start(bf16[1,64,512]{2,1,0:T(8,128)(2,1)S(1)} %get-tuple-element.153), channel_id=1, source_target_pairs={{0,2},{1,3},{2,0},{3,1},{4,6},{5,7},{6,4},{7,5},{8,10},{9,11},{10,... | collective-permute-start | bytes 196616 | tf_op jit(solution)/shard_map/ppermute | solution.py:153
  94.5 1.6 %collective-permute-start.35 = (bf16[1,64,512]{2,1,0:T(8,128)(2,1)S(1)}, bf16[1,64,512]{2,1,0:T(8,128)(2,1)S(1)}, u32[]{:S(2)}, u32[]{:S(2)}) collective-permute-start(bf16[1,64,512]{2,1,0:T(8,128)(2,1)S(1)} %get-tuple-element.154), channel_id=1, source_target_pairs={{0,4},{4,0},{8,12},{12,8},{16,20},{20,16},{24,28},{28,24},{1,5},{5... | collective-permute-start | bytes 196616 | tf_op jit(solution)/shard_map/ppermute | solution.py:153
  97.4 2.0 %collective-permute-done.35 = bf16[1,64,512]{2,1,0:T(8,128)(2,1)S(1)} collective-permute-done((bf16[1,64,512]{2,1,0:T(8,128)(2,1)S(1)}, bf16[1,64,512]{2,1,0:T(8,128)(2,1)S(1)}, u32[]{:S(2)}, u32[]{:S(2)}) %collective-permute-start.35) | collective-permute-done | bytes 65568 | tf_op jit(solution)/shard_map/ppermute | solution.py:153
  99.5 1.7 %collective-permute-start.38 = (bf16[1,128,512]{2,1,0:T(8,128)(2,1)S(1)}, bf16[1,128,512]{2,1,0:T(8,128)(2,1)S(1)}, u32[]{:S(2)}, u32[]{:S(2)}) collective-permute-start(bf16[1,128,512]{2,1,0:T(8,128)(2,1)S(1)} %pad_maximum_fusion.4), channel_id=1, source_target_pairs={{0,4},{4,0},{8,12},{12,8},{16,20},{20,16},{24,28},{28,24},{1,5},{5... | collective-permute-start | bytes 393224 | tf_op jit(solution)/shard_map/ppermute | solution.py:153
  101.2 1.3 %collective-permute-start.37 = (bf16[128,512]{1,0:T(8,128)(2,1)S(1)}, bf16[128,512]{1,0:T(8,128)(2,1)S(1)}, u32[]{:S(2)}, u32[]{:S(2)}) collective-permute-start(bf16[128,512]{1,0:T(8,128)(2,1)S(1)} %fusion.5), channel_id=1, source_target_pairs={{0,16},{4,20},{8,24},{12,28},{16,0},{20,4},{24,8},{28,12},{1,17},{... | collective-permute-start | bytes 393224 | tf_op jit(solution)/shard_map/ppermute | solution.py:153
  104.6 3.9 %collective-permute-done.37.z2_ref = bf16[128,512]{1,0:T(8,128)(2,1)S(1)} collective-permute-done((bf16[128,512]{1,0:T(8,128)(2,1)S(1)}, bf16[128,512]{1,0:T(8,128)(2,1)S(1)}, u32[]{:S(2)}, u32[]{:S(2)}) %collective-permute-start.37) | collective-permute-done | bytes 131104 | tf_op jit(solution)/shard_map/ppermute | solution.py:153
  (100 shorter events, 25.2 us)
Async XLA Ops:
  0.0 6.7 %collective-permute-start.1 = (bf16[128,512]{1,0:T(8,128)(2,1)}, bf16[128,512]{1,0:T(8,128)(2,1)S(1)}, u32[]{:S(2)}, u32[]{:S(2)}) collective-permute-start(bf16[128,512]{1,0:T(8,128)(2,1)} %refs_0_.1), channel_id=1, source_target_pairs={{0,2},{1,3},{2,0},{3,1},{4,6},{5,7},{6,4},{7,5},{8,10},{9,11},{10,... | collective-permute-start | bytes 393224 | tf_op jit(solution)/shard_map/ppermute | solution.py:153
  3.0 3.7 %collective-permute-start = (bf16[128,512]{1,0:T(8,128)(2,1)}, bf16[128,512]{1,0:T(8,128)(2,1)S(1)}, u32[]{:S(2)}, u32[]{:S(2)}) collective-permute-start(bf16[128,512]{1,0:T(8,128)(2,1)} %refs_0_.1), channel_id=1, source_target_pairs={{0,1},{1,0},{2,3},{3,2},{4,5},{5,4},{6,7},{7,6},{8,9},{9,8},{10,11... | collective-permute-start | bytes 393224 | tf_op jit(solution)/shard_map/ppermute | solution.py:153
  20.8 5.6 %collective-permute-start.4 = (bf16[32,2048]{1,0:T(8,128)(2,1)S(1)}, bf16[32,2048]{1,0:T(8,128)(2,1)S(1)}, u32[]{:S(2)}, u32[]{:S(2)}) collective-permute-start(bf16[32,2048]{1,0:T(8,128)(2,1)S(1)} %get-tuple-element.151), channel_id=1, source_target_pairs={{0,2},{1,3},{2,0},{3,1},{4,6},{5,7},{6,4},{7,5},{8,10},{9,11},{10,... | collective-permute-start | bytes 393224 | tf_op jit(solution)/shard_map/ppermute | solution.py:153
  26.6 10.2 %collective-permute-start.6 = (bf16[1,32,2176]{2,1,0:T(8,128)(2,1)S(1)}, bf16[1,32,2176]{2,1,0:T(8,128)(2,1)S(1)}, u32[]{:S(2)}, u32[]{:S(2)}) collective-permute-start(bf16[1,32,2176]{2,1,0:T(8,128)(2,1)S(1)} %bitcast.64), channel_id=1, source_target_pairs={{0,16},{4,20},{8,24},{12,28},{16,0},{20,4},{24,8},{28,12},{1,17},{... | collective-permute-start | bytes 417800 | tf_op jit(solution)/shard_map/ppermute | solution.py:153
  31.8 7.3 %collective-permute-start.5 = (bf16[1,32,2176]{2,1,0:T(8,128)(2,1)S(1)}, bf16[1,32,2176]{2,1,0:T(8,128)(2,1)S(1)}, u32[]{:S(2)}, u32[]{:S(2)}) collective-permute-start(bf16[1,32,2176]{2,1,0:T(8,128)(2,1)S(1)} %bitcast.65), channel_id=1, source_target_pairs={{0,8},{4,12},{8,0},{12,4},{16,24},{20,28},{24,16},{28,20},{1,9},{5... | collective-permute-start | bytes 417800 | tf_op jit(solution)/shard_map/ppermute | solution.py:153
  31.8 7.4 %collective-permute-start.8 = (bf16[1,32,2176]{2,1,0:T(8,128)(2,1)S(1)}, bf16[1,32,2176]{2,1,0:T(8,128)(2,1)S(1)}, u32[]{:S(2)}, u32[]{:S(2)}) collective-permute-start(bf16[1,32,2176]{2,1,0:T(8,128)(2,1)S(1)} %bitcast.66), channel_id=1, source_target_pairs={{0,4},{4,0},{8,12},{12,8},{16,20},{20,16},{24,28},{28,24},{1,5},{5... | collective-permute-start | bytes 417800 | tf_op jit(solution)/shard_map/ppermute | solution.py:153
  32.6 6.6 %collective-permute-start.7 = (bf16[1,32,2176]{2,1,0:T(8,128)(2,1)S(1)}, bf16[1,32,2176]{2,1,0:T(8,128)(2,1)S(1)}, u32[]{:S(2)}, u32[]{:S(2)}) collective-permute-start(bf16[1,32,2176]{2,1,0:T(8,128)(2,1)S(1)} %bitcast.67), channel_id=1, source_target_pairs={{0,2},{1,3},{2,0},{3,1},{4,6},{5,7},{6,4},{7,5},{8,10},{9,11},{10,... | collective-permute-start | bytes 417800 | tf_op jit(solution)/shard_map/ppermute | solution.py:153
  39.2 5.1 %collective-permute-start.9 = (bf16[1,32,2176]{2,1,0:T(8,128)(2,1)S(1)}, bf16[1,32,2176]{2,1,0:T(8,128)(2,1)S(1)}, u32[]{:S(2)}, u32[]{:S(2)}) collective-permute-start(bf16[1,32,2176]{2,1,0:T(8,128)(2,1)S(1)} %collective-permute-done.6), channel_id=1, source_target_pairs={{0,8},{4,12},{8,0},{12,4},{16,24},{20,28},{24,16},{28,20},{1,9},{5... | collective-permute-start | bytes 417800 | tf_op jit(solution)/shard_map/ppermute | solution.py:153
  39.9 4.5 %collective-permute-start.12 = (bf16[1,32,2176]{2,1,0:T(8,128)(2,1)S(1)}, bf16[1,32,2176]{2,1,0:T(8,128)(2,1)S(1)}, u32[]{:S(2)}, u32[]{:S(2)}) collective-permute-start(bf16[1,32,2176]{2,1,0:T(8,128)(2,1)S(1)} %bitcast.68), channel_id=1, source_target_pairs={{0,1},{1,0},{2,3},{3,2},{4,5},{5,4},{6,7},{7,6},{8,9},{9,8},{10,11... | collective-permute-start | bytes 417800 | tf_op jit(solution)/shard_map/ppermute | solution.py:153
  39.9 5.9 %collective-permute-start.13 = (bf16[1,32,2176]{2,1,0:T(8,128)(2,1)S(1)}, bf16[1,32,2176]{2,1,0:T(8,128)(2,1)S(1)}, u32[]{:S(2)}, u32[]{:S(2)}) collective-permute-start(bf16[1,32,2176]{2,1,0:T(8,128)(2,1)S(1)} %collective-permute-done.7.refs_2_), channel_id=1, source_target_pairs={{0,1},{1,0},{2,3},{3,2},{4,5},{5,4},{6,7},{7,6},{8,9},{9,8},{10,11... | collective-permute-start | bytes 417800 | tf_op jit(solution)/shard_map/ppermute | solution.py:153
  40.4 4.3 %collective-permute-start.11 = (bf16[1,16,2176]{2,1,0:T(8,128)(2,1)S(1)}, bf16[1,16,2176]{2,1,0:T(8,128)(2,1)S(1)}, u32[]{:S(2)}, u32[]{:S(2)}) collective-permute-start(bf16[1,16,2176]{2,1,0:T(8,128)(2,1)S(1)} %slice.120), channel_id=1, source_target_pairs={{0,4},{4,0},{8,12},{12,8},{16,20},{20,16},{24,28},{28,24},{1,5},{5... | collective-permute-start | bytes 208904 | tf_op jit(solution)/shard_map/ppermute | solution.py:153
  41.4 4.3 %collective-permute-start.10 = (bf16[1,16,2176]{2,1,0:T(8,128)(2,1)S(1)}, bf16[1,16,2176]{2,1,0:T(8,128)(2,1)S(1)}, u32[]{:S(2)}, u32[]{:S(2)}) collective-permute-start(bf16[1,16,2176]{2,1,0:T(8,128)(2,1)S(1)} %slice.119), channel_id=1, source_target_pairs={{0,2},{1,3},{2,0},{3,1},{4,6},{5,7},{6,4},{7,5},{8,10},{9,11},{10,... | collective-permute-start | bytes 208904 | tf_op jit(solution)/shard_map/ppermute | solution.py:153
  45.8 10.5 %collective-permute-start.19 = (bf16[3,32,2176]{2,1,0:T(8,128)(2,1)S(1)}, bf16[3,32,2176]{2,1,0:T(8,128)(2,1)S(1)}, u32[]{:S(2)}, u32[]{:S(2)}) collective-permute-start(bf16[3,32,2176]{2,1,0:T(8,128)(2,1)S(1)} %pad_maximum_fusion.refs_0_), channel_id=1, source_target_pairs={{0,4},{4,0},{8,12},{12,8},{16,20},{20,16},{24,28},{28,24},{1,5},{5... | collective-permute-start | bytes 1253384 | tf_op jit(solution)/shard_map/ppermute | solution.py:153
  46.7 10.2 %collective-permute-start.18 = (bf16[3,32,2176]{2,1,0:T(8,128)(2,1)S(1)}, bf16[3,32,2176]{2,1,0:T(8,128)(2,1)S(1)}, u32[]{:S(2)}, u32[]{:S(2)}) collective-permute-start(bf16[3,32,2176]{2,1,0:T(8,128)(2,1)S(1)} %pad_maximum_fusion.refs_0_), channel_id=1, source_target_pairs={{0,2},{1,3},{2,0},{3,1},{4,6},{5,7},{6,4},{7,5},{8,10},{9,11},{10,... | collective-permute-start | bytes 1253384 | tf_op jit(solution)/shard_map/ppermute | solution.py:153
  48.2 8.7 %collective-permute-start.17 = (bf16[3,32,2176]{2,1,0:T(8,128)(2,1)S(1)}, bf16[3,32,2176]{2,1,0:T(8,128)(2,1)S(1)}, u32[]{:S(2)}, u32[]{:S(2)}) collective-permute-start(bf16[3,32,2176]{2,1,0:T(8,128)(2,1)S(1)} %pad_maximum_fusion.refs_0_), channel_id=1, source_target_pairs={{0,1},{1,0},{2,3},{3,2},{4,5},{5,4},{6,7},{7,6},{8,9},{9,8},{10,11... | collective-permute-start | bytes 1253384 | tf_op jit(solution)/shard_map/ppermute | solution.py:153
  57.0 3.2 %collective-permute-start.20 = (bf16[3,32,2176]{2,1,0:T(8,128)(2,1)S(1)}, bf16[3,32,2176]{2,1,0:T(8,128)(2,1)S(1)}, u32[]{:S(2)}, u32[]{:S(2)}) collective-permute-start(bf16[3,32,2176]{2,1,0:T(8,128)(2,1)S(1)} %collective-permute-done.18.refs_2_), channel_id=1, source_target_pairs={{0,1},{1,0},{2,3},{3,2},{4,5},{5,4},{6,7},{7,6},{8,9},{9,8},{10,11... | collective-permute-start | bytes 1253384 | tf_op jit(solution)/shard_map/ppermute | solution.py:153
  57.0 8.9 %collective-permute-start.21 = (bf16[3,32,2176]{2,1,0:T(8,128)(2,1)S(1)}, bf16[3,32,2176]{2,1,0:T(8,128)(2,1)S(1)}, u32[]{:S(2)}, u32[]{:S(2)}) collective-permute-start(bf16[3,32,2176]{2,1,0:T(8,128)(2,1)S(1)} %collective-permute-done.19.refs_0_), channel_id=1, source_target_pairs={{0,1},{1,0},{2,3},{3,2},{4,5},{5,4},{6,7},{7,6},{8,9},{9,8},{10,11... | collective-permute-start | bytes 1253384 | tf_op jit(solution)/shard_map/ppermute | solution.py:153
  57.5 7.1 %collective-permute-start.22 = (bf16[3,16,2176]{2,1,0:T(8,128)(2,1)S(1)}, bf16[3,16,2176]{2,1,0:T(8,128)(2,1)S(1)}, u32[]{:S(2)}, u32[]{:S(2)}) collective-permute-start(bf16[3,16,2176]{2,1,0:T(8,128)(2,1)S(1)} %slice.121), channel_id=1, source_target_pairs={{0,2},{1,3},{2,0},{3,1},{4,6},{5,7},{6,4},{7,5},{8,10},{9,11},{10,... | collective-permute-start | bytes 626696 | tf_op jit(solution)/shard_map/ppermute | solution.py:153
  59.1 6.8 %collective-permute-start.23 = (bf16[3,16,2176]{2,1,0:T(8,128)(2,1)S(1)}, bf16[3,16,2176]{2,1,0:T(8,128)(2,1)S(1)}, u32[]{:S(2)}, u32[]{:S(2)}) collective-permute-start(bf16[3,16,2176]{2,1,0:T(8,128)(2,1)S(1)} %slice.122), channel_id=1, source_target_pairs={{0,4},{4,0},{8,12},{12,8},{16,20},{20,16},{24,28},{28,24},{1,5},{5... | collective-permute-start | bytes 626696 | tf_op jit(solution)/shard_map/ppermute | solution.py:153
  72.7 8.1 %collective-permute-start.27 = (bf16[1,2,3,128,512]{4,3,2,1,0:T(8,128)(2,1)S(1)}, bf16[1,2,3,128,512]{4,3,2,1,0:T(8,128)(2,1)S(1)}, u32[]{:S(2)}, u32[]{:S(2)}) collective-permute-start(bf16[1,2,3,128,512]{4,3,2,1,0:T(8,128)(2,1)S(1)} %get-tuple-element.120), channel_id=1, source_target_pairs={{0,1},{1,0},{2,3},{3,2},{4,5},{5,4},{6,7},{7,6},{8,9},{9,8},{10,11... | collective-permute-start | bytes 2359304 | tf_op jit(solution)/shard_map/ppermute | solution.py:153
  72.9 7.9 %collective-permute-start.28 = (bf16[2,2,1,128,512]{4,3,2,1,0:T(8,128)(2,1)S(1)}, bf16[2,2,1,128,512]{4,3,2,1,0:T(8,128)(2,1)S(1)}, u32[]{:S(2)}, u32[]{:S(2)}) collective-permute-start(bf16[2,2,1,128,512]{4,3,2,1,0:T(8,128)(2,1)S(1)} %get-tuple-element.122), channel_id=1, source_target_pairs={{0,1},{1,0},{2,3},{3,2},{4,5},{5,4},{6,7},{7,6},{8,9},{9,8},{10,11... | collective-permute-start | bytes 1572872 | tf_op jit(solution)/shard_map/ppermute | solution.py:153
  73.5 7.1 %collective-permute-start.30 = (bf16[3,64,512]{2,1,0:T(8,128)(2,1)S(1)}, bf16[3,64,512]{2,1,0:T(8,128)(2,1)S(1)}, u32[]{:S(2)}, u32[]{:S(2)}) collective-permute-start(bf16[3,64,512]{2,1,0:T(8,128)(2,1)S(1)} %get-tuple-element.149), channel_id=1, source_target_pairs={{0,2},{1,3},{2,0},{3,1},{4,6},{5,7},{6,4},{7,5},{8,10},{9,11},{10,... | collective-permute-start | bytes 589832 | tf_op jit(solution)/shard_map/ppermute | solution.py:153
  74.1 6.7 %collective-permute-start.29 = (bf16[3,64,512]{2,1,0:T(8,128)(2,1)S(1)}, bf16[3,64,512]{2,1,0:T(8,128)(2,1)S(1)}, u32[]{:S(2)}, u32[]{:S(2)}) collective-permute-start(bf16[3,64,512]{2,1,0:T(8,128)(2,1)S(1)} %get-tuple-element.150), channel_id=1, source_target_pairs={{0,4},{4,0},{8,12},{12,8},{16,20},{20,16},{24,28},{28,24},{1,5},{5... | collective-permute-start | bytes 589832 | tf_op jit(solution)/shard_map/ppermute | solution.py:153
  80.9 10.3 %collective-permute-start.31 = (bf16[3,128,512]{2,1,0:T(8,128)(2,1)S(1)}, bf16[3,128,512]{2,1,0:T(8,128)(2,1)S(1)}, u32[]{:S(2)}, u32[]{:S(2)}) collective-permute-start(bf16[3,128,512]{2,1,0:T(8,128)(2,1)S(1)} %pad_maximum_fusion.1), channel_id=1, source_target_pairs={{0,4},{4,0},{8,12},{12,8},{16,20},{20,16},{24,28},{28,24},{1,5},{5... | collective-permute-start | bytes 1179656 | tf_op jit(solution)/shard_map/ppermute | solution.py:153
  82.3 10.0 %collective-permute-start.32 = (bf16[3,128,512]{2,1,0:T(8,128)(2,1)S(1)}, bf16[3,128,512]{2,1,0:T(8,128)(2,1)S(1)}, u32[]{:S(2)}, u32[]{:S(2)}) collective-permute-start(bf16[3,128,512]{2,1,0:T(8,128)(2,1)S(1)} %pad_maximum_fusion.2), channel_id=1, source_target_pairs={{0,2},{1,3},{2,0},{3,1},{4,6},{5,7},{6,4},{7,5},{8,10},{9,11},{10,... | collective-permute-start | bytes 1179656 | tf_op jit(solution)/shard_map/ppermute | solution.py:153
  92.5 6.9 %collective-permute-start.34 = (bf16[128,512]{1,0:T(8,128)(2,1)S(1)}, bf16[128,512]{1,0:T(8,128)(2,1)S(1)}, u32[]{:S(2)}, u32[]{:S(2)}) collective-permute-start(bf16[128,512]{1,0:T(8,128)(2,1)S(1)} %get-tuple-element.147), channel_id=1, source_target_pairs={{0,8},{4,12},{8,0},{12,4},{16,24},{20,28},{24,16},{28,20},{1,9},{5... | collective-permute-start | bytes 393224 | tf_op jit(solution)/shard_map/ppermute | solution.py:153
  93.1 4.3 %collective-permute-start.36 = (bf16[1,64,512]{2,1,0:T(8,128)(2,1)S(1)}, bf16[1,64,512]{2,1,0:T(8,128)(2,1)S(1)}, u32[]{:S(2)}, u32[]{:S(2)}) collective-permute-start(bf16[1,64,512]{2,1,0:T(8,128)(2,1)S(1)} %get-tuple-element.153), channel_id=1, source_target_pairs={{0,2},{1,3},{2,0},{3,1},{4,6},{5,7},{6,4},{7,5},{8,10},{9,11},{10,... | collective-permute-start | bytes 196616 | tf_op jit(solution)/shard_map/ppermute | solution.py:153
  94.5 4.9 %collective-permute-start.35 = (bf16[1,64,512]{2,1,0:T(8,128)(2,1)S(1)}, bf16[1,64,512]{2,1,0:T(8,128)(2,1)S(1)}, u32[]{:S(2)}, u32[]{:S(2)}) collective-permute-start(bf16[1,64,512]{2,1,0:T(8,128)(2,1)S(1)} %get-tuple-element.154), channel_id=1, source_target_pairs={{0,4},{4,0},{8,12},{12,8},{16,20},{20,16},{24,28},{28,24},{1,5},{5... | collective-permute-start | bytes 196616 | tf_op jit(solution)/shard_map/ppermute | solution.py:153
  96.2 7.1 %collective-permute-start.33 = (bf16[128,512]{1,0:T(8,128)(2,1)S(1)}, bf16[128,512]{1,0:T(8,128)(2,1)S(1)}, u32[]{:S(2)}, u32[]{:S(2)}) collective-permute-start(bf16[128,512]{1,0:T(8,128)(2,1)S(1)} %get-tuple-element.148), channel_id=1, source_target_pairs={{0,8},{4,12},{8,0},{12,4},{16,24},{20,28},{24,16},{28,20},{1,9},{5... | collective-permute-start | bytes 393224 | tf_op jit(solution)/shard_map/ppermute | solution.py:153
  99.5 5.0 %collective-permute-start.38 = (bf16[1,128,512]{2,1,0:T(8,128)(2,1)S(1)}, bf16[1,128,512]{2,1,0:T(8,128)(2,1)S(1)}, u32[]{:S(2)}, u32[]{:S(2)}) collective-permute-start(bf16[1,128,512]{2,1,0:T(8,128)(2,1)S(1)} %pad_maximum_fusion.4), channel_id=1, source_target_pairs={{0,4},{4,0},{8,12},{12,8},{16,20},{20,16},{24,28},{28,24},{1,5},{5... | collective-permute-start | bytes 393224 | tf_op jit(solution)/shard_map/ppermute | solution.py:153
  101.2 7.3 %collective-permute-start.37 = (bf16[128,512]{1,0:T(8,128)(2,1)S(1)}, bf16[128,512]{1,0:T(8,128)(2,1)S(1)}, u32[]{:S(2)}, u32[]{:S(2)}) collective-permute-start(bf16[128,512]{1,0:T(8,128)(2,1)S(1)} %fusion.5), channel_id=1, source_target_pairs={{0,16},{4,20},{8,24},{12,28},{16,0},{20,4},{24,8},{28,12},{1,17},{... | collective-permute-start | bytes 393224 | tf_op jit(solution)/shard_map/ppermute | solution.py:153
  102.6 6.0 %collective-permute-start.39 = (bf16[1,128,512]{2,1,0:T(8,128)(2,1)S(1)}, bf16[1,128,512]{2,1,0:T(8,128)(2,1)S(1)}, u32[]{:S(2)}, u32[]{:S(2)}) collective-permute-start(bf16[1,128,512]{2,1,0:T(8,128)(2,1)S(1)} %pad_maximum_fusion.5), channel_id=1, source_target_pairs={{0,2},{1,3},{2,0},{3,1},{4,6},{5,7},{6,4},{7,5},{8,10},{9,11},{10,... | collective-permute-start | bytes 393224 | tf_op jit(solution)/shard_map/ppermute | solution.py:153
  (17 other events, 176.8 us)

commit v11 on v10

--- a/solution.py
+++ b/solution.py
@@ -204,7 +204,7 @@
         pltpu.make_async_copy(source, target, sems.at[i])
         for i, (source, target) in enumerate(zip(hbm_refs, local_refs))
     ]
-    for copy in copies[:12]:
+    for copy in copies:
         copy.start()
     tp_index = lax.axis_index("tp")
     heads = q_ref.shape[1] // head_dim
@@ -229,8 +229,6 @@
     contract = (((1,), (1,)), ((), ()))
     for copy in copies[9:12]:
         copy.wait()
-    for copy in copies[12:]:
-        copy.start()
     key_lin = jnp.dot(normed, k_ref[...], preferred_element_type=jnp.float32)
     values_new = jnp.dot(normed, v_ref[...], preferred_element_type=jnp.float32).astype(jnp.bfloat16)
     query_lin = jnp.dot(normed, q_ref[...], preferred_element_type=jnp.float32)
@@ -438,9 +436,9 @@
     rows_ref[:, width:] = jnp.where(lane < LANES // 2, high, spread - high).astype(jnp.bfloat16)
 
 
-def experts_kernel(plan, *refs):
-    pieces, residual_refs = refs[: len(plan)], refs[len(plan) : -7]
-    gate_ref, up_ref, down_ref, keep_ref, send_ref, rows_ref, sums_ref = refs[-7:]
+def experts_kernel(plan, residuals, *refs):
+    pieces, residual_refs = refs[: len(plan)], refs[len(plan) : len(plan) + residuals]
+    gate_ref, up_ref, down_ref, keep_ref, *send_refs, rows_ref, sums_ref = refs[len(plan) + residuals :]
     req_index, tp_index = lax.axis_index("req"), lax.axis_index("tp")
     columns, _, levels, group_rows, share_width = keep_ref.shape
     width = gate_ref.shape[1]
@@ -475,10 +473,12 @@
             sums_ref[...] = part
             sums_ref[mine, :] += residual_ref[:, pl.ds(start, share_width)]
             part = sums_ref[...]
-        target = send_ref if step % 2 else keep_ref
-        part = part.reshape(columns, levels, group_rows, share_width).astype(target.dtype)
+        part = part.reshape(columns, levels, group_rows, share_width)
+        if step % 2:
+            send_refs[step // 2][...] = part.astype(jnp.bfloat16)
+            continue
         for column in range(columns):
-            target[column, step // 2] = part[column]
+            keep_ref[column, step // 2] = part[column]
 
 
 def run_experts(pieces, weights, group_rows, *residual):
@@ -486,15 +486,13 @@
     pieces = [piece for _, piece in pieces]
     columns, levels, packed = 1 + max(place[0] for place in plan), *pieces[0].shape[::2]
     rows, share_width = columns * levels * group_rows, weights[2].shape[1] // 4
-    out_shape = (columns, 2, levels, group_rows, share_width)
-    return pl.pallas_call(
-        functools.partial(experts_kernel, plan),
-        out_shape=[
-            jax.ShapeDtypeStruct(out_shape, jnp.float32),
-            jax.ShapeDtypeStruct(out_shape, jnp.bfloat16),
-        ],
+    sums = (levels, group_rows, share_width)
+    keep, *send = pl.pallas_call(
+        functools.partial(experts_kernel, plan, len(residual)),
+        out_shape=[jax.ShapeDtypeStruct((columns, 2, *sums), jnp.float32)]
+        + [jax.ShapeDtypeStruct((columns, *sums), jnp.bfloat16)] * 2,
         in_specs=[VMEM] * (len(pieces) + len(residual) + 3),
-        out_specs=[VMEM] * 2,
+        out_specs=[VMEM] * 3,
         scratch_shapes=[
             pltpu.VMEM((rows, packed), jnp.bfloat16),
             pltpu.VMEM((rows, share_width), jnp.float32),
@@ -502,6 +500,7 @@
         compiler_params=pltpu.CompilerParams(vmem_limit_bytes=VMEM_LIMIT),
         name="experts",
     )(*pieces, *residual, *weights)
+    return keep, send
 
 
 def finish_kernel(own_ref, z1_ref, z2_ref, x_ref, y_ref, out_ref):
@@ -527,11 +526,11 @@
 
 
 def with_core(pair):
-    return pair[0], flip(pair[1], "tp", 1)
+    return pair[0], list(other_core(pair[1]))
 
 
 def joined(pair, column, y):
-    return pair[0][column, y] + pair[1][column, y].astype(jnp.float32)
+    return pair[0][column, y] + pair[1][y][column].astype(jnp.float32)
 
 
 def near_pieces(column, line, core):
@@ -574,8 +573,8 @@
     share_rows, width = kept.shape
     token_count, share_width = 4 * share_rows, width // 4
     core = flip(core, "tp", 1)
-    far = flip((far + core[1].astype(jnp.float32)).astype(jnp.bfloat16), "tp", 2)
-    kept, far = ordered(kept + core[0].astype(jnp.float32), far)
+    far, kept, core = ordered((far + core[1].astype(jnp.float32)).astype(jnp.bfloat16), kept, core)
+    kept, far = ordered(kept + core[0].astype(jnp.float32), flip(far, "tp", 2))
     rows, residual = pl.pallas_call(
         pack_kernel,
         out_shape=[
@@ -622,9 +621,11 @@
         token_count,
     )
     all_0, near_3, side_3 = ordered(all_0, near_3, side_3)
-    all_0, near_3, side_3 = ordered(all_0, near_3, with_core(side_3))
-    near_3, all_0, relay_3 = ordered(
-        with_core(near_3), with_core(all_0), relayed(joined(side_3, 0, 1))
+    keep, (send, first) = side_3
+    all_0, near_3, keep, send, first = ordered(all_0, near_3, keep, send, flip(first, "tp", 1))
+    relay_3 = relayed(joined((keep, (send, first)), 0, 1))
+    near_3, all_0, side_3, relay_3 = ordered(
+        with_core(near_3), with_core(all_0), (keep, [flip(send, "tp", 1), first]), relay_3
     )
     sums_3 = ordered(*neighbours(joined(side_3, 0, 0), joined(near_3, 0, 1), *relay_3))
     sent = joined(near_3, 0, 0) + sums_3[0].astype(jnp.float32) + sums_3[1].astype(jnp.float32)

time: 109 us -> 108 us (level)
    ppermute x40 -> x43, waiting for transfers between devices: 49.5 us -> 48.6 us  [flip(): lax.ppermute(value, axis, [(i, i ^ bits) for i in range(lax.axis_size(axi...]
    ppermute x40 -> x43, starting transfers between devices: 36.5 us -> 35.8 us  [flip(): lax.ppermute(value, axis, [(i, i ^ bits) for i in range(lax.axis_size(axi...]
  transfers between devices with their start and end apart: 40 -> 43, of which waited for: 26 -> 30; matrix products, arithmetic and copies ran while one was open for 1% -> 1% of each run, Pallas kernels for 6% -> 7%
where the time goes in v11:
time: 108 us
  waiting for transfers between devices  48.6 us (45%)
  starting transfers between devices  35.8 us (33%)
  Pallas kernels  19 us (18%)
  other arithmetic  3.17 us (3%)
    ppermute x43, waiting for transfers between devices, flip(): lax.ppermute(value, axis, [(i, i ^ bits) for i in range(lax.axis_size(axi...  48.6 us
    ppermute x43, starting transfers between devices, flip(): lax.ppermute(value, axis, [(i, i ^ bits) for i in range(lax.axis_size(axi...  35.8 us
    pallas_call x1, Pallas kernels, attention_shares(): pl.pallas_call(attention_kernel, out_shape=[jax.ShapeDtypeStruct(share, j...  8.22 us
    pallas_call x3, Pallas kernels, run_experts(): pl.pallas_call(functools.partial(experts_kernel, plan, len(residual)), ou...  7.44 us
    pallas_call x1, Pallas kernels, attention_shares(): pl.pallas_call(layout_kernel, out_shape=[rope, rope, jax.ShapeDtypeStruct...  2.39 us
  transfers between devices with their start and end apart: 43, of which 30 were waited for; matrix products, arithmetic and copies ran while one was open for 1% of the time, Pallas kernels for 7%

profile of v11, /device:TPU:0, one launch (start us, length us, event | category | flops | bytes accessed | tf_op | source)
XLA Modules:
  0.0 107.7 jit_solution(4879117191920503440)
XLA Ops:
  0.0 3.0 %collective-permute-start.1 = (bf16[128,512]{1,0:T(8,128)(2,1)}, bf16[128,512]{1,0:T(8,128)(2,1)S(1)}, u32[]{:S(2)}, u32[]{:S(2)}) collective-permute-start(bf16[128,512]{1,0:T(8,128)(2,1)} %refs_0_.1), channel_id=1, source_target_pairs={{0,2},{1,3},{2,0},{3,1},{4,6},{5,7},{6,4},{7,5},{8,10},{9,11},{10,... | collective-permute-start | bytes 393224 | tf_op jit(solution)/shard_map/ppermute | solution.py:153
  3.0 2.4 %layout.1 = (f32[128,128]{1,0:T(8,128)}, f32[128,128]{1,0:T(8,128)}, s32[1,6144]{1,0:T(1,128)}, s32[48]{0:T(128)}) custom-call(s32[9]{0:T(128)} %refs_4_.1, s32[9,32]{1,0:T(8,128)} %refs_5_.1, f32[1,128]{1,0:T(1,128)} %constant.2.clone.frequency_ref), custom_call_target="tpu_custom_call" | custom-call | tf_op jit(solution)/shard_map/layout/pallas_call | solution.py:365
  6.7 1.3 %collective-permute-done.2.refs_3_ = bf16[128,512]{1,0:T(8,128)(2,1)S(1)} collective-permute-done((bf16[128,512]{1,0:T(8,128)(2,1)S(1)}, bf16[128,512]{1,0:T(8,128)(2,1)S(1)}, u32[]{:S(2)}, u32[]{:S(2)}) %collective-permute-start.2) | collective-permute-done | bytes 131104 | tf_op jit(solution)/shard_map/ppermute | solution.py:153
  8.7 8.2 %attention.1 = (f32[32,2048]{1,0:T(8,128)}, f32[32,2048]{1,0:T(8,128)}, bf16[2,32,2048]{2,1,0:T(8,128)(2,1)}) custom-call(bf16[128,512]{1,0:T(8,128)(2,1)} %refs_0_.1, bf16[128,512]{1,0:T(8,128)(2,1)} %copy-done.7, bf16[128,512]{1,0:T(8,128)(2,1)} %copy-done.6, bf16[128,512]{1,0:T(8,128)(2,1)} %copy-done.8, s32[9]{0:T(128)} %refs_4_.1, s32[9,32]{1,0:T(8,128)} %refs_5_.1, ...), custom_call_target="tpu_custom_call" | custom-call | tf_op jit(solution)/shard_map/attention/pallas_call | solution.py:390
  17.1 1.6 %collective-permute-done.3 = bf16[2,32,2048]{2,1,0:T(8,128)(2,1)S(1)} collective-permute-done((bf16[2,32,2048]{2,1,0:T(8,128)(2,1)}, bf16[2,32,2048]{2,1,0:T(8,128)(2,1)S(1)}, u32[]{:S(2)}, u32[]{:S(2)}) %collective-permute-start.3) | collective-permute-done | bytes 262176 | tf_op jit(solution)/shard_map/ppermute | solution.py:153
  19.9 1.8 %collective-permute-start.4 = (bf16[32,2048]{1,0:T(8,128)(2,1)S(1)}, bf16[32,2048]{1,0:T(8,128)(2,1)S(1)}, u32[]{:S(2)}, u32[]{:S(2)}) collective-permute-start(bf16[32,2048]{1,0:T(8,128)(2,1)S(1)} %fusion.8), channel_id=1, source_target_pairs={{0,2},{1,3},{2,0},{3,1},{4,6},{5,7},{6,4},{7,5},{8,10},{9,11},{10,... | collective-permute-start | bytes 393224 | tf_op jit(solution)/shard_map/ppermute | solution.py:153
  22.7 2.8 %collective-permute-done.4.far_ref = bf16[32,2048]{1,0:T(8,128)(2,1)S(1)} collective-permute-done((bf16[32,2048]{1,0:T(8,128)(2,1)S(1)}, bf16[32,2048]{1,0:T(8,128)(2,1)S(1)}, u32[]{:S(2)}, u32[]{:S(2)}) %collective-permute-start.4) | collective-permute-done | bytes 131104 | tf_op jit(solution)/shard_map/ppermute | solution.py:153
  25.7 2.9 %collective-permute-start.6 = (bf16[1,32,2176]{2,1,0:T(8,128)(2,1)S(1)}, bf16[1,32,2176]{2,1,0:T(8,128)(2,1)S(1)}, u32[]{:S(2)}, u32[]{:S(2)}) collective-permute-start(bf16[1,32,2176]{2,1,0:T(8,128)(2,1)S(1)} %bitcast.85), channel_id=1, source_target_pairs={{0,16},{4,20},{8,24},{12,28},{16,0},{20,4},{24,8},{28,12},{1,17},{... | collective-permute-start | bytes 417800 | tf_op jit(solution)/shard_map/ppermute | solution.py:153
  28.6 1.6 %collective-permute-start.5 = (bf16[1,32,2176]{2,1,0:T(8,128)(2,1)S(1)}, bf16[1,32,2176]{2,1,0:T(8,128)(2,1)S(1)}, u32[]{:S(2)}, u32[]{:S(2)}) collective-permute-start(bf16[1,32,2176]{2,1,0:T(8,128)(2,1)S(1)} %bitcast.86), channel_id=1, source_target_pairs={{0,8},{4,12},{8,0},{12,4},{16,24},{20,28},{24,16},{28,20},{1,9},{5... | collective-permute-start | bytes 417800 | tf_op jit(solution)/shard_map/ppermute | solution.py:153
  30.2 1.5 %collective-permute-start.8 = (bf16[1,32,2176]{2,1,0:T(8,128)(2,1)S(1)}, bf16[1,32,2176]{2,1,0:T(8,128)(2,1)S(1)}, u32[]{:S(2)}, u32[]{:S(2)}) collective-permute-start(bf16[1,32,2176]{2,1,0:T(8,128)(2,1)S(1)} %bitcast.87), channel_id=1, source_target_pairs={{0,4},{4,0},{8,12},{12,8},{16,20},{20,16},{24,28},{28,24},{1,5},{5... | collective-permute-start | bytes 417800 | tf_op jit(solution)/shard_map/ppermute | solution.py:153
  31.7 1.5 %collective-permute-start.7 = (bf16[1,32,2176]{2,1,0:T(8,128)(2,1)S(1)}, bf16[1,32,2176]{2,1,0:T(8,128)(2,1)S(1)}, u32[]{:S(2)}, u32[]{:S(2)}) collective-permute-start(bf16[1,32,2176]{2,1,0:T(8,128)(2,1)S(1)} %bitcast.88), channel_id=1, source_target_pairs={{0,2},{1,3},{2,0},{3,1},{4,6},{5,7},{6,4},{7,5},{8,10},{9,11},{10,... | collective-permute-start | bytes 417800 | tf_op jit(solution)/shard_map/ppermute | solution.py:153
  33.2 1.6 %collective-permute-done.6 = bf16[1,32,2176]{2,1,0:T(8,128)(2,1)S(1)} collective-permute-done((bf16[1,32,2176]{2,1,0:T(8,128)(2,1)S(1)}, bf16[1,32,2176]{2,1,0:T(8,128)(2,1)S(1)}, u32[]{:S(2)}, u32[]{:S(2)}) %collective-permute-start.6) | collective-permute-done | bytes 139296 | tf_op jit(solution)/shard_map/ppermute | solution.py:153
  35.2 1.5 %collective-permute-done.7.refs_2_ = bf16[1,32,2176]{2,1,0:T(8,128)(2,1)S(1)} collective-permute-done((bf16[1,32,2176]{2,1,0:T(8,128)(2,1)S(1)}, bf16[1,32,2176]{2,1,0:T(8,128)(2,1)S(1)}, u32[]{:S(2)}, u32[]{:S(2)}) %collective-permute-start.7) | collective-permute-done | bytes 139296 | tf_op jit(solution)/shard_map/ppermute | solution.py:153
  38.6 1.5 %collective-permute-start.10 = (bf16[1,16,2176]{2,1,0:T(8,128)(2,1)S(1)}, bf16[1,16,2176]{2,1,0:T(8,128)(2,1)S(1)}, u32[]{:S(2)}, u32[]{:S(2)}) collective-permute-start(bf16[1,16,2176]{2,1,0:T(8,128)(2,1)S(1)} %slice.107), channel_id=1, source_target_pairs={{0,2},{1,3},{2,0},{3,1},{4,6},{5,7},{6,4},{7,5},{8,10},{9,11},{10,... | collective-permute-start | bytes 208904 | tf_op jit(solution)/shard_map/ppermute | solution.py:153
  40.1 1.6 %collective-permute-done.9 = bf16[1,32,2176]{2,1,0:T(8,128)(2,1)S(1)} collective-permute-done((bf16[1,32,2176]{2,1,0:T(8,128)(2,1)S(1)}, bf16[1,32,2176]{2,1,0:T(8,128)(2,1)S(1)}, u32[]{:S(2)}, u32[]{:S(2)}) %collective-permute-start.9) | collective-permute-done | bytes 139296 | tf_op jit(solution)/shard_map/ppermute | solution.py:153
  44.0 1.5 %collective-permute-start.18 = (bf16[3,32,2176]{2,1,0:T(8,128)(2,1)S(1)}, bf16[3,32,2176]{2,1,0:T(8,128)(2,1)S(1)}, u32[]{:S(2)}, u32[]{:S(2)}) collective-permute-start(bf16[3,32,2176]{2,1,0:T(8,128)(2,1)S(1)} %pad_maximum_fusion.refs_0_), channel_id=1, source_target_pairs={{0,2},{1,3},{2,0},{3,1},{4,6},{5,7},{6,4},{7,5},{8,10},{9,11},{10,... | collective-permute-start | bytes 1253384 | tf_op jit(solution)/shard_map/ppermute | solution.py:153
  46.1 1.4 %collective-permute-done.14.refs_5_ = bf16[1,32,2176]{2,1,0:T(8,128)(2,1)S(1)} collective-permute-done((bf16[1,32,2176]{2,1,0:T(8,128)(2,1)S(1)}, bf16[1,32,2176]{2,1,0:T(8,128)(2,1)S(1)}, u32[]{:S(2)}, u32[]{:S(2)}) %collective-permute-start.14) | collective-permute-done | bytes 139296 | tf_op jit(solution)/shard_map/ppermute | solution.py:153
  48.8 2.0 %experts.3 = (f32[2,2,1,128,512]{4,3,2,1,0:T(8,128)S(1)}, bf16[2,1,128,512]{3,2,1,0:T(8,128)(2,1)S(1)}, bf16[2,1,128,512]{3,2,1,0:T(8,128)(2,1)S(1)}) custom-call(bf16[1,32,2176]{2,1,0:T(8,128)(2,1)S(1)} %bitcast.90, bf16[1,32,2176]{2,1,0:T(8,128)(2,1)S(1)} %collective-permute-done.12.refs_1_, bf16[1,32,2176]{2,1,0:T(8,128)(2,1)S(1)} %collective-permute-done.7.refs_2_, ...), custom_call_target="tpu_custom_call" | custom-call | tf_op jit(solution)/shard_map/experts/pallas_call | solution.py:490
  50.8 2.7 %collective-permute-done.19.refs_0_ = bf16[3,32,2176]{2,1,0:T(8,128)(2,1)S(1)} collective-permute-done((bf16[3,32,2176]{2,1,0:T(8,128)(2,1)S(1)}, bf16[3,32,2176]{2,1,0:T(8,128)(2,1)S(1)}, u32[]{:S(2)}, u32[]{:S(2)}) %collective-permute-start.19) | collective-permute-done | bytes 417824 | tf_op jit(solution)/shard_map/ppermute | solution.py:153
  54.8 1.6 %collective-permute-start.22 = (bf16[3,16,2176]{2,1,0:T(8,128)(2,1)S(1)}, bf16[3,16,2176]{2,1,0:T(8,128)(2,1)S(1)}, u32[]{:S(2)}, u32[]{:S(2)}) collective-permute-start(bf16[3,16,2176]{2,1,0:T(8,128)(2,1)S(1)} %slice.109), channel_id=1, source_target_pairs={{0,2},{1,3},{2,0},{3,1},{4,6},{5,7},{6,4},{7,5},{8,10},{9,11},{10,... | collective-permute-start | bytes 626696 | tf_op jit(solution)/shard_map/ppermute | solution.py:153
  57.3 2.7 %experts.4 = (f32[1,2,3,128,512]{4,3,2,1,0:T(8,128)S(1)}, bf16[1,3,128,512]{3,2,1,0:T(8,128)(2,1)S(1)}, bf16[1,3,128,512]{3,2,1,0:T(8,128)(2,1)S(1)}) custom-call(bf16[3,32,2176]{2,1,0:T(8,128)(2,1)S(1)} %pad_maximum_fusion.refs_0_, bf16[3,32,2176]{2,1,0:T(8,128)(2,1)S(1)} %collective-permute-done.17.refs_1_, ...), custom_call_target="tpu_custom_call" | custom-call | tf_op jit(solution)/shard_map/experts/pallas_call | solution.py:490
  60.0 1.9 %collective-permute-done.22.refs_2_ = bf16[3,16,2176]{2,1,0:T(8,128)(2,1)S(1)} collective-permute-done((bf16[3,16,2176]{2,1,0:T(8,128)(2,1)S(1)}, bf16[3,16,2176]{2,1,0:T(8,128)(2,1)S(1)}, u32[]{:S(2)}, u32[]{:S(2)}) %collective-permute-start.22) | collective-permute-done | bytes 208928 | tf_op jit(solution)/shard_map/ppermute | solution.py:153
  65.0 2.7 %experts.5 = (f32[1,2,3,128,512]{4,3,2,1,0:T(8,128)S(1)}, bf16[1,3,128,512]{3,2,1,0:T(8,128)(2,1)S(1)}, bf16[1,3,128,512]{3,2,1,0:T(8,128)(2,1)S(1)}) custom-call(bf16[3,32,2176]{2,1,0:T(8,128)(2,1)S(1)} %collective-permute-done.19.refs_0_, bf16[3,32,2176]{2,1,0:T(8,128)(2,1)S(1)} %collective-permute-done.21.refs_1_, ...), custom_call_target="tpu_custom_call" | custom-call | tf_op jit(solution)/shard_map/experts/pallas_call | solution.py:490
  68.0 1.5 %collective-permute-done.26 = bf16[1,3,128,512]{3,2,1,0:T(8,128)(2,1)S(1)} collective-permute-done((bf16[1,3,128,512]{3,2,1,0:T(8,128)(2,1)S(1)}, bf16[1,3,128,512]{3,2,1,0:T(8,128)(2,1)S(1)}, u32[]{:S(2)}, u32[]{:S(2)}) %collective-permute-start.26) | collective-permute-done | bytes 393248 | tf_op jit(solution)/shard_map/ppermute | solution.py:153
  71.7 5.1 %collective-permute-done.33 = bf16[3,64,512]{2,1,0:T(8,128)(2,1)S(1)} collective-permute-done((bf16[3,64,512]{2,1,0:T(8,128)(2,1)S(1)}, bf16[3,64,512]{2,1,0:T(8,128)(2,1)S(1)}, u32[]{:S(2)}, u32[]{:S(2)}) %collective-permute-start.33) | collective-permute-done | bytes 196640 | tf_op jit(solution)/shard_map/ppermute | solution.py:153
  80.1 1.4 %collective-permute-start.35 = (bf16[3,128,512]{2,1,0:T(8,128)(2,1)S(1)}, bf16[3,128,512]{2,1,0:T(8,128)(2,1)S(1)}, u32[]{:S(2)}, u32[]{:S(2)}) collective-permute-start(bf16[3,128,512]{2,1,0:T(8,128)(2,1)S(1)} %pad_maximum_fusion.2), channel_id=1, source_target_pairs={{0,2},{1,3},{2,0},{3,1},{4,6},{5,7},{6,4},{7,5},{8,10},{9,11},{10,... | collective-permute-start | bytes 1179656 | tf_op jit(solution)/shard_map/ppermute | solution.py:153
  81.7 8.4 %collective-permute-done.34 = bf16[3,128,512]{2,1,0:T(8,128)(2,1)S(1)} collective-permute-done((bf16[3,128,512]{2,1,0:T(8,128)(2,1)S(1)}, bf16[3,128,512]{2,1,0:T(8,128)(2,1)S(1)}, u32[]{:S(2)}, u32[]{:S(2)}) %collective-permute-start.34) | collective-permute-done | bytes 393248 | tf_op jit(solution)/shard_map/ppermute | solution.py:153
  92.6 1.4 %collective-permute-start.39 = (bf16[1,64,512]{2,1,0:T(8,128)(2,1)S(1)}, bf16[1,64,512]{2,1,0:T(8,128)(2,1)S(1)}, u32[]{:S(2)}, u32[]{:S(2)}) collective-permute-start(bf16[1,64,512]{2,1,0:T(8,128)(2,1)S(1)} %get-tuple-element.187), channel_id=1, source_target_pairs={{0,2},{1,3},{2,0},{3,1},{4,6},{5,7},{6,4},{7,5},{8,10},{9,11},{10,... | collective-permute-start | bytes 196616 | tf_op jit(solution)/shard_map/ppermute | solution.py:153
  96.9 1.4 %collective-permute-done.38 = bf16[1,64,512]{2,1,0:T(8,128)(2,1)S(1)} collective-permute-done((bf16[1,64,512]{2,1,0:T(8,128)(2,1)S(1)}, bf16[1,64,512]{2,1,0:T(8,128)(2,1)S(1)}, u32[]{:S(2)}, u32[]{:S(2)}) %collective-permute-start.38) | collective-permute-done | bytes 65568 | tf_op jit(solution)/shard_map/ppermute | solution.py:153
  100.5 1.3 %collective-permute-start.42 = (bf16[1,128,512]{2,1,0:T(8,128)(2,1)S(1)}, bf16[1,128,512]{2,1,0:T(8,128)(2,1)S(1)}, u32[]{:S(2)}, u32[]{:S(2)}) collective-permute-start(bf16[1,128,512]{2,1,0:T(8,128)(2,1)S(1)} %pad_maximum_fusion.5), channel_id=1, source_target_pairs={{0,2},{1,3},{2,0},{3,1},{4,6},{5,7},{6,4},{7,5},{8,10},{9,11},{10,... | collective-permute-start | bytes 393224 | tf_op jit(solution)/shard_map/ppermute | solution.py:153
  101.9 1.6 %collective-permute-done.41.x_ref = bf16[1,128,512]{2,1,0:T(8,128)(2,1)S(1)} collective-permute-done((bf16[1,128,512]{2,1,0:T(8,128)(2,1)S(1)}, bf16[1,128,512]{2,1,0:T(8,128)(2,1)S(1)}, u32[]{:S(2)}, u32[]{:S(2)}) %collective-permute-start.41) | collective-permute-done | bytes 131104 | tf_op jit(solution)/shard_map/ppermute | solution.py:153
  103.4 3.5 %collective-permute-done.40.z2_ref = bf16[128,512]{1,0:T(8,128)(2,1)S(1)} collective-permute-done((bf16[128,512]{1,0:T(8,128)(2,1)S(1)}, bf16[128,512]{1,0:T(8,128)(2,1)S(1)}, u32[]{:S(2)}, u32[]{:S(2)}) %collective-permute-start.40) | collective-permute-done | bytes 131104 | tf_op jit(solution)/shard_map/ppermute | solution.py:153
  (108 shorter events, 30.4 us)
Async XLA Ops:
  0.0 6.7 %collective-permute-start.1 = (bf16[128,512]{1,0:T(8,128)(2,1)}, bf16[128,512]{1,0:T(8,128)(2,1)S(1)}, u32[]{:S(2)}, u32[]{:S(2)}) collective-permute-start(bf16[128,512]{1,0:T(8,128)(2,1)} %refs_0_.1), channel_id=1, source_target_pairs={{0,2},{1,3},{2,0},{3,1},{4,6},{5,7},{6,4},{7,5},{8,10},{9,11},{10,... | collective-permute-start | bytes 393224 | tf_op jit(solution)/shard_map/ppermute | solution.py:153
  3.0 3.7 %collective-permute-start = (bf16[128,512]{1,0:T(8,128)(2,1)}, bf16[128,512]{1,0:T(8,128)(2,1)S(1)}, u32[]{:S(2)}, u32[]{:S(2)}) collective-permute-start(bf16[128,512]{1,0:T(8,128)(2,1)} %refs_0_.1), channel_id=1, source_target_pairs={{0,1},{1,0},{2,3},{3,2},{4,5},{5,4},{6,7},{7,6},{8,9},{9,8},{10,11... | collective-permute-start | bytes 393224 | tf_op jit(solution)/shard_map/ppermute | solution.py:153
  19.9 5.6 %collective-permute-start.4 = (bf16[32,2048]{1,0:T(8,128)(2,1)S(1)}, bf16[32,2048]{1,0:T(8,128)(2,1)S(1)}, u32[]{:S(2)}, u32[]{:S(2)}) collective-permute-start(bf16[32,2048]{1,0:T(8,128)(2,1)S(1)} %fusion.8), channel_id=1, source_target_pairs={{0,2},{1,3},{2,0},{3,1},{4,6},{5,7},{6,4},{7,5},{8,10},{9,11},{10,... | collective-permute-start | bytes 393224 | tf_op jit(solution)/shard_map/ppermute | solution.py:153
  25.7 9.1 %collective-permute-start.6 = (bf16[1,32,2176]{2,1,0:T(8,128)(2,1)S(1)}, bf16[1,32,2176]{2,1,0:T(8,128)(2,1)S(1)}, u32[]{:S(2)}, u32[]{:S(2)}) collective-permute-start(bf16[1,32,2176]{2,1,0:T(8,128)(2,1)S(1)} %bitcast.85), channel_id=1, source_target_pairs={{0,16},{4,20},{8,24},{12,28},{16,0},{20,4},{24,8},{28,12},{1,17},{... | collective-permute-start | bytes 417800 | tf_op jit(solution)/shard_map/ppermute | solution.py:153
  28.6 6.4 %collective-permute-start.5 = (bf16[1,32,2176]{2,1,0:T(8,128)(2,1)S(1)}, bf16[1,32,2176]{2,1,0:T(8,128)(2,1)S(1)}, u32[]{:S(2)}, u32[]{:S(2)}) collective-permute-start(bf16[1,32,2176]{2,1,0:T(8,128)(2,1)S(1)} %bitcast.86), channel_id=1, source_target_pairs={{0,8},{4,12},{8,0},{12,4},{16,24},{20,28},{24,16},{28,20},{1,9},{5... | collective-permute-start | bytes 417800 | tf_op jit(solution)/shard_map/ppermute | solution.py:153
  30.2 5.1 %collective-permute-start.8 = (bf16[1,32,2176]{2,1,0:T(8,128)(2,1)S(1)}, bf16[1,32,2176]{2,1,0:T(8,128)(2,1)S(1)}, u32[]{:S(2)}, u32[]{:S(2)}) collective-permute-start(bf16[1,32,2176]{2,1,0:T(8,128)(2,1)S(1)} %bitcast.87), channel_id=1, source_target_pairs={{0,4},{4,0},{8,12},{12,8},{16,20},{20,16},{24,28},{28,24},{1,5},{5... | collective-permute-start | bytes 417800 | tf_op jit(solution)/shard_map/ppermute | solution.py:153
  31.7 5.1 %collective-permute-start.7 = (bf16[1,32,2176]{2,1,0:T(8,128)(2,1)S(1)}, bf16[1,32,2176]{2,1,0:T(8,128)(2,1)S(1)}, u32[]{:S(2)}, u32[]{:S(2)}) collective-permute-start(bf16[1,32,2176]{2,1,0:T(8,128)(2,1)S(1)} %bitcast.88), channel_id=1, source_target_pairs={{0,2},{1,3},{2,0},{3,1},{4,6},{5,7},{6,4},{7,5},{8,10},{9,11},{10,... | collective-permute-start | bytes 417800 | tf_op jit(solution)/shard_map/ppermute | solution.py:153
  36.7 5.1 %collective-permute-start.9 = (bf16[1,32,2176]{2,1,0:T(8,128)(2,1)S(1)}, bf16[1,32,2176]{2,1,0:T(8,128)(2,1)S(1)}, u32[]{:S(2)}, u32[]{:S(2)}) collective-permute-start(bf16[1,32,2176]{2,1,0:T(8,128)(2,1)S(1)} %collective-permute-done.6), channel_id=1, source_target_pairs={{0,8},{4,12},{8,0},{12,4},{16,24},{20,28},{24,16},{28,20},{1,9},{5... | collective-permute-start | bytes 417800 | tf_op jit(solution)/shard_map/ppermute | solution.py:153
  37.2 4.7 %collective-permute-start.12 = (bf16[1,32,2176]{2,1,0:T(8,128)(2,1)S(1)}, bf16[1,32,2176]{2,1,0:T(8,128)(2,1)S(1)}, u32[]{:S(2)}, u32[]{:S(2)}) collective-permute-start(bf16[1,32,2176]{2,1,0:T(8,128)(2,1)S(1)} %bitcast.89), channel_id=1, source_target_pairs={{0,1},{1,0},{2,3},{3,2},{4,5},{5,4},{6,7},{7,6},{8,9},{9,8},{10,11... | collective-permute-start | bytes 417800 | tf_op jit(solution)/shard_map/ppermute | solution.py:153
  37.2 5.7 %collective-permute-start.13 = (bf16[1,32,2176]{2,1,0:T(8,128)(2,1)S(1)}, bf16[1,32,2176]{2,1,0:T(8,128)(2,1)S(1)}, u32[]{:S(2)}, u32[]{:S(2)}) collective-permute-start(bf16[1,32,2176]{2,1,0:T(8,128)(2,1)S(1)} %collective-permute-done.7.refs_2_), channel_id=1, source_target_pairs={{0,1},{1,0},{2,3},{3,2},{4,5},{5,4},{6,7},{7,6},{8,9},{9,8},{10,11... | collective-permute-start | bytes 417800 | tf_op jit(solution)/shard_map/ppermute | solution.py:153
  37.7 4.3 %collective-permute-start.11 = (bf16[1,16,2176]{2,1,0:T(8,128)(2,1)S(1)}, bf16[1,16,2176]{2,1,0:T(8,128)(2,1)S(1)}, u32[]{:S(2)}, u32[]{:S(2)}) collective-permute-start(bf16[1,16,2176]{2,1,0:T(8,128)(2,1)S(1)} %slice.108), channel_id=1, source_target_pairs={{0,4},{4,0},{8,12},{12,8},{16,20},{20,16},{24,28},{28,24},{1,5},{5... | collective-permute-start | bytes 208904 | tf_op jit(solution)/shard_map/ppermute | solution.py:153
  38.6 4.3 %collective-permute-start.10 = (bf16[1,16,2176]{2,1,0:T(8,128)(2,1)S(1)}, bf16[1,16,2176]{2,1,0:T(8,128)(2,1)S(1)}, u32[]{:S(2)}, u32[]{:S(2)}) collective-permute-start(bf16[1,16,2176]{2,1,0:T(8,128)(2,1)S(1)} %slice.107), channel_id=1, source_target_pairs={{0,2},{1,3},{2,0},{3,1},{4,6},{5,7},{6,4},{7,5},{8,10},{9,11},{10,... | collective-permute-start | bytes 208904 | tf_op jit(solution)/shard_map/ppermute | solution.py:153
  42.9 10.5 %collective-permute-start.19 = (bf16[3,32,2176]{2,1,0:T(8,128)(2,1)S(1)}, bf16[3,32,2176]{2,1,0:T(8,128)(2,1)S(1)}, u32[]{:S(2)}, u32[]{:S(2)}) collective-permute-start(bf16[3,32,2176]{2,1,0:T(8,128)(2,1)S(1)} %pad_maximum_fusion.refs_0_), channel_id=1, source_target_pairs={{0,4},{4,0},{8,12},{12,8},{16,20},{20,16},{24,28},{28,24},{1,5},{5... | collective-permute-start | bytes 1253384 | tf_op jit(solution)/shard_map/ppermute | solution.py:153
  44.0 10.2 %collective-permute-start.18 = (bf16[3,32,2176]{2,1,0:T(8,128)(2,1)S(1)}, bf16[3,32,2176]{2,1,0:T(8,128)(2,1)S(1)}, u32[]{:S(2)}, u32[]{:S(2)}) collective-permute-start(bf16[3,32,2176]{2,1,0:T(8,128)(2,1)S(1)} %pad_maximum_fusion.refs_0_), channel_id=1, source_target_pairs={{0,2},{1,3},{2,0},{3,1},{4,6},{5,7},{6,4},{7,5},{8,10},{9,11},{10,... | collective-permute-start | bytes 1253384 | tf_op jit(solution)/shard_map/ppermute | solution.py:153
  45.5 8.7 %collective-permute-start.17 = (bf16[3,32,2176]{2,1,0:T(8,128)(2,1)S(1)}, bf16[3,32,2176]{2,1,0:T(8,128)(2,1)S(1)}, u32[]{:S(2)}, u32[]{:S(2)}) collective-permute-start(bf16[3,32,2176]{2,1,0:T(8,128)(2,1)S(1)} %pad_maximum_fusion.refs_0_), channel_id=1, source_target_pairs={{0,1},{1,0},{2,3},{3,2},{4,5},{5,4},{6,7},{7,6},{8,9},{9,8},{10,11... | collective-permute-start | bytes 1253384 | tf_op jit(solution)/shard_map/ppermute | solution.py:153
  54.3 8.9 %collective-permute-start.21 = (bf16[3,32,2176]{2,1,0:T(8,128)(2,1)S(1)}, bf16[3,32,2176]{2,1,0:T(8,128)(2,1)S(1)}, u32[]{:S(2)}, u32[]{:S(2)}) collective-permute-start(bf16[3,32,2176]{2,1,0:T(8,128)(2,1)S(1)} %collective-permute-done.19.refs_0_), channel_id=1, source_target_pairs={{0,1},{1,0},{2,3},{3,2},{4,5},{5,4},{6,7},{7,6},{8,9},{9,8},{10,11... | collective-permute-start | bytes 1253384 | tf_op jit(solution)/shard_map/ppermute | solution.py:153
  54.8 7.1 %collective-permute-start.22 = (bf16[3,16,2176]{2,1,0:T(8,128)(2,1)S(1)}, bf16[3,16,2176]{2,1,0:T(8,128)(2,1)S(1)}, u32[]{:S(2)}, u32[]{:S(2)}) collective-permute-start(bf16[3,16,2176]{2,1,0:T(8,128)(2,1)S(1)} %slice.109), channel_id=1, source_target_pairs={{0,2},{1,3},{2,0},{3,1},{4,6},{5,7},{6,4},{7,5},{8,10},{9,11},{10,... | collective-permute-start | bytes 626696 | tf_op jit(solution)/shard_map/ppermute | solution.py:153
  56.4 6.8 %collective-permute-start.23 = (bf16[3,16,2176]{2,1,0:T(8,128)(2,1)S(1)}, bf16[3,16,2176]{2,1,0:T(8,128)(2,1)S(1)}, u32[]{:S(2)}, u32[]{:S(2)}) collective-permute-start(bf16[3,16,2176]{2,1,0:T(8,128)(2,1)S(1)} %slice.110), channel_id=1, source_target_pairs={{0,4},{4,0},{8,12},{12,8},{16,20},{20,16},{24,28},{28,24},{1,5},{5... | collective-permute-start | bytes 626696 | tf_op jit(solution)/shard_map/ppermute | solution.py:153
  69.6 7.1 %collective-permute-start.33 = (bf16[3,64,512]{2,1,0:T(8,128)(2,1)S(1)}, bf16[3,64,512]{2,1,0:T(8,128)(2,1)S(1)}, u32[]{:S(2)}, u32[]{:S(2)}) collective-permute-start(bf16[3,64,512]{2,1,0:T(8,128)(2,1)S(1)} %get-tuple-element.185), channel_id=1, source_target_pairs={{0,2},{1,3},{2,0},{3,1},{4,6},{5,7},{6,4},{7,5},{8,10},{9,11},{10,... | collective-permute-start | bytes 589832 | tf_op jit(solution)/shard_map/ppermute | solution.py:153
  70.2 6.7 %collective-permute-start.32 = (bf16[3,64,512]{2,1,0:T(8,128)(2,1)S(1)}, bf16[3,64,512]{2,1,0:T(8,128)(2,1)S(1)}, u32[]{:S(2)}, u32[]{:S(2)}) collective-permute-start(bf16[3,64,512]{2,1,0:T(8,128)(2,1)S(1)} %get-tuple-element.186), channel_id=1, source_target_pairs={{0,4},{4,0},{8,12},{12,8},{16,20},{20,16},{24,28},{28,24},{1,5},{5... | collective-permute-start | bytes 589832 | tf_op jit(solution)/shard_map/ppermute | solution.py:153
  71.1 7.5 %collective-permute-start.27 = (bf16[1,3,128,512]{3,2,1,0:T(8,128)(2,1)S(1)}, bf16[1,3,128,512]{3,2,1,0:T(8,128)(2,1)S(1)}, u32[]{:S(2)}, u32[]{:S(2)}) collective-permute-start(bf16[1,3,128,512]{3,2,1,0:T(8,128)(2,1)S(1)} %get-tuple-element.149), channel_id=1, source_target_pairs={{0,1},{1,0},{2,3},{3,2},{4,5},{5,4},{6,7},{7,6},{8,9},{9,8},{10,11... | collective-permute-start | bytes 1179656 | tf_op jit(solution)/shard_map/ppermute | solution.py:153
  71.1 7.5 %collective-permute-start.28 = (bf16[1,3,128,512]{3,2,1,0:T(8,128)(2,1)S(1)}, bf16[1,3,128,512]{3,2,1,0:T(8,128)(2,1)S(1)}, u32[]{:S(2)}, u32[]{:S(2)}) collective-permute-start(bf16[1,3,128,512]{3,2,1,0:T(8,128)(2,1)S(1)} %get-tuple-element.150), channel_id=1, source_target_pairs={{0,1},{1,0},{2,3},{3,2},{4,5},{5,4},{6,7},{7,6},{8,9},{9,8},{10,11... | collective-permute-start | bytes 1179656 | tf_op jit(solution)/shard_map/ppermute | solution.py:153
  71.7 7.0 %collective-permute-start.31 = (bf16[1,3,128,512]{3,2,1,0:T(8,128)(2,1)S(1)}, bf16[1,3,128,512]{3,2,1,0:T(8,128)(2,1)S(1)}, u32[]{:S(2)}, u32[]{:S(2)}) collective-permute-start(bf16[1,3,128,512]{3,2,1,0:T(8,128)(2,1)S(1)} %get-tuple-element.155), channel_id=1, source_target_pairs={{0,1},{1,0},{2,3},{3,2},{4,5},{5,4},{6,7},{7,6},{8,9},{9,8},{10,11... | collective-permute-start | bytes 1179656 | tf_op jit(solution)/shard_map/ppermute | solution.py:153
  78.9 11.2 %collective-permute-start.34 = (bf16[3,128,512]{2,1,0:T(8,128)(2,1)S(1)}, bf16[3,128,512]{2,1,0:T(8,128)(2,1)S(1)}, u32[]{:S(2)}, u32[]{:S(2)}) collective-permute-start(bf16[3,128,512]{2,1,0:T(8,128)(2,1)S(1)} %pad_maximum_fusion.1), channel_id=1, source_target_pairs={{0,4},{4,0},{8,12},{12,8},{16,20},{20,16},{24,28},{28,24},{1,5},{5... | collective-permute-start | bytes 1179656 | tf_op jit(solution)/shard_map/ppermute | solution.py:153
  80.1 10.9 %collective-permute-start.35 = (bf16[3,128,512]{2,1,0:T(8,128)(2,1)S(1)}, bf16[3,128,512]{2,1,0:T(8,128)(2,1)S(1)}, u32[]{:S(2)}, u32[]{:S(2)}) collective-permute-start(bf16[3,128,512]{2,1,0:T(8,128)(2,1)S(1)} %pad_maximum_fusion.2), channel_id=1, source_target_pairs={{0,2},{1,3},{2,0},{3,1},{4,6},{5,7},{6,4},{7,5},{8,10},{9,11},{10,... | collective-permute-start | bytes 1179656 | tf_op jit(solution)/shard_map/ppermute | solution.py:153
  91.3 7.0 %collective-permute-start.37 = (bf16[128,512]{1,0:T(8,128)(2,1)S(1)}, bf16[128,512]{1,0:T(8,128)(2,1)S(1)}, u32[]{:S(2)}, u32[]{:S(2)}) collective-permute-start(bf16[128,512]{1,0:T(8,128)(2,1)S(1)} %get-tuple-element.183), channel_id=1, source_target_pairs={{0,8},{4,12},{8,0},{12,4},{16,24},{20,28},{24,16},{28,20},{1,9},{5... | collective-permute-start | bytes 393224 | tf_op jit(solution)/shard_map/ppermute | solution.py:153
  92.6 4.3 %collective-permute-start.39 = (bf16[1,64,512]{2,1,0:T(8,128)(2,1)S(1)}, bf16[1,64,512]{2,1,0:T(8,128)(2,1)S(1)}, u32[]{:S(2)}, u32[]{:S(2)}) collective-permute-start(bf16[1,64,512]{2,1,0:T(8,128)(2,1)S(1)} %get-tuple-element.187), channel_id=1, source_target_pairs={{0,2},{1,3},{2,0},{3,1},{4,6},{5,7},{6,4},{7,5},{8,10},{9,11},{10,... | collective-permute-start | bytes 196616 | tf_op jit(solution)/shard_map/ppermute | solution.py:153
  94.0 4.3 %collective-permute-start.38 = (bf16[1,64,512]{2,1,0:T(8,128)(2,1)S(1)}, bf16[1,64,512]{2,1,0:T(8,128)(2,1)S(1)}, u32[]{:S(2)}, u32[]{:S(2)}) collective-permute-start(bf16[1,64,512]{2,1,0:T(8,128)(2,1)S(1)} %get-tuple-element.188), channel_id=1, source_target_pairs={{0,4},{4,0},{8,12},{12,8},{16,20},{20,16},{24,28},{28,24},{1,5},{5... | collective-permute-start | bytes 196616 | tf_op jit(solution)/shard_map/ppermute | solution.py:153
  95.3 6.6 %collective-permute-start.36 = (bf16[128,512]{1,0:T(8,128)(2,1)S(1)}, bf16[128,512]{1,0:T(8,128)(2,1)S(1)}, u32[]{:S(2)}, u32[]{:S(2)}) collective-permute-start(bf16[128,512]{1,0:T(8,128)(2,1)S(1)} %get-tuple-element.184), channel_id=1, source_target_pairs={{0,8},{4,12},{8,0},{12,4},{16,24},{20,28},{24,16},{28,20},{1,9},{5... | collective-permute-start | bytes 393224 | tf_op jit(solution)/shard_map/ppermute | solution.py:153
  98.4 5.0 %collective-permute-start.41 = (bf16[1,128,512]{2,1,0:T(8,128)(2,1)S(1)}, bf16[1,128,512]{2,1,0:T(8,128)(2,1)S(1)}, u32[]{:S(2)}, u32[]{:S(2)}) collective-permute-start(bf16[1,128,512]{2,1,0:T(8,128)(2,1)S(1)} %pad_maximum_fusion.4), channel_id=1, source_target_pairs={{0,4},{4,0},{8,12},{12,8},{16,20},{20,16},{24,28},{28,24},{1,5},{5... | collective-permute-start | bytes 393224 | tf_op jit(solution)/shard_map/ppermute | solution.py:153
  99.7 7.3 %collective-permute-start.40 = (bf16[128,512]{1,0:T(8,128)(2,1)S(1)}, bf16[128,512]{1,0:T(8,128)(2,1)S(1)}, u32[]{:S(2)}, u32[]{:S(2)}) collective-permute-start(bf16[128,512]{1,0:T(8,128)(2,1)S(1)} %fusion.6), channel_id=1, source_target_pairs={{0,16},{4,20},{8,24},{12,28},{16,0},{20,4},{24,8},{28,12},{1,17},{... | collective-permute-start | bytes 393224 | tf_op jit(solution)/shard_map/ppermute | solution.py:153
  100.5 6.4 %collective-permute-start.42 = (bf16[1,128,512]{2,1,0:T(8,128)(2,1)S(1)}, bf16[1,128,512]{2,1,0:T(8,128)(2,1)S(1)}, u32[]{:S(2)}, u32[]{:S(2)}) collective-permute-start(bf16[1,128,512]{2,1,0:T(8,128)(2,1)S(1)} %pad_maximum_fusion.5), channel_id=1, source_target_pairs={{0,2},{1,3},{2,0},{3,1},{4,6},{5,7},{6,4},{7,5},{8,10},{9,11},{10,... | collective-permute-start | bytes 393224 | tf_op jit(solution)/shard_map/ppermute | solution.py:153
  (20 other events, 173.2 us)

commit v12 on v11

--- a/solution.py
+++ b/solution.py
@@ -153,9 +153,22 @@
     return lax.ppermute(value, axis, [(i, i ^ bits) for i in range(lax.axis_size(axis))])
 
 
-def layout_kernel(
-    length_ref, table_ref, frequency_ref, cosine_ref, sine_ref, owner_ref, list_ref, owners
-):
+def stage_kernel(*refs):
+    length_hbm, table_hbm, frequency_hbm, *large = refs[:12]
+    cosine_ref, sine_ref, owner_ref, *staged = refs[12:24]
+    list_ref, length_out, table_out = refs[24:27]
+    frequency_ref, owners, sems = refs[27:]
+    length_ref, table_ref = length_out, table_out
+    sources = (length_hbm, table_hbm, frequency_hbm, *large)
+    targets = (length_out, table_out, frequency_ref, *staged)
+    copies = [
+        pltpu.make_async_copy(source, target, sems.at[i])
+        for i, (source, target) in enumerate(zip(sources, targets))
+    ]
+    for copy in copies:
+        copy.start()
+    for copy in copies[:3]:
+        copy.wait()
     tokens, head_dim = cosine_ref.shape
     for entry in range(POOL):
         list_ref[entry] = 0
@@ -188,24 +201,18 @@
     sine = jnp.sin(angle)
     cosine_ref[...] = jnp.cos(angle)
     sine_ref[...] = jnp.where(lane < head_dim // 2, -sine, sine)
+    for copy in copies[3:]:
+        copy.wait()
 
 
 def attention_kernel(*refs):
-    pieces, hbm_refs, (keep_out, far_out, core_out) = refs[:4], refs[4:19], refs[19:22]
-    local_refs = refs[22:37]
-    (length_ref, table_ref, list_ref, gain_ref, q_gain_ref, k_gain_ref) = local_refs[:6]
-    (cosine_ref, sine_ref, owner_ref, q_ref, k_ref, v_ref, key_ref, value_ref, o_ref) = local_refs[6:]
+    pieces, (keep_out, far_out, core_out) = refs[:4], refs[19:22]
+    (cosine_ref, sine_ref, owner_ref, gain_ref, q_gain_ref, k_gain_ref) = refs[4:10]
+    (q_ref, k_ref, v_ref, key_ref, value_ref, o_ref, list_ref, length_ref, table_ref) = refs[10:19]
     (
         x_ref, query_ref, own_scores, scores_ref, mix_ref, mixed_ref, part_ref, slots_ref, decoded_ref,
-        sems,
-    ) = refs[37:]
+    ) = refs[22:]
     tokens, head_dim = x_ref.shape[0], k_gain_ref.shape[1]
-    copies = [
-        pltpu.make_async_copy(source, target, sems.at[i])
-        for i, (source, target) in enumerate(zip(hbm_refs, local_refs))
-    ]
-    for copy in copies:
-        copy.start()
     tp_index = lax.axis_index("tp")
     heads = q_ref.shape[1] // head_dim
     decodes = tokens - PRE
@@ -213,8 +220,6 @@
         width = piece.shape[1]
         start = pl.multiple_of((tp_index ^ step) * width, width)
         x_ref[:, pl.ds(start, width)] = piece[...]
-    for copy in copies[:9]:
-        copy.wait()
     token = lax.broadcasted_iota(jnp.int32, (tokens, head_dim), 0)
     lane = lax.broadcasted_iota(jnp.int32, (tokens, head_dim), 1)
 
@@ -227,8 +232,6 @@
 
     normed = rms_scale(x_ref[...].astype(jnp.float32), gain_ref[...]).astype(jnp.bfloat16)
     contract = (((1,), (1,)), ((), ()))
-    for copy in copies[9:12]:
-        copy.wait()
     key_lin = jnp.dot(normed, k_ref[...], preferred_element_type=jnp.float32)
     values_new = jnp.dot(normed, v_ref[...], preferred_element_type=jnp.float32).astype(jnp.bfloat16)
     query_lin = jnp.dot(normed, q_ref[...], preferred_element_type=jnp.float32)
@@ -249,8 +252,6 @@
         decode_own.append(scores[PRE:])
     decode_query = jnp.concatenate(decode_query, axis=0).astype(jnp.bfloat16)
     decode_own = jnp.concatenate(decode_own, axis=0)
-    for copy in copies[12:14]:
-        copy.wait()
 
     def raised(top, scores):
         for start in range(0, scores.shape[1], head_dim):
@@ -335,7 +336,6 @@
         columns = slice(head * head_dim, (head + 1) * head_dim)
         mixed_ref[:, columns] = part[:, :head_dim] / part[:, head_dim:]
         mixed_ref[PRE:, columns] = decoded_ref[head * decodes : (head + 1) * decodes]
-    copies[14].wait()
     part_ref[...] = jnp.dot(
         mixed_ref[...].astype(jnp.bfloat16), o_ref[...], preferred_element_type=jnp.float32
     )
@@ -360,31 +360,34 @@
     decode_rows = rows // tokens * (tokens - PRE)
     half = ROPE_BASE ** (-np.arange(head_dim // 2) / (head_dim // 2))
     frequency = jnp.asarray(np.concatenate([half, half])[None, :], jnp.float32)
-    params = pltpu.CompilerParams(vmem_limit_bytes=56 * 1024 * 1024)
-    rope = jax.ShapeDtypeStruct((tokens, head_dim), jnp.float32)
-    cosine, sine, owner, page_list = pl.pallas_call(
-        layout_kernel,
-        out_shape=[
-            rope,
-            rope,
-            jax.ShapeDtypeStruct((1, POOL * PAGE), jnp.int32),
-            jax.ShapeDtypeStruct((POOL,), jnp.int32),
+    large = (
+        norm_in_gain[None, :], q_gain[None, :], k_gain[None, :], q_weight, k_weight, v_weight,
+        key_pages[0], value_pages[0], o_weight,
+    )
+    scalars = (cache_len, page_table)
+    sources = [
+        pltpu.with_memory_space_constraint(array, pltpu.HBM)
+        for array in (*scalars, frequency, *large)
+    ]
+    rope = pltpu.VMEM((tokens, head_dim), jnp.float32)
+    *staged, page_list, lengths, table = pl.pallas_call(
+        stage_kernel,
+        out_shape=[rope, rope, pltpu.VMEM((1, POOL * PAGE), jnp.int32)]
+        + [pltpu.VMEM(array.shape, array.dtype) for array in large]
+        + [jax.ShapeDtypeStruct((POOL,), jnp.int32)]
+        + [jax.ShapeDtypeStruct(array.shape, array.dtype) for array in scalars],
+        in_specs=[pl.BlockSpec(memory_space=pltpu.HBM)] * 12,
+        out_specs=[VMEM] * 12 + [SMEM] * 3,
+        scratch_shapes=[
+            pltpu.VMEM(frequency.shape, frequency.dtype),
+            pltpu.SMEM((2, POOL), jnp.int32),
+            pltpu.SemaphoreType.DMA((12,)),
         ],
-        in_specs=[SMEM, SMEM, VMEM],
-        out_specs=[VMEM, VMEM, VMEM, SMEM],
-        scratch_shapes=[pltpu.SMEM((2, POOL), jnp.int32)],
-        compiler_params=params,
-        name="layout",
-    )(cache_len, page_table, frequency)
-    far, cosine, sine, owner, page_list = ordered(
-        flip(hidden_in, "tp", 2), cosine, sine, owner, page_list
-    )
+        compiler_params=pltpu.CompilerParams(vmem_limit_bytes=4 * 1024 * 1024),
+        name="stage",
+    )(*sources)
+    far, *staged = ordered(flip(hidden_in, "tp", 2), *staged, page_list, lengths, table)
     pieces = (hidden_in, flip(hidden_in, "tp", 1), far, flip(far, "tp", 1))
-    scalars = (cache_len, page_table, page_list)
-    arrays = (
-        norm_in_gain[None, :], q_gain[None, :], k_gain[None, :], cosine, sine, owner,
-        q_weight, k_weight, v_weight, key_pages[0], value_pages[0], o_weight,
-    )
     share = (tokens // 4, width)
     score_pages, list_pages = 4, 8
     return pl.pallas_call(
@@ -394,11 +397,9 @@
             jax.ShapeDtypeStruct(share, jnp.float32),
             jax.ShapeDtypeStruct((2, *share), jnp.bfloat16),
         ],
-        in_specs=[VMEM] * 4 + [pl.BlockSpec(memory_space=pltpu.HBM)] * 15,
+        in_specs=[VMEM] * 16 + [SMEM] * 3,
         out_specs=[VMEM] * 3,
-        scratch_shapes=[pltpu.SMEM(array.shape, array.dtype) for array in scalars]
-        + [pltpu.VMEM(array.shape, array.dtype) for array in arrays]
-        + [
+        scratch_shapes=[
             pltpu.VMEM((tokens, width), jnp.bfloat16),
             pltpu.VMEM((rows, head_dim), jnp.bfloat16),
             pltpu.VMEM((rows, tokens), jnp.float32),
@@ -408,11 +409,10 @@
             pltpu.VMEM((tokens, width), jnp.float32),
             pltpu.VMEM((POOL // list_pages, decode_rows, list_pages * PAGE), jnp.float32),
             pltpu.VMEM((decode_rows, head_dim), jnp.float32),
-            pltpu.SemaphoreType.DMA((15,)),
         ],
-        compiler_params=params,
+        compiler_params=pltpu.CompilerParams(vmem_limit_bytes=24 * 1024 * 1024),
         name="attention",
-    )(*pieces, *scalars, *arrays)
+    )(*pieces, *staged)
 
 
 def pack_kernel(
@@ -624,10 +624,15 @@
     keep, (send, first) = side_3
     all_0, near_3, keep, send, first = ordered(all_0, near_3, keep, send, flip(first, "tp", 1))
     relay_3 = relayed(joined((keep, (send, first)), 0, 1))
-    near_3, all_0, side_3, relay_3 = ordered(
-        with_core(near_3), with_core(all_0), (keep, [flip(send, "tp", 1), first]), relay_3
-    )
-    sums_3 = ordered(*neighbours(joined(side_3, 0, 0), joined(near_3, 0, 1), *relay_3))
+    near_keep, (near_send, near_first) = near_3
+    all_0, near_send, near_first, send, relay_3 = ordered(
+        all_0, near_send, flip(near_first, "tp", 1), flip(send, "tp", 1), relay_3
+    )
+    sums_3 = neighbours(
+        joined((keep, (send, first)), 0, 0), joined((near_keep, (near_send, near_first)), 0, 1), *relay_3
+    )
+    all_0, near_send, sums_3 = ordered(with_core(all_0), flip(near_send, "tp", 1), sums_3)
+    near_3 = (near_keep, (near_send, near_first))
     sent = joined(near_3, 0, 0) + sums_3[0].astype(jnp.float32) + sums_3[1].astype(jnp.float32)
     sent_3, relay_0 = ordered(
         flip(sent[2].astype(jnp.bfloat16), "req", 2), relayed(joined(all_0, 1, 1))

time: 108 us -> 102 us (0.944)
  starting transfers between devices: 35.8 us -> 31.5 us
  other arithmetic: 3.17 us -> 1.12 us
  waiting for transfers between devices: 48.6 us -> 50.4 us
  Pallas kernels: 19 us -> 17.6 us
    ppermute x43, starting transfers between devices: 35.8 us -> 31.5 us  [flip(): lax.ppermute(value, axis, [(i, i ^ bits) for i in range(lax.axis_size(axi...]
    pallas_call x1, Pallas kernels: 8.22 us -> 4.88 us  [attention_shares(): pl.pallas_call(attention_kernel, out_shape=[jax.ShapeDtypeStruct(share, j...]
    pallas_call x1, Pallas kernels: 2.39 us -> 4.41 us  [attention_shares(): pl.pallas_call(stage_kernel, out_shape=[rope, rope, pltpu.VMEM((1, POOL *...]
    ppermute x43, waiting for transfers between devices: 48.6 us -> 50.4 us  [flip(): lax.ppermute(value, axis, [(i, i ^ bits) for i in range(lax.axis_size(axi...]
    convert_element_type x1, other arithmetic: 1.14 us -> 0.04 us  [moe_dense(): (far + core[1].astype(jnp.float32)).astype(jnp.bfloat16)]
  transfers between devices with their start and end apart: 43 -> 43, of which waited for: 30 -> 28; matrix products, arithmetic and copies ran while one was open for 1% -> 1% of each run, Pallas kernels for 7% -> 9%
where the time goes in v12:
time: 102 us; the launch traced here: 101 us
  waiting for transfers between devices  50.4 us (49%)
  starting transfers between devices  31.5 us (31%)
  Pallas kernels  17.6 us (17%)
  other arithmetic  1.12 us (1%)
    ppermute x43, waiting for transfers between devices, flip(): lax.ppermute(value, axis, [(i, i ^ bits) for i in range(lax.axis_size(axi...  50.4 us
    ppermute x43, starting transfers between devices, flip(): lax.ppermute(value, axis, [(i, i ^ bits) for i in range(lax.axis_size(axi...  31.5 us
    pallas_call x3, Pallas kernels, run_experts(): pl.pallas_call(functools.partial(experts_kernel, plan, len(residual)), ou...  7.44 us
    pallas_call x1, Pallas kernels, attention_shares(): pl.pallas_call(attention_kernel, out_shape=[jax.ShapeDtypeStruct(share, j...  4.88 us
    pallas_call x1, Pallas kernels, attention_shares(): pl.pallas_call(stage_kernel, out_shape=[rope, rope, pltpu.VMEM((1, POOL *...  4.41 us
  transfers between devices with their start and end apart: 43, of which 28 were waited for; matrix products, arithmetic and copies ran while one was open for 1% of the time, Pallas kernels for 9%

profile of v12, /device:TPU:0, one launch (start us, length us, event | category | flops | bytes accessed | tf_op | source)
XLA Modules:
  0.0 101.1 jit_solution(3407146825856749474)
XLA Ops:
  0.0 3.0 %collective-permute-start.1 = (bf16[128,512]{1,0:T(8,128)(2,1)}, bf16[128,512]{1,0:T(8,128)(2,1)S(1)}, u32[]{:S(2)}, u32[]{:S(2)}) collective-permute-start(bf16[128,512]{1,0:T(8,128)(2,1)} %refs_0_.3), channel_id=1, source_target_pairs={{0,2},{1,3},{2,0},{3,1},{4,6},{5,7},{6,4},{7,5},{8,10},{9,11},{10,... | collective-permute-start | bytes 393224 | tf_op jit(solution)/shard_map/ppermute | solution.py:153
  3.0 4.4 %stage.1 = (f32[128,128]{1,0:T(8,128)S(1)}, f32[128,128]{1,0:T(8,128)S(1)}, s32[1,6144]{1,0:T(1,128)S(1)}, f32[1,2048]{1,0:T(1,128)S(1)}, f32[1,128]{1,0:T(1,128...) custom-call(s32[9]{0:T(128)} %refs_0_.2, ...), custom_call_target="tpu_custom_call" | custom-call | tf_op jit(solution)/shard_map/stage/pallas_call | solution.py:373
  9.0 4.9 %attention.1 = (f32[32,2048]{1,0:T(8,128)S(1)}, f32[32,2048]{1,0:T(8,128)S(1)}, bf16[2,32,2048]{2,1,0:T(8,128)(2,1)S(1)}) custom-call(bf16[128,512]{1,0:T(8,128)(2,1)S(1)} %copy-done.3, bf16[128,512]{1,0:T(8,128)(2,1)S(1)} %collective-permute-done.refs_1_, bf16[128,512]{1,0:T(8,128)(2,1)S(1)} %collective-permute-done.1.refs_2_, ...), custom_call_target="tpu_custom_call" | custom-call | tf_op jit(solution)/shard_map/attention/pallas_call | solution.py:393
  14.3 1.2 %collective-permute-done.3 = bf16[2,32,2048]{2,1,0:T(8,128)(2,1)S(1)} collective-permute-done((bf16[2,32,2048]{2,1,0:T(8,128)(2,1)S(1)}, bf16[2,32,2048]{2,1,0:T(8,128)(2,1)S(1)}, u32[]{:S(2)}, u32[]{:S(2)}) %collective-permute-start.3) | collective-permute-done | bytes 262176 | tf_op jit(solution)/shard_map/ppermute | solution.py:153
  16.4 4.9 %collective-permute-done.4.far_ref = bf16[32,2048]{1,0:T(8,128)(2,1)S(1)} collective-permute-done((bf16[32,2048]{1,0:T(8,128)(2,1)S(1)}, bf16[32,2048]{1,0:T(8,128)(2,1)S(1)}, u32[]{:S(2)}, u32[]{:S(2)}) %collective-permute-start.4) | collective-permute-done | bytes 131104 | tf_op jit(solution)/shard_map/ppermute | solution.py:153
  21.6 2.7 %collective-permute-start.6 = (bf16[1,32,2176]{2,1,0:T(8,128)(2,1)S(1)}, bf16[1,32,2176]{2,1,0:T(8,128)(2,1)S(1)}, u32[]{:S(2)}, u32[]{:S(2)}) collective-permute-start(bf16[1,32,2176]{2,1,0:T(8,128)(2,1)S(1)} %bitcast.85), channel_id=1, source_target_pairs={{0,16},{4,20},{8,24},{12,28},{16,0},{20,4},{24,8},{28,12},{1,17},{... | collective-permute-start | bytes 417800 | tf_op jit(solution)/shard_map/ppermute | solution.py:153
  24.2 1.6 %collective-permute-start.5 = (bf16[1,32,2176]{2,1,0:T(8,128)(2,1)S(1)}, bf16[1,32,2176]{2,1,0:T(8,128)(2,1)S(1)}, u32[]{:S(2)}, u32[]{:S(2)}) collective-permute-start(bf16[1,32,2176]{2,1,0:T(8,128)(2,1)S(1)} %bitcast.86), channel_id=1, source_target_pairs={{0,8},{4,12},{8,0},{12,4},{16,24},{20,28},{24,16},{28,20},{1,9},{5... | collective-permute-start | bytes 417800 | tf_op jit(solution)/shard_map/ppermute | solution.py:153
  25.8 1.5 %collective-permute-start.8 = (bf16[1,32,2176]{2,1,0:T(8,128)(2,1)S(1)}, bf16[1,32,2176]{2,1,0:T(8,128)(2,1)S(1)}, u32[]{:S(2)}, u32[]{:S(2)}) collective-permute-start(bf16[1,32,2176]{2,1,0:T(8,128)(2,1)S(1)} %bitcast.87), channel_id=1, source_target_pairs={{0,4},{4,0},{8,12},{12,8},{16,20},{20,16},{24,28},{28,24},{1,5},{5... | collective-permute-start | bytes 417800 | tf_op jit(solution)/shard_map/ppermute | solution.py:153
  27.9 2.9 %collective-permute-done.6 = bf16[1,32,2176]{2,1,0:T(8,128)(2,1)S(1)} collective-permute-done((bf16[1,32,2176]{2,1,0:T(8,128)(2,1)S(1)}, bf16[1,32,2176]{2,1,0:T(8,128)(2,1)S(1)}, u32[]{:S(2)}, u32[]{:S(2)}) %collective-permute-start.6) | collective-permute-done | bytes 139296 | tf_op jit(solution)/shard_map/ppermute | solution.py:153
  31.0 1.3 %collective-permute-done.7.refs_2_ = bf16[1,32,2176]{2,1,0:T(8,128)(2,1)S(1)} collective-permute-done((bf16[1,32,2176]{2,1,0:T(8,128)(2,1)S(1)}, bf16[1,32,2176]{2,1,0:T(8,128)(2,1)S(1)}, u32[]{:S(2)}, u32[]{:S(2)}) %collective-permute-start.7) | collective-permute-done | bytes 139296 | tf_op jit(solution)/shard_map/ppermute | solution.py:153
  34.8 2.6 %collective-permute-done.9 = bf16[1,32,2176]{2,1,0:T(8,128)(2,1)S(1)} collective-permute-done((bf16[1,32,2176]{2,1,0:T(8,128)(2,1)S(1)}, bf16[1,32,2176]{2,1,0:T(8,128)(2,1)S(1)}, u32[]{:S(2)}, u32[]{:S(2)}) %collective-permute-start.9) | collective-permute-done | bytes 139296 | tf_op jit(solution)/shard_map/ppermute | solution.py:153
  40.7 1.4 %collective-permute-done.14.refs_5_ = bf16[1,32,2176]{2,1,0:T(8,128)(2,1)S(1)} collective-permute-done((bf16[1,32,2176]{2,1,0:T(8,128)(2,1)S(1)}, bf16[1,32,2176]{2,1,0:T(8,128)(2,1)S(1)}, u32[]{:S(2)}, u32[]{:S(2)}) %collective-permute-start.14) | collective-permute-done | bytes 139296 | tf_op jit(solution)/shard_map/ppermute | solution.py:153
  43.5 2.0 %experts.3 = (f32[2,2,1,128,512]{4,3,2,1,0:T(8,128)S(1)}, bf16[2,1,128,512]{3,2,1,0:T(8,128)(2,1)S(1)}, bf16[2,1,128,512]{3,2,1,0:T(8,128)(2,1)S(1)}) custom-call(bf16[1,32,2176]{2,1,0:T(8,128)(2,1)S(1)} %bitcast.90, bf16[1,32,2176]{2,1,0:T(8,128)(2,1)S(1)} %collective-permute-done.12.refs_1_, bf16[1,32,2176]{2,1,0:T(8,128)(2,1)S(1)} %collective-permute-done.7.refs_2_, ...), custom_call_target="tpu_custom_call" | custom-call | tf_op jit(solution)/shard_map/experts/pallas_call | solution.py:490
  45.5 3.8 %collective-permute-done.19.refs_0_ = bf16[3,32,2176]{2,1,0:T(8,128)(2,1)S(1)} collective-permute-done((bf16[3,32,2176]{2,1,0:T(8,128)(2,1)S(1)}, bf16[3,32,2176]{2,1,0:T(8,128)(2,1)S(1)}, u32[]{:S(2)}, u32[]{:S(2)}) %collective-permute-start.19) | collective-permute-done | bytes 417824 | tf_op jit(solution)/shard_map/ppermute | solution.py:153
  52.0 2.7 %experts.4 = (f32[1,2,3,128,512]{4,3,2,1,0:T(8,128)S(1)}, bf16[1,3,128,512]{3,2,1,0:T(8,128)(2,1)S(1)}, bf16[1,3,128,512]{3,2,1,0:T(8,128)(2,1)S(1)}) custom-call(bf16[3,32,2176]{2,1,0:T(8,128)(2,1)S(1)} %pad_maximum_fusion.refs_0_, bf16[3,32,2176]{2,1,0:T(8,128)(2,1)S(1)} %collective-permute-done.17.refs_1_, ...), custom_call_target="tpu_custom_call" | custom-call | tf_op jit(solution)/shard_map/experts/pallas_call | solution.py:490
  54.7 2.8 %collective-permute-done.22.refs_2_ = bf16[3,16,2176]{2,1,0:T(8,128)(2,1)S(1)} collective-permute-done((bf16[3,16,2176]{2,1,0:T(8,128)(2,1)S(1)}, bf16[3,16,2176]{2,1,0:T(8,128)(2,1)S(1)}, u32[]{:S(2)}, u32[]{:S(2)}) %collective-permute-start.22) | collective-permute-done | bytes 208928 | tf_op jit(solution)/shard_map/ppermute | solution.py:153
  59.6 2.7 %experts.5 = (f32[1,2,3,128,512]{4,3,2,1,0:T(8,128)S(1)}, bf16[1,3,128,512]{3,2,1,0:T(8,128)(2,1)S(1)}, bf16[1,3,128,512]{3,2,1,0:T(8,128)(2,1)S(1)}) custom-call(bf16[3,32,2176]{2,1,0:T(8,128)(2,1)S(1)} %collective-permute-done.19.refs_0_, bf16[3,32,2176]{2,1,0:T(8,128)(2,1)S(1)} %collective-permute-done.21.refs_1_, ...), custom_call_target="tpu_custom_call" | custom-call | tf_op jit(solution)/shard_map/experts/pallas_call | solution.py:490
  62.6 1.5 %collective-permute-done.26 = bf16[1,3,128,512]{3,2,1,0:T(8,128)(2,1)S(1)} collective-permute-done((bf16[1,3,128,512]{3,2,1,0:T(8,128)(2,1)S(1)}, bf16[1,3,128,512]{3,2,1,0:T(8,128)(2,1)S(1)}, u32[]{:S(2)}, u32[]{:S(2)}) %collective-permute-start.26) | collective-permute-done | bytes 393248 | tf_op jit(solution)/shard_map/ppermute | solution.py:153
  64.8 1.5 %collective-permute-start.30 = (bf16[3,64,512]{2,1,0:T(8,128)(2,1)S(1)}, bf16[3,64,512]{2,1,0:T(8,128)(2,1)S(1)}, u32[]{:S(2)}, u32[]{:S(2)}) collective-permute-start(bf16[3,64,512]{2,1,0:T(8,128)(2,1)S(1)} %get-tuple-element.233), channel_id=1, source_target_pairs={{0,2},{1,3},{2,0},{3,1},{4,6},{5,7},{6,4},{7,5},{8,10},{9,11},{10,... | collective-permute-start | bytes 589832 | tf_op jit(solution)/shard_map/ppermute | solution.py:153
  66.4 1.1 %collective-permute-start.29 = (bf16[3,64,512]{2,1,0:T(8,128)(2,1)S(1)}, bf16[3,64,512]{2,1,0:T(8,128)(2,1)S(1)}, u32[]{:S(2)}, u32[]{:S(2)}) collective-permute-start(bf16[3,64,512]{2,1,0:T(8,128)(2,1)S(1)} %get-tuple-element.234), channel_id=1, source_target_pairs={{0,4},{4,0},{8,12},{12,8},{16,20},{20,16},{24,28},{28,24},{1,5},{5... | collective-permute-start | bytes 589832 | tf_op jit(solution)/shard_map/ppermute | solution.py:153
  67.5 4.4 %collective-permute-done.30 = bf16[3,64,512]{2,1,0:T(8,128)(2,1)S(1)} collective-permute-done((bf16[3,64,512]{2,1,0:T(8,128)(2,1)S(1)}, bf16[3,64,512]{2,1,0:T(8,128)(2,1)S(1)}, u32[]{:S(2)}, u32[]{:S(2)}) %collective-permute-start.30) | collective-permute-done | bytes 196640 | tf_op jit(solution)/shard_map/ppermute | solution.py:153
  71.9 1.2 %collective-permute-done.29 = bf16[3,64,512]{2,1,0:T(8,128)(2,1)S(1)} collective-permute-done((bf16[3,64,512]{2,1,0:T(8,128)(2,1)S(1)}, bf16[3,64,512]{2,1,0:T(8,128)(2,1)S(1)}, u32[]{:S(2)}, u32[]{:S(2)}) %collective-permute-start.29) | collective-permute-done | bytes 196640 | tf_op jit(solution)/shard_map/ppermute | solution.py:153
  73.5 1.2 %collective-permute-start.34 = (bf16[3,128,512]{2,1,0:T(8,128)(2,1)S(1)}, bf16[3,128,512]{2,1,0:T(8,128)(2,1)S(1)}, u32[]{:S(2)}, u32[]{:S(2)}) collective-permute-start(bf16[3,128,512]{2,1,0:T(8,128)(2,1)S(1)} %pad_maximum_fusion.1), channel_id=1, source_target_pairs={{0,4},{4,0},{8,12},{12,8},{16,20},{20,16},{24,28},{28,24},{1,5},{5... | collective-permute-start | bytes 1179656 | tf_op jit(solution)/shard_map/ppermute | solution.py:153
  75.7 1.6 %collective-permute-done.31 = bf16[2,1,128,512]{3,2,1,0:T(8,128)(2,1)S(1)} collective-permute-done((bf16[2,1,128,512]{3,2,1,0:T(8,128)(2,1)S(1)}, bf16[2,1,128,512]{3,2,1,0:T(8,128)(2,1)S(1)}, u32[]{:S(2)}, u32[]{:S(2)}) %collective-permute-start.31) | collective-permute-done | bytes 262176 | tf_op jit(solution)/shard_map/ppermute | solution.py:153
  77.7 6.0 %collective-permute-done.34 = bf16[3,128,512]{2,1,0:T(8,128)(2,1)S(1)} collective-permute-done((bf16[3,128,512]{2,1,0:T(8,128)(2,1)S(1)}, bf16[3,128,512]{2,1,0:T(8,128)(2,1)S(1)}, u32[]{:S(2)}, u32[]{:S(2)}) %collective-permute-start.34) | collective-permute-done | bytes 393248 | tf_op jit(solution)/shard_map/ppermute | solution.py:153
  86.8 1.2 %collective-permute-start.38 = (bf16[1,64,512]{2,1,0:T(8,128)(2,1)S(1)}, bf16[1,64,512]{2,1,0:T(8,128)(2,1)S(1)}, u32[]{:S(2)}, u32[]{:S(2)}) collective-permute-start(bf16[1,64,512]{2,1,0:T(8,128)(2,1)S(1)} %get-tuple-element.236), channel_id=1, source_target_pairs={{0,4},{4,0},{8,12},{12,8},{16,20},{20,16},{24,28},{28,24},{1,5},{5... | collective-permute-start | bytes 196616 | tf_op jit(solution)/shard_map/ppermute | solution.py:153
  88.8 1.6 %collective-permute-done.39 = bf16[1,64,512]{2,1,0:T(8,128)(2,1)S(1)} collective-permute-done((bf16[1,64,512]{2,1,0:T(8,128)(2,1)S(1)}, bf16[1,64,512]{2,1,0:T(8,128)(2,1)S(1)}, u32[]{:S(2)}, u32[]{:S(2)}) %collective-permute-start.39) | collective-permute-done | bytes 65568 | tf_op jit(solution)/shard_map/ppermute | solution.py:153
  90.5 1.3 %collective-permute-done.38 = bf16[1,64,512]{2,1,0:T(8,128)(2,1)S(1)} collective-permute-done((bf16[1,64,512]{2,1,0:T(8,128)(2,1)S(1)}, bf16[1,64,512]{2,1,0:T(8,128)(2,1)S(1)}, u32[]{:S(2)}, u32[]{:S(2)}) %collective-permute-start.38) | collective-permute-done | bytes 65568 | tf_op jit(solution)/shard_map/ppermute | solution.py:153
  91.9 1.3 %collective-permute-start.41 = (bf16[1,128,512]{2,1,0:T(8,128)(2,1)S(1)}, bf16[1,128,512]{2,1,0:T(8,128)(2,1)S(1)}, u32[]{:S(2)}, u32[]{:S(2)}) collective-permute-start(bf16[1,128,512]{2,1,0:T(8,128)(2,1)S(1)} %pad_maximum_fusion.4), channel_id=1, source_target_pairs={{0,4},{4,0},{8,12},{12,8},{16,20},{20,16},{24,28},{28,24},{1,5},{5... | collective-permute-start | bytes 393224 | tf_op jit(solution)/shard_map/ppermute | solution.py:153
  93.1 1.3 %collective-permute-start.40 = (bf16[128,512]{1,0:T(8,128)(2,1)S(1)}, bf16[128,512]{1,0:T(8,128)(2,1)S(1)}, u32[]{:S(2)}, u32[]{:S(2)}) collective-permute-start(bf16[128,512]{1,0:T(8,128)(2,1)S(1)} %fusion.6), channel_id=1, source_target_pairs={{0,16},{4,20},{8,24},{12,28},{16,0},{20,4},{24,8},{28,12},{1,17},{... | collective-permute-start | bytes 393224 | tf_op jit(solution)/shard_map/ppermute | solution.py:153
  94.5 1.4 %collective-permute-start.42 = (bf16[1,128,512]{2,1,0:T(8,128)(2,1)S(1)}, bf16[1,128,512]{2,1,0:T(8,128)(2,1)S(1)}, u32[]{:S(2)}, u32[]{:S(2)}) collective-permute-start(bf16[1,128,512]{2,1,0:T(8,128)(2,1)S(1)} %pad_maximum_fusion.5), channel_id=1, source_target_pairs={{0,2},{1,3},{2,0},{3,1},{4,6},{5,7},{6,4},{7,5},{8,10},{9,11},{10,... | collective-permute-start | bytes 393224 | tf_op jit(solution)/shard_map/ppermute | solution.py:153
  96.9 3.5 %collective-permute-done.40.z2_ref = bf16[128,512]{1,0:T(8,128)(2,1)S(1)} collective-permute-done((bf16[128,512]{1,0:T(8,128)(2,1)S(1)}, bf16[128,512]{1,0:T(8,128)(2,1)S(1)}, u32[]{:S(2)}, u32[]{:S(2)}) %collective-permute-start.40) | collective-permute-done | bytes 131104 | tf_op jit(solution)/shard_map/ppermute | solution.py:153
  (103 shorter events, 24.2 us)
Async XLA Ops:
  0.0 7.4 %collective-permute-start.1 = (bf16[128,512]{1,0:T(8,128)(2,1)}, bf16[128,512]{1,0:T(8,128)(2,1)S(1)}, u32[]{:S(2)}, u32[]{:S(2)}) collective-permute-start(bf16[128,512]{1,0:T(8,128)(2,1)} %refs_0_.3), channel_id=1, source_target_pairs={{0,2},{1,3},{2,0},{3,1},{4,6},{5,7},{6,4},{7,5},{8,10},{9,11},{10,... | collective-permute-start | bytes 393224 | tf_op jit(solution)/shard_map/ppermute | solution.py:153
  3.0 5.0 %collective-permute-start = (bf16[128,512]{1,0:T(8,128)(2,1)}, bf16[128,512]{1,0:T(8,128)(2,1)S(1)}, u32[]{:S(2)}, u32[]{:S(2)}) collective-permute-start(bf16[128,512]{1,0:T(8,128)(2,1)} %refs_0_.3), channel_id=1, source_target_pairs={{0,1},{1,0},{2,3},{3,2},{4,5},{5,4},{6,7},{7,6},{8,9},{9,8},{10,11... | collective-permute-start | bytes 393224 | tf_op jit(solution)/shard_map/ppermute | solution.py:153
  15.5 5.8 %collective-permute-start.4 = (bf16[32,2048]{1,0:T(8,128)(2,1)S(1)}, bf16[32,2048]{1,0:T(8,128)(2,1)S(1)}, u32[]{:S(2)}, u32[]{:S(2)}) collective-permute-start(bf16[32,2048]{1,0:T(8,128)(2,1)S(1)} %fusion.8), channel_id=1, source_target_pairs={{0,2},{1,3},{2,0},{3,1},{4,6},{5,7},{6,4},{7,5},{8,10},{9,11},{10,... | collective-permute-start | bytes 393224 | tf_op jit(solution)/shard_map/ppermute | solution.py:153
  21.6 9.2 %collective-permute-start.6 = (bf16[1,32,2176]{2,1,0:T(8,128)(2,1)S(1)}, bf16[1,32,2176]{2,1,0:T(8,128)(2,1)S(1)}, u32[]{:S(2)}, u32[]{:S(2)}) collective-permute-start(bf16[1,32,2176]{2,1,0:T(8,128)(2,1)S(1)} %bitcast.85), channel_id=1, source_target_pairs={{0,16},{4,20},{8,24},{12,28},{16,0},{20,4},{24,8},{28,12},{1,17},{... | collective-permute-start | bytes 417800 | tf_op jit(solution)/shard_map/ppermute | solution.py:153
  24.2 6.7 %collective-permute-start.5 = (bf16[1,32,2176]{2,1,0:T(8,128)(2,1)S(1)}, bf16[1,32,2176]{2,1,0:T(8,128)(2,1)S(1)}, u32[]{:S(2)}, u32[]{:S(2)}) collective-permute-start(bf16[1,32,2176]{2,1,0:T(8,128)(2,1)S(1)} %bitcast.86), channel_id=1, source_target_pairs={{0,8},{4,12},{8,0},{12,4},{16,24},{20,28},{24,16},{28,20},{1,9},{5... | collective-permute-start | bytes 417800 | tf_op jit(solution)/shard_map/ppermute | solution.py:153
  25.8 5.2 %collective-permute-start.8 = (bf16[1,32,2176]{2,1,0:T(8,128)(2,1)S(1)}, bf16[1,32,2176]{2,1,0:T(8,128)(2,1)S(1)}, u32[]{:S(2)}, u32[]{:S(2)}) collective-permute-start(bf16[1,32,2176]{2,1,0:T(8,128)(2,1)S(1)} %bitcast.87), channel_id=1, source_target_pairs={{0,4},{4,0},{8,12},{12,8},{16,20},{20,16},{24,28},{28,24},{1,5},{5... | collective-permute-start | bytes 417800 | tf_op jit(solution)/shard_map/ppermute | solution.py:153
  27.3 5.1 %collective-permute-start.7 = (bf16[1,32,2176]{2,1,0:T(8,128)(2,1)S(1)}, bf16[1,32,2176]{2,1,0:T(8,128)(2,1)S(1)}, u32[]{:S(2)}, u32[]{:S(2)}) collective-permute-start(bf16[1,32,2176]{2,1,0:T(8,128)(2,1)S(1)} %bitcast.88), channel_id=1, source_target_pairs={{0,2},{1,3},{2,0},{3,1},{4,6},{5,7},{6,4},{7,5},{8,10},{9,11},{10,... | collective-permute-start | bytes 417800 | tf_op jit(solution)/shard_map/ppermute | solution.py:153
  32.3 5.1 %collective-permute-start.9 = (bf16[1,32,2176]{2,1,0:T(8,128)(2,1)S(1)}, bf16[1,32,2176]{2,1,0:T(8,128)(2,1)S(1)}, u32[]{:S(2)}, u32[]{:S(2)}) collective-permute-start(bf16[1,32,2176]{2,1,0:T(8,128)(2,1)S(1)} %collective-permute-done.6), channel_id=1, source_target_pairs={{0,8},{4,12},{8,0},{12,4},{16,24},{20,28},{24,16},{28,20},{1,9},{5... | collective-permute-start | bytes 417800 | tf_op jit(solution)/shard_map/ppermute | solution.py:153
  32.8 4.7 %collective-permute-start.12 = (bf16[1,32,2176]{2,1,0:T(8,128)(2,1)S(1)}, bf16[1,32,2176]{2,1,0:T(8,128)(2,1)S(1)}, u32[]{:S(2)}, u32[]{:S(2)}) collective-permute-start(bf16[1,32,2176]{2,1,0:T(8,128)(2,1)S(1)} %bitcast.89), channel_id=1, source_target_pairs={{0,1},{1,0},{2,3},{3,2},{4,5},{5,4},{6,7},{7,6},{8,9},{9,8},{10,11... | collective-permute-start | bytes 417800 | tf_op jit(solution)/shard_map/ppermute | solution.py:153
  32.8 6.0 %collective-permute-start.13 = (bf16[1,32,2176]{2,1,0:T(8,128)(2,1)S(1)}, bf16[1,32,2176]{2,1,0:T(8,128)(2,1)S(1)}, u32[]{:S(2)}, u32[]{:S(2)}) collective-permute-start(bf16[1,32,2176]{2,1,0:T(8,128)(2,1)S(1)} %collective-permute-done.7.refs_2_), channel_id=1, source_target_pairs={{0,1},{1,0},{2,3},{3,2},{4,5},{5,4},{6,7},{7,6},{8,9},{9,8},{10,11... | collective-permute-start | bytes 417800 | tf_op jit(solution)/shard_map/ppermute | solution.py:153
  33.3 4.3 %collective-permute-start.11 = (bf16[1,16,2176]{2,1,0:T(8,128)(2,1)S(1)}, bf16[1,16,2176]{2,1,0:T(8,128)(2,1)S(1)}, u32[]{:S(2)}, u32[]{:S(2)}) collective-permute-start(bf16[1,16,2176]{2,1,0:T(8,128)(2,1)S(1)} %slice.108), channel_id=1, source_target_pairs={{0,4},{4,0},{8,12},{12,8},{16,20},{20,16},{24,28},{28,24},{1,5},{5... | collective-permute-start | bytes 208904 | tf_op jit(solution)/shard_map/ppermute | solution.py:153
  34.5 4.3 %collective-permute-start.10 = (bf16[1,16,2176]{2,1,0:T(8,128)(2,1)S(1)}, bf16[1,16,2176]{2,1,0:T(8,128)(2,1)S(1)}, u32[]{:S(2)}, u32[]{:S(2)}) collective-permute-start(bf16[1,16,2176]{2,1,0:T(8,128)(2,1)S(1)} %slice.107), channel_id=1, source_target_pairs={{0,2},{1,3},{2,0},{3,1},{4,6},{5,7},{6,4},{7,5},{8,10},{9,11},{10,... | collective-permute-start | bytes 208904 | tf_op jit(solution)/shard_map/ppermute | solution.py:153
  38.8 10.5 %collective-permute-start.19 = (bf16[3,32,2176]{2,1,0:T(8,128)(2,1)S(1)}, bf16[3,32,2176]{2,1,0:T(8,128)(2,1)S(1)}, u32[]{:S(2)}, u32[]{:S(2)}) collective-permute-start(bf16[3,32,2176]{2,1,0:T(8,128)(2,1)S(1)} %pad_maximum_fusion.refs_0_), channel_id=1, source_target_pairs={{0,4},{4,0},{8,12},{12,8},{16,20},{20,16},{24,28},{28,24},{1,5},{5... | collective-permute-start | bytes 1253384 | tf_op jit(solution)/shard_map/ppermute | solution.py:153
  39.7 10.2 %collective-permute-start.18 = (bf16[3,32,2176]{2,1,0:T(8,128)(2,1)S(1)}, bf16[3,32,2176]{2,1,0:T(8,128)(2,1)S(1)}, u32[]{:S(2)}, u32[]{:S(2)}) collective-permute-start(bf16[3,32,2176]{2,1,0:T(8,128)(2,1)S(1)} %pad_maximum_fusion.refs_0_), channel_id=1, source_target_pairs={{0,2},{1,3},{2,0},{3,1},{4,6},{5,7},{6,4},{7,5},{8,10},{9,11},{10,... | collective-permute-start | bytes 1253384 | tf_op jit(solution)/shard_map/ppermute | solution.py:153
  40.2 9.7 %collective-permute-start.17 = (bf16[3,32,2176]{2,1,0:T(8,128)(2,1)S(1)}, bf16[3,32,2176]{2,1,0:T(8,128)(2,1)S(1)}, u32[]{:S(2)}, u32[]{:S(2)}) collective-permute-start(bf16[3,32,2176]{2,1,0:T(8,128)(2,1)S(1)} %pad_maximum_fusion.refs_0_), channel_id=1, source_target_pairs={{0,1},{1,0},{2,3},{3,2},{4,5},{5,4},{6,7},{7,6},{8,9},{9,8},{10,11... | collective-permute-start | bytes 1253384 | tf_op jit(solution)/shard_map/ppermute | solution.py:153
  49.9 8.0 %collective-permute-start.21 = (bf16[3,32,2176]{2,1,0:T(8,128)(2,1)S(1)}, bf16[3,32,2176]{2,1,0:T(8,128)(2,1)S(1)}, u32[]{:S(2)}, u32[]{:S(2)}) collective-permute-start(bf16[3,32,2176]{2,1,0:T(8,128)(2,1)S(1)} %collective-permute-done.19.refs_0_), channel_id=1, source_target_pairs={{0,1},{1,0},{2,3},{3,2},{4,5},{5,4},{6,7},{7,6},{8,9},{9,8},{10,11... | collective-permute-start | bytes 1253384 | tf_op jit(solution)/shard_map/ppermute | solution.py:153
  50.4 7.1 %collective-permute-start.22 = (bf16[3,16,2176]{2,1,0:T(8,128)(2,1)S(1)}, bf16[3,16,2176]{2,1,0:T(8,128)(2,1)S(1)}, u32[]{:S(2)}, u32[]{:S(2)}) collective-permute-start(bf16[3,16,2176]{2,1,0:T(8,128)(2,1)S(1)} %slice.109), channel_id=1, source_target_pairs={{0,2},{1,3},{2,0},{3,1},{4,6},{5,7},{6,4},{7,5},{8,10},{9,11},{10,... | collective-permute-start | bytes 626696 | tf_op jit(solution)/shard_map/ppermute | solution.py:153
  51.1 6.8 %collective-permute-start.23 = (bf16[3,16,2176]{2,1,0:T(8,128)(2,1)S(1)}, bf16[3,16,2176]{2,1,0:T(8,128)(2,1)S(1)}, u32[]{:S(2)}, u32[]{:S(2)}) collective-permute-start(bf16[3,16,2176]{2,1,0:T(8,128)(2,1)S(1)} %slice.110), channel_id=1, source_target_pairs={{0,4},{4,0},{8,12},{12,8},{16,20},{20,16},{24,28},{28,24},{1,5},{5... | collective-permute-start | bytes 626696 | tf_op jit(solution)/shard_map/ppermute | solution.py:153
  64.1 9.0 %collective-permute-start.27 = (bf16[1,3,128,512]{3,2,1,0:T(8,128)(2,1)S(1)}, bf16[1,3,128,512]{3,2,1,0:T(8,128)(2,1)S(1)}, u32[]{:S(2)}, u32[]{:S(2)}) collective-permute-start(bf16[1,3,128,512]{3,2,1,0:T(8,128)(2,1)S(1)} %get-tuple-element.198), channel_id=1, source_target_pairs={{0,1},{1,0},{2,3},{3,2},{4,5},{5,4},{6,7},{7,6},{8,9},{9,8},{10,11... | collective-permute-start | bytes 1179656 | tf_op jit(solution)/shard_map/ppermute | solution.py:153
  64.4 8.7 %collective-permute-start.28 = (bf16[1,3,128,512]{3,2,1,0:T(8,128)(2,1)S(1)}, bf16[1,3,128,512]{3,2,1,0:T(8,128)(2,1)S(1)}, u32[]{:S(2)}, u32[]{:S(2)}) collective-permute-start(bf16[1,3,128,512]{3,2,1,0:T(8,128)(2,1)S(1)} %get-tuple-element.199), channel_id=1, source_target_pairs={{0,1},{1,0},{2,3},{3,2},{4,5},{5,4},{6,7},{7,6},{8,9},{9,8},{10,11... | collective-permute-start | bytes 1179656 | tf_op jit(solution)/shard_map/ppermute | solution.py:153
  64.8 7.1 %collective-permute-start.30 = (bf16[3,64,512]{2,1,0:T(8,128)(2,1)S(1)}, bf16[3,64,512]{2,1,0:T(8,128)(2,1)S(1)}, u32[]{:S(2)}, u32[]{:S(2)}) collective-permute-start(bf16[3,64,512]{2,1,0:T(8,128)(2,1)S(1)} %get-tuple-element.233), channel_id=1, source_target_pairs={{0,2},{1,3},{2,0},{3,1},{4,6},{5,7},{6,4},{7,5},{8,10},{9,11},{10,... | collective-permute-start | bytes 589832 | tf_op jit(solution)/shard_map/ppermute | solution.py:153
  66.4 6.7 %collective-permute-start.29 = (bf16[3,64,512]{2,1,0:T(8,128)(2,1)S(1)}, bf16[3,64,512]{2,1,0:T(8,128)(2,1)S(1)}, u32[]{:S(2)}, u32[]{:S(2)}) collective-permute-start(bf16[3,64,512]{2,1,0:T(8,128)(2,1)S(1)} %get-tuple-element.234), channel_id=1, source_target_pairs={{0,4},{4,0},{8,12},{12,8},{16,20},{20,16},{24,28},{28,24},{1,5},{5... | collective-permute-start | bytes 589832 | tf_op jit(solution)/shard_map/ppermute | solution.py:153
  73.5 10.2 %collective-permute-start.34 = (bf16[3,128,512]{2,1,0:T(8,128)(2,1)S(1)}, bf16[3,128,512]{2,1,0:T(8,128)(2,1)S(1)}, u32[]{:S(2)}, u32[]{:S(2)}) collective-permute-start(bf16[3,128,512]{2,1,0:T(8,128)(2,1)S(1)} %pad_maximum_fusion.1), channel_id=1, source_target_pairs={{0,4},{4,0},{8,12},{12,8},{16,20},{20,16},{24,28},{28,24},{1,5},{5... | collective-permute-start | bytes 1179656 | tf_op jit(solution)/shard_map/ppermute | solution.py:153
  74.8 9.9 %collective-permute-start.35 = (bf16[3,128,512]{2,1,0:T(8,128)(2,1)S(1)}, bf16[3,128,512]{2,1,0:T(8,128)(2,1)S(1)}, u32[]{:S(2)}, u32[]{:S(2)}) collective-permute-start(bf16[3,128,512]{2,1,0:T(8,128)(2,1)S(1)} %pad_maximum_fusion.2), channel_id=1, source_target_pairs={{0,2},{1,3},{2,0},{3,1},{4,6},{5,7},{6,4},{7,5},{8,10},{9,11},{10,... | collective-permute-start | bytes 1179656 | tf_op jit(solution)/shard_map/ppermute | solution.py:153
  75.2 9.5 %collective-permute-start.33 = (bf16[1,3,128,512]{3,2,1,0:T(8,128)(2,1)S(1)}, bf16[1,3,128,512]{3,2,1,0:T(8,128)(2,1)S(1)}, u32[]{:S(2)}, u32[]{:S(2)}) collective-permute-start(bf16[1,3,128,512]{3,2,1,0:T(8,128)(2,1)S(1)} %get-tuple-element.205), channel_id=1, source_target_pairs={{0,1},{1,0},{2,3},{3,2},{4,5},{5,4},{6,7},{7,6},{8,9},{9,8},{10,11... | collective-permute-start | bytes 1179656 | tf_op jit(solution)/shard_map/ppermute | solution.py:153
  84.9 6.9 %collective-permute-start.37 = (bf16[128,512]{1,0:T(8,128)(2,1)S(1)}, bf16[128,512]{1,0:T(8,128)(2,1)S(1)}, u32[]{:S(2)}, u32[]{:S(2)}) collective-permute-start(bf16[128,512]{1,0:T(8,128)(2,1)S(1)} %get-tuple-element.231), channel_id=1, source_target_pairs={{0,8},{4,12},{8,0},{12,4},{16,24},{20,28},{24,16},{28,20},{1,9},{5... | collective-permute-start | bytes 393224 | tf_op jit(solution)/shard_map/ppermute | solution.py:153
  86.1 4.3 %collective-permute-start.39 = (bf16[1,64,512]{2,1,0:T(8,128)(2,1)S(1)}, bf16[1,64,512]{2,1,0:T(8,128)(2,1)S(1)}, u32[]{:S(2)}, u32[]{:S(2)}) collective-permute-start(bf16[1,64,512]{2,1,0:T(8,128)(2,1)S(1)} %get-tuple-element.235), channel_id=1, source_target_pairs={{0,2},{1,3},{2,0},{3,1},{4,6},{5,7},{6,4},{7,5},{8,10},{9,11},{10,... | collective-permute-start | bytes 196616 | tf_op jit(solution)/shard_map/ppermute | solution.py:153
  86.8 5.0 %collective-permute-start.38 = (bf16[1,64,512]{2,1,0:T(8,128)(2,1)S(1)}, bf16[1,64,512]{2,1,0:T(8,128)(2,1)S(1)}, u32[]{:S(2)}, u32[]{:S(2)}) collective-permute-start(bf16[1,64,512]{2,1,0:T(8,128)(2,1)S(1)} %get-tuple-element.236), channel_id=1, source_target_pairs={{0,4},{4,0},{8,12},{12,8},{16,20},{20,16},{24,28},{28,24},{1,5},{5... | collective-permute-start | bytes 196616 | tf_op jit(solution)/shard_map/ppermute | solution.py:153
  88.0 7.8 %collective-permute-start.36 = (bf16[128,512]{1,0:T(8,128)(2,1)S(1)}, bf16[128,512]{1,0:T(8,128)(2,1)S(1)}, u32[]{:S(2)}, u32[]{:S(2)}) collective-permute-start(bf16[128,512]{1,0:T(8,128)(2,1)S(1)} %get-tuple-element.232), channel_id=1, source_target_pairs={{0,8},{4,12},{8,0},{12,4},{16,24},{20,28},{24,16},{28,20},{1,9},{5... | collective-permute-start | bytes 393224 | tf_op jit(solution)/shard_map/ppermute | solution.py:153
  91.9 5.0 %collective-permute-start.41 = (bf16[1,128,512]{2,1,0:T(8,128)(2,1)S(1)}, bf16[1,128,512]{2,1,0:T(8,128)(2,1)S(1)}, u32[]{:S(2)}, u32[]{:S(2)}) collective-permute-start(bf16[1,128,512]{2,1,0:T(8,128)(2,1)S(1)} %pad_maximum_fusion.4), channel_id=1, source_target_pairs={{0,4},{4,0},{8,12},{12,8},{16,20},{20,16},{24,28},{28,24},{1,5},{5... | collective-permute-start | bytes 393224 | tf_op jit(solution)/shard_map/ppermute | solution.py:153
  93.1 7.3 %collective-permute-start.40 = (bf16[128,512]{1,0:T(8,128)(2,1)S(1)}, bf16[128,512]{1,0:T(8,128)(2,1)S(1)}, u32[]{:S(2)}, u32[]{:S(2)}) collective-permute-start(bf16[128,512]{1,0:T(8,128)(2,1)S(1)} %fusion.6), channel_id=1, source_target_pairs={{0,16},{4,20},{8,24},{12,28},{16,0},{20,4},{24,8},{28,12},{1,17},{... | collective-permute-start | bytes 393224 | tf_op jit(solution)/shard_map/ppermute | solution.py:153
  94.5 5.9 %collective-permute-start.42 = (bf16[1,128,512]{2,1,0:T(8,128)(2,1)S(1)}, bf16[1,128,512]{2,1,0:T(8,128)(2,1)S(1)}, u32[]{:S(2)}, u32[]{:S(2)}) collective-permute-start(bf16[1,128,512]{2,1,0:T(8,128)(2,1)S(1)} %pad_maximum_fusion.5), channel_id=1, source_target_pairs={{0,2},{1,3},{2,0},{3,1},{4,6},{5,7},{6,4},{7,5},{8,10},{9,11},{10,... | collective-permute-start | bytes 393224 | tf_op jit(solution)/shard_map/ppermute | solution.py:153
  (18 other events, 157.4 us)

commit v13 on v12

--- a/solution.py
+++ b/solution.py
@@ -590,38 +590,41 @@
     gate_up = [w.transpose(0, 2, 1).reshape(-1, width) for w in (gate_weight, up_weight)]
     weights = (*gate_up, down_weight.reshape(-1, width))
     line_0 = rows[None]
-    z_1, z_2 = flip(line_0, "req", 2), flip(line_0, "req", 4)
+    levels = [flip(line_0, "req", 2 * bits) for bits in (1, 2, 3)]
     y_0, x_0 = flip(line_0, "tp", 2), flip(line_0, "req", 1)
-    line_12, z_2, y_0, x_0 = ordered(jnp.concatenate([z_1, z_2]), z_2, y_0, x_0)
-    line_3, across_0, core_0, y_core_0 = ordered(
-        jnp.concatenate([line_12, flip(z_2, "req", 2)]),
+    line_3, y_0, x_0 = ordered(jnp.concatenate(levels), y_0, x_0)
+    core_0, core_3, across_0, y_3, x_3 = ordered(
+        *other_core((line_0, line_3)),
         across_parts(x_0, y_0),
-        flip(line_0, "tp", 1),
-        flip(y_0, "tp", 1),
-    )
-    y_3, x_3 = flip(line_3, "tp", 2), flip(line_3, "req", 1)
+        flip(line_3, "tp", 2),
+        flip(line_3, "req", 1),
+    )
+    y_core_3, x_core_3 = other_core((y_3, x_3))
+    near_3 = run_experts(
+        near_pieces(0, line_3, core_3) + far_pieces(0, (y_3,), (y_core_3,)), weights, token_count
+    )
+    near_3, y_core_0, x_core_0, across_core_0, x_core_3, across_3 = ordered(
+        near_3,
+        *other_core((y_0, x_0)),
+        other_core(across_0),
+        x_core_3,
+        across_parts(x_3, y_3),
+    )
+    keep, (send, first) = run_experts(
+        near_pieces(0, x_3, x_core_3) + far_pieces(0, across_3, other_core(across_3)),
+        weights,
+        token_count,
+    )
+    near_3, keep, send, first = ordered(near_3, keep, send, first)
     all_0 = run_experts(
         near_pieces(0, line_0, core_0)
         + far_pieces(0, (y_0,), (y_core_0,))
-        + near_pieces(1, x_0, flip(x_0, "tp", 1))
-        + far_pieces(1, across_0, other_core(across_0)),
+        + near_pieces(1, x_0, x_core_0)
+        + far_pieces(1, across_0, across_core_0),
         weights,
         token_count,
         residual,
     )
-    all_0, core_3, y_3, x_3 = ordered(all_0, flip(line_3, "tp", 1), y_3, x_3)
-    y_core_3, x_core_3 = other_core((y_3, x_3))
-    near_3 = run_experts(
-        near_pieces(0, line_3, core_3) + far_pieces(0, (y_3,), (y_core_3,)), weights, token_count
-    )
-    near_3, x_core_3, across_3 = ordered(near_3, x_core_3, across_parts(x_3, y_3))
-    side_3 = run_experts(
-        near_pieces(0, x_3, x_core_3) + far_pieces(0, across_3, other_core(across_3)),
-        weights,
-        token_count,
-    )
-    all_0, near_3, side_3 = ordered(all_0, near_3, side_3)
-    keep, (send, first) = side_3
     all_0, near_3, keep, send, first = ordered(all_0, near_3, keep, send, flip(first, "tp", 1))
     relay_3 = relayed(joined((keep, (send, first)), 0, 1))
     near_keep, (near_send, near_first) = near_3

time: 102 us -> 103 us (level); the launches traced: 101 us -> 103 us
  starting transfers between devices: 31.5 us -> 33.3 us
    ppermute x43, starting transfers between devices: 31.5 us -> 33.3 us  [flip(): lax.ppermute(value, axis, [(i, i ^ bits) for i in range(lax.axis_size(axi...]
  transfers between devices with their start and end apart: 43 -> 43, of which waited for: 28 -> 23; matrix products, arithmetic and copies ran while one was open for 1% -> 1% of each run, Pallas kernels for 9% -> 9%
where the time goes in v13:
time: 103 us
  waiting for transfers between devices  50.5 us (49%)
  starting transfers between devices  33.3 us (32%)
  Pallas kernels  17.7 us (17%)
  other arithmetic  1.18 us (1%)
    ppermute x43, waiting for transfers between devices, flip(): lax.ppermute(value, axis, [(i, i ^ bits) for i in range(lax.axis_size(axi...  50.5 us
    ppermute x43, starting transfers between devices, flip(): lax.ppermute(value, axis, [(i, i ^ bits) for i in range(lax.axis_size(axi...  33.3 us
    pallas_call x3, Pallas kernels, run_experts(): pl.pallas_call(functools.partial(experts_kernel, plan, len(residual)), ou...  7.45 us
    pallas_call x1, Pallas kernels, attention_shares(): pl.pallas_call(attention_kernel, out_shape=[jax.ShapeDtypeStruct(share, j...  4.88 us
    pallas_call x1, Pallas kernels, attention_shares(): pl.pallas_call(stage_kernel, out_shape=[rope, rope, pltpu.VMEM((1, POOL *...  4.41 us
  transfers between devices with their start and end apart: 43, of which 23 were waited for; matrix products, arithmetic and copies ran while one was open for 1% of the time, Pallas kernels for 9%

profile of v13, /device:TPU:0, one launch (start us, length us, event | category | flops | bytes accessed | tf_op | source)
XLA Modules:
  0.0 103.2 jit_solution(13651259923247075988)
XLA Ops:
  0.0 3.0 %collective-permute-start.1 = (bf16[128,512]{1,0:T(8,128)(2,1)}, bf16[128,512]{1,0:T(8,128)(2,1)S(1)}, u32[]{:S(2)}, u32[]{:S(2)}) collective-permute-start(bf16[128,512]{1,0:T(8,128)(2,1)} %refs_0_.3), channel_id=1, source_target_pairs={{0,2},{1,3},{2,0},{3,1},{4,6},{5,7},{6,4},{7,5},{8,10},{9,11},{10,... | collective-permute-start | bytes 393224 | tf_op jit(solution)/shard_map/ppermute | solution.py:153
  3.0 4.4 %stage.1 = (f32[128,128]{1,0:T(8,128)S(1)}, f32[128,128]{1,0:T(8,128)S(1)}, s32[1,6144]{1,0:T(1,128)S(1)}, f32[1,2048]{1,0:T(1,128)S(1)}, f32[1,128]{1,0:T(1,128...) custom-call(s32[9]{0:T(128)} %refs_0_.2, ...), custom_call_target="tpu_custom_call" | custom-call | tf_op jit(solution)/shard_map/stage/pallas_call | solution.py:373
  8.0 1.0 collective-permute-done.2.refs_3_
  9.0 4.9 %attention.1 = (f32[32,2048]{1,0:T(8,128)S(1)}, f32[32,2048]{1,0:T(8,128)S(1)}, bf16[2,32,2048]{2,1,0:T(8,128)(2,1)S(1)}) custom-call(bf16[128,512]{1,0:T(8,128)(2,1)S(1)} %copy-done.3, bf16[128,512]{1,0:T(8,128)(2,1)S(1)} %collective-permute-done.refs_1_, bf16[128,512]{1,0:T(8,128)(2,1)S(1)} %collective-permute-done.1.refs_2_, ...), custom_call_target="tpu_custom_call" | custom-call | tf_op jit(solution)/shard_map/attention/pallas_call | solution.py:393
  14.3 1.2 %collective-permute-done.3 = bf16[2,32,2048]{2,1,0:T(8,128)(2,1)S(1)} collective-permute-done((bf16[2,32,2048]{2,1,0:T(8,128)(2,1)S(1)}, bf16[2,32,2048]{2,1,0:T(8,128)(2,1)S(1)}, u32[]{:S(2)}, u32[]{:S(2)}) %collective-permute-start.3) | collective-permute-done | bytes 262176 | tf_op jit(solution)/shard_map/ppermute | solution.py:153
  16.4 5.0 %collective-permute-done.4.far_ref = bf16[32,2048]{1,0:T(8,128)(2,1)S(1)} collective-permute-done((bf16[32,2048]{1,0:T(8,128)(2,1)S(1)}, bf16[32,2048]{1,0:T(8,128)(2,1)S(1)}, u32[]{:S(2)}, u32[]{:S(2)}) %collective-permute-start.4) | collective-permute-done | bytes 131104 | tf_op jit(solution)/shard_map/ppermute | solution.py:153
  21.6 3.7 %collective-permute-start.8 = (bf16[1,32,2176]{2,1,0:T(8,128)(2,1)S(1)}, bf16[1,32,2176]{2,1,0:T(8,128)(2,1)S(1)}, u32[]{:S(2)}, u32[]{:S(2)}) collective-permute-start(bf16[1,32,2176]{2,1,0:T(8,128)(2,1)S(1)} %bitcast.85), channel_id=1, source_target_pairs={{0,24},{4,28},{8,16},{12,20},{16,8},{20,12},{24,0},{28,4},{1,25},{... | collective-permute-start | bytes 417800 | tf_op jit(solution)/shard_map/ppermute | solution.py:153
  26.0 1.5 %collective-permute-start.10 = (bf16[1,32,2176]{2,1,0:T(8,128)(2,1)S(1)}, bf16[1,32,2176]{2,1,0:T(8,128)(2,1)S(1)}, u32[]{:S(2)}, u32[]{:S(2)}) collective-permute-start(bf16[1,32,2176]{2,1,0:T(8,128)(2,1)S(1)} %bitcast.88), channel_id=1, source_target_pairs={{0,4},{4,0},{8,12},{12,8},{16,20},{20,16},{24,28},{28,24},{1,5},{5... | collective-permute-start | bytes 417800 | tf_op jit(solution)/shard_map/ppermute | solution.py:153
  28.1 2.0 %collective-permute-done.8 = bf16[1,32,2176]{2,1,0:T(8,128)(2,1)S(1)} collective-permute-done((bf16[1,32,2176]{2,1,0:T(8,128)(2,1)S(1)}, bf16[1,32,2176]{2,1,0:T(8,128)(2,1)S(1)}, u32[]{:S(2)}, u32[]{:S(2)}) %collective-permute-start.8) | collective-permute-done | bytes 139296 | tf_op jit(solution)/shard_map/ppermute | solution.py:153
  30.1 6.6 %collective-permute-done.7 = bf16[1,32,2176]{2,1,0:T(8,128)(2,1)S(1)} collective-permute-done((bf16[1,32,2176]{2,1,0:T(8,128)(2,1)S(1)}, bf16[1,32,2176]{2,1,0:T(8,128)(2,1)S(1)}, u32[]{:S(2)}, u32[]{:S(2)}) %collective-permute-start.7) | collective-permute-done | bytes 139296 | tf_op jit(solution)/shard_map/ppermute | solution.py:153
  36.8 1.5 %collective-permute-start.15 = (bf16[3,32,2176]{2,1,0:T(8,128)(2,1)S(1)}, bf16[3,32,2176]{2,1,0:T(8,128)(2,1)S(1)}, u32[]{:S(2)}, u32[]{:S(2)}) collective-permute-start(bf16[3,32,2176]{2,1,0:T(8,128)(2,1)S(1)} %pad_maximum_fusion.refs_0_), channel_id=1, source_target_pairs={{0,4},{4,0},{8,12},{12,8},{16,20},{20,16},{24,28},{28,24},{1,5},{5... | collective-permute-start | bytes 1253384 | tf_op jit(solution)/shard_map/ppermute | solution.py:153
  40.7 1.7 %collective-permute-start.12 = (bf16[1,16,2176]{2,1,0:T(8,128)(2,1)S(1)}, bf16[1,16,2176]{2,1,0:T(8,128)(2,1)S(1)}, u32[]{:S(2)}, u32[]{:S(2)}) collective-permute-start(bf16[1,16,2176]{2,1,0:T(8,128)(2,1)S(1)} %slice.107), channel_id=1, source_target_pairs={{0,2},{1,3},{2,0},{3,1},{4,6},{5,7},{6,4},{7,5},{8,10},{9,11},{10,... | collective-permute-start | bytes 208904 | tf_op jit(solution)/shard_map/ppermute | solution.py:153
  42.4 6.7 %collective-permute-done.13.refs_7_ = bf16[1,16,2176]{2,1,0:T(8,128)(2,1)S(1)} collective-permute-done((bf16[1,16,2176]{2,1,0:T(8,128)(2,1)S(1)}, bf16[1,16,2176]{2,1,0:T(8,128)(2,1)S(1)}, u32[]{:S(2)}, u32[]{:S(2)}) %collective-permute-start.13) | collective-permute-done | bytes 69664 | tf_op jit(solution)/shard_map/ppermute | solution.py:153
  49.0 1.2 %collective-permute-done.12.refs_6_ = bf16[1,16,2176]{2,1,0:T(8,128)(2,1)S(1)} collective-permute-done((bf16[1,16,2176]{2,1,0:T(8,128)(2,1)S(1)}, bf16[1,16,2176]{2,1,0:T(8,128)(2,1)S(1)}, u32[]{:S(2)}, u32[]{:S(2)}) %collective-permute-start.12) | collective-permute-done | bytes 69664 | tf_op jit(solution)/shard_map/ppermute | solution.py:153
  51.8 1.1 %collective-permute-done.18.refs_5_ = bf16[1,32,2176]{2,1,0:T(8,128)(2,1)S(1)} collective-permute-done((bf16[1,32,2176]{2,1,0:T(8,128)(2,1)S(1)}, bf16[1,32,2176]{2,1,0:T(8,128)(2,1)S(1)}, u32[]{:S(2)}, u32[]{:S(2)}) %collective-permute-start.18) | collective-permute-done | bytes 139296 | tf_op jit(solution)/shard_map/ppermute | solution.py:153
  53.9 2.7 %experts.3 = (f32[1,2,3,128,512]{4,3,2,1,0:T(8,128)S(1)}, bf16[1,3,128,512]{3,2,1,0:T(8,128)(2,1)S(1)}, bf16[1,3,128,512]{3,2,1,0:T(8,128)(2,1)S(1)}) custom-call(bf16[3,32,2176]{2,1,0:T(8,128)(2,1)S(1)} %pad_maximum_fusion.refs_0_, bf16[3,32,2176]{2,1,0:T(8,128)(2,1)S(1)} %collective-permute-done.11.refs_1_, ...), custom_call_target="tpu_custom_call" | custom-call | tf_op jit(solution)/shard_map/experts/pallas_call | solution.py:490
  56.7 1.9 %collective-permute-done.22.refs_2_ = bf16[3,16,2176]{2,1,0:T(8,128)(2,1)S(1)} collective-permute-done((bf16[3,16,2176]{2,1,0:T(8,128)(2,1)S(1)}, bf16[3,16,2176]{2,1,0:T(8,128)(2,1)S(1)}, u32[]{:S(2)}, u32[]{:S(2)}) %collective-permute-start.22) | collective-permute-done | bytes 208928 | tf_op jit(solution)/shard_map/ppermute | solution.py:153
  58.6 1.5 %collective-permute-done.23.refs_3_ = bf16[3,16,2176]{2,1,0:T(8,128)(2,1)S(1)} collective-permute-done((bf16[3,16,2176]{2,1,0:T(8,128)(2,1)S(1)}, bf16[3,16,2176]{2,1,0:T(8,128)(2,1)S(1)}, u32[]{:S(2)}, u32[]{:S(2)}) %collective-permute-start.23) | collective-permute-done | bytes 208928 | tf_op jit(solution)/shard_map/ppermute | solution.py:153
  61.8 2.7 %experts.5 = (f32[1,2,3,128,512]{4,3,2,1,0:T(8,128)S(1)}, bf16[1,3,128,512]{3,2,1,0:T(8,128)(2,1)S(1)}, bf16[1,3,128,512]{3,2,1,0:T(8,128)(2,1)S(1)}) custom-call(bf16[3,32,2176]{2,1,0:T(8,128)(2,1)S(1)} %collective-permute-done.15.refs_0_, bf16[3,32,2176]{2,1,0:T(8,128)(2,1)S(1)} %collective-permute-done.21.refs_1_, ...), custom_call_target="tpu_custom_call" | custom-call | tf_op jit(solution)/shard_map/experts/pallas_call | solution.py:490
  64.9 2.0 %experts.4 = (f32[2,2,1,128,512]{4,3,2,1,0:T(8,128)S(1)}, bf16[2,1,128,512]{3,2,1,0:T(8,128)(2,1)S(1)}, bf16[2,1,128,512]{3,2,1,0:T(8,128)(2,1)S(1)}) custom-call(bf16[1,32,2176]{2,1,0:T(8,128)(2,1)S(1)} %bitcast.91, bf16[1,32,2176]{2,1,0:T(8,128)(2,1)S(1)} %collective-permute-done.5.refs_1_, bf16[1,32,2176]{2,1,0:T(8,128)(2,1)S(1)} %collective-permute-done.9.refs_2_, ...), custom_call_target="tpu_custom_call" | custom-call | tf_op jit(solution)/shard_map/experts/pallas_call | solution.py:490
  68.6 6.2 %collective-permute-done.30 = bf16[3,64,512]{2,1,0:T(8,128)(2,1)S(1)} collective-permute-done((bf16[3,64,512]{2,1,0:T(8,128)(2,1)S(1)}, bf16[3,64,512]{2,1,0:T(8,128)(2,1)S(1)}, u32[]{:S(2)}, u32[]{:S(2)}) %collective-permute-start.30) | collective-permute-done | bytes 196640 | tf_op jit(solution)/shard_map/ppermute | solution.py:153
  76.0 1.7 %collective-permute-start.35 = (bf16[3,128,512]{2,1,0:T(8,128)(2,1)S(1)}, bf16[3,128,512]{2,1,0:T(8,128)(2,1)S(1)}, u32[]{:S(2)}, u32[]{:S(2)}) collective-permute-start(bf16[3,128,512]{2,1,0:T(8,128)(2,1)S(1)} %pad_maximum_fusion.2), channel_id=1, source_target_pairs={{0,2},{1,3},{2,0},{3,1},{4,6},{5,7},{6,4},{7,5},{8,10},{9,11},{10,... | collective-permute-start | bytes 1179656 | tf_op jit(solution)/shard_map/ppermute | solution.py:153
  78.3 1.6 %collective-permute-done.31 = bf16[2,1,128,512]{3,2,1,0:T(8,128)(2,1)S(1)} collective-permute-done((bf16[2,1,128,512]{3,2,1,0:T(8,128)(2,1)S(1)}, bf16[2,1,128,512]{3,2,1,0:T(8,128)(2,1)S(1)}, u32[]{:S(2)}, u32[]{:S(2)}) %collective-permute-start.31) | collective-permute-done | bytes 262176 | tf_op jit(solution)/shard_map/ppermute | solution.py:153
  80.3 5.6 %collective-permute-done.34 = bf16[3,128,512]{2,1,0:T(8,128)(2,1)S(1)} collective-permute-done((bf16[3,128,512]{2,1,0:T(8,128)(2,1)S(1)}, bf16[3,128,512]{2,1,0:T(8,128)(2,1)S(1)}, u32[]{:S(2)}, u32[]{:S(2)}) %collective-permute-start.34) | collective-permute-done | bytes 393248 | tf_op jit(solution)/shard_map/ppermute | solution.py:153
  86.8 1.5 %collective-permute-start.39 = (bf16[1,64,512]{2,1,0:T(8,128)(2,1)S(1)}, bf16[1,64,512]{2,1,0:T(8,128)(2,1)S(1)}, u32[]{:S(2)}, u32[]{:S(2)}) collective-permute-start(bf16[1,64,512]{2,1,0:T(8,128)(2,1)S(1)} %get-tuple-element.225), channel_id=1, source_target_pairs={{0,2},{1,3},{2,0},{3,1},{4,6},{5,7},{6,4},{7,5},{8,10},{9,11},{10,... | collective-permute-start | bytes 196616 | tf_op jit(solution)/shard_map/ppermute | solution.py:153
  88.3 1.5 %collective-permute-start.38 = (bf16[1,64,512]{2,1,0:T(8,128)(2,1)S(1)}, bf16[1,64,512]{2,1,0:T(8,128)(2,1)S(1)}, u32[]{:S(2)}, u32[]{:S(2)}) collective-permute-start(bf16[1,64,512]{2,1,0:T(8,128)(2,1)S(1)} %get-tuple-element.226), channel_id=1, source_target_pairs={{0,4},{4,0},{8,12},{12,8},{16,20},{20,16},{24,28},{28,24},{1,5},{5... | collective-permute-start | bytes 196616 | tf_op jit(solution)/shard_map/ppermute | solution.py:153
  89.8 2.1 %collective-permute-start.36 = (bf16[128,512]{1,0:T(8,128)(2,1)S(1)}, bf16[128,512]{1,0:T(8,128)(2,1)S(1)}, u32[]{:S(2)}, u32[]{:S(2)}) collective-permute-start(bf16[128,512]{1,0:T(8,128)(2,1)S(1)} %get-tuple-element.222), channel_id=1, source_target_pairs={{0,8},{4,12},{8,0},{12,4},{16,24},{20,28},{24,16},{28,20},{1,9},{5... | collective-permute-start | bytes 393224 | tf_op jit(solution)/shard_map/ppermute | solution.py:153
  91.9 1.4 %collective-permute-done.38 = bf16[1,64,512]{2,1,0:T(8,128)(2,1)S(1)} collective-permute-done((bf16[1,64,512]{2,1,0:T(8,128)(2,1)S(1)}, bf16[1,64,512]{2,1,0:T(8,128)(2,1)S(1)}, u32[]{:S(2)}, u32[]{:S(2)}) %collective-permute-start.38) | collective-permute-done | bytes 65568 | tf_op jit(solution)/shard_map/ppermute | solution.py:153
  93.3 1.5 %collective-permute-start.41 = (bf16[1,128,512]{2,1,0:T(8,128)(2,1)S(1)}, bf16[1,128,512]{2,1,0:T(8,128)(2,1)S(1)}, u32[]{:S(2)}, u32[]{:S(2)}) collective-permute-start(bf16[1,128,512]{2,1,0:T(8,128)(2,1)S(1)} %pad_maximum_fusion.3), channel_id=1, source_target_pairs={{0,4},{4,0},{8,12},{12,8},{16,20},{20,16},{24,28},{28,24},{1,5},{5... | collective-permute-start | bytes 393224 | tf_op jit(solution)/shard_map/ppermute | solution.py:153
  94.9 2.5 %collective-permute-start.40 = (bf16[128,512]{1,0:T(8,128)(2,1)S(1)}, bf16[128,512]{1,0:T(8,128)(2,1)S(1)}, u32[]{:S(2)}, u32[]{:S(2)}) collective-permute-start(bf16[128,512]{1,0:T(8,128)(2,1)S(1)} %fusion.6), channel_id=1, source_target_pairs={{0,16},{4,20},{8,24},{12,28},{16,0},{20,4},{24,8},{28,12},{1,17},{... | collective-permute-start | bytes 393224 | tf_op jit(solution)/shard_map/ppermute | solution.py:153
  98.4 2.4 %collective-permute-done.40.z2_ref = bf16[128,512]{1,0:T(8,128)(2,1)S(1)} collective-permute-done((bf16[128,512]{1,0:T(8,128)(2,1)S(1)}, bf16[128,512]{1,0:T(8,128)(2,1)S(1)}, u32[]{:S(2)}, u32[]{:S(2)}) %collective-permute-start.40) | collective-permute-done | bytes 131104 | tf_op jit(solution)/shard_map/ppermute | solution.py:153
  100.7 1.7 %collective-permute-done.42.y_ref = bf16[1,128,512]{2,1,0:T(8,128)(2,1)S(1)} collective-permute-done((bf16[1,128,512]{2,1,0:T(8,128)(2,1)S(1)}, bf16[1,128,512]{2,1,0:T(8,128)(2,1)S(1)}, u32[]{:S(2)}, u32[]{:S(2)}) %collective-permute-start.42) | collective-permute-done | bytes 131104 | tf_op jit(solution)/shard_map/ppermute | solution.py:153
  (102 shorter events, 16.9 us)
Async XLA Ops:
  0.0 7.4 %collective-permute-start.1 = (bf16[128,512]{1,0:T(8,128)(2,1)}, bf16[128,512]{1,0:T(8,128)(2,1)S(1)}, u32[]{:S(2)}, u32[]{:S(2)}) collective-permute-start(bf16[128,512]{1,0:T(8,128)(2,1)} %refs_0_.3), channel_id=1, source_target_pairs={{0,2},{1,3},{2,0},{3,1},{4,6},{5,7},{6,4},{7,5},{8,10},{9,11},{10,... | collective-permute-start | bytes 393224 | tf_op jit(solution)/shard_map/ppermute | solution.py:153
  3.0 5.0 %collective-permute-start = (bf16[128,512]{1,0:T(8,128)(2,1)}, bf16[128,512]{1,0:T(8,128)(2,1)S(1)}, u32[]{:S(2)}, u32[]{:S(2)}) collective-permute-start(bf16[128,512]{1,0:T(8,128)(2,1)} %refs_0_.3), channel_id=1, source_target_pairs={{0,1},{1,0},{2,3},{3,2},{4,5},{5,4},{6,7},{7,6},{8,9},{9,8},{10,11... | collective-permute-start | bytes 393224 | tf_op jit(solution)/shard_map/ppermute | solution.py:153
  15.5 5.8 %collective-permute-start.4 = (bf16[32,2048]{1,0:T(8,128)(2,1)S(1)}, bf16[32,2048]{1,0:T(8,128)(2,1)S(1)}, u32[]{:S(2)}, u32[]{:S(2)}) collective-permute-start(bf16[32,2048]{1,0:T(8,128)(2,1)S(1)} %fusion.8), channel_id=1, source_target_pairs={{0,2},{1,3},{2,0},{3,1},{4,6},{5,7},{6,4},{7,5},{8,10},{9,11},{10,... | collective-permute-start | bytes 393224 | tf_op jit(solution)/shard_map/ppermute | solution.py:153
  21.6 8.5 %collective-permute-start.8 = (bf16[1,32,2176]{2,1,0:T(8,128)(2,1)S(1)}, bf16[1,32,2176]{2,1,0:T(8,128)(2,1)S(1)}, u32[]{:S(2)}, u32[]{:S(2)}) collective-permute-start(bf16[1,32,2176]{2,1,0:T(8,128)(2,1)S(1)} %bitcast.85), channel_id=1, source_target_pairs={{0,24},{4,28},{8,16},{12,20},{16,8},{20,12},{24,0},{28,4},{1,25},{... | collective-permute-start | bytes 417800 | tf_op jit(solution)/shard_map/ppermute | solution.py:153
  25.2 11.5 %collective-permute-start.7 = (bf16[1,32,2176]{2,1,0:T(8,128)(2,1)S(1)}, bf16[1,32,2176]{2,1,0:T(8,128)(2,1)S(1)}, u32[]{:S(2)}, u32[]{:S(2)}) collective-permute-start(bf16[1,32,2176]{2,1,0:T(8,128)(2,1)S(1)} %bitcast.86), channel_id=1, source_target_pairs={{0,16},{4,20},{8,24},{12,28},{16,0},{20,4},{24,8},{28,12},{1,17},{... | collective-permute-start | bytes 417800 | tf_op jit(solution)/shard_map/ppermute | solution.py:153
  25.2 11.5 %collective-permute-start.6 = (bf16[1,32,2176]{2,1,0:T(8,128)(2,1)S(1)}, bf16[1,32,2176]{2,1,0:T(8,128)(2,1)S(1)}, u32[]{:S(2)}, u32[]{:S(2)}) collective-permute-start(bf16[1,32,2176]{2,1,0:T(8,128)(2,1)S(1)} %bitcast.87), channel_id=1, source_target_pairs={{0,8},{4,12},{8,0},{12,4},{16,24},{20,28},{24,16},{28,20},{1,9},{5... | collective-permute-start | bytes 417800 | tf_op jit(solution)/shard_map/ppermute | solution.py:153
  26.0 10.8 %collective-permute-start.10 = (bf16[1,32,2176]{2,1,0:T(8,128)(2,1)S(1)}, bf16[1,32,2176]{2,1,0:T(8,128)(2,1)S(1)}, u32[]{:S(2)}, u32[]{:S(2)}) collective-permute-start(bf16[1,32,2176]{2,1,0:T(8,128)(2,1)S(1)} %bitcast.88), channel_id=1, source_target_pairs={{0,4},{4,0},{8,12},{12,8},{16,20},{20,16},{24,28},{28,24},{1,5},{5... | collective-permute-start | bytes 417800 | tf_op jit(solution)/shard_map/ppermute | solution.py:153
  27.5 9.3 %collective-permute-start.9 = (bf16[1,32,2176]{2,1,0:T(8,128)(2,1)S(1)}, bf16[1,32,2176]{2,1,0:T(8,128)(2,1)S(1)}, u32[]{:S(2)}, u32[]{:S(2)}) collective-permute-start(bf16[1,32,2176]{2,1,0:T(8,128)(2,1)S(1)} %bitcast.89), channel_id=1, source_target_pairs={{0,2},{1,3},{2,0},{3,1},{4,6},{5,7},{6,4},{7,5},{8,10},{9,11},{10,... | collective-permute-start | bytes 417800 | tf_op jit(solution)/shard_map/ppermute | solution.py:153
  36.8 13.4 %collective-permute-start.15 = (bf16[3,32,2176]{2,1,0:T(8,128)(2,1)S(1)}, bf16[3,32,2176]{2,1,0:T(8,128)(2,1)S(1)}, u32[]{:S(2)}, u32[]{:S(2)}) collective-permute-start(bf16[3,32,2176]{2,1,0:T(8,128)(2,1)S(1)} %pad_maximum_fusion.refs_0_), channel_id=1, source_target_pairs={{0,4},{4,0},{8,12},{12,8},{16,20},{20,16},{24,28},{28,24},{1,5},{5... | collective-permute-start | bytes 1253384 | tf_op jit(solution)/shard_map/ppermute | solution.py:153
  38.4 11.9 %collective-permute-start.14 = (bf16[3,32,2176]{2,1,0:T(8,128)(2,1)S(1)}, bf16[3,32,2176]{2,1,0:T(8,128)(2,1)S(1)}, u32[]{:S(2)}, u32[]{:S(2)}) collective-permute-start(bf16[3,32,2176]{2,1,0:T(8,128)(2,1)S(1)} %pad_maximum_fusion.refs_0_), channel_id=1, source_target_pairs={{0,2},{1,3},{2,0},{3,1},{4,6},{5,7},{6,4},{7,5},{8,10},{9,11},{10,... | collective-permute-start | bytes 1253384 | tf_op jit(solution)/shard_map/ppermute | solution.py:153
  38.7 11.5 %collective-permute-start.11 = (bf16[3,32,2176]{2,1,0:T(8,128)(2,1)S(1)}, bf16[3,32,2176]{2,1,0:T(8,128)(2,1)S(1)}, u32[]{:S(2)}, u32[]{:S(2)}) collective-permute-start(bf16[3,32,2176]{2,1,0:T(8,128)(2,1)S(1)} %pad_maximum_fusion.refs_0_), channel_id=1, source_target_pairs={{0,1},{1,0},{2,3},{3,2},{4,5},{5,4},{6,7},{7,6},{8,9},{9,8},{10,11... | collective-permute-start | bytes 1253384 | tf_op jit(solution)/shard_map/ppermute | solution.py:153
  39.2 9.8 %collective-permute-start.13 = (bf16[1,16,2176]{2,1,0:T(8,128)(2,1)S(1)}, bf16[1,16,2176]{2,1,0:T(8,128)(2,1)S(1)}, u32[]{:S(2)}, u32[]{:S(2)}) collective-permute-start(bf16[1,16,2176]{2,1,0:T(8,128)(2,1)S(1)} %slice.108), channel_id=1, source_target_pairs={{0,4},{4,0},{8,12},{12,8},{16,20},{20,16},{24,28},{28,24},{1,5},{5... | collective-permute-start | bytes 208904 | tf_op jit(solution)/shard_map/ppermute | solution.py:153
  40.7 9.6 %collective-permute-start.12 = (bf16[1,16,2176]{2,1,0:T(8,128)(2,1)S(1)}, bf16[1,16,2176]{2,1,0:T(8,128)(2,1)S(1)}, u32[]{:S(2)}, u32[]{:S(2)}) collective-permute-start(bf16[1,16,2176]{2,1,0:T(8,128)(2,1)S(1)} %slice.107), channel_id=1, source_target_pairs={{0,2},{1,3},{2,0},{3,1},{4,6},{5,7},{6,4},{7,5},{8,10},{9,11},{10,... | collective-permute-start | bytes 208904 | tf_op jit(solution)/shard_map/ppermute | solution.py:153
  50.3 9.8 %collective-permute-start.21 = (bf16[3,32,2176]{2,1,0:T(8,128)(2,1)S(1)}, bf16[3,32,2176]{2,1,0:T(8,128)(2,1)S(1)}, u32[]{:S(2)}, u32[]{:S(2)}) collective-permute-start(bf16[3,32,2176]{2,1,0:T(8,128)(2,1)S(1)} %collective-permute-done.15.refs_0_), channel_id=1, source_target_pairs={{0,1},{1,0},{2,3},{3,2},{4,5},{5,4},{6,7},{7,6},{8,9},{9,8},{10,11... | collective-permute-start | bytes 1253384 | tf_op jit(solution)/shard_map/ppermute | solution.py:153
  51.4 7.2 %collective-permute-start.22 = (bf16[3,16,2176]{2,1,0:T(8,128)(2,1)S(1)}, bf16[3,16,2176]{2,1,0:T(8,128)(2,1)S(1)}, u32[]{:S(2)}, u32[]{:S(2)}) collective-permute-start(bf16[3,16,2176]{2,1,0:T(8,128)(2,1)S(1)} %slice.109), channel_id=1, source_target_pairs={{0,2},{1,3},{2,0},{3,1},{4,6},{5,7},{6,4},{7,5},{8,10},{9,11},{10,... | collective-permute-start | bytes 626696 | tf_op jit(solution)/shard_map/ppermute | solution.py:153
  52.9 7.2 %collective-permute-start.23 = (bf16[3,16,2176]{2,1,0:T(8,128)(2,1)S(1)}, bf16[3,16,2176]{2,1,0:T(8,128)(2,1)S(1)}, u32[]{:S(2)}, u32[]{:S(2)}) collective-permute-start(bf16[3,16,2176]{2,1,0:T(8,128)(2,1)S(1)} %slice.110), channel_id=1, source_target_pairs={{0,4},{4,0},{8,12},{12,8},{16,20},{20,16},{24,28},{28,24},{1,5},{5... | collective-permute-start | bytes 626696 | tf_op jit(solution)/shard_map/ppermute | solution.py:153
  53.4 3.3 %collective-permute-start.19 = (bf16[1,16,2176]{2,1,0:T(8,128)(2,1)S(1)}, bf16[1,16,2176]{2,1,0:T(8,128)(2,1)S(1)}, u32[]{:S(2)}, u32[]{:S(2)}) collective-permute-start(bf16[1,16,2176]{2,1,0:T(8,128)(2,1)S(1)} %collective-permute-done.12.refs_6_), channel_id=1, source_target_pairs={{0,1},{1,0},{2,3},{3,2},{4,5},{5,4},{6,7},{7,6},{8,9},{9,8},{10,11... | collective-permute-start | bytes 208904 | tf_op jit(solution)/shard_map/ppermute | solution.py:153
  53.4 3.3 %collective-permute-start.20 = (bf16[1,16,2176]{2,1,0:T(8,128)(2,1)S(1)}, bf16[1,16,2176]{2,1,0:T(8,128)(2,1)S(1)}, u32[]{:S(2)}, u32[]{:S(2)}) collective-permute-start(bf16[1,16,2176]{2,1,0:T(8,128)(2,1)S(1)} %collective-permute-done.13.refs_7_), channel_id=1, source_target_pairs={{0,1},{1,0},{2,3},{3,2},{4,5},{5,4},{6,7},{7,6},{8,9},{9,8},{10,11... | collective-permute-start | bytes 208904 | tf_op jit(solution)/shard_map/ppermute | solution.py:153
  66.9 8.0 %collective-permute-start.27 = (bf16[1,3,128,512]{3,2,1,0:T(8,128)(2,1)S(1)}, bf16[1,3,128,512]{3,2,1,0:T(8,128)(2,1)S(1)}, u32[]{:S(2)}, u32[]{:S(2)}) collective-permute-start(bf16[1,3,128,512]{3,2,1,0:T(8,128)(2,1)S(1)} %get-tuple-element.188), channel_id=1, source_target_pairs={{0,1},{1,0},{2,3},{3,2},{4,5},{5,4},{6,7},{7,6},{8,9},{9,8},{10,11... | collective-permute-start | bytes 1179656 | tf_op jit(solution)/shard_map/ppermute | solution.py:153
  67.2 7.6 %collective-permute-start.28 = (bf16[1,3,128,512]{3,2,1,0:T(8,128)(2,1)S(1)}, bf16[1,3,128,512]{3,2,1,0:T(8,128)(2,1)S(1)}, u32[]{:S(2)}, u32[]{:S(2)}) collective-permute-start(bf16[1,3,128,512]{3,2,1,0:T(8,128)(2,1)S(1)} %get-tuple-element.189), channel_id=1, source_target_pairs={{0,1},{1,0},{2,3},{3,2},{4,5},{5,4},{6,7},{7,6},{8,9},{9,8},{10,11... | collective-permute-start | bytes 1179656 | tf_op jit(solution)/shard_map/ppermute | solution.py:153
  67.6 7.2 %collective-permute-start.30 = (bf16[3,64,512]{2,1,0:T(8,128)(2,1)S(1)}, bf16[3,64,512]{2,1,0:T(8,128)(2,1)S(1)}, u32[]{:S(2)}, u32[]{:S(2)}) collective-permute-start(bf16[3,64,512]{2,1,0:T(8,128)(2,1)S(1)} %get-tuple-element.223), channel_id=1, source_target_pairs={{0,2},{1,3},{2,0},{3,1},{4,6},{5,7},{6,4},{7,5},{8,10},{9,11},{10,... | collective-permute-start | bytes 589832 | tf_op jit(solution)/shard_map/ppermute | solution.py:153
  68.0 6.8 %collective-permute-start.29 = (bf16[3,64,512]{2,1,0:T(8,128)(2,1)S(1)}, bf16[3,64,512]{2,1,0:T(8,128)(2,1)S(1)}, u32[]{:S(2)}, u32[]{:S(2)}) collective-permute-start(bf16[3,64,512]{2,1,0:T(8,128)(2,1)S(1)} %get-tuple-element.224), channel_id=1, source_target_pairs={{0,4},{4,0},{8,12},{12,8},{16,20},{20,16},{24,28},{28,24},{1,5},{5... | collective-permute-start | bytes 589832 | tf_op jit(solution)/shard_map/ppermute | solution.py:153
  75.4 10.5 %collective-permute-start.34 = (bf16[3,128,512]{2,1,0:T(8,128)(2,1)S(1)}, bf16[3,128,512]{2,1,0:T(8,128)(2,1)S(1)}, u32[]{:S(2)}, u32[]{:S(2)}) collective-permute-start(bf16[3,128,512]{2,1,0:T(8,128)(2,1)S(1)} %pad_maximum_fusion.1), channel_id=1, source_target_pairs={{0,4},{4,0},{8,12},{12,8},{16,20},{20,16},{24,28},{28,24},{1,5},{5... | collective-permute-start | bytes 1179656 | tf_op jit(solution)/shard_map/ppermute | solution.py:153
  76.0 10.2 %collective-permute-start.35 = (bf16[3,128,512]{2,1,0:T(8,128)(2,1)S(1)}, bf16[3,128,512]{2,1,0:T(8,128)(2,1)S(1)}, u32[]{:S(2)}, u32[]{:S(2)}) collective-permute-start(bf16[3,128,512]{2,1,0:T(8,128)(2,1)S(1)} %pad_maximum_fusion.2), channel_id=1, source_target_pairs={{0,2},{1,3},{2,0},{3,1},{4,6},{5,7},{6,4},{7,5},{8,10},{9,11},{10,... | collective-permute-start | bytes 1179656 | tf_op jit(solution)/shard_map/ppermute | solution.py:153
  77.8 8.5 %collective-permute-start.33 = (bf16[1,3,128,512]{3,2,1,0:T(8,128)(2,1)S(1)}, bf16[1,3,128,512]{3,2,1,0:T(8,128)(2,1)S(1)}, u32[]{:S(2)}, u32[]{:S(2)}) collective-permute-start(bf16[1,3,128,512]{3,2,1,0:T(8,128)(2,1)S(1)} %get-tuple-element.195), channel_id=1, source_target_pairs={{0,1},{1,0},{2,3},{3,2},{4,5},{5,4},{6,7},{7,6},{8,9},{9,8},{10,11... | collective-permute-start | bytes 1179656 | tf_op jit(solution)/shard_map/ppermute | solution.py:153
  86.5 6.7 %collective-permute-start.37 = (bf16[128,512]{1,0:T(8,128)(2,1)S(1)}, bf16[128,512]{1,0:T(8,128)(2,1)S(1)}, u32[]{:S(2)}, u32[]{:S(2)}) collective-permute-start(bf16[128,512]{1,0:T(8,128)(2,1)S(1)} %get-tuple-element.221), channel_id=1, source_target_pairs={{0,8},{4,12},{8,0},{12,4},{16,24},{20,28},{24,16},{28,20},{1,9},{5... | collective-permute-start | bytes 393224 | tf_op jit(solution)/shard_map/ppermute | solution.py:153
  86.8 5.1 %collective-permute-start.39 = (bf16[1,64,512]{2,1,0:T(8,128)(2,1)S(1)}, bf16[1,64,512]{2,1,0:T(8,128)(2,1)S(1)}, u32[]{:S(2)}, u32[]{:S(2)}) collective-permute-start(bf16[1,64,512]{2,1,0:T(8,128)(2,1)S(1)} %get-tuple-element.225), channel_id=1, source_target_pairs={{0,2},{1,3},{2,0},{3,1},{4,6},{5,7},{6,4},{7,5},{8,10},{9,11},{10,... | collective-permute-start | bytes 196616 | tf_op jit(solution)/shard_map/ppermute | solution.py:153
  88.3 5.0 %collective-permute-start.38 = (bf16[1,64,512]{2,1,0:T(8,128)(2,1)S(1)}, bf16[1,64,512]{2,1,0:T(8,128)(2,1)S(1)}, u32[]{:S(2)}, u32[]{:S(2)}) collective-permute-start(bf16[1,64,512]{2,1,0:T(8,128)(2,1)S(1)} %get-tuple-element.226), channel_id=1, source_target_pairs={{0,4},{4,0},{8,12},{12,8},{16,20},{20,16},{24,28},{28,24},{1,5},{5... | collective-permute-start | bytes 196616 | tf_op jit(solution)/shard_map/ppermute | solution.py:153
  89.8 8.1 %collective-permute-start.36 = (bf16[128,512]{1,0:T(8,128)(2,1)S(1)}, bf16[128,512]{1,0:T(8,128)(2,1)S(1)}, u32[]{:S(2)}, u32[]{:S(2)}) collective-permute-start(bf16[128,512]{1,0:T(8,128)(2,1)S(1)} %get-tuple-element.222), channel_id=1, source_target_pairs={{0,8},{4,12},{8,0},{12,4},{16,24},{20,28},{24,16},{28,20},{1,9},{5... | collective-permute-start | bytes 393224 | tf_op jit(solution)/shard_map/ppermute | solution.py:153
  93.3 5.0 %collective-permute-start.41 = (bf16[1,128,512]{2,1,0:T(8,128)(2,1)S(1)}, bf16[1,128,512]{2,1,0:T(8,128)(2,1)S(1)}, u32[]{:S(2)}, u32[]{:S(2)}) collective-permute-start(bf16[1,128,512]{2,1,0:T(8,128)(2,1)S(1)} %pad_maximum_fusion.3), channel_id=1, source_target_pairs={{0,4},{4,0},{8,12},{12,8},{16,20},{20,16},{24,28},{28,24},{1,5},{5... | collective-permute-start | bytes 393224 | tf_op jit(solution)/shard_map/ppermute | solution.py:153
  94.9 5.9 %collective-permute-start.40 = (bf16[128,512]{1,0:T(8,128)(2,1)S(1)}, bf16[128,512]{1,0:T(8,128)(2,1)S(1)}, u32[]{:S(2)}, u32[]{:S(2)}) collective-permute-start(bf16[128,512]{1,0:T(8,128)(2,1)S(1)} %fusion.6), channel_id=1, source_target_pairs={{0,16},{4,20},{8,24},{12,28},{16,0},{20,4},{24,8},{28,12},{1,17},{... | collective-permute-start | bytes 393224 | tf_op jit(solution)/shard_map/ppermute | solution.py:153
  97.4 5.0 %collective-permute-start.42 = (bf16[1,128,512]{2,1,0:T(8,128)(2,1)S(1)}, bf16[1,128,512]{2,1,0:T(8,128)(2,1)S(1)}, u32[]{:S(2)}, u32[]{:S(2)}) collective-permute-start(bf16[1,128,512]{2,1,0:T(8,128)(2,1)S(1)} %pad_maximum_fusion.4), channel_id=1, source_target_pairs={{0,2},{1,3},{2,0},{3,1},{4,6},{5,7},{6,4},{7,5},{8,10},{9,11},{10,... | collective-permute-start | bytes 393224 | tf_op jit(solution)/shard_map/ppermute | solution.py:153
  (18 other events, 192.1 us)

commit v14 on v12

--- a/solution.py
+++ b/solution.py
@@ -552,11 +552,20 @@
     return flip(part[:, :half], "req", 1), flip(part[:, half:], "tp", 2)
 
 
+def with_lower(sums, part):
+    half = part.shape[1]
+    sums = [sums[:, :half] + part.astype(jnp.float32), sums[:, half:]]
+    return jnp.concatenate(sums, axis=1).astype(jnp.bfloat16)
+
+
+def with_upper(sums, part):
+    half = part.shape[1]
+    sums = [sums[:, :half], sums[:, half:] + part.astype(jnp.float32)]
+    return jnp.concatenate(sums, axis=1).astype(jnp.bfloat16)
+
+
 def neighbours(to_x, to_y, by_x, by_y):
-    half = by_x.shape[1]
-    to_y = jnp.concatenate([to_y[:, :half] + by_x.astype(jnp.float32), to_y[:, half:]], axis=1)
-    to_x = jnp.concatenate([to_x[:, :half], to_x[:, half:] + by_y.astype(jnp.float32)], axis=1)
-    return flip(to_x.astype(jnp.bfloat16), "req", 1), flip(to_y.astype(jnp.bfloat16), "tp", 2)
+    return flip(with_upper(to_x, by_y), "req", 1), flip(with_lower(to_y, by_x), "tp", 2)
 
 
 def moe_dense(
@@ -600,37 +609,44 @@
         flip(y_0, "tp", 1),
     )
     y_3, x_3 = flip(line_3, "tp", 2), flip(line_3, "req", 1)
+    x_core_0, across_core_0, core_3, y_3, x_3 = ordered(
+        flip(x_0, "tp", 1), other_core(across_0), flip(line_3, "tp", 1), y_3, x_3
+    )
     all_0 = run_experts(
         near_pieces(0, line_0, core_0)
         + far_pieces(0, (y_0,), (y_core_0,))
-        + near_pieces(1, x_0, flip(x_0, "tp", 1))
-        + far_pieces(1, across_0, other_core(across_0)),
+        + near_pieces(1, x_0, x_core_0)
+        + far_pieces(1, across_0, across_core_0),
         weights,
         token_count,
         residual,
     )
-    all_0, core_3, y_3, x_3 = ordered(all_0, flip(line_3, "tp", 1), y_3, x_3)
-    y_core_3, x_core_3 = other_core((y_3, x_3))
-    near_3 = run_experts(
-        near_pieces(0, line_3, core_3) + far_pieces(0, (y_3,), (y_core_3,)), weights, token_count
-    )
-    near_3, x_core_3, across_3 = ordered(near_3, x_core_3, across_parts(x_3, y_3))
+    x_core_3, all_0, y_3, across_3 = ordered(
+        flip(x_3, "tp", 1), all_0, y_3, jnp.concatenate(across_parts(x_3, y_3), axis=1)
+    )
     side_3 = run_experts(
-        near_pieces(0, x_3, x_core_3) + far_pieces(0, across_3, other_core(across_3)),
+        near_pieces(0, x_3, x_core_3) + far_pieces(0, (across_3,), (flip(across_3, "tp", 1),)),
         weights,
         token_count,
     )
-    all_0, near_3, side_3 = ordered(all_0, near_3, side_3)
-    keep, (send, first) = side_3
-    all_0, near_3, keep, send, first = ordered(all_0, near_3, keep, send, flip(first, "tp", 1))
-    relay_3 = relayed(joined((keep, (send, first)), 0, 1))
-    near_keep, (near_send, near_first) = near_3
-    all_0, near_send, near_first, send, relay_3 = ordered(
-        all_0, near_send, flip(near_first, "tp", 1), flip(send, "tp", 1), relay_3
-    )
-    sums_3 = neighbours(
-        joined((keep, (send, first)), 0, 0), joined((near_keep, (near_send, near_first)), 0, 1), *relay_3
-    )
+    y_core_3, all_0, (keep, (send, first)) = ordered(flip(y_3, "tp", 1), all_0, side_3)
+    all_0, y_core_3, keep, send, first = ordered(all_0, y_core_3, keep, send, flip(first, "tp", 1))
+    diagonal, keep, send = ordered(joined((keep, (send, first)), 0, 1).astype(jnp.bfloat16), keep, send)
+    by_x, by_y = relayed(diagonal)
+    near_keep, (near_send, near_first) = run_experts(
+        near_pieces(0, line_3, core_3) + far_pieces(0, (y_3,), (y_core_3,)), weights, token_count
+    )
+    send = flip(send, "tp", 1)
+    all_0, near_keep, near_send, near_first, by_x, to_x = ordered(
+        all_0,
+        near_keep,
+        near_send,
+        flip(near_first, "tp", 1),
+        by_x.astype(jnp.float32),
+        with_upper(joined((keep, (send, first)), 0, 0), by_y),
+    )
+    to_y = with_lower(joined((near_keep, (near_send, near_first)), 0, 1), by_x)
+    sums_3 = flip(to_x, "req", 1), flip(to_y, "tp", 2)
     all_0, near_send, sums_3 = ordered(with_core(all_0), flip(near_send, "tp", 1), sums_3)
     near_3 = (near_keep, (near_send, near_first))
     sent = joined(near_3, 0, 0) + sums_3[0].astype(jnp.float32) + sums_3[1].astype(jnp.float32)

time: 102 us -> 102 us (level)
  starting transfers between devices: 31.5 us -> 32.9 us
    ppermute x43 -> x42, starting transfers between devices: 31.5 us -> 32.9 us  [flip(): lax.ppermute(value, axis, [(i, i ^ bits) for i in range(lax.axis_size(axi...]
    ppermute x43 -> x42, waiting for transfers between devices: 50.4 us -> 49.6 us  [flip(): lax.ppermute(value, axis, [(i, i ^ bits) for i in range(lax.axis_size(axi...]
  transfers between devices with their start and end apart: 43 -> 42, of which waited for: 28 -> 26; matrix products, arithmetic and copies ran while one was open for 1% -> 1% of each run, Pallas kernels for 9% -> 12%
where the time goes in v14:
time: 102 us
  waiting for transfers between devices  49.6 us (49%)
  starting transfers between devices  32.9 us (32%)
  Pallas kernels  17.7 us (17%)
  other arithmetic  1.21 us (1%)
    ppermute x42, waiting for transfers between devices, flip(): lax.ppermute(value, axis, [(i, i ^ bits) for i in range(lax.axis_size(axi...  49.6 us
    ppermute x42, starting transfers between devices, flip(): lax.ppermute(value, axis, [(i, i ^ bits) for i in range(lax.axis_size(axi...  32.9 us
    pallas_call x3, Pallas kernels, run_experts(): pl.pallas_call(functools.partial(experts_kernel, plan, len(residual)), ou...  7.44 us
    pallas_call x1, Pallas kernels, attention_shares(): pl.pallas_call(attention_kernel, out_shape=[jax.ShapeDtypeStruct(share, j...  4.88 us
    pallas_call x1, Pallas kernels, attention_shares(): pl.pallas_call(stage_kernel, out_shape=[rope, rope, pltpu.VMEM((1, POOL *...  4.41 us
  transfers between devices with their start and end apart: 42, of which 26 were waited for; matrix products, arithmetic and copies ran while one was open for 1% of the time, Pallas kernels for 12%

profile of v14, /device:TPU:0, one launch (start us, length us, event | category | flops | bytes accessed | tf_op | source)
XLA Modules:
  0.0 102.0 jit_solution(16255767013917884733)
XLA Ops:
  0.0 3.0 %collective-permute-start.1 = (bf16[128,512]{1,0:T(8,128)(2,1)}, bf16[128,512]{1,0:T(8,128)(2,1)S(1)}, u32[]{:S(2)}, u32[]{:S(2)}) collective-permute-start(bf16[128,512]{1,0:T(8,128)(2,1)} %refs_0_.3), channel_id=1, source_target_pairs={{0,2},{1,3},{2,0},{3,1},{4,6},{5,7},{6,4},{7,5},{8,10},{9,11},{10,... | collective-permute-start | bytes 393224 | tf_op jit(solution)/shard_map/ppermute | solution.py:153
  3.0 4.4 %stage.1 = (f32[128,128]{1,0:T(8,128)S(1)}, f32[128,128]{1,0:T(8,128)S(1)}, s32[1,6144]{1,0:T(1,128)S(1)}, f32[1,2048]{1,0:T(1,128)S(1)}, f32[1,128]{1,0:T(1,128...) custom-call(s32[9]{0:T(128)} %refs_0_.2, ...), custom_call_target="tpu_custom_call" | custom-call | tf_op jit(solution)/shard_map/stage/pallas_call | solution.py:373
  9.0 4.9 %attention.1 = (f32[32,2048]{1,0:T(8,128)S(1)}, f32[32,2048]{1,0:T(8,128)S(1)}, bf16[2,32,2048]{2,1,0:T(8,128)(2,1)S(1)}) custom-call(bf16[128,512]{1,0:T(8,128)(2,1)S(1)} %copy-done.3, bf16[128,512]{1,0:T(8,128)(2,1)S(1)} %collective-permute-done.refs_1_, bf16[128,512]{1,0:T(8,128)(2,1)S(1)} %collective-permute-done.1.refs_2_, ...), custom_call_target="tpu_custom_call" | custom-call | tf_op jit(solution)/shard_map/attention/pallas_call | solution.py:393
  16.4 4.9 %collective-permute-done.4.far_ref = bf16[32,2048]{1,0:T(8,128)(2,1)S(1)} collective-permute-done((bf16[32,2048]{1,0:T(8,128)(2,1)S(1)}, bf16[32,2048]{1,0:T(8,128)(2,1)S(1)}, u32[]{:S(2)}, u32[]{:S(2)}) %collective-permute-start.4) | collective-permute-done | bytes 131104 | tf_op jit(solution)/shard_map/ppermute | solution.py:153
  21.5 2.7 %collective-permute-start.6 = (bf16[1,32,2176]{2,1,0:T(8,128)(2,1)S(1)}, bf16[1,32,2176]{2,1,0:T(8,128)(2,1)S(1)}, u32[]{:S(2)}, u32[]{:S(2)}) collective-permute-start(bf16[1,32,2176]{2,1,0:T(8,128)(2,1)S(1)} %bitcast.85), channel_id=1, source_target_pairs={{0,16},{4,20},{8,24},{12,28},{16,0},{20,4},{24,8},{28,12},{1,17},{... | collective-permute-start | bytes 417800 | tf_op jit(solution)/shard_map/ppermute | solution.py:153
  24.2 1.6 %collective-permute-start.5 = (bf16[1,32,2176]{2,1,0:T(8,128)(2,1)S(1)}, bf16[1,32,2176]{2,1,0:T(8,128)(2,1)S(1)}, u32[]{:S(2)}, u32[]{:S(2)}) collective-permute-start(bf16[1,32,2176]{2,1,0:T(8,128)(2,1)S(1)} %bitcast.86), channel_id=1, source_target_pairs={{0,8},{4,12},{8,0},{12,4},{16,24},{20,28},{24,16},{28,20},{1,9},{5... | collective-permute-start | bytes 417800 | tf_op jit(solution)/shard_map/ppermute | solution.py:153
  25.8 3.8 %collective-permute-start.8 = (bf16[1,32,2176]{2,1,0:T(8,128)(2,1)S(1)}, bf16[1,32,2176]{2,1,0:T(8,128)(2,1)S(1)}, u32[]{:S(2)}, u32[]{:S(2)}) collective-permute-start(bf16[1,32,2176]{2,1,0:T(8,128)(2,1)S(1)} %bitcast.87), channel_id=1, source_target_pairs={{0,4},{4,0},{8,12},{12,8},{16,20},{20,16},{24,28},{28,24},{1,5},{5... | collective-permute-start | bytes 417800 | tf_op jit(solution)/shard_map/ppermute | solution.py:153
  31.0 1.6 %collective-permute-done.8.refs_4_ = bf16[1,32,2176]{2,1,0:T(8,128)(2,1)S(1)} collective-permute-done((bf16[1,32,2176]{2,1,0:T(8,128)(2,1)S(1)}, bf16[1,32,2176]{2,1,0:T(8,128)(2,1)S(1)}, u32[]{:S(2)}, u32[]{:S(2)}) %collective-permute-start.8) | collective-permute-done | bytes 139296 | tf_op jit(solution)/shard_map/ppermute | solution.py:153
  32.6 2.0 %collective-permute-done.7.refs_2_ = bf16[1,32,2176]{2,1,0:T(8,128)(2,1)S(1)} collective-permute-done((bf16[1,32,2176]{2,1,0:T(8,128)(2,1)S(1)}, bf16[1,32,2176]{2,1,0:T(8,128)(2,1)S(1)}, u32[]{:S(2)}, u32[]{:S(2)}) %collective-permute-start.7) | collective-permute-done | bytes 139296 | tf_op jit(solution)/shard_map/ppermute | solution.py:153
  35.8 3.8 %collective-permute-done.10 = bf16[1,32,2176]{2,1,0:T(8,128)(2,1)S(1)} collective-permute-done((bf16[1,32,2176]{2,1,0:T(8,128)(2,1)S(1)}, bf16[1,32,2176]{2,1,0:T(8,128)(2,1)S(1)}, u32[]{:S(2)}, u32[]{:S(2)}) %collective-permute-start.10) | collective-permute-done | bytes 139296 | tf_op jit(solution)/shard_map/ppermute | solution.py:153
  39.8 1.7 %collective-permute-start.19 = (bf16[3,32,2176]{2,1,0:T(8,128)(2,1)S(1)}, bf16[3,32,2176]{2,1,0:T(8,128)(2,1)S(1)}, u32[]{:S(2)}, u32[]{:S(2)}) collective-permute-start(bf16[3,32,2176]{2,1,0:T(8,128)(2,1)S(1)} %pad_maximum_fusion.refs_0_), channel_id=1, source_target_pairs={{0,4},{4,0},{8,12},{12,8},{16,20},{20,16},{24,28},{28,24},{1,5},{5... | collective-permute-start | bytes 1253384 | tf_op jit(solution)/shard_map/ppermute | solution.py:153
  42.6 1.4 %collective-permute-done.9.refs_5_ = bf16[1,32,2176]{2,1,0:T(8,128)(2,1)S(1)} collective-permute-done((bf16[1,32,2176]{2,1,0:T(8,128)(2,1)S(1)}, bf16[1,32,2176]{2,1,0:T(8,128)(2,1)S(1)}, u32[]{:S(2)}, u32[]{:S(2)}) %collective-permute-start.9) | collective-permute-done | bytes 139296 | tf_op jit(solution)/shard_map/ppermute | solution.py:153
  45.3 5.1 %collective-permute-done.19.refs_0_ = bf16[3,32,2176]{2,1,0:T(8,128)(2,1)S(1)} collective-permute-done((bf16[3,32,2176]{2,1,0:T(8,128)(2,1)S(1)}, bf16[3,32,2176]{2,1,0:T(8,128)(2,1)S(1)}, u32[]{:S(2)}, u32[]{:S(2)}) %collective-permute-start.19) | collective-permute-done | bytes 417824 | tf_op jit(solution)/shard_map/ppermute | solution.py:153
  52.8 2.0 %experts.3 = (f32[2,2,1,128,512]{4,3,2,1,0:T(8,128)S(1)}, bf16[2,1,128,512]{3,2,1,0:T(8,128)(2,1)S(1)}, bf16[2,1,128,512]{3,2,1,0:T(8,128)(2,1)S(1)}) custom-call(bf16[1,32,2176]{2,1,0:T(8,128)(2,1)S(1)} %bitcast.90, bf16[1,32,2176]{2,1,0:T(8,128)(2,1)S(1)} %collective-permute-done.13.refs_1_, bf16[1,32,2176]{2,1,0:T(8,128)(2,1)S(1)} %collective-permute-done.7.refs_2_, ...), custom_call_target="tpu_custom_call" | custom-call | tf_op jit(solution)/shard_map/experts/pallas_call | solution.py:490
  54.8 2.6 %collective-permute-done.21 = bf16[3,16,2176]{2,1,0:T(8,128)(2,1)S(1)} collective-permute-done((bf16[3,16,2176]{2,1,0:T(8,128)(2,1)S(1)}, bf16[3,16,2176]{2,1,0:T(8,128)(2,1)S(1)}, u32[]{:S(2)}, u32[]{:S(2)}) %collective-permute-start.21) | collective-permute-done | bytes 208928 | tf_op jit(solution)/shard_map/ppermute | solution.py:153
  58.5 1.2 %collective-permute-done.24.refs_3_ = bf16[3,32,2176]{2,1,0:T(8,128)(2,1)S(1)} collective-permute-done((bf16[3,32,2176]{2,1,0:T(8,128)(2,1)S(1)}, bf16[3,32,2176]{2,1,0:T(8,128)(2,1)S(1)}, u32[]{:S(2)}, u32[]{:S(2)}) %collective-permute-start.24) | collective-permute-done | bytes 417824 | tf_op jit(solution)/shard_map/ppermute | solution.py:153
  59.8 2.7 %experts.4 = (f32[1,2,3,128,512]{4,3,2,1,0:T(8,128)S(1)}, bf16[1,3,128,512]{3,2,1,0:T(8,128)(2,1)S(1)}, bf16[1,3,128,512]{3,2,1,0:T(8,128)(2,1)S(1)}) custom-call(bf16[3,32,2176]{2,1,0:T(8,128)(2,1)S(1)} %collective-permute-done.19.refs_0_, bf16[3,32,2176]{2,1,0:T(8,128)(2,1)S(1)} %collective-permute-done.20.refs_1_, ...), custom_call_target="tpu_custom_call" | custom-call | tf_op jit(solution)/shard_map/experts/pallas_call | solution.py:490
  62.7 1.6 %collective-permute-done.25 = bf16[1,3,128,512]{3,2,1,0:T(8,128)(2,1)S(1)} collective-permute-done((bf16[1,3,128,512]{3,2,1,0:T(8,128)(2,1)S(1)}, bf16[1,3,128,512]{3,2,1,0:T(8,128)(2,1)S(1)}, u32[]{:S(2)}, u32[]{:S(2)}) %collective-permute-start.25) | collective-permute-done | bytes 393248 | tf_op jit(solution)/shard_map/ppermute | solution.py:153
  65.4 1.5 %collective-permute-start.29 = (bf16[3,64,512]{2,1,0:T(8,128)(2,1)S(1)}, bf16[3,64,512]{2,1,0:T(8,128)(2,1)S(1)}, u32[]{:S(2)}, u32[]{:S(2)}) collective-permute-start(bf16[3,64,512]{2,1,0:T(8,128)(2,1)S(1)} %get-tuple-element.231), channel_id=1, source_target_pairs={{0,2},{1,3},{2,0},{3,1},{4,6},{5,7},{6,4},{7,5},{8,10},{9,11},{10,... | collective-permute-start | bytes 589832 | tf_op jit(solution)/shard_map/ppermute | solution.py:153
  66.9 2.7 %experts.5 = (f32[1,2,3,128,512]{4,3,2,1,0:T(8,128)S(1)}, bf16[1,3,128,512]{3,2,1,0:T(8,128)(2,1)S(1)}, bf16[1,3,128,512]{3,2,1,0:T(8,128)(2,1)S(1)}) custom-call(bf16[3,32,2176]{2,1,0:T(8,128)(2,1)S(1)} %pad_maximum_fusion.refs_0_, bf16[3,32,2176]{2,1,0:T(8,128)(2,1)S(1)} %collective-permute-done.17.refs_1_, ...), custom_call_target="tpu_custom_call" | custom-call | tf_op jit(solution)/shard_map/experts/pallas_call | solution.py:490
  69.7 2.2 %collective-permute-done.27 = bf16[3,64,512]{2,1,0:T(8,128)(2,1)S(1)} collective-permute-done((bf16[3,64,512]{2,1,0:T(8,128)(2,1)S(1)}, bf16[3,64,512]{2,1,0:T(8,128)(2,1)S(1)}, u32[]{:S(2)}, u32[]{:S(2)}) %collective-permute-start.27) | collective-permute-done | bytes 196640 | tf_op jit(solution)/shard_map/ppermute | solution.py:153
  72.5 1.4 %collective-permute-start.33 = (bf16[3,128,512]{2,1,0:T(8,128)(2,1)S(1)}, bf16[3,128,512]{2,1,0:T(8,128)(2,1)S(1)}, u32[]{:S(2)}, u32[]{:S(2)}) collective-permute-start(bf16[3,128,512]{2,1,0:T(8,128)(2,1)S(1)} %pad_maximum_fusion.2), channel_id=1, source_target_pairs={{0,4},{4,0},{8,12},{12,8},{16,20},{20,16},{24,28},{28,24},{1,5},{5... | collective-permute-start | bytes 1179656 | tf_op jit(solution)/shard_map/ppermute | solution.py:153
  74.2 1.5 %collective-permute-start.34 = (bf16[3,128,512]{2,1,0:T(8,128)(2,1)S(1)}, bf16[3,128,512]{2,1,0:T(8,128)(2,1)S(1)}, u32[]{:S(2)}, u32[]{:S(2)}) collective-permute-start(bf16[3,128,512]{2,1,0:T(8,128)(2,1)S(1)} %pad_maximum_fusion.3), channel_id=1, source_target_pairs={{0,2},{1,3},{2,0},{3,1},{4,6},{5,7},{6,4},{7,5},{8,10},{9,11},{10,... | collective-permute-start | bytes 1179656 | tf_op jit(solution)/shard_map/ppermute | solution.py:153
  77.6 6.4 %collective-permute-done.33 = bf16[3,128,512]{2,1,0:T(8,128)(2,1)S(1)} collective-permute-done((bf16[3,128,512]{2,1,0:T(8,128)(2,1)S(1)}, bf16[3,128,512]{2,1,0:T(8,128)(2,1)S(1)}, u32[]{:S(2)}, u32[]{:S(2)}) %collective-permute-start.33) | collective-permute-done | bytes 393248 | tf_op jit(solution)/shard_map/ppermute | solution.py:153
  84.0 1.4 %collective-permute-done.34 = bf16[3,128,512]{2,1,0:T(8,128)(2,1)S(1)} collective-permute-done((bf16[3,128,512]{2,1,0:T(8,128)(2,1)S(1)}, bf16[3,128,512]{2,1,0:T(8,128)(2,1)S(1)}, u32[]{:S(2)}, u32[]{:S(2)}) %collective-permute-start.34) | collective-permute-done | bytes 393248 | tf_op jit(solution)/shard_map/ppermute | solution.py:153
  85.7 2.1 %collective-permute-start.36 = (bf16[128,512]{1,0:T(8,128)(2,1)S(1)}, bf16[128,512]{1,0:T(8,128)(2,1)S(1)}, u32[]{:S(2)}, u32[]{:S(2)}) collective-permute-start(bf16[128,512]{1,0:T(8,128)(2,1)S(1)} %get-tuple-element.229), channel_id=1, source_target_pairs={{0,8},{4,12},{8,0},{12,4},{16,24},{20,28},{24,16},{28,20},{1,9},{5... | collective-permute-start | bytes 393224 | tf_op jit(solution)/shard_map/ppermute | solution.py:153
  87.9 1.5 %collective-permute-start.38 = (bf16[1,64,512]{2,1,0:T(8,128)(2,1)S(1)}, bf16[1,64,512]{2,1,0:T(8,128)(2,1)S(1)}, u32[]{:S(2)}, u32[]{:S(2)}) collective-permute-start(bf16[1,64,512]{2,1,0:T(8,128)(2,1)S(1)} %get-tuple-element.233), channel_id=1, source_target_pairs={{0,2},{1,3},{2,0},{3,1},{4,6},{5,7},{6,4},{7,5},{8,10},{9,11},{10,... | collective-permute-start | bytes 196616 | tf_op jit(solution)/shard_map/ppermute | solution.py:153
  90.2 2.1 %collective-permute-done.38 = bf16[1,64,512]{2,1,0:T(8,128)(2,1)S(1)} collective-permute-done((bf16[1,64,512]{2,1,0:T(8,128)(2,1)S(1)}, bf16[1,64,512]{2,1,0:T(8,128)(2,1)S(1)}, u32[]{:S(2)}, u32[]{:S(2)}) %collective-permute-start.38) | collective-permute-done | bytes 65568 | tf_op jit(solution)/shard_map/ppermute | solution.py:153
  92.3 1.5 %collective-permute-done.37 = bf16[1,64,512]{2,1,0:T(8,128)(2,1)S(1)} collective-permute-done((bf16[1,64,512]{2,1,0:T(8,128)(2,1)S(1)}, bf16[1,64,512]{2,1,0:T(8,128)(2,1)S(1)}, u32[]{:S(2)}, u32[]{:S(2)}) %collective-permute-start.37) | collective-permute-done | bytes 65568 | tf_op jit(solution)/shard_map/ppermute | solution.py:153
  95.4 1.4 %collective-permute-start.41 = (bf16[1,128,512]{2,1,0:T(8,128)(2,1)S(1)}, bf16[1,128,512]{2,1,0:T(8,128)(2,1)S(1)}, u32[]{:S(2)}, u32[]{:S(2)}) collective-permute-start(bf16[1,128,512]{2,1,0:T(8,128)(2,1)S(1)} %pad_maximum_fusion.6), channel_id=1, source_target_pairs={{0,2},{1,3},{2,0},{3,1},{4,6},{5,7},{6,4},{7,5},{8,10},{9,11},{10,... | collective-permute-start | bytes 393224 | tf_op jit(solution)/shard_map/ppermute | solution.py:153
  96.8 2.0 %collective-permute-done.40.x_ref = bf16[1,128,512]{2,1,0:T(8,128)(2,1)S(1)} collective-permute-done((bf16[1,128,512]{2,1,0:T(8,128)(2,1)S(1)}, bf16[1,128,512]{2,1,0:T(8,128)(2,1)S(1)}, u32[]{:S(2)}, u32[]{:S(2)}) %collective-permute-start.40) | collective-permute-done | bytes 131104 | tf_op jit(solution)/shard_map/ppermute | solution.py:153
  98.9 2.4 %collective-permute-done.39.z2_ref = bf16[128,512]{1,0:T(8,128)(2,1)S(1)} collective-permute-done((bf16[128,512]{1,0:T(8,128)(2,1)S(1)}, bf16[128,512]{1,0:T(8,128)(2,1)S(1)}, u32[]{:S(2)}, u32[]{:S(2)}) %collective-permute-start.39) | collective-permute-done | bytes 131104 | tf_op jit(solution)/shard_map/ppermute | solution.py:153
  (104 shorter events, 20.4 us)
Async XLA Ops:
  0.0 7.4 %collective-permute-start.1 = (bf16[128,512]{1,0:T(8,128)(2,1)}, bf16[128,512]{1,0:T(8,128)(2,1)S(1)}, u32[]{:S(2)}, u32[]{:S(2)}) collective-permute-start(bf16[128,512]{1,0:T(8,128)(2,1)} %refs_0_.3), channel_id=1, source_target_pairs={{0,2},{1,3},{2,0},{3,1},{4,6},{5,7},{6,4},{7,5},{8,10},{9,11},{10,... | collective-permute-start | bytes 393224 | tf_op jit(solution)/shard_map/ppermute | solution.py:153
  3.0 5.0 %collective-permute-start = (bf16[128,512]{1,0:T(8,128)(2,1)}, bf16[128,512]{1,0:T(8,128)(2,1)S(1)}, u32[]{:S(2)}, u32[]{:S(2)}) collective-permute-start(bf16[128,512]{1,0:T(8,128)(2,1)} %refs_0_.3), channel_id=1, source_target_pairs={{0,1},{1,0},{2,3},{3,2},{4,5},{5,4},{6,7},{7,6},{8,9},{9,8},{10,11... | collective-permute-start | bytes 393224 | tf_op jit(solution)/shard_map/ppermute | solution.py:153
  15.5 5.8 %collective-permute-start.4 = (bf16[32,2048]{1,0:T(8,128)(2,1)S(1)}, bf16[32,2048]{1,0:T(8,128)(2,1)S(1)}, u32[]{:S(2)}, u32[]{:S(2)}) collective-permute-start(bf16[32,2048]{1,0:T(8,128)(2,1)S(1)} %fusion.8), channel_id=1, source_target_pairs={{0,2},{1,3},{2,0},{3,1},{4,6},{5,7},{6,4},{7,5},{8,10},{9,11},{10,... | collective-permute-start | bytes 393224 | tf_op jit(solution)/shard_map/ppermute | solution.py:153
  21.5 9.2 %collective-permute-start.6 = (bf16[1,32,2176]{2,1,0:T(8,128)(2,1)S(1)}, bf16[1,32,2176]{2,1,0:T(8,128)(2,1)S(1)}, u32[]{:S(2)}, u32[]{:S(2)}) collective-permute-start(bf16[1,32,2176]{2,1,0:T(8,128)(2,1)S(1)} %bitcast.85), channel_id=1, source_target_pairs={{0,16},{4,20},{8,24},{12,28},{16,0},{20,4},{24,8},{28,12},{1,17},{... | collective-permute-start | bytes 417800 | tf_op jit(solution)/shard_map/ppermute | solution.py:153
  24.2 6.7 %collective-permute-start.5 = (bf16[1,32,2176]{2,1,0:T(8,128)(2,1)S(1)}, bf16[1,32,2176]{2,1,0:T(8,128)(2,1)S(1)}, u32[]{:S(2)}, u32[]{:S(2)}) collective-permute-start(bf16[1,32,2176]{2,1,0:T(8,128)(2,1)S(1)} %bitcast.86), channel_id=1, source_target_pairs={{0,8},{4,12},{8,0},{12,4},{16,24},{20,28},{24,16},{28,20},{1,9},{5... | collective-permute-start | bytes 417800 | tf_op jit(solution)/shard_map/ppermute | solution.py:153
  25.8 6.8 %collective-permute-start.8 = (bf16[1,32,2176]{2,1,0:T(8,128)(2,1)S(1)}, bf16[1,32,2176]{2,1,0:T(8,128)(2,1)S(1)}, u32[]{:S(2)}, u32[]{:S(2)}) collective-permute-start(bf16[1,32,2176]{2,1,0:T(8,128)(2,1)S(1)} %bitcast.87), channel_id=1, source_target_pairs={{0,4},{4,0},{8,12},{12,8},{16,20},{20,16},{24,28},{28,24},{1,5},{5... | collective-permute-start | bytes 417800 | tf_op jit(solution)/shard_map/ppermute | solution.py:153
  29.6 5.1 %collective-permute-start.7 = (bf16[1,32,2176]{2,1,0:T(8,128)(2,1)S(1)}, bf16[1,32,2176]{2,1,0:T(8,128)(2,1)S(1)}, u32[]{:S(2)}, u32[]{:S(2)}) collective-permute-start(bf16[1,32,2176]{2,1,0:T(8,128)(2,1)S(1)} %bitcast.88), channel_id=1, source_target_pairs={{0,2},{1,3},{2,0},{3,1},{4,6},{5,7},{6,4},{7,5},{8,10},{9,11},{10,... | collective-permute-start | bytes 417800 | tf_op jit(solution)/shard_map/ppermute | solution.py:153
  34.6 5.1 %collective-permute-start.10 = (bf16[1,32,2176]{2,1,0:T(8,128)(2,1)S(1)}, bf16[1,32,2176]{2,1,0:T(8,128)(2,1)S(1)}, u32[]{:S(2)}, u32[]{:S(2)}) collective-permute-start(bf16[1,32,2176]{2,1,0:T(8,128)(2,1)S(1)} %collective-permute-done.6), channel_id=1, source_target_pairs={{0,8},{4,12},{8,0},{12,4},{16,24},{20,28},{24,16},{28,20},{1,9},{5... | collective-permute-start | bytes 417800 | tf_op jit(solution)/shard_map/ppermute | solution.py:153
  34.6 5.1 %collective-permute-start.13 = (bf16[1,32,2176]{2,1,0:T(8,128)(2,1)S(1)}, bf16[1,32,2176]{2,1,0:T(8,128)(2,1)S(1)}, u32[]{:S(2)}, u32[]{:S(2)}) collective-permute-start(bf16[1,32,2176]{2,1,0:T(8,128)(2,1)S(1)} %bitcast.89), channel_id=1, source_target_pairs={{0,1},{1,0},{2,3},{3,2},{4,5},{5,4},{6,7},{7,6},{8,9},{9,8},{10,11... | collective-permute-start | bytes 417800 | tf_op jit(solution)/shard_map/ppermute | solution.py:153
  34.6 5.1 %collective-permute-start.14 = (bf16[1,32,2176]{2,1,0:T(8,128)(2,1)S(1)}, bf16[1,32,2176]{2,1,0:T(8,128)(2,1)S(1)}, u32[]{:S(2)}, u32[]{:S(2)}) collective-permute-start(bf16[1,32,2176]{2,1,0:T(8,128)(2,1)S(1)} %collective-permute-done.7.refs_2_), channel_id=1, source_target_pairs={{0,1},{1,0},{2,3},{3,2},{4,5},{5,4},{6,7},{7,6},{8,9},{9,8},{10,11... | collective-permute-start | bytes 417800 | tf_op jit(solution)/shard_map/ppermute | solution.py:153
  35.2 4.6 %collective-permute-start.12 = (bf16[1,16,2176]{2,1,0:T(8,128)(2,1)S(1)}, bf16[1,16,2176]{2,1,0:T(8,128)(2,1)S(1)}, u32[]{:S(2)}, u32[]{:S(2)}) collective-permute-start(bf16[1,16,2176]{2,1,0:T(8,128)(2,1)S(1)} %slice.108), channel_id=1, source_target_pairs={{0,4},{4,0},{8,12},{12,8},{16,20},{20,16},{24,28},{28,24},{1,5},{5... | collective-permute-start | bytes 208904 | tf_op jit(solution)/shard_map/ppermute | solution.py:153
  35.3 4.5 %collective-permute-start.11 = (bf16[1,16,2176]{2,1,0:T(8,128)(2,1)S(1)}, bf16[1,16,2176]{2,1,0:T(8,128)(2,1)S(1)}, u32[]{:S(2)}, u32[]{:S(2)}) collective-permute-start(bf16[1,16,2176]{2,1,0:T(8,128)(2,1)S(1)} %slice.107), channel_id=1, source_target_pairs={{0,2},{1,3},{2,0},{3,1},{4,6},{5,7},{6,4},{7,5},{8,10},{9,11},{10,... | collective-permute-start | bytes 208904 | tf_op jit(solution)/shard_map/ppermute | solution.py:153
  39.8 10.6 %collective-permute-start.19 = (bf16[3,32,2176]{2,1,0:T(8,128)(2,1)S(1)}, bf16[3,32,2176]{2,1,0:T(8,128)(2,1)S(1)}, u32[]{:S(2)}, u32[]{:S(2)}) collective-permute-start(bf16[3,32,2176]{2,1,0:T(8,128)(2,1)S(1)} %pad_maximum_fusion.refs_0_), channel_id=1, source_target_pairs={{0,4},{4,0},{8,12},{12,8},{16,20},{20,16},{24,28},{28,24},{1,5},{5... | collective-permute-start | bytes 1253384 | tf_op jit(solution)/shard_map/ppermute | solution.py:153
  41.5 9.9 %collective-permute-start.18 = (bf16[3,32,2176]{2,1,0:T(8,128)(2,1)S(1)}, bf16[3,32,2176]{2,1,0:T(8,128)(2,1)S(1)}, u32[]{:S(2)}, u32[]{:S(2)}) collective-permute-start(bf16[3,32,2176]{2,1,0:T(8,128)(2,1)S(1)} %pad_maximum_fusion.refs_0_), channel_id=1, source_target_pairs={{0,2},{1,3},{2,0},{3,1},{4,6},{5,7},{6,4},{7,5},{8,10},{9,11},{10,... | collective-permute-start | bytes 1253384 | tf_op jit(solution)/shard_map/ppermute | solution.py:153
  42.1 9.4 %collective-permute-start.17 = (bf16[3,32,2176]{2,1,0:T(8,128)(2,1)S(1)}, bf16[3,32,2176]{2,1,0:T(8,128)(2,1)S(1)}, u32[]{:S(2)}, u32[]{:S(2)}) collective-permute-start(bf16[3,32,2176]{2,1,0:T(8,128)(2,1)S(1)} %pad_maximum_fusion.refs_0_), channel_id=1, source_target_pairs={{0,1},{1,0},{2,3},{3,2},{4,5},{5,4},{6,7},{7,6},{8,9},{9,8},{10,11... | collective-permute-start | bytes 1253384 | tf_op jit(solution)/shard_map/ppermute | solution.py:153
  51.5 5.9 %collective-permute-start.21 = (bf16[3,16,2176]{2,1,0:T(8,128)(2,1)S(1)}, bf16[3,16,2176]{2,1,0:T(8,128)(2,1)S(1)}, u32[]{:S(2)}, u32[]{:S(2)}) collective-permute-start(bf16[3,16,2176]{2,1,0:T(8,128)(2,1)S(1)} %slice.109), channel_id=1, source_target_pairs={{0,2},{1,3},{2,0},{3,1},{4,6},{5,7},{6,4},{7,5},{8,10},{9,11},{10,... | collective-permute-start | bytes 626696 | tf_op jit(solution)/shard_map/ppermute | solution.py:153
  52.1 5.8 %collective-permute-start.22 = (bf16[3,16,2176]{2,1,0:T(8,128)(2,1)S(1)}, bf16[3,16,2176]{2,1,0:T(8,128)(2,1)S(1)}, u32[]{:S(2)}, u32[]{:S(2)}) collective-permute-start(bf16[3,16,2176]{2,1,0:T(8,128)(2,1)S(1)} %slice.110), channel_id=1, source_target_pairs={{0,4},{4,0},{8,12},{12,8},{16,20},{20,16},{24,28},{28,24},{1,5},{5... | collective-permute-start | bytes 626696 | tf_op jit(solution)/shard_map/ppermute | solution.py:153
  52.8 5.2 %collective-permute-start.20 = (bf16[3,32,2176]{2,1,0:T(8,128)(2,1)S(1)}, bf16[3,32,2176]{2,1,0:T(8,128)(2,1)S(1)}, u32[]{:S(2)}, u32[]{:S(2)}) collective-permute-start(bf16[3,32,2176]{2,1,0:T(8,128)(2,1)S(1)} %collective-permute-done.19.refs_0_), channel_id=1, source_target_pairs={{0,1},{1,0},{2,3},{3,2},{4,5},{5,4},{6,7},{7,6},{8,9},{9,8},{10,11... | collective-permute-start | bytes 1253384 | tf_op jit(solution)/shard_map/ppermute | solution.py:153
  58.0 4.5 %collective-permute-start.23 = (bf16[3,32,2176]{2,1,0:T(8,128)(2,1)S(1)}, bf16[3,32,2176]{2,1,0:T(8,128)(2,1)S(1)}, u32[]{:S(2)}, u32[]{:S(2)}) collective-permute-start(bf16[3,32,2176]{2,1,0:T(8,128)(2,1)S(1)} %collective-permute-done.18.refs_2_), channel_id=1, source_target_pairs={{0,1},{1,0},{2,3},{3,2},{4,5},{5,4},{6,7},{7,6},{8,9},{9,8},{10,11... | collective-permute-start | bytes 1253384 | tf_op jit(solution)/shard_map/ppermute | solution.py:153
  64.5 7.5 %collective-permute-start.28 = (bf16[1,3,128,512]{3,2,1,0:T(8,128)(2,1)S(1)}, bf16[1,3,128,512]{3,2,1,0:T(8,128)(2,1)S(1)}, u32[]{:S(2)}, u32[]{:S(2)}) collective-permute-start(bf16[1,3,128,512]{3,2,1,0:T(8,128)(2,1)S(1)} %get-tuple-element.200), channel_id=1, source_target_pairs={{0,1},{1,0},{2,3},{3,2},{4,5},{5,4},{6,7},{7,6},{8,9},{9,8},{10,11... | collective-permute-start | bytes 1179656 | tf_op jit(solution)/shard_map/ppermute | solution.py:153
  64.7 7.2 %collective-permute-start.27 = (bf16[3,64,512]{2,1,0:T(8,128)(2,1)S(1)}, bf16[3,64,512]{2,1,0:T(8,128)(2,1)S(1)}, u32[]{:S(2)}, u32[]{:S(2)}) collective-permute-start(bf16[3,64,512]{2,1,0:T(8,128)(2,1)S(1)} %get-tuple-element.232), channel_id=1, source_target_pairs={{0,4},{4,0},{8,12},{12,8},{16,20},{20,16},{24,28},{28,24},{1,5},{5... | collective-permute-start | bytes 589832 | tf_op jit(solution)/shard_map/ppermute | solution.py:153
  65.4 6.9 %collective-permute-start.29 = (bf16[3,64,512]{2,1,0:T(8,128)(2,1)S(1)}, bf16[3,64,512]{2,1,0:T(8,128)(2,1)S(1)}, u32[]{:S(2)}, u32[]{:S(2)}) collective-permute-start(bf16[3,64,512]{2,1,0:T(8,128)(2,1)S(1)} %get-tuple-element.231), channel_id=1, source_target_pairs={{0,2},{1,3},{2,0},{3,1},{4,6},{5,7},{6,4},{7,5},{8,10},{9,11},{10,... | collective-permute-start | bytes 589832 | tf_op jit(solution)/shard_map/ppermute | solution.py:153
  72.4 5.2 %collective-permute-start.32 = (bf16[1,3,128,512]{3,2,1,0:T(8,128)(2,1)S(1)}, bf16[1,3,128,512]{3,2,1,0:T(8,128)(2,1)S(1)}, u32[]{:S(2)}, u32[]{:S(2)}) collective-permute-start(bf16[1,3,128,512]{3,2,1,0:T(8,128)(2,1)S(1)} %get-tuple-element.204), channel_id=1, source_target_pairs={{0,1},{1,0},{2,3},{3,2},{4,5},{5,4},{6,7},{7,6},{8,9},{9,8},{10,11... | collective-permute-start | bytes 1179656 | tf_op jit(solution)/shard_map/ppermute | solution.py:153
  72.5 11.5 %collective-permute-start.33 = (bf16[3,128,512]{2,1,0:T(8,128)(2,1)S(1)}, bf16[3,128,512]{2,1,0:T(8,128)(2,1)S(1)}, u32[]{:S(2)}, u32[]{:S(2)}) collective-permute-start(bf16[3,128,512]{2,1,0:T(8,128)(2,1)S(1)} %pad_maximum_fusion.2), channel_id=1, source_target_pairs={{0,4},{4,0},{8,12},{12,8},{16,20},{20,16},{24,28},{28,24},{1,5},{5... | collective-permute-start | bytes 1179656 | tf_op jit(solution)/shard_map/ppermute | solution.py:153
  74.2 11.3 %collective-permute-start.34 = (bf16[3,128,512]{2,1,0:T(8,128)(2,1)S(1)}, bf16[3,128,512]{2,1,0:T(8,128)(2,1)S(1)}, u32[]{:S(2)}, u32[]{:S(2)}) collective-permute-start(bf16[3,128,512]{2,1,0:T(8,128)(2,1)S(1)} %pad_maximum_fusion.3), channel_id=1, source_target_pairs={{0,2},{1,3},{2,0},{3,1},{4,6},{5,7},{6,4},{7,5},{8,10},{9,11},{10,... | collective-permute-start | bytes 1179656 | tf_op jit(solution)/shard_map/ppermute | solution.py:153
  85.7 8.1 %collective-permute-start.36 = (bf16[128,512]{1,0:T(8,128)(2,1)S(1)}, bf16[128,512]{1,0:T(8,128)(2,1)S(1)}, u32[]{:S(2)}, u32[]{:S(2)}) collective-permute-start(bf16[128,512]{1,0:T(8,128)(2,1)S(1)} %get-tuple-element.229), channel_id=1, source_target_pairs={{0,8},{4,12},{8,0},{12,4},{16,24},{20,28},{24,16},{28,20},{1,9},{5... | collective-permute-start | bytes 393224 | tf_op jit(solution)/shard_map/ppermute | solution.py:153
  87.9 4.3 %collective-permute-start.38 = (bf16[1,64,512]{2,1,0:T(8,128)(2,1)S(1)}, bf16[1,64,512]{2,1,0:T(8,128)(2,1)S(1)}, u32[]{:S(2)}, u32[]{:S(2)}) collective-permute-start(bf16[1,64,512]{2,1,0:T(8,128)(2,1)S(1)} %get-tuple-element.233), channel_id=1, source_target_pairs={{0,2},{1,3},{2,0},{3,1},{4,6},{5,7},{6,4},{7,5},{8,10},{9,11},{10,... | collective-permute-start | bytes 196616 | tf_op jit(solution)/shard_map/ppermute | solution.py:153
  89.5 4.3 %collective-permute-start.37 = (bf16[1,64,512]{2,1,0:T(8,128)(2,1)S(1)}, bf16[1,64,512]{2,1,0:T(8,128)(2,1)S(1)}, u32[]{:S(2)}, u32[]{:S(2)}) collective-permute-start(bf16[1,64,512]{2,1,0:T(8,128)(2,1)S(1)} %get-tuple-element.234), channel_id=1, source_target_pairs={{0,4},{4,0},{8,12},{12,8},{16,20},{20,16},{24,28},{28,24},{1,5},{5... | collective-permute-start | bytes 196616 | tf_op jit(solution)/shard_map/ppermute | solution.py:153
  90.0 6.8 %collective-permute-start.35 = (bf16[128,512]{1,0:T(8,128)(2,1)S(1)}, bf16[128,512]{1,0:T(8,128)(2,1)S(1)}, u32[]{:S(2)}, u32[]{:S(2)}) collective-permute-start(bf16[128,512]{1,0:T(8,128)(2,1)S(1)} %get-tuple-element.230), channel_id=1, source_target_pairs={{0,8},{4,12},{8,0},{12,4},{16,24},{20,28},{24,16},{28,20},{1,9},{5... | collective-permute-start | bytes 393224 | tf_op jit(solution)/shard_map/ppermute | solution.py:153
  93.8 5.0 %collective-permute-start.40 = (bf16[1,128,512]{2,1,0:T(8,128)(2,1)S(1)}, bf16[1,128,512]{2,1,0:T(8,128)(2,1)S(1)}, u32[]{:S(2)}, u32[]{:S(2)}) collective-permute-start(bf16[1,128,512]{2,1,0:T(8,128)(2,1)S(1)} %pad_maximum_fusion.5), channel_id=1, source_target_pairs={{0,4},{4,0},{8,12},{12,8},{16,20},{20,16},{24,28},{28,24},{1,5},{5... | collective-permute-start | bytes 393224 | tf_op jit(solution)/shard_map/ppermute | solution.py:153
  94.4 6.8 %collective-permute-start.39 = (bf16[128,512]{1,0:T(8,128)(2,1)S(1)}, bf16[128,512]{1,0:T(8,128)(2,1)S(1)}, u32[]{:S(2)}, u32[]{:S(2)}) collective-permute-start(bf16[128,512]{1,0:T(8,128)(2,1)S(1)} %fusion.6), channel_id=1, source_target_pairs={{0,16},{4,20},{8,24},{12,28},{16,0},{20,4},{24,8},{28,12},{1,17},{... | collective-permute-start | bytes 393224 | tf_op jit(solution)/shard_map/ppermute | solution.py:153
  95.4 5.8 %collective-permute-start.41 = (bf16[1,128,512]{2,1,0:T(8,128)(2,1)S(1)}, bf16[1,128,512]{2,1,0:T(8,128)(2,1)S(1)}, u32[]{:S(2)}, u32[]{:S(2)}) collective-permute-start(bf16[1,128,512]{2,1,0:T(8,128)(2,1)S(1)} %pad_maximum_fusion.6), channel_id=1, source_target_pairs={{0,2},{1,3},{2,0},{3,1},{4,6},{5,7},{6,4},{7,5},{8,10},{9,11},{10,... | collective-permute-start | bytes 393224 | tf_op jit(solution)/shard_map/ppermute | solution.py:153
  (17 other events, 182.2 us)

commit v15 on v14

--- a/solution.py
+++ b/solution.py
@@ -154,10 +154,10 @@
 
 
 def stage_kernel(*refs):
-    length_hbm, table_hbm, frequency_hbm, *large = refs[:12]
-    cosine_ref, sine_ref, owner_ref, *staged = refs[12:24]
-    list_ref, length_out, table_out = refs[24:27]
-    frequency_ref, owners, sems = refs[27:]
+    length_hbm, table_hbm, frequency_hbm, *large = refs[:10]
+    cosine_ref, sine_ref, owner_ref, *staged = refs[10:20]
+    list_ref, length_out, table_out = refs[20:23]
+    frequency_ref, owners, sems = refs[23:]
     length_ref, table_ref = length_out, table_out
     sources = (length_hbm, table_hbm, frequency_hbm, *large)
     targets = (length_out, table_out, frequency_ref, *staged)
@@ -208,10 +208,17 @@
 def attention_kernel(*refs):
     pieces, (keep_out, far_out, core_out) = refs[:4], refs[19:22]
     (cosine_ref, sine_ref, owner_ref, gain_ref, q_gain_ref, k_gain_ref) = refs[4:10]
-    (q_ref, k_ref, v_ref, key_ref, value_ref, o_ref, list_ref, length_ref, table_ref) = refs[10:19]
+    (q_ref, k_ref, v_ref, key_ref, list_ref, length_ref, table_ref) = refs[10:17]
     (
         x_ref, query_ref, own_scores, scores_ref, mix_ref, mixed_ref, part_ref, slots_ref, decoded_ref,
+        value_ref, o_ref, sems,
     ) = refs[22:]
+    value_copy, o_copy = (
+        pltpu.make_async_copy(source, target, sems.at[i])
+        for i, (source, target) in enumerate(zip(refs[17:19], (value_ref, o_ref)))
+    )
+    value_copy.start()
+    o_copy.start()
     tokens, head_dim = x_ref.shape[0], k_gain_ref.shape[1]
     tp_index = lax.axis_index("tp")
     heads = q_ref.shape[1] // head_dim
@@ -309,6 +316,7 @@
         )
         decoded_ref[...] = mix[:, :head_dim] / mix[:, head_dim:]
 
+    value_copy.wait()
     length = length_ref[0]
     listed = slots_ref.shape[2] // PAGE
     pages = scores_ref.shape[2] // PAGE
@@ -336,6 +344,7 @@
         columns = slice(head * head_dim, (head + 1) * head_dim)
         mixed_ref[:, columns] = part[:, :head_dim] / part[:, head_dim:]
         mixed_ref[PRE:, columns] = decoded_ref[head * decodes : (head + 1) * decodes]
+    o_copy.wait()
     part_ref[...] = jnp.dot(
         mixed_ref[...].astype(jnp.bfloat16), o_ref[...], preferred_element_type=jnp.float32
     )
@@ -362,12 +371,13 @@
     frequency = jnp.asarray(np.concatenate([half, half])[None, :], jnp.float32)
     large = (
         norm_in_gain[None, :], q_gain[None, :], k_gain[None, :], q_weight, k_weight, v_weight,
-        key_pages[0], value_pages[0], o_weight,
+        key_pages[0],
     )
     scalars = (cache_len, page_table)
+    later = (value_pages[0], o_weight)
     sources = [
         pltpu.with_memory_space_constraint(array, pltpu.HBM)
-        for array in (*scalars, frequency, *large)
+        for array in (*scalars, frequency, *large, *later)
     ]
     rope = pltpu.VMEM((tokens, head_dim), jnp.float32)
     *staged, page_list, lengths, table = pl.pallas_call(
@@ -376,16 +386,16 @@
         + [pltpu.VMEM(array.shape, array.dtype) for array in large]
         + [jax.ShapeDtypeStruct((POOL,), jnp.int32)]
         + [jax.ShapeDtypeStruct(array.shape, array.dtype) for array in scalars],
-        in_specs=[pl.BlockSpec(memory_space=pltpu.HBM)] * 12,
-        out_specs=[VMEM] * 12 + [SMEM] * 3,
+        in_specs=[pl.BlockSpec(memory_space=pltpu.HBM)] * 10,
+        out_specs=[VMEM] * 10 + [SMEM] * 3,
         scratch_shapes=[
             pltpu.VMEM(frequency.shape, frequency.dtype),
             pltpu.SMEM((2, POOL), jnp.int32),
-            pltpu.SemaphoreType.DMA((12,)),
+            pltpu.SemaphoreType.DMA((10,)),
         ],
         compiler_params=pltpu.CompilerParams(vmem_limit_bytes=4 * 1024 * 1024),
         name="stage",
-    )(*sources)
+    )(*sources[:10])
     far, *staged = ordered(flip(hidden_in, "tp", 2), *staged, page_list, lengths, table)
     pieces = (hidden_in, flip(hidden_in, "tp", 1), far, flip(far, "tp", 1))
     share = (tokens // 4, width)
@@ -397,7 +407,7 @@
             jax.ShapeDtypeStruct(share, jnp.float32),
             jax.ShapeDtypeStruct((2, *share), jnp.bfloat16),
         ],
-        in_specs=[VMEM] * 16 + [SMEM] * 3,
+        in_specs=[VMEM] * 14 + [SMEM] * 3 + [pl.BlockSpec(memory_space=pltpu.HBM)] * 2,
         out_specs=[VMEM] * 3,
         scratch_shapes=[
             pltpu.VMEM((tokens, width), jnp.bfloat16),
@@ -409,10 +419,12 @@
             pltpu.VMEM((tokens, width), jnp.float32),
             pltpu.VMEM((POOL // list_pages, decode_rows, list_pages * PAGE), jnp.float32),
             pltpu.VMEM((decode_rows, head_dim), jnp.float32),
+            *(pltpu.VMEM(array.shape, array.dtype) for array in later),
+            pltpu.SemaphoreType.DMA((2,)),
         ],
-        compiler_params=pltpu.CompilerParams(vmem_limit_bytes=24 * 1024 * 1024),
+        compiler_params=pltpu.CompilerParams(vmem_limit_bytes=28 * 1024 * 1024),
         name="attention",
-    )(*pieces, *staged)
+    )(*pieces, *staged, *sources[10:])
 
 
 def pack_kernel(
@@ -503,15 +515,6 @@
     return keep, send
 
 
-def finish_kernel(own_ref, z1_ref, z2_ref, x_ref, y_ref, out_ref):
-    total = own_ref[0]
-    for extra_ref in (x_ref, y_ref):
-        total = total + extra_ref[0].astype(jnp.float32)
-    for extra_ref in (z1_ref, z2_ref):
-        total = total + extra_ref[...].astype(jnp.float32)
-    out_ref[...] = total.astype(jnp.bfloat16)
-
-
 def ordered(*values):
     return lax.optimization_barrier(values)
 
@@ -646,10 +649,9 @@
         with_upper(joined((keep, (send, first)), 0, 0), by_y),
     )
     to_y = with_lower(joined((near_keep, (near_send, near_first)), 0, 1), by_x)
-    sums_3 = flip(to_x, "req", 1), flip(to_y, "tp", 2)
+    sums_3 = flip(to_x, "req", 1).astype(jnp.float32) + flip(to_y, "tp", 2).astype(jnp.float32)
     all_0, near_send, sums_3 = ordered(with_core(all_0), flip(near_send, "tp", 1), sums_3)
-    near_3 = (near_keep, (near_send, near_first))
-    sent = joined(near_3, 0, 0) + sums_3[0].astype(jnp.float32) + sums_3[1].astype(jnp.float32)
+    sent = joined((near_keep, (near_send, near_first)), 0, 0) + sums_3
     sent_3, relay_0 = ordered(
         flip(sent[2].astype(jnp.bfloat16), "req", 2), relayed(joined(all_0, 1, 1))
     )
@@ -658,14 +660,9 @@
     )
     from_z = [flip(sent[0].astype(jnp.bfloat16), "req", 2), flip(sent_2, "req", 4)]
     sums_0 = neighbours(joined(all_0, 1, 0), joined(all_0, 0, 1), *relay_0)
-    return pl.pallas_call(
-        finish_kernel,
-        out_shape=jax.ShapeDtypeStruct((token_count, share_width), jnp.bfloat16),
-        in_specs=[VMEM] * 5,
-        out_specs=VMEM,
-        compiler_params=pltpu.CompilerParams(vmem_limit_bytes=8 * 1024 * 1024),
-        name="finish",
-    )(joined(all_0, 0, 0), *from_z, *sums_0)
+    total = joined(all_0, 0, 0) + from_z[0].astype(jnp.float32) + from_z[1].astype(jnp.float32)
+    total, from_x, from_y = ordered(total[0], *sums_0)
+    return (total + from_x[0].astype(jnp.float32) + from_y[0].astype(jnp.float32)).astype(jnp.bfloat16)
 
 
 def moe_routed(

time: 102 us -> 105 us (1.029)
  starting transfers between devices: 32.9 us -> 37.1 us
  waiting for transfers between devices: 49.6 us -> 47.7 us
    ppermute x42, starting transfers between devices: 32.9 us -> 37.1 us  [flip(): lax.ppermute(value, axis, [(i, i ^ bits) for i in range(lax.axis_size(axi...]
    ppermute x42, waiting for transfers between devices: 49.6 us -> 47.7 us  [flip(): lax.ppermute(value, axis, [(i, i ^ bits) for i in range(lax.axis_size(axi...]
    pallas_call x1, Pallas kernels: 4.88 us -> 6.2 us  [attention_shares(): pl.pallas_call(attention_kernel, out_shape=[jax.ShapeDtypeStruct(share, j...]
    pallas_call x1, Pallas kernels: 4.41 us -> 3.28 us  [attention_shares(): pl.pallas_call(stage_kernel, out_shape=[rope, rope, pltpu.VMEM((1, POOL *...]
  transfers between devices with their start and end apart: 42 -> 42, of which waited for: 26 -> 22; matrix products, arithmetic and copies ran while one was open for 1% -> 1% of each run, Pallas kernels for 12% -> 10%
where the time goes in v15:
time: 105 us
  waiting for transfers between devices  47.7 us (45%)
  starting transfers between devices  37.1 us (35%)
  Pallas kernels  17.1 us (16%)
  other arithmetic  2.03 us (2%)
    ppermute x42, waiting for transfers between devices, flip(): lax.ppermute(value, axis, [(i, i ^ bits) for i in range(lax.axis_size(axi...  47.7 us
    ppermute x42, starting transfers between devices, flip(): lax.ppermute(value, axis, [(i, i ^ bits) for i in range(lax.axis_size(axi...  37.1 us
    pallas_call x3, Pallas kernels, run_experts(): pl.pallas_call(functools.partial(experts_kernel, plan, len(residual)), ou...  7.45 us
    pallas_call x1, Pallas kernels, attention_shares(): pl.pallas_call(attention_kernel, out_shape=[jax.ShapeDtypeStruct(share, j...  6.2 us
    pallas_call x1, Pallas kernels, attention_shares(): pl.pallas_call(stage_kernel, out_shape=[rope, rope, pltpu.VMEM((1, POOL *...  3.28 us
  transfers between devices with their start and end apart: 42, of which 22 were waited for; matrix products, arithmetic and copies ran while one was open for 1% of the time, Pallas kernels for 10%

profile of v15, /device:TPU:0, one launch (start us, length us, event | category | flops | bytes accessed | tf_op | source)
XLA Modules:
  0.0 104.5 jit_solution(14661303802359521789)
XLA Ops:
  0.0 3.0 %collective-permute-start.1 = (bf16[128,512]{1,0:T(8,128)(2,1)}, bf16[128,512]{1,0:T(8,128)(2,1)S(1)}, u32[]{:S(2)}, u32[]{:S(2)}) collective-permute-start(bf16[128,512]{1,0:T(8,128)(2,1)} %refs_0_.3), channel_id=1, source_target_pairs={{0,2},{1,3},{2,0},{3,1},{4,6},{5,7},{6,4},{7,5},{8,10},{9,11},{10,... | collective-permute-start | bytes 393224 | tf_op jit(solution)/shard_map/ppermute | solution.py:153
  3.0 3.3 %stage.1 = (f32[128,128]{1,0:T(8,128)S(1)}, f32[128,128]{1,0:T(8,128)S(1)}, s32[1,6144]{1,0:T(1,128)S(1)}, f32[1,2048]{1,0:T(1,128)S(1)}, f32[1,128]{1,0:T(1,128...) custom-call(s32[9]{0:T(128)} %refs_0_.2, ...), custom_call_target="tpu_custom_call" | custom-call | tf_op jit(solution)/shard_map/stage/pallas_call | solution.py:383
  8.0 6.2 %attention.1 = (f32[32,2048]{1,0:T(8,128)S(1)}, f32[32,2048]{1,0:T(8,128)S(1)}, bf16[2,32,2048]{2,1,0:T(8,128)(2,1)S(1)}) custom-call(bf16[128,512]{1,0:T(8,128)(2,1)S(1)} %copy-done.3, bf16[128,512]{1,0:T(8,128)(2,1)S(1)} %collective-permute-done.refs_1_, bf16[128,512]{1,0:T(8,128)(2,1)S(1)} %collective-permute-done.1.refs_2_, ...), custom_call_target="tpu_custom_call" | custom-call | tf_op jit(solution)/shard_map/attention/pallas_call | solution.py:403
  14.5 1.4 %collective-permute-done.3 = bf16[2,32,2048]{2,1,0:T(8,128)(2,1)S(1)} collective-permute-done((bf16[2,32,2048]{2,1,0:T(8,128)(2,1)S(1)}, bf16[2,32,2048]{2,1,0:T(8,128)(2,1)S(1)}, u32[]{:S(2)}, u32[]{:S(2)}) %collective-permute-start.3) | collective-permute-done | bytes 262176 | tf_op jit(solution)/shard_map/ppermute | solution.py:153
  15.9 1.8 %collective-permute-start.4 = (bf16[32,2048]{1,0:T(8,128)(2,1)S(1)}, bf16[32,2048]{1,0:T(8,128)(2,1)S(1)}, u32[]{:S(2)}, u32[]{:S(2)}) collective-permute-start(bf16[32,2048]{1,0:T(8,128)(2,1)S(1)} %fusion.10), channel_id=1, source_target_pairs={{0,2},{1,3},{2,0},{3,1},{4,6},{5,7},{6,4},{7,5},{8,10},{9,11},{10,... | collective-permute-start | bytes 393224 | tf_op jit(solution)/shard_map/ppermute | solution.py:153
  17.7 3.8 %collective-permute-done.4.far_ref = bf16[32,2048]{1,0:T(8,128)(2,1)S(1)} collective-permute-done((bf16[32,2048]{1,0:T(8,128)(2,1)S(1)}, bf16[32,2048]{1,0:T(8,128)(2,1)S(1)}, u32[]{:S(2)}, u32[]{:S(2)}) %collective-permute-start.4) | collective-permute-done | bytes 131104 | tf_op jit(solution)/shard_map/ppermute | solution.py:153
  21.7 1.8 %collective-permute-start.5 = (bf16[1,32,2176]{2,1,0:T(8,128)(2,1)S(1)}, bf16[1,32,2176]{2,1,0:T(8,128)(2,1)S(1)}, u32[]{:S(2)}, u32[]{:S(2)}) collective-permute-start(bf16[1,32,2176]{2,1,0:T(8,128)(2,1)S(1)} %bitcast.91), channel_id=1, source_target_pairs={{0,8},{4,12},{8,0},{12,4},{16,24},{20,28},{24,16},{28,20},{1,9},{5... | collective-permute-start | bytes 417800 | tf_op jit(solution)/shard_map/ppermute | solution.py:153
  23.6 2.6 %collective-permute-start.6 = (bf16[1,32,2176]{2,1,0:T(8,128)(2,1)S(1)}, bf16[1,32,2176]{2,1,0:T(8,128)(2,1)S(1)}, u32[]{:S(2)}, u32[]{:S(2)}) collective-permute-start(bf16[1,32,2176]{2,1,0:T(8,128)(2,1)S(1)} %bitcast.92), channel_id=1, source_target_pairs={{0,16},{4,20},{8,24},{12,28},{16,0},{20,4},{24,8},{28,12},{1,17},{... | collective-permute-start | bytes 417800 | tf_op jit(solution)/shard_map/ppermute | solution.py:153
  26.2 1.5 %collective-permute-start.7 = (bf16[1,32,2176]{2,1,0:T(8,128)(2,1)S(1)}, bf16[1,32,2176]{2,1,0:T(8,128)(2,1)S(1)}, u32[]{:S(2)}, u32[]{:S(2)}) collective-permute-start(bf16[1,32,2176]{2,1,0:T(8,128)(2,1)S(1)} %bitcast.93), channel_id=1, source_target_pairs={{0,2},{1,3},{2,0},{3,1},{4,6},{5,7},{6,4},{7,5},{8,10},{9,11},{10,... | collective-permute-start | bytes 417800 | tf_op jit(solution)/shard_map/ppermute | solution.py:153
  27.7 1.5 %collective-permute-start.8 = (bf16[1,32,2176]{2,1,0:T(8,128)(2,1)S(1)}, bf16[1,32,2176]{2,1,0:T(8,128)(2,1)S(1)}, u32[]{:S(2)}, u32[]{:S(2)}) collective-permute-start(bf16[1,32,2176]{2,1,0:T(8,128)(2,1)S(1)} %bitcast.94), channel_id=1, source_target_pairs={{0,4},{4,0},{8,12},{12,8},{16,20},{20,16},{24,28},{28,24},{1,5},{5... | collective-permute-start | bytes 417800 | tf_op jit(solution)/shard_map/ppermute | solution.py:153
  29.2 2.9 %collective-permute-done.6 = bf16[1,32,2176]{2,1,0:T(8,128)(2,1)S(1)} collective-permute-done((bf16[1,32,2176]{2,1,0:T(8,128)(2,1)S(1)}, bf16[1,32,2176]{2,1,0:T(8,128)(2,1)S(1)}, u32[]{:S(2)}, u32[]{:S(2)}) %collective-permute-start.6) | collective-permute-done | bytes 139296 | tf_op jit(solution)/shard_map/ppermute | solution.py:153
  34.6 3.3 %collective-permute-start.12 = (bf16[1,16,2176]{2,1,0:T(8,128)(2,1)S(1)}, bf16[1,16,2176]{2,1,0:T(8,128)(2,1)S(1)}, u32[]{:S(2)}, u32[]{:S(2)}) collective-permute-start(bf16[1,16,2176]{2,1,0:T(8,128)(2,1)S(1)} %slice.108), channel_id=1, source_target_pairs={{0,4},{4,0},{8,12},{12,8},{16,20},{20,16},{24,28},{28,24},{1,5},{5... | collective-permute-start | bytes 208904 | tf_op jit(solution)/shard_map/ppermute | solution.py:153
  38.0 2.2 %collective-permute-done.12.refs_7_ = bf16[1,16,2176]{2,1,0:T(8,128)(2,1)S(1)} collective-permute-done((bf16[1,16,2176]{2,1,0:T(8,128)(2,1)S(1)}, bf16[1,16,2176]{2,1,0:T(8,128)(2,1)S(1)}, u32[]{:S(2)}, u32[]{:S(2)}) %collective-permute-start.12) | collective-permute-done | bytes 69664 | tf_op jit(solution)/shard_map/ppermute | solution.py:153
  40.8 2.0 %collective-permute-start.19 = (bf16[3,32,2176]{2,1,0:T(8,128)(2,1)S(1)}, bf16[3,32,2176]{2,1,0:T(8,128)(2,1)S(1)}, u32[]{:S(2)}, u32[]{:S(2)}) collective-permute-start(bf16[3,32,2176]{2,1,0:T(8,128)(2,1)S(1)} %pad_maximum_fusion.refs_0_), channel_id=1, source_target_pairs={{0,4},{4,0},{8,12},{12,8},{16,20},{20,16},{24,28},{28,24},{1,5},{5... | collective-permute-start | bytes 1253384 | tf_op jit(solution)/shard_map/ppermute | solution.py:153
  45.4 6.9 %collective-permute-done.18.refs_2_ = bf16[3,32,2176]{2,1,0:T(8,128)(2,1)S(1)} collective-permute-done((bf16[3,32,2176]{2,1,0:T(8,128)(2,1)S(1)}, bf16[3,32,2176]{2,1,0:T(8,128)(2,1)S(1)}, u32[]{:S(2)}, u32[]{:S(2)}) %collective-permute-start.18) | collective-permute-done | bytes 417824 | tf_op jit(solution)/shard_map/ppermute | solution.py:153
  52.8 1.6 %collective-permute-start.21 = (bf16[3,16,2176]{2,1,0:T(8,128)(2,1)S(1)}, bf16[3,16,2176]{2,1,0:T(8,128)(2,1)S(1)}, u32[]{:S(2)}, u32[]{:S(2)}) collective-permute-start(bf16[3,16,2176]{2,1,0:T(8,128)(2,1)S(1)} %slice.109), channel_id=1, source_target_pairs={{0,2},{1,3},{2,0},{3,1},{4,6},{5,7},{6,4},{7,5},{8,10},{9,11},{10,... | collective-permute-start | bytes 626696 | tf_op jit(solution)/shard_map/ppermute | solution.py:153
  54.4 1.8 %collective-permute-start.22 = (bf16[3,16,2176]{2,1,0:T(8,128)(2,1)S(1)}, bf16[3,16,2176]{2,1,0:T(8,128)(2,1)S(1)}, u32[]{:S(2)}, u32[]{:S(2)}) collective-permute-start(bf16[3,16,2176]{2,1,0:T(8,128)(2,1)S(1)} %slice.110), channel_id=1, source_target_pairs={{0,4},{4,0},{8,12},{12,8},{16,20},{20,16},{24,28},{28,24},{1,5},{5... | collective-permute-start | bytes 626696 | tf_op jit(solution)/shard_map/ppermute | solution.py:153
  56.3 2.0 %experts.3 = (f32[2,2,1,128,512]{4,3,2,1,0:T(8,128)S(1)}, bf16[2,1,128,512]{3,2,1,0:T(8,128)(2,1)S(1)}, bf16[2,1,128,512]{3,2,1,0:T(8,128)(2,1)S(1)}) custom-call(bf16[1,32,2176]{2,1,0:T(8,128)(2,1)S(1)} %bitcast.96, bf16[1,32,2176]{2,1,0:T(8,128)(2,1)S(1)} %collective-permute-done.13.refs_1_, bf16[1,32,2176]{2,1,0:T(8,128)(2,1)S(1)} %collective-permute-done.7.refs_2_, ...), custom_call_target="tpu_custom_call" | custom-call | tf_op jit(solution)/shard_map/experts/pallas_call | solution.py:502
  58.3 1.4 %collective-permute-done.21 = bf16[3,16,2176]{2,1,0:T(8,128)(2,1)S(1)} collective-permute-done((bf16[3,16,2176]{2,1,0:T(8,128)(2,1)S(1)}, bf16[3,16,2176]{2,1,0:T(8,128)(2,1)S(1)}, u32[]{:S(2)}, u32[]{:S(2)}) %collective-permute-start.21) | collective-permute-done | bytes 208928 | tf_op jit(solution)/shard_map/ppermute | solution.py:153
  59.7 1.3 %collective-permute-done.22 = bf16[3,16,2176]{2,1,0:T(8,128)(2,1)S(1)} collective-permute-done((bf16[3,16,2176]{2,1,0:T(8,128)(2,1)S(1)}, bf16[3,16,2176]{2,1,0:T(8,128)(2,1)S(1)}, u32[]{:S(2)}, u32[]{:S(2)}) %collective-permute-start.22) | collective-permute-done | bytes 208928 | tf_op jit(solution)/shard_map/ppermute | solution.py:153
  62.9 2.7 %experts.4 = (f32[1,2,3,128,512]{4,3,2,1,0:T(8,128)S(1)}, bf16[1,3,128,512]{3,2,1,0:T(8,128)(2,1)S(1)}, bf16[1,3,128,512]{3,2,1,0:T(8,128)(2,1)S(1)}) custom-call(bf16[3,32,2176]{2,1,0:T(8,128)(2,1)S(1)} %collective-permute-done.19.refs_0_, bf16[3,32,2176]{2,1,0:T(8,128)(2,1)S(1)} %collective-permute-done.20.refs_1_, ...), custom_call_target="tpu_custom_call" | custom-call | tf_op jit(solution)/shard_map/experts/pallas_call | solution.py:502
  65.8 1.6 %collective-permute-done.25 = bf16[1,3,128,512]{3,2,1,0:T(8,128)(2,1)S(1)} collective-permute-done((bf16[1,3,128,512]{3,2,1,0:T(8,128)(2,1)S(1)}, bf16[1,3,128,512]{3,2,1,0:T(8,128)(2,1)S(1)}, u32[]{:S(2)}, u32[]{:S(2)}) %collective-permute-start.25) | collective-permute-done | bytes 393248 | tf_op jit(solution)/shard_map/ppermute | solution.py:153
  67.8 1.5 %collective-permute-start.27 = (bf16[3,64,512]{2,1,0:T(8,128)(2,1)S(1)}, bf16[3,64,512]{2,1,0:T(8,128)(2,1)S(1)}, u32[]{:S(2)}, u32[]{:S(2)}) collective-permute-start(bf16[3,64,512]{2,1,0:T(8,128)(2,1)S(1)} %get-tuple-element.225), channel_id=1, source_target_pairs={{0,4},{4,0},{8,12},{12,8},{16,20},{20,16},{24,28},{28,24},{1,5},{5... | collective-permute-start | bytes 589832 | tf_op jit(solution)/shard_map/ppermute | solution.py:153
  69.9 2.7 %experts.5 = (f32[1,2,3,128,512]{4,3,2,1,0:T(8,128)S(1)}, bf16[1,3,128,512]{3,2,1,0:T(8,128)(2,1)S(1)}, bf16[1,3,128,512]{3,2,1,0:T(8,128)(2,1)S(1)}) custom-call(bf16[3,32,2176]{2,1,0:T(8,128)(2,1)S(1)} %pad_maximum_fusion.refs_0_, bf16[3,32,2176]{2,1,0:T(8,128)(2,1)S(1)} %collective-permute-done.17.refs_1_, ...), custom_call_target="tpu_custom_call" | custom-call | tf_op jit(solution)/shard_map/experts/pallas_call | solution.py:502
  72.7 2.3 %collective-permute-done.27 = bf16[3,64,512]{2,1,0:T(8,128)(2,1)S(1)} collective-permute-done((bf16[3,64,512]{2,1,0:T(8,128)(2,1)S(1)}, bf16[3,64,512]{2,1,0:T(8,128)(2,1)S(1)}, u32[]{:S(2)}, u32[]{:S(2)}) %collective-permute-start.27) | collective-permute-done | bytes 196640 | tf_op jit(solution)/shard_map/ppermute | solution.py:153
  78.2 8.6 %collective-permute-done.34 = bf16[3,128,512]{2,1,0:T(8,128)(2,1)S(1)} collective-permute-done((bf16[3,128,512]{2,1,0:T(8,128)(2,1)S(1)}, bf16[3,128,512]{2,1,0:T(8,128)(2,1)S(1)}, u32[]{:S(2)}, u32[]{:S(2)}) %collective-permute-start.34) | collective-permute-done | bytes 393248 | tf_op jit(solution)/shard_map/ppermute | solution.py:153
  87.6 2.0 %collective-permute-start.36 = (bf16[128,512]{1,0:T(8,128)(2,1)S(1)}, bf16[128,512]{1,0:T(8,128)(2,1)S(1)}, u32[]{:S(2)}, u32[]{:S(2)}) collective-permute-start(bf16[128,512]{1,0:T(8,128)(2,1)S(1)} %get-tuple-element.223), channel_id=1, source_target_pairs={{0,8},{4,12},{8,0},{12,4},{16,24},{20,28},{24,16},{28,20},{1,9},{5... | collective-permute-start | bytes 393224 | tf_op jit(solution)/shard_map/ppermute | solution.py:153
  90.6 1.4 %collective-permute-start.38 = (bf16[1,64,512]{2,1,0:T(8,128)(2,1)S(1)}, bf16[1,64,512]{2,1,0:T(8,128)(2,1)S(1)}, u32[]{:S(2)}, u32[]{:S(2)}) collective-permute-start(bf16[1,64,512]{2,1,0:T(8,128)(2,1)S(1)} %get-tuple-element.226), channel_id=1, source_target_pairs={{0,2},{1,3},{2,0},{3,1},{4,6},{5,7},{6,4},{7,5},{8,10},{9,11},{10,... | collective-permute-start | bytes 196616 | tf_op jit(solution)/shard_map/ppermute | solution.py:153
  92.2 1.9 %collective-permute-done.37 = bf16[1,64,512]{2,1,0:T(8,128)(2,1)S(1)} collective-permute-done((bf16[1,64,512]{2,1,0:T(8,128)(2,1)S(1)}, bf16[1,64,512]{2,1,0:T(8,128)(2,1)S(1)}, u32[]{:S(2)}, u32[]{:S(2)}) %collective-permute-start.37) | collective-permute-done | bytes 65568 | tf_op jit(solution)/shard_map/ppermute | solution.py:153
  95.4 1.5 %collective-permute-start.41 = (bf16[1,128,512]{2,1,0:T(8,128)(2,1)S(1)}, bf16[1,128,512]{2,1,0:T(8,128)(2,1)S(1)}, u32[]{:S(2)}, u32[]{:S(2)}) collective-permute-start(bf16[1,128,512]{2,1,0:T(8,128)(2,1)S(1)} %pad_maximum_fusion.6), channel_id=1, source_target_pairs={{0,2},{1,3},{2,0},{3,1},{4,6},{5,7},{6,4},{7,5},{8,10},{9,11},{10,... | collective-permute-start | bytes 393224 | tf_op jit(solution)/shard_map/ppermute | solution.py:153
  97.3 1.5 %collective-permute-start.40 = (bf16[1,128,512]{2,1,0:T(8,128)(2,1)S(1)}, bf16[1,128,512]{2,1,0:T(8,128)(2,1)S(1)}, u32[]{:S(2)}, u32[]{:S(2)}) collective-permute-start(bf16[1,128,512]{2,1,0:T(8,128)(2,1)S(1)} %pad_maximum_fusion.5), channel_id=1, source_target_pairs={{0,4},{4,0},{8,12},{12,8},{16,20},{20,16},{24,28},{28,24},{1,5},{5... | collective-permute-start | bytes 393224 | tf_op jit(solution)/shard_map/ppermute | solution.py:153
  98.8 4.9 %collective-permute-done.39 = bf16[128,512]{1,0:T(8,128)(2,1)S(1)} collective-permute-done((bf16[128,512]{1,0:T(8,128)(2,1)S(1)}, bf16[128,512]{1,0:T(8,128)(2,1)S(1)}, u32[]{:S(2)}, u32[]{:S(2)}) %collective-permute-start.39) | collective-permute-done | bytes 131104 | tf_op jit(solution)/shard_map/ppermute | solution.py:153
  (106 shorter events, 19.0 us)
Async XLA Ops:
  0.0 6.7 %collective-permute-start.1 = (bf16[128,512]{1,0:T(8,128)(2,1)}, bf16[128,512]{1,0:T(8,128)(2,1)S(1)}, u32[]{:S(2)}, u32[]{:S(2)}) collective-permute-start(bf16[128,512]{1,0:T(8,128)(2,1)} %refs_0_.3), channel_id=1, source_target_pairs={{0,2},{1,3},{2,0},{3,1},{4,6},{5,7},{6,4},{7,5},{8,10},{9,11},{10,... | collective-permute-start | bytes 393224 | tf_op jit(solution)/shard_map/ppermute | solution.py:153
  15.9 5.6 %collective-permute-start.4 = (bf16[32,2048]{1,0:T(8,128)(2,1)S(1)}, bf16[32,2048]{1,0:T(8,128)(2,1)S(1)}, u32[]{:S(2)}, u32[]{:S(2)}) collective-permute-start(bf16[32,2048]{1,0:T(8,128)(2,1)S(1)} %fusion.10), channel_id=1, source_target_pairs={{0,2},{1,3},{2,0},{3,1},{4,6},{5,7},{6,4},{7,5},{8,10},{9,11},{10,... | collective-permute-start | bytes 393224 | tf_op jit(solution)/shard_map/ppermute | solution.py:153
  21.7 7.5 %collective-permute-start.5 = (bf16[1,32,2176]{2,1,0:T(8,128)(2,1)S(1)}, bf16[1,32,2176]{2,1,0:T(8,128)(2,1)S(1)}, u32[]{:S(2)}, u32[]{:S(2)}) collective-permute-start(bf16[1,32,2176]{2,1,0:T(8,128)(2,1)S(1)} %bitcast.91), channel_id=1, source_target_pairs={{0,8},{4,12},{8,0},{12,4},{16,24},{20,28},{24,16},{28,20},{1,9},{5... | collective-permute-start | bytes 417800 | tf_op jit(solution)/shard_map/ppermute | solution.py:153
  23.6 8.5 %collective-permute-start.6 = (bf16[1,32,2176]{2,1,0:T(8,128)(2,1)S(1)}, bf16[1,32,2176]{2,1,0:T(8,128)(2,1)S(1)}, u32[]{:S(2)}, u32[]{:S(2)}) collective-permute-start(bf16[1,32,2176]{2,1,0:T(8,128)(2,1)S(1)} %bitcast.92), channel_id=1, source_target_pairs={{0,16},{4,20},{8,24},{12,28},{16,0},{20,4},{24,8},{28,12},{1,17},{... | collective-permute-start | bytes 417800 | tf_op jit(solution)/shard_map/ppermute | solution.py:153
  26.2 6.0 %collective-permute-start.7 = (bf16[1,32,2176]{2,1,0:T(8,128)(2,1)S(1)}, bf16[1,32,2176]{2,1,0:T(8,128)(2,1)S(1)}, u32[]{:S(2)}, u32[]{:S(2)}) collective-permute-start(bf16[1,32,2176]{2,1,0:T(8,128)(2,1)S(1)} %bitcast.93), channel_id=1, source_target_pairs={{0,2},{1,3},{2,0},{3,1},{4,6},{5,7},{6,4},{7,5},{8,10},{9,11},{10,... | collective-permute-start | bytes 417800 | tf_op jit(solution)/shard_map/ppermute | solution.py:153
  27.7 5.1 %collective-permute-start.8 = (bf16[1,32,2176]{2,1,0:T(8,128)(2,1)S(1)}, bf16[1,32,2176]{2,1,0:T(8,128)(2,1)S(1)}, u32[]{:S(2)}, u32[]{:S(2)}) collective-permute-start(bf16[1,32,2176]{2,1,0:T(8,128)(2,1)S(1)} %bitcast.94), channel_id=1, source_target_pairs={{0,4},{4,0},{8,12},{12,8},{16,20},{20,16},{24,28},{28,24},{1,5},{5... | collective-permute-start | bytes 417800 | tf_op jit(solution)/shard_map/ppermute | solution.py:153
  32.7 5.2 %collective-permute-start.10 = (bf16[1,32,2176]{2,1,0:T(8,128)(2,1)S(1)}, bf16[1,32,2176]{2,1,0:T(8,128)(2,1)S(1)}, u32[]{:S(2)}, u32[]{:S(2)}) collective-permute-start(bf16[1,32,2176]{2,1,0:T(8,128)(2,1)S(1)} %collective-permute-done.6), channel_id=1, source_target_pairs={{0,8},{4,12},{8,0},{12,4},{16,24},{20,28},{24,16},{28,20},{1,9},{5... | collective-permute-start | bytes 417800 | tf_op jit(solution)/shard_map/ppermute | solution.py:153
  33.2 4.8 %collective-permute-start.13 = (bf16[1,32,2176]{2,1,0:T(8,128)(2,1)S(1)}, bf16[1,32,2176]{2,1,0:T(8,128)(2,1)S(1)}, u32[]{:S(2)}, u32[]{:S(2)}) collective-permute-start(bf16[1,32,2176]{2,1,0:T(8,128)(2,1)S(1)} %bitcast.95), channel_id=1, source_target_pairs={{0,1},{1,0},{2,3},{3,2},{4,5},{5,4},{6,7},{7,6},{8,9},{9,8},{10,11... | collective-permute-start | bytes 417800 | tf_op jit(solution)/shard_map/ppermute | solution.py:153
  33.2 7.1 %collective-permute-start.14 = (bf16[1,32,2176]{2,1,0:T(8,128)(2,1)S(1)}, bf16[1,32,2176]{2,1,0:T(8,128)(2,1)S(1)}, u32[]{:S(2)}, u32[]{:S(2)}) collective-permute-start(bf16[1,32,2176]{2,1,0:T(8,128)(2,1)S(1)} %collective-permute-done.7.refs_2_), channel_id=1, source_target_pairs={{0,1},{1,0},{2,3},{3,2},{4,5},{5,4},{6,7},{7,6},{8,9},{9,8},{10,11... | collective-permute-start | bytes 417800 | tf_op jit(solution)/shard_map/ppermute | solution.py:153
  34.6 5.6 %collective-permute-start.12 = (bf16[1,16,2176]{2,1,0:T(8,128)(2,1)S(1)}, bf16[1,16,2176]{2,1,0:T(8,128)(2,1)S(1)}, u32[]{:S(2)}, u32[]{:S(2)}) collective-permute-start(bf16[1,16,2176]{2,1,0:T(8,128)(2,1)S(1)} %slice.108), channel_id=1, source_target_pairs={{0,4},{4,0},{8,12},{12,8},{16,20},{20,16},{24,28},{28,24},{1,5},{5... | collective-permute-start | bytes 208904 | tf_op jit(solution)/shard_map/ppermute | solution.py:153
  40.2 5.2 %collective-permute-start.17 = (bf16[3,32,2176]{2,1,0:T(8,128)(2,1)S(1)}, bf16[3,32,2176]{2,1,0:T(8,128)(2,1)S(1)}, u32[]{:S(2)}, u32[]{:S(2)}) collective-permute-start(bf16[3,32,2176]{2,1,0:T(8,128)(2,1)S(1)} %pad_maximum_fusion.refs_0_), channel_id=1, source_target_pairs={{0,1},{1,0},{2,3},{3,2},{4,5},{5,4},{6,7},{7,6},{8,9},{9,8},{10,11... | collective-permute-start | bytes 1253384 | tf_op jit(solution)/shard_map/ppermute | solution.py:153
  40.2 12.1 %collective-permute-start.18 = (bf16[3,32,2176]{2,1,0:T(8,128)(2,1)S(1)}, bf16[3,32,2176]{2,1,0:T(8,128)(2,1)S(1)}, u32[]{:S(2)}, u32[]{:S(2)}) collective-permute-start(bf16[3,32,2176]{2,1,0:T(8,128)(2,1)S(1)} %pad_maximum_fusion.refs_0_), channel_id=1, source_target_pairs={{0,2},{1,3},{2,0},{3,1},{4,6},{5,7},{6,4},{7,5},{8,10},{9,11},{10,... | collective-permute-start | bytes 1253384 | tf_op jit(solution)/shard_map/ppermute | solution.py:153
  40.8 12.1 %collective-permute-start.19 = (bf16[3,32,2176]{2,1,0:T(8,128)(2,1)S(1)}, bf16[3,32,2176]{2,1,0:T(8,128)(2,1)S(1)}, u32[]{:S(2)}, u32[]{:S(2)}) collective-permute-start(bf16[3,32,2176]{2,1,0:T(8,128)(2,1)S(1)} %pad_maximum_fusion.refs_0_), channel_id=1, source_target_pairs={{0,4},{4,0},{8,12},{12,8},{16,20},{20,16},{24,28},{28,24},{1,5},{5... | collective-permute-start | bytes 1253384 | tf_op jit(solution)/shard_map/ppermute | solution.py:153
  52.8 6.9 %collective-permute-start.21 = (bf16[3,16,2176]{2,1,0:T(8,128)(2,1)S(1)}, bf16[3,16,2176]{2,1,0:T(8,128)(2,1)S(1)}, u32[]{:S(2)}, u32[]{:S(2)}) collective-permute-start(bf16[3,16,2176]{2,1,0:T(8,128)(2,1)S(1)} %slice.109), channel_id=1, source_target_pairs={{0,2},{1,3},{2,0},{3,1},{4,6},{5,7},{6,4},{7,5},{8,10},{9,11},{10,... | collective-permute-start | bytes 626696 | tf_op jit(solution)/shard_map/ppermute | solution.py:153
  54.4 6.6 %collective-permute-start.22 = (bf16[3,16,2176]{2,1,0:T(8,128)(2,1)S(1)}, bf16[3,16,2176]{2,1,0:T(8,128)(2,1)S(1)}, u32[]{:S(2)}, u32[]{:S(2)}) collective-permute-start(bf16[3,16,2176]{2,1,0:T(8,128)(2,1)S(1)} %slice.110), channel_id=1, source_target_pairs={{0,4},{4,0},{8,12},{12,8},{16,20},{20,16},{24,28},{28,24},{1,5},{5... | collective-permute-start | bytes 626696 | tf_op jit(solution)/shard_map/ppermute | solution.py:153
  56.2 4.8 %collective-permute-start.20 = (bf16[3,32,2176]{2,1,0:T(8,128)(2,1)S(1)}, bf16[3,32,2176]{2,1,0:T(8,128)(2,1)S(1)}, u32[]{:S(2)}, u32[]{:S(2)}) collective-permute-start(bf16[3,32,2176]{2,1,0:T(8,128)(2,1)S(1)} %collective-permute-done.19.refs_0_), channel_id=1, source_target_pairs={{0,1},{1,0},{2,3},{3,2},{4,5},{5,4},{6,7},{7,6},{8,9},{9,8},{10,11... | collective-permute-start | bytes 1253384 | tf_op jit(solution)/shard_map/ppermute | solution.py:153
  61.1 4.5 %collective-permute-start.23 = (bf16[3,32,2176]{2,1,0:T(8,128)(2,1)S(1)}, bf16[3,32,2176]{2,1,0:T(8,128)(2,1)S(1)}, u32[]{:S(2)}, u32[]{:S(2)}) collective-permute-start(bf16[3,32,2176]{2,1,0:T(8,128)(2,1)S(1)} %collective-permute-done.18.refs_2_), channel_id=1, source_target_pairs={{0,1},{1,0},{2,3},{3,2},{4,5},{5,4},{6,7},{7,6},{8,9},{9,8},{10,11... | collective-permute-start | bytes 1253384 | tf_op jit(solution)/shard_map/ppermute | solution.py:153
  67.6 7.5 %collective-permute-start.28 = (bf16[1,3,128,512]{3,2,1,0:T(8,128)(2,1)S(1)}, bf16[1,3,128,512]{3,2,1,0:T(8,128)(2,1)S(1)}, u32[]{:S(2)}, u32[]{:S(2)}) collective-permute-start(bf16[1,3,128,512]{3,2,1,0:T(8,128)(2,1)S(1)} %get-tuple-element.194), channel_id=1, source_target_pairs={{0,1},{1,0},{2,3},{3,2},{4,5},{5,4},{6,7},{7,6},{8,9},{9,8},{10,11... | collective-permute-start | bytes 1179656 | tf_op jit(solution)/shard_map/ppermute | solution.py:153
  67.8 7.2 %collective-permute-start.27 = (bf16[3,64,512]{2,1,0:T(8,128)(2,1)S(1)}, bf16[3,64,512]{2,1,0:T(8,128)(2,1)S(1)}, u32[]{:S(2)}, u32[]{:S(2)}) collective-permute-start(bf16[3,64,512]{2,1,0:T(8,128)(2,1)S(1)} %get-tuple-element.225), channel_id=1, source_target_pairs={{0,4},{4,0},{8,12},{12,8},{16,20},{20,16},{24,28},{28,24},{1,5},{5... | collective-permute-start | bytes 589832 | tf_op jit(solution)/shard_map/ppermute | solution.py:153
  69.3 6.9 %collective-permute-start.29 = (bf16[3,64,512]{2,1,0:T(8,128)(2,1)S(1)}, bf16[3,64,512]{2,1,0:T(8,128)(2,1)S(1)}, u32[]{:S(2)}, u32[]{:S(2)}) collective-permute-start(bf16[3,64,512]{2,1,0:T(8,128)(2,1)S(1)} %get-tuple-element.224), channel_id=1, source_target_pairs={{0,2},{1,3},{2,0},{3,1},{4,6},{5,7},{6,4},{7,5},{8,10},{9,11},{10,... | collective-permute-start | bytes 589832 | tf_op jit(solution)/shard_map/ppermute | solution.py:153
  76.6 10.3 %collective-permute-start.34 = (bf16[3,128,512]{2,1,0:T(8,128)(2,1)S(1)}, bf16[3,128,512]{2,1,0:T(8,128)(2,1)S(1)}, u32[]{:S(2)}, u32[]{:S(2)}) collective-permute-start(bf16[3,128,512]{2,1,0:T(8,128)(2,1)S(1)} %pad_maximum_fusion.3), channel_id=1, source_target_pairs={{0,2},{1,3},{2,0},{3,1},{4,6},{5,7},{6,4},{7,5},{8,10},{9,11},{10,... | collective-permute-start | bytes 1179656 | tf_op jit(solution)/shard_map/ppermute | solution.py:153
  77.2 10.0 %collective-permute-start.33 = (bf16[3,128,512]{2,1,0:T(8,128)(2,1)S(1)}, bf16[3,128,512]{2,1,0:T(8,128)(2,1)S(1)}, u32[]{:S(2)}, u32[]{:S(2)}) collective-permute-start(bf16[3,128,512]{2,1,0:T(8,128)(2,1)S(1)} %pad_maximum_fusion.2), channel_id=1, source_target_pairs={{0,4},{4,0},{8,12},{12,8},{16,20},{20,16},{24,28},{28,24},{1,5},{5... | collective-permute-start | bytes 1179656 | tf_op jit(solution)/shard_map/ppermute | solution.py:153
  77.7 9.6 %collective-permute-start.32 = (bf16[1,3,128,512]{3,2,1,0:T(8,128)(2,1)S(1)}, bf16[1,3,128,512]{3,2,1,0:T(8,128)(2,1)S(1)}, u32[]{:S(2)}, u32[]{:S(2)}) collective-permute-start(bf16[1,3,128,512]{3,2,1,0:T(8,128)(2,1)S(1)} %get-tuple-element.198), channel_id=1, source_target_pairs={{0,1},{1,0},{2,3},{3,2},{4,5},{5,4},{6,7},{7,6},{8,9},{9,8},{10,11... | collective-permute-start | bytes 1179656 | tf_op jit(solution)/shard_map/ppermute | solution.py:153
  77.7 9.6 %collective-permute-start.30 = (bf16[2,1,128,512]{3,2,1,0:T(8,128)(2,1)S(1)}, bf16[2,1,128,512]{3,2,1,0:T(8,128)(2,1)S(1)}, u32[]{:S(2)}, u32[]{:S(2)}) collective-permute-start(bf16[2,1,128,512]{3,2,1,0:T(8,128)(2,1)S(1)} %get-tuple-element.196), channel_id=1, source_target_pairs={{0,1},{1,0},{2,3},{3,2},{4,5},{5,4},{6,7},{7,6},{8,9},{9,8},{10,11... | collective-permute-start | bytes 786440 | tf_op jit(solution)/shard_map/ppermute | solution.py:153
  78.2 9.1 %collective-permute-start.31 = (bf16[2,1,128,512]{3,2,1,0:T(8,128)(2,1)S(1)}, bf16[2,1,128,512]{3,2,1,0:T(8,128)(2,1)S(1)}, u32[]{:S(2)}, u32[]{:S(2)}) collective-permute-start(bf16[2,1,128,512]{3,2,1,0:T(8,128)(2,1)S(1)} %get-tuple-element.197), channel_id=1, source_target_pairs={{0,1},{1,0},{2,3},{3,2},{4,5},{5,4},{6,7},{7,6},{8,9},{9,8},{10,11... | collective-permute-start | bytes 786440 | tf_op jit(solution)/shard_map/ppermute | solution.py:153
  87.6 7.7 %collective-permute-start.36 = (bf16[128,512]{1,0:T(8,128)(2,1)S(1)}, bf16[128,512]{1,0:T(8,128)(2,1)S(1)}, u32[]{:S(2)}, u32[]{:S(2)}) collective-permute-start(bf16[128,512]{1,0:T(8,128)(2,1)S(1)} %get-tuple-element.223), channel_id=1, source_target_pairs={{0,8},{4,12},{8,0},{12,4},{16,24},{20,28},{24,16},{28,20},{1,9},{5... | collective-permute-start | bytes 393224 | tf_op jit(solution)/shard_map/ppermute | solution.py:153
  89.8 4.3 %collective-permute-start.37 = (bf16[1,64,512]{2,1,0:T(8,128)(2,1)S(1)}, bf16[1,64,512]{2,1,0:T(8,128)(2,1)S(1)}, u32[]{:S(2)}, u32[]{:S(2)}) collective-permute-start(bf16[1,64,512]{2,1,0:T(8,128)(2,1)S(1)} %get-tuple-element.227), channel_id=1, source_target_pairs={{0,4},{4,0},{8,12},{12,8},{16,20},{20,16},{24,28},{28,24},{1,5},{5... | collective-permute-start | bytes 196616 | tf_op jit(solution)/shard_map/ppermute | solution.py:153
  90.6 4.7 %collective-permute-start.38 = (bf16[1,64,512]{2,1,0:T(8,128)(2,1)S(1)}, bf16[1,64,512]{2,1,0:T(8,128)(2,1)S(1)}, u32[]{:S(2)}, u32[]{:S(2)}) collective-permute-start(bf16[1,64,512]{2,1,0:T(8,128)(2,1)S(1)} %get-tuple-element.226), channel_id=1, source_target_pairs={{0,2},{1,3},{2,0},{3,1},{4,6},{5,7},{6,4},{7,5},{8,10},{9,11},{10,... | collective-permute-start | bytes 196616 | tf_op jit(solution)/shard_map/ppermute | solution.py:153
  92.1 6.7 %collective-permute-start.35 = (bf16[128,512]{1,0:T(8,128)(2,1)S(1)}, bf16[128,512]{1,0:T(8,128)(2,1)S(1)}, u32[]{:S(2)}, u32[]{:S(2)}) collective-permute-start(bf16[128,512]{1,0:T(8,128)(2,1)S(1)} %get-tuple-element.222), channel_id=1, source_target_pairs={{0,8},{4,12},{8,0},{12,4},{16,24},{20,28},{24,16},{28,20},{1,9},{5... | collective-permute-start | bytes 393224 | tf_op jit(solution)/shard_map/ppermute | solution.py:153
  95.4 8.4 %collective-permute-start.41 = (bf16[1,128,512]{2,1,0:T(8,128)(2,1)S(1)}, bf16[1,128,512]{2,1,0:T(8,128)(2,1)S(1)}, u32[]{:S(2)}, u32[]{:S(2)}) collective-permute-start(bf16[1,128,512]{2,1,0:T(8,128)(2,1)S(1)} %pad_maximum_fusion.6), channel_id=1, source_target_pairs={{0,2},{1,3},{2,0},{3,1},{4,6},{5,7},{6,4},{7,5},{8,10},{9,11},{10,... | collective-permute-start | bytes 393224 | tf_op jit(solution)/shard_map/ppermute | solution.py:153
  96.9 6.9 %collective-permute-start.39 = (bf16[128,512]{1,0:T(8,128)(2,1)S(1)}, bf16[128,512]{1,0:T(8,128)(2,1)S(1)}, u32[]{:S(2)}, u32[]{:S(2)}) collective-permute-start(bf16[128,512]{1,0:T(8,128)(2,1)S(1)} %fusion.5), channel_id=1, source_target_pairs={{0,16},{4,20},{8,24},{12,28},{16,0},{20,4},{24,8},{28,12},{1,17},{... | collective-permute-start | bytes 393224 | tf_op jit(solution)/shard_map/ppermute | solution.py:153
  97.3 6.5 %collective-permute-start.40 = (bf16[1,128,512]{2,1,0:T(8,128)(2,1)S(1)}, bf16[1,128,512]{2,1,0:T(8,128)(2,1)S(1)}, u32[]{:S(2)}, u32[]{:S(2)}) collective-permute-start(bf16[1,128,512]{2,1,0:T(8,128)(2,1)S(1)} %pad_maximum_fusion.5), channel_id=1, source_target_pairs={{0,4},{4,0},{8,12},{12,8},{16,20},{20,16},{24,28},{28,24},{1,5},{5... | collective-permute-start | bytes 393224 | tf_op jit(solution)/shard_map/ppermute | solution.py:153
  (17 other events, 193.4 us)

commit v16 on v14

--- a/solution.py
+++ b/solution.py
@@ -503,15 +503,6 @@
     return keep, send
 
 
-def finish_kernel(own_ref, z1_ref, z2_ref, x_ref, y_ref, out_ref):
-    total = own_ref[0]
-    for extra_ref in (x_ref, y_ref):
-        total = total + extra_ref[0].astype(jnp.float32)
-    for extra_ref in (z1_ref, z2_ref):
-        total = total + extra_ref[...].astype(jnp.float32)
-    out_ref[...] = total.astype(jnp.bfloat16)
-
-
 def ordered(*values):
     return lax.optimization_barrier(values)
 
@@ -646,10 +637,9 @@
         with_upper(joined((keep, (send, first)), 0, 0), by_y),
     )
     to_y = with_lower(joined((near_keep, (near_send, near_first)), 0, 1), by_x)
-    sums_3 = flip(to_x, "req", 1), flip(to_y, "tp", 2)
+    sums_3 = flip(to_x, "req", 1).astype(jnp.float32) + flip(to_y, "tp", 2).astype(jnp.float32)
     all_0, near_send, sums_3 = ordered(with_core(all_0), flip(near_send, "tp", 1), sums_3)
-    near_3 = (near_keep, (near_send, near_first))
-    sent = joined(near_3, 0, 0) + sums_3[0].astype(jnp.float32) + sums_3[1].astype(jnp.float32)
+    sent = joined((near_keep, (near_send, near_first)), 0, 0) + sums_3
     sent_3, relay_0 = ordered(
         flip(sent[2].astype(jnp.bfloat16), "req", 2), relayed(joined(all_0, 1, 1))
     )
@@ -658,14 +648,9 @@
     )
     from_z = [flip(sent[0].astype(jnp.bfloat16), "req", 2), flip(sent_2, "req", 4)]
     sums_0 = neighbours(joined(all_0, 1, 0), joined(all_0, 0, 1), *relay_0)
-    return pl.pallas_call(
-        finish_kernel,
-        out_shape=jax.ShapeDtypeStruct((token_count, share_width), jnp.bfloat16),
-        in_specs=[VMEM] * 5,
-        out_specs=VMEM,
-        compiler_params=pltpu.CompilerParams(vmem_limit_bytes=8 * 1024 * 1024),
-        name="finish",
-    )(joined(all_0, 0, 0), *from_z, *sums_0)
+    total = joined(all_0, 0, 0) + from_z[0].astype(jnp.float32) + from_z[1].astype(jnp.float32)
+    total, from_x, from_y = ordered(total[0], *sums_0)
+    return (total + from_x[0].astype(jnp.float32) + from_y[0].astype(jnp.float32)).astype(jnp.bfloat16)
 
 
 def moe_routed(

time: 102 us -> 98.7 us (0.968)
  waiting for transfers between devices: 49.6 us -> 47.2 us
  starting transfers between devices: 32.9 us -> 31.8 us
    ppermute x42, waiting for transfers between devices: 49.6 us -> 47.2 us  [flip(): lax.ppermute(value, axis, [(i, i ^ bits) for i in range(lax.axis_size(axi...]
    ppermute x42, starting transfers between devices: 32.9 us -> 31.8 us  [flip(): lax.ppermute(value, axis, [(i, i ^ bits) for i in range(lax.axis_size(axi...]
  transfers between devices with their start and end apart: 42 -> 42, of which waited for: 26 -> 25; matrix products, arithmetic and copies ran while one was open for 1% -> 1% of each run, Pallas kernels for 12% -> 12%
where the time goes in v16:
time: 98.7 us; the launch traced here: 98.6 us
  waiting for transfers between devices  47.2 us (48%)
  starting transfers between devices  31.8 us (32%)
  Pallas kernels  16.9 us (17%)
  other arithmetic  2.02 us (2%)
    ppermute x42, waiting for transfers between devices, flip(): lax.ppermute(value, axis, [(i, i ^ bits) for i in range(lax.axis_size(axi...  47.2 us
    ppermute x42, starting transfers between devices, flip(): lax.ppermute(value, axis, [(i, i ^ bits) for i in range(lax.axis_size(axi...  31.8 us
    pallas_call x3, Pallas kernels, run_experts(): pl.pallas_call(functools.partial(experts_kernel, plan, len(residual)), ou...  7.46 us
    pallas_call x1, Pallas kernels, attention_shares(): pl.pallas_call(attention_kernel, out_shape=[jax.ShapeDtypeStruct(share, j...  4.88 us
    pallas_call x1, Pallas kernels, attention_shares(): pl.pallas_call(stage_kernel, out_shape=[rope, rope, pltpu.VMEM((1, POOL *...  4.41 us
  transfers between devices with their start and end apart: 42, of which 25 were waited for; matrix products, arithmetic and copies ran while one was open for 1% of the time, Pallas kernels for 12%

profile of v16, /device:TPU:0, one launch (start us, length us, event | category | flops | bytes accessed | tf_op | source)
XLA Modules:
  0.0 98.6 jit_solution(1018085576841674601)
XLA Ops:
  0.0 3.0 %collective-permute-start.1 = (bf16[128,512]{1,0:T(8,128)(2,1)}, bf16[128,512]{1,0:T(8,128)(2,1)S(1)}, u32[]{:S(2)}, u32[]{:S(2)}) collective-permute-start(bf16[128,512]{1,0:T(8,128)(2,1)} %refs_0_.3), channel_id=1, source_target_pairs={{0,2},{1,3},{2,0},{3,1},{4,6},{5,7},{6,4},{7,5},{8,10},{9,11},{10,... | collective-permute-start | bytes 393224 | tf_op jit(solution)/shard_map/ppermute | solution.py:153
  3.0 4.4 %stage.1 = (f32[128,128]{1,0:T(8,128)S(1)}, f32[128,128]{1,0:T(8,128)S(1)}, s32[1,6144]{1,0:T(1,128)S(1)}, f32[1,2048]{1,0:T(1,128)S(1)}, f32[1,128]{1,0:T(1,128...) custom-call(s32[9]{0:T(128)} %refs_0_.2, ...), custom_call_target="tpu_custom_call" | custom-call | tf_op jit(solution)/shard_map/stage/pallas_call | solution.py:373
  9.0 4.9 %attention.1 = (f32[32,2048]{1,0:T(8,128)S(1)}, f32[32,2048]{1,0:T(8,128)S(1)}, bf16[2,32,2048]{2,1,0:T(8,128)(2,1)S(1)}) custom-call(bf16[128,512]{1,0:T(8,128)(2,1)S(1)} %copy-done.3, bf16[128,512]{1,0:T(8,128)(2,1)S(1)} %collective-permute-done.refs_1_, bf16[128,512]{1,0:T(8,128)(2,1)S(1)} %collective-permute-done.1.refs_2_, ...), custom_call_target="tpu_custom_call" | custom-call | tf_op jit(solution)/shard_map/attention/pallas_call | solution.py:393
  14.3 1.2 %collective-permute-done.3 = bf16[2,32,2048]{2,1,0:T(8,128)(2,1)S(1)} collective-permute-done((bf16[2,32,2048]{2,1,0:T(8,128)(2,1)S(1)}, bf16[2,32,2048]{2,1,0:T(8,128)(2,1)S(1)}, u32[]{:S(2)}, u32[]{:S(2)}) %collective-permute-start.3) | collective-permute-done | bytes 262176 | tf_op jit(solution)/shard_map/ppermute | solution.py:153
  16.4 4.9 %collective-permute-done.4.far_ref = bf16[32,2048]{1,0:T(8,128)(2,1)S(1)} collective-permute-done((bf16[32,2048]{1,0:T(8,128)(2,1)S(1)}, bf16[32,2048]{1,0:T(8,128)(2,1)S(1)}, u32[]{:S(2)}, u32[]{:S(2)}) %collective-permute-start.4) | collective-permute-done | bytes 131104 | tf_op jit(solution)/shard_map/ppermute | solution.py:153
  21.5 2.7 %collective-permute-start.6 = (bf16[1,32,2176]{2,1,0:T(8,128)(2,1)S(1)}, bf16[1,32,2176]{2,1,0:T(8,128)(2,1)S(1)}, u32[]{:S(2)}, u32[]{:S(2)}) collective-permute-start(bf16[1,32,2176]{2,1,0:T(8,128)(2,1)S(1)} %bitcast.91), channel_id=1, source_target_pairs={{0,16},{4,20},{8,24},{12,28},{16,0},{20,4},{24,8},{28,12},{1,17},{... | collective-permute-start | bytes 417800 | tf_op jit(solution)/shard_map/ppermute | solution.py:153
  24.2 1.6 %collective-permute-start.5 = (bf16[1,32,2176]{2,1,0:T(8,128)(2,1)S(1)}, bf16[1,32,2176]{2,1,0:T(8,128)(2,1)S(1)}, u32[]{:S(2)}, u32[]{:S(2)}) collective-permute-start(bf16[1,32,2176]{2,1,0:T(8,128)(2,1)S(1)} %bitcast.92), channel_id=1, source_target_pairs={{0,8},{4,12},{8,0},{12,4},{16,24},{20,28},{24,16},{28,20},{1,9},{5... | collective-permute-start | bytes 417800 | tf_op jit(solution)/shard_map/ppermute | solution.py:153
  25.8 1.5 %collective-permute-start.8 = (bf16[1,32,2176]{2,1,0:T(8,128)(2,1)S(1)}, bf16[1,32,2176]{2,1,0:T(8,128)(2,1)S(1)}, u32[]{:S(2)}, u32[]{:S(2)}) collective-permute-start(bf16[1,32,2176]{2,1,0:T(8,128)(2,1)S(1)} %bitcast.93), channel_id=1, source_target_pairs={{0,4},{4,0},{8,12},{12,8},{16,20},{20,16},{24,28},{28,24},{1,5},{5... | collective-permute-start | bytes 417800 | tf_op jit(solution)/shard_map/ppermute | solution.py:153
  27.8 2.9 %collective-permute-done.6 = bf16[1,32,2176]{2,1,0:T(8,128)(2,1)S(1)} collective-permute-done((bf16[1,32,2176]{2,1,0:T(8,128)(2,1)S(1)}, bf16[1,32,2176]{2,1,0:T(8,128)(2,1)S(1)}, u32[]{:S(2)}, u32[]{:S(2)}) %collective-permute-start.6) | collective-permute-done | bytes 139296 | tf_op jit(solution)/shard_map/ppermute | solution.py:153
  31.0 1.3 %collective-permute-done.7.refs_2_ = bf16[1,32,2176]{2,1,0:T(8,128)(2,1)S(1)} collective-permute-done((bf16[1,32,2176]{2,1,0:T(8,128)(2,1)S(1)}, bf16[1,32,2176]{2,1,0:T(8,128)(2,1)S(1)}, u32[]{:S(2)}, u32[]{:S(2)}) %collective-permute-start.7) | collective-permute-done | bytes 139296 | tf_op jit(solution)/shard_map/ppermute | solution.py:153
  33.3 1.1 %collective-permute-start.12 = (bf16[1,16,2176]{2,1,0:T(8,128)(2,1)S(1)}, bf16[1,16,2176]{2,1,0:T(8,128)(2,1)S(1)}, u32[]{:S(2)}, u32[]{:S(2)}) collective-permute-start(bf16[1,16,2176]{2,1,0:T(8,128)(2,1)S(1)} %slice.108), channel_id=1, source_target_pairs={{0,4},{4,0},{8,12},{12,8},{16,20},{20,16},{24,28},{28,24},{1,5},{5... | collective-permute-start | bytes 208904 | tf_op jit(solution)/shard_map/ppermute | solution.py:153
  34.8 2.6 %collective-permute-done.10 = bf16[1,32,2176]{2,1,0:T(8,128)(2,1)S(1)} collective-permute-done((bf16[1,32,2176]{2,1,0:T(8,128)(2,1)S(1)}, bf16[1,32,2176]{2,1,0:T(8,128)(2,1)S(1)}, u32[]{:S(2)}, u32[]{:S(2)}) %collective-permute-start.10) | collective-permute-done | bytes 139296 | tf_op jit(solution)/shard_map/ppermute | solution.py:153
  37.6 1.1 %collective-permute-done.11.refs_6_ = bf16[1,16,2176]{2,1,0:T(8,128)(2,1)S(1)} collective-permute-done((bf16[1,16,2176]{2,1,0:T(8,128)(2,1)S(1)}, bf16[1,16,2176]{2,1,0:T(8,128)(2,1)S(1)}, u32[]{:S(2)}, u32[]{:S(2)}) %collective-permute-start.11) | collective-permute-done | bytes 69664 | tf_op jit(solution)/shard_map/ppermute | solution.py:153
  40.7 1.4 %collective-permute-done.9.refs_5_ = bf16[1,32,2176]{2,1,0:T(8,128)(2,1)S(1)} collective-permute-done((bf16[1,32,2176]{2,1,0:T(8,128)(2,1)S(1)}, bf16[1,32,2176]{2,1,0:T(8,128)(2,1)S(1)}, u32[]{:S(2)}, u32[]{:S(2)}) %collective-permute-start.9) | collective-permute-done | bytes 139296 | tf_op jit(solution)/shard_map/ppermute | solution.py:153
  42.3 1.1 %collective-permute-done.16.refs_9_ = bf16[1,16,2176]{2,1,0:T(8,128)(2,1)S(1)} collective-permute-done((bf16[1,16,2176]{2,1,0:T(8,128)(2,1)S(1)}, bf16[1,16,2176]{2,1,0:T(8,128)(2,1)S(1)}, u32[]{:S(2)}, u32[]{:S(2)}) %collective-permute-start.16) | collective-permute-done | bytes 69664 | tf_op jit(solution)/shard_map/ppermute | solution.py:153
  43.4 5.8 %collective-permute-done.19.refs_0_ = bf16[3,32,2176]{2,1,0:T(8,128)(2,1)S(1)} collective-permute-done((bf16[3,32,2176]{2,1,0:T(8,128)(2,1)S(1)}, bf16[3,32,2176]{2,1,0:T(8,128)(2,1)S(1)}, u32[]{:S(2)}, u32[]{:S(2)}) %collective-permute-start.19) | collective-permute-done | bytes 417824 | tf_op jit(solution)/shard_map/ppermute | solution.py:153
  51.5 2.0 %experts.3 = (f32[2,2,1,128,512]{4,3,2,1,0:T(8,128)S(1)}, bf16[2,1,128,512]{3,2,1,0:T(8,128)(2,1)S(1)}, bf16[2,1,128,512]{3,2,1,0:T(8,128)(2,1)S(1)}) custom-call(bf16[1,32,2176]{2,1,0:T(8,128)(2,1)S(1)} %bitcast.96, bf16[1,32,2176]{2,1,0:T(8,128)(2,1)S(1)} %collective-permute-done.13.refs_1_, bf16[1,32,2176]{2,1,0:T(8,128)(2,1)S(1)} %collective-permute-done.7.refs_2_, ...), custom_call_target="tpu_custom_call" | custom-call | tf_op jit(solution)/shard_map/experts/pallas_call | solution.py:490
  53.5 2.3 %collective-permute-done.21 = bf16[3,16,2176]{2,1,0:T(8,128)(2,1)S(1)} collective-permute-done((bf16[3,16,2176]{2,1,0:T(8,128)(2,1)S(1)}, bf16[3,16,2176]{2,1,0:T(8,128)(2,1)S(1)}, u32[]{:S(2)}, u32[]{:S(2)}) %collective-permute-start.21) | collective-permute-done | bytes 208928 | tf_op jit(solution)/shard_map/ppermute | solution.py:153
  57.0 1.2 %collective-permute-done.24.refs_3_ = bf16[3,32,2176]{2,1,0:T(8,128)(2,1)S(1)} collective-permute-done((bf16[3,32,2176]{2,1,0:T(8,128)(2,1)S(1)}, bf16[3,32,2176]{2,1,0:T(8,128)(2,1)S(1)}, u32[]{:S(2)}, u32[]{:S(2)}) %collective-permute-start.24) | collective-permute-done | bytes 417824 | tf_op jit(solution)/shard_map/ppermute | solution.py:153
  58.2 2.7 %experts.4 = (f32[1,2,3,128,512]{4,3,2,1,0:T(8,128)S(1)}, bf16[1,3,128,512]{3,2,1,0:T(8,128)(2,1)S(1)}, bf16[1,3,128,512]{3,2,1,0:T(8,128)(2,1)S(1)}) custom-call(bf16[3,32,2176]{2,1,0:T(8,128)(2,1)S(1)} %collective-permute-done.19.refs_0_, bf16[3,32,2176]{2,1,0:T(8,128)(2,1)S(1)} %collective-permute-done.20.refs_1_, ...), custom_call_target="tpu_custom_call" | custom-call | tf_op jit(solution)/shard_map/experts/pallas_call | solution.py:490
  61.2 1.6 %collective-permute-done.25 = bf16[1,3,128,512]{3,2,1,0:T(8,128)(2,1)S(1)} collective-permute-done((bf16[1,3,128,512]{3,2,1,0:T(8,128)(2,1)S(1)}, bf16[1,3,128,512]{3,2,1,0:T(8,128)(2,1)S(1)}, u32[]{:S(2)}, u32[]{:S(2)}) %collective-permute-start.25) | collective-permute-done | bytes 393248 | tf_op jit(solution)/shard_map/ppermute | solution.py:153
  64.1 1.7 %collective-permute-start.29 = (bf16[3,64,512]{2,1,0:T(8,128)(2,1)S(1)}, bf16[3,64,512]{2,1,0:T(8,128)(2,1)S(1)}, u32[]{:S(2)}, u32[]{:S(2)}) collective-permute-start(bf16[3,64,512]{2,1,0:T(8,128)(2,1)S(1)} %get-tuple-element.232), channel_id=1, source_target_pairs={{0,2},{1,3},{2,0},{3,1},{4,6},{5,7},{6,4},{7,5},{8,10},{9,11},{10,... | collective-permute-start | bytes 589832 | tf_op jit(solution)/shard_map/ppermute | solution.py:153
  65.8 2.7 %experts.5 = (f32[1,2,3,128,512]{4,3,2,1,0:T(8,128)S(1)}, bf16[1,3,128,512]{3,2,1,0:T(8,128)(2,1)S(1)}, bf16[1,3,128,512]{3,2,1,0:T(8,128)(2,1)S(1)}) custom-call(bf16[3,32,2176]{2,1,0:T(8,128)(2,1)S(1)} %pad_maximum_fusion.refs_0_, bf16[3,32,2176]{2,1,0:T(8,128)(2,1)S(1)} %collective-permute-done.17.refs_1_, ...), custom_call_target="tpu_custom_call" | custom-call | tf_op jit(solution)/shard_map/experts/pallas_call | solution.py:490
  68.6 1.8 %collective-permute-done.27 = bf16[3,64,512]{2,1,0:T(8,128)(2,1)S(1)} collective-permute-done((bf16[3,64,512]{2,1,0:T(8,128)(2,1)S(1)}, bf16[3,64,512]{2,1,0:T(8,128)(2,1)S(1)}, u32[]{:S(2)}, u32[]{:S(2)}) %collective-permute-start.27) | collective-permute-done | bytes 196640 | tf_op jit(solution)/shard_map/ppermute | solution.py:153
  71.1 1.2 %collective-permute-start.33 = (bf16[3,128,512]{2,1,0:T(8,128)(2,1)S(1)}, bf16[3,128,512]{2,1,0:T(8,128)(2,1)S(1)}, u32[]{:S(2)}, u32[]{:S(2)}) collective-permute-start(bf16[3,128,512]{2,1,0:T(8,128)(2,1)S(1)} %pad_maximum_fusion.2), channel_id=1, source_target_pairs={{0,4},{4,0},{8,12},{12,8},{16,20},{20,16},{24,28},{28,24},{1,5},{5... | collective-permute-start | bytes 1179656 | tf_op jit(solution)/shard_map/ppermute | solution.py:153
  72.6 1.5 %collective-permute-start.34 = (bf16[3,128,512]{2,1,0:T(8,128)(2,1)S(1)}, bf16[3,128,512]{2,1,0:T(8,128)(2,1)S(1)}, u32[]{:S(2)}, u32[]{:S(2)}) collective-permute-start(bf16[3,128,512]{2,1,0:T(8,128)(2,1)S(1)} %pad_maximum_fusion.3), channel_id=1, source_target_pairs={{0,2},{1,3},{2,0},{3,1},{4,6},{5,7},{6,4},{7,5},{8,10},{9,11},{10,... | collective-permute-start | bytes 1179656 | tf_op jit(solution)/shard_map/ppermute | solution.py:153
  74.6 6.9 %collective-permute-done.33 = bf16[3,128,512]{2,1,0:T(8,128)(2,1)S(1)} collective-permute-done((bf16[3,128,512]{2,1,0:T(8,128)(2,1)S(1)}, bf16[3,128,512]{2,1,0:T(8,128)(2,1)S(1)}, u32[]{:S(2)}, u32[]{:S(2)}) %collective-permute-start.33) | collective-permute-done | bytes 393248 | tf_op jit(solution)/shard_map/ppermute | solution.py:153
  83.0 1.3 %collective-permute-start.36 = (bf16[128,512]{1,0:T(8,128)(2,1)S(1)}, bf16[128,512]{1,0:T(8,128)(2,1)S(1)}, u32[]{:S(2)}, u32[]{:S(2)}) collective-permute-start(bf16[128,512]{1,0:T(8,128)(2,1)S(1)} %get-tuple-element.231), channel_id=1, source_target_pairs={{0,8},{4,12},{8,0},{12,4},{16,24},{20,28},{24,16},{28,20},{1,9},{5... | collective-permute-start | bytes 393224 | tf_op jit(solution)/shard_map/ppermute | solution.py:153
  84.5 1.5 %collective-permute-start.38 = (bf16[1,64,512]{2,1,0:T(8,128)(2,1)S(1)}, bf16[1,64,512]{2,1,0:T(8,128)(2,1)S(1)}, u32[]{:S(2)}, u32[]{:S(2)}) collective-permute-start(bf16[1,64,512]{2,1,0:T(8,128)(2,1)S(1)} %get-tuple-element.234), channel_id=1, source_target_pairs={{0,2},{1,3},{2,0},{3,1},{4,6},{5,7},{6,4},{7,5},{8,10},{9,11},{10,... | collective-permute-start | bytes 196616 | tf_op jit(solution)/shard_map/ppermute | solution.py:153
  88.8 1.5 %collective-permute-done.37 = bf16[1,64,512]{2,1,0:T(8,128)(2,1)S(1)} collective-permute-done((bf16[1,64,512]{2,1,0:T(8,128)(2,1)S(1)}, bf16[1,64,512]{2,1,0:T(8,128)(2,1)S(1)}, u32[]{:S(2)}, u32[]{:S(2)}) %collective-permute-start.37) | collective-permute-done | bytes 65568 | tf_op jit(solution)/shard_map/ppermute | solution.py:153
  90.4 1.4 %collective-permute-start.39 = (bf16[128,512]{1,0:T(8,128)(2,1)S(1)}, bf16[128,512]{1,0:T(8,128)(2,1)S(1)}, u32[]{:S(2)}, u32[]{:S(2)}) collective-permute-start(bf16[128,512]{1,0:T(8,128)(2,1)S(1)} %fusion.5), channel_id=1, source_target_pairs={{0,16},{4,20},{8,24},{12,28},{16,0},{20,4},{24,8},{28,12},{1,17},{... | collective-permute-start | bytes 393224 | tf_op jit(solution)/shard_map/ppermute | solution.py:153
  93.3 4.4 %collective-permute-done.39 = bf16[128,512]{1,0:T(8,128)(2,1)S(1)} collective-permute-done((bf16[128,512]{1,0:T(8,128)(2,1)S(1)}, bf16[128,512]{1,0:T(8,128)(2,1)S(1)}, u32[]{:S(2)}, u32[]{:S(2)}) %collective-permute-start.39) | collective-permute-done | bytes 131104 | tf_op jit(solution)/shard_map/ppermute | solution.py:153
  (106 shorter events, 20.8 us)
Async XLA Ops:
  0.0 7.4 %collective-permute-start.1 = (bf16[128,512]{1,0:T(8,128)(2,1)}, bf16[128,512]{1,0:T(8,128)(2,1)S(1)}, u32[]{:S(2)}, u32[]{:S(2)}) collective-permute-start(bf16[128,512]{1,0:T(8,128)(2,1)} %refs_0_.3), channel_id=1, source_target_pairs={{0,2},{1,3},{2,0},{3,1},{4,6},{5,7},{6,4},{7,5},{8,10},{9,11},{10,... | collective-permute-start | bytes 393224 | tf_op jit(solution)/shard_map/ppermute | solution.py:153
  3.0 5.0 %collective-permute-start = (bf16[128,512]{1,0:T(8,128)(2,1)}, bf16[128,512]{1,0:T(8,128)(2,1)S(1)}, u32[]{:S(2)}, u32[]{:S(2)}) collective-permute-start(bf16[128,512]{1,0:T(8,128)(2,1)} %refs_0_.3), channel_id=1, source_target_pairs={{0,1},{1,0},{2,3},{3,2},{4,5},{5,4},{6,7},{7,6},{8,9},{9,8},{10,11... | collective-permute-start | bytes 393224 | tf_op jit(solution)/shard_map/ppermute | solution.py:153
  15.5 5.8 %collective-permute-start.4 = (bf16[32,2048]{1,0:T(8,128)(2,1)S(1)}, bf16[32,2048]{1,0:T(8,128)(2,1)S(1)}, u32[]{:S(2)}, u32[]{:S(2)}) collective-permute-start(bf16[32,2048]{1,0:T(8,128)(2,1)S(1)} %fusion.10), channel_id=1, source_target_pairs={{0,2},{1,3},{2,0},{3,1},{4,6},{5,7},{6,4},{7,5},{8,10},{9,11},{10,... | collective-permute-start | bytes 393224 | tf_op jit(solution)/shard_map/ppermute | solution.py:153
  21.5 9.2 %collective-permute-start.6 = (bf16[1,32,2176]{2,1,0:T(8,128)(2,1)S(1)}, bf16[1,32,2176]{2,1,0:T(8,128)(2,1)S(1)}, u32[]{:S(2)}, u32[]{:S(2)}) collective-permute-start(bf16[1,32,2176]{2,1,0:T(8,128)(2,1)S(1)} %bitcast.91), channel_id=1, source_target_pairs={{0,16},{4,20},{8,24},{12,28},{16,0},{20,4},{24,8},{28,12},{1,17},{... | collective-permute-start | bytes 417800 | tf_op jit(solution)/shard_map/ppermute | solution.py:153
  24.2 6.7 %collective-permute-start.5 = (bf16[1,32,2176]{2,1,0:T(8,128)(2,1)S(1)}, bf16[1,32,2176]{2,1,0:T(8,128)(2,1)S(1)}, u32[]{:S(2)}, u32[]{:S(2)}) collective-permute-start(bf16[1,32,2176]{2,1,0:T(8,128)(2,1)S(1)} %bitcast.92), channel_id=1, source_target_pairs={{0,8},{4,12},{8,0},{12,4},{16,24},{20,28},{24,16},{28,20},{1,9},{5... | collective-permute-start | bytes 417800 | tf_op jit(solution)/shard_map/ppermute | solution.py:153
  25.8 5.2 %collective-permute-start.8 = (bf16[1,32,2176]{2,1,0:T(8,128)(2,1)S(1)}, bf16[1,32,2176]{2,1,0:T(8,128)(2,1)S(1)}, u32[]{:S(2)}, u32[]{:S(2)}) collective-permute-start(bf16[1,32,2176]{2,1,0:T(8,128)(2,1)S(1)} %bitcast.93), channel_id=1, source_target_pairs={{0,4},{4,0},{8,12},{12,8},{16,20},{20,16},{24,28},{28,24},{1,5},{5... | collective-permute-start | bytes 417800 | tf_op jit(solution)/shard_map/ppermute | solution.py:153
  27.3 5.1 %collective-permute-start.7 = (bf16[1,32,2176]{2,1,0:T(8,128)(2,1)S(1)}, bf16[1,32,2176]{2,1,0:T(8,128)(2,1)S(1)}, u32[]{:S(2)}, u32[]{:S(2)}) collective-permute-start(bf16[1,32,2176]{2,1,0:T(8,128)(2,1)S(1)} %bitcast.94), channel_id=1, source_target_pairs={{0,2},{1,3},{2,0},{3,1},{4,6},{5,7},{6,4},{7,5},{8,10},{9,11},{10,... | collective-permute-start | bytes 417800 | tf_op jit(solution)/shard_map/ppermute | solution.py:153
  32.3 5.1 %collective-permute-start.10 = (bf16[1,32,2176]{2,1,0:T(8,128)(2,1)S(1)}, bf16[1,32,2176]{2,1,0:T(8,128)(2,1)S(1)}, u32[]{:S(2)}, u32[]{:S(2)}) collective-permute-start(bf16[1,32,2176]{2,1,0:T(8,128)(2,1)S(1)} %collective-permute-done.6), channel_id=1, source_target_pairs={{0,8},{4,12},{8,0},{12,4},{16,24},{20,28},{24,16},{28,20},{1,9},{5... | collective-permute-start | bytes 417800 | tf_op jit(solution)/shard_map/ppermute | solution.py:153
  32.8 4.7 %collective-permute-start.13 = (bf16[1,32,2176]{2,1,0:T(8,128)(2,1)S(1)}, bf16[1,32,2176]{2,1,0:T(8,128)(2,1)S(1)}, u32[]{:S(2)}, u32[]{:S(2)}) collective-permute-start(bf16[1,32,2176]{2,1,0:T(8,128)(2,1)S(1)} %bitcast.95), channel_id=1, source_target_pairs={{0,1},{1,0},{2,3},{3,2},{4,5},{5,4},{6,7},{7,6},{8,9},{9,8},{10,11... | collective-permute-start | bytes 417800 | tf_op jit(solution)/shard_map/ppermute | solution.py:153
  32.8 6.0 %collective-permute-start.14 = (bf16[1,32,2176]{2,1,0:T(8,128)(2,1)S(1)}, bf16[1,32,2176]{2,1,0:T(8,128)(2,1)S(1)}, u32[]{:S(2)}, u32[]{:S(2)}) collective-permute-start(bf16[1,32,2176]{2,1,0:T(8,128)(2,1)S(1)} %collective-permute-done.7.refs_2_), channel_id=1, source_target_pairs={{0,1},{1,0},{2,3},{3,2},{4,5},{5,4},{6,7},{7,6},{8,9},{9,8},{10,11... | collective-permute-start | bytes 417800 | tf_op jit(solution)/shard_map/ppermute | solution.py:153
  33.3 4.3 %collective-permute-start.12 = (bf16[1,16,2176]{2,1,0:T(8,128)(2,1)S(1)}, bf16[1,16,2176]{2,1,0:T(8,128)(2,1)S(1)}, u32[]{:S(2)}, u32[]{:S(2)}) collective-permute-start(bf16[1,16,2176]{2,1,0:T(8,128)(2,1)S(1)} %slice.108), channel_id=1, source_target_pairs={{0,4},{4,0},{8,12},{12,8},{16,20},{20,16},{24,28},{28,24},{1,5},{5... | collective-permute-start | bytes 208904 | tf_op jit(solution)/shard_map/ppermute | solution.py:153
  38.8 10.5 %collective-permute-start.19 = (bf16[3,32,2176]{2,1,0:T(8,128)(2,1)S(1)}, bf16[3,32,2176]{2,1,0:T(8,128)(2,1)S(1)}, u32[]{:S(2)}, u32[]{:S(2)}) collective-permute-start(bf16[3,32,2176]{2,1,0:T(8,128)(2,1)S(1)} %pad_maximum_fusion.refs_0_), channel_id=1, source_target_pairs={{0,4},{4,0},{8,12},{12,8},{16,20},{20,16},{24,28},{28,24},{1,5},{5... | collective-permute-start | bytes 1253384 | tf_op jit(solution)/shard_map/ppermute | solution.py:153
  39.6 10.2 %collective-permute-start.18 = (bf16[3,32,2176]{2,1,0:T(8,128)(2,1)S(1)}, bf16[3,32,2176]{2,1,0:T(8,128)(2,1)S(1)}, u32[]{:S(2)}, u32[]{:S(2)}) collective-permute-start(bf16[3,32,2176]{2,1,0:T(8,128)(2,1)S(1)} %pad_maximum_fusion.refs_0_), channel_id=1, source_target_pairs={{0,2},{1,3},{2,0},{3,1},{4,6},{5,7},{6,4},{7,5},{8,10},{9,11},{10,... | collective-permute-start | bytes 1253384 | tf_op jit(solution)/shard_map/ppermute | solution.py:153
  40.2 9.7 %collective-permute-start.17 = (bf16[3,32,2176]{2,1,0:T(8,128)(2,1)S(1)}, bf16[3,32,2176]{2,1,0:T(8,128)(2,1)S(1)}, u32[]{:S(2)}, u32[]{:S(2)}) collective-permute-start(bf16[3,32,2176]{2,1,0:T(8,128)(2,1)S(1)} %pad_maximum_fusion.refs_0_), channel_id=1, source_target_pairs={{0,1},{1,0},{2,3},{3,2},{4,5},{5,4},{6,7},{7,6},{8,9},{9,8},{10,11... | collective-permute-start | bytes 1253384 | tf_op jit(solution)/shard_map/ppermute | solution.py:153
  49.9 5.9 %collective-permute-start.21 = (bf16[3,16,2176]{2,1,0:T(8,128)(2,1)S(1)}, bf16[3,16,2176]{2,1,0:T(8,128)(2,1)S(1)}, u32[]{:S(2)}, u32[]{:S(2)}) collective-permute-start(bf16[3,16,2176]{2,1,0:T(8,128)(2,1)S(1)} %slice.109), channel_id=1, source_target_pairs={{0,2},{1,3},{2,0},{3,1},{4,6},{5,7},{6,4},{7,5},{8,10},{9,11},{10,... | collective-permute-start | bytes 626696 | tf_op jit(solution)/shard_map/ppermute | solution.py:153
  50.6 5.8 %collective-permute-start.22 = (bf16[3,16,2176]{2,1,0:T(8,128)(2,1)S(1)}, bf16[3,16,2176]{2,1,0:T(8,128)(2,1)S(1)}, u32[]{:S(2)}, u32[]{:S(2)}) collective-permute-start(bf16[3,16,2176]{2,1,0:T(8,128)(2,1)S(1)} %slice.110), channel_id=1, source_target_pairs={{0,4},{4,0},{8,12},{12,8},{16,20},{20,16},{24,28},{28,24},{1,5},{5... | collective-permute-start | bytes 626696 | tf_op jit(solution)/shard_map/ppermute | solution.py:153
  51.5 4.9 %collective-permute-start.20 = (bf16[3,32,2176]{2,1,0:T(8,128)(2,1)S(1)}, bf16[3,32,2176]{2,1,0:T(8,128)(2,1)S(1)}, u32[]{:S(2)}, u32[]{:S(2)}) collective-permute-start(bf16[3,32,2176]{2,1,0:T(8,128)(2,1)S(1)} %collective-permute-done.19.refs_0_), channel_id=1, source_target_pairs={{0,1},{1,0},{2,3},{3,2},{4,5},{5,4},{6,7},{7,6},{8,9},{9,8},{10,11... | collective-permute-start | bytes 1253384 | tf_op jit(solution)/shard_map/ppermute | solution.py:153
  56.5 4.5 %collective-permute-start.23 = (bf16[3,32,2176]{2,1,0:T(8,128)(2,1)S(1)}, bf16[3,32,2176]{2,1,0:T(8,128)(2,1)S(1)}, u32[]{:S(2)}, u32[]{:S(2)}) collective-permute-start(bf16[3,32,2176]{2,1,0:T(8,128)(2,1)S(1)} %collective-permute-done.18.refs_2_), channel_id=1, source_target_pairs={{0,1},{1,0},{2,3},{3,2},{4,5},{5,4},{6,7},{7,6},{8,9},{9,8},{10,11... | collective-permute-start | bytes 1253384 | tf_op jit(solution)/shard_map/ppermute | solution.py:153
  62.9 7.5 %collective-permute-start.28 = (bf16[1,3,128,512]{3,2,1,0:T(8,128)(2,1)S(1)}, bf16[1,3,128,512]{3,2,1,0:T(8,128)(2,1)S(1)}, u32[]{:S(2)}, u32[]{:S(2)}) collective-permute-start(bf16[1,3,128,512]{3,2,1,0:T(8,128)(2,1)S(1)} %get-tuple-element.202), channel_id=1, source_target_pairs={{0,1},{1,0},{2,3},{3,2},{4,5},{5,4},{6,7},{7,6},{8,9},{9,8},{10,11... | collective-permute-start | bytes 1179656 | tf_op jit(solution)/shard_map/ppermute | solution.py:153
  63.1 7.2 %collective-permute-start.27 = (bf16[3,64,512]{2,1,0:T(8,128)(2,1)S(1)}, bf16[3,64,512]{2,1,0:T(8,128)(2,1)S(1)}, u32[]{:S(2)}, u32[]{:S(2)}) collective-permute-start(bf16[3,64,512]{2,1,0:T(8,128)(2,1)S(1)} %get-tuple-element.233), channel_id=1, source_target_pairs={{0,4},{4,0},{8,12},{12,8},{16,20},{20,16},{24,28},{28,24},{1,5},{5... | collective-permute-start | bytes 589832 | tf_op jit(solution)/shard_map/ppermute | solution.py:153
  64.1 6.9 %collective-permute-start.29 = (bf16[3,64,512]{2,1,0:T(8,128)(2,1)S(1)}, bf16[3,64,512]{2,1,0:T(8,128)(2,1)S(1)}, u32[]{:S(2)}, u32[]{:S(2)}) collective-permute-start(bf16[3,64,512]{2,1,0:T(8,128)(2,1)S(1)} %get-tuple-element.232), channel_id=1, source_target_pairs={{0,2},{1,3},{2,0},{3,1},{4,6},{5,7},{6,4},{7,5},{8,10},{9,11},{10,... | collective-permute-start | bytes 589832 | tf_op jit(solution)/shard_map/ppermute | solution.py:153
  71.1 10.4 %collective-permute-start.33 = (bf16[3,128,512]{2,1,0:T(8,128)(2,1)S(1)}, bf16[3,128,512]{2,1,0:T(8,128)(2,1)S(1)}, u32[]{:S(2)}, u32[]{:S(2)}) collective-permute-start(bf16[3,128,512]{2,1,0:T(8,128)(2,1)S(1)} %pad_maximum_fusion.2), channel_id=1, source_target_pairs={{0,4},{4,0},{8,12},{12,8},{16,20},{20,16},{24,28},{28,24},{1,5},{5... | collective-permute-start | bytes 1179656 | tf_op jit(solution)/shard_map/ppermute | solution.py:153
  72.6 10.0 %collective-permute-start.34 = (bf16[3,128,512]{2,1,0:T(8,128)(2,1)S(1)}, bf16[3,128,512]{2,1,0:T(8,128)(2,1)S(1)}, u32[]{:S(2)}, u32[]{:S(2)}) collective-permute-start(bf16[3,128,512]{2,1,0:T(8,128)(2,1)S(1)} %pad_maximum_fusion.3), channel_id=1, source_target_pairs={{0,2},{1,3},{2,0},{3,1},{4,6},{5,7},{6,4},{7,5},{8,10},{9,11},{10,... | collective-permute-start | bytes 1179656 | tf_op jit(solution)/shard_map/ppermute | solution.py:153
  74.1 8.7 %collective-permute-start.32 = (bf16[1,3,128,512]{3,2,1,0:T(8,128)(2,1)S(1)}, bf16[1,3,128,512]{3,2,1,0:T(8,128)(2,1)S(1)}, u32[]{:S(2)}, u32[]{:S(2)}) collective-permute-start(bf16[1,3,128,512]{3,2,1,0:T(8,128)(2,1)S(1)} %get-tuple-element.206), channel_id=1, source_target_pairs={{0,1},{1,0},{2,3},{3,2},{4,5},{5,4},{6,7},{7,6},{8,9},{9,8},{10,11... | collective-permute-start | bytes 1179656 | tf_op jit(solution)/shard_map/ppermute | solution.py:153
  74.1 8.6 %collective-permute-start.30 = (bf16[2,1,128,512]{3,2,1,0:T(8,128)(2,1)S(1)}, bf16[2,1,128,512]{3,2,1,0:T(8,128)(2,1)S(1)}, u32[]{:S(2)}, u32[]{:S(2)}) collective-permute-start(bf16[2,1,128,512]{3,2,1,0:T(8,128)(2,1)S(1)} %get-tuple-element.204), channel_id=1, source_target_pairs={{0,1},{1,0},{2,3},{3,2},{4,5},{5,4},{6,7},{7,6},{8,9},{9,8},{10,11... | collective-permute-start | bytes 786440 | tf_op jit(solution)/shard_map/ppermute | solution.py:153
  74.6 8.1 %collective-permute-start.31 = (bf16[2,1,128,512]{3,2,1,0:T(8,128)(2,1)S(1)}, bf16[2,1,128,512]{3,2,1,0:T(8,128)(2,1)S(1)}, u32[]{:S(2)}, u32[]{:S(2)}) collective-permute-start(bf16[2,1,128,512]{3,2,1,0:T(8,128)(2,1)S(1)} %get-tuple-element.205), channel_id=1, source_target_pairs={{0,1},{1,0},{2,3},{3,2},{4,5},{5,4},{6,7},{7,6},{8,9},{9,8},{10,11... | collective-permute-start | bytes 786440 | tf_op jit(solution)/shard_map/ppermute | solution.py:153
  83.0 7.3 %collective-permute-start.36 = (bf16[128,512]{1,0:T(8,128)(2,1)S(1)}, bf16[128,512]{1,0:T(8,128)(2,1)S(1)}, u32[]{:S(2)}, u32[]{:S(2)}) collective-permute-start(bf16[128,512]{1,0:T(8,128)(2,1)S(1)} %get-tuple-element.231), channel_id=1, source_target_pairs={{0,8},{4,12},{8,0},{12,4},{16,24},{20,28},{24,16},{28,20},{1,9},{5... | collective-permute-start | bytes 393224 | tf_op jit(solution)/shard_map/ppermute | solution.py:153
  84.5 4.3 %collective-permute-start.38 = (bf16[1,64,512]{2,1,0:T(8,128)(2,1)S(1)}, bf16[1,64,512]{2,1,0:T(8,128)(2,1)S(1)}, u32[]{:S(2)}, u32[]{:S(2)}) collective-permute-start(bf16[1,64,512]{2,1,0:T(8,128)(2,1)S(1)} %get-tuple-element.234), channel_id=1, source_target_pairs={{0,2},{1,3},{2,0},{3,1},{4,6},{5,7},{6,4},{7,5},{8,10},{9,11},{10,... | collective-permute-start | bytes 196616 | tf_op jit(solution)/shard_map/ppermute | solution.py:153
  86.8 6.4 %collective-permute-start.35 = (bf16[128,512]{1,0:T(8,128)(2,1)S(1)}, bf16[128,512]{1,0:T(8,128)(2,1)S(1)}, u32[]{:S(2)}, u32[]{:S(2)}) collective-permute-start(bf16[128,512]{1,0:T(8,128)(2,1)S(1)} %get-tuple-element.230), channel_id=1, source_target_pairs={{0,8},{4,12},{8,0},{12,4},{16,24},{20,28},{24,16},{28,20},{1,9},{5... | collective-permute-start | bytes 393224 | tf_op jit(solution)/shard_map/ppermute | solution.py:153
  90.4 7.3 %collective-permute-start.39 = (bf16[128,512]{1,0:T(8,128)(2,1)S(1)}, bf16[128,512]{1,0:T(8,128)(2,1)S(1)}, u32[]{:S(2)}, u32[]{:S(2)}) collective-permute-start(bf16[128,512]{1,0:T(8,128)(2,1)S(1)} %fusion.5), channel_id=1, source_target_pairs={{0,16},{4,20},{8,24},{12,28},{16,0},{20,4},{24,8},{28,12},{1,17},{... | collective-permute-start | bytes 393224 | tf_op jit(solution)/shard_map/ppermute | solution.py:153
  91.8 6.0 %collective-permute-start.40 = (bf16[1,128,512]{2,1,0:T(8,128)(2,1)S(1)}, bf16[1,128,512]{2,1,0:T(8,128)(2,1)S(1)}, u32[]{:S(2)}, u32[]{:S(2)}) collective-permute-start(bf16[1,128,512]{2,1,0:T(8,128)(2,1)S(1)} %pad_maximum_fusion.5), channel_id=1, source_target_pairs={{0,4},{4,0},{8,12},{12,8},{16,20},{20,16},{24,28},{28,24},{1,5},{5... | collective-permute-start | bytes 393224 | tf_op jit(solution)/shard_map/ppermute | solution.py:153
  92.8 5.0 %collective-permute-start.41 = (bf16[1,128,512]{2,1,0:T(8,128)(2,1)S(1)}, bf16[1,128,512]{2,1,0:T(8,128)(2,1)S(1)}, u32[]{:S(2)}, u32[]{:S(2)}) collective-permute-start(bf16[1,128,512]{2,1,0:T(8,128)(2,1)S(1)} %pad_maximum_fusion.6), channel_id=1, source_target_pairs={{0,2},{1,3},{2,0},{3,1},{4,6},{5,7},{6,4},{7,5},{8,10},{9,11},{10,... | collective-permute-start | bytes 393224 | tf_op jit(solution)/shard_map/ppermute | solution.py:153
  (17 other events, 183.3 us)

commit v17 on v16

--- a/solution.py
+++ b/solution.py
@@ -612,15 +612,15 @@
         token_count,
         residual,
     )
-    x_core_3, all_0, y_3, across_3 = ordered(
-        flip(x_3, "tp", 1), all_0, y_3, jnp.concatenate(across_parts(x_3, y_3), axis=1)
+    x_core_3, y_core_3, all_0, across_3 = ordered(
+        *other_core((x_3, y_3)), all_0, jnp.concatenate(across_parts(x_3, y_3), axis=1)
     )
     side_3 = run_experts(
         near_pieces(0, x_3, x_core_3) + far_pieces(0, (across_3,), (flip(across_3, "tp", 1),)),
         weights,
         token_count,
     )
-    y_core_3, all_0, (keep, (send, first)) = ordered(flip(y_3, "tp", 1), all_0, side_3)
+    y_core_3, all_0, (keep, (send, first)) = ordered(y_core_3, all_0, side_3)
     all_0, y_core_3, keep, send, first = ordered(all_0, y_core_3, keep, send, flip(first, "tp", 1))
     diagonal, keep, send = ordered(joined((keep, (send, first)), 0, 1).astype(jnp.bfloat16), keep, send)
     by_x, by_y = relayed(diagonal)

time: 98.7 us -> 99 us (level)
  starting transfers between devices: 31.8 us -> 29.7 us
  waiting for transfers between devices: 47.2 us -> 48.7 us
    ppermute x42, starting transfers between devices: 31.8 us -> 29.7 us  [flip(): lax.ppermute(value, axis, [(i, i ^ bits) for i in range(lax.axis_size(axi...]
    ppermute x42, waiting for transfers between devices: 47.2 us -> 48.7 us  [flip(): lax.ppermute(value, axis, [(i, i ^ bits) for i in range(lax.axis_size(axi...]
  transfers between devices with their start and end apart: 42 -> 42, of which waited for: 25 -> 25; matrix products, arithmetic and copies ran while one was open for 1% -> 1% of each run, Pallas kernels for 12% -> 9%
where the time goes in v17:
time: 99 us; the launch traced here: 98 us
  waiting for transfers between devices  48.7 us (49%)
  starting transfers between devices  29.7 us (30%)
  Pallas kernels  16.9 us (17%)
  other arithmetic  2.01 us (2%)
    ppermute x42, waiting for transfers between devices, flip(): lax.ppermute(value, axis, [(i, i ^ bits) for i in range(lax.axis_size(axi...  48.7 us
    ppermute x42, starting transfers between devices, flip(): lax.ppermute(value, axis, [(i, i ^ bits) for i in range(lax.axis_size(axi...  29.7 us
    pallas_call x3, Pallas kernels, run_experts(): pl.pallas_call(functools.partial(experts_kernel, plan, len(residual)), ou...  7.45 us
    pallas_call x1, Pallas kernels, attention_shares(): pl.pallas_call(attention_kernel, out_shape=[jax.ShapeDtypeStruct(share, j...  4.88 us
    pallas_call x1, Pallas kernels, attention_shares(): pl.pallas_call(stage_kernel, out_shape=[rope, rope, pltpu.VMEM((1, POOL *...  4.41 us
  transfers between devices with their start and end apart: 42, of which 25 were waited for; matrix products, arithmetic and copies ran while one was open for 1% of the time, Pallas kernels for 9%

profile of v17, /device:TPU:0, one launch (start us, length us, event | category | flops | bytes accessed | tf_op | source)
XLA Modules:
  0.0 98.0 jit_solution(1176569949303199362)
XLA Ops:
  0.0 3.0 %collective-permute-start.1 = (bf16[128,512]{1,0:T(8,128)(2,1)}, bf16[128,512]{1,0:T(8,128)(2,1)S(1)}, u32[]{:S(2)}, u32[]{:S(2)}) collective-permute-start(bf16[128,512]{1,0:T(8,128)(2,1)} %refs_0_.3), channel_id=1, source_target_pairs={{0,2},{1,3},{2,0},{3,1},{4,6},{5,7},{6,4},{7,5},{8,10},{9,11},{10,... | collective-permute-start | bytes 393224 | tf_op jit(solution)/shard_map/ppermute | solution.py:153
  3.0 4.4 %stage.1 = (f32[128,128]{1,0:T(8,128)S(1)}, f32[128,128]{1,0:T(8,128)S(1)}, s32[1,6144]{1,0:T(1,128)S(1)}, f32[1,2048]{1,0:T(1,128)S(1)}, f32[1,128]{1,0:T(1,128...) custom-call(s32[9]{0:T(128)} %refs_0_.2, ...), custom_call_target="tpu_custom_call" | custom-call | tf_op jit(solution)/shard_map/stage/pallas_call | solution.py:373
  9.0 4.9 %attention.1 = (f32[32,2048]{1,0:T(8,128)S(1)}, f32[32,2048]{1,0:T(8,128)S(1)}, bf16[2,32,2048]{2,1,0:T(8,128)(2,1)S(1)}) custom-call(bf16[128,512]{1,0:T(8,128)(2,1)S(1)} %copy-done.3, bf16[128,512]{1,0:T(8,128)(2,1)S(1)} %collective-permute-done.refs_1_, bf16[128,512]{1,0:T(8,128)(2,1)S(1)} %collective-permute-done.1.refs_2_, ...), custom_call_target="tpu_custom_call" | custom-call | tf_op jit(solution)/shard_map/attention/pallas_call | solution.py:393
  14.3 1.2 %collective-permute-done.3 = bf16[2,32,2048]{2,1,0:T(8,128)(2,1)S(1)} collective-permute-done((bf16[2,32,2048]{2,1,0:T(8,128)(2,1)S(1)}, bf16[2,32,2048]{2,1,0:T(8,128)(2,1)S(1)}, u32[]{:S(2)}, u32[]{:S(2)}) %collective-permute-start.3) | collective-permute-done | bytes 262176 | tf_op jit(solution)/shard_map/ppermute | solution.py:153
  16.4 4.9 %collective-permute-done.4.far_ref = bf16[32,2048]{1,0:T(8,128)(2,1)S(1)} collective-permute-done((bf16[32,2048]{1,0:T(8,128)(2,1)S(1)}, bf16[32,2048]{1,0:T(8,128)(2,1)S(1)}, u32[]{:S(2)}, u32[]{:S(2)}) %collective-permute-start.4) | collective-permute-done | bytes 131104 | tf_op jit(solution)/shard_map/ppermute | solution.py:153
  21.5 2.7 %collective-permute-start.6 = (bf16[1,32,2176]{2,1,0:T(8,128)(2,1)S(1)}, bf16[1,32,2176]{2,1,0:T(8,128)(2,1)S(1)}, u32[]{:S(2)}, u32[]{:S(2)}) collective-permute-start(bf16[1,32,2176]{2,1,0:T(8,128)(2,1)S(1)} %bitcast.91), channel_id=1, source_target_pairs={{0,16},{4,20},{8,24},{12,28},{16,0},{20,4},{24,8},{28,12},{1,17},{... | collective-permute-start | bytes 417800 | tf_op jit(solution)/shard_map/ppermute | solution.py:153
  24.2 1.6 %collective-permute-start.5 = (bf16[1,32,2176]{2,1,0:T(8,128)(2,1)S(1)}, bf16[1,32,2176]{2,1,0:T(8,128)(2,1)S(1)}, u32[]{:S(2)}, u32[]{:S(2)}) collective-permute-start(bf16[1,32,2176]{2,1,0:T(8,128)(2,1)S(1)} %bitcast.92), channel_id=1, source_target_pairs={{0,8},{4,12},{8,0},{12,4},{16,24},{20,28},{24,16},{28,20},{1,9},{5... | collective-permute-start | bytes 417800 | tf_op jit(solution)/shard_map/ppermute | solution.py:153
  25.8 1.5 %collective-permute-start.8 = (bf16[1,32,2176]{2,1,0:T(8,128)(2,1)S(1)}, bf16[1,32,2176]{2,1,0:T(8,128)(2,1)S(1)}, u32[]{:S(2)}, u32[]{:S(2)}) collective-permute-start(bf16[1,32,2176]{2,1,0:T(8,128)(2,1)S(1)} %bitcast.93), channel_id=1, source_target_pairs={{0,4},{4,0},{8,12},{12,8},{16,20},{20,16},{24,28},{28,24},{1,5},{5... | collective-permute-start | bytes 417800 | tf_op jit(solution)/shard_map/ppermute | solution.py:153
  27.8 2.9 %collective-permute-done.6 = bf16[1,32,2176]{2,1,0:T(8,128)(2,1)S(1)} collective-permute-done((bf16[1,32,2176]{2,1,0:T(8,128)(2,1)S(1)}, bf16[1,32,2176]{2,1,0:T(8,128)(2,1)S(1)}, u32[]{:S(2)}, u32[]{:S(2)}) %collective-permute-start.6) | collective-permute-done | bytes 139296 | tf_op jit(solution)/shard_map/ppermute | solution.py:153
  31.0 1.3 %collective-permute-done.7.refs_2_ = bf16[1,32,2176]{2,1,0:T(8,128)(2,1)S(1)} collective-permute-done((bf16[1,32,2176]{2,1,0:T(8,128)(2,1)S(1)}, bf16[1,32,2176]{2,1,0:T(8,128)(2,1)S(1)}, u32[]{:S(2)}, u32[]{:S(2)}) %collective-permute-start.7) | collective-permute-done | bytes 139296 | tf_op jit(solution)/shard_map/ppermute | solution.py:153
  33.3 1.1 %collective-permute-start.12 = (bf16[1,16,2176]{2,1,0:T(8,128)(2,1)S(1)}, bf16[1,16,2176]{2,1,0:T(8,128)(2,1)S(1)}, u32[]{:S(2)}, u32[]{:S(2)}) collective-permute-start(bf16[1,16,2176]{2,1,0:T(8,128)(2,1)S(1)} %slice.108), channel_id=1, source_target_pairs={{0,4},{4,0},{8,12},{12,8},{16,20},{20,16},{24,28},{28,24},{1,5},{5... | collective-permute-start | bytes 208904 | tf_op jit(solution)/shard_map/ppermute | solution.py:153
  34.8 2.6 %collective-permute-done.10 = bf16[1,32,2176]{2,1,0:T(8,128)(2,1)S(1)} collective-permute-done((bf16[1,32,2176]{2,1,0:T(8,128)(2,1)S(1)}, bf16[1,32,2176]{2,1,0:T(8,128)(2,1)S(1)}, u32[]{:S(2)}, u32[]{:S(2)}) %collective-permute-start.10) | collective-permute-done | bytes 139296 | tf_op jit(solution)/shard_map/ppermute | solution.py:153
  37.6 1.1 %collective-permute-done.11.refs_6_ = bf16[1,16,2176]{2,1,0:T(8,128)(2,1)S(1)} collective-permute-done((bf16[1,16,2176]{2,1,0:T(8,128)(2,1)S(1)}, bf16[1,16,2176]{2,1,0:T(8,128)(2,1)S(1)}, u32[]{:S(2)}, u32[]{:S(2)}) %collective-permute-start.11) | collective-permute-done | bytes 69664 | tf_op jit(solution)/shard_map/ppermute | solution.py:153
  40.7 1.4 %collective-permute-done.9.refs_5_ = bf16[1,32,2176]{2,1,0:T(8,128)(2,1)S(1)} collective-permute-done((bf16[1,32,2176]{2,1,0:T(8,128)(2,1)S(1)}, bf16[1,32,2176]{2,1,0:T(8,128)(2,1)S(1)}, u32[]{:S(2)}, u32[]{:S(2)}) %collective-permute-start.9) | collective-permute-done | bytes 139296 | tf_op jit(solution)/shard_map/ppermute | solution.py:153
  43.4 5.8 %collective-permute-done.19.refs_0_ = bf16[3,32,2176]{2,1,0:T(8,128)(2,1)S(1)} collective-permute-done((bf16[3,32,2176]{2,1,0:T(8,128)(2,1)S(1)}, bf16[3,32,2176]{2,1,0:T(8,128)(2,1)S(1)}, u32[]{:S(2)}, u32[]{:S(2)}) %collective-permute-start.19) | collective-permute-done | bytes 417824 | tf_op jit(solution)/shard_map/ppermute | solution.py:153
  49.9 1.2 %collective-permute-start.23 = (bf16[3,16,2176]{2,1,0:T(8,128)(2,1)S(1)}, bf16[3,16,2176]{2,1,0:T(8,128)(2,1)S(1)}, u32[]{:S(2)}, u32[]{:S(2)}) collective-permute-start(bf16[3,16,2176]{2,1,0:T(8,128)(2,1)S(1)} %slice.110), channel_id=1, source_target_pairs={{0,4},{4,0},{8,12},{12,8},{16,20},{20,16},{24,28},{28,24},{1,5},{5... | collective-permute-start | bytes 626696 | tf_op jit(solution)/shard_map/ppermute | solution.py:153
  52.0 2.0 %experts.3 = (f32[2,2,1,128,512]{4,3,2,1,0:T(8,128)S(1)}, bf16[2,1,128,512]{3,2,1,0:T(8,128)(2,1)S(1)}, bf16[2,1,128,512]{3,2,1,0:T(8,128)(2,1)S(1)}) custom-call(bf16[1,32,2176]{2,1,0:T(8,128)(2,1)S(1)} %bitcast.96, bf16[1,32,2176]{2,1,0:T(8,128)(2,1)S(1)} %collective-permute-done.13.refs_1_, bf16[1,32,2176]{2,1,0:T(8,128)(2,1)S(1)} %collective-permute-done.7.refs_2_, ...), custom_call_target="tpu_custom_call" | custom-call | tf_op jit(solution)/shard_map/experts/pallas_call | solution.py:490
  54.0 1.8 %collective-permute-done.23 = bf16[3,16,2176]{2,1,0:T(8,128)(2,1)S(1)} collective-permute-done((bf16[3,16,2176]{2,1,0:T(8,128)(2,1)S(1)}, bf16[3,16,2176]{2,1,0:T(8,128)(2,1)S(1)}, u32[]{:S(2)}, u32[]{:S(2)}) %collective-permute-start.23) | collective-permute-done | bytes 208928 | tf_op jit(solution)/shard_map/ppermute | solution.py:153
  55.8 1.1 %collective-permute-done.22 = bf16[3,16,2176]{2,1,0:T(8,128)(2,1)S(1)} collective-permute-done((bf16[3,16,2176]{2,1,0:T(8,128)(2,1)S(1)}, bf16[3,16,2176]{2,1,0:T(8,128)(2,1)S(1)}, u32[]{:S(2)}, u32[]{:S(2)}) %collective-permute-start.22) | collective-permute-done | bytes 208928 | tf_op jit(solution)/shard_map/ppermute | solution.py:153
  57.1 1.7 %collective-permute-done.24.refs_3_ = bf16[3,32,2176]{2,1,0:T(8,128)(2,1)S(1)} collective-permute-done((bf16[3,32,2176]{2,1,0:T(8,128)(2,1)S(1)}, bf16[3,32,2176]{2,1,0:T(8,128)(2,1)S(1)}, u32[]{:S(2)}, u32[]{:S(2)}) %collective-permute-start.24) | collective-permute-done | bytes 417824 | tf_op jit(solution)/shard_map/ppermute | solution.py:153
  58.8 2.7 %experts.4 = (f32[1,2,3,128,512]{4,3,2,1,0:T(8,128)S(1)}, bf16[1,3,128,512]{3,2,1,0:T(8,128)(2,1)S(1)}, bf16[1,3,128,512]{3,2,1,0:T(8,128)(2,1)S(1)}) custom-call(bf16[3,32,2176]{2,1,0:T(8,128)(2,1)S(1)} %collective-permute-done.19.refs_0_, bf16[3,32,2176]{2,1,0:T(8,128)(2,1)S(1)} %collective-permute-done.20.refs_1_, ...), custom_call_target="tpu_custom_call" | custom-call | tf_op jit(solution)/shard_map/experts/pallas_call | solution.py:490
  61.8 1.6 %collective-permute-done.25 = bf16[1,3,128,512]{3,2,1,0:T(8,128)(2,1)S(1)} collective-permute-done((bf16[1,3,128,512]{3,2,1,0:T(8,128)(2,1)S(1)}, bf16[1,3,128,512]{3,2,1,0:T(8,128)(2,1)S(1)}, u32[]{:S(2)}, u32[]{:S(2)}) %collective-permute-start.25) | collective-permute-done | bytes 393248 | tf_op jit(solution)/shard_map/ppermute | solution.py:153
  65.2 2.7 %experts.5 = (f32[1,2,3,128,512]{4,3,2,1,0:T(8,128)S(1)}, bf16[1,3,128,512]{3,2,1,0:T(8,128)(2,1)S(1)}, bf16[1,3,128,512]{3,2,1,0:T(8,128)(2,1)S(1)}) custom-call(bf16[3,32,2176]{2,1,0:T(8,128)(2,1)S(1)} %pad_maximum_fusion.refs_0_, bf16[3,32,2176]{2,1,0:T(8,128)(2,1)S(1)} %collective-permute-done.17.refs_1_, ...), custom_call_target="tpu_custom_call" | custom-call | tf_op jit(solution)/shard_map/experts/pallas_call | solution.py:490
  68.0 2.9 %collective-permute-done.27 = bf16[3,64,512]{2,1,0:T(8,128)(2,1)S(1)} collective-permute-done((bf16[3,64,512]{2,1,0:T(8,128)(2,1)S(1)}, bf16[3,64,512]{2,1,0:T(8,128)(2,1)S(1)}, u32[]{:S(2)}, u32[]{:S(2)}) %collective-permute-start.27) | collective-permute-done | bytes 196640 | tf_op jit(solution)/shard_map/ppermute | solution.py:153
  71.7 1.2 %collective-permute-start.33 = (bf16[3,128,512]{2,1,0:T(8,128)(2,1)S(1)}, bf16[3,128,512]{2,1,0:T(8,128)(2,1)S(1)}, u32[]{:S(2)}, u32[]{:S(2)}) collective-permute-start(bf16[3,128,512]{2,1,0:T(8,128)(2,1)S(1)} %pad_maximum_fusion.2), channel_id=1, source_target_pairs={{0,4},{4,0},{8,12},{12,8},{16,20},{20,16},{24,28},{28,24},{1,5},{5... | collective-permute-start | bytes 1179656 | tf_op jit(solution)/shard_map/ppermute | solution.py:153
  74.1 7.9 %collective-permute-done.33 = bf16[3,128,512]{2,1,0:T(8,128)(2,1)S(1)} collective-permute-done((bf16[3,128,512]{2,1,0:T(8,128)(2,1)S(1)}, bf16[3,128,512]{2,1,0:T(8,128)(2,1)S(1)}, u32[]{:S(2)}, u32[]{:S(2)}) %collective-permute-start.33) | collective-permute-done | bytes 393248 | tf_op jit(solution)/shard_map/ppermute | solution.py:153
  82.0 1.2 %collective-permute-done.34 = bf16[3,128,512]{2,1,0:T(8,128)(2,1)S(1)} collective-permute-done((bf16[3,128,512]{2,1,0:T(8,128)(2,1)S(1)}, bf16[3,128,512]{2,1,0:T(8,128)(2,1)S(1)}, u32[]{:S(2)}, u32[]{:S(2)}) %collective-permute-start.34) | collective-permute-done | bytes 393248 | tf_op jit(solution)/shard_map/ppermute | solution.py:153
  85.4 1.2 %collective-permute-start.37 = (bf16[1,64,512]{2,1,0:T(8,128)(2,1)S(1)}, bf16[1,64,512]{2,1,0:T(8,128)(2,1)S(1)}, u32[]{:S(2)}, u32[]{:S(2)}) collective-permute-start(bf16[1,64,512]{2,1,0:T(8,128)(2,1)S(1)} %get-tuple-element.235), channel_id=1, source_target_pairs={{0,4},{4,0},{8,12},{12,8},{16,20},{20,16},{24,28},{28,24},{1,5},{5... | collective-permute-start | bytes 196616 | tf_op jit(solution)/shard_map/ppermute | solution.py:153
  87.4 1.7 %collective-permute-done.38 = bf16[1,64,512]{2,1,0:T(8,128)(2,1)S(1)} collective-permute-done((bf16[1,64,512]{2,1,0:T(8,128)(2,1)S(1)}, bf16[1,64,512]{2,1,0:T(8,128)(2,1)S(1)}, u32[]{:S(2)}, u32[]{:S(2)}) %collective-permute-start.38) | collective-permute-done | bytes 65568 | tf_op jit(solution)/shard_map/ppermute | solution.py:153
  89.7 1.4 %collective-permute-start.39 = (bf16[128,512]{1,0:T(8,128)(2,1)S(1)}, bf16[128,512]{1,0:T(8,128)(2,1)S(1)}, u32[]{:S(2)}, u32[]{:S(2)}) collective-permute-start(bf16[128,512]{1,0:T(8,128)(2,1)S(1)} %fusion.5), channel_id=1, source_target_pairs={{0,16},{4,20},{8,24},{12,28},{16,0},{20,4},{24,8},{28,12},{1,17},{... | collective-permute-start | bytes 393224 | tf_op jit(solution)/shard_map/ppermute | solution.py:153
  92.2 1.7 %collective-permute-start.41 = (bf16[1,128,512]{2,1,0:T(8,128)(2,1)S(1)}, bf16[1,128,512]{2,1,0:T(8,128)(2,1)S(1)}, u32[]{:S(2)}, u32[]{:S(2)}) collective-permute-start(bf16[1,128,512]{2,1,0:T(8,128)(2,1)S(1)} %pad_maximum_fusion.6), channel_id=1, source_target_pairs={{0,2},{1,3},{2,0},{3,1},{4,6},{5,7},{6,4},{7,5},{8,10},{9,11},{10,... | collective-permute-start | bytes 393224 | tf_op jit(solution)/shard_map/ppermute | solution.py:153
  93.9 3.1 %collective-permute-done.39 = bf16[128,512]{1,0:T(8,128)(2,1)S(1)} collective-permute-done((bf16[128,512]{1,0:T(8,128)(2,1)S(1)}, bf16[128,512]{1,0:T(8,128)(2,1)S(1)}, u32[]{:S(2)}, u32[]{:S(2)}) %collective-permute-start.39) | collective-permute-done | bytes 131104 | tf_op jit(solution)/shard_map/ppermute | solution.py:153
  (106 shorter events, 19.8 us)
Async XLA Ops:
  0.0 7.4 %collective-permute-start.1 = (bf16[128,512]{1,0:T(8,128)(2,1)}, bf16[128,512]{1,0:T(8,128)(2,1)S(1)}, u32[]{:S(2)}, u32[]{:S(2)}) collective-permute-start(bf16[128,512]{1,0:T(8,128)(2,1)} %refs_0_.3), channel_id=1, source_target_pairs={{0,2},{1,3},{2,0},{3,1},{4,6},{5,7},{6,4},{7,5},{8,10},{9,11},{10,... | collective-permute-start | bytes 393224 | tf_op jit(solution)/shard_map/ppermute | solution.py:153
  3.0 5.0 %collective-permute-start = (bf16[128,512]{1,0:T(8,128)(2,1)}, bf16[128,512]{1,0:T(8,128)(2,1)S(1)}, u32[]{:S(2)}, u32[]{:S(2)}) collective-permute-start(bf16[128,512]{1,0:T(8,128)(2,1)} %refs_0_.3), channel_id=1, source_target_pairs={{0,1},{1,0},{2,3},{3,2},{4,5},{5,4},{6,7},{7,6},{8,9},{9,8},{10,11... | collective-permute-start | bytes 393224 | tf_op jit(solution)/shard_map/ppermute | solution.py:153
  15.5 5.8 %collective-permute-start.4 = (bf16[32,2048]{1,0:T(8,128)(2,1)S(1)}, bf16[32,2048]{1,0:T(8,128)(2,1)S(1)}, u32[]{:S(2)}, u32[]{:S(2)}) collective-permute-start(bf16[32,2048]{1,0:T(8,128)(2,1)S(1)} %fusion.10), channel_id=1, source_target_pairs={{0,2},{1,3},{2,0},{3,1},{4,6},{5,7},{6,4},{7,5},{8,10},{9,11},{10,... | collective-permute-start | bytes 393224 | tf_op jit(solution)/shard_map/ppermute | solution.py:153
  21.5 9.2 %collective-permute-start.6 = (bf16[1,32,2176]{2,1,0:T(8,128)(2,1)S(1)}, bf16[1,32,2176]{2,1,0:T(8,128)(2,1)S(1)}, u32[]{:S(2)}, u32[]{:S(2)}) collective-permute-start(bf16[1,32,2176]{2,1,0:T(8,128)(2,1)S(1)} %bitcast.91), channel_id=1, source_target_pairs={{0,16},{4,20},{8,24},{12,28},{16,0},{20,4},{24,8},{28,12},{1,17},{... | collective-permute-start | bytes 417800 | tf_op jit(solution)/shard_map/ppermute | solution.py:153
  24.2 6.7 %collective-permute-start.5 = (bf16[1,32,2176]{2,1,0:T(8,128)(2,1)S(1)}, bf16[1,32,2176]{2,1,0:T(8,128)(2,1)S(1)}, u32[]{:S(2)}, u32[]{:S(2)}) collective-permute-start(bf16[1,32,2176]{2,1,0:T(8,128)(2,1)S(1)} %bitcast.92), channel_id=1, source_target_pairs={{0,8},{4,12},{8,0},{12,4},{16,24},{20,28},{24,16},{28,20},{1,9},{5... | collective-permute-start | bytes 417800 | tf_op jit(solution)/shard_map/ppermute | solution.py:153
  25.8 5.2 %collective-permute-start.8 = (bf16[1,32,2176]{2,1,0:T(8,128)(2,1)S(1)}, bf16[1,32,2176]{2,1,0:T(8,128)(2,1)S(1)}, u32[]{:S(2)}, u32[]{:S(2)}) collective-permute-start(bf16[1,32,2176]{2,1,0:T(8,128)(2,1)S(1)} %bitcast.93), channel_id=1, source_target_pairs={{0,4},{4,0},{8,12},{12,8},{16,20},{20,16},{24,28},{28,24},{1,5},{5... | collective-permute-start | bytes 417800 | tf_op jit(solution)/shard_map/ppermute | solution.py:153
  27.3 5.1 %collective-permute-start.7 = (bf16[1,32,2176]{2,1,0:T(8,128)(2,1)S(1)}, bf16[1,32,2176]{2,1,0:T(8,128)(2,1)S(1)}, u32[]{:S(2)}, u32[]{:S(2)}) collective-permute-start(bf16[1,32,2176]{2,1,0:T(8,128)(2,1)S(1)} %bitcast.94), channel_id=1, source_target_pairs={{0,2},{1,3},{2,0},{3,1},{4,6},{5,7},{6,4},{7,5},{8,10},{9,11},{10,... | collective-permute-start | bytes 417800 | tf_op jit(solution)/shard_map/ppermute | solution.py:153
  32.3 5.1 %collective-permute-start.10 = (bf16[1,32,2176]{2,1,0:T(8,128)(2,1)S(1)}, bf16[1,32,2176]{2,1,0:T(8,128)(2,1)S(1)}, u32[]{:S(2)}, u32[]{:S(2)}) collective-permute-start(bf16[1,32,2176]{2,1,0:T(8,128)(2,1)S(1)} %collective-permute-done.6), channel_id=1, source_target_pairs={{0,8},{4,12},{8,0},{12,4},{16,24},{20,28},{24,16},{28,20},{1,9},{5... | collective-permute-start | bytes 417800 | tf_op jit(solution)/shard_map/ppermute | solution.py:153
  32.8 4.7 %collective-permute-start.13 = (bf16[1,32,2176]{2,1,0:T(8,128)(2,1)S(1)}, bf16[1,32,2176]{2,1,0:T(8,128)(2,1)S(1)}, u32[]{:S(2)}, u32[]{:S(2)}) collective-permute-start(bf16[1,32,2176]{2,1,0:T(8,128)(2,1)S(1)} %bitcast.95), channel_id=1, source_target_pairs={{0,1},{1,0},{2,3},{3,2},{4,5},{5,4},{6,7},{7,6},{8,9},{9,8},{10,11... | collective-permute-start | bytes 417800 | tf_op jit(solution)/shard_map/ppermute | solution.py:153
  32.8 6.0 %collective-permute-start.14 = (bf16[1,32,2176]{2,1,0:T(8,128)(2,1)S(1)}, bf16[1,32,2176]{2,1,0:T(8,128)(2,1)S(1)}, u32[]{:S(2)}, u32[]{:S(2)}) collective-permute-start(bf16[1,32,2176]{2,1,0:T(8,128)(2,1)S(1)} %collective-permute-done.7.refs_2_), channel_id=1, source_target_pairs={{0,1},{1,0},{2,3},{3,2},{4,5},{5,4},{6,7},{7,6},{8,9},{9,8},{10,11... | collective-permute-start | bytes 417800 | tf_op jit(solution)/shard_map/ppermute | solution.py:153
  33.3 4.3 %collective-permute-start.12 = (bf16[1,16,2176]{2,1,0:T(8,128)(2,1)S(1)}, bf16[1,16,2176]{2,1,0:T(8,128)(2,1)S(1)}, u32[]{:S(2)}, u32[]{:S(2)}) collective-permute-start(bf16[1,16,2176]{2,1,0:T(8,128)(2,1)S(1)} %slice.108), channel_id=1, source_target_pairs={{0,4},{4,0},{8,12},{12,8},{16,20},{20,16},{24,28},{28,24},{1,5},{5... | collective-permute-start | bytes 208904 | tf_op jit(solution)/shard_map/ppermute | solution.py:153
  38.8 10.5 %collective-permute-start.19 = (bf16[3,32,2176]{2,1,0:T(8,128)(2,1)S(1)}, bf16[3,32,2176]{2,1,0:T(8,128)(2,1)S(1)}, u32[]{:S(2)}, u32[]{:S(2)}) collective-permute-start(bf16[3,32,2176]{2,1,0:T(8,128)(2,1)S(1)} %pad_maximum_fusion.refs_0_), channel_id=1, source_target_pairs={{0,4},{4,0},{8,12},{12,8},{16,20},{20,16},{24,28},{28,24},{1,5},{5... | collective-permute-start | bytes 1253384 | tf_op jit(solution)/shard_map/ppermute | solution.py:153
  39.6 10.2 %collective-permute-start.18 = (bf16[3,32,2176]{2,1,0:T(8,128)(2,1)S(1)}, bf16[3,32,2176]{2,1,0:T(8,128)(2,1)S(1)}, u32[]{:S(2)}, u32[]{:S(2)}) collective-permute-start(bf16[3,32,2176]{2,1,0:T(8,128)(2,1)S(1)} %pad_maximum_fusion.refs_0_), channel_id=1, source_target_pairs={{0,2},{1,3},{2,0},{3,1},{4,6},{5,7},{6,4},{7,5},{8,10},{9,11},{10,... | collective-permute-start | bytes 1253384 | tf_op jit(solution)/shard_map/ppermute | solution.py:153
  40.2 9.7 %collective-permute-start.17 = (bf16[3,32,2176]{2,1,0:T(8,128)(2,1)S(1)}, bf16[3,32,2176]{2,1,0:T(8,128)(2,1)S(1)}, u32[]{:S(2)}, u32[]{:S(2)}) collective-permute-start(bf16[3,32,2176]{2,1,0:T(8,128)(2,1)S(1)} %pad_maximum_fusion.refs_0_), channel_id=1, source_target_pairs={{0,1},{1,0},{2,3},{3,2},{4,5},{5,4},{6,7},{7,6},{8,9},{9,8},{10,11... | collective-permute-start | bytes 1253384 | tf_op jit(solution)/shard_map/ppermute | solution.py:153
  49.9 5.9 %collective-permute-start.23 = (bf16[3,16,2176]{2,1,0:T(8,128)(2,1)S(1)}, bf16[3,16,2176]{2,1,0:T(8,128)(2,1)S(1)}, u32[]{:S(2)}, u32[]{:S(2)}) collective-permute-start(bf16[3,16,2176]{2,1,0:T(8,128)(2,1)S(1)} %slice.110), channel_id=1, source_target_pairs={{0,4},{4,0},{8,12},{12,8},{16,20},{20,16},{24,28},{28,24},{1,5},{5... | collective-permute-start | bytes 626696 | tf_op jit(solution)/shard_map/ppermute | solution.py:153
  51.1 5.8 %collective-permute-start.22 = (bf16[3,16,2176]{2,1,0:T(8,128)(2,1)S(1)}, bf16[3,16,2176]{2,1,0:T(8,128)(2,1)S(1)}, u32[]{:S(2)}, u32[]{:S(2)}) collective-permute-start(bf16[3,16,2176]{2,1,0:T(8,128)(2,1)S(1)} %slice.109), channel_id=1, source_target_pairs={{0,2},{1,3},{2,0},{3,1},{4,6},{5,7},{6,4},{7,5},{8,10},{9,11},{10,... | collective-permute-start | bytes 626696 | tf_op jit(solution)/shard_map/ppermute | solution.py:153
  51.5 5.5 %collective-permute-start.20 = (bf16[3,32,2176]{2,1,0:T(8,128)(2,1)S(1)}, bf16[3,32,2176]{2,1,0:T(8,128)(2,1)S(1)}, u32[]{:S(2)}, u32[]{:S(2)}) collective-permute-start(bf16[3,32,2176]{2,1,0:T(8,128)(2,1)S(1)} %collective-permute-done.19.refs_0_), channel_id=1, source_target_pairs={{0,1},{1,0},{2,3},{3,2},{4,5},{5,4},{6,7},{7,6},{8,9},{9,8},{10,11... | collective-permute-start | bytes 1253384 | tf_op jit(solution)/shard_map/ppermute | solution.py:153
  51.5 5.5 %collective-permute-start.21 = (bf16[3,32,2176]{2,1,0:T(8,128)(2,1)S(1)}, bf16[3,32,2176]{2,1,0:T(8,128)(2,1)S(1)}, u32[]{:S(2)}, u32[]{:S(2)}) collective-permute-start(bf16[3,32,2176]{2,1,0:T(8,128)(2,1)S(1)} %collective-permute-done.18.refs_2_), channel_id=1, source_target_pairs={{0,1},{1,0},{2,3},{3,2},{4,5},{5,4},{6,7},{7,6},{8,9},{9,8},{10,11... | collective-permute-start | bytes 1253384 | tf_op jit(solution)/shard_map/ppermute | solution.py:153
  63.5 7.5 %collective-permute-start.28 = (bf16[1,3,128,512]{3,2,1,0:T(8,128)(2,1)S(1)}, bf16[1,3,128,512]{3,2,1,0:T(8,128)(2,1)S(1)}, u32[]{:S(2)}, u32[]{:S(2)}) collective-permute-start(bf16[1,3,128,512]{3,2,1,0:T(8,128)(2,1)S(1)} %get-tuple-element.202), channel_id=1, source_target_pairs={{0,1},{1,0},{2,3},{3,2},{4,5},{5,4},{6,7},{7,6},{8,9},{9,8},{10,11... | collective-permute-start | bytes 1179656 | tf_op jit(solution)/shard_map/ppermute | solution.py:153
  63.7 7.2 %collective-permute-start.27 = (bf16[3,64,512]{2,1,0:T(8,128)(2,1)S(1)}, bf16[3,64,512]{2,1,0:T(8,128)(2,1)S(1)}, u32[]{:S(2)}, u32[]{:S(2)}) collective-permute-start(bf16[3,64,512]{2,1,0:T(8,128)(2,1)S(1)} %get-tuple-element.233), channel_id=1, source_target_pairs={{0,4},{4,0},{8,12},{12,8},{16,20},{20,16},{24,28},{28,24},{1,5},{5... | collective-permute-start | bytes 589832 | tf_op jit(solution)/shard_map/ppermute | solution.py:153
  64.7 6.9 %collective-permute-start.29 = (bf16[3,64,512]{2,1,0:T(8,128)(2,1)S(1)}, bf16[3,64,512]{2,1,0:T(8,128)(2,1)S(1)}, u32[]{:S(2)}, u32[]{:S(2)}) collective-permute-start(bf16[3,64,512]{2,1,0:T(8,128)(2,1)S(1)} %get-tuple-element.232), channel_id=1, source_target_pairs={{0,2},{1,3},{2,0},{3,1},{4,6},{5,7},{6,4},{7,5},{8,10},{9,11},{10,... | collective-permute-start | bytes 589832 | tf_op jit(solution)/shard_map/ppermute | solution.py:153
  71.7 10.3 %collective-permute-start.33 = (bf16[3,128,512]{2,1,0:T(8,128)(2,1)S(1)}, bf16[3,128,512]{2,1,0:T(8,128)(2,1)S(1)}, u32[]{:S(2)}, u32[]{:S(2)}) collective-permute-start(bf16[3,128,512]{2,1,0:T(8,128)(2,1)S(1)} %pad_maximum_fusion.2), channel_id=1, source_target_pairs={{0,4},{4,0},{8,12},{12,8},{16,20},{20,16},{24,28},{28,24},{1,5},{5... | collective-permute-start | bytes 1179656 | tf_op jit(solution)/shard_map/ppermute | solution.py:153
  73.1 10.0 %collective-permute-start.34 = (bf16[3,128,512]{2,1,0:T(8,128)(2,1)S(1)}, bf16[3,128,512]{2,1,0:T(8,128)(2,1)S(1)}, u32[]{:S(2)}, u32[]{:S(2)}) collective-permute-start(bf16[3,128,512]{2,1,0:T(8,128)(2,1)S(1)} %pad_maximum_fusion.3), channel_id=1, source_target_pairs={{0,2},{1,3},{2,0},{3,1},{4,6},{5,7},{6,4},{7,5},{8,10},{9,11},{10,... | collective-permute-start | bytes 1179656 | tf_op jit(solution)/shard_map/ppermute | solution.py:153
  73.5 9.8 %collective-permute-start.32 = (bf16[1,3,128,512]{3,2,1,0:T(8,128)(2,1)S(1)}, bf16[1,3,128,512]{3,2,1,0:T(8,128)(2,1)S(1)}, u32[]{:S(2)}, u32[]{:S(2)}) collective-permute-start(bf16[1,3,128,512]{3,2,1,0:T(8,128)(2,1)S(1)} %get-tuple-element.206), channel_id=1, source_target_pairs={{0,1},{1,0},{2,3},{3,2},{4,5},{5,4},{6,7},{7,6},{8,9},{9,8},{10,11... | collective-permute-start | bytes 1179656 | tf_op jit(solution)/shard_map/ppermute | solution.py:153
  73.5 9.7 %collective-permute-start.30 = (bf16[2,1,128,512]{3,2,1,0:T(8,128)(2,1)S(1)}, bf16[2,1,128,512]{3,2,1,0:T(8,128)(2,1)S(1)}, u32[]{:S(2)}, u32[]{:S(2)}) collective-permute-start(bf16[2,1,128,512]{3,2,1,0:T(8,128)(2,1)S(1)} %get-tuple-element.204), channel_id=1, source_target_pairs={{0,1},{1,0},{2,3},{3,2},{4,5},{5,4},{6,7},{7,6},{8,9},{9,8},{10,11... | collective-permute-start | bytes 786440 | tf_op jit(solution)/shard_map/ppermute | solution.py:153
  74.1 9.2 %collective-permute-start.31 = (bf16[2,1,128,512]{3,2,1,0:T(8,128)(2,1)S(1)}, bf16[2,1,128,512]{3,2,1,0:T(8,128)(2,1)S(1)}, u32[]{:S(2)}, u32[]{:S(2)}) collective-permute-start(bf16[2,1,128,512]{3,2,1,0:T(8,128)(2,1)S(1)} %get-tuple-element.205), channel_id=1, source_target_pairs={{0,1},{1,0},{2,3},{3,2},{4,5},{5,4},{6,7},{7,6},{8,9},{9,8},{10,11... | collective-permute-start | bytes 786440 | tf_op jit(solution)/shard_map/ppermute | solution.py:153
  83.6 6.1 %collective-permute-start.36 = (bf16[128,512]{1,0:T(8,128)(2,1)S(1)}, bf16[128,512]{1,0:T(8,128)(2,1)S(1)}, u32[]{:S(2)}, u32[]{:S(2)}) collective-permute-start(bf16[128,512]{1,0:T(8,128)(2,1)S(1)} %get-tuple-element.231), channel_id=1, source_target_pairs={{0,8},{4,12},{8,0},{12,4},{16,24},{20,28},{24,16},{28,20},{1,9},{5... | collective-permute-start | bytes 393224 | tf_op jit(solution)/shard_map/ppermute | solution.py:153
  84.7 4.3 %collective-permute-start.38 = (bf16[1,64,512]{2,1,0:T(8,128)(2,1)S(1)}, bf16[1,64,512]{2,1,0:T(8,128)(2,1)S(1)}, u32[]{:S(2)}, u32[]{:S(2)}) collective-permute-start(bf16[1,64,512]{2,1,0:T(8,128)(2,1)S(1)} %get-tuple-element.234), channel_id=1, source_target_pairs={{0,2},{1,3},{2,0},{3,1},{4,6},{5,7},{6,4},{7,5},{8,10},{9,11},{10,... | collective-permute-start | bytes 196616 | tf_op jit(solution)/shard_map/ppermute | solution.py:153
  86.6 7.4 %collective-permute-start.35 = (bf16[128,512]{1,0:T(8,128)(2,1)S(1)}, bf16[128,512]{1,0:T(8,128)(2,1)S(1)}, u32[]{:S(2)}, u32[]{:S(2)}) collective-permute-start(bf16[128,512]{1,0:T(8,128)(2,1)S(1)} %get-tuple-element.230), channel_id=1, source_target_pairs={{0,8},{4,12},{8,0},{12,4},{16,24},{20,28},{24,16},{28,20},{1,9},{5... | collective-permute-start | bytes 393224 | tf_op jit(solution)/shard_map/ppermute | solution.py:153
  89.7 7.3 %collective-permute-start.39 = (bf16[128,512]{1,0:T(8,128)(2,1)S(1)}, bf16[128,512]{1,0:T(8,128)(2,1)S(1)}, u32[]{:S(2)}, u32[]{:S(2)}) collective-permute-start(bf16[128,512]{1,0:T(8,128)(2,1)S(1)} %fusion.5), channel_id=1, source_target_pairs={{0,16},{4,20},{8,24},{12,28},{16,0},{20,4},{24,8},{28,12},{1,17},{... | collective-permute-start | bytes 393224 | tf_op jit(solution)/shard_map/ppermute | solution.py:153
  91.1 6.0 %collective-permute-start.40 = (bf16[1,128,512]{2,1,0:T(8,128)(2,1)S(1)}, bf16[1,128,512]{2,1,0:T(8,128)(2,1)S(1)}, u32[]{:S(2)}, u32[]{:S(2)}) collective-permute-start(bf16[1,128,512]{2,1,0:T(8,128)(2,1)S(1)} %pad_maximum_fusion.5), channel_id=1, source_target_pairs={{0,4},{4,0},{8,12},{12,8},{16,20},{20,16},{24,28},{28,24},{1,5},{5... | collective-permute-start | bytes 393224 | tf_op jit(solution)/shard_map/ppermute | solution.py:153
  92.2 5.0 %collective-permute-start.41 = (bf16[1,128,512]{2,1,0:T(8,128)(2,1)S(1)}, bf16[1,128,512]{2,1,0:T(8,128)(2,1)S(1)}, u32[]{:S(2)}, u32[]{:S(2)}) collective-permute-start(bf16[1,128,512]{2,1,0:T(8,128)(2,1)S(1)} %pad_maximum_fusion.6), channel_id=1, source_target_pairs={{0,2},{1,3},{2,0},{3,1},{4,6},{5,7},{6,4},{7,5},{8,10},{9,11},{10,... | collective-permute-start | bytes 393224 | tf_op jit(solution)/shard_map/ppermute | solution.py:153
  (17 other events, 185.9 us)

commit v18 on v17

--- a/solution.py
+++ b/solution.py
@@ -389,7 +389,7 @@
     far, *staged = ordered(flip(hidden_in, "tp", 2), *staged, page_list, lengths, table)
     pieces = (hidden_in, flip(hidden_in, "tp", 1), far, flip(far, "tp", 1))
     share = (tokens // 4, width)
-    score_pages, list_pages = 4, 8
+    score_pages, list_pages = 8, 8
     return pl.pallas_call(
         attention_kernel,
         out_shape=[

time: 99 us -> 98.1 us (level)
  no operation moved by 1% of the time
where the time goes in v18:
time: 98.1 us; the launch traced here: 98 us
  waiting for transfers between devices  48.7 us (50%)
  starting transfers between devices  29.7 us (30%)
  Pallas kernels  16.9 us (17%)
  other arithmetic  2.01 us (2%)
    ppermute x42, waiting for transfers between devices, flip(): lax.ppermute(value, axis, [(i, i ^ bits) for i in range(lax.axis_size(axi...  48.7 us
    ppermute x42, starting transfers between devices, flip(): lax.ppermute(value, axis, [(i, i ^ bits) for i in range(lax.axis_size(axi...  29.7 us
    pallas_call x3, Pallas kernels, run_experts(): pl.pallas_call(functools.partial(experts_kernel, plan, len(residual)), ou...  7.45 us
    pallas_call x1, Pallas kernels, attention_shares(): pl.pallas_call(attention_kernel, out_shape=[jax.ShapeDtypeStruct(share, j...  4.88 us
    pallas_call x1, Pallas kernels, attention_shares(): pl.pallas_call(stage_kernel, out_shape=[rope, rope, pltpu.VMEM((1, POOL *...  4.41 us
  transfers between devices with their start and end apart: 42, of which 25 were waited for; matrix products, arithmetic and copies ran while one was open for 1% of the time, Pallas kernels for 9%

profile of v18, /device:TPU:0, one launch (start us, length us, event | category | flops | bytes accessed | tf_op | source)
XLA Modules:
  0.0 98.0 jit_solution(14969478248509796557)
XLA Ops:
  0.0 3.0 %collective-permute-start.1 = (bf16[128,512]{1,0:T(8,128)(2,1)}, bf16[128,512]{1,0:T(8,128)(2,1)S(1)}, u32[]{:S(2)}, u32[]{:S(2)}) collective-permute-start(bf16[128,512]{1,0:T(8,128)(2,1)} %refs_0_.3), channel_id=1, source_target_pairs={{0,2},{1,3},{2,0},{3,1},{4,6},{5,7},{6,4},{7,5},{8,10},{9,11},{10,... | collective-permute-start | bytes 393224 | tf_op jit(solution)/shard_map/ppermute | solution.py:153
  3.0 4.4 %stage.1 = (f32[128,128]{1,0:T(8,128)S(1)}, f32[128,128]{1,0:T(8,128)S(1)}, s32[1,6144]{1,0:T(1,128)S(1)}, f32[1,2048]{1,0:T(1,128)S(1)}, f32[1,128]{1,0:T(1,128...) custom-call(s32[9]{0:T(128)} %refs_0_.2, ...), custom_call_target="tpu_custom_call" | custom-call | tf_op jit(solution)/shard_map/stage/pallas_call | solution.py:373
  9.0 4.9 %attention.1 = (f32[32,2048]{1,0:T(8,128)S(1)}, f32[32,2048]{1,0:T(8,128)S(1)}, bf16[2,32,2048]{2,1,0:T(8,128)(2,1)S(1)}) custom-call(bf16[128,512]{1,0:T(8,128)(2,1)S(1)} %copy-done.3, bf16[128,512]{1,0:T(8,128)(2,1)S(1)} %collective-permute-done.refs_1_, bf16[128,512]{1,0:T(8,128)(2,1)S(1)} %collective-permute-done.1.refs_2_, ...), custom_call_target="tpu_custom_call" | custom-call | tf_op jit(solution)/shard_map/attention/pallas_call | solution.py:393
  14.3 1.2 %collective-permute-done.3 = bf16[2,32,2048]{2,1,0:T(8,128)(2,1)S(1)} collective-permute-done((bf16[2,32,2048]{2,1,0:T(8,128)(2,1)S(1)}, bf16[2,32,2048]{2,1,0:T(8,128)(2,1)S(1)}, u32[]{:S(2)}, u32[]{:S(2)}) %collective-permute-start.3) | collective-permute-done | bytes 262176 | tf_op jit(solution)/shard_map/ppermute | solution.py:153
  16.4 4.9 %collective-permute-done.4.far_ref = bf16[32,2048]{1,0:T(8,128)(2,1)S(1)} collective-permute-done((bf16[32,2048]{1,0:T(8,128)(2,1)S(1)}, bf16[32,2048]{1,0:T(8,128)(2,1)S(1)}, u32[]{:S(2)}, u32[]{:S(2)}) %collective-permute-start.4) | collective-permute-done | bytes 131104 | tf_op jit(solution)/shard_map/ppermute | solution.py:153
  21.5 2.7 %collective-permute-start.6 = (bf16[1,32,2176]{2,1,0:T(8,128)(2,1)S(1)}, bf16[1,32,2176]{2,1,0:T(8,128)(2,1)S(1)}, u32[]{:S(2)}, u32[]{:S(2)}) collective-permute-start(bf16[1,32,2176]{2,1,0:T(8,128)(2,1)S(1)} %bitcast.91), channel_id=1, source_target_pairs={{0,16},{4,20},{8,24},{12,28},{16,0},{20,4},{24,8},{28,12},{1,17},{... | collective-permute-start | bytes 417800 | tf_op jit(solution)/shard_map/ppermute | solution.py:153
  24.2 1.6 %collective-permute-start.5 = (bf16[1,32,2176]{2,1,0:T(8,128)(2,1)S(1)}, bf16[1,32,2176]{2,1,0:T(8,128)(2,1)S(1)}, u32[]{:S(2)}, u32[]{:S(2)}) collective-permute-start(bf16[1,32,2176]{2,1,0:T(8,128)(2,1)S(1)} %bitcast.92), channel_id=1, source_target_pairs={{0,8},{4,12},{8,0},{12,4},{16,24},{20,28},{24,16},{28,20},{1,9},{5... | collective-permute-start | bytes 417800 | tf_op jit(solution)/shard_map/ppermute | solution.py:153
  25.8 1.5 %collective-permute-start.8 = (bf16[1,32,2176]{2,1,0:T(8,128)(2,1)S(1)}, bf16[1,32,2176]{2,1,0:T(8,128)(2,1)S(1)}, u32[]{:S(2)}, u32[]{:S(2)}) collective-permute-start(bf16[1,32,2176]{2,1,0:T(8,128)(2,1)S(1)} %bitcast.93), channel_id=1, source_target_pairs={{0,4},{4,0},{8,12},{12,8},{16,20},{20,16},{24,28},{28,24},{1,5},{5... | collective-permute-start | bytes 417800 | tf_op jit(solution)/shard_map/ppermute | solution.py:153
  27.8 2.9 %collective-permute-done.6 = bf16[1,32,2176]{2,1,0:T(8,128)(2,1)S(1)} collective-permute-done((bf16[1,32,2176]{2,1,0:T(8,128)(2,1)S(1)}, bf16[1,32,2176]{2,1,0:T(8,128)(2,1)S(1)}, u32[]{:S(2)}, u32[]{:S(2)}) %collective-permute-start.6) | collective-permute-done | bytes 139296 | tf_op jit(solution)/shard_map/ppermute | solution.py:153
  31.0 1.3 %collective-permute-done.7.refs_2_ = bf16[1,32,2176]{2,1,0:T(8,128)(2,1)S(1)} collective-permute-done((bf16[1,32,2176]{2,1,0:T(8,128)(2,1)S(1)}, bf16[1,32,2176]{2,1,0:T(8,128)(2,1)S(1)}, u32[]{:S(2)}, u32[]{:S(2)}) %collective-permute-start.7) | collective-permute-done | bytes 139296 | tf_op jit(solution)/shard_map/ppermute | solution.py:153
  33.3 1.1 %collective-permute-start.12 = (bf16[1,16,2176]{2,1,0:T(8,128)(2,1)S(1)}, bf16[1,16,2176]{2,1,0:T(8,128)(2,1)S(1)}, u32[]{:S(2)}, u32[]{:S(2)}) collective-permute-start(bf16[1,16,2176]{2,1,0:T(8,128)(2,1)S(1)} %slice.108), channel_id=1, source_target_pairs={{0,4},{4,0},{8,12},{12,8},{16,20},{20,16},{24,28},{28,24},{1,5},{5... | collective-permute-start | bytes 208904 | tf_op jit(solution)/shard_map/ppermute | solution.py:153
  34.8 2.6 %collective-permute-done.10 = bf16[1,32,2176]{2,1,0:T(8,128)(2,1)S(1)} collective-permute-done((bf16[1,32,2176]{2,1,0:T(8,128)(2,1)S(1)}, bf16[1,32,2176]{2,1,0:T(8,128)(2,1)S(1)}, u32[]{:S(2)}, u32[]{:S(2)}) %collective-permute-start.10) | collective-permute-done | bytes 139296 | tf_op jit(solution)/shard_map/ppermute | solution.py:153
  37.6 1.1 %collective-permute-done.11.refs_6_ = bf16[1,16,2176]{2,1,0:T(8,128)(2,1)S(1)} collective-permute-done((bf16[1,16,2176]{2,1,0:T(8,128)(2,1)S(1)}, bf16[1,16,2176]{2,1,0:T(8,128)(2,1)S(1)}, u32[]{:S(2)}, u32[]{:S(2)}) %collective-permute-start.11) | collective-permute-done | bytes 69664 | tf_op jit(solution)/shard_map/ppermute | solution.py:153
  40.7 1.4 %collective-permute-done.9.refs_5_ = bf16[1,32,2176]{2,1,0:T(8,128)(2,1)S(1)} collective-permute-done((bf16[1,32,2176]{2,1,0:T(8,128)(2,1)S(1)}, bf16[1,32,2176]{2,1,0:T(8,128)(2,1)S(1)}, u32[]{:S(2)}, u32[]{:S(2)}) %collective-permute-start.9) | collective-permute-done | bytes 139296 | tf_op jit(solution)/shard_map/ppermute | solution.py:153
  43.4 5.8 %collective-permute-done.19.refs_0_ = bf16[3,32,2176]{2,1,0:T(8,128)(2,1)S(1)} collective-permute-done((bf16[3,32,2176]{2,1,0:T(8,128)(2,1)S(1)}, bf16[3,32,2176]{2,1,0:T(8,128)(2,1)S(1)}, u32[]{:S(2)}, u32[]{:S(2)}) %collective-permute-start.19) | collective-permute-done | bytes 417824 | tf_op jit(solution)/shard_map/ppermute | solution.py:153
  49.9 1.2 %collective-permute-start.23 = (bf16[3,16,2176]{2,1,0:T(8,128)(2,1)S(1)}, bf16[3,16,2176]{2,1,0:T(8,128)(2,1)S(1)}, u32[]{:S(2)}, u32[]{:S(2)}) collective-permute-start(bf16[3,16,2176]{2,1,0:T(8,128)(2,1)S(1)} %slice.110), channel_id=1, source_target_pairs={{0,4},{4,0},{8,12},{12,8},{16,20},{20,16},{24,28},{28,24},{1,5},{5... | collective-permute-start | bytes 626696 | tf_op jit(solution)/shard_map/ppermute | solution.py:153
  52.0 2.0 %experts.3 = (f32[2,2,1,128,512]{4,3,2,1,0:T(8,128)S(1)}, bf16[2,1,128,512]{3,2,1,0:T(8,128)(2,1)S(1)}, bf16[2,1,128,512]{3,2,1,0:T(8,128)(2,1)S(1)}) custom-call(bf16[1,32,2176]{2,1,0:T(8,128)(2,1)S(1)} %bitcast.96, bf16[1,32,2176]{2,1,0:T(8,128)(2,1)S(1)} %collective-permute-done.13.refs_1_, bf16[1,32,2176]{2,1,0:T(8,128)(2,1)S(1)} %collective-permute-done.7.refs_2_, ...), custom_call_target="tpu_custom_call" | custom-call | tf_op jit(solution)/shard_map/experts/pallas_call | solution.py:490
  54.0 1.8 %collective-permute-done.23 = bf16[3,16,2176]{2,1,0:T(8,128)(2,1)S(1)} collective-permute-done((bf16[3,16,2176]{2,1,0:T(8,128)(2,1)S(1)}, bf16[3,16,2176]{2,1,0:T(8,128)(2,1)S(1)}, u32[]{:S(2)}, u32[]{:S(2)}) %collective-permute-start.23) | collective-permute-done | bytes 208928 | tf_op jit(solution)/shard_map/ppermute | solution.py:153
  55.8 1.1 %collective-permute-done.22 = bf16[3,16,2176]{2,1,0:T(8,128)(2,1)S(1)} collective-permute-done((bf16[3,16,2176]{2,1,0:T(8,128)(2,1)S(1)}, bf16[3,16,2176]{2,1,0:T(8,128)(2,1)S(1)}, u32[]{:S(2)}, u32[]{:S(2)}) %collective-permute-start.22) | collective-permute-done | bytes 208928 | tf_op jit(solution)/shard_map/ppermute | solution.py:153
  57.1 1.7 %collective-permute-done.24.refs_3_ = bf16[3,32,2176]{2,1,0:T(8,128)(2,1)S(1)} collective-permute-done((bf16[3,32,2176]{2,1,0:T(8,128)(2,1)S(1)}, bf16[3,32,2176]{2,1,0:T(8,128)(2,1)S(1)}, u32[]{:S(2)}, u32[]{:S(2)}) %collective-permute-start.24) | collective-permute-done | bytes 417824 | tf_op jit(solution)/shard_map/ppermute | solution.py:153
  58.8 2.7 %experts.4 = (f32[1,2,3,128,512]{4,3,2,1,0:T(8,128)S(1)}, bf16[1,3,128,512]{3,2,1,0:T(8,128)(2,1)S(1)}, bf16[1,3,128,512]{3,2,1,0:T(8,128)(2,1)S(1)}) custom-call(bf16[3,32,2176]{2,1,0:T(8,128)(2,1)S(1)} %collective-permute-done.19.refs_0_, bf16[3,32,2176]{2,1,0:T(8,128)(2,1)S(1)} %collective-permute-done.20.refs_1_, ...), custom_call_target="tpu_custom_call" | custom-call | tf_op jit(solution)/shard_map/experts/pallas_call | solution.py:490
  61.8 1.6 %collective-permute-done.25 = bf16[1,3,128,512]{3,2,1,0:T(8,128)(2,1)S(1)} collective-permute-done((bf16[1,3,128,512]{3,2,1,0:T(8,128)(2,1)S(1)}, bf16[1,3,128,512]{3,2,1,0:T(8,128)(2,1)S(1)}, u32[]{:S(2)}, u32[]{:S(2)}) %collective-permute-start.25) | collective-permute-done | bytes 393248 | tf_op jit(solution)/shard_map/ppermute | solution.py:153
  65.2 2.7 %experts.5 = (f32[1,2,3,128,512]{4,3,2,1,0:T(8,128)S(1)}, bf16[1,3,128,512]{3,2,1,0:T(8,128)(2,1)S(1)}, bf16[1,3,128,512]{3,2,1,0:T(8,128)(2,1)S(1)}) custom-call(bf16[3,32,2176]{2,1,0:T(8,128)(2,1)S(1)} %pad_maximum_fusion.refs_0_, bf16[3,32,2176]{2,1,0:T(8,128)(2,1)S(1)} %collective-permute-done.17.refs_1_, ...), custom_call_target="tpu_custom_call" | custom-call | tf_op jit(solution)/shard_map/experts/pallas_call | solution.py:490
  68.0 2.9 %collective-permute-done.27 = bf16[3,64,512]{2,1,0:T(8,128)(2,1)S(1)} collective-permute-done((bf16[3,64,512]{2,1,0:T(8,128)(2,1)S(1)}, bf16[3,64,512]{2,1,0:T(8,128)(2,1)S(1)}, u32[]{:S(2)}, u32[]{:S(2)}) %collective-permute-start.27) | collective-permute-done | bytes 196640 | tf_op jit(solution)/shard_map/ppermute | solution.py:153
  71.7 1.2 %collective-permute-start.33 = (bf16[3,128,512]{2,1,0:T(8,128)(2,1)S(1)}, bf16[3,128,512]{2,1,0:T(8,128)(2,1)S(1)}, u32[]{:S(2)}, u32[]{:S(2)}) collective-permute-start(bf16[3,128,512]{2,1,0:T(8,128)(2,1)S(1)} %pad_maximum_fusion.2), channel_id=1, source_target_pairs={{0,4},{4,0},{8,12},{12,8},{16,20},{20,16},{24,28},{28,24},{1,5},{5... | collective-permute-start | bytes 1179656 | tf_op jit(solution)/shard_map/ppermute | solution.py:153
  74.1 7.9 %collective-permute-done.33 = bf16[3,128,512]{2,1,0:T(8,128)(2,1)S(1)} collective-permute-done((bf16[3,128,512]{2,1,0:T(8,128)(2,1)S(1)}, bf16[3,128,512]{2,1,0:T(8,128)(2,1)S(1)}, u32[]{:S(2)}, u32[]{:S(2)}) %collective-permute-start.33) | collective-permute-done | bytes 393248 | tf_op jit(solution)/shard_map/ppermute | solution.py:153
  82.0 1.2 %collective-permute-done.34 = bf16[3,128,512]{2,1,0:T(8,128)(2,1)S(1)} collective-permute-done((bf16[3,128,512]{2,1,0:T(8,128)(2,1)S(1)}, bf16[3,128,512]{2,1,0:T(8,128)(2,1)S(1)}, u32[]{:S(2)}, u32[]{:S(2)}) %collective-permute-start.34) | collective-permute-done | bytes 393248 | tf_op jit(solution)/shard_map/ppermute | solution.py:153
  85.4 1.2 %collective-permute-start.37 = (bf16[1,64,512]{2,1,0:T(8,128)(2,1)S(1)}, bf16[1,64,512]{2,1,0:T(8,128)(2,1)S(1)}, u32[]{:S(2)}, u32[]{:S(2)}) collective-permute-start(bf16[1,64,512]{2,1,0:T(8,128)(2,1)S(1)} %get-tuple-element.235), channel_id=1, source_target_pairs={{0,4},{4,0},{8,12},{12,8},{16,20},{20,16},{24,28},{28,24},{1,5},{5... | collective-permute-start | bytes 196616 | tf_op jit(solution)/shard_map/ppermute | solution.py:153
  87.4 1.7 %collective-permute-done.38 = bf16[1,64,512]{2,1,0:T(8,128)(2,1)S(1)} collective-permute-done((bf16[1,64,512]{2,1,0:T(8,128)(2,1)S(1)}, bf16[1,64,512]{2,1,0:T(8,128)(2,1)S(1)}, u32[]{:S(2)}, u32[]{:S(2)}) %collective-permute-start.38) | collective-permute-done | bytes 65568 | tf_op jit(solution)/shard_map/ppermute | solution.py:153
  89.7 1.4 %collective-permute-start.39 = (bf16[128,512]{1,0:T(8,128)(2,1)S(1)}, bf16[128,512]{1,0:T(8,128)(2,1)S(1)}, u32[]{:S(2)}, u32[]{:S(2)}) collective-permute-start(bf16[128,512]{1,0:T(8,128)(2,1)S(1)} %fusion.5), channel_id=1, source_target_pairs={{0,16},{4,20},{8,24},{12,28},{16,0},{20,4},{24,8},{28,12},{1,17},{... | collective-permute-start | bytes 393224 | tf_op jit(solution)/shard_map/ppermute | solution.py:153
  92.2 1.7 %collective-permute-start.41 = (bf16[1,128,512]{2,1,0:T(8,128)(2,1)S(1)}, bf16[1,128,512]{2,1,0:T(8,128)(2,1)S(1)}, u32[]{:S(2)}, u32[]{:S(2)}) collective-permute-start(bf16[1,128,512]{2,1,0:T(8,128)(2,1)S(1)} %pad_maximum_fusion.6), channel_id=1, source_target_pairs={{0,2},{1,3},{2,0},{3,1},{4,6},{5,7},{6,4},{7,5},{8,10},{9,11},{10,... | collective-permute-start | bytes 393224 | tf_op jit(solution)/shard_map/ppermute | solution.py:153
  93.9 3.1 %collective-permute-done.39 = bf16[128,512]{1,0:T(8,128)(2,1)S(1)} collective-permute-done((bf16[128,512]{1,0:T(8,128)(2,1)S(1)}, bf16[128,512]{1,0:T(8,128)(2,1)S(1)}, u32[]{:S(2)}, u32[]{:S(2)}) %collective-permute-start.39) | collective-permute-done | bytes 131104 | tf_op jit(solution)/shard_map/ppermute | solution.py:153
  (106 shorter events, 19.8 us)
Async XLA Ops:
  0.0 7.4 %collective-permute-start.1 = (bf16[128,512]{1,0:T(8,128)(2,1)}, bf16[128,512]{1,0:T(8,128)(2,1)S(1)}, u32[]{:S(2)}, u32[]{:S(2)}) collective-permute-start(bf16[128,512]{1,0:T(8,128)(2,1)} %refs_0_.3), channel_id=1, source_target_pairs={{0,2},{1,3},{2,0},{3,1},{4,6},{5,7},{6,4},{7,5},{8,10},{9,11},{10,... | collective-permute-start | bytes 393224 | tf_op jit(solution)/shard_map/ppermute | solution.py:153
  3.0 5.0 %collective-permute-start = (bf16[128,512]{1,0:T(8,128)(2,1)}, bf16[128,512]{1,0:T(8,128)(2,1)S(1)}, u32[]{:S(2)}, u32[]{:S(2)}) collective-permute-start(bf16[128,512]{1,0:T(8,128)(2,1)} %refs_0_.3), channel_id=1, source_target_pairs={{0,1},{1,0},{2,3},{3,2},{4,5},{5,4},{6,7},{7,6},{8,9},{9,8},{10,11... | collective-permute-start | bytes 393224 | tf_op jit(solution)/shard_map/ppermute | solution.py:153
  15.5 5.8 %collective-permute-start.4 = (bf16[32,2048]{1,0:T(8,128)(2,1)S(1)}, bf16[32,2048]{1,0:T(8,128)(2,1)S(1)}, u32[]{:S(2)}, u32[]{:S(2)}) collective-permute-start(bf16[32,2048]{1,0:T(8,128)(2,1)S(1)} %fusion.10), channel_id=1, source_target_pairs={{0,2},{1,3},{2,0},{3,1},{4,6},{5,7},{6,4},{7,5},{8,10},{9,11},{10,... | collective-permute-start | bytes 393224 | tf_op jit(solution)/shard_map/ppermute | solution.py:153
  21.5 9.2 %collective-permute-start.6 = (bf16[1,32,2176]{2,1,0:T(8,128)(2,1)S(1)}, bf16[1,32,2176]{2,1,0:T(8,128)(2,1)S(1)}, u32[]{:S(2)}, u32[]{:S(2)}) collective-permute-start(bf16[1,32,2176]{2,1,0:T(8,128)(2,1)S(1)} %bitcast.91), channel_id=1, source_target_pairs={{0,16},{4,20},{8,24},{12,28},{16,0},{20,4},{24,8},{28,12},{1,17},{... | collective-permute-start | bytes 417800 | tf_op jit(solution)/shard_map/ppermute | solution.py:153
  24.2 6.7 %collective-permute-start.5 = (bf16[1,32,2176]{2,1,0:T(8,128)(2,1)S(1)}, bf16[1,32,2176]{2,1,0:T(8,128)(2,1)S(1)}, u32[]{:S(2)}, u32[]{:S(2)}) collective-permute-start(bf16[1,32,2176]{2,1,0:T(8,128)(2,1)S(1)} %bitcast.92), channel_id=1, source_target_pairs={{0,8},{4,12},{8,0},{12,4},{16,24},{20,28},{24,16},{28,20},{1,9},{5... | collective-permute-start | bytes 417800 | tf_op jit(solution)/shard_map/ppermute | solution.py:153
  25.8 5.2 %collective-permute-start.8 = (bf16[1,32,2176]{2,1,0:T(8,128)(2,1)S(1)}, bf16[1,32,2176]{2,1,0:T(8,128)(2,1)S(1)}, u32[]{:S(2)}, u32[]{:S(2)}) collective-permute-start(bf16[1,32,2176]{2,1,0:T(8,128)(2,1)S(1)} %bitcast.93), channel_id=1, source_target_pairs={{0,4},{4,0},{8,12},{12,8},{16,20},{20,16},{24,28},{28,24},{1,5},{5... | collective-permute-start | bytes 417800 | tf_op jit(solution)/shard_map/ppermute | solution.py:153
  27.3 5.1 %collective-permute-start.7 = (bf16[1,32,2176]{2,1,0:T(8,128)(2,1)S(1)}, bf16[1,32,2176]{2,1,0:T(8,128)(2,1)S(1)}, u32[]{:S(2)}, u32[]{:S(2)}) collective-permute-start(bf16[1,32,2176]{2,1,0:T(8,128)(2,1)S(1)} %bitcast.94), channel_id=1, source_target_pairs={{0,2},{1,3},{2,0},{3,1},{4,6},{5,7},{6,4},{7,5},{8,10},{9,11},{10,... | collective-permute-start | bytes 417800 | tf_op jit(solution)/shard_map/ppermute | solution.py:153
  32.3 5.1 %collective-permute-start.10 = (bf16[1,32,2176]{2,1,0:T(8,128)(2,1)S(1)}, bf16[1,32,2176]{2,1,0:T(8,128)(2,1)S(1)}, u32[]{:S(2)}, u32[]{:S(2)}) collective-permute-start(bf16[1,32,2176]{2,1,0:T(8,128)(2,1)S(1)} %collective-permute-done.6), channel_id=1, source_target_pairs={{0,8},{4,12},{8,0},{12,4},{16,24},{20,28},{24,16},{28,20},{1,9},{5... | collective-permute-start | bytes 417800 | tf_op jit(solution)/shard_map/ppermute | solution.py:153
  32.8 4.7 %collective-permute-start.13 = (bf16[1,32,2176]{2,1,0:T(8,128)(2,1)S(1)}, bf16[1,32,2176]{2,1,0:T(8,128)(2,1)S(1)}, u32[]{:S(2)}, u32[]{:S(2)}) collective-permute-start(bf16[1,32,2176]{2,1,0:T(8,128)(2,1)S(1)} %bitcast.95), channel_id=1, source_target_pairs={{0,1},{1,0},{2,3},{3,2},{4,5},{5,4},{6,7},{7,6},{8,9},{9,8},{10,11... | collective-permute-start | bytes 417800 | tf_op jit(solution)/shard_map/ppermute | solution.py:153
  32.8 6.0 %collective-permute-start.14 = (bf16[1,32,2176]{2,1,0:T(8,128)(2,1)S(1)}, bf16[1,32,2176]{2,1,0:T(8,128)(2,1)S(1)}, u32[]{:S(2)}, u32[]{:S(2)}) collective-permute-start(bf16[1,32,2176]{2,1,0:T(8,128)(2,1)S(1)} %collective-permute-done.7.refs_2_), channel_id=1, source_target_pairs={{0,1},{1,0},{2,3},{3,2},{4,5},{5,4},{6,7},{7,6},{8,9},{9,8},{10,11... | collective-permute-start | bytes 417800 | tf_op jit(solution)/shard_map/ppermute | solution.py:153
  33.3 4.3 %collective-permute-start.12 = (bf16[1,16,2176]{2,1,0:T(8,128)(2,1)S(1)}, bf16[1,16,2176]{2,1,0:T(8,128)(2,1)S(1)}, u32[]{:S(2)}, u32[]{:S(2)}) collective-permute-start(bf16[1,16,2176]{2,1,0:T(8,128)(2,1)S(1)} %slice.108), channel_id=1, source_target_pairs={{0,4},{4,0},{8,12},{12,8},{16,20},{20,16},{24,28},{28,24},{1,5},{5... | collective-permute-start | bytes 208904 | tf_op jit(solution)/shard_map/ppermute | solution.py:153
  38.8 10.5 %collective-permute-start.19 = (bf16[3,32,2176]{2,1,0:T(8,128)(2,1)S(1)}, bf16[3,32,2176]{2,1,0:T(8,128)(2,1)S(1)}, u32[]{:S(2)}, u32[]{:S(2)}) collective-permute-start(bf16[3,32,2176]{2,1,0:T(8,128)(2,1)S(1)} %pad_maximum_fusion.refs_0_), channel_id=1, source_target_pairs={{0,4},{4,0},{8,12},{12,8},{16,20},{20,16},{24,28},{28,24},{1,5},{5... | collective-permute-start | bytes 1253384 | tf_op jit(solution)/shard_map/ppermute | solution.py:153
  39.6 10.2 %collective-permute-start.18 = (bf16[3,32,2176]{2,1,0:T(8,128)(2,1)S(1)}, bf16[3,32,2176]{2,1,0:T(8,128)(2,1)S(1)}, u32[]{:S(2)}, u32[]{:S(2)}) collective-permute-start(bf16[3,32,2176]{2,1,0:T(8,128)(2,1)S(1)} %pad_maximum_fusion.refs_0_), channel_id=1, source_target_pairs={{0,2},{1,3},{2,0},{3,1},{4,6},{5,7},{6,4},{7,5},{8,10},{9,11},{10,... | collective-permute-start | bytes 1253384 | tf_op jit(solution)/shard_map/ppermute | solution.py:153
  40.2 9.7 %collective-permute-start.17 = (bf16[3,32,2176]{2,1,0:T(8,128)(2,1)S(1)}, bf16[3,32,2176]{2,1,0:T(8,128)(2,1)S(1)}, u32[]{:S(2)}, u32[]{:S(2)}) collective-permute-start(bf16[3,32,2176]{2,1,0:T(8,128)(2,1)S(1)} %pad_maximum_fusion.refs_0_), channel_id=1, source_target_pairs={{0,1},{1,0},{2,3},{3,2},{4,5},{5,4},{6,7},{7,6},{8,9},{9,8},{10,11... | collective-permute-start | bytes 1253384 | tf_op jit(solution)/shard_map/ppermute | solution.py:153
  49.9 5.9 %collective-permute-start.23 = (bf16[3,16,2176]{2,1,0:T(8,128)(2,1)S(1)}, bf16[3,16,2176]{2,1,0:T(8,128)(2,1)S(1)}, u32[]{:S(2)}, u32[]{:S(2)}) collective-permute-start(bf16[3,16,2176]{2,1,0:T(8,128)(2,1)S(1)} %slice.110), channel_id=1, source_target_pairs={{0,4},{4,0},{8,12},{12,8},{16,20},{20,16},{24,28},{28,24},{1,5},{5... | collective-permute-start | bytes 626696 | tf_op jit(solution)/shard_map/ppermute | solution.py:153
  51.1 5.8 %collective-permute-start.22 = (bf16[3,16,2176]{2,1,0:T(8,128)(2,1)S(1)}, bf16[3,16,2176]{2,1,0:T(8,128)(2,1)S(1)}, u32[]{:S(2)}, u32[]{:S(2)}) collective-permute-start(bf16[3,16,2176]{2,1,0:T(8,128)(2,1)S(1)} %slice.109), channel_id=1, source_target_pairs={{0,2},{1,3},{2,0},{3,1},{4,6},{5,7},{6,4},{7,5},{8,10},{9,11},{10,... | collective-permute-start | bytes 626696 | tf_op jit(solution)/shard_map/ppermute | solution.py:153
  51.5 5.5 %collective-permute-start.20 = (bf16[3,32,2176]{2,1,0:T(8,128)(2,1)S(1)}, bf16[3,32,2176]{2,1,0:T(8,128)(2,1)S(1)}, u32[]{:S(2)}, u32[]{:S(2)}) collective-permute-start(bf16[3,32,2176]{2,1,0:T(8,128)(2,1)S(1)} %collective-permute-done.19.refs_0_), channel_id=1, source_target_pairs={{0,1},{1,0},{2,3},{3,2},{4,5},{5,4},{6,7},{7,6},{8,9},{9,8},{10,11... | collective-permute-start | bytes 1253384 | tf_op jit(solution)/shard_map/ppermute | solution.py:153
  51.5 5.5 %collective-permute-start.21 = (bf16[3,32,2176]{2,1,0:T(8,128)(2,1)S(1)}, bf16[3,32,2176]{2,1,0:T(8,128)(2,1)S(1)}, u32[]{:S(2)}, u32[]{:S(2)}) collective-permute-start(bf16[3,32,2176]{2,1,0:T(8,128)(2,1)S(1)} %collective-permute-done.18.refs_2_), channel_id=1, source_target_pairs={{0,1},{1,0},{2,3},{3,2},{4,5},{5,4},{6,7},{7,6},{8,9},{9,8},{10,11... | collective-permute-start | bytes 1253384 | tf_op jit(solution)/shard_map/ppermute | solution.py:153
  63.5 7.5 %collective-permute-start.28 = (bf16[1,3,128,512]{3,2,1,0:T(8,128)(2,1)S(1)}, bf16[1,3,128,512]{3,2,1,0:T(8,128)(2,1)S(1)}, u32[]{:S(2)}, u32[]{:S(2)}) collective-permute-start(bf16[1,3,128,512]{3,2,1,0:T(8,128)(2,1)S(1)} %get-tuple-element.202), channel_id=1, source_target_pairs={{0,1},{1,0},{2,3},{3,2},{4,5},{5,4},{6,7},{7,6},{8,9},{9,8},{10,11... | collective-permute-start | bytes 1179656 | tf_op jit(solution)/shard_map/ppermute | solution.py:153
  63.7 7.2 %collective-permute-start.27 = (bf16[3,64,512]{2,1,0:T(8,128)(2,1)S(1)}, bf16[3,64,512]{2,1,0:T(8,128)(2,1)S(1)}, u32[]{:S(2)}, u32[]{:S(2)}) collective-permute-start(bf16[3,64,512]{2,1,0:T(8,128)(2,1)S(1)} %get-tuple-element.233), channel_id=1, source_target_pairs={{0,4},{4,0},{8,12},{12,8},{16,20},{20,16},{24,28},{28,24},{1,5},{5... | collective-permute-start | bytes 589832 | tf_op jit(solution)/shard_map/ppermute | solution.py:153
  64.7 6.9 %collective-permute-start.29 = (bf16[3,64,512]{2,1,0:T(8,128)(2,1)S(1)}, bf16[3,64,512]{2,1,0:T(8,128)(2,1)S(1)}, u32[]{:S(2)}, u32[]{:S(2)}) collective-permute-start(bf16[3,64,512]{2,1,0:T(8,128)(2,1)S(1)} %get-tuple-element.232), channel_id=1, source_target_pairs={{0,2},{1,3},{2,0},{3,1},{4,6},{5,7},{6,4},{7,5},{8,10},{9,11},{10,... | collective-permute-start | bytes 589832 | tf_op jit(solution)/shard_map/ppermute | solution.py:153
  71.7 10.3 %collective-permute-start.33 = (bf16[3,128,512]{2,1,0:T(8,128)(2,1)S(1)}, bf16[3,128,512]{2,1,0:T(8,128)(2,1)S(1)}, u32[]{:S(2)}, u32[]{:S(2)}) collective-permute-start(bf16[3,128,512]{2,1,0:T(8,128)(2,1)S(1)} %pad_maximum_fusion.2), channel_id=1, source_target_pairs={{0,4},{4,0},{8,12},{12,8},{16,20},{20,16},{24,28},{28,24},{1,5},{5... | collective-permute-start | bytes 1179656 | tf_op jit(solution)/shard_map/ppermute | solution.py:153
  73.1 10.0 %collective-permute-start.34 = (bf16[3,128,512]{2,1,0:T(8,128)(2,1)S(1)}, bf16[3,128,512]{2,1,0:T(8,128)(2,1)S(1)}, u32[]{:S(2)}, u32[]{:S(2)}) collective-permute-start(bf16[3,128,512]{2,1,0:T(8,128)(2,1)S(1)} %pad_maximum_fusion.3), channel_id=1, source_target_pairs={{0,2},{1,3},{2,0},{3,1},{4,6},{5,7},{6,4},{7,5},{8,10},{9,11},{10,... | collective-permute-start | bytes 1179656 | tf_op jit(solution)/shard_map/ppermute | solution.py:153
  73.5 9.8 %collective-permute-start.32 = (bf16[1,3,128,512]{3,2,1,0:T(8,128)(2,1)S(1)}, bf16[1,3,128,512]{3,2,1,0:T(8,128)(2,1)S(1)}, u32[]{:S(2)}, u32[]{:S(2)}) collective-permute-start(bf16[1,3,128,512]{3,2,1,0:T(8,128)(2,1)S(1)} %get-tuple-element.206), channel_id=1, source_target_pairs={{0,1},{1,0},{2,3},{3,2},{4,5},{5,4},{6,7},{7,6},{8,9},{9,8},{10,11... | collective-permute-start | bytes 1179656 | tf_op jit(solution)/shard_map/ppermute | solution.py:153
  73.5 9.7 %collective-permute-start.30 = (bf16[2,1,128,512]{3,2,1,0:T(8,128)(2,1)S(1)}, bf16[2,1,128,512]{3,2,1,0:T(8,128)(2,1)S(1)}, u32[]{:S(2)}, u32[]{:S(2)}) collective-permute-start(bf16[2,1,128,512]{3,2,1,0:T(8,128)(2,1)S(1)} %get-tuple-element.204), channel_id=1, source_target_pairs={{0,1},{1,0},{2,3},{3,2},{4,5},{5,4},{6,7},{7,6},{8,9},{9,8},{10,11... | collective-permute-start | bytes 786440 | tf_op jit(solution)/shard_map/ppermute | solution.py:153
  74.1 9.2 %collective-permute-start.31 = (bf16[2,1,128,512]{3,2,1,0:T(8,128)(2,1)S(1)}, bf16[2,1,128,512]{3,2,1,0:T(8,128)(2,1)S(1)}, u32[]{:S(2)}, u32[]{:S(2)}) collective-permute-start(bf16[2,1,128,512]{3,2,1,0:T(8,128)(2,1)S(1)} %get-tuple-element.205), channel_id=1, source_target_pairs={{0,1},{1,0},{2,3},{3,2},{4,5},{5,4},{6,7},{7,6},{8,9},{9,8},{10,11... | collective-permute-start | bytes 786440 | tf_op jit(solution)/shard_map/ppermute | solution.py:153
  83.6 6.1 %collective-permute-start.36 = (bf16[128,512]{1,0:T(8,128)(2,1)S(1)}, bf16[128,512]{1,0:T(8,128)(2,1)S(1)}, u32[]{:S(2)}, u32[]{:S(2)}) collective-permute-start(bf16[128,512]{1,0:T(8,128)(2,1)S(1)} %get-tuple-element.231), channel_id=1, source_target_pairs={{0,8},{4,12},{8,0},{12,4},{16,24},{20,28},{24,16},{28,20},{1,9},{5... | collective-permute-start | bytes 393224 | tf_op jit(solution)/shard_map/ppermute | solution.py:153
  84.7 4.3 %collective-permute-start.38 = (bf16[1,64,512]{2,1,0:T(8,128)(2,1)S(1)}, bf16[1,64,512]{2,1,0:T(8,128)(2,1)S(1)}, u32[]{:S(2)}, u32[]{:S(2)}) collective-permute-start(bf16[1,64,512]{2,1,0:T(8,128)(2,1)S(1)} %get-tuple-element.234), channel_id=1, source_target_pairs={{0,2},{1,3},{2,0},{3,1},{4,6},{5,7},{6,4},{7,5},{8,10},{9,11},{10,... | collective-permute-start | bytes 196616 | tf_op jit(solution)/shard_map/ppermute | solution.py:153
  86.6 7.4 %collective-permute-start.35 = (bf16[128,512]{1,0:T(8,128)(2,1)S(1)}, bf16[128,512]{1,0:T(8,128)(2,1)S(1)}, u32[]{:S(2)}, u32[]{:S(2)}) collective-permute-start(bf16[128,512]{1,0:T(8,128)(2,1)S(1)} %get-tuple-element.230), channel_id=1, source_target_pairs={{0,8},{4,12},{8,0},{12,4},{16,24},{20,28},{24,16},{28,20},{1,9},{5... | collective-permute-start | bytes 393224 | tf_op jit(solution)/shard_map/ppermute | solution.py:153
  89.7 7.3 %collective-permute-start.39 = (bf16[128,512]{1,0:T(8,128)(2,1)S(1)}, bf16[128,512]{1,0:T(8,128)(2,1)S(1)}, u32[]{:S(2)}, u32[]{:S(2)}) collective-permute-start(bf16[128,512]{1,0:T(8,128)(2,1)S(1)} %fusion.5), channel_id=1, source_target_pairs={{0,16},{4,20},{8,24},{12,28},{16,0},{20,4},{24,8},{28,12},{1,17},{... | collective-permute-start | bytes 393224 | tf_op jit(solution)/shard_map/ppermute | solution.py:153
  91.1 6.0 %collective-permute-start.40 = (bf16[1,128,512]{2,1,0:T(8,128)(2,1)S(1)}, bf16[1,128,512]{2,1,0:T(8,128)(2,1)S(1)}, u32[]{:S(2)}, u32[]{:S(2)}) collective-permute-start(bf16[1,128,512]{2,1,0:T(8,128)(2,1)S(1)} %pad_maximum_fusion.5), channel_id=1, source_target_pairs={{0,4},{4,0},{8,12},{12,8},{16,20},{20,16},{24,28},{28,24},{1,5},{5... | collective-permute-start | bytes 393224 | tf_op jit(solution)/shard_map/ppermute | solution.py:153
  92.2 5.0 %collective-permute-start.41 = (bf16[1,128,512]{2,1,0:T(8,128)(2,1)S(1)}, bf16[1,128,512]{2,1,0:T(8,128)(2,1)S(1)}, u32[]{:S(2)}, u32[]{:S(2)}) collective-permute-start(bf16[1,128,512]{2,1,0:T(8,128)(2,1)S(1)} %pad_maximum_fusion.6), channel_id=1, source_target_pairs={{0,2},{1,3},{2,0},{3,1},{4,6},{5,7},{6,4},{7,5},{8,10},{9,11},{10,... | collective-permute-start | bytes 393224 | tf_op jit(solution)/shard_map/ppermute | solution.py:153
  (17 other events, 185.9 us)
